TPU v7x, 32 devices: a whole 2x2x4 slice. The times are simulated.
32 devices in a mesh: groups: 2 (over y), pass: 16 (over z, x, core).
Axes of the slice: x: 2, y: 2, z: 4, core: 2. Of those that a mesh axis runs over, the one named last changes fastest.
Arguments:
- passage_states: bfloat16 [128, 128, 4096], P(('groups', 'pass')), parts along dimension 0, may hold values from -500 to 500
- memory_queries: bfloat16 [32, 4096], replicated, may hold values from -6 to 6
- memory_gain: bfloat16 [4096], replicated, may hold values from 0.099609375 to 1.8984375
- kv_weight: bfloat16 [4096, 512], P('pass'), may hold values from -0.09375 to 0.09375
- retrieval: int32 [128, 16], P(('groups', 'pass')), parts along dimension 0, may hold values from 0 to 63, as said below
- question_queries: bfloat16 [128, 64, 7424], P(('groups', 'pass')), parts along dimension 0, may hold values from -6 to 6
- question_kv: bfloat16 [128, 64, 512], P(('groups', 'pass')), parts along dimension 0, may hold values from -500 to 500
- question_lengths: int32 [128], P(('groups', 'pass')), parts along dimension 0, may hold values from 1 to 64, 3072 in all
Outputs:
- context: bfloat16 [128, 64, 7424], P(('groups', 'pass')), parts along dimension 0
There are 2 independent parts, one for each index of `groups`. A program takes and returns all parts, laid end to end along the dimension named above; an argument that names none is the same for every part. Nothing has to cross between parts.
Inputs may be any that keep to these rules, and one draw needn't show every extreme that they name: `retrieval`: passage id p is the (p % 4)-th passage of device p // 4. The 16 ids of one query lie on 16 different devices; the 64 ids of one device's queries name each device's passages at most 4 times in all, and some device's exactly 4 times.
All inputs are finite; a program needn't handle non-finite values. No bound on the sum of `question_lengths` on one device may be relied on, other than what follows from the above.
Results may differ from a plain program's by a relative error of at most 0.0065.
Values may be sent and summed in bfloat16 or wider, within the bound.
No kernel may reach another device: no remote copies, remote signals or barrier semaphores. Data moves between devices by JAX's collectives and lax.ppermute only.
A program may use at most 128 MiB of HBM per device.

v0:
```python
import math

import jax
import jax.numpy as jnp
from jax import lax
from jax.sharding import PartitionSpec as P

D = 4096
CH = 32
CHD = 128
MEM = 32
LEN = 128
QLEN = 64
TOPK = 16
H = 116
HD = 64
KVH = 4
GROUP = 29
KVW = 512


def compress_passage(states, memory_queries, memory_gain):
    token_heads = states.reshape(LEN, CH, CHD)
    query_heads = memory_queries.reshape(MEM, CH, CHD)
    scores = jnp.einsum(
        "rhc,thc->hrt", query_heads, token_heads, preferred_element_type=jnp.float32
    ) * (1.0 / math.sqrt(CHD))
    weights = jax.nn.softmax(scores, axis=-1).astype(jnp.bfloat16)
    pooled = jnp.einsum(
        "hrt,thc->rhc", weights, token_heads, preferred_element_type=jnp.float32
    ).reshape(MEM, D)
    mean_square = jnp.mean(pooled * pooled, axis=-1, keepdims=True)
    normed = pooled * lax.rsqrt(mean_square + 1e-06) * memory_gain.astype(jnp.float32)
    return normed.astype(jnp.bfloat16)


def key_mask(length, memory_count):
    position = jnp.arange(QLEN)
    causal = (position[None, :] <= position[:, None]) & (position[None, :] < length)
    return jnp.concatenate([jnp.ones((QLEN, memory_count), dtype=bool), causal], axis=1)


def attend_query(question, memory_kv, own_kv, length):
    half_width = KVH * HD
    key_rows = jnp.concatenate([memory_kv[:, :half_width], own_kv[:, :half_width]], axis=0).reshape(
        -1, KVH, HD
    )
    value_rows = jnp.concatenate(
        [memory_kv[:, half_width:], own_kv[:, half_width:]], axis=0
    ).reshape(-1, KVH, HD)
    query_heads = question.reshape(QLEN, KVH, GROUP, HD)
    scores = jnp.einsum(
        "tgjd,sgd->gjts", query_heads, key_rows, preferred_element_type=jnp.float32
    ) * (1.0 / math.sqrt(HD))
    visible = key_mask(length, memory_kv.shape[0])
    scores = jnp.where(visible, scores, -jnp.inf)
    weights = jax.nn.softmax(scores, axis=-1).astype(jnp.bfloat16)
    context = jnp.einsum(
        "gjts,sgd->tgjd", weights, value_rows, preferred_element_type=jnp.float32
    ).reshape(QLEN, H * HD)
    alive_rows = jnp.arange(QLEN) < length
    return jnp.where(alive_rows[:, None], context, 0.0).astype(jnp.bfloat16)


def local(
    passage_states,
    memory_queries,
    memory_gain,
    kv_weight,
    retrieval,
    question_queries,
    question_kv,
    question_lengths,
):
    own_count = passage_states.shape[0]
    memory_rows = lax.map(
        lambda states: compress_passage(states, memory_queries, memory_gain), passage_states
    )
    flat_rows = memory_rows.reshape(own_count * MEM, D)
    projected = jnp.dot(
        flat_rows,
        lax.all_gather(kv_weight, "pass", axis=0, tiled=True),
        preferred_element_type=jnp.float32,
    )
    memory_kv = projected.astype(jnp.bfloat16).reshape(own_count, MEM, KVW)
    wanted = retrieval.reshape(-1)
    everything = lax.all_gather(memory_kv, "pass", axis=0, tiled=True)
    chosen = jnp.take(everything, wanted, axis=0)
    chosen = chosen.reshape(-1, TOPK * MEM, KVW)

    def answer(inputs):
        memory_part, question, own_kv, length = inputs
        return attend_query(question, memory_part, own_kv, length)

    return lax.map(answer, (chosen, question_queries, question_kv, question_lengths))


def solution(mesh):
    placed = (
        P(("groups", "pass"), None, None),
        P(),
        P(),
        P("pass", None),
        P(("groups", "pass"), None),
        P(("groups", "pass"), None, None),
        P(("groups", "pass"), None, None),
        P(("groups", "pass")),
    )
    return jax.shard_map(
        local,
        mesh=mesh,
        in_specs=placed,
        out_specs=P(("groups", "pass"), None, None),
        check_vma=False,
    )
```

profile of v0, /device:TPU:1, one launch (start us, length us, event | category | flops | bytes accessed | tf_op | source)
XLA Modules:
  0.0 241.3 jit_solution(3462216372957472435)
XLA Ops:
  6.5 0.7 all-gather.3.cloned.1.call-update
  7.3 21.1 %while.20 = (s32[]{:T(128)}, bf16[4,32,4096]{2,1,0:T(8,128)(2,1)S(1)}, bf16[4,128,4096]{2,1,0:T(8,128)(2,1)}, bf16[32,4096]{1,0:T(8,128)(2,1)}, bf16[4096]{0:T(1024)(128)(2,1)}, /*index=5*/s32[]{:T(128)}) while((s32[]{:T(128)}, bf16[4,32,4096]{2,1,0:T(8,128)(2,1)S(1)}, bf16[4,128,4096]{2,1,0:T(8,128)(2,1)}, bf16[32,4096]{1,0:T(8,128)(2,1)}, ...), condition=%wide.region_4.5_spmd, body=%wide.region_0.4_spmd.sunk | while | flops 68556064 | bytes 12665861 | solution.py:76
  7.3 1.3 constant_dynamic-slice_fusion.8
  8.7 0.7 copy.64
  10.1 1.9 multiply_reduce_fusion.2
  12.6 1.3 constant_dynamic-slice_fusion.8
  13.9 0.7 copy.64
  15.4 1.9 multiply_reduce_fusion.2
  17.9 1.4 constant_dynamic-slice_fusion.8
  19.2 0.7 copy.64
  20.6 1.9 multiply_reduce_fusion.2
  23.1 1.3 constant_dynamic-slice_fusion.8
  24.5 0.7 copy.64
  25.9 1.9 multiply_reduce_fusion.2
  28.4 34.4 %all-gather.3.cloned.1.call-done = bf16[4096,512]{1,0:T(8,128)(2,1)} async-done(((bf16[256,512]{1,0:T(8,128)(2,1)}), bf16[4096,512]{1,0:T(8,128)(2,1)}) %all-gather.3.cloned.1.call-update) | async-done | bytes 4194320 | tf_op jit(solution)/shard_map/all_gather | solution.py:82
  62.8 3.5 %convolution_convert_fusion = bf16[128,512]{1,0:T(8,128)(2,1)} fusion(bf16[128,4096]{1,0:T(8,128)(2,1)S(1)} %bitcast.97, bf16[4096,512]{1,0:T(8,128)(2,1)} %all-gather.3.cloned.1.call-done), kind=kOutput, calls=%fused_computation.43 | convolution fusion | flops 536936448 | bytes 5373952 | tf_op jit(solution)/shard_map/dot_general | solution.py:80
  66.7 39.7 %all-gather.5.cloned.1.call-done = bf16[64,32,512]{2,1,0:T(8,128)(2,1)} async-done(((bf16[4,32,512]{2,1,0:T(8,128)(2,1)}), bf16[64,32,512]{2,1,0:T(8,128)(2,1)}) %all-gather.5.cloned.1.call-update) | async-done | bytes 2097168 | tf_op jit(solution)/shard_map/all_gather | solution.py:87
  106.4 2.3 gather_fusion
  108.7 1.6 bitcast_select_fusion.4
  110.3 124.2 %while.21 = (s32[]{:T(128)}, bf16[4,64,7424]{2,1,0:T(8,128)(2,1)}, s32[4]{0:T(128)S(1)}, bf16[4,512,512]{2,1,0:T(8,128)(2,1)}, bf16[4,64,512]{2,1,0:T(8,128)(2,1...) while((s32[]{:T(128)}, bf16[4,64,7424]{2,1,0:T(8,128)(2,1)}, s32[4]{0:T(128)S(1)}, ...), condition=%wide.region_8.9_spmd, body=%wide.region_5.8_spmd.sunk | while | flops 1122034304 | bytes 51063600 | solution.py:95
  110.3 1.1 constant_dynamic-slice_fusion.10
  111.6 0.9 constant_dynamic-slice_fusion.9
  112.6 0.8 pad_maximum_fusion.3
  113.4 0.7 dynamic_slice.33
  114.0 0.7 iota_compare_fusion.3
  114.8 1.3 constant_dynamic-slice_fusion.11
  116.0 2.3 reshape.199
  118.3 11.6 %fusion.78 = (f32[4,29,64]{2,1,0:T(8,128)S(1)}, f32[4,29,64,576]{3,2,1,0:T(8,128)}) fusion(pred[64,576]{1,0:T(8,128)(4,1)S(1)} %concatenate.10, bf16[576,4,64,1]{0,2,3,1:T(8,128)(2,1)} %bitcast.96, bf16[64,4,29,64]{3,2,1,0:T(8,128)(2,1)S(1)} %reshape.199), kind=kOutput, calls=%fused_computation.52.clone.1 | convolution fusion | flops 564462144 | bytes 18416640 | tf_op jit(solution)/shard_map/while/body/eval_jaxpr/sub | solution.py:57
  129.9 9.1 %fusion.79 = bf16[4,64,29,64]{3,1,2,0:T(8,128)(2,1)S(1)} fusion(bf16[576,4,64,1]{0,2,3,1:T(8,128)(2,1)S(1)} %bitcast.95, f32[4,29,64,576]{3,2,1,0:T(8,128)} %get-tuple-element.212, f32[4,29,64]{2,1,0:T(8,128)S(1)} %get-tuple-element.213), kind=kOutput, calls=%fused_computation.25.clone.1 | convolution fusion | flops 555909120 | bytes 18379776 | tf_op jit(solution)/shard_map/while/body/eval_jaxpr/gjts,sgd->tgjd/dot_general | solution.py:58
  139.4 0.9 copy.69
  140.3 1.0 constant_dynamic-update-slice_fusion.2
  141.3 1.1 constant_dynamic-slice_fusion.10
  142.7 0.9 constant_dynamic-slice_fusion.9
  143.6 0.8 pad_maximum_fusion.3
  144.4 0.7 dynamic_slice.33
  145.1 0.7 iota_compare_fusion.3
  145.8 1.3 constant_dynamic-slice_fusion.11
  147.1 2.3 reshape.199
  149.4 11.6 %fusion.78 = (f32[4,29,64]{2,1,0:T(8,128)S(1)}, f32[4,29,64,576]{3,2,1,0:T(8,128)}) fusion(pred[64,576]{1,0:T(8,128)(4,1)S(1)} %concatenate.10, bf16[576,4,64,1]{0,2,3,1:T(8,128)(2,1)} %bitcast.96, bf16[64,4,29,64]{3,2,1,0:T(8,128)(2,1)S(1)} %reshape.199), kind=kOutput, calls=%fused_computation.52.clone.1 | convolution fusion | flops 564462144 | bytes 18416640 | tf_op jit(solution)/shard_map/while/body/eval_jaxpr/sub | solution.py:57
  161.0 9.1 %fusion.79 = bf16[4,64,29,64]{3,1,2,0:T(8,128)(2,1)S(1)} fusion(bf16[576,4,64,1]{0,2,3,1:T(8,128)(2,1)S(1)} %bitcast.95, f32[4,29,64,576]{3,2,1,0:T(8,128)} %get-tuple-element.212, f32[4,29,64]{2,1,0:T(8,128)S(1)} %get-tuple-element.213), kind=kOutput, calls=%fused_computation.25.clone.1 | convolution fusion | flops 555909120 | bytes 18379776 | tf_op jit(solution)/shard_map/while/body/eval_jaxpr/gjts,sgd->tgjd/dot_general | solution.py:58
  170.5 0.9 copy.69
  171.4 1.0 constant_dynamic-update-slice_fusion.2
  172.4 1.1 constant_dynamic-slice_fusion.10
  173.7 0.9 constant_dynamic-slice_fusion.9
  174.7 0.8 pad_maximum_fusion.3
  175.5 0.7 dynamic_slice.33
  176.1 0.7 iota_compare_fusion.3
  176.9 1.3 constant_dynamic-slice_fusion.11
  178.1 2.3 reshape.199
  180.4 11.6 %fusion.78 = (f32[4,29,64]{2,1,0:T(8,128)S(1)}, f32[4,29,64,576]{3,2,1,0:T(8,128)}) fusion(pred[64,576]{1,0:T(8,128)(4,1)S(1)} %concatenate.10, bf16[576,4,64,1]{0,2,3,1:T(8,128)(2,1)} %bitcast.96, bf16[64,4,29,64]{3,2,1,0:T(8,128)(2,1)S(1)} %reshape.199), kind=kOutput, calls=%fused_computation.52.clone.1 | convolution fusion | flops 564462144 | bytes 18416640 | tf_op jit(solution)/shard_map/while/body/eval_jaxpr/sub | solution.py:57
  192.1 9.1 %fusion.79 = bf16[4,64,29,64]{3,1,2,0:T(8,128)(2,1)S(1)} fusion(bf16[576,4,64,1]{0,2,3,1:T(8,128)(2,1)S(1)} %bitcast.95, f32[4,29,64,576]{3,2,1,0:T(8,128)} %get-tuple-element.212, f32[4,29,64]{2,1,0:T(8,128)S(1)} %get-tuple-element.213), kind=kOutput, calls=%fused_computation.25.clone.1 | convolution fusion | flops 555909120 | bytes 18379776 | tf_op jit(solution)/shard_map/while/body/eval_jaxpr/gjts,sgd->tgjd/dot_general | solution.py:58
  201.5 0.9 copy.69
  202.4 1.0 constant_dynamic-update-slice_fusion.2
  203.4 1.1 constant_dynamic-slice_fusion.10
  204.8 0.9 constant_dynamic-slice_fusion.9
  205.7 0.8 pad_maximum_fusion.3
  206.5 0.7 dynamic_slice.33
  207.2 0.7 iota_compare_fusion.3
  207.9 1.3 constant_dynamic-slice_fusion.11
  209.2 2.3 reshape.199
  211.5 11.6 %fusion.78 = (f32[4,29,64]{2,1,0:T(8,128)S(1)}, f32[4,29,64,576]{3,2,1,0:T(8,128)}) fusion(pred[64,576]{1,0:T(8,128)(4,1)S(1)} %concatenate.10, bf16[576,4,64,1]{0,2,3,1:T(8,128)(2,1)} %bitcast.96, bf16[64,4,29,64]{3,2,1,0:T(8,128)(2,1)S(1)} %reshape.199), kind=kOutput, calls=%fused_computation.52.clone.1 | convolution fusion | flops 564462144 | bytes 18416640 | tf_op jit(solution)/shard_map/while/body/eval_jaxpr/sub | solution.py:57
  223.1 9.1 %fusion.79 = bf16[4,64,29,64]{3,1,2,0:T(8,128)(2,1)S(1)} fusion(bf16[576,4,64,1]{0,2,3,1:T(8,128)(2,1)S(1)} %bitcast.95, f32[4,29,64,576]{3,2,1,0:T(8,128)} %get-tuple-element.212, f32[4,29,64]{2,1,0:T(8,128)S(1)} %get-tuple-element.213), kind=kOutput, calls=%fused_computation.25.clone.1 | convolution fusion | flops 555909120 | bytes 18379776 | tf_op jit(solution)/shard_map/while/body/eval_jaxpr/gjts,sgd->tgjd/dot_general | solution.py:58
  232.5 0.9 copy.69
  233.5 1.0 constant_dynamic-update-slice_fusion.2
  (87 shorter events, 8.6 us)
Async XLA Ops:
  6.5 56.3 %all-gather.3.cloned.1.call-start = ((), (), s32[]{:S(2)}) async-start(), calls=%async_computation | async-start | bytes 4456448 | tf_op jit(solution)/shard_map/all_gather | solution.py:82
  7.3 99.2 %all-gather.5.cloned.1.call-start = ((), (), s32[]{:S(2)}) async-start(), calls=%async_computation.1 | async-start | bytes 2228224 | tf_op jit(solution)/shard_map/all_gather | solution.py:87
  7.3 2.0 copy-start
  9.4 3.1 %copy-start.1 = (bf16[4096]{0:T(1024)(128)(2,1)S(1)}, bf16[4096]{0:T(1024)(128)(2,1)}, u32[]{:S(2)}) copy-start(bf16[4096]{0:T(1024)(128)(2,1)} %get-tuple-element.230) | copy-start | bytes 24580 | tf_op jit(solution)/shard_map/while
  12.6 2.0 copy-start
  14.6 3.1 %copy-start.1 = (bf16[4096]{0:T(1024)(128)(2,1)S(1)}, bf16[4096]{0:T(1024)(128)(2,1)}, u32[]{:S(2)}) copy-start(bf16[4096]{0:T(1024)(128)(2,1)} %get-tuple-element.230) | copy-start | bytes 24580 | tf_op jit(solution)/shard_map/while
  17.9 2.0 copy-start
  19.9 3.1 %copy-start.1 = (bf16[4096]{0:T(1024)(128)(2,1)S(1)}, bf16[4096]{0:T(1024)(128)(2,1)}, u32[]{:S(2)}) copy-start(bf16[4096]{0:T(1024)(128)(2,1)} %get-tuple-element.230) | copy-start | bytes 24580 | tf_op jit(solution)/shard_map/while
  23.1 2.0 copy-start
  25.2 3.1 %copy-start.1 = (bf16[4096]{0:T(1024)(128)(2,1)S(1)}, bf16[4096]{0:T(1024)(128)(2,1)}, u32[]{:S(2)}) copy-start(bf16[4096]{0:T(1024)(128)(2,1)} %get-tuple-element.230) | copy-start | bytes 24580 | tf_op jit(solution)/shard_map/while
  28.4 38.0 %copy-start.2 = (s32[4,16]{1,0:T(4,128)S(1)}, s32[4,16]{1,0:T(4,128)}, u32[]{:S(2)}) copy-start(s32[4,16]{1,0:T(4,128)} %param.16) | copy-start | bytes 772
  66.7 43.6 %copy-start.3 = (s32[4]{0:T(128)S(1)}, s32[4]{0:T(128)}, u32[]{:S(2)}) copy-start(s32[4]{0:T(128)} %param.19) | copy-start | bytes 52
Sparse Core Ops, SparseCore 0:
  9.5 53.2 all-gather.2
  66.5 39.8 all-gather.4
where the time goes:
time: 242 us; the launch traced here: 241 us
  matrix products  95.4 us (39%)
  waiting for transfers between devices  74.9 us (31%)
  local copies, waits for them, and re-layouts  45.9 us (19%)
  between operations  13.5 us (6%)
  other arithmetic  10.9 us (5%)
    sub x4, matrix products, attend_query(): weights = jax.nn.softmax(scores, axis=-1).astype(jnp.bfloat16)  46.5 us
    all_gather x1, waiting for transfers between devices, local(): everything = lax.all_gather(memory_kv, 'pass', axis=0, tiled=True)  39.7 us
    dot_general x4, matrix products, attend_query(): jnp.einsum('gjts,sgd->tgjd', weights, value_rows, preferred_element_type=...  36.3 us
    all_gather x1, waiting for transfers between devices, local(): lax.all_gather(kv_weight, 'pass', axis=0, tiled=True)  34.4 us
    dynamic_slice x24, local copies, waits for them, and re-layouts, local(): lax.map(answer, (chosen, question_queries, question_kv, question_lengths))  16.7 us
    reshape x4, local copies, waits for them, and re-layouts, attend_query(): query_heads = question.reshape(QLEN, KVH, GROUP, HD)  9.07 us
    dynamic_slice x8, local copies, waits for them, and re-layouts, local(): lax.map(lambda states: compress_passage(states, memory_queries, memory_ga...  8.01 us
    dynamic_update_slice x8, local copies, waits for them, and re-layouts, local(): lax.map(answer, (chosen, question_queries, question_kv, question_lengths))  7.62 us
  transfers between devices with their start and end apart: 2, of which 2 were waited for; matrix products, arithmetic and copies ran while one was open for 9% of the time, Pallas kernels for 0%

commit v1 on v0

v1 whole, which is shorter than its diff:
```python
import functools
import math

import jax
import jax.numpy as jnp
from jax import lax
from jax.experimental import pallas as pl
from jax.experimental.pallas import tpu as pltpu
from jax.sharding import PartitionSpec as P

D = 4096
CH = 32
CHD = 128
MEM = 32
LEN = 128
QLEN = 64
TOPK = 16
H = 116
HD = 64
KVH = 4
GROUP = 29
KVW = 512

LANES = 2 * HD
PAIRS = GROUP
HALF = PAIRS * LANES
ROWS = TOPK * MEM
KEYS = 2 * (ROWS + QLEN)
NEG = -1e30
VMEM_LIMIT = 52 * 1024 * 1024


def pool_kernel(states_ref, queries_ref, gain_ref, out_ref, pooled):
    squares = jnp.zeros((MEM, CHD), jnp.float32)
    for head in range(CH):
        span = slice(head * CHD, (head + 1) * CHD)
        tokens = states_ref[0, :, span]
        scores = lax.dot_general(
            queries_ref[:, span], tokens, (((1,), (1,)), ((), ())),
            preferred_element_type=jnp.float32,
        ) * (1.0 / math.sqrt(CHD))
        scores = jnp.exp(scores - jnp.max(scores, axis=1, keepdims=True))
        weights = scores / jnp.sum(scores, axis=1, keepdims=True)
        part = jnp.dot(weights.astype(jnp.bfloat16), tokens, preferred_element_type=jnp.float32)
        pooled[:, span] = part
        squares += part * part
    mean_square = jnp.sum(squares, axis=1, keepdims=True) * (1.0 / D)
    scale = lax.rsqrt(mean_square + 1e-06)
    out_ref[0] = (pooled[...] * scale * gain_ref[...].astype(jnp.float32)).astype(jnp.bfloat16)


def pool(states, queries, gain):
    count = states.shape[0]
    return pl.pallas_call(
        pool_kernel,
        grid=(count,),
        in_specs=[
            pl.BlockSpec((1, LEN, D), lambda p: (p, 0, 0)),
            pl.BlockSpec((MEM, D), lambda p: (0, 0)),
            pl.BlockSpec((1, D), lambda p: (0, 0)),
        ],
        out_specs=pl.BlockSpec((1, MEM, D), lambda p: (p, 0, 0)),
        out_shape=jax.ShapeDtypeStruct((count, MEM, D), jnp.bfloat16),
        scratch_shapes=[pltpu.VMEM((MEM, D), jnp.float32)],
        compiler_params=pltpu.CompilerParams(vmem_limit_bytes=VMEM_LIMIT),
        cost_estimate=pl.CostEstimate(
            flops=4 * count * MEM * LEN * D, bytes_accessed=2 * count * LEN * D,
            transcendentals=count * CH * MEM * LEN,
        ),
        name="pool",
    )(states, queries, gain.reshape(1, D))


def attend_kernel(
    start_ref, length_ref, q_ref, k_ref, v_ref, own_k_ref, own_v_ref, out_ref,
    keys, values, key_side, value_side,
):
    first = (pl.program_id(0) == 0) & (pl.program_id(1) == 0)
    query = pl.program_id(1)

    @pl.when(first)
    def _():
        key_side[...] = jnp.zeros_like(key_side)
        lane = lax.broadcasted_iota(jnp.int32, (KEYS, LANES), 1)
        row = lax.broadcasted_iota(jnp.int32, (KEYS, LANES), 0)
        in_b = ((row >= ROWS) & (row < 2 * ROWS)) | (row >= 2 * ROWS + QLEN)
        ones = jnp.where((lane >= HD) == in_b, 1.0, 0.0).astype(jnp.bfloat16)
        for kind in range(3):
            value_side[kind, :, LANES:] = ones

    for slot in range(TOPK):
        start = pl.multiple_of(start_ref[query, slot], MEM)
        keys[slot * MEM:(slot + 1) * MEM, :] = k_ref[pl.ds(start, MEM), :].astype(jnp.float32)
        values[slot * MEM:(slot + 1) * MEM, :] = v_ref[pl.ds(start, MEM), :].astype(jnp.float32)
    length = length_ref[query]

    turned = jnp.transpose(keys[...]).astype(jnp.bfloat16)
    own_k = own_k_ref[0].astype(jnp.float32)
    own_turned = jnp.transpose(jnp.concatenate([own_k, own_k], axis=0))
    column = lax.broadcasted_iota(jnp.int32, (HD, LANES), 1)
    for kind in range(3):
        for member in range(2):
            g = (kind + member) // 2
            rows = slice(member * HD, (member + 1) * HD)
            key_side[kind, rows, member * ROWS:(member + 1) * ROWS] = turned[g * HD:(g + 1) * HD]
            own = own_turned[g * HD:(g + 1) * HD]
            mine = (column >= HD) if member else (column < HD)
            key_side[kind, rows, 2 * ROWS:] = jnp.where(mine, own, 0.0).astype(jnp.bfloat16)

    memory_v = values[...]
    own_v = own_v_ref[0].astype(jnp.float32)
    sides = []
    for block in (memory_v, own_v):
        swapped = pltpu.roll(block, HD, 1)
        low = lax.broadcasted_iota(jnp.int32, block.shape, 1) < HD
        sides.append((
            (jnp.where(low, block, 0.0).astype(jnp.bfloat16), jnp.where(low, swapped, 0.0).astype(jnp.bfloat16)),
            (jnp.where(low, 0.0, swapped).astype(jnp.bfloat16), jnp.where(low, 0.0, block).astype(jnp.bfloat16)),
        ))
    for kind in range(3):
        for member in range(2):
            g = (kind + member) // 2
            value_side[kind, member * ROWS:(member + 1) * ROWS, :LANES] = sides[0][member][g]
            at = 2 * ROWS + member * QLEN
            value_side[kind, at:at + QLEN, :LANES] = sides[1][member][g]

    token = lax.broadcasted_iota(jnp.int32, (QLEN, LANES), 0)
    lane = lax.broadcasted_iota(jnp.int32, (QLEN, LANES), 1)
    key = lax.rem(lane, HD)
    bias = jnp.where((key <= token) & (key < length), 0.0, NEG)
    low = lane < HD
    alive = token < length
    factor = math.log2(math.e) / math.sqrt(HD)

    def chunk(kind, tiles):
        count = len(tiles)
        lhs = jnp.concatenate([q_ref[0, :, t * LANES:(t + 1) * LANES] for t in tiles], axis=0)
        scores = jnp.dot(lhs, key_side[kind], preferred_element_type=jnp.float32)

        def spread(x):
            return jnp.concatenate([x] * count, axis=0) if count > 1 else x

        own = scores[:, 2 * ROWS:] + spread(bias)
        is_low = spread(low)
        tops = []
        for member in range(2):
            top = jnp.where(is_low == (member == 0), own, NEG)
            for at in range(member * ROWS, (member + 1) * ROWS, LANES):
                top = jnp.maximum(top, scores[:, at:at + LANES])
            tops.append(jnp.max(top, axis=1, keepdims=True))
        weights = jnp.concatenate(
            [
                jnp.exp2((scores[:, :ROWS] - tops[0]) * factor).astype(jnp.bfloat16),
                jnp.exp2((scores[:, ROWS:2 * ROWS] - tops[1]) * factor).astype(jnp.bfloat16),
                jnp.exp2((own - jnp.where(is_low, tops[0], tops[1])) * factor).astype(jnp.bfloat16),
            ],
            axis=1,
        )
        mixed = jnp.dot(weights, value_side[kind], preferred_element_type=jnp.float32)
        result = jnp.where(spread(alive), mixed[:, :LANES] / mixed[:, LANES:], 0.0)
        result = result.astype(jnp.bfloat16)
        for i, t in enumerate(tiles):
            out_ref[0, :, t * LANES:(t + 1) * LANES] = result[i * QLEN:(i + 1) * QLEN]

    half = PAIRS // 2
    step = 7
    for at in range(0, half, step):
        chunk(0, list(range(at, min(at + step, half))))
    chunk(1, [half])
    for at in range(half + 1, PAIRS, step):
        chunk(2, list(range(at, min(at + step, PAIRS))))


def attend(starts, lengths, questions, memory_kv, own_kv):
    count = questions.shape[0]
    total = memory_kv.shape[0]
    return pl.pallas_call(
        attend_kernel,
        grid_spec=pltpu.PrefetchScalarGridSpec(
            num_scalar_prefetch=2,
            grid=(2, count),
            in_specs=[
                pl.BlockSpec((1, QLEN, HALF), lambda c, q, *_: (q, 0, c)),
                pl.BlockSpec((total, LANES), lambda c, q, *_: (0, c)),
                pl.BlockSpec((total, LANES), lambda c, q, *_: (0, 2 + c)),
                pl.BlockSpec((1, QLEN, LANES), lambda c, q, *_: (q, 0, c)),
                pl.BlockSpec((1, QLEN, LANES), lambda c, q, *_: (q, 0, 2 + c)),
            ],
            out_specs=pl.BlockSpec((1, QLEN, HALF), lambda c, q, *_: (q, 0, c)),
            scratch_shapes=[
                pltpu.VMEM((ROWS, LANES), jnp.float32),
                pltpu.VMEM((ROWS, LANES), jnp.float32),
                pltpu.VMEM((3, LANES, KEYS), jnp.bfloat16),
                pltpu.VMEM((3, KEYS, 2 * LANES), jnp.bfloat16),
            ],
        ),
        out_shape=jax.ShapeDtypeStruct((count, QLEN, H * HD), jnp.bfloat16),
        compiler_params=pltpu.CompilerParams(vmem_limit_bytes=VMEM_LIMIT),
        cost_estimate=pl.CostEstimate(
            flops=4 * count * QLEN * H * HD * (ROWS + QLEN),
            bytes_accessed=4 * count * QLEN * H * HD + 2 * total * KVW,
            transcendentals=count * QLEN * H * (ROWS + QLEN),
        ),
        name="attend",
    )(starts, lengths, questions, memory_kv, memory_kv, own_kv, own_kv)


def local(
    passage_states,
    memory_queries,
    memory_gain,
    kv_weight,
    retrieval,
    question_queries,
    question_kv,
    question_lengths,
):
    own_count = passage_states.shape[0]
    whole_weight = lax.all_gather(kv_weight, "pass", axis=0, tiled=True)
    memory_rows = pool(passage_states, memory_queries, memory_gain)
    projected = jnp.dot(
        memory_rows.reshape(own_count * MEM, D), whole_weight, preferred_element_type=jnp.float32
    )
    memory_kv = projected.astype(jnp.bfloat16)
    everything = lax.all_gather(memory_kv, "pass", axis=0, tiled=True)
    return attend(retrieval * MEM, question_lengths, question_queries, everything, question_kv)


def solution(mesh):
    placed = (
        P(("groups", "pass"), None, None),
        P(),
        P(),
        P("pass", None),
        P(("groups", "pass"), None),
        P(("groups", "pass"), None, None),
        P(("groups", "pass"), None, None),
        P(("groups", "pass")),
    )
    return jax.shard_map(
        local,
        mesh=mesh,
        in_specs=placed,
        out_specs=P(("groups", "pass"), None, None),
        check_vma=False,
    )
```

time: 242 us -> 147 us (0.61)
  matrix products: 95.4 us -> 3.62 us
  Pallas kernels: 0 us -> 76.2 us
  local copies, waits for them, and re-layouts: 45.9 us -> 1.66 us
  waiting for transfers between devices: 74.9 us -> 51.9 us
  other arithmetic: 10.9 us -> 0.01 us
    pallas_call x0 -> x2, Pallas kernels: none -> 76.2 us  [the longest x1 42.9 us: pool(): pl.pallas_call(pool_kernel, grid=(count,), in_specs=[pl.BlockSpec((1, LEN...]
    sub x4 -> x0, matrix products: 46.5 us -> none  [attend_query(): weights = jax.nn.softmax(scores, axis=-1).astype(jnp.bfloat16)]
    dot_general x13 -> x1, matrix products: 48.9 us -> 3.62 us  [local(): jnp.dot(memory_rows.reshape(own_count * MEM, D), whole_weight, preferred_...]
    dynamic_slice x32 -> x0, local copies, waits for them, and re-layouts: 24.7 us -> none  [the longest x24 16.7 us: local(): lax.map(answer, (chosen, question_queries, question_kv, question_lengths))]
    all_gather x1, waiting for transfers between devices: 34.4 us -> 11.1 us  [local(): whole_weight = lax.all_gather(kv_weight, 'pass', axis=0, tiled=True)]
    reshape x9 -> x1, local copies, waits for them, and re-layouts: 9.55 us -> 0.71 us  [pool(): gain.reshape(1, D)]
    dynamic_update_slice x8 -> x0, local copies, waits for them, and re-layouts: 7.62 us -> none  [local(): lax.map(answer, (chosen, question_queries, question_kv, question_lengths))]
    concatenate x4 -> x0, other arithmetic: 3.12 us -> none  [attend_query(): jnp.concatenate([memory_kv[:, half_width:], own_kv[:, half_width:]], axis=0)]
  transfers between devices with their start and end apart: 2 -> 2, of which waited for: 2 -> 2; matrix products, arithmetic and copies ran while one was open for 9% -> 0% of each run, Pallas kernels for 0% -> 29%
where the time goes in v1:
time: 147 us
  Pallas kernels  76.2 us (52%)
  waiting for transfers between devices  51.9 us (35%)
  between operations  13.4 us (9%)
  matrix products  3.62 us (2%)
  local copies, waits for them, and re-layouts  1.66 us (1%)
    pallas_call x1, Pallas kernels, pool(): pl.pallas_call(pool_kernel, grid=(count,), in_specs=[pl.BlockSpec((1, LEN...  42.9 us
    all_gather x1, waiting for transfers between devices, local(): everything = lax.all_gather(memory_kv, 'pass', axis=0, tiled=True)  40 us
    pallas_call x1, Pallas kernels, attend(): pl.pallas_call(attend_kernel, grid_spec=pltpu.PrefetchScalarGridSpec(num_...  33.3 us
    all_gather x1, waiting for transfers between devices, local(): whole_weight = lax.all_gather(kv_weight, 'pass', axis=0, tiled=True)  11.1 us
    dot_general x1, matrix products, local(): jnp.dot(memory_rows.reshape(own_count * MEM, D), whole_weight, preferred_...  3.62 us
  transfers between devices with their start and end apart: 2, of which 2 were waited for; matrix products, arithmetic and copies ran while one was open for 0% of the time, Pallas kernels for 29%

profile of v1, /device:TPU:1, one launch (start us, length us, event | category | flops | bytes accessed | tf_op | source)
XLA Modules:
  0.0 146.9 jit_solution(9206601265296306439)
XLA Ops:
  6.5 0.0 all-gather.3.cloned.1.call-start
  6.5 0.7 all-gather.3.cloned.1.call-update
  7.3 0.0 all-gather.5.cloned.1.call-start
  7.3 0.7 reshape.6.gain_ref
  8.0 0.0 copy-start
  8.0 0.9 copy-done
  9.0 0.0 copy-start.3
  9.0 0.0 copy-start.1
  9.0 0.0 copy-start.2
  9.0 42.9 %pool.1 = bf16[4,32,4096]{2,1,0:T(8,128)(2,1)S(1)} custom-call(bf16[4,128,4096]{2,1,0:T(8,128)(2,1)} %states_ref.1, bf16[32,4096]{1,0:T(8,128)(2,1)S(1)} %copy-done, bf16[1,4096]{1,0:T(2,128)(2,1)S(1)} %reshape.6.gain_ref), custom_call_target="tpu_custom_call" | custom-call | flops 268435456 | bytes 4194304 | tf_op jit(solution)/shard_map/pool/pallas_call | solution.py:54
  51.9 11.1 %all-gather.3.cloned.1.call-done = bf16[4096,512]{1,0:T(8,128)(2,1)} async-done(((bf16[256,512]{1,0:T(8,128)(2,1)}), bf16[4096,512]{1,0:T(8,128)(2,1)}) %all-gather.3.cloned.1.call-update) | async-done | bytes 4194320 | tf_op jit(solution)/shard_map/all_gather | solution.py:219
  63.0 3.6 %convolution_convert_fusion = bf16[128,512]{1,0:T(8,128)(2,1)} fusion(bf16[128,4096]{1,0:T(8,128)(2,1)S(1)} %bitcast.3, bf16[4096,512]{1,0:T(8,128)(2,1)} %all-gather.3.cloned.1.call-done), kind=kOutput, calls=%fused_computation | convolution fusion | flops 536936448 | bytes 5373952 | tf_op jit(solution)/shard_map/dot_general | solution.py:221
  66.6 0.0 all-gather.5.cloned.1.call-update
  66.6 0.0 copy-done.3
  66.7 40.0 %all-gather.5.cloned.1.call-done.k_ref.v_ref = bf16[2048,512]{1,0:T(8,128)(2,1)} async-done(((bf16[128,512]{1,0:T(8,128)(2,1)}), bf16[2048,512]{1,0:T(8,128)(2,1)}) %all-gather.5.cloned.1.call-update) | async-done | bytes 2097168 | tf_op jit(solution)/shard_map/all_gather | solution.py:225
  106.7 0.0 copy-done.1
  106.7 0.0 copy-done.2
  106.7 33.3 %attend.1 = bf16[4,64,7424]{2,1,0:T(8,128)(2,1)} custom-call(s32[4,16]{1,0:T(4,128)S(1)} %broadcast_multiply_fusion.start_ref, s32[4]{0:T(128)S(1)} %copy-done.2, bf16[4,64,7424]{2,1,0:T(8,128)(2,1)} %q_ref.1, bf16[2048,512]{1,0:T(8,128)(2,1)} %all-gather.5.cloned.1.call-done.k_ref.v_ref, bf16[2048,512]{1,0:T(8,128)(2,1)} %all-gather.5.cloned.1.call-done.k_ref.v_ref, ...), custom_call_target="tpu_custom_call" | custom-call | flops 4378853376 | bytes 9699328 | tf_op jit(solution)/shard_map/attend/pallas_call | solution.py:177
  (1 shorter events, 0.0 us)
Async XLA Ops:
  6.5 56.5 %all-gather.3.cloned.1.call-start = ((), (), s32[]{:S(2)}) async-start(), calls=%async_computation | async-start | bytes 4456448 | tf_op jit(solution)/shard_map/all_gather | solution.py:219
  7.3 99.5 %all-gather.5.cloned.1.call-start = ((), (), s32[]{:S(2)}) async-start(), calls=%async_computation.1 | async-start | bytes 2228224 | tf_op jit(solution)/shard_map/all_gather | solution.py:225
  8.0 1.0 copy-start
  9.0 57.7 %copy-start.3 = (s32[4,16]{1,0:T(4,128)S(1)}, s32[4,16]{1,0:T(4,128)}, u32[]{:S(2)}) copy-start(s32[4,16]{1,0:T(4,128)} %param.12) | copy-start | bytes 772
  9.0 97.7 %copy-start.1 = (bf16[4,64,512]{2,1,0:T(8,128)(2,1)S(1)}, bf16[4,64,512]{2,1,0:T(8,128)(2,1)}, u32[]{:S(2)}) copy-start(bf16[4,64,512]{2,1,0:T(8,128)(2,1)} %own_v_ref.1) | copy-start | bytes 786436
  9.0 97.7 %copy-start.2 = (s32[4]{0:T(128)S(1)}, s32[4]{0:T(128)}, u32[]{:S(2)}) copy-start(s32[4]{0:T(128)} %length_ref.1) | copy-start | bytes 52
Sparse Core Ops, SparseCore 0:
  9.5 53.4 all-gather.2
  66.8 39.9 all-gather.4

commit v2 on v1

--- a/solution.py
+++ b/solution.py
@@ -27,58 +27,66 @@
 ROWS = TOPK * MEM
 KEYS = 2 * (ROWS + QLEN)
 NEG = -1e30
-VMEM_LIMIT = 52 * 1024 * 1024
+POOL_HEADS = 16
+LINES = 4
+CHIP = 8
+MIB = 1024 * 1024
 
 
 def pool_kernel(states_ref, queries_ref, gain_ref, out_ref, pooled):
     squares = jnp.zeros((MEM, CHD), jnp.float32)
-    for head in range(CH):
-        span = slice(head * CHD, (head + 1) * CHD)
-        tokens = states_ref[0, :, span]
-        scores = lax.dot_general(
-            queries_ref[:, span], tokens, (((1,), (1,)), ((), ())),
-            preferred_element_type=jnp.float32,
+    for base in range(0, CH, POOL_HEADS):
+        spans = [slice(h * CHD, (h + 1) * CHD) for h in range(base, base + POOL_HEADS)]
+        scores = jnp.concatenate(
+            [
+                lax.dot_general(
+                    queries_ref[:, span], states_ref[0, :, span], (((1,), (1,)), ((), ())),
+                    preferred_element_type=jnp.float32,
+                )
+                for span in spans
+            ],
+            axis=0,
         ) * (1.0 / math.sqrt(CHD))
         scores = jnp.exp(scores - jnp.max(scores, axis=1, keepdims=True))
-        weights = scores / jnp.sum(scores, axis=1, keepdims=True)
-        part = jnp.dot(weights.astype(jnp.bfloat16), tokens, preferred_element_type=jnp.float32)
-        pooled[:, span] = part
-        squares += part * part
+        weights = (scores / jnp.sum(scores, axis=1, keepdims=True)).astype(jnp.bfloat16)
+        for i, span in enumerate(spans):
+            part = jnp.dot(
+                weights[i * MEM:(i + 1) * MEM], states_ref[0, :, span], preferred_element_type=jnp.float32
+            )
+            pooled[:, span] = part
+            squares += part * part
     mean_square = jnp.sum(squares, axis=1, keepdims=True) * (1.0 / D)
     scale = lax.rsqrt(mean_square + 1e-06)
-    out_ref[0] = (pooled[...] * scale * gain_ref[...].astype(jnp.float32)).astype(jnp.bfloat16)
-
-
-def pool(states, queries, gain):
-    count = states.shape[0]
+    out_ref[...] = (pooled[...] * scale * gain_ref[...].astype(jnp.float32)).astype(jnp.bfloat16)
+
+
+def pool(states, queries, gain, passage):
     return pl.pallas_call(
         pool_kernel,
-        grid=(count,),
+        grid=(1,),
         in_specs=[
-            pl.BlockSpec((1, LEN, D), lambda p: (p, 0, 0)),
-            pl.BlockSpec((MEM, D), lambda p: (0, 0)),
-            pl.BlockSpec((1, D), lambda p: (0, 0)),
+            pl.BlockSpec((1, LEN, D), lambda _: (passage, 0, 0)),
+            pl.BlockSpec((MEM, D), lambda _: (0, 0)),
+            pl.BlockSpec((1, D), lambda _: (0, 0)),
         ],
-        out_specs=pl.BlockSpec((1, MEM, D), lambda p: (p, 0, 0)),
-        out_shape=jax.ShapeDtypeStruct((count, MEM, D), jnp.bfloat16),
+        out_specs=pl.BlockSpec((MEM, D), lambda _: (0, 0)),
+        out_shape=jax.ShapeDtypeStruct((MEM, D), jnp.bfloat16),
         scratch_shapes=[pltpu.VMEM((MEM, D), jnp.float32)],
-        compiler_params=pltpu.CompilerParams(vmem_limit_bytes=VMEM_LIMIT),
+        compiler_params=pltpu.CompilerParams(vmem_limit_bytes=16 * MIB),
         cost_estimate=pl.CostEstimate(
-            flops=4 * count * MEM * LEN * D, bytes_accessed=2 * count * LEN * D,
-            transcendentals=count * CH * MEM * LEN,
+            flops=4 * MEM * LEN * D, bytes_accessed=2 * LEN * D, transcendentals=CH * MEM * LEN
         ),
         name="pool",
     )(states, queries, gain.reshape(1, D))
 
 
 def attend_kernel(
-    start_ref, length_ref, q_ref, k_ref, v_ref, own_k_ref, own_v_ref, out_ref,
-    keys, values, key_side, value_side,
+    lanes, half_ref, place_ref, passage_ref, length_ref, q_ref, k_ref, v_ref, own_k_ref, own_v_ref, *rest
 ):
-    first = (pl.program_id(0) == 0) & (pl.program_id(1) == 0)
-    query = pl.program_id(1)
-
-    @pl.when(first)
+    out_ref, keys, values, key_side, value_side = rest[-5:]
+    query = pl.program_id(0)
+
+    @pl.when(query == 0)
     def _():
         key_side[...] = jnp.zeros_like(key_side)
         lane = lax.broadcasted_iota(jnp.int32, (KEYS, LANES), 1)
@@ -89,7 +97,13 @@
             value_side[kind, :, LANES:] = ones
 
     for slot in range(TOPK):
-        start = pl.multiple_of(start_ref[query, slot], MEM)
+        passage = passage_ref[query, slot]
+        if lanes:
+            chip, inside = lax.div(passage, CHIP), lax.rem(passage, CHIP)
+            chip_line, chip_lane = lax.div(chip, lanes), lax.rem(chip, lanes)
+            back = lax.rem(place_ref[0] + lanes - chip_lane, lanes) * LINES
+            passage = (back + lax.rem(place_ref[1] + LINES - chip_line, LINES)) * CHIP + inside
+        start = pl.multiple_of(passage * MEM, MEM)
         keys[slot * MEM:(slot + 1) * MEM, :] = k_ref[pl.ds(start, MEM), :].astype(jnp.float32)
         values[slot * MEM:(slot + 1) * MEM, :] = v_ref[pl.ds(start, MEM), :].astype(jnp.float32)
     length = length_ref[query]
@@ -171,22 +185,29 @@
         chunk(2, list(range(at, min(at + step, PAIRS))))
 
 
-def attend(starts, lengths, questions, memory_kv, own_kv):
+def attend(lanes, half, place, retrieval, lengths, questions, memory_kv, own_kv, earlier=None):
     count = questions.shape[0]
     total = memory_kv.shape[0]
+    operands = [half.reshape(1), place, retrieval, lengths, questions, memory_kv, memory_kv, own_kv, own_kv]
+    in_specs = [
+        pl.BlockSpec((1, QLEN, HALF), lambda q, h, *_: (q, 0, h[0])),
+        pl.BlockSpec((total, LANES), lambda q, h, *_: (0, 0)),
+        pl.BlockSpec((total, LANES), lambda q, h, *_: (0, 1)),
+        pl.BlockSpec((1, QLEN, LANES), lambda q, h, *_: (q, 0, h[0])),
+        pl.BlockSpec((1, QLEN, LANES), lambda q, h, *_: (q, 0, 2 + h[0])),
+    ]
+    aliases = {}
+    if earlier is not None:
+        aliases = {len(operands): 0}
+        operands.append(earlier)
+        in_specs.append(pl.BlockSpec(memory_space=pl.ANY))
     return pl.pallas_call(
-        attend_kernel,
+        functools.partial(attend_kernel, lanes),
         grid_spec=pltpu.PrefetchScalarGridSpec(
-            num_scalar_prefetch=2,
-            grid=(2, count),
-            in_specs=[
-                pl.BlockSpec((1, QLEN, HALF), lambda c, q, *_: (q, 0, c)),
-                pl.BlockSpec((total, LANES), lambda c, q, *_: (0, c)),
-                pl.BlockSpec((total, LANES), lambda c, q, *_: (0, 2 + c)),
-                pl.BlockSpec((1, QLEN, LANES), lambda c, q, *_: (q, 0, c)),
-                pl.BlockSpec((1, QLEN, LANES), lambda c, q, *_: (q, 0, 2 + c)),
-            ],
-            out_specs=pl.BlockSpec((1, QLEN, HALF), lambda c, q, *_: (q, 0, c)),
+            num_scalar_prefetch=4,
+            grid=(count,),
+            in_specs=in_specs,
+            out_specs=pl.BlockSpec((1, QLEN, HALF), lambda q, h, *_: (q, 0, h[0])),
             scratch_shapes=[
                 pltpu.VMEM((ROWS, LANES), jnp.float32),
                 pltpu.VMEM((ROWS, LANES), jnp.float32),
@@ -195,17 +216,57 @@
             ],
         ),
         out_shape=jax.ShapeDtypeStruct((count, QLEN, H * HD), jnp.bfloat16),
-        compiler_params=pltpu.CompilerParams(vmem_limit_bytes=VMEM_LIMIT),
+        input_output_aliases=aliases,
+        compiler_params=pltpu.CompilerParams(vmem_limit_bytes=36 * MIB),
         cost_estimate=pl.CostEstimate(
-            flops=4 * count * QLEN * H * HD * (ROWS + QLEN),
-            bytes_accessed=4 * count * QLEN * H * HD + 2 * total * KVW,
-            transcendentals=count * QLEN * H * (ROWS + QLEN),
+            flops=2 * count * QLEN * H * HD * (ROWS + QLEN),
+            bytes_accessed=2 * count * QLEN * H * HD + total * KVW,
+            transcendentals=count * QLEN * H * (ROWS + QLEN) // 2,
         ),
         name="attend",
-    )(starts, lengths, questions, memory_kv, memory_kv, own_kv, own_kv)
+    )(*operands)
+
+
+def project_kernel(lanes, passages, core_ref, place_ref, *rest):
+    own, other, weights, out_ref = rest[:passages], rest[passages:2 * passages], rest[2 * passages:-1], rest[-1]
+    count = passages * MEM
+    depth = weights[0].shape[0] // 2
+    total = jnp.zeros((2 * count, weights[0].shape[1]), jnp.float32)
+    core = core_ref[0]
+    for i, weight in enumerate(weights):
+        line = lax.rem(place_ref[1] + LINES - i % LINES, LINES)
+        chip = line * lanes + lax.rem(place_ref[0] + lanes - i // LINES, lanes)
+        for part in range(2):
+            at = pl.multiple_of((2 * chip + (1 - core if part else core)) * depth, depth)
+            rows = jnp.concatenate([x[:, pl.ds(at, depth)] for x in own + other], axis=0)
+            total += jnp.dot(
+                rows, weight[part * depth:(part + 1) * depth], preferred_element_type=jnp.float32
+            )
+    result = total.astype(jnp.bfloat16)
+    out_ref[pl.ds(pl.multiple_of(core * count, count), count)] = result[:count]
+    out_ref[pl.ds(pl.multiple_of((1 - core) * count, count), count)] = result[count:]
+
+
+def project(lanes, core, place, own_rows, other_rows, weights):
+    passages = len(own_rows)
+    width = weights[0].shape[1]
+    vmem = pl.BlockSpec(memory_space=pltpu.VMEM)
+    smem = pl.BlockSpec(memory_space=pltpu.SMEM)
+    return pl.pallas_call(
+        functools.partial(project_kernel, lanes, passages),
+        in_specs=[smem, smem] + [vmem] * (2 * passages + len(weights)),
+        out_specs=vmem,
+        out_shape=jax.ShapeDtypeStruct((2 * passages * MEM, width), jnp.bfloat16),
+        compiler_params=pltpu.CompilerParams(vmem_limit_bytes=16 * MIB),
+        cost_estimate=pl.CostEstimate(
+            flops=4 * passages * MEM * D * width, bytes_accessed=2 * D * width, transcendentals=0
+        ),
+        name="project",
+    )(core.reshape(1), place, *own_rows, *other_rows, *weights)
 
 
 def local(
+    extent,
     passage_states,
     memory_queries,
     memory_gain,
@@ -215,15 +276,64 @@
     question_kv,
     question_lengths,
 ):
+    lines, lanes = LINES, extent // (2 * LINES)
     own_count = passage_states.shape[0]
-    whole_weight = lax.all_gather(kv_weight, "pass", axis=0, tiled=True)
-    memory_rows = pool(passage_states, memory_queries, memory_gain)
-    projected = jnp.dot(
-        memory_rows.reshape(own_count * MEM, D), whole_weight, preferred_element_type=jnp.float32
-    )
-    memory_kv = projected.astype(jnp.bfloat16)
-    everything = lax.all_gather(memory_kv, "pass", axis=0, tiled=True)
-    return attend(retrieval * MEM, question_lengths, question_queries, everything, question_kv)
+    depth = kv_weight.shape[0]
+    me = lax.axis_index("pass")
+    core = me & 1
+    place = jnp.stack([lax.rem(lax.div(me, 2), lanes), lax.div(me, 2 * lanes)])
+
+    def number(a, b, c):
+        return ((a % lines) * lanes + b % lanes) * 2 + c
+
+    every = [(a, b, c) for a in range(lines) for b in range(lanes) for c in range(2)]
+
+    def to_partner(x):
+        return lax.ppermute(x, "pass", [(number(a, b, c), number(a, b, 1 - c)) for a, b, c in every])
+
+    def along_line(x, k):
+        return lax.ppermute(x, "pass", [(number(a, b, c), number(a + k, b, c)) for a, b, c in every])
+
+    def along_lane(x, j):
+        return lax.ppermute(x, "pass", [(number(a, b, c), number(a, b + j, c)) for a, b, c in every])
+
+    def along_lines(block):
+        return [block] + [along_line(block, k) for k in range(1, lines)]
+
+    def all_chips(blocks):
+        return blocks + [along_lane(x, j) for j in range(1, lanes) for x in blocks]
+
+    if depth % LANES:
+        memory_rows = [pool(passage_states, memory_queries, memory_gain, i) for i in range(own_count)]
+        whole_weight = lax.all_gather(kv_weight, "pass", axis=0, tiled=True)
+        memory_kv = jnp.dot(jnp.concatenate(memory_rows, axis=0), whole_weight, preferred_element_type=jnp.float32)
+        everything = lax.all_gather(memory_kv.astype(jnp.bfloat16), "pass", axis=0, tiled=True)
+        halves = everything.reshape(-1, 2, 2, LANES).transpose(2, 0, 1, 3).reshape(2, -1, 2 * LANES)
+        first, second = jnp.int32(0), jnp.int32(1)
+        rest = (place, retrieval, question_lengths, question_queries)
+        context = attend(0, first, *rest, halves[0], question_kv)
+        return attend(0, second, *rest, halves[1], question_kv, context)
+
+    def columns(half):
+        return jnp.concatenate(
+            [
+                lax.dynamic_slice_in_dim(kv_weight, half * LANES + at, LANES, axis=1)
+                for at in (0, KVH * HD)
+            ],
+            axis=1,
+        )
+
+    weight = jnp.concatenate([columns(core), to_partner(columns(1 - core))], axis=0)
+    weight, memory_queries = lax.optimization_barrier((weight, memory_queries))
+    weights = all_chips(along_lines(weight))
+    memory_rows = [pool(passage_states, memory_queries, memory_gain, i) for i in range(own_count)]
+    memory_kv = project(lanes, core, place, memory_rows, [to_partner(x) for x in memory_rows], weights)
+    near = jnp.concatenate(all_chips(along_lines(memory_kv)), axis=0)
+    far = to_partner(near)
+
+    rest = (place, retrieval, question_lengths, question_queries)
+    context = attend(lanes, core, *rest, near, question_kv)
+    return attend(lanes, 1 - core, *rest, far, question_kv, context)
 
 
 def solution(mesh):
@@ -238,7 +348,7 @@
         P(("groups", "pass")),
     )
     return jax.shard_map(
-        local,
+        functools.partial(local, mesh.shape["pass"]),
         mesh=mesh,
         in_specs=placed,
         out_specs=P(("groups", "pass"), None, None),

time: 147 us -> 106 us (0.72)
  Pallas kernels: 76.2 us -> 41.8 us
  starting transfers between devices: 0.04 us -> 22.7 us
  waiting for transfers between devices: 51.9 us -> 36.1 us
  between operations: 13.4 us -> 0.21 us
  matrix products: 3.62 us -> 0 us
  local copies, waits for them, and re-layouts: 1.66 us -> 4.9 us
    all_gather x2 -> x0, waiting for transfers between devices: 51.2 us -> none  [the longest x1 40 us: local(): everything = lax.all_gather(memory_kv, 'pass', axis=0, tiled=True)]
    ppermute x0 -> x20, waiting for transfers between devices: none -> 36.1 us  [the longest x6 20.6 us: along_line(): lax.ppermute(x, 'pass', [(number(a, b, c), number(a + k, b, c)) for a, b,...]
    pallas_call x2 -> x7, Pallas kernels: 76.2 us -> 41.8 us  [the longest x2 34.5 us: attend(): pl.pallas_call(functools.partial(attend_kernel, lanes), grid_spec=pltpu.P...]
    ppermute x0 -> x20, starting transfers between devices: none -> 22.7 us  [the longest x8 8.48 us: along_lane(): lax.ppermute(x, 'pass', [(number(a, b, c), number(a, b + j, c)) for a, b,...]
    dot_general x1 -> x0, matrix products: 3.62 us -> none  [local(): jnp.dot(memory_rows.reshape(own_count * MEM, D), whole_weight, preferred_...]
    unnamed x8 -> x19, local copies, waits for them, and re-layouts: 0.96 us -> 3.23 us
  transfers between devices with their start and end apart: 2 -> 20, of which waited for: 2 -> 8; matrix products, arithmetic and copies ran while one was open for 0% -> 1% of each run, Pallas kernels for 29% -> 20%
where the time goes in v2:
time: 106 us
  Pallas kernels  41.8 us (39%)
  waiting for transfers between devices  36.1 us (34%)
  starting transfers between devices  22.7 us (21%)
  local copies, waits for them, and re-layouts  4.9 us (5%)
    pallas_call x2, Pallas kernels, attend(): pl.pallas_call(functools.partial(attend_kernel, lanes), grid_spec=pltpu.P...  34.5 us
    ppermute x6, waiting for transfers between devices, along_line(): lax.ppermute(x, 'pass', [(number(a, b, c), number(a + k, b, c)) for a, b,...  20.6 us
    ppermute x8, waiting for transfers between devices, along_lane(): lax.ppermute(x, 'pass', [(number(a, b, c), number(a, b + j, c)) for a, b,...  15 us
    ppermute x8, starting transfers between devices, along_lane(): lax.ppermute(x, 'pass', [(number(a, b, c), number(a, b + j, c)) for a, b,...  8.48 us
    ppermute x6, starting transfers between devices, to_partner(): lax.ppermute(x, 'pass', [(number(a, b, c), number(a, b, 1 - c)) for a, b,...  7.62 us
    ppermute x6, starting transfers between devices, along_line(): lax.ppermute(x, 'pass', [(number(a, b, c), number(a + k, b, c)) for a, b,...  6.64 us
    pallas_call x4, Pallas kernels, pool(): pl.pallas_call(pool_kernel, grid=(1,), in_specs=[pl.BlockSpec((1, LEN, D)...  5.46 us
    unnamed x19, local copies, waits for them, and re-layouts  3.23 us
  transfers between devices with their start and end apart: 20, of which 8 were waited for; matrix products, arithmetic and copies ran while one was open for 1% of the time, Pallas kernels for 20%

profile of v2, /device:TPU:1, one launch (start us, length us, event | category | flops | bytes accessed | tf_op | source)
XLA Modules:
  0.0 105.9 jit_solution(7510744582393627475)
XLA Ops:
  0.0 1.0 constant_dynamic-slice_fusion.3
  1.0 0.1 collective-permute-start
  1.1 0.7 reshape.15.gain_ref
  1.8 0.6 collective-permute-done
  2.4 0.0 copy-start
  2.4 2.2 %copy-done = bf16[4,128,4096]{2,1,0:T(8,128)(2,1)S(1)} copy-done((bf16[4,128,4096]{2,1,0:T(8,128)(2,1)S(1)}, bf16[4,128,4096]{2,1,0:T(8,128)(2,1)}, u32[]{:S(2)}) %copy-start) | copy-done | bytes 4194328
  4.6 0.0 copy-start.1
  4.6 0.9 copy-done.1
  5.6 1.4 %pool.4.rest_0_ = bf16[32,4096]{1,0:T(8,128)(2,1)S(1)} custom-call(bf16[4,128,4096]{2,1,0:T(8,128)(2,1)S(1)} %copy-done, bf16[32,4096]{1,0:T(8,128)(2,1)S(1)} %copy-done.1, bf16[1,4096]{1,0:T(2,128)(2,1)S(1)} %reshape.15.gain_ref), custom_call_target="tpu_custom_call" | custom-call | flops 67108864 | bytes 1048576 | tf_op jit(solution)/shard_map/pool/pallas_call | solution.py:64
  6.9 0.2 collective-permute-start.1
  7.2 1.4 %pool.5.rest_1_ = bf16[32,4096]{1,0:T(8,128)(2,1)S(1)} custom-call(bf16[4,128,4096]{2,1,0:T(8,128)(2,1)S(1)} %copy-done, bf16[32,4096]{1,0:T(8,128)(2,1)S(1)} %copy-done.1, bf16[1,4096]{1,0:T(2,128)(2,1)S(1)} %reshape.15.gain_ref), custom_call_target="tpu_custom_call" | custom-call | flops 67108864 | bytes 1048576 | tf_op jit(solution)/shard_map/pool/pallas_call | solution.py:64
  8.5 0.4 collective-permute-start.2
  9.0 1.4 %pool.6.rest_2_ = bf16[32,4096]{1,0:T(8,128)(2,1)S(1)} custom-call(bf16[4,128,4096]{2,1,0:T(8,128)(2,1)S(1)} %copy-done, bf16[32,4096]{1,0:T(8,128)(2,1)S(1)} %copy-done.1, bf16[1,4096]{1,0:T(2,128)(2,1)S(1)} %reshape.15.gain_ref), custom_call_target="tpu_custom_call" | custom-call | flops 67108864 | bytes 1048576 | tf_op jit(solution)/shard_map/pool/pallas_call | solution.py:64
  10.3 0.2 collective-permute-start.3
  10.5 4.7 %collective-permute-start.7 = (bf16[512,256]{1,0:T(8,128)(2,1)S(1)}, bf16[512,256]{1,0:T(8,128)(2,1)S(1)}, u32[]{:S(2)}, u32[]{:S(2)}) collective-permute-start(bf16[512,256]{1,0:T(8,128)(2,1)S(1)} %pad_maximum_fusion.rest_8_), channel_id=1, source_target_pairs={{0,12},{1,13},{2,14},{3,15},{4,0},{5,1},{6,2},{7,3},{8,4},{9,5},{1... | collective-permute-start | bytes 786440 | tf_op jit(solution)/shard_map/ppermute | solution.py:295
  15.2 0.0 collective-permute-start.6
  15.2 0.0 collective-permute-done.1.rest_4_
  15.2 0.5 collective-permute-start.5
  15.7 1.4 %pool.7.rest_3_ = bf16[32,4096]{1,0:T(8,128)(2,1)S(1)} custom-call(bf16[4,128,4096]{2,1,0:T(8,128)(2,1)S(1)} %copy-done, bf16[32,4096]{1,0:T(8,128)(2,1)S(1)} %copy-done.1, bf16[1,4096]{1,0:T(2,128)(2,1)S(1)} %reshape.15.gain_ref), custom_call_target="tpu_custom_call" | custom-call | flops 67108864 | bytes 1048576 | tf_op jit(solution)/shard_map/pool/pallas_call | solution.py:64
  17.1 0.0 copy-start.4
  17.1 0.0 copy-start.5
  17.1 0.0 collective-permute-done.2.rest_5_
  17.1 1.3 %collective-permute-start.8 = (bf16[512,256]{1,0:T(8,128)(2,1)S(1)}, bf16[512,256]{1,0:T(8,128)(2,1)S(1)}, u32[]{:S(2)}, u32[]{:S(2)}) collective-permute-start(bf16[512,256]{1,0:T(8,128)(2,1)S(1)} %pad_maximum_fusion.rest_8_), channel_id=1, source_target_pairs={{0,2},{1,3},{2,0},{3,1},{4,6},{5,7},{6,4},{7,5},{8,10},{9,11},{10,... | collective-permute-start | bytes 786440 | tf_op jit(solution)/shard_map/ppermute | solution.py:298
  18.4 0.0 collective-permute-done.3.rest_6_
  18.4 1.3 %collective-permute-start.4 = (bf16[32,4096]{1,0:T(8,128)(2,1)S(1)}, bf16[32,4096]{1,0:T(8,128)(2,1)S(1)}, u32[]{:S(2)}, u32[]{:S(2)}) collective-permute-start(bf16[32,4096]{1,0:T(8,128)(2,1)S(1)} %pool.7.rest_3_), channel_id=1, source_target_pairs={{0,1},{1,0},{2,3},{3,2},{4,5},{5,4},{6,7},{7,6},{8,9},{9,8},{10,11... | collective-permute-start | bytes 786440 | tf_op jit(solution)/shard_map/ppermute | solution.py:292
  19.7 1.2 %collective-permute-done.7.rest_11_ = bf16[512,256]{1,0:T(8,128)(2,1)S(1)} collective-permute-done((bf16[512,256]{1,0:T(8,128)(2,1)S(1)}, bf16[512,256]{1,0:T(8,128)(2,1)S(1)}, u32[]{:S(2)}, u32[]{:S(2)}) %collective-permute-start.7) | collective-permute-done | bytes 262176 | tf_op jit(solution)/shard_map/ppermute | solution.py:295
  20.9 1.2 %collective-permute-start.11 = (bf16[512,256]{1,0:T(8,128)(2,1)S(1)}, bf16[512,256]{1,0:T(8,128)(2,1)}, u32[]{:S(2)}, u32[]{:S(2)}) collective-permute-start(bf16[512,256]{1,0:T(8,128)(2,1)S(1)} %collective-permute-done.7.rest_11_), channel_id=1, source_target_pairs={{0,2},{1,3},{2,0},{3,1},{4,6},{5,7},{6,4},{7,5},{8,10},{9,11},{10,... | collective-permute-start | bytes 786440 | tf_op jit(solution)/shard_map/ppermute | solution.py:298
  22.1 15.4 %collective-permute-done.6.rest_10_ = bf16[512,256]{1,0:T(8,128)(2,1)S(1)} collective-permute-done((bf16[512,256]{1,0:T(8,128)(2,1)S(1)}, bf16[512,256]{1,0:T(8,128)(2,1)S(1)}, u32[]{:S(2)}, u32[]{:S(2)}) %collective-permute-start.6) | collective-permute-done | bytes 262176 | tf_op jit(solution)/shard_map/ppermute | solution.py:295
  37.5 1.2 %collective-permute-start.10 = (bf16[512,256]{1,0:T(8,128)(2,1)S(1)}, bf16[512,256]{1,0:T(8,128)(2,1)}, u32[]{:S(2)}, u32[]{:S(2)}) collective-permute-start(bf16[512,256]{1,0:T(8,128)(2,1)S(1)} %collective-permute-done.6.rest_10_), channel_id=1, source_target_pairs={{0,2},{1,3},{2,0},{3,1},{4,6},{5,7},{6,4},{7,5},{8,10},{9,11},{10,... | collective-permute-start | bytes 786440 | tf_op jit(solution)/shard_map/ppermute | solution.py:298
  38.7 0.0 collective-permute-done.5.rest_9_
  38.7 0.3 collective-permute-start.9
  39.0 0.0 copy-start.2
  39.0 0.0 copy-start.3
  39.0 0.1 pad_add_fusion.place_ref
  39.1 0.0 collective-permute-done.4.rest_7_
  39.1 0.0 collective-permute-done.8.rest_12_
  39.1 0.0 collective-permute-done.11.rest_15_
  39.1 5.4 %collective-permute-done.10.rest_14_ = bf16[512,256]{1,0:T(8,128)(2,1)} collective-permute-done((bf16[512,256]{1,0:T(8,128)(2,1)S(1)}, bf16[512,256]{1,0:T(8,128)(2,1)}, u32[]{:S(2)}, u32[]{:S(2)}) %collective-permute-start.10) | collective-permute-done | bytes 262176 | tf_op jit(solution)/shard_map/ppermute | solution.py:298
  44.5 5.6 %collective-permute-done.9.rest_13_ = bf16[512,256]{1,0:T(8,128)(2,1)} collective-permute-done((bf16[512,256]{1,0:T(8,128)(2,1)S(1)}, bf16[512,256]{1,0:T(8,128)(2,1)}, u32[]{:S(2)}, u32[]{:S(2)}) %collective-permute-start.9) | collective-permute-done | bytes 262176 | tf_op jit(solution)/shard_map/ppermute | solution.py:298
  50.1 1.9 %project.1 = bf16[256,256]{1,0:T(8,128)(2,1)S(1)} custom-call(s32[1]{0:T(128)} %bitcast.3.core_ref.half_ref, s32[2]{0:T(128)S(1)} %pad_add_fusion.place_ref, bf16[32,4096]{1,0:T(8,128)(2,1)S(1)} %pool.4.rest_0_, bf16[32,4096]{1,0:T(8,128)(2,1)S(1)} %pool.5.rest_1_, bf16[32,4096]{1,0:T(8,128)(2,1)S(1)} %pool.6.rest_2_, bf16[32,4096]{1,0:T(8,128)(2,1)S(1)} %pool.7.rest_3_, ...), custom_call_target="tpu_custom_call" | custom-call | flops 536870912 | bytes 2097152 | tf_op jit(solution)/shard_map/project/pallas_call | solution.py:255
  52.0 0.1 collective-permute-start.14
  52.0 0.1 collective-permute-start.13
  52.1 1.4 %collective-permute-start.12 = (bf16[256,256]{1,0:T(8,128)(2,1)S(1)}, bf16[256,256]{1,0:T(8,128)(2,1)S(1)}, u32[]{:S(2)}, u32[]{:S(2)}) collective-permute-start(bf16[256,256]{1,0:T(8,128)(2,1)S(1)} %project.1), channel_id=1, source_target_pairs={{0,4},{1,5},{2,6},{3,7},{4,8},{5,9},{6,10},{7,11},{8,12},{9,13},{1... | collective-permute-start | bytes 393224 | tf_op jit(solution)/shard_map/ppermute | solution.py:295
  53.5 1.2 %collective-permute-start.15 = (bf16[256,256]{1,0:T(8,128)(2,1)S(1)}, bf16[256,256]{1,0:T(8,128)(2,1)S(1)}, u32[]{:S(2)}, u32[]{:S(2)}) collective-permute-start(bf16[256,256]{1,0:T(8,128)(2,1)S(1)} %project.1), channel_id=1, source_target_pairs={{0,2},{1,3},{2,0},{3,1},{4,6},{5,7},{6,4},{7,5},{8,10},{9,11},{10,... | collective-permute-start | bytes 393224 | tf_op jit(solution)/shard_map/ppermute | solution.py:298
  54.7 2.1 %collective-permute-done.14 = bf16[256,256]{1,0:T(8,128)(2,1)S(1)} collective-permute-done((bf16[256,256]{1,0:T(8,128)(2,1)S(1)}, bf16[256,256]{1,0:T(8,128)(2,1)S(1)}, u32[]{:S(2)}, u32[]{:S(2)}) %collective-permute-start.14) | collective-permute-done | bytes 131104 | tf_op jit(solution)/shard_map/ppermute | solution.py:295
  56.8 1.2 %collective-permute-start.18 = (bf16[256,256]{1,0:T(8,128)(2,1)S(1)}, bf16[256,256]{1,0:T(8,128)(2,1)S(1)}, u32[]{:S(2)}, u32[]{:S(2)}) collective-permute-start(bf16[256,256]{1,0:T(8,128)(2,1)S(1)} %collective-permute-done.14), channel_id=1, source_target_pairs={{0,2},{1,3},{2,0},{3,1},{4,6},{5,7},{6,4},{7,5},{8,10},{9,11},{10,... | collective-permute-start | bytes 393224 | tf_op jit(solution)/shard_map/ppermute | solution.py:298
  57.9 0.0 collective-permute-done.13
  57.9 1.0 collective-permute-start.17
  58.9 1.8 %collective-permute-done.12 = bf16[256,256]{1,0:T(8,128)(2,1)S(1)} collective-permute-done((bf16[256,256]{1,0:T(8,128)(2,1)S(1)}, bf16[256,256]{1,0:T(8,128)(2,1)S(1)}, u32[]{:S(2)}, u32[]{:S(2)}) %collective-permute-start.12) | collective-permute-done | bytes 131104 | tf_op jit(solution)/shard_map/ppermute | solution.py:295
  60.7 1.2 %collective-permute-start.16 = (bf16[256,256]{1,0:T(8,128)(2,1)S(1)}, bf16[256,256]{1,0:T(8,128)(2,1)S(1)}, u32[]{:S(2)}, u32[]{:S(2)}) collective-permute-start(bf16[256,256]{1,0:T(8,128)(2,1)S(1)} %collective-permute-done.12), channel_id=1, source_target_pairs={{0,2},{1,3},{2,0},{3,1},{4,6},{5,7},{6,4},{7,5},{8,10},{9,11},{10,... | collective-permute-start | bytes 393224 | tf_op jit(solution)/shard_map/ppermute | solution.py:298
  62.0 0.0 collective-permute-done.15
  62.0 4.0 %collective-permute-done.16 = bf16[256,256]{1,0:T(8,128)(2,1)S(1)} collective-permute-done((bf16[256,256]{1,0:T(8,128)(2,1)S(1)}, bf16[256,256]{1,0:T(8,128)(2,1)S(1)}, u32[]{:S(2)}, u32[]{:S(2)}) %collective-permute-start.16) | collective-permute-done | bytes 131104 | tf_op jit(solution)/shard_map/ppermute | solution.py:298
  66.0 0.0 collective-permute-done.17
  66.0 0.0 collective-permute-done.18
  66.0 5.4 %collective-permute-start.19 = (bf16[2048,256]{1,0:T(8,128)(2,1)S(1)}, bf16[2048,256]{1,0:T(8,128)(2,1)S(1)}, u32[]{:S(2)}, u32[]{:S(2)}) collective-permute-start(bf16[2048,256]{1,0:T(8,128)(2,1)S(1)} %constant_dynamic-update-slice_fusion.k_ref.v_ref), channel_id=1, source_target_pairs={{0,1},{1,0},{2,3},{3,2},{4,5},{5,4},{6,7},{7,6},{8,9},{9,8},{10,11... | collective-permute-start | bytes 3145736 | tf_op jit(solution)/shard_map/ppermute | solution.py:292
  71.4 0.0 copy-done.4
  71.4 0.0 copy-done.5
  71.4 0.0 copy-done.2
  71.4 0.0 copy-done.3
  71.4 17.2 %attend.2.rest_0_ = bf16[4,64,7424]{2,1,0:T(8,128)(2,1)} custom-call(s32[1]{0:T(128)} %bitcast.3.core_ref.half_ref, s32[2]{0:T(128)S(1)} %pad_add_fusion.place_ref, s32[4,16]{1,0:T(4,128)S(1)} %copy-done.4, s32[4]{0:T(128)S(1)} %copy-done.5, bf16[4,64,7424]{2,1,0:T(8,128)(2,1)S(1)} %copy-done.2, ...), custom_call_target="tpu_custom_call" | custom-call | flops 2189426688 | bytes 4849664 | tf_op jit(solution)/shard_map/attend/pallas_call | solution.py:204
  88.7 0.0 collective-permute-done.19.k_ref.v_ref
  88.7 17.2 %attend.3 = bf16[4,64,7424]{2,1,0:T(8,128)(2,1)} custom-call(s32[1]{0:T(128)} %bitcast.half_ref, s32[2]{0:T(128)S(1)} %pad_add_fusion.place_ref, s32[4,16]{1,0:T(4,128)S(1)} %copy-done.4, s32[4]{0:T(128)S(1)} %copy-done.5, bf16[4,64,7424]{2,1,0:T(8,128)(2,1)S(1)} %copy-done.2, ...), custom_call_target="tpu_custom_call", output_to_operand_aliasing={{}: (9, {})} | custom-call | flops 2189426688 | bytes 4849664 | tf_op jit(solution)/shard_map/attend/pallas_call | solution.py:204
  (10 shorter events, 0.1 us)
Async XLA Ops:
  1.0 1.4 %collective-permute-start = (bf16[256,256]{1,0:T(8,128)(2,1)S(1)}, bf16[256,256]{1,0:T(8,128)(2,1)S(1)}, u32[]{:S(2)}, u32[]{:S(2)}) collective-permute-start(bf16[256,256]{1,0:T(8,128)(2,1)S(1)} %pad_maximum_fusion.1), channel_id=1, source_target_pairs={{0,1},{1,0},{2,3},{3,2},{4,5},{5,4},{6,7},{7,6},{8,9},{9,8},{10,11... | collective-permute-start | bytes 393224 | tf_op jit(solution)/shard_map/ppermute | solution.py:292
  2.4 2.2 %copy-start = (bf16[4,128,4096]{2,1,0:T(8,128)(2,1)S(1)}, bf16[4,128,4096]{2,1,0:T(8,128)(2,1)}, u32[]{:S(2)}) copy-start(bf16[4,128,4096]{2,1,0:T(8,128)(2,1)} %states_ref.7) | copy-start | bytes 12582916
  4.6 0.9 copy-start.1
  6.9 8.3 %collective-permute-start.1 = (bf16[32,4096]{1,0:T(8,128)(2,1)S(1)}, bf16[32,4096]{1,0:T(8,128)(2,1)S(1)}, u32[]{:S(2)}, u32[]{:S(2)}) collective-permute-start(bf16[32,4096]{1,0:T(8,128)(2,1)S(1)} %pool.4.rest_0_), channel_id=1, source_target_pairs={{0,1},{1,0},{2,3},{3,2},{4,5},{5,4},{6,7},{7,6},{8,9},{9,8},{10,11... | collective-permute-start | bytes 786440 | tf_op jit(solution)/shard_map/ppermute | solution.py:292
  8.5 8.6 %collective-permute-start.2 = (bf16[32,4096]{1,0:T(8,128)(2,1)S(1)}, bf16[32,4096]{1,0:T(8,128)(2,1)S(1)}, u32[]{:S(2)}, u32[]{:S(2)}) collective-permute-start(bf16[32,4096]{1,0:T(8,128)(2,1)S(1)} %pool.5.rest_1_), channel_id=1, source_target_pairs={{0,1},{1,0},{2,3},{3,2},{4,5},{5,4},{6,7},{7,6},{8,9},{9,8},{10,11... | collective-permute-start | bytes 786440 | tf_op jit(solution)/shard_map/ppermute | solution.py:292
  10.3 8.0 %collective-permute-start.3 = (bf16[32,4096]{1,0:T(8,128)(2,1)S(1)}, bf16[32,4096]{1,0:T(8,128)(2,1)S(1)}, u32[]{:S(2)}, u32[]{:S(2)}) collective-permute-start(bf16[32,4096]{1,0:T(8,128)(2,1)S(1)} %pool.6.rest_2_), channel_id=1, source_target_pairs={{0,1},{1,0},{2,3},{3,2},{4,5},{5,4},{6,7},{7,6},{8,9},{9,8},{10,11... | collective-permute-start | bytes 786440 | tf_op jit(solution)/shard_map/ppermute | solution.py:292
  10.5 10.3 %collective-permute-start.7 = (bf16[512,256]{1,0:T(8,128)(2,1)S(1)}, bf16[512,256]{1,0:T(8,128)(2,1)S(1)}, u32[]{:S(2)}, u32[]{:S(2)}) collective-permute-start(bf16[512,256]{1,0:T(8,128)(2,1)S(1)} %pad_maximum_fusion.rest_8_), channel_id=1, source_target_pairs={{0,12},{1,13},{2,14},{3,15},{4,0},{5,1},{6,2},{7,3},{8,4},{9,5},{1... | collective-permute-start | bytes 786440 | tf_op jit(solution)/shard_map/ppermute | solution.py:295
  15.2 22.3 %collective-permute-start.6 = (bf16[512,256]{1,0:T(8,128)(2,1)S(1)}, bf16[512,256]{1,0:T(8,128)(2,1)S(1)}, u32[]{:S(2)}, u32[]{:S(2)}) collective-permute-start(bf16[512,256]{1,0:T(8,128)(2,1)S(1)} %pad_maximum_fusion.rest_8_), channel_id=1, source_target_pairs={{0,8},{1,9},{2,10},{3,11},{4,12},{5,13},{6,14},{7,15},{8,0},{9,1},... | collective-permute-start | bytes 786440 | tf_op jit(solution)/shard_map/ppermute | solution.py:295
  15.2 23.5 %collective-permute-start.5 = (bf16[512,256]{1,0:T(8,128)(2,1)S(1)}, bf16[512,256]{1,0:T(8,128)(2,1)S(1)}, u32[]{:S(2)}, u32[]{:S(2)}) collective-permute-start(bf16[512,256]{1,0:T(8,128)(2,1)S(1)} %pad_maximum_fusion.rest_8_), channel_id=1, source_target_pairs={{0,4},{1,5},{2,6},{3,7},{4,8},{5,9},{6,10},{7,11},{8,12},{9,13},{1... | collective-permute-start | bytes 786440 | tf_op jit(solution)/shard_map/ppermute | solution.py:295
  17.1 54.3 %copy-start.4 = (s32[4,16]{1,0:T(4,128)S(1)}, s32[4,16]{1,0:T(4,128)}, u32[]{:S(2)}) copy-start(s32[4,16]{1,0:T(4,128)} %passage_ref.3) | copy-start | bytes 772
  17.1 54.3 %copy-start.5 = (s32[4]{0:T(128)S(1)}, s32[4]{0:T(128)}, u32[]{:S(2)}) copy-start(s32[4]{0:T(128)} %length_ref.3) | copy-start | bytes 52
  17.1 22.0 %collective-permute-start.8 = (bf16[512,256]{1,0:T(8,128)(2,1)S(1)}, bf16[512,256]{1,0:T(8,128)(2,1)S(1)}, u32[]{:S(2)}, u32[]{:S(2)}) collective-permute-start(bf16[512,256]{1,0:T(8,128)(2,1)S(1)} %pad_maximum_fusion.rest_8_), channel_id=1, source_target_pairs={{0,2},{1,3},{2,0},{3,1},{4,6},{5,7},{6,4},{7,5},{8,10},{9,11},{10,... | collective-permute-start | bytes 786440 | tf_op jit(solution)/shard_map/ppermute | solution.py:298
  18.4 20.7 %collective-permute-start.4 = (bf16[32,4096]{1,0:T(8,128)(2,1)S(1)}, bf16[32,4096]{1,0:T(8,128)(2,1)S(1)}, u32[]{:S(2)}, u32[]{:S(2)}) collective-permute-start(bf16[32,4096]{1,0:T(8,128)(2,1)S(1)} %pool.7.rest_3_), channel_id=1, source_target_pairs={{0,1},{1,0},{2,3},{3,2},{4,5},{5,4},{6,7},{7,6},{8,9},{9,8},{10,11... | collective-permute-start | bytes 786440 | tf_op jit(solution)/shard_map/ppermute | solution.py:292
  20.9 18.2 %collective-permute-start.11 = (bf16[512,256]{1,0:T(8,128)(2,1)S(1)}, bf16[512,256]{1,0:T(8,128)(2,1)}, u32[]{:S(2)}, u32[]{:S(2)}) collective-permute-start(bf16[512,256]{1,0:T(8,128)(2,1)S(1)} %collective-permute-done.7.rest_11_), channel_id=1, source_target_pairs={{0,2},{1,3},{2,0},{3,1},{4,6},{5,7},{6,4},{7,5},{8,10},{9,11},{10,... | collective-permute-start | bytes 786440 | tf_op jit(solution)/shard_map/ppermute | solution.py:298
  37.5 7.0 %collective-permute-start.10 = (bf16[512,256]{1,0:T(8,128)(2,1)S(1)}, bf16[512,256]{1,0:T(8,128)(2,1)}, u32[]{:S(2)}, u32[]{:S(2)}) collective-permute-start(bf16[512,256]{1,0:T(8,128)(2,1)S(1)} %collective-permute-done.6.rest_10_), channel_id=1, source_target_pairs={{0,2},{1,3},{2,0},{3,1},{4,6},{5,7},{6,4},{7,5},{8,10},{9,11},{10,... | collective-permute-start | bytes 786440 | tf_op jit(solution)/shard_map/ppermute | solution.py:298
  38.7 11.4 %collective-permute-start.9 = (bf16[512,256]{1,0:T(8,128)(2,1)S(1)}, bf16[512,256]{1,0:T(8,128)(2,1)}, u32[]{:S(2)}, u32[]{:S(2)}) collective-permute-start(bf16[512,256]{1,0:T(8,128)(2,1)S(1)} %collective-permute-done.5.rest_9_), channel_id=1, source_target_pairs={{0,2},{1,3},{2,0},{3,1},{4,6},{5,7},{6,4},{7,5},{8,10},{9,11},{10,... | collective-permute-start | bytes 786440 | tf_op jit(solution)/shard_map/ppermute | solution.py:298
  39.0 32.4 %copy-start.2 = (bf16[4,64,7424]{2,1,0:T(8,128)(2,1)S(1)}, bf16[4,64,7424]{2,1,0:T(8,128)(2,1)}, u32[]{:S(2)}) copy-start(bf16[4,64,7424]{2,1,0:T(8,128)(2,1)} %q_ref.3) | copy-start | bytes 11403268
  39.0 32.4 %copy-start.3 = (bf16[4,64,512]{2,1,0:T(8,128)(2,1)S(1)}, bf16[4,64,512]{2,1,0:T(8,128)(2,1)}, u32[]{:S(2)}) copy-start(bf16[4,64,512]{2,1,0:T(8,128)(2,1)} %own_v_ref.3) | copy-start | bytes 786436
  52.0 4.8 %collective-permute-start.14 = (bf16[256,256]{1,0:T(8,128)(2,1)S(1)}, bf16[256,256]{1,0:T(8,128)(2,1)S(1)}, u32[]{:S(2)}, u32[]{:S(2)}) collective-permute-start(bf16[256,256]{1,0:T(8,128)(2,1)S(1)} %project.1), channel_id=1, source_target_pairs={{0,12},{1,13},{2,14},{3,15},{4,0},{5,1},{6,2},{7,3},{8,4},{9,5},{1... | collective-permute-start | bytes 393224 | tf_op jit(solution)/shard_map/ppermute | solution.py:295
  52.0 5.9 %collective-permute-start.13 = (bf16[256,256]{1,0:T(8,128)(2,1)S(1)}, bf16[256,256]{1,0:T(8,128)(2,1)S(1)}, u32[]{:S(2)}, u32[]{:S(2)}) collective-permute-start(bf16[256,256]{1,0:T(8,128)(2,1)S(1)} %project.1), channel_id=1, source_target_pairs={{0,8},{1,9},{2,10},{3,11},{4,12},{5,13},{6,14},{7,15},{8,0},{9,1},... | collective-permute-start | bytes 393224 | tf_op jit(solution)/shard_map/ppermute | solution.py:295
  52.1 8.6 %collective-permute-start.12 = (bf16[256,256]{1,0:T(8,128)(2,1)S(1)}, bf16[256,256]{1,0:T(8,128)(2,1)S(1)}, u32[]{:S(2)}, u32[]{:S(2)}) collective-permute-start(bf16[256,256]{1,0:T(8,128)(2,1)S(1)} %project.1), channel_id=1, source_target_pairs={{0,4},{1,5},{2,6},{3,7},{4,8},{5,9},{6,10},{7,11},{8,12},{9,13},{1... | collective-permute-start | bytes 393224 | tf_op jit(solution)/shard_map/ppermute | solution.py:295
  53.5 8.5 %collective-permute-start.15 = (bf16[256,256]{1,0:T(8,128)(2,1)S(1)}, bf16[256,256]{1,0:T(8,128)(2,1)S(1)}, u32[]{:S(2)}, u32[]{:S(2)}) collective-permute-start(bf16[256,256]{1,0:T(8,128)(2,1)S(1)} %project.1), channel_id=1, source_target_pairs={{0,2},{1,3},{2,0},{3,1},{4,6},{5,7},{6,4},{7,5},{8,10},{9,11},{10,... | collective-permute-start | bytes 393224 | tf_op jit(solution)/shard_map/ppermute | solution.py:298
  56.8 9.3 %collective-permute-start.18 = (bf16[256,256]{1,0:T(8,128)(2,1)S(1)}, bf16[256,256]{1,0:T(8,128)(2,1)S(1)}, u32[]{:S(2)}, u32[]{:S(2)}) collective-permute-start(bf16[256,256]{1,0:T(8,128)(2,1)S(1)} %collective-permute-done.14), channel_id=1, source_target_pairs={{0,2},{1,3},{2,0},{3,1},{4,6},{5,7},{6,4},{7,5},{8,10},{9,11},{10,... | collective-permute-start | bytes 393224 | tf_op jit(solution)/shard_map/ppermute | solution.py:298
  57.9 8.0 %collective-permute-start.17 = (bf16[256,256]{1,0:T(8,128)(2,1)S(1)}, bf16[256,256]{1,0:T(8,128)(2,1)S(1)}, u32[]{:S(2)}, u32[]{:S(2)}) collective-permute-start(bf16[256,256]{1,0:T(8,128)(2,1)S(1)} %collective-permute-done.13), channel_id=1, source_target_pairs={{0,2},{1,3},{2,0},{3,1},{4,6},{5,7},{6,4},{7,5},{8,10},{9,11},{10,... | collective-permute-start | bytes 393224 | tf_op jit(solution)/shard_map/ppermute | solution.py:298
  60.7 5.2 %collective-permute-start.16 = (bf16[256,256]{1,0:T(8,128)(2,1)S(1)}, bf16[256,256]{1,0:T(8,128)(2,1)S(1)}, u32[]{:S(2)}, u32[]{:S(2)}) collective-permute-start(bf16[256,256]{1,0:T(8,128)(2,1)S(1)} %collective-permute-done.12), channel_id=1, source_target_pairs={{0,2},{1,3},{2,0},{3,1},{4,6},{5,7},{6,4},{7,5},{8,10},{9,11},{10,... | collective-permute-start | bytes 393224 | tf_op jit(solution)/shard_map/ppermute | solution.py:298
  66.0 22.6 %collective-permute-start.19 = (bf16[2048,256]{1,0:T(8,128)(2,1)S(1)}, bf16[2048,256]{1,0:T(8,128)(2,1)S(1)}, u32[]{:S(2)}, u32[]{:S(2)}) collective-permute-start(bf16[2048,256]{1,0:T(8,128)(2,1)S(1)} %constant_dynamic-update-slice_fusion.k_ref.v_ref), channel_id=1, source_target_pairs={{0,1},{1,0},{2,3},{3,2},{4,5},{5,4},{6,7},{7,6},{8,9},{9,8},{10,11... | collective-permute-start | bytes 3145736 | tf_op jit(solution)/shard_map/ppermute | solution.py:292

commit v3 on v2

--- a/solution.py
+++ b/solution.py
@@ -28,9 +28,19 @@
 KEYS = 2 * (ROWS + QLEN)
 NEG = -1e30
 POOL_HEADS = 16
-LINES = 4
 CHIP = 8
 MIB = 1024 * 1024
+
+
+def place_of(chip, ring):
+    line, lane = lax.div(chip, 2), lax.rem(chip, 2)
+    return line + lane * (ring - 1 - 2 * line)
+
+
+def chip_at(place, ring):
+    lane = lax.div(place, ring // 2)
+    line = place + lane * (ring - 1 - 2 * place)
+    return 2 * line + lane
 
 
 def pool_kernel(states_ref, queries_ref, gain_ref, out_ref, pooled):
@@ -60,28 +70,30 @@
     out_ref[...] = (pooled[...] * scale * gain_ref[...].astype(jnp.float32)).astype(jnp.bfloat16)
 
 
-def pool(states, queries, gain, passage):
+def pool(states, queries, gain):
+    count = states.shape[0]
     return pl.pallas_call(
         pool_kernel,
-        grid=(1,),
+        grid=(count,),
         in_specs=[
-            pl.BlockSpec((1, LEN, D), lambda _: (passage, 0, 0)),
-            pl.BlockSpec((MEM, D), lambda _: (0, 0)),
-            pl.BlockSpec((1, D), lambda _: (0, 0)),
+            pl.BlockSpec((1, LEN, D), lambda p: (p, 0, 0)),
+            pl.BlockSpec((MEM, D), lambda p: (0, 0)),
+            pl.BlockSpec((1, D), lambda p: (0, 0)),
         ],
-        out_specs=pl.BlockSpec((MEM, D), lambda _: (0, 0)),
-        out_shape=jax.ShapeDtypeStruct((MEM, D), jnp.bfloat16),
+        out_specs=pl.BlockSpec((MEM, D), lambda p: (p, 0)),
+        out_shape=jax.ShapeDtypeStruct((count * MEM, D), jnp.bfloat16),
         scratch_shapes=[pltpu.VMEM((MEM, D), jnp.float32)],
         compiler_params=pltpu.CompilerParams(vmem_limit_bytes=16 * MIB),
         cost_estimate=pl.CostEstimate(
-            flops=4 * MEM * LEN * D, bytes_accessed=2 * LEN * D, transcendentals=CH * MEM * LEN
+            flops=4 * count * MEM * LEN * D, bytes_accessed=2 * count * LEN * D,
+            transcendentals=count * CH * MEM * LEN,
         ),
         name="pool",
     )(states, queries, gain.reshape(1, D))
 
 
 def attend_kernel(
-    lanes, half_ref, place_ref, passage_ref, length_ref, q_ref, k_ref, v_ref, own_k_ref, own_v_ref, *rest
+    ring, half_ref, place_ref, passage_ref, length_ref, q_ref, k_ref, v_ref, own_k_ref, own_v_ref, *rest
 ):
     out_ref, keys, values, key_side, value_side = rest[-5:]
     query = pl.program_id(0)
@@ -98,11 +110,9 @@
 
     for slot in range(TOPK):
         passage = passage_ref[query, slot]
-        if lanes:
+        if ring:
             chip, inside = lax.div(passage, CHIP), lax.rem(passage, CHIP)
-            chip_line, chip_lane = lax.div(chip, lanes), lax.rem(chip, lanes)
-            back = lax.rem(place_ref[0] + lanes - chip_lane, lanes) * LINES
-            passage = (back + lax.rem(place_ref[1] + LINES - chip_line, LINES)) * CHIP + inside
+            passage = lax.rem(ring + place_ref[0] - place_of(chip, ring), ring) * CHIP + inside
         start = pl.multiple_of(passage * MEM, MEM)
         keys[slot * MEM:(slot + 1) * MEM, :] = k_ref[pl.ds(start, MEM), :].astype(jnp.float32)
         values[slot * MEM:(slot + 1) * MEM, :] = v_ref[pl.ds(start, MEM), :].astype(jnp.float32)
@@ -185,7 +195,7 @@
         chunk(2, list(range(at, min(at + step, PAIRS))))
 
 
-def attend(lanes, half, place, retrieval, lengths, questions, memory_kv, own_kv, earlier=None):
+def attend(ring, half, place, retrieval, lengths, questions, memory_kv, own_kv, earlier=None):
     count = questions.shape[0]
     total = memory_kv.shape[0]
     operands = [half.reshape(1), place, retrieval, lengths, questions, memory_kv, memory_kv, own_kv, own_kv]
@@ -202,7 +212,7 @@
         operands.append(earlier)
         in_specs.append(pl.BlockSpec(memory_space=pl.ANY))
     return pl.pallas_call(
-        functools.partial(attend_kernel, lanes),
+        functools.partial(attend_kernel, ring),
         grid_spec=pltpu.PrefetchScalarGridSpec(
             num_scalar_prefetch=4,
             grid=(count,),
@@ -227,18 +237,17 @@
     )(*operands)
 
 
-def project_kernel(lanes, passages, core_ref, place_ref, *rest):
-    own, other, weights, out_ref = rest[:passages], rest[passages:2 * passages], rest[2 * passages:-1], rest[-1]
-    count = passages * MEM
+def project_kernel(ring, core_ref, place_ref, own_ref, other_ref, *rest):
+    weights, out_ref = rest[:-1], rest[-1]
+    count = own_ref.shape[0]
     depth = weights[0].shape[0] // 2
     total = jnp.zeros((2 * count, weights[0].shape[1]), jnp.float32)
     core = core_ref[0]
     for i, weight in enumerate(weights):
-        line = lax.rem(place_ref[1] + LINES - i % LINES, LINES)
-        chip = line * lanes + lax.rem(place_ref[0] + lanes - i // LINES, lanes)
+        chip = chip_at(lax.rem(ring + place_ref[0] - i, ring), ring)
         for part in range(2):
             at = pl.multiple_of((2 * chip + (1 - core if part else core)) * depth, depth)
-            rows = jnp.concatenate([x[:, pl.ds(at, depth)] for x in own + other], axis=0)
+            rows = jnp.concatenate([own_ref[:, pl.ds(at, depth)], other_ref[:, pl.ds(at, depth)]], axis=0)
             total += jnp.dot(
                 rows, weight[part * depth:(part + 1) * depth], preferred_element_type=jnp.float32
             )
@@ -247,22 +256,22 @@
     out_ref[pl.ds(pl.multiple_of((1 - core) * count, count), count)] = result[count:]
 
 
-def project(lanes, core, place, own_rows, other_rows, weights):
-    passages = len(own_rows)
+def project(core, place, own_rows, other_rows, weights):
+    count = own_rows.shape[0]
     width = weights[0].shape[1]
     vmem = pl.BlockSpec(memory_space=pltpu.VMEM)
     smem = pl.BlockSpec(memory_space=pltpu.SMEM)
     return pl.pallas_call(
-        functools.partial(project_kernel, lanes, passages),
-        in_specs=[smem, smem] + [vmem] * (2 * passages + len(weights)),
+        functools.partial(project_kernel, len(weights)),
+        in_specs=[smem, smem] + [vmem] * (2 + len(weights)),
         out_specs=vmem,
-        out_shape=jax.ShapeDtypeStruct((2 * passages * MEM, width), jnp.bfloat16),
+        out_shape=jax.ShapeDtypeStruct((2 * count, width), jnp.bfloat16),
         compiler_params=pltpu.CompilerParams(vmem_limit_bytes=16 * MIB),
         cost_estimate=pl.CostEstimate(
-            flops=4 * passages * MEM * D * width, bytes_accessed=2 * D * width, transcendentals=0
+            flops=4 * count * D * width, bytes_accessed=2 * D * width, transcendentals=0
         ),
         name="project",
-    )(core.reshape(1), place, *own_rows, *other_rows, *weights)
+    )(core.reshape(1), place, own_rows, other_rows, *weights)
 
 
 def local(
@@ -276,43 +285,38 @@
     question_kv,
     question_lengths,
 ):
-    lines, lanes = LINES, extent // (2 * LINES)
-    own_count = passage_states.shape[0]
+    me = lax.axis_index("pass")
+    core, chip = me & 1, lax.div(me, 2)
+    chips = extent // 2
     depth = kv_weight.shape[0]
-    me = lax.axis_index("pass")
-    core = me & 1
-    place = jnp.stack([lax.rem(lax.div(me, 2), lanes), lax.div(me, 2 * lanes)])
-
-    def number(a, b, c):
-        return ((a % lines) * lanes + b % lanes) * 2 + c
-
-    every = [(a, b, c) for a in range(lines) for b in range(lanes) for c in range(2)]
-
-    def to_partner(x):
-        return lax.ppermute(x, "pass", [(number(a, b, c), number(a, b, 1 - c)) for a, b, c in every])
-
-    def along_line(x, k):
-        return lax.ppermute(x, "pass", [(number(a, b, c), number(a + k, b, c)) for a, b, c in every])
-
-    def along_lane(x, j):
-        return lax.ppermute(x, "pass", [(number(a, b, c), number(a, b + j, c)) for a, b, c in every])
-
-    def along_lines(block):
-        return [block] + [along_line(block, k) for k in range(1, lines)]
-
-    def all_chips(blocks):
-        return blocks + [along_lane(x, j) for j in range(1, lanes) for x in blocks]
-
-    if depth % LANES:
-        memory_rows = [pool(passage_states, memory_queries, memory_gain, i) for i in range(own_count)]
+
+    if chips != 8 or depth % LANES:
+        memory_rows = pool(passage_states, memory_queries, memory_gain)
         whole_weight = lax.all_gather(kv_weight, "pass", axis=0, tiled=True)
-        memory_kv = jnp.dot(jnp.concatenate(memory_rows, axis=0), whole_weight, preferred_element_type=jnp.float32)
+        memory_kv = jnp.dot(memory_rows, whole_weight, preferred_element_type=jnp.float32)
         everything = lax.all_gather(memory_kv.astype(jnp.bfloat16), "pass", axis=0, tiled=True)
         halves = everything.reshape(-1, 2, 2, LANES).transpose(2, 0, 1, 3).reshape(2, -1, 2 * LANES)
-        first, second = jnp.int32(0), jnp.int32(1)
-        rest = (place, retrieval, question_lengths, question_queries)
-        context = attend(0, first, *rest, halves[0], question_kv)
-        return attend(0, second, *rest, halves[1], question_kv, context)
+        rest = (jnp.zeros((1,), jnp.int32), retrieval, question_lengths, question_queries)
+        context = attend(0, jnp.int32(0), *rest, halves[0], question_kv)
+        return attend(0, jnp.int32(1), *rest, halves[1], question_kv, context)
+
+    place = place_of(chip, chips).reshape(1)
+    order = [2 * line for line in range(chips // 2)] + [2 * line + 1 for line in range(chips // 2)][::-1]
+
+    def to_partner(x):
+        return lax.ppermute(x, "pass", [(i, i ^ 1) for i in range(extent)])
+
+    def along_ring(x, step):
+        pairs = [(order[p], order[(p + step) % chips]) for p in range(chips)]
+        return lax.ppermute(x, "pass", [(2 * s + c, 2 * d + c) for s, d in pairs for c in range(2)])
+
+    def all_chips(block):
+        up, down = [block], [block]
+        for i in range(1, chips // 2 + 1):
+            up.append(along_ring(up[-1], 1))
+            if i < chips // 2:
+                down.append(along_ring(down[-1], -1))
+        return up + down[:0:-1]
 
     def columns(half):
         return jnp.concatenate(
@@ -325,15 +329,15 @@
 
     weight = jnp.concatenate([columns(core), to_partner(columns(1 - core))], axis=0)
     weight, memory_queries = lax.optimization_barrier((weight, memory_queries))
-    weights = all_chips(along_lines(weight))
-    memory_rows = [pool(passage_states, memory_queries, memory_gain, i) for i in range(own_count)]
-    memory_kv = project(lanes, core, place, memory_rows, [to_partner(x) for x in memory_rows], weights)
-    near = jnp.concatenate(all_chips(along_lines(memory_kv)), axis=0)
+    weights = all_chips(weight)
+    memory_rows = pool(passage_states, memory_queries, memory_gain)
+    memory_kv = project(core, place, memory_rows, to_partner(memory_rows), weights)
+    near = jnp.concatenate(all_chips(memory_kv), axis=0)
     far = to_partner(near)
 
     rest = (place, retrieval, question_lengths, question_queries)
-    context = attend(lanes, core, *rest, near, question_kv)
-    return attend(lanes, 1 - core, *rest, far, question_kv, context)
+    context = attend(chips, core, *rest, near, question_kv)
+    return attend(chips, 1 - core, *rest, far, question_kv, context)
 
 
 def solution(mesh):

time: 106 us -> 97.6 us (0.921)
  waiting for transfers between devices: 36.1 us -> 30.9 us
  starting transfers between devices: 22.7 us -> 19.6 us
    ppermute x20 -> x17, waiting for transfers between devices: 36.1 us -> 30.9 us  [the longest x14 30.3 us: along_ring(): lax.ppermute(x, 'pass', [(2 * s + c, 2 * d + c) for s, d in pairs for c i...]
    ppermute x20 -> x17, starting transfers between devices: 22.7 us -> 19.6 us  [the longest x14 12.3 us: along_ring(): lax.ppermute(x, 'pass', [(2 * s + c, 2 * d + c) for s, d in pairs for c i...]
    pallas_call x7 -> x4, Pallas kernels: 41.8 us -> 41.7 us  [the longest x2 34.4 us: attend(): pl.pallas_call(functools.partial(attend_kernel, ring), grid_spec=pltpu.Pr...]
  transfers between devices with their start and end apart: 20 -> 17, of which waited for: 8 -> 9; matrix products, arithmetic and copies ran while one was open for 1% -> 1% of each run, Pallas kernels for 20% -> 23%
where the time goes in v3:
time: 97.6 us; the launch traced here: 97.3 us
  Pallas kernels  41.7 us (43%)
  waiting for transfers between devices  30.9 us (32%)
  starting transfers between devices  19.6 us (20%)
  local copies, waits for them, and re-layouts  4.91 us (5%)
    pallas_call x2, Pallas kernels, attend(): pl.pallas_call(functools.partial(attend_kernel, ring), grid_spec=pltpu.Pr...  34.4 us
    ppermute x14, waiting for transfers between devices, along_ring(): lax.ppermute(x, 'pass', [(2 * s + c, 2 * d + c) for s, d in pairs for c i...  30.3 us
    ppermute x14, starting transfers between devices, along_ring(): lax.ppermute(x, 'pass', [(2 * s + c, 2 * d + c) for s, d in pairs for c i...  12.3 us
    ppermute x3, starting transfers between devices, to_partner(): return lax.ppermute(x, 'pass', [(i, i ^ 1) for i in range(extent)])  7.3 us
    pallas_call x1, Pallas kernels, pool(): pl.pallas_call(pool_kernel, grid=(count,), in_specs=[pl.BlockSpec((1, LEN...  5.51 us
    unnamed x19, local copies, waits for them, and re-layouts  3.23 us
  transfers between devices with their start and end apart: 17, of which 9 were waited for; matrix products, arithmetic and copies ran while one was open for 1% of the time, Pallas kernels for 23%

profile of v3, /device:TPU:1, one launch (start us, length us, event | category | flops | bytes accessed | tf_op | source)
XLA Modules:
  0.0 97.3 jit_solution(2822191582913465237)
XLA Ops:
  0.0 1.0 constant_dynamic-slice_fusion.3
  1.0 0.1 collective-permute-start
  1.1 0.7 reshape.16.gain_ref
  1.8 0.6 collective-permute-done
  2.4 2.5 %collective-permute-start.2 = (bf16[512,256]{1,0:T(8,128)(2,1)S(1)}, bf16[512,256]{1,0:T(8,128)(2,1)S(1)}, u32[]{:S(2)}, u32[]{:S(2)}) collective-permute-start(bf16[512,256]{1,0:T(8,128)(2,1)S(1)} %pad_maximum_fusion.rest_0_), channel_id=1, source_target_pairs={{0,4},{1,5},{4,8},{5,9},{8,12},{9,13},{12,14},{13,15},{14,10},{15,... | collective-permute-start | bytes 786440 | tf_op jit(solution)/shard_map/ppermute | solution.py:311
  4.9 0.0 copy-start
  4.9 2.2 %copy-done = bf16[4,128,4096]{2,1,0:T(8,128)(2,1)S(1)} copy-done((bf16[4,128,4096]{2,1,0:T(8,128)(2,1)S(1)}, bf16[4,128,4096]{2,1,0:T(8,128)(2,1)}, u32[]{:S(2)}) %copy-start) | copy-done | bytes 4194328
  7.1 0.0 copy-start.1
  7.1 0.9 copy-done.1
  8.1 5.5 %pool.1.own_ref = bf16[128,4096]{1,0:T(8,128)(2,1)S(1)} custom-call(bf16[4,128,4096]{2,1,0:T(8,128)(2,1)S(1)} %copy-done, bf16[32,4096]{1,0:T(8,128)(2,1)S(1)} %copy-done.1, bf16[1,4096]{1,0:T(2,128)(2,1)S(1)} %reshape.16.gain_ref), custom_call_target="tpu_custom_call" | custom-call | flops 268435456 | bytes 4194304 | tf_op jit(solution)/shard_map/pool/pallas_call | solution.py:75
  13.6 0.0 copy-start.4
  13.6 0.0 copy-start.5
  13.6 0.7 collective-permute-start.1
  14.3 0.0 collective-permute-start.6
  14.3 0.0 collective-permute-done.2.rest_1_
  14.3 1.5 %collective-permute-start.3 = (bf16[512,256]{1,0:T(8,128)(2,1)S(1)}, bf16[512,256]{1,0:T(8,128)(2,1)S(1)}, u32[]{:S(2)}, u32[]{:S(2)}) collective-permute-start(bf16[512,256]{1,0:T(8,128)(2,1)S(1)} %collective-permute-done.2.rest_1_), channel_id=1, source_target_pairs={{0,4},{1,5},{4,8},{5,9},{8,12},{9,13},{12,14},{13,15},{14,10},{15,... | collective-permute-start | bytes 786440 | tf_op jit(solution)/shard_map/ppermute | solution.py:311
  15.8 6.4 %collective-permute-done.6.rest_7_ = bf16[512,256]{1,0:T(8,128)(2,1)S(1)} collective-permute-done((bf16[512,256]{1,0:T(8,128)(2,1)S(1)}, bf16[512,256]{1,0:T(8,128)(2,1)S(1)}, u32[]{:S(2)}, u32[]{:S(2)}) %collective-permute-start.6) | collective-permute-done | bytes 262176 | tf_op jit(solution)/shard_map/ppermute | solution.py:311
  22.2 0.2 collective-permute-start.7
  22.4 0.0 collective-permute-done.3.rest_2_
  22.4 1.3 %collective-permute-start.4 = (bf16[512,256]{1,0:T(8,128)(2,1)S(1)}, bf16[512,256]{1,0:T(8,128)(2,1)}, u32[]{:S(2)}, u32[]{:S(2)}) collective-permute-start(bf16[512,256]{1,0:T(8,128)(2,1)S(1)} %collective-permute-done.3.rest_2_), channel_id=1, source_target_pairs={{0,4},{1,5},{4,8},{5,9},{8,12},{9,13},{12,14},{13,15},{14,10},{15,... | collective-permute-start | bytes 786440 | tf_op jit(solution)/shard_map/ppermute | solution.py:311
  23.7 5.6 %collective-permute-done.7.rest_6_ = bf16[512,256]{1,0:T(8,128)(2,1)S(1)} collective-permute-done((bf16[512,256]{1,0:T(8,128)(2,1)S(1)}, bf16[512,256]{1,0:T(8,128)(2,1)S(1)}, u32[]{:S(2)}, u32[]{:S(2)}) %collective-permute-start.7) | collective-permute-done | bytes 262176 | tf_op jit(solution)/shard_map/ppermute | solution.py:311
  29.3 0.4 collective-permute-start.8
  29.7 0.0 collective-permute-done.4.rest_3_
  29.7 1.1 %collective-permute-start.5 = (bf16[512,256]{1,0:T(8,128)(2,1)}, bf16[512,256]{1,0:T(8,128)(2,1)}, u32[]{:S(2)}, u32[]{:S(2)}) collective-permute-start(bf16[512,256]{1,0:T(8,128)(2,1)} %collective-permute-done.4.rest_3_), channel_id=1, source_target_pairs={{0,4},{1,5},{4,8},{5,9},{8,12},{9,13},{12,14},{13,15},{14,10},{15,... | collective-permute-start | bytes 786440 | tf_op jit(solution)/shard_map/ppermute | solution.py:311
  30.7 0.0 copy-start.2
  30.7 0.0 copy-start.3
  30.7 4.8 %collective-permute-done.8.rest_5_ = bf16[512,256]{1,0:T(8,128)(2,1)} collective-permute-done((bf16[512,256]{1,0:T(8,128)(2,1)S(1)}, bf16[512,256]{1,0:T(8,128)(2,1)}, u32[]{:S(2)}, u32[]{:S(2)}) %collective-permute-start.8) | collective-permute-done | bytes 262176 | tf_op jit(solution)/shard_map/ppermute | solution.py:311
  35.5 0.0 collective-permute-done.1.other_ref
  35.5 0.5 collective-permute-done.5.rest_4_
  36.1 1.8 %project.1 = bf16[256,256]{1,0:T(8,128)(2,1)S(1)} custom-call(s32[1]{0:T(128)} %bitcast.2.core_ref.half_ref, s32[1]{0:T(128)} %bitcast.1.place_ref, bf16[128,4096]{1,0:T(8,128)(2,1)S(1)} %pool.1.own_ref, bf16[128,4096]{1,0:T(8,128)(2,1)S(1)} %collective-permute-done.1.other_ref, bf16[512,256]{1,0:T(8,128)(2,1)S(1)} %pad_maximum_fusion.rest_0_, ...), custom_call_target="tpu_custom_call" | custom-call | flops 536870912 | bytes 2097152 | tf_op jit(solution)/shard_map/project/pallas_call | solution.py:264
  37.9 0.9 collective-permute-start.9
  38.8 0.6 collective-permute-start.13
  39.4 2.4 %collective-permute-done.9 = bf16[256,256]{1,0:T(8,128)(2,1)S(1)} collective-permute-done((bf16[256,256]{1,0:T(8,128)(2,1)S(1)}, bf16[256,256]{1,0:T(8,128)(2,1)S(1)}, u32[]{:S(2)}, u32[]{:S(2)}) %collective-permute-start.9) | collective-permute-done | bytes 131104 | tf_op jit(solution)/shard_map/ppermute | solution.py:311
  41.8 0.9 collective-permute-start.10
  42.6 0.0 collective-permute-done.13
  42.6 0.6 collective-permute-start.14
  43.2 3.3 %collective-permute-done.10 = bf16[256,256]{1,0:T(8,128)(2,1)S(1)} collective-permute-done((bf16[256,256]{1,0:T(8,128)(2,1)S(1)}, bf16[256,256]{1,0:T(8,128)(2,1)S(1)}, u32[]{:S(2)}, u32[]{:S(2)}) %collective-permute-start.10) | collective-permute-done | bytes 131104 | tf_op jit(solution)/shard_map/ppermute | solution.py:311
  46.6 1.1 %collective-permute-start.11 = (bf16[256,256]{1,0:T(8,128)(2,1)S(1)}, bf16[256,256]{1,0:T(8,128)(2,1)S(1)}, u32[]{:S(2)}, u32[]{:S(2)}) collective-permute-start(bf16[256,256]{1,0:T(8,128)(2,1)S(1)} %collective-permute-done.10), channel_id=1, source_target_pairs={{0,4},{1,5},{4,8},{5,9},{8,12},{9,13},{12,14},{13,15},{14,10},{15,... | collective-permute-start | bytes 393224 | tf_op jit(solution)/shard_map/ppermute | solution.py:311
  47.7 0.0 collective-permute-done.14
  47.7 0.4 collective-permute-start.15
  48.1 3.8 %collective-permute-done.11 = bf16[256,256]{1,0:T(8,128)(2,1)S(1)} collective-permute-done((bf16[256,256]{1,0:T(8,128)(2,1)S(1)}, bf16[256,256]{1,0:T(8,128)(2,1)S(1)}, u32[]{:S(2)}, u32[]{:S(2)}) %collective-permute-start.11) | collective-permute-done | bytes 131104 | tf_op jit(solution)/shard_map/ppermute | solution.py:311
  51.9 0.9 collective-permute-start.12
  52.9 3.5 %collective-permute-done.12 = bf16[256,256]{1,0:T(8,128)(2,1)S(1)} collective-permute-done((bf16[256,256]{1,0:T(8,128)(2,1)S(1)}, bf16[256,256]{1,0:T(8,128)(2,1)S(1)}, u32[]{:S(2)}, u32[]{:S(2)}) %collective-permute-start.12) | collective-permute-done | bytes 131104 | tf_op jit(solution)/shard_map/ppermute | solution.py:311
  56.4 0.0 collective-permute-done.15
  56.5 6.5 %collective-permute-start.16 = (bf16[2048,256]{1,0:T(8,128)(2,1)S(1)}, bf16[2048,256]{1,0:T(8,128)(2,1)S(1)}, u32[]{:S(2)}, u32[]{:S(2)}) collective-permute-start(bf16[2048,256]{1,0:T(8,128)(2,1)S(1)} %constant_dynamic-update-slice_fusion.k_ref.v_ref), channel_id=1, source_target_pairs={{0,1},{1,0},{2,3},{3,2},{4,5},{5,4},{6,7},{7,6},{8,9},{9,8},{10,11... | collective-permute-start | bytes 3145736 | tf_op jit(solution)/shard_map/ppermute | solution.py:307
  62.9 0.0 copy-done.4
  62.9 0.0 copy-done.5
  62.9 0.0 copy-done.2
  62.9 0.0 copy-done.3
  62.9 17.2 %attend.2.rest_0_ = bf16[4,64,7424]{2,1,0:T(8,128)(2,1)} custom-call(s32[1]{0:T(128)} %bitcast.2.core_ref.half_ref, s32[1]{0:T(128)} %bitcast.1.place_ref, s32[4,16]{1,0:T(4,128)S(1)} %copy-done.4, s32[4]{0:T(128)S(1)} %copy-done.5, bf16[4,64,7424]{2,1,0:T(8,128)(2,1)S(1)} %copy-done.2, bf16[2048,256]{1,0:T(8,128)(2,1)S(1)} %constant_dynamic-update-slice_fusion.k_ref.v_ref, ...), custom_call_target="tpu_custom_call" | custom-call | flops 2189426688 | bytes 4849664 | tf_op jit(solution)/shard_map/attend/pallas_call | solution.py:214
  80.1 0.0 collective-permute-done.16.k_ref.v_ref
  80.1 17.2 %attend.3 = bf16[4,64,7424]{2,1,0:T(8,128)(2,1)} custom-call(s32[1]{0:T(128)} %bitcast.half_ref, s32[1]{0:T(128)} %bitcast.1.place_ref, s32[4,16]{1,0:T(4,128)S(1)} %copy-done.4, s32[4]{0:T(128)S(1)} %copy-done.5, bf16[4,64,7424]{2,1,0:T(8,128)(2,1)S(1)} %copy-done.2, ...), custom_call_target="tpu_custom_call", output_to_operand_aliasing={{}: (9, {})} | custom-call | flops 2189426688 | bytes 4849664 | tf_op jit(solution)/shard_map/attend/pallas_call | solution.py:214
  (10 shorter events, 0.1 us)
Async XLA Ops:
  1.0 1.4 %collective-permute-start = (bf16[256,256]{1,0:T(8,128)(2,1)S(1)}, bf16[256,256]{1,0:T(8,128)(2,1)S(1)}, u32[]{:S(2)}, u32[]{:S(2)}) collective-permute-start(bf16[256,256]{1,0:T(8,128)(2,1)S(1)} %pad_maximum_fusion.1), channel_id=1, source_target_pairs={{0,1},{1,0},{2,3},{3,2},{4,5},{5,4},{6,7},{7,6},{8,9},{9,8},{10,11... | collective-permute-start | bytes 393224 | tf_op jit(solution)/shard_map/ppermute | solution.py:307
  2.4 11.9 %collective-permute-start.2 = (bf16[512,256]{1,0:T(8,128)(2,1)S(1)}, bf16[512,256]{1,0:T(8,128)(2,1)S(1)}, u32[]{:S(2)}, u32[]{:S(2)}) collective-permute-start(bf16[512,256]{1,0:T(8,128)(2,1)S(1)} %pad_maximum_fusion.rest_0_), channel_id=1, source_target_pairs={{0,4},{1,5},{4,8},{5,9},{8,12},{9,13},{12,14},{13,15},{14,10},{15,... | collective-permute-start | bytes 786440 | tf_op jit(solution)/shard_map/ppermute | solution.py:311
  4.9 2.2 %copy-start = (bf16[4,128,4096]{2,1,0:T(8,128)(2,1)S(1)}, bf16[4,128,4096]{2,1,0:T(8,128)(2,1)}, u32[]{:S(2)}) copy-start(bf16[4,128,4096]{2,1,0:T(8,128)(2,1)} %states_ref.1) | copy-start | bytes 12582916
  7.1 0.9 copy-start.1
  13.6 49.4 %copy-start.4 = (s32[4,16]{1,0:T(4,128)S(1)}, s32[4,16]{1,0:T(4,128)}, u32[]{:S(2)}) copy-start(s32[4,16]{1,0:T(4,128)} %passage_ref.3) | copy-start | bytes 772
  13.6 49.3 %copy-start.5 = (s32[4]{0:T(128)S(1)}, s32[4]{0:T(128)}, u32[]{:S(2)}) copy-start(s32[4]{0:T(128)} %length_ref.3) | copy-start | bytes 52
  13.6 21.9 %collective-permute-start.1 = (bf16[128,4096]{1,0:T(8,128)(2,1)S(1)}, bf16[128,4096]{1,0:T(8,128)(2,1)S(1)}, u32[]{:S(2)}, u32[]{:S(2)}) collective-permute-start(bf16[128,4096]{1,0:T(8,128)(2,1)S(1)} %pool.1.own_ref), channel_id=1, source_target_pairs={{0,1},{1,0},{2,3},{3,2},{4,5},{5,4},{6,7},{7,6},{8,9},{9,8},{10,11... | collective-permute-start | bytes 3145736 | tf_op jit(solution)/shard_map/ppermute | solution.py:307
  14.3 7.9 %collective-permute-start.6 = (bf16[512,256]{1,0:T(8,128)(2,1)S(1)}, bf16[512,256]{1,0:T(8,128)(2,1)S(1)}, u32[]{:S(2)}, u32[]{:S(2)}) collective-permute-start(bf16[512,256]{1,0:T(8,128)(2,1)S(1)} %pad_maximum_fusion.rest_0_), channel_id=1, source_target_pairs={{0,2},{1,3},{4,0},{5,1},{8,4},{9,5},{12,8},{13,9},{14,12},{15,13},... | collective-permute-start | bytes 786440 | tf_op jit(solution)/shard_map/ppermute | solution.py:311
  14.3 8.1 %collective-permute-start.3 = (bf16[512,256]{1,0:T(8,128)(2,1)S(1)}, bf16[512,256]{1,0:T(8,128)(2,1)S(1)}, u32[]{:S(2)}, u32[]{:S(2)}) collective-permute-start(bf16[512,256]{1,0:T(8,128)(2,1)S(1)} %collective-permute-done.2.rest_1_), channel_id=1, source_target_pairs={{0,4},{1,5},{4,8},{5,9},{8,12},{9,13},{12,14},{13,15},{14,10},{15,... | collective-permute-start | bytes 786440 | tf_op jit(solution)/shard_map/ppermute | solution.py:311
  22.2 7.1 %collective-permute-start.7 = (bf16[512,256]{1,0:T(8,128)(2,1)S(1)}, bf16[512,256]{1,0:T(8,128)(2,1)S(1)}, u32[]{:S(2)}, u32[]{:S(2)}) collective-permute-start(bf16[512,256]{1,0:T(8,128)(2,1)S(1)} %collective-permute-done.6.rest_7_), channel_id=1, source_target_pairs={{0,2},{1,3},{4,0},{5,1},{8,4},{9,5},{12,8},{13,9},{14,12},{15,13},... | collective-permute-start | bytes 786440 | tf_op jit(solution)/shard_map/ppermute | solution.py:311
  22.4 7.3 %collective-permute-start.4 = (bf16[512,256]{1,0:T(8,128)(2,1)S(1)}, bf16[512,256]{1,0:T(8,128)(2,1)}, u32[]{:S(2)}, u32[]{:S(2)}) collective-permute-start(bf16[512,256]{1,0:T(8,128)(2,1)S(1)} %collective-permute-done.3.rest_2_), channel_id=1, source_target_pairs={{0,4},{1,5},{4,8},{5,9},{8,12},{9,13},{12,14},{13,15},{14,10},{15,... | collective-permute-start | bytes 786440 | tf_op jit(solution)/shard_map/ppermute | solution.py:311
  29.3 6.3 %collective-permute-start.8 = (bf16[512,256]{1,0:T(8,128)(2,1)S(1)}, bf16[512,256]{1,0:T(8,128)(2,1)}, u32[]{:S(2)}, u32[]{:S(2)}) collective-permute-start(bf16[512,256]{1,0:T(8,128)(2,1)S(1)} %collective-permute-done.7.rest_6_), channel_id=1, source_target_pairs={{0,2},{1,3},{4,0},{5,1},{8,4},{9,5},{12,8},{13,9},{14,12},{15,13},... | collective-permute-start | bytes 786440 | tf_op jit(solution)/shard_map/ppermute | solution.py:311
  29.7 6.4 %collective-permute-start.5 = (bf16[512,256]{1,0:T(8,128)(2,1)}, bf16[512,256]{1,0:T(8,128)(2,1)}, u32[]{:S(2)}, u32[]{:S(2)}) collective-permute-start(bf16[512,256]{1,0:T(8,128)(2,1)} %collective-permute-done.4.rest_3_), channel_id=1, source_target_pairs={{0,4},{1,5},{4,8},{5,9},{8,12},{9,13},{12,14},{13,15},{14,10},{15,... | collective-permute-start | bytes 786440 | tf_op jit(solution)/shard_map/ppermute | solution.py:311
  30.7 32.2 %copy-start.2 = (bf16[4,64,7424]{2,1,0:T(8,128)(2,1)S(1)}, bf16[4,64,7424]{2,1,0:T(8,128)(2,1)}, u32[]{:S(2)}) copy-start(bf16[4,64,7424]{2,1,0:T(8,128)(2,1)} %q_ref.3) | copy-start | bytes 11403268
  30.7 32.2 %copy-start.3 = (bf16[4,64,512]{2,1,0:T(8,128)(2,1)S(1)}, bf16[4,64,512]{2,1,0:T(8,128)(2,1)}, u32[]{:S(2)}) copy-start(bf16[4,64,512]{2,1,0:T(8,128)(2,1)} %own_v_ref.3) | copy-start | bytes 786436
  37.9 3.9 %collective-permute-start.9 = (bf16[256,256]{1,0:T(8,128)(2,1)S(1)}, bf16[256,256]{1,0:T(8,128)(2,1)S(1)}, u32[]{:S(2)}, u32[]{:S(2)}) collective-permute-start(bf16[256,256]{1,0:T(8,128)(2,1)S(1)} %project.1), channel_id=1, source_target_pairs={{0,4},{1,5},{4,8},{5,9},{8,12},{9,13},{12,14},{13,15},{14,10},{15,... | collective-permute-start | bytes 393224 | tf_op jit(solution)/shard_map/ppermute | solution.py:311
  38.8 3.8 %collective-permute-start.13 = (bf16[256,256]{1,0:T(8,128)(2,1)S(1)}, bf16[256,256]{1,0:T(8,128)(2,1)S(1)}, u32[]{:S(2)}, u32[]{:S(2)}) collective-permute-start(bf16[256,256]{1,0:T(8,128)(2,1)S(1)} %project.1), channel_id=1, source_target_pairs={{0,2},{1,3},{4,0},{5,1},{8,4},{9,5},{12,8},{13,9},{14,12},{15,13},... | collective-permute-start | bytes 393224 | tf_op jit(solution)/shard_map/ppermute | solution.py:311
  41.8 4.8 %collective-permute-start.10 = (bf16[256,256]{1,0:T(8,128)(2,1)S(1)}, bf16[256,256]{1,0:T(8,128)(2,1)S(1)}, u32[]{:S(2)}, u32[]{:S(2)}) collective-permute-start(bf16[256,256]{1,0:T(8,128)(2,1)S(1)} %collective-permute-done.9), channel_id=1, source_target_pairs={{0,4},{1,5},{4,8},{5,9},{8,12},{9,13},{12,14},{13,15},{14,10},{15,... | collective-permute-start | bytes 393224 | tf_op jit(solution)/shard_map/ppermute | solution.py:311
  42.6 5.0 %collective-permute-start.14 = (bf16[256,256]{1,0:T(8,128)(2,1)S(1)}, bf16[256,256]{1,0:T(8,128)(2,1)S(1)}, u32[]{:S(2)}, u32[]{:S(2)}) collective-permute-start(bf16[256,256]{1,0:T(8,128)(2,1)S(1)} %collective-permute-done.13), channel_id=1, source_target_pairs={{0,2},{1,3},{4,0},{5,1},{8,4},{9,5},{12,8},{13,9},{14,12},{15,13},... | collective-permute-start | bytes 393224 | tf_op jit(solution)/shard_map/ppermute | solution.py:311
  46.6 5.3 %collective-permute-start.11 = (bf16[256,256]{1,0:T(8,128)(2,1)S(1)}, bf16[256,256]{1,0:T(8,128)(2,1)S(1)}, u32[]{:S(2)}, u32[]{:S(2)}) collective-permute-start(bf16[256,256]{1,0:T(8,128)(2,1)S(1)} %collective-permute-done.10), channel_id=1, source_target_pairs={{0,4},{1,5},{4,8},{5,9},{8,12},{9,13},{12,14},{13,15},{14,10},{15,... | collective-permute-start | bytes 393224 | tf_op jit(solution)/shard_map/ppermute | solution.py:311
  47.7 8.7 %collective-permute-start.15 = (bf16[256,256]{1,0:T(8,128)(2,1)S(1)}, bf16[256,256]{1,0:T(8,128)(2,1)S(1)}, u32[]{:S(2)}, u32[]{:S(2)}) collective-permute-start(bf16[256,256]{1,0:T(8,128)(2,1)S(1)} %collective-permute-done.14), channel_id=1, source_target_pairs={{0,2},{1,3},{4,0},{5,1},{8,4},{9,5},{12,8},{13,9},{14,12},{15,13},... | collective-permute-start | bytes 393224 | tf_op jit(solution)/shard_map/ppermute | solution.py:311
  51.9 4.5 %collective-permute-start.12 = (bf16[256,256]{1,0:T(8,128)(2,1)S(1)}, bf16[256,256]{1,0:T(8,128)(2,1)S(1)}, u32[]{:S(2)}, u32[]{:S(2)}) collective-permute-start(bf16[256,256]{1,0:T(8,128)(2,1)S(1)} %collective-permute-done.11), channel_id=1, source_target_pairs={{0,4},{1,5},{4,8},{5,9},{8,12},{9,13},{12,14},{13,15},{14,10},{15,... | collective-permute-start | bytes 393224 | tf_op jit(solution)/shard_map/ppermute | solution.py:311
  56.5 23.7 %collective-permute-start.16 = (bf16[2048,256]{1,0:T(8,128)(2,1)S(1)}, bf16[2048,256]{1,0:T(8,128)(2,1)S(1)}, u32[]{:S(2)}, u32[]{:S(2)}) collective-permute-start(bf16[2048,256]{1,0:T(8,128)(2,1)S(1)} %constant_dynamic-update-slice_fusion.k_ref.v_ref), channel_id=1, source_target_pairs={{0,1},{1,0},{2,3},{3,2},{4,5},{5,4},{6,7},{7,6},{8,9},{9,8},{10,11... | collective-permute-start | bytes 3145736 | tf_op jit(solution)/shard_map/ppermute | solution.py:307

commit v4 on v3

v4 whole, which is shorter than its diff:
```python
import functools
import math

import jax
import jax.numpy as jnp
from jax import lax
from jax.experimental import pallas as pl
from jax.experimental.pallas import tpu as pltpu
from jax.sharding import PartitionSpec as P

D = 4096
CH = 32
CHD = 128
MEM = 32
LEN = 128
QLEN = 64
TOPK = 16
H = 116
HD = 64
KVH = 4
GROUP = 29
KVW = 512

LANES = 2 * HD
PAIRS = GROUP
HALF = PAIRS * LANES
ROWS = TOPK * MEM
KEYS = 2 * (ROWS + QLEN)
NEG = -1e30
POOL_HEADS = 16
POOL_CALLS = 2
CHIP = 8
STEP = 8
BLOCK = 16
MIB = 1024 * 1024


def place_of(chip, ring):
    line, lane = lax.div(chip, 2), lax.rem(chip, 2)
    return line + lane * (ring - 1 - 2 * line)


def chip_at(place, ring):
    lane = lax.div(place, ring // 2)
    line = place + lane * (ring - 1 - 2 * place)
    return 2 * line + lane


def slot_of(chip, place, ring):
    mine = chip_at(place, ring)
    lines = ring // 2
    back = lax.rem(lines + lax.div(mine, 2) - lax.div(chip, 2), lines)
    return back + lines * lax.rem(lax.rem(mine, 2) + lax.rem(chip, 2), 2)


def pool_kernel(states_ref, queries_ref, gain_ref, out_ref, pooled):
    squares = jnp.zeros((MEM, CHD), jnp.float32)
    for base in range(0, CH, POOL_HEADS):
        spans = [slice(h * CHD, (h + 1) * CHD) for h in range(base, base + POOL_HEADS)]
        scores = jnp.concatenate(
            [
                lax.dot_general(
                    queries_ref[:, span], states_ref[0, :, span], (((1,), (1,)), ((), ())),
                    preferred_element_type=jnp.float32,
                )
                for span in spans
            ],
            axis=0,
        ) * (1.0 / math.sqrt(CHD))
        scores = jnp.exp(scores - jnp.max(scores, axis=1, keepdims=True))
        weights = (scores / jnp.sum(scores, axis=1, keepdims=True)).astype(jnp.bfloat16)
        for i, span in enumerate(spans):
            part = jnp.dot(
                weights[i * MEM:(i + 1) * MEM], states_ref[0, :, span], preferred_element_type=jnp.float32
            )
            pooled[:, span] = part
            squares += part * part
    mean_square = jnp.sum(squares, axis=1, keepdims=True) * (1.0 / D)
    scale = lax.rsqrt(mean_square + 1e-06)
    out_ref[...] = (pooled[...] * scale * gain_ref[...].astype(jnp.float32)).astype(jnp.bfloat16)


def pool(states, queries, gain, first, count):
    return pl.pallas_call(
        pool_kernel,
        grid=(count,),
        in_specs=[
            pl.BlockSpec((1, LEN, D), lambda p: (first + p, 0, 0)),
            pl.BlockSpec((MEM, D), lambda p: (0, 0)),
            pl.BlockSpec((1, D), lambda p: (0, 0)),
        ],
        out_specs=pl.BlockSpec((MEM, D), lambda p: (p, 0)),
        out_shape=jax.ShapeDtypeStruct((count * MEM, D), jnp.bfloat16),
        scratch_shapes=[pltpu.VMEM((MEM, D), jnp.float32)],
        compiler_params=pltpu.CompilerParams(vmem_limit_bytes=16 * MIB),
        cost_estimate=pl.CostEstimate(
            flops=4 * count * MEM * LEN * D, bytes_accessed=2 * count * LEN * D,
            transcendentals=count * CH * MEM * LEN,
        ),
        name="pool",
    )(states, queries, gain.reshape(1, D))


def attend_kernel(
    chips, half_ref, place_ref, passage_ref, length_ref, q_ref, k_ref, v_ref, own_k_ref, own_v_ref, *rest
):
    out_ref, keys, values, key_side, value_side, scores, weights, bias = rest[-8:]
    query = pl.program_id(0)

    @pl.when(query == 0)
    def _():
        key_side[...] = jnp.zeros_like(key_side)
        lane = lax.broadcasted_iota(jnp.int32, (KEYS, LANES), 1)
        row = lax.broadcasted_iota(jnp.int32, (KEYS, LANES), 0)
        in_b = ((row >= ROWS) & (row < 2 * ROWS)) | (row >= 2 * ROWS + QLEN)
        ones = jnp.where((lane >= HD) == in_b, 1.0, 0.0).astype(jnp.bfloat16)
        for g in range(2):
            value_side[g, :, LANES:] = ones

    for slot in range(TOPK):
        passage = passage_ref[query, slot]
        if chips:
            chip, inside = lax.div(passage, CHIP), lax.rem(passage, CHIP)
            passage = slot_of(chip, place_ref[0], chips) * CHIP + inside
        start = pl.multiple_of(passage * MEM, MEM)
        keys[slot * MEM:(slot + 1) * MEM, :] = k_ref[pl.ds(start, MEM), :].astype(jnp.float32)
        values[slot * MEM:(slot + 1) * MEM, :] = v_ref[pl.ds(start, MEM), :].astype(jnp.float32)
    length = length_ref[query]

    turned = jnp.transpose(keys[...]).astype(jnp.bfloat16)
    own_k = own_k_ref[0].astype(jnp.float32)
    own_turned = jnp.transpose(jnp.concatenate([own_k, own_k], axis=0))
    column = lax.broadcasted_iota(jnp.int32, (HD, LANES), 1)
    for g in range(2):
        for member in range(2):
            rows = slice(member * HD, (member + 1) * HD)
            key_side[g, rows, member * ROWS:(member + 1) * ROWS] = turned[g * HD:(g + 1) * HD]
            own = own_turned[g * HD:(g + 1) * HD]
            mine = (column >= HD) if member else (column < HD)
            key_side[g, rows, 2 * ROWS:] = jnp.where(mine, own, 0.0).astype(jnp.bfloat16)

    token = lax.broadcasted_iota(jnp.int32, (QLEN, LANES), 0)
    lane = lax.broadcasted_iota(jnp.int32, (QLEN, LANES), 1)
    key = lax.rem(lane, HD)
    bias[...] = jnp.where((key <= token) & (key < length), 0.0, NEG)
    alive = token < length
    low_tile = lane < HD
    low = lax.broadcasted_iota(jnp.int32, (BLOCK, LANES), 1) < HD
    factor = math.log2(math.e) / math.sqrt(HD)

    half = PAIRS // 2
    chunks = []
    for g in range(2):
        tiles = list(range(half + 1)) if g == 0 else list(range(half, PAIRS))
        chunks += [(g, tiles[at:at + STEP]) for at in range(0, len(tiles), STEP)]

    def key_product(i):
        g, tiles = chunks[i]
        lhs = jnp.concatenate([q_ref[0, :, t * LANES:(t + 1) * LANES] for t in tiles], axis=0)
        scores[i % 2, :len(tiles) * QLEN, :] = jnp.dot(
            lhs, key_side[g], preferred_element_type=jnp.float32
        )

    def softmax(i):
        for at in range(0, len(chunks[i][1]) * QLEN, BLOCK):
            rows = slice(at, at + BLOCK)
            own = scores[i % 2, rows, 2 * ROWS:] + bias[at % QLEN:at % QLEN + BLOCK, :]
            tops = []
            for member in range(2):
                top = jnp.where(low, own, NEG) if member == 0 else jnp.where(low, NEG, own)
                for c in range(member * ROWS, (member + 1) * ROWS, LANES):
                    top = jnp.maximum(top, scores[i % 2, rows, c:c + LANES])
                top = jnp.max(top, axis=1, keepdims=True)
                tops.append(top)
                for c in range(member * ROWS, (member + 1) * ROWS, LANES):
                    weights[i % 2, rows, c:c + LANES] = jnp.exp2(
                        (scores[i % 2, rows, c:c + LANES] - top) * factor
                    ).astype(jnp.bfloat16)
            weights[i % 2, rows, 2 * ROWS:] = jnp.exp2(
                (own - jnp.where(low, tops[0], tops[1])) * factor
            ).astype(jnp.bfloat16)

    def value_product(i):
        g, tiles = chunks[i]
        count = len(tiles)
        mixed = jnp.dot(
            weights[i % 2, :count * QLEN, :], value_side[g], preferred_element_type=jnp.float32
        )
        for n, t in enumerate(tiles):
            rows = slice(n * QLEN, (n + 1) * QLEN)
            result = jnp.where(alive, mixed[rows, :LANES] / mixed[rows, LANES:], 0.0).astype(jnp.bfloat16)
            at = slice(t * LANES, (t + 1) * LANES)
            if t == half and g == 1:
                result = jnp.where(low_tile, out_ref[0, :, at], result)
            out_ref[0, :, at] = result

    key_product(0)

    memory_v = values[...]
    own_v = own_v_ref[0].astype(jnp.float32)
    for block, spans in (
        (memory_v, ((0, ROWS), (ROWS, 2 * ROWS))),
        (own_v, ((2 * ROWS, 2 * ROWS + QLEN), (2 * ROWS + QLEN, KEYS))),
    ):
        swapped = pltpu.roll(block, HD, 1)
        lower = lax.broadcasted_iota(jnp.int32, block.shape, 1) < HD
        for g in range(2):
            first, second = (block, swapped) if g == 0 else (swapped, block)
            for (start, stop), side in zip(
                spans, (jnp.where(lower, first, 0.0), jnp.where(lower, 0.0, second))
            ):
                value_side[g, start:stop, :LANES] = side.astype(jnp.bfloat16)

    for i in range(len(chunks)):
        if i + 1 < len(chunks):
            key_product(i + 1)
        softmax(i)
        value_product(i)


def attend(chips, half, place, retrieval, lengths, questions, memory_kv, own_kv, earlier=None):
    count = questions.shape[0]
    total = memory_kv.shape[0]
    operands = [half.reshape(1), place, retrieval, lengths, questions, memory_kv, memory_kv, own_kv, own_kv]
    in_specs = [
        pl.BlockSpec((1, QLEN, HALF), lambda q, h, *_: (q, 0, h[0])),
        pl.BlockSpec((total, LANES), lambda q, h, *_: (0, 0)),
        pl.BlockSpec((total, LANES), lambda q, h, *_: (0, 1)),
        pl.BlockSpec((1, QLEN, LANES), lambda q, h, *_: (q, 0, h[0])),
        pl.BlockSpec((1, QLEN, LANES), lambda q, h, *_: (q, 0, 2 + h[0])),
    ]
    aliases = {}
    if earlier is not None:
        aliases = {len(operands): 0}
        operands.append(earlier)
        in_specs.append(pl.BlockSpec(memory_space=pl.ANY))
    return pl.pallas_call(
        functools.partial(attend_kernel, chips),
        grid_spec=pltpu.PrefetchScalarGridSpec(
            num_scalar_prefetch=4,
            grid=(count,),
            in_specs=in_specs,
            out_specs=pl.BlockSpec((1, QLEN, HALF), lambda q, h, *_: (q, 0, h[0])),
            scratch_shapes=[
                pltpu.VMEM((ROWS, LANES), jnp.float32),
                pltpu.VMEM((ROWS, LANES), jnp.float32),
                pltpu.VMEM((2, LANES, KEYS), jnp.bfloat16),
                pltpu.VMEM((2, KEYS, 2 * LANES), jnp.bfloat16),
                pltpu.VMEM((2, STEP * QLEN, KEYS), jnp.float32),
                pltpu.VMEM((2, STEP * QLEN, KEYS), jnp.bfloat16),
                pltpu.VMEM((QLEN, LANES), jnp.float32),
            ],
        ),
        out_shape=jax.ShapeDtypeStruct((count, QLEN, H * HD), jnp.bfloat16),
        input_output_aliases=aliases,
        compiler_params=pltpu.CompilerParams(vmem_limit_bytes=36 * MIB),
        cost_estimate=pl.CostEstimate(
            flops=2 * count * QLEN * H * HD * (ROWS + QLEN),
            bytes_accessed=2 * count * QLEN * H * HD + total * KVW,
            transcendentals=count * QLEN * H * (ROWS + QLEN) // 2,
        ),
        name="attend",
    )(*operands)


def project_kernel(ring, core_ref, place_ref, *rest):
    row_refs, weights, out_ref = rest[:2 * POOL_CALLS], rest[2 * POOL_CALLS:-1], rest[-1]
    count = POOL_CALLS * row_refs[0].shape[0]
    depth = weights[0].shape[0] // 2
    pieces = []
    for i in range(ring):
        if i == ring // 2:
            pieces += [(i, 0, weights[i], 0), (i, 1, weights[i + 1], 0)]
        else:
            pieces += [(i, part, weights[i + (i > ring // 2)], part * depth) for part in range(2)]
    total = jnp.zeros((2 * count, weights[0].shape[1]), jnp.float32)
    core = core_ref[0]
    for i, part, weight, top in pieces:
        chip = chip_at(lax.rem(ring + place_ref[0] - i, ring), ring)
        at = pl.multiple_of((2 * chip + (1 - core if part else core)) * depth, depth)
        rows = jnp.concatenate([x[:, pl.ds(at, depth)] for x in row_refs], axis=0)
        total += jnp.dot(rows, weight[top:top + depth], preferred_element_type=jnp.float32)
    result = total.astype(jnp.bfloat16)
    out_ref[pl.ds(pl.multiple_of(core * count, count), count)] = result[:count]
    out_ref[pl.ds(pl.multiple_of((1 - core) * count, count), count)] = result[count:]


def project(core, place, own_rows, other_rows, weights):
    count = POOL_CALLS * own_rows[0].shape[0]
    width = weights[0].shape[1]
    vmem = pl.BlockSpec(memory_space=pltpu.VMEM)
    smem = pl.BlockSpec(memory_space=pltpu.SMEM)
    return pl.pallas_call(
        functools.partial(project_kernel, len(weights) - 1),
        in_specs=[smem, smem] + [vmem] * (2 * POOL_CALLS + len(weights)),
        out_specs=vmem,
        out_shape=jax.ShapeDtypeStruct((2 * count, width), jnp.bfloat16),
        compiler_params=pltpu.CompilerParams(vmem_limit_bytes=16 * MIB),
        cost_estimate=pl.CostEstimate(
            flops=4 * count * D * width, bytes_accessed=2 * D * width, transcendentals=0
        ),
        name="project",
    )(core.reshape(1), place, *own_rows, *other_rows, *weights)


def local(
    extent,
    passage_states,
    memory_queries,
    memory_gain,
    kv_weight,
    retrieval,
    question_queries,
    question_kv,
    question_lengths,
):
    me = lax.axis_index("pass")
    core, chip = me & 1, lax.div(me, 2)
    chips = extent // 2
    depth = kv_weight.shape[0]

    if chips != 8 or depth % LANES:
        memory_rows = pool(passage_states, memory_queries, memory_gain, 0, passage_states.shape[0])
        whole_weight = lax.all_gather(kv_weight, "pass", axis=0, tiled=True)
        memory_kv = jnp.dot(memory_rows, whole_weight, preferred_element_type=jnp.float32)
        everything = lax.all_gather(memory_kv.astype(jnp.bfloat16), "pass", axis=0, tiled=True)
        halves = everything.reshape(-1, 2, 2, LANES).transpose(2, 0, 1, 3).reshape(2, -1, 2 * LANES)
        rest = (jnp.zeros((1,), jnp.int32), retrieval, question_lengths, question_queries)
        context = attend(0, jnp.int32(0), *rest, halves[0], question_kv)
        return attend(0, jnp.int32(1), *rest, halves[1], question_kv, context)

    place = place_of(chip, chips).reshape(1)
    order = [2 * line for line in range(chips // 2)] + [2 * line + 1 for line in range(chips // 2)][::-1]

    def to_partner(x):
        return lax.ppermute(x, "pass", [(i, i ^ 1) for i in range(extent)])

    def along(x, target):
        pairs = [(c, target(c // 2, c % 2)) for c in range(chips)]
        return lax.ppermute(x, "pass", [(2 * s + c, 2 * d + c) for s, d in pairs for c in range(2)])

    def along_ring(x, step):
        return along(x, lambda line, lane: order[(order.index(2 * line + lane) + step) % chips])

    def round_the_ring(block):
        up, down = [block], [block]
        for i in range(1, chips // 2):
            up.append(along_ring(up[-1], 1))
            down.append(along_ring(down[-1], -1))
        middle = block.shape[0] // 2
        halves = [along_ring(up[-1][:middle], 1), along_ring(down[-1][middle:], -1)]
        return up + halves + down[:0:-1]

    def line_by_line(block):
        lines = chips // 2
        blocks = [block]
        for k in range(1, lines):
            blocks.append(along(block, lambda line, lane: 2 * ((line + k) % lines) + lane))
        return blocks + [along(x, lambda line, lane: 2 * line + 1 - lane) for x in blocks]

    def columns(half):
        return jnp.concatenate(
            [
                lax.dynamic_slice_in_dim(kv_weight, half * LANES + at, LANES, axis=1)
                for at in (0, KVH * HD)
            ],
            axis=1,
        )

    weight = jnp.concatenate([columns(core), to_partner(columns(1 - core))], axis=0)
    weight, memory_queries = lax.optimization_barrier((weight, memory_queries))
    weights = round_the_ring(weight)
    part = passage_states.shape[0] // POOL_CALLS
    memory_rows = [
        pool(passage_states, memory_queries, memory_gain, i * part, part) for i in range(POOL_CALLS)
    ]
    memory_kv = project(core, place, memory_rows, [to_partner(x) for x in memory_rows], weights)
    near = jnp.concatenate(line_by_line(memory_kv), axis=0)
    far = to_partner(near)

    rest = (place, retrieval, question_lengths, question_queries)
    context = attend(chips, core, *rest, near, question_kv)
    return attend(chips, 1 - core, *rest, far, question_kv, context)


def solution(mesh):
    placed = (
        P(("groups", "pass"), None, None),
        P(),
        P(),
        P("pass", None),
        P(("groups", "pass"), None),
        P(("groups", "pass"), None, None),
        P(("groups", "pass"), None, None),
        P(("groups", "pass")),
    )
    return jax.shard_map(
        functools.partial(local, mesh.shape["pass"]),
        mesh=mesh,
        in_specs=placed,
        out_specs=P(("groups", "pass"), None, None),
        check_vma=False,
    )
```

time: 97.6 us -> 98.8 us (1.012)
  local copies, waits for them, and re-layouts: 4.91 us -> 8.14 us
    ppermute x3 -> x4, starting transfers between devices: 7.3 us -> 4.7 us  [to_partner(): return lax.ppermute(x, 'pass', [(i, i ^ 1) for i in range(extent)])]
    ppermute x14 -> x15, starting transfers between devices: 12.3 us -> 14.4 us  [along(): lax.ppermute(x, 'pass', [(2 * s + c, 2 * d + c) for s, d in pairs for c i...]
    unnamed x19 -> x27, local copies, waits for them, and re-layouts: 3.23 us -> 5.13 us
    ppermute x14 -> x15, waiting for transfers between devices: 30.3 us -> 28.8 us  [along(): lax.ppermute(x, 'pass', [(2 * s + c, 2 * d + c) for s, d in pairs for c i...]
    slice x0 -> x2, local copies, waits for them, and re-layouts: none -> 1.33 us  [round_the_ring(): halves = [along_ring(up[-1][:middle], 1), along_ring(down[-1][middle:], -1)]]
    pallas_call x1 -> x2, Pallas kernels: 5.51 us -> 5.53 us  [pool(): pl.pallas_call(pool_kernel, grid=(count,), in_specs=[pl.BlockSpec((1, LEN...]
  transfers between devices with their start and end apart: 17 -> 19, of which waited for: 9 -> 7; matrix products, arithmetic and copies ran while one was open for 1% -> 2% of each run, Pallas kernels for 23% -> 23%
where the time goes in v4:
time: 98.8 us; the launch traced here: 98.5 us
  Pallas kernels  41 us (41%)
  waiting for transfers between devices  30.1 us (30%)
  starting transfers between devices  19.1 us (19%)
  local copies, waits for them, and re-layouts  8.14 us (8%)
    pallas_call x2, Pallas kernels, attend(): pl.pallas_call(functools.partial(attend_kernel, chips), grid_spec=pltpu.P...  33.7 us
    ppermute x15, waiting for transfers between devices, along(): lax.ppermute(x, 'pass', [(2 * s + c, 2 * d + c) for s, d in pairs for c i...  28.8 us
    ppermute x15, starting transfers between devices, along(): lax.ppermute(x, 'pass', [(2 * s + c, 2 * d + c) for s, d in pairs for c i...  14.4 us
    pallas_call x2, Pallas kernels, pool(): pl.pallas_call(pool_kernel, grid=(count,), in_specs=[pl.BlockSpec((1, LEN...  5.53 us
    unnamed x27, local copies, waits for them, and re-layouts  5.13 us
    ppermute x4, starting transfers between devices, to_partner(): return lax.ppermute(x, 'pass', [(i, i ^ 1) for i in range(extent)])  4.7 us
  transfers between devices with their start and end apart: 19, of which 7 were waited for; matrix products, arithmetic and copies ran while one was open for 2% of the time, Pallas kernels for 23%

profile of v4, /device:TPU:1, one launch (start us, length us, event | category | flops | bytes accessed | tf_op | source)
XLA Modules:
  0.0 98.5 jit_solution(15151769008038907526)
XLA Ops:
  0.0 1.0 constant_dynamic-slice_fusion.3
  1.0 0.1 collective-permute-start
  1.1 1.3 %collective-permute-done = bf16[256,256]{1,0:T(8,128)(2,1)S(1)} collective-permute-done((bf16[256,256]{1,0:T(8,128)(2,1)S(1)}, bf16[256,256]{1,0:T(8,128)(2,1)S(1)}, u32[]{:S(2)}, u32[]{:S(2)}) %collective-permute-start) | collective-permute-done | bytes 131104 | tf_op jit(solution)/shard_map/ppermute | solution.py:336
  2.4 2.4 %collective-permute-start.7 = (bf16[512,256]{1,0:T(8,128)(2,1)S(1)}, bf16[512,256]{1,0:T(8,128)(2,1)S(1)}, u32[]{:S(2)}, u32[]{:S(2)}) collective-permute-start(bf16[512,256]{1,0:T(8,128)(2,1)S(1)} %pad_maximum_fusion.rest_4_), channel_id=1, source_target_pairs={{0,2},{1,3},{2,6},{3,7},{4,0},{5,1},{6,10},{7,11},{8,4},{9,5},{10,... | collective-permute-start | bytes 786440 | tf_op jit(solution)/shard_map/ppermute | solution.py:340
  4.8 0.2 collective-permute-start.3
  5.0 6.3 %collective-permute-done.7.rest_12_ = bf16[512,256]{1,0:T(8,128)(2,1)S(1)} collective-permute-done((bf16[512,256]{1,0:T(8,128)(2,1)S(1)}, bf16[512,256]{1,0:T(8,128)(2,1)S(1)}, u32[]{:S(2)}, u32[]{:S(2)}) %collective-permute-start.7) | collective-permute-done | bytes 262176 | tf_op jit(solution)/shard_map/ppermute | solution.py:340
  11.3 1.1 %collective-permute-start.8 = (bf16[512,256]{1,0:T(8,128)(2,1)S(1)}, bf16[512,256]{1,0:T(8,128)(2,1)S(1)}, u32[]{:S(2)}, u32[]{:S(2)}) collective-permute-start(bf16[512,256]{1,0:T(8,128)(2,1)S(1)} %collective-permute-done.7.rest_12_), channel_id=1, source_target_pairs={{0,2},{1,3},{2,6},{3,7},{4,0},{5,1},{6,10},{7,11},{8,4},{9,5},{10,... | collective-permute-start | bytes 786440 | tf_op jit(solution)/shard_map/ppermute | solution.py:340
  12.4 0.0 collective-permute-done.3.rest_5_
  12.4 0.4 collective-permute-start.4
  12.8 0.7 reshape.17.gain_ref
  13.5 0.0 copy-start
  13.5 2.2 %copy-done = bf16[4,128,4096]{2,1,0:T(8,128)(2,1)S(1)} copy-done((bf16[4,128,4096]{2,1,0:T(8,128)(2,1)S(1)}, bf16[4,128,4096]{2,1,0:T(8,128)(2,1)}, u32[]{:S(2)}) %copy-start) | copy-done | bytes 4194328
  15.7 0.9 copy-done.1
  16.6 2.8 %pool.3.rest_1_ = bf16[64,4096]{1,0:T(8,128)(2,1)S(1)} custom-call(bf16[4,128,4096]{2,1,0:T(8,128)(2,1)S(1)} %copy-done, bf16[32,4096]{1,0:T(8,128)(2,1)S(1)} %copy-done.1, bf16[1,4096]{1,0:T(2,128)(2,1)S(1)} %reshape.17.gain_ref), custom_call_target="tpu_custom_call" | custom-call | flops 134217728 | bytes 2097152 | tf_op jit(solution)/shard_map/pool/pallas_call | solution.py:84
  19.4 2.8 %pool.2.rest_0_ = bf16[64,4096]{1,0:T(8,128)(2,1)S(1)} custom-call(bf16[4,128,4096]{2,1,0:T(8,128)(2,1)S(1)} %copy-done, bf16[32,4096]{1,0:T(8,128)(2,1)S(1)} %copy-done.1, bf16[1,4096]{1,0:T(2,128)(2,1)S(1)} %reshape.17.gain_ref), custom_call_target="tpu_custom_call" | custom-call | flops 134217728 | bytes 2097152 | tf_op jit(solution)/shard_map/pool/pallas_call | solution.py:84
  22.2 0.0 copy-start.8
  22.2 0.0 copy-start.9
  22.2 1.5 %collective-permute-start.1 = (bf16[64,4096]{1,0:T(8,128)(2,1)S(1)}, bf16[64,4096]{1,0:T(8,128)(2,1)S(1)}, u32[]{:S(2)}, u32[]{:S(2)}) collective-permute-start(bf16[64,4096]{1,0:T(8,128)(2,1)S(1)} %pool.2.rest_0_), channel_id=1, source_target_pairs={{0,1},{1,0},{2,3},{3,2},{4,5},{5,4},{6,7},{7,6},{8,9},{9,8},{10,11... | collective-permute-start | bytes 1572872 | tf_op jit(solution)/shard_map/ppermute | solution.py:336
  23.7 0.1 collective-permute-start.2
  23.8 0.0 collective-permute-done.8.rest_11_
  23.8 0.0 copy-start.2
  23.8 1.4 %collective-permute-start.9 = (bf16[512,256]{1,0:T(8,128)(2,1)S(1)}, bf16[512,256]{1,0:T(8,128)(2,1)S(1)}, u32[]{:S(2)}, u32[]{:S(2)}) collective-permute-start(bf16[512,256]{1,0:T(8,128)(2,1)S(1)} %collective-permute-done.8.rest_11_), channel_id=1, source_target_pairs={{0,2},{1,3},{2,6},{3,7},{4,0},{5,1},{6,10},{7,11},{8,4},{9,5},{10,... | collective-permute-start | bytes 786440 | tf_op jit(solution)/shard_map/ppermute | solution.py:340
  25.2 0.0 collective-permute-done.4.rest_6_
  25.2 0.0 copy-start.4
  25.2 0.2 collective-permute-start.5
  25.3 5.9 %collective-permute-done.9.rest_10_ = bf16[512,256]{1,0:T(8,128)(2,1)S(1)} collective-permute-done((bf16[512,256]{1,0:T(8,128)(2,1)S(1)}, bf16[512,256]{1,0:T(8,128)(2,1)S(1)}, u32[]{:S(2)}, u32[]{:S(2)}) %collective-permute-start.9) | collective-permute-done | bytes 262176 | tf_op jit(solution)/shard_map/ppermute | solution.py:340
  31.2 0.7 slice.9
  31.9 1.4 %collective-permute-start.10 = (bf16[256,256]{1,0:T(8,128)(2,1)}, bf16[256,256]{1,0:T(8,128)(2,1)S(1)}, u32[]{:S(2)}, u32[]{:S(2)}) collective-permute-start(bf16[256,256]{1,0:T(8,128)(2,1)} %slice.9), channel_id=1, source_target_pairs={{0,2},{1,3},{2,6},{3,7},{4,0},{5,1},{6,10},{7,11},{8,4},{9,5},{10,... | collective-permute-start | bytes 393224 | tf_op jit(solution)/shard_map/ppermute | solution.py:340
  33.3 0.0 collective-permute-done.5.rest_7_
  33.3 0.0 copy-done.2
  33.3 0.7 slice.8
  34.0 0.0 copy-done.4
  34.0 0.1 collective-permute-start.6
  34.0 0.0 collective-permute-done.1.rest_2_
  34.0 0.0 collective-permute-done.2.rest_3_
  34.1 1.9 %collective-permute-done.10.rest_9_ = bf16[256,256]{1,0:T(8,128)(2,1)S(1)} collective-permute-done((bf16[256,256]{1,0:T(8,128)(2,1)}, bf16[256,256]{1,0:T(8,128)(2,1)S(1)}, u32[]{:S(2)}, u32[]{:S(2)}) %collective-permute-start.10) | collective-permute-done | bytes 131104 | tf_op jit(solution)/shard_map/ppermute | solution.py:340
  35.9 2.2 %collective-permute-done.6.rest_8_ = bf16[256,256]{1,0:T(8,128)(2,1)} collective-permute-done((bf16[256,256]{1,0:T(8,128)(2,1)}, bf16[256,256]{1,0:T(8,128)(2,1)}, u32[]{:S(2)}, u32[]{:S(2)}) %collective-permute-start.6) | collective-permute-done | bytes 131104 | tf_op jit(solution)/shard_map/ppermute | solution.py:340
  38.1 0.0 copy-start.3
  38.1 0.9 copy-done.3
  39.0 0.0 copy-start.5
  39.0 0.9 copy-done.5
  40.0 1.8 %project.1 = bf16[256,256]{1,0:T(8,128)(2,1)S(1)} custom-call(s32[1]{0:T(128)} %bitcast.2.core_ref.half_ref, s32[1]{0:T(128)} %bitcast.1.place_ref, bf16[64,4096]{1,0:T(8,128)(2,1)S(1)} %pool.2.rest_0_, bf16[64,4096]{1,0:T(8,128)(2,1)S(1)} %pool.3.rest_1_, bf16[64,4096]{1,0:T(8,128)(2,1)S(1)} %collective-permute-done.1.rest_2_, ...), custom_call_target="tpu_custom_call" | custom-call | flops 536870912 | bytes 2097152 | tf_op jit(solution)/shard_map/project/pallas_call | solution.py:293
  41.8 2.5 %collective-permute-start.13 = (bf16[256,256]{1,0:T(8,128)(2,1)S(1)}, bf16[256,256]{1,0:T(8,128)(2,1)S(1)}, u32[]{:S(2)}, u32[]{:S(2)}) collective-permute-start(bf16[256,256]{1,0:T(8,128)(2,1)S(1)} %project.1), channel_id=1, source_target_pairs={{0,12},{1,13},{2,14},{3,15},{4,0},{5,1},{6,2},{7,3},{8,4},{9,5},{1... | collective-permute-start | bytes 393224 | tf_op jit(solution)/shard_map/ppermute | solution.py:340
  44.3 0.0 collective-permute-start.12
  44.3 0.5 collective-permute-start.11
  44.8 2.1 %collective-permute-start.14 = (bf16[256,256]{1,0:T(8,128)(2,1)S(1)}, bf16[256,256]{1,0:T(8,128)(2,1)S(1)}, u32[]{:S(2)}, u32[]{:S(2)}) collective-permute-start(bf16[256,256]{1,0:T(8,128)(2,1)S(1)} %project.1), channel_id=1, source_target_pairs={{0,2},{1,3},{2,0},{3,1},{4,6},{5,7},{6,4},{7,5},{8,10},{9,11},{10,... | collective-permute-start | bytes 393224 | tf_op jit(solution)/shard_map/ppermute | solution.py:340
  46.9 0.0 collective-permute-done.13
  46.9 0.6 collective-permute-start.17
  47.6 8.0 %collective-permute-done.12 = bf16[256,256]{1,0:T(8,128)(2,1)S(1)} collective-permute-done((bf16[256,256]{1,0:T(8,128)(2,1)S(1)}, bf16[256,256]{1,0:T(8,128)(2,1)S(1)}, u32[]{:S(2)}, u32[]{:S(2)}) %collective-permute-start.12) | collective-permute-done | bytes 131104 | tf_op jit(solution)/shard_map/ppermute | solution.py:340
  55.6 1.6 %collective-permute-start.16 = (bf16[256,256]{1,0:T(8,128)(2,1)S(1)}, bf16[256,256]{1,0:T(8,128)(2,1)S(1)}, u32[]{:S(2)}, u32[]{:S(2)}) collective-permute-start(bf16[256,256]{1,0:T(8,128)(2,1)S(1)} %collective-permute-done.12), channel_id=1, source_target_pairs={{0,2},{1,3},{2,0},{3,1},{4,6},{5,7},{6,4},{7,5},{8,10},{9,11},{10,... | collective-permute-start | bytes 393224 | tf_op jit(solution)/shard_map/ppermute | solution.py:340
  57.2 0.0 collective-permute-done.11
  57.2 0.0 collective-permute-start.15
  57.3 0.0 collective-permute-done.14
  57.3 4.4 %collective-permute-done.15 = bf16[256,256]{1,0:T(8,128)(2,1)S(1)} collective-permute-done((bf16[256,256]{1,0:T(8,128)(2,1)S(1)}, bf16[256,256]{1,0:T(8,128)(2,1)S(1)}, u32[]{:S(2)}, u32[]{:S(2)}) %collective-permute-start.15) | collective-permute-done | bytes 131104 | tf_op jit(solution)/shard_map/ppermute | solution.py:340
  61.8 0.0 collective-permute-done.16
  61.8 0.0 collective-permute-done.17
  61.8 3.0 %collective-permute-start.18 = (bf16[2048,256]{1,0:T(8,128)(2,1)S(1)}, bf16[2048,256]{1,0:T(8,128)(2,1)S(1)}, u32[]{:S(2)}, u32[]{:S(2)}) collective-permute-start(bf16[2048,256]{1,0:T(8,128)(2,1)S(1)} %constant_dynamic-update-slice_fusion.k_ref.v_ref), channel_id=1, source_target_pairs={{0,1},{1,0},{2,3},{3,2},{4,5},{5,4},{6,7},{7,6},{8,9},{9,8},{10,11... | collective-permute-start | bytes 3145736 | tf_op jit(solution)/shard_map/ppermute | solution.py:336
  64.8 0.0 copy-done.8
  64.8 0.0 copy-done.9
  64.8 0.0 copy-done.6
  64.8 0.0 copy-done.7
  64.8 16.8 %attend.2.rest_0_ = bf16[4,64,7424]{2,1,0:T(8,128)(2,1)} custom-call(s32[1]{0:T(128)} %bitcast.2.core_ref.half_ref, s32[1]{0:T(128)} %bitcast.1.place_ref, s32[4,16]{1,0:T(4,128)S(1)} %copy-done.8, s32[4]{0:T(128)S(1)} %copy-done.9, bf16[4,64,7424]{2,1,0:T(8,128)(2,1)S(1)} %copy-done.6, bf16[2048,256]{1,0:T(8,128)(2,1)S(1)} %constant_dynamic-update-slice_fusion.k_ref.v_ref, ...), custom_call_target="tpu_custom_call" | custom-call | flops 2189426688 | bytes 4849664 | tf_op jit(solution)/shard_map/attend/pallas_call | solution.py:237
  81.7 0.0 collective-permute-done.18.k_ref.v_ref
  81.7 16.8 %attend.3 = bf16[4,64,7424]{2,1,0:T(8,128)(2,1)} custom-call(s32[1]{0:T(128)} %bitcast.half_ref, s32[1]{0:T(128)} %bitcast.1.place_ref, s32[4,16]{1,0:T(4,128)S(1)} %copy-done.8, s32[4]{0:T(128)S(1)} %copy-done.9, bf16[4,64,7424]{2,1,0:T(8,128)(2,1)S(1)} %copy-done.6, ...), custom_call_target="tpu_custom_call", output_to_operand_aliasing={{}: (9, {})} | custom-call | flops 2189426688 | bytes 4849664 | tf_op jit(solution)/shard_map/attend/pallas_call | solution.py:237
  (13 shorter events, 0.1 us)
Async XLA Ops:
  1.0 1.4 %collective-permute-start = (bf16[256,256]{1,0:T(8,128)(2,1)S(1)}, bf16[256,256]{1,0:T(8,128)(2,1)S(1)}, u32[]{:S(2)}, u32[]{:S(2)}) collective-permute-start(bf16[256,256]{1,0:T(8,128)(2,1)S(1)} %pad_maximum_fusion.1), channel_id=1, source_target_pairs={{0,1},{1,0},{2,3},{3,2},{4,5},{5,4},{6,7},{7,6},{8,9},{9,8},{10,11... | collective-permute-start | bytes 393224 | tf_op jit(solution)/shard_map/ppermute | solution.py:336
  2.4 8.9 %collective-permute-start.7 = (bf16[512,256]{1,0:T(8,128)(2,1)S(1)}, bf16[512,256]{1,0:T(8,128)(2,1)S(1)}, u32[]{:S(2)}, u32[]{:S(2)}) collective-permute-start(bf16[512,256]{1,0:T(8,128)(2,1)S(1)} %pad_maximum_fusion.rest_4_), channel_id=1, source_target_pairs={{0,2},{1,3},{2,6},{3,7},{4,0},{5,1},{6,10},{7,11},{8,4},{9,5},{10,... | collective-permute-start | bytes 786440 | tf_op jit(solution)/shard_map/ppermute | solution.py:340
  4.8 7.5 %collective-permute-start.3 = (bf16[512,256]{1,0:T(8,128)(2,1)S(1)}, bf16[512,256]{1,0:T(8,128)(2,1)S(1)}, u32[]{:S(2)}, u32[]{:S(2)}) collective-permute-start(bf16[512,256]{1,0:T(8,128)(2,1)S(1)} %pad_maximum_fusion.rest_4_), channel_id=1, source_target_pairs={{0,4},{1,5},{2,0},{3,1},{4,8},{5,9},{6,2},{7,3},{8,12},{9,13},{10,... | collective-permute-start | bytes 786440 | tf_op jit(solution)/shard_map/ppermute | solution.py:340
  11.3 12.5 %collective-permute-start.8 = (bf16[512,256]{1,0:T(8,128)(2,1)S(1)}, bf16[512,256]{1,0:T(8,128)(2,1)S(1)}, u32[]{:S(2)}, u32[]{:S(2)}) collective-permute-start(bf16[512,256]{1,0:T(8,128)(2,1)S(1)} %collective-permute-done.7.rest_12_), channel_id=1, source_target_pairs={{0,2},{1,3},{2,6},{3,7},{4,0},{5,1},{6,10},{7,11},{8,4},{9,5},{10,... | collective-permute-start | bytes 786440 | tf_op jit(solution)/shard_map/ppermute | solution.py:340
  12.4 12.8 %collective-permute-start.4 = (bf16[512,256]{1,0:T(8,128)(2,1)S(1)}, bf16[512,256]{1,0:T(8,128)(2,1)S(1)}, u32[]{:S(2)}, u32[]{:S(2)}) collective-permute-start(bf16[512,256]{1,0:T(8,128)(2,1)S(1)} %collective-permute-done.3.rest_5_), channel_id=1, source_target_pairs={{0,4},{1,5},{2,0},{3,1},{4,8},{5,9},{6,2},{7,3},{8,12},{9,13},{10,... | collective-permute-start | bytes 786440 | tf_op jit(solution)/shard_map/ppermute | solution.py:340
  13.5 2.2 %copy-start = (bf16[4,128,4096]{2,1,0:T(8,128)(2,1)S(1)}, bf16[4,128,4096]{2,1,0:T(8,128)(2,1)}, u32[]{:S(2)}) copy-start(bf16[4,128,4096]{2,1,0:T(8,128)(2,1)} %states_ref.3) | copy-start | bytes 12582916
  15.7 0.9 copy-start.1
  22.2 42.6 %copy-start.8 = (s32[4,16]{1,0:T(4,128)S(1)}, s32[4,16]{1,0:T(4,128)}, u32[]{:S(2)}) copy-start(s32[4,16]{1,0:T(4,128)} %passage_ref.3) | copy-start | bytes 772
  22.2 42.6 %copy-start.9 = (s32[4]{0:T(128)S(1)}, s32[4]{0:T(128)}, u32[]{:S(2)}) copy-start(s32[4]{0:T(128)} %length_ref.3) | copy-start | bytes 52
  22.2 11.8 %collective-permute-start.1 = (bf16[64,4096]{1,0:T(8,128)(2,1)S(1)}, bf16[64,4096]{1,0:T(8,128)(2,1)S(1)}, u32[]{:S(2)}, u32[]{:S(2)}) collective-permute-start(bf16[64,4096]{1,0:T(8,128)(2,1)S(1)} %pool.2.rest_0_), channel_id=1, source_target_pairs={{0,1},{1,0},{2,3},{3,2},{4,5},{5,4},{6,7},{7,6},{8,9},{9,8},{10,11... | collective-permute-start | bytes 1572872 | tf_op jit(solution)/shard_map/ppermute | solution.py:336
  23.7 10.3 %collective-permute-start.2 = (bf16[64,4096]{1,0:T(8,128)(2,1)S(1)}, bf16[64,4096]{1,0:T(8,128)(2,1)S(1)}, u32[]{:S(2)}, u32[]{:S(2)}) collective-permute-start(bf16[64,4096]{1,0:T(8,128)(2,1)S(1)} %pool.3.rest_1_), channel_id=1, source_target_pairs={{0,1},{1,0},{2,3},{3,2},{4,5},{5,4},{6,7},{7,6},{8,9},{9,8},{10,11... | collective-permute-start | bytes 1572872 | tf_op jit(solution)/shard_map/ppermute | solution.py:336
  23.8 9.5 %copy-start.2 = (bf16[512,256]{1,0:T(8,128)(2,1)}, bf16[512,256]{1,0:T(8,128)(2,1)S(1)}, u32[]{:S(2)}) copy-start(bf16[512,256]{1,0:T(8,128)(2,1)S(1)} %collective-permute-done.8.rest_11_) | copy-start | bytes 786436
  23.8 7.4 %collective-permute-start.9 = (bf16[512,256]{1,0:T(8,128)(2,1)S(1)}, bf16[512,256]{1,0:T(8,128)(2,1)S(1)}, u32[]{:S(2)}, u32[]{:S(2)}) collective-permute-start(bf16[512,256]{1,0:T(8,128)(2,1)S(1)} %collective-permute-done.8.rest_11_), channel_id=1, source_target_pairs={{0,2},{1,3},{2,6},{3,7},{4,0},{5,1},{6,10},{7,11},{8,4},{9,5},{10,... | collective-permute-start | bytes 786440 | tf_op jit(solution)/shard_map/ppermute | solution.py:340
  25.2 8.8 %copy-start.4 = (bf16[512,256]{1,0:T(8,128)(2,1)}, bf16[512,256]{1,0:T(8,128)(2,1)S(1)}, u32[]{:S(2)}) copy-start(bf16[512,256]{1,0:T(8,128)(2,1)S(1)} %collective-permute-done.4.rest_6_) | copy-start | bytes 786436
  25.2 8.1 %collective-permute-start.5 = (bf16[512,256]{1,0:T(8,128)(2,1)S(1)}, bf16[512,256]{1,0:T(8,128)(2,1)S(1)}, u32[]{:S(2)}, u32[]{:S(2)}) collective-permute-start(bf16[512,256]{1,0:T(8,128)(2,1)S(1)} %collective-permute-done.4.rest_6_), channel_id=1, source_target_pairs={{0,4},{1,5},{2,0},{3,1},{4,8},{5,9},{6,2},{7,3},{8,12},{9,13},{10,... | collective-permute-start | bytes 786440 | tf_op jit(solution)/shard_map/ppermute | solution.py:340
  31.9 4.0 %collective-permute-start.10 = (bf16[256,256]{1,0:T(8,128)(2,1)}, bf16[256,256]{1,0:T(8,128)(2,1)S(1)}, u32[]{:S(2)}, u32[]{:S(2)}) collective-permute-start(bf16[256,256]{1,0:T(8,128)(2,1)} %slice.9), channel_id=1, source_target_pairs={{0,2},{1,3},{2,6},{3,7},{4,0},{5,1},{6,10},{7,11},{8,4},{9,5},{10,... | collective-permute-start | bytes 393224 | tf_op jit(solution)/shard_map/ppermute | solution.py:340
  34.0 4.1 %collective-permute-start.6 = (bf16[256,256]{1,0:T(8,128)(2,1)}, bf16[256,256]{1,0:T(8,128)(2,1)}, u32[]{:S(2)}, u32[]{:S(2)}) collective-permute-start(bf16[256,256]{1,0:T(8,128)(2,1)} %slice.8), channel_id=1, source_target_pairs={{0,4},{1,5},{2,0},{3,1},{4,8},{5,9},{6,2},{7,3},{8,12},{9,13},{10,... | collective-permute-start | bytes 393224 | tf_op jit(solution)/shard_map/ppermute | solution.py:340
  38.1 1.0 copy-start.3
  39.0 0.9 copy-start.5
  40.0 24.8 %copy-start.6 = (bf16[4,64,7424]{2,1,0:T(8,128)(2,1)S(1)}, bf16[4,64,7424]{2,1,0:T(8,128)(2,1)}, u32[]{:S(2)}) copy-start(bf16[4,64,7424]{2,1,0:T(8,128)(2,1)} %q_ref.3) | copy-start | bytes 11403268
  40.0 24.8 %copy-start.7 = (bf16[4,64,512]{2,1,0:T(8,128)(2,1)S(1)}, bf16[4,64,512]{2,1,0:T(8,128)(2,1)}, u32[]{:S(2)}) copy-start(bf16[4,64,512]{2,1,0:T(8,128)(2,1)} %own_v_ref.3) | copy-start | bytes 786436
  41.8 5.1 %collective-permute-start.13 = (bf16[256,256]{1,0:T(8,128)(2,1)S(1)}, bf16[256,256]{1,0:T(8,128)(2,1)S(1)}, u32[]{:S(2)}, u32[]{:S(2)}) collective-permute-start(bf16[256,256]{1,0:T(8,128)(2,1)S(1)} %project.1), channel_id=1, source_target_pairs={{0,12},{1,13},{2,14},{3,15},{4,0},{5,1},{6,2},{7,3},{8,4},{9,5},{1... | collective-permute-start | bytes 393224 | tf_op jit(solution)/shard_map/ppermute | solution.py:340
  44.3 11.3 %collective-permute-start.12 = (bf16[256,256]{1,0:T(8,128)(2,1)S(1)}, bf16[256,256]{1,0:T(8,128)(2,1)S(1)}, u32[]{:S(2)}, u32[]{:S(2)}) collective-permute-start(bf16[256,256]{1,0:T(8,128)(2,1)S(1)} %project.1), channel_id=1, source_target_pairs={{0,8},{1,9},{2,10},{3,11},{4,12},{5,13},{6,14},{7,15},{8,0},{9,1},... | collective-permute-start | bytes 393224 | tf_op jit(solution)/shard_map/ppermute | solution.py:340
  44.3 12.9 %collective-permute-start.11 = (bf16[256,256]{1,0:T(8,128)(2,1)S(1)}, bf16[256,256]{1,0:T(8,128)(2,1)S(1)}, u32[]{:S(2)}, u32[]{:S(2)}) collective-permute-start(bf16[256,256]{1,0:T(8,128)(2,1)S(1)} %project.1), channel_id=1, source_target_pairs={{0,4},{1,5},{2,6},{3,7},{4,8},{5,9},{6,10},{7,11},{8,12},{9,13},{1... | collective-permute-start | bytes 393224 | tf_op jit(solution)/shard_map/ppermute | solution.py:340
  44.8 12.5 %collective-permute-start.14 = (bf16[256,256]{1,0:T(8,128)(2,1)S(1)}, bf16[256,256]{1,0:T(8,128)(2,1)S(1)}, u32[]{:S(2)}, u32[]{:S(2)}) collective-permute-start(bf16[256,256]{1,0:T(8,128)(2,1)S(1)} %project.1), channel_id=1, source_target_pairs={{0,2},{1,3},{2,0},{3,1},{4,6},{5,7},{6,4},{7,5},{8,10},{9,11},{10,... | collective-permute-start | bytes 393224 | tf_op jit(solution)/shard_map/ppermute | solution.py:340
  46.9 14.9 %collective-permute-start.17 = (bf16[256,256]{1,0:T(8,128)(2,1)S(1)}, bf16[256,256]{1,0:T(8,128)(2,1)S(1)}, u32[]{:S(2)}, u32[]{:S(2)}) collective-permute-start(bf16[256,256]{1,0:T(8,128)(2,1)S(1)} %collective-permute-done.13), channel_id=1, source_target_pairs={{0,2},{1,3},{2,0},{3,1},{4,6},{5,7},{6,4},{7,5},{8,10},{9,11},{10,... | collective-permute-start | bytes 393224 | tf_op jit(solution)/shard_map/ppermute | solution.py:340
  55.6 6.2 %collective-permute-start.16 = (bf16[256,256]{1,0:T(8,128)(2,1)S(1)}, bf16[256,256]{1,0:T(8,128)(2,1)S(1)}, u32[]{:S(2)}, u32[]{:S(2)}) collective-permute-start(bf16[256,256]{1,0:T(8,128)(2,1)S(1)} %collective-permute-done.12), channel_id=1, source_target_pairs={{0,2},{1,3},{2,0},{3,1},{4,6},{5,7},{6,4},{7,5},{8,10},{9,11},{10,... | collective-permute-start | bytes 393224 | tf_op jit(solution)/shard_map/ppermute | solution.py:340
  57.2 4.6 %collective-permute-start.15 = (bf16[256,256]{1,0:T(8,128)(2,1)S(1)}, bf16[256,256]{1,0:T(8,128)(2,1)S(1)}, u32[]{:S(2)}, u32[]{:S(2)}) collective-permute-start(bf16[256,256]{1,0:T(8,128)(2,1)S(1)} %collective-permute-done.11), channel_id=1, source_target_pairs={{0,2},{1,3},{2,0},{3,1},{4,6},{5,7},{6,4},{7,5},{8,10},{9,11},{10,... | collective-permute-start | bytes 393224 | tf_op jit(solution)/shard_map/ppermute | solution.py:340
  61.8 19.9 %collective-permute-start.18 = (bf16[2048,256]{1,0:T(8,128)(2,1)S(1)}, bf16[2048,256]{1,0:T(8,128)(2,1)S(1)}, u32[]{:S(2)}, u32[]{:S(2)}) collective-permute-start(bf16[2048,256]{1,0:T(8,128)(2,1)S(1)} %constant_dynamic-update-slice_fusion.k_ref.v_ref), channel_id=1, source_target_pairs={{0,1},{1,0},{2,3},{3,2},{4,5},{5,4},{6,7},{7,6},{8,9},{9,8},{10,11... | collective-permute-start | bytes 3145736 | tf_op jit(solution)/shard_map/ppermute | solution.py:336

commit v5 on v4

--- a/solution.py
+++ b/solution.py
@@ -27,8 +27,8 @@
 ROWS = TOPK * MEM
 KEYS = 2 * (ROWS + QLEN)
 NEG = -1e30
+SUM_LOW, SUM_HIGH = 2.0 ** -40, 2.0 ** 60
 POOL_HEADS = 16
-POOL_CALLS = 2
 CHIP = 8
 STEP = 8
 BLOCK = 16
@@ -80,19 +80,20 @@
     out_ref[...] = (pooled[...] * scale * gain_ref[...].astype(jnp.float32)).astype(jnp.bfloat16)
 
 
-def pool(states, queries, gain, first, count):
+def pool(states, queries, gain):
+    count = states.shape[0]
     return pl.pallas_call(
         pool_kernel,
         grid=(count,),
         in_specs=[
-            pl.BlockSpec((1, LEN, D), lambda p: (first + p, 0, 0)),
+            pl.BlockSpec((1, LEN, D), lambda p: (p, 0, 0)),
             pl.BlockSpec((MEM, D), lambda p: (0, 0)),
             pl.BlockSpec((1, D), lambda p: (0, 0)),
         ],
         out_specs=pl.BlockSpec((MEM, D), lambda p: (p, 0)),
         out_shape=jax.ShapeDtypeStruct((count * MEM, D), jnp.bfloat16),
         scratch_shapes=[pltpu.VMEM((MEM, D), jnp.float32)],
-        compiler_params=pltpu.CompilerParams(vmem_limit_bytes=16 * MIB),
+        compiler_params=pltpu.CompilerParams(vmem_limit_bytes=56 * MIB),
         cost_estimate=pl.CostEstimate(
             flops=4 * count * MEM * LEN * D, bytes_accessed=2 * count * LEN * D,
             transcendentals=count * CH * MEM * LEN,
@@ -180,12 +181,27 @@
                 (own - jnp.where(low, tops[0], tops[1])) * factor
             ).astype(jnp.bfloat16)
 
-    def value_product(i):
+    def key_product_plain(i):
+        g, tiles = chunks[i]
+        lhs = jnp.concatenate([q_ref[0, :, t * LANES:(t + 1) * LANES] for t in tiles], axis=0)
+        rows = slice(0, len(tiles) * QLEN)
+        for c in range(0, KEYS, 2 * LANES):
+            part = slice(c, min(c + 2 * LANES, KEYS))
+            got = jnp.dot(lhs, key_side[g, :, part], preferred_element_type=jnp.float32) * factor
+            if c == 2 * ROWS:
+                got = got + jnp.concatenate([bias[...]] * len(tiles), axis=0)
+            weights[i % 2, rows, part] = jnp.exp2(got).astype(jnp.bfloat16)
+
+    def value_product(i, seen=None):
         g, tiles = chunks[i]
         count = len(tiles)
         mixed = jnp.dot(
             weights[i % 2, :count * QLEN, :], value_side[g], preferred_element_type=jnp.float32
         )
+        if seen is not None:
+            for at in range(0, count * QLEN, QLEN):
+                sums = mixed[at:at + QLEN, LANES:]
+                seen = jnp.where((sums > SUM_LOW) & (sums < SUM_HIGH), seen, 1.0)
         for n, t in enumerate(tiles):
             rows = slice(n * QLEN, (n + 1) * QLEN)
             result = jnp.where(alive, mixed[rows, :LANES] / mixed[rows, LANES:], 0.0).astype(jnp.bfloat16)
@@ -193,8 +209,9 @@
             if t == half and g == 1:
                 result = jnp.where(low_tile, out_ref[0, :, at], result)
             out_ref[0, :, at] = result
-
-    key_product(0)
+        return seen
+
+    key_product_plain(0)
 
     memory_v = values[...]
     own_v = own_v_ref[0].astype(jnp.float32)
@@ -211,11 +228,18 @@
             ):
                 value_side[g, start:stop, :LANES] = side.astype(jnp.bfloat16)
 
+    seen = jnp.zeros((QLEN, LANES), jnp.float32)
     for i in range(len(chunks)):
         if i + 1 < len(chunks):
-            key_product(i + 1)
-        softmax(i)
-        value_product(i)
+            key_product_plain(i + 1)
+        seen = value_product(i, seen)
+
+    @pl.when(jnp.max(seen) > 0.0)
+    def _():
+        for i in range(len(chunks)):
+            key_product(i)
+            softmax(i)
+            value_product(i)
 
 
 def attend(chips, half, place, retrieval, lengths, questions, memory_kv, own_kv, earlier=None):
@@ -253,7 +277,7 @@
         ),
         out_shape=jax.ShapeDtypeStruct((count, QLEN, H * HD), jnp.bfloat16),
         input_output_aliases=aliases,
-        compiler_params=pltpu.CompilerParams(vmem_limit_bytes=36 * MIB),
+        compiler_params=pltpu.CompilerParams(vmem_limit_bytes=48 * MIB),
         cost_estimate=pl.CostEstimate(
             flops=2 * count * QLEN * H * HD * (ROWS + QLEN),
             bytes_accessed=2 * count * QLEN * H * HD + total * KVW,
@@ -264,35 +288,30 @@
 
 
 def project_kernel(ring, core_ref, place_ref, *rest):
-    row_refs, weights, out_ref = rest[:2 * POOL_CALLS], rest[2 * POOL_CALLS:-1], rest[-1]
-    count = POOL_CALLS * row_refs[0].shape[0]
-    depth = weights[0].shape[0] // 2
-    pieces = []
-    for i in range(ring):
-        if i == ring // 2:
-            pieces += [(i, 0, weights[i], 0), (i, 1, weights[i + 1], 0)]
-        else:
-            pieces += [(i, part, weights[i + (i > ring // 2)], part * depth) for part in range(2)]
+    own_ref, other_ref, *weights, out_ref = rest
+    count = own_ref.shape[0]
+    depth = weights[0].shape[0]
     total = jnp.zeros((2 * count, weights[0].shape[1]), jnp.float32)
     core = core_ref[0]
-    for i, part, weight, top in pieces:
+    for n, weight in enumerate(weights):
+        part, i = n // ring, n % ring
         chip = chip_at(lax.rem(ring + place_ref[0] - i, ring), ring)
         at = pl.multiple_of((2 * chip + (1 - core if part else core)) * depth, depth)
-        rows = jnp.concatenate([x[:, pl.ds(at, depth)] for x in row_refs], axis=0)
-        total += jnp.dot(rows, weight[top:top + depth], preferred_element_type=jnp.float32)
+        rows = jnp.concatenate([own_ref[:, pl.ds(at, depth)], other_ref[:, pl.ds(at, depth)]], axis=0)
+        total += jnp.dot(rows, weight[...], preferred_element_type=jnp.float32)
     result = total.astype(jnp.bfloat16)
     out_ref[pl.ds(pl.multiple_of(core * count, count), count)] = result[:count]
     out_ref[pl.ds(pl.multiple_of((1 - core) * count, count), count)] = result[count:]
 
 
 def project(core, place, own_rows, other_rows, weights):
-    count = POOL_CALLS * own_rows[0].shape[0]
+    count = own_rows.shape[0]
     width = weights[0].shape[1]
     vmem = pl.BlockSpec(memory_space=pltpu.VMEM)
     smem = pl.BlockSpec(memory_space=pltpu.SMEM)
     return pl.pallas_call(
-        functools.partial(project_kernel, len(weights) - 1),
-        in_specs=[smem, smem] + [vmem] * (2 * POOL_CALLS + len(weights)),
+        functools.partial(project_kernel, len(weights) // 2),
+        in_specs=[smem, smem] + [vmem] * (2 + len(weights)),
         out_specs=vmem,
         out_shape=jax.ShapeDtypeStruct((2 * count, width), jnp.bfloat16),
         compiler_params=pltpu.CompilerParams(vmem_limit_bytes=16 * MIB),
@@ -300,7 +319,7 @@
             flops=4 * count * D * width, bytes_accessed=2 * D * width, transcendentals=0
         ),
         name="project",
-    )(core.reshape(1), place, *own_rows, *other_rows, *weights)
+    )(core.reshape(1), place, own_rows, other_rows, *weights)
 
 
 def local(
@@ -320,7 +339,7 @@
     depth = kv_weight.shape[0]
 
     if chips != 8 or depth % LANES:
-        memory_rows = pool(passage_states, memory_queries, memory_gain, 0, passage_states.shape[0])
+        memory_rows = pool(passage_states, memory_queries, memory_gain)
         whole_weight = lax.all_gather(kv_weight, "pass", axis=0, tiled=True)
         memory_kv = jnp.dot(memory_rows, whole_weight, preferred_element_type=jnp.float32)
         everything = lax.all_gather(memory_kv.astype(jnp.bfloat16), "pass", axis=0, tiled=True)
@@ -342,14 +361,13 @@
     def along_ring(x, step):
         return along(x, lambda line, lane: order[(order.index(2 * line + lane) + step) % chips])
 
-    def round_the_ring(block):
-        up, down = [block], [block]
-        for i in range(1, chips // 2):
+    def round_the_ring(x, up, down, rounds):
+        up, down = [x, up], [down]
+        while len(up) <= rounds:
             up.append(along_ring(up[-1], 1))
+        while len(up) + len(down) < chips:
             down.append(along_ring(down[-1], -1))
-        middle = block.shape[0] // 2
-        halves = [along_ring(up[-1][:middle], 1), along_ring(down[-1][middle:], -1)]
-        return up + halves + down[:0:-1]
+        return up + down[::-1]
 
     def line_by_line(block):
         lines = chips // 2
@@ -367,14 +385,13 @@
             axis=1,
         )
 
-    weight = jnp.concatenate([columns(core), to_partner(columns(1 - core))], axis=0)
-    weight, memory_queries = lax.optimization_barrier((weight, memory_queries))
-    weights = round_the_ring(weight)
-    part = passage_states.shape[0] // POOL_CALLS
-    memory_rows = [
-        pool(passage_states, memory_queries, memory_gain, i * part, part) for i in range(POOL_CALLS)
-    ]
-    memory_kv = project(core, place, memory_rows, [to_partner(x) for x in memory_rows], weights)
+    pieces = [columns(core), to_partner(columns(1 - core))]
+    hops = [along_ring(x, step) for x in pieces for step in (1, -1)]
+    memory_rows = pool(passage_states, memory_queries, memory_gain)
+    *hops, memory_rows = lax.optimization_barrier((*hops, memory_rows))
+    weights = round_the_ring(pieces[0], hops[0], hops[1], chips // 2)
+    weights += round_the_ring(pieces[1], hops[2], hops[3], chips // 2 - 1)
+    memory_kv = project(core, place, memory_rows, to_partner(memory_rows), weights)
     near = jnp.concatenate(line_by_line(memory_kv), axis=0)
     far = to_partner(near)
 

time: 98.8 us -> 115 us (1.16)
  Pallas kernels: 41 us -> 65.4 us
  waiting for transfers between devices: 30.1 us -> 24.6 us
  local copies, waits for them, and re-layouts: 8.14 us -> 3.58 us
  starting transfers between devices: 19.1 us -> 21.2 us
    pallas_call x2, Pallas kernels: 33.7 us -> 57 us  [attend(): pl.pallas_call(functools.partial(attend_kernel, chips), grid_spec=pltpu.P...]
    ppermute x15 -> x21, waiting for transfers between devices: 28.8 us -> 24.6 us  [along(): lax.ppermute(x, 'pass', [(2 * s + c, 2 * d + c) for s, d in pairs for c i...]
    unnamed x27 -> x17, local copies, waits for them, and re-layouts: 5.13 us -> 1.31 us
    ppermute x15 -> x21, starting transfers between devices: 14.4 us -> 17.4 us  [along(): lax.ppermute(x, 'pass', [(2 * s + c, 2 * d + c) for s, d in pairs for c i...]
    pallas_call x2 -> x1, Pallas kernels: 5.53 us -> 7.75 us  [pool(): pl.pallas_call(pool_kernel, grid=(count,), in_specs=[pl.BlockSpec((1, LEN...]
    slice x2 -> x0, local copies, waits for them, and re-layouts: 1.33 us -> none  [round_the_ring(): halves = [along_ring(up[-1][:middle], 1), along_ring(down[-1][middle:], -1)]]
    ppermute x4 -> x3, waiting for transfers between devices: 1.3 us -> 0.01 us  [to_partner(): return lax.ppermute(x, 'pass', [(i, i ^ 1) for i in range(extent)])]
    ppermute x4 -> x3, starting transfers between devices: 4.7 us -> 3.81 us  [to_partner(): return lax.ppermute(x, 'pass', [(i, i ^ 1) for i in range(extent)])]
  transfers between devices with their start and end apart: 19 -> 24, of which waited for: 7 -> 8; matrix products, arithmetic and copies ran while one was open for 2% -> 1% of each run, Pallas kernels for 23% -> 31%
where the time goes in v5:
time: 115 us
  Pallas kernels  65.4 us (57%)
  waiting for transfers between devices  24.6 us (21%)
  starting transfers between devices  21.2 us (18%)
  local copies, waits for them, and re-layouts  3.58 us (3%)
    pallas_call x2, Pallas kernels, attend(): pl.pallas_call(functools.partial(attend_kernel, chips), grid_spec=pltpu.P...  57 us
    ppermute x21, waiting for transfers between devices, along(): lax.ppermute(x, 'pass', [(2 * s + c, 2 * d + c) for s, d in pairs for c i...  24.6 us
    ppermute x21, starting transfers between devices, along(): lax.ppermute(x, 'pass', [(2 * s + c, 2 * d + c) for s, d in pairs for c i...  17.4 us
    pallas_call x1, Pallas kernels, pool(): pl.pallas_call(pool_kernel, grid=(count,), in_specs=[pl.BlockSpec((1, LEN...  7.75 us
    ppermute x3, starting transfers between devices, to_partner(): return lax.ppermute(x, 'pass', [(i, i ^ 1) for i in range(extent)])  3.81 us
  transfers between devices with their start and end apart: 24, of which 8 were waited for; matrix products, arithmetic and copies ran while one was open for 1% of the time, Pallas kernels for 31%

profile of v5, /device:TPU:1, one launch (start us, length us, event | category | flops | bytes accessed | tf_op | source)
XLA Modules:
  0.0 115.1 jit_solution(1714294956669572087)
XLA Ops:
  0.0 1.0 constant_dynamic-slice_fusion.1
  1.0 0.1 collective-permute-start.2
  1.1 2.7 %collective-permute-start.1 = (bf16[256,256]{1,0:T(8,128)(2,1)S(1)}, bf16[256,256]{1,0:T(8,128)(2,1)S(1)}, u32[]{:S(2)}, u32[]{:S(2)}) collective-permute-start(bf16[256,256]{1,0:T(8,128)(2,1)S(1)} %pad_maximum_fusion.rest_2_), channel_id=1, source_target_pairs={{0,2},{1,3},{2,6},{3,7},{4,0},{5,1},{6,10},{7,11},{8,4},{9,5},{10,... | collective-permute-start | bytes 393224 | tf_op jit(solution)/shard_map/ppermute | solution.py:359
  3.8 0.2 collective-permute-start
  4.0 0.0 collective-permute-done.2.rest_10_
  4.0 1.3 %collective-permute-start.4 = (bf16[256,256]{1,0:T(8,128)(2,1)S(1)}, bf16[256,256]{1,0:T(8,128)(2,1)S(1)}, u32[]{:S(2)}, u32[]{:S(2)}) collective-permute-start(bf16[256,256]{1,0:T(8,128)(2,1)S(1)} %collective-permute-done.2.rest_10_), channel_id=1, source_target_pairs={{0,2},{1,3},{2,6},{3,7},{4,0},{5,1},{6,10},{7,11},{8,4},{9,5},{10,... | collective-permute-start | bytes 393224 | tf_op jit(solution)/shard_map/ppermute | solution.py:359
  5.3 0.2 collective-permute-start.3
  5.5 1.3 %reshape.16.gain_ref = bf16[1,4096]{1,0:T(2,128)(2,1)} reshape(bf16[4096]{0:T(1024)(128)(2,1)} %param.10) | data formatting | bytes 16384 | tf_op jit(solution)/shard_map/reshape | solution.py:102
  6.8 0.0 copy-start.2
  6.8 7.7 %pool.1.rest_0_ = bf16[128,4096]{1,0:T(8,128)(2,1)} custom-call(bf16[4,128,4096]{2,1,0:T(8,128)(2,1)} %states_ref.1, bf16[32,4096]{1,0:T(8,128)(2,1)} %queries_ref.1, bf16[1,4096]{1,0:T(2,128)(2,1)} %reshape.16.gain_ref), custom_call_target="tpu_custom_call" | custom-call | flops 268435456 | bytes 4194304 | tf_op jit(solution)/shard_map/pool/pallas_call | solution.py:85
  14.5 0.0 copy-start.3
  14.5 0.0 copy-start.4
  14.5 0.0 collective-permute-done.1.rest_9_
  14.5 0.0 collective-permute-done.rest_3_
  14.5 0.0 collective-permute-done.4.rest_17_
  14.5 0.0 collective-permute-done.3.rest_11_
  14.6 0.9 collective-permute-start.5
  15.5 1.7 %collective-permute-start.6 = (bf16[256,256]{1,0:T(8,128)(2,1)S(1)}, bf16[256,256]{1,0:T(8,128)(2,1)S(1)}, u32[]{:S(2)}, u32[]{:S(2)}) collective-permute-start(bf16[256,256]{1,0:T(8,128)(2,1)S(1)} %collective-permute-done.rest_3_), channel_id=1, source_target_pairs={{0,4},{1,5},{2,0},{3,1},{4,8},{5,9},{6,2},{7,3},{8,12},{9,13},{10,... | collective-permute-start | bytes 393224 | tf_op jit(solution)/shard_map/ppermute | solution.py:359
  17.2 0.0 collective-permute-start.13
  17.2 1.4 %collective-permute-start.9 = (bf16[256,256]{1,0:T(8,128)(2,1)S(1)}, bf16[256,256]{1,0:T(8,128)(2,1)S(1)}, u32[]{:S(2)}, u32[]{:S(2)}) collective-permute-start(bf16[256,256]{1,0:T(8,128)(2,1)S(1)} %collective-permute-done.1.rest_9_), channel_id=1, source_target_pairs={{0,2},{1,3},{2,6},{3,7},{4,0},{5,1},{6,10},{7,11},{8,4},{9,5},{10,... | collective-permute-start | bytes 393224 | tf_op jit(solution)/shard_map/ppermute | solution.py:359
  18.5 0.1 collective-permute-start.11
  18.7 2.2 %collective-permute-done.6.rest_4_ = bf16[256,256]{1,0:T(8,128)(2,1)S(1)} collective-permute-done((bf16[256,256]{1,0:T(8,128)(2,1)S(1)}, bf16[256,256]{1,0:T(8,128)(2,1)S(1)}, u32[]{:S(2)}, u32[]{:S(2)}) %collective-permute-start.6) | collective-permute-done | bytes 131104 | tf_op jit(solution)/shard_map/ppermute | solution.py:359
  20.8 1.4 %collective-permute-start.7 = (bf16[256,256]{1,0:T(8,128)(2,1)S(1)}, bf16[256,256]{1,0:T(8,128)(2,1)S(1)}, u32[]{:S(2)}, u32[]{:S(2)}) collective-permute-start(bf16[256,256]{1,0:T(8,128)(2,1)S(1)} %collective-permute-done.6.rest_4_), channel_id=1, source_target_pairs={{0,4},{1,5},{2,0},{3,1},{4,8},{5,9},{6,2},{7,3},{8,12},{9,13},{10,... | collective-permute-start | bytes 393224 | tf_op jit(solution)/shard_map/ppermute | solution.py:359
  22.2 0.0 collective-permute-done.13.rest_16_
  22.2 0.1 collective-permute-start.14
  22.3 2.4 %collective-permute-done.9.rest_8_ = bf16[256,256]{1,0:T(8,128)(2,1)S(1)} collective-permute-done((bf16[256,256]{1,0:T(8,128)(2,1)S(1)}, bf16[256,256]{1,0:T(8,128)(2,1)S(1)}, u32[]{:S(2)}, u32[]{:S(2)}) %collective-permute-start.9) | collective-permute-done | bytes 131104 | tf_op jit(solution)/shard_map/ppermute | solution.py:359
  24.7 0.2 collective-permute-start.10
  25.0 0.0 collective-permute-done.11.rest_12_
  25.0 1.2 %collective-permute-start.12 = (bf16[256,256]{1,0:T(8,128)(2,1)S(1)}, bf16[256,256]{1,0:T(8,128)(2,1)S(1)}, u32[]{:S(2)}, u32[]{:S(2)}) collective-permute-start(bf16[256,256]{1,0:T(8,128)(2,1)S(1)} %collective-permute-done.11.rest_12_), channel_id=1, source_target_pairs={{0,4},{1,5},{2,0},{3,1},{4,8},{5,9},{6,2},{7,3},{8,12},{9,13},{10,... | collective-permute-start | bytes 393224 | tf_op jit(solution)/shard_map/ppermute | solution.py:359
  26.2 0.0 collective-permute-done.7.rest_5_
  26.2 1.3 %collective-permute-start.8 = (bf16[256,256]{1,0:T(8,128)(2,1)S(1)}, bf16[256,256]{1,0:T(8,128)(2,1)S(1)}, u32[]{:S(2)}, u32[]{:S(2)}) collective-permute-start(bf16[256,256]{1,0:T(8,128)(2,1)S(1)} %collective-permute-done.7.rest_5_), channel_id=1, source_target_pairs={{0,4},{1,5},{2,0},{3,1},{4,8},{5,9},{6,2},{7,3},{8,12},{9,13},{10,... | collective-permute-start | bytes 393224 | tf_op jit(solution)/shard_map/ppermute | solution.py:359
  27.5 0.0 collective-permute-done.14.rest_15_
  27.5 0.2 collective-permute-start.15
  27.7 2.4 %collective-permute-done.10.rest_7_ = bf16[256,256]{1,0:T(8,128)(2,1)S(1)} collective-permute-done((bf16[256,256]{1,0:T(8,128)(2,1)S(1)}, bf16[256,256]{1,0:T(8,128)(2,1)S(1)}, u32[]{:S(2)}, u32[]{:S(2)}) %collective-permute-start.10) | collective-permute-done | bytes 131104 | tf_op jit(solution)/shard_map/ppermute | solution.py:359
  30.1 0.0 collective-permute-done.12.rest_13_
  30.1 1.1 collective-permute-done.8.rest_6_
  31.1 1.5 %collective-permute-done.15.rest_14_ = bf16[256,256]{1,0:T(8,128)(2,1)S(1)} collective-permute-done((bf16[256,256]{1,0:T(8,128)(2,1)S(1)}, bf16[256,256]{1,0:T(8,128)(2,1)S(1)}, u32[]{:S(2)}, u32[]{:S(2)}) %collective-permute-start.15) | collective-permute-done | bytes 131104 | tf_op jit(solution)/shard_map/ppermute | solution.py:359
  32.6 0.0 collective-permute-done.5.rest_1_
  32.6 0.0 copy-start
  32.6 1.2 %copy-done = bf16[128,4096]{1,0:T(8,128)(2,1)S(1)} copy-done((bf16[128,4096]{1,0:T(8,128)(2,1)S(1)}, bf16[128,4096]{1,0:T(8,128)(2,1)}, u32[]{:S(2)}) %copy-start) | copy-done | bytes 1048600
  33.9 0.0 copy-start.1
  33.9 0.7 project.1
  34.6 3.3 %collective-permute-start.18 = (bf16[256,256]{1,0:T(8,128)(2,1)S(1)}, bf16[256,256]{1,0:T(8,128)(2,1)S(1)}, u32[]{:S(2)}, u32[]{:S(2)}) collective-permute-start(bf16[256,256]{1,0:T(8,128)(2,1)S(1)} %project.1), channel_id=1, source_target_pairs={{0,12},{1,13},{2,14},{3,15},{4,0},{5,1},{6,2},{7,3},{8,4},{9,5},{1... | collective-permute-start | bytes 393224 | tf_op jit(solution)/shard_map/ppermute | solution.py:359
  37.9 0.0 collective-permute-start.17
  37.9 0.5 collective-permute-start.16
  38.4 0.1 collective-permute-start.19
  38.5 1.3 %collective-permute-done.18 = bf16[256,256]{1,0:T(8,128)(2,1)S(1)} collective-permute-done((bf16[256,256]{1,0:T(8,128)(2,1)S(1)}, bf16[256,256]{1,0:T(8,128)(2,1)S(1)}, u32[]{:S(2)}, u32[]{:S(2)}) %collective-permute-start.18) | collective-permute-done | bytes 131104 | tf_op jit(solution)/shard_map/ppermute | solution.py:359
  39.8 0.2 collective-permute-start.22
  40.0 9.2 %collective-permute-done.17 = bf16[256,256]{1,0:T(8,128)(2,1)S(1)} collective-permute-done((bf16[256,256]{1,0:T(8,128)(2,1)S(1)}, bf16[256,256]{1,0:T(8,128)(2,1)S(1)}, u32[]{:S(2)}, u32[]{:S(2)}) %collective-permute-start.17) | collective-permute-done | bytes 131104 | tf_op jit(solution)/shard_map/ppermute | solution.py:359
  49.2 0.1 collective-permute-start.21
  49.3 0.0 collective-permute-done.16
  49.3 1.4 %collective-permute-start.20 = (bf16[256,256]{1,0:T(8,128)(2,1)S(1)}, bf16[256,256]{1,0:T(8,128)(2,1)S(1)}, u32[]{:S(2)}, u32[]{:S(2)}) collective-permute-start(bf16[256,256]{1,0:T(8,128)(2,1)S(1)} %collective-permute-done.16), channel_id=1, source_target_pairs={{0,2},{1,3},{2,0},{3,1},{4,6},{5,7},{6,4},{7,5},{8,10},{9,11},{10,... | collective-permute-start | bytes 393224 | tf_op jit(solution)/shard_map/ppermute | solution.py:359
  50.8 0.0 collective-permute-done.19
  50.8 4.5 %collective-permute-done.20 = bf16[256,256]{1,0:T(8,128)(2,1)S(1)} collective-permute-done((bf16[256,256]{1,0:T(8,128)(2,1)S(1)}, bf16[256,256]{1,0:T(8,128)(2,1)S(1)}, u32[]{:S(2)}, u32[]{:S(2)}) %collective-permute-start.20) | collective-permute-done | bytes 131104 | tf_op jit(solution)/shard_map/ppermute | solution.py:359
  55.3 0.0 collective-permute-done.21
  55.3 0.0 collective-permute-done.22
  55.3 2.8 %collective-permute-start.23 = (bf16[2048,256]{1,0:T(8,128)(2,1)S(1)}, bf16[2048,256]{1,0:T(8,128)(2,1)S(1)}, u32[]{:S(2)}, u32[]{:S(2)}) collective-permute-start(bf16[2048,256]{1,0:T(8,128)(2,1)S(1)} %constant_dynamic-update-slice_fusion.k_ref.v_ref), channel_id=1, source_target_pairs={{0,1},{1,0},{2,3},{3,2},{4,5},{5,4},{6,7},{7,6},{8,9},{9,8},{10,11... | collective-permute-start | bytes 3145736 | tf_op jit(solution)/shard_map/ppermute | solution.py:355
  58.1 0.0 copy-done.2
  58.1 0.0 copy-done.3
  58.1 0.0 copy-done.4
  58.1 0.0 copy-done.1
  58.1 28.4 %attend.2.rest_0_ = bf16[4,64,7424]{2,1,0:T(8,128)(2,1)} custom-call(s32[1]{0:T(128)} %bitcast.2.core_ref.half_ref, s32[1]{0:T(128)} %bitcast.1.place_ref, s32[4,16]{1,0:T(4,128)S(1)} %copy-done.3, s32[4]{0:T(128)S(1)} %copy-done.4, bf16[4,64,7424]{2,1,0:T(8,128)(2,1)S(1)} %copy-done.1, bf16[2048,256]{1,0:T(8,128)(2,1)S(1)} %constant_dynamic-update-slice_fusion.k_ref.v_ref, ...), custom_call_target="tpu_custom_call" | custom-call | flops 2189426688 | bytes 4849664 | tf_op jit(solution)/shard_map/attend/pallas_call | solution.py:261
  86.5 0.0 collective-permute-done.23.k_ref.v_ref
  86.5 28.6 %attend.3 = bf16[4,64,7424]{2,1,0:T(8,128)(2,1)} custom-call(s32[1]{0:T(128)} %bitcast.half_ref, s32[1]{0:T(128)} %bitcast.1.place_ref, s32[4,16]{1,0:T(4,128)S(1)} %copy-done.3, s32[4]{0:T(128)S(1)} %copy-done.4, bf16[4,64,7424]{2,1,0:T(8,128)(2,1)S(1)} %copy-done.1, ...), custom_call_target="tpu_custom_call", output_to_operand_aliasing={{}: (9, {})} | custom-call | flops 2189426688 | bytes 4849664 | tf_op jit(solution)/shard_map/attend/pallas_call | solution.py:261
  (10 shorter events, 0.1 us)
Async XLA Ops:
  1.0 3.0 %collective-permute-start.2 = (bf16[256,256]{1,0:T(8,128)(2,1)S(1)}, bf16[256,256]{1,0:T(8,128)(2,1)S(1)}, u32[]{:S(2)}, u32[]{:S(2)}) collective-permute-start(bf16[256,256]{1,0:T(8,128)(2,1)S(1)} %pad_maximum_fusion.1), channel_id=1, source_target_pairs={{0,1},{1,0},{2,3},{3,2},{4,5},{5,4},{6,7},{7,6},{8,9},{9,8},{10,11... | collective-permute-start | bytes 393224 | tf_op jit(solution)/shard_map/ppermute | solution.py:355
  1.1 13.4 %collective-permute-start.1 = (bf16[256,256]{1,0:T(8,128)(2,1)S(1)}, bf16[256,256]{1,0:T(8,128)(2,1)S(1)}, u32[]{:S(2)}, u32[]{:S(2)}) collective-permute-start(bf16[256,256]{1,0:T(8,128)(2,1)S(1)} %pad_maximum_fusion.rest_2_), channel_id=1, source_target_pairs={{0,2},{1,3},{2,6},{3,7},{4,0},{5,1},{6,10},{7,11},{8,4},{9,5},{10,... | collective-permute-start | bytes 393224 | tf_op jit(solution)/shard_map/ppermute | solution.py:359
  3.8 10.7 %collective-permute-start = (bf16[256,256]{1,0:T(8,128)(2,1)S(1)}, bf16[256,256]{1,0:T(8,128)(2,1)S(1)}, u32[]{:S(2)}, u32[]{:S(2)}) collective-permute-start(bf16[256,256]{1,0:T(8,128)(2,1)S(1)} %pad_maximum_fusion.rest_2_), channel_id=1, source_target_pairs={{0,4},{1,5},{2,0},{3,1},{4,8},{5,9},{6,2},{7,3},{8,12},{9,13},{10,... | collective-permute-start | bytes 393224 | tf_op jit(solution)/shard_map/ppermute | solution.py:359
  4.0 10.5 %collective-permute-start.4 = (bf16[256,256]{1,0:T(8,128)(2,1)S(1)}, bf16[256,256]{1,0:T(8,128)(2,1)S(1)}, u32[]{:S(2)}, u32[]{:S(2)}) collective-permute-start(bf16[256,256]{1,0:T(8,128)(2,1)S(1)} %collective-permute-done.2.rest_10_), channel_id=1, source_target_pairs={{0,2},{1,3},{2,6},{3,7},{4,0},{5,1},{6,10},{7,11},{8,4},{9,5},{10,... | collective-permute-start | bytes 393224 | tf_op jit(solution)/shard_map/ppermute | solution.py:359
  5.3 9.2 %collective-permute-start.3 = (bf16[256,256]{1,0:T(8,128)(2,1)S(1)}, bf16[256,256]{1,0:T(8,128)(2,1)S(1)}, u32[]{:S(2)}, u32[]{:S(2)}) collective-permute-start(bf16[256,256]{1,0:T(8,128)(2,1)S(1)} %collective-permute-done.2.rest_10_), channel_id=1, source_target_pairs={{0,4},{1,5},{2,0},{3,1},{4,8},{5,9},{6,2},{7,3},{8,12},{9,13},{10,... | collective-permute-start | bytes 393224 | tf_op jit(solution)/shard_map/ppermute | solution.py:359
  6.8 51.3 %copy-start.2 = (bf16[4,64,512]{2,1,0:T(8,128)(2,1)S(1)}, bf16[4,64,512]{2,1,0:T(8,128)(2,1)}, u32[]{:S(2)}) copy-start(bf16[4,64,512]{2,1,0:T(8,128)(2,1)} %own_v_ref.3) | copy-start | bytes 786436
  14.5 43.6 %copy-start.3 = (s32[4,16]{1,0:T(4,128)S(1)}, s32[4,16]{1,0:T(4,128)}, u32[]{:S(2)}) copy-start(s32[4,16]{1,0:T(4,128)} %passage_ref.3) | copy-start | bytes 772
  14.5 43.6 %copy-start.4 = (s32[4]{0:T(128)S(1)}, s32[4]{0:T(128)}, u32[]{:S(2)}) copy-start(s32[4]{0:T(128)} %length_ref.3) | copy-start | bytes 52
  14.6 18.1 %collective-permute-start.5 = (bf16[128,4096]{1,0:T(8,128)(2,1)}, bf16[128,4096]{1,0:T(8,128)(2,1)S(1)}, u32[]{:S(2)}, u32[]{:S(2)}) collective-permute-start(bf16[128,4096]{1,0:T(8,128)(2,1)} %pool.1.rest_0_), channel_id=1, source_target_pairs={{0,1},{1,0},{2,3},{3,2},{4,5},{5,4},{6,7},{7,6},{8,9},{9,8},{10,11... | collective-permute-start | bytes 3145736 | tf_op jit(solution)/shard_map/ppermute | solution.py:355
  15.5 5.3 %collective-permute-start.6 = (bf16[256,256]{1,0:T(8,128)(2,1)S(1)}, bf16[256,256]{1,0:T(8,128)(2,1)S(1)}, u32[]{:S(2)}, u32[]{:S(2)}) collective-permute-start(bf16[256,256]{1,0:T(8,128)(2,1)S(1)} %collective-permute-done.rest_3_), channel_id=1, source_target_pairs={{0,4},{1,5},{2,0},{3,1},{4,8},{5,9},{6,2},{7,3},{8,12},{9,13},{10,... | collective-permute-start | bytes 393224 | tf_op jit(solution)/shard_map/ppermute | solution.py:359
  17.2 5.1 %collective-permute-start.13 = (bf16[256,256]{1,0:T(8,128)(2,1)S(1)}, bf16[256,256]{1,0:T(8,128)(2,1)S(1)}, u32[]{:S(2)}, u32[]{:S(2)}) collective-permute-start(bf16[256,256]{1,0:T(8,128)(2,1)S(1)} %collective-permute-done.4.rest_17_), channel_id=1, source_target_pairs={{0,2},{1,3},{2,6},{3,7},{4,0},{5,1},{6,10},{7,11},{8,4},{9,5},{10,... | collective-permute-start | bytes 393224 | tf_op jit(solution)/shard_map/ppermute | solution.py:359
  17.2 7.5 %collective-permute-start.9 = (bf16[256,256]{1,0:T(8,128)(2,1)S(1)}, bf16[256,256]{1,0:T(8,128)(2,1)S(1)}, u32[]{:S(2)}, u32[]{:S(2)}) collective-permute-start(bf16[256,256]{1,0:T(8,128)(2,1)S(1)} %collective-permute-done.1.rest_9_), channel_id=1, source_target_pairs={{0,2},{1,3},{2,6},{3,7},{4,0},{5,1},{6,10},{7,11},{8,4},{9,5},{10,... | collective-permute-start | bytes 393224 | tf_op jit(solution)/shard_map/ppermute | solution.py:359
  18.5 6.4 %collective-permute-start.11 = (bf16[256,256]{1,0:T(8,128)(2,1)S(1)}, bf16[256,256]{1,0:T(8,128)(2,1)S(1)}, u32[]{:S(2)}, u32[]{:S(2)}) collective-permute-start(bf16[256,256]{1,0:T(8,128)(2,1)S(1)} %collective-permute-done.3.rest_11_), channel_id=1, source_target_pairs={{0,4},{1,5},{2,0},{3,1},{4,8},{5,9},{6,2},{7,3},{8,12},{9,13},{10,... | collective-permute-start | bytes 393224 | tf_op jit(solution)/shard_map/ppermute | solution.py:359
  20.8 5.4 %collective-permute-start.7 = (bf16[256,256]{1,0:T(8,128)(2,1)S(1)}, bf16[256,256]{1,0:T(8,128)(2,1)S(1)}, u32[]{:S(2)}, u32[]{:S(2)}) collective-permute-start(bf16[256,256]{1,0:T(8,128)(2,1)S(1)} %collective-permute-done.6.rest_4_), channel_id=1, source_target_pairs={{0,4},{1,5},{2,0},{3,1},{4,8},{5,9},{6,2},{7,3},{8,12},{9,13},{10,... | collective-permute-start | bytes 393224 | tf_op jit(solution)/shard_map/ppermute | solution.py:359
  22.2 5.3 %collective-permute-start.14 = (bf16[256,256]{1,0:T(8,128)(2,1)S(1)}, bf16[256,256]{1,0:T(8,128)(2,1)S(1)}, u32[]{:S(2)}, u32[]{:S(2)}) collective-permute-start(bf16[256,256]{1,0:T(8,128)(2,1)S(1)} %collective-permute-done.13.rest_16_), channel_id=1, source_target_pairs={{0,2},{1,3},{2,6},{3,7},{4,0},{5,1},{6,10},{7,11},{8,4},{9,5},{10,... | collective-permute-start | bytes 393224 | tf_op jit(solution)/shard_map/ppermute | solution.py:359
  24.7 5.3 %collective-permute-start.10 = (bf16[256,256]{1,0:T(8,128)(2,1)S(1)}, bf16[256,256]{1,0:T(8,128)(2,1)S(1)}, u32[]{:S(2)}, u32[]{:S(2)}) collective-permute-start(bf16[256,256]{1,0:T(8,128)(2,1)S(1)} %collective-permute-done.9.rest_8_), channel_id=1, source_target_pairs={{0,2},{1,3},{2,6},{3,7},{4,0},{5,1},{6,10},{7,11},{8,4},{9,5},{10,... | collective-permute-start | bytes 393224 | tf_op jit(solution)/shard_map/ppermute | solution.py:359
  25.0 5.1 %collective-permute-start.12 = (bf16[256,256]{1,0:T(8,128)(2,1)S(1)}, bf16[256,256]{1,0:T(8,128)(2,1)S(1)}, u32[]{:S(2)}, u32[]{:S(2)}) collective-permute-start(bf16[256,256]{1,0:T(8,128)(2,1)S(1)} %collective-permute-done.11.rest_12_), channel_id=1, source_target_pairs={{0,4},{1,5},{2,0},{3,1},{4,8},{5,9},{6,2},{7,3},{8,12},{9,13},{10,... | collective-permute-start | bytes 393224 | tf_op jit(solution)/shard_map/ppermute | solution.py:359
  26.2 4.9 %collective-permute-start.8 = (bf16[256,256]{1,0:T(8,128)(2,1)S(1)}, bf16[256,256]{1,0:T(8,128)(2,1)S(1)}, u32[]{:S(2)}, u32[]{:S(2)}) collective-permute-start(bf16[256,256]{1,0:T(8,128)(2,1)S(1)} %collective-permute-done.7.rest_5_), channel_id=1, source_target_pairs={{0,4},{1,5},{2,0},{3,1},{4,8},{5,9},{6,2},{7,3},{8,12},{9,13},{10,... | collective-permute-start | bytes 393224 | tf_op jit(solution)/shard_map/ppermute | solution.py:359
  27.5 5.2 %collective-permute-start.15 = (bf16[256,256]{1,0:T(8,128)(2,1)S(1)}, bf16[256,256]{1,0:T(8,128)(2,1)S(1)}, u32[]{:S(2)}, u32[]{:S(2)}) collective-permute-start(bf16[256,256]{1,0:T(8,128)(2,1)S(1)} %collective-permute-done.14.rest_15_), channel_id=1, source_target_pairs={{0,2},{1,3},{2,6},{3,7},{4,0},{5,1},{6,10},{7,11},{8,4},{9,5},{10,... | collective-permute-start | bytes 393224 | tf_op jit(solution)/shard_map/ppermute | solution.py:359
  32.6 1.2 %copy-start = (bf16[128,4096]{1,0:T(8,128)(2,1)S(1)}, bf16[128,4096]{1,0:T(8,128)(2,1)}, u32[]{:S(2)}) copy-start(bf16[128,4096]{1,0:T(8,128)(2,1)} %pool.1.rest_0_) | copy-start | bytes 3145732
  33.9 24.3 %copy-start.1 = (bf16[4,64,7424]{2,1,0:T(8,128)(2,1)S(1)}, bf16[4,64,7424]{2,1,0:T(8,128)(2,1)}, u32[]{:S(2)}) copy-start(bf16[4,64,7424]{2,1,0:T(8,128)(2,1)} %q_ref.3) | copy-start | bytes 11403268
  34.6 5.2 %collective-permute-start.18 = (bf16[256,256]{1,0:T(8,128)(2,1)S(1)}, bf16[256,256]{1,0:T(8,128)(2,1)S(1)}, u32[]{:S(2)}, u32[]{:S(2)}) collective-permute-start(bf16[256,256]{1,0:T(8,128)(2,1)S(1)} %project.1), channel_id=1, source_target_pairs={{0,12},{1,13},{2,14},{3,15},{4,0},{5,1},{6,2},{7,3},{8,4},{9,5},{1... | collective-permute-start | bytes 393224 | tf_op jit(solution)/shard_map/ppermute | solution.py:359
  37.9 11.4 %collective-permute-start.17 = (bf16[256,256]{1,0:T(8,128)(2,1)S(1)}, bf16[256,256]{1,0:T(8,128)(2,1)S(1)}, u32[]{:S(2)}, u32[]{:S(2)}) collective-permute-start(bf16[256,256]{1,0:T(8,128)(2,1)S(1)} %project.1), channel_id=1, source_target_pairs={{0,8},{1,9},{2,10},{3,11},{4,12},{5,13},{6,14},{7,15},{8,0},{9,1},... | collective-permute-start | bytes 393224 | tf_op jit(solution)/shard_map/ppermute | solution.py:359
  37.9 11.5 %collective-permute-start.16 = (bf16[256,256]{1,0:T(8,128)(2,1)S(1)}, bf16[256,256]{1,0:T(8,128)(2,1)S(1)}, u32[]{:S(2)}, u32[]{:S(2)}) collective-permute-start(bf16[256,256]{1,0:T(8,128)(2,1)S(1)} %project.1), channel_id=1, source_target_pairs={{0,4},{1,5},{2,6},{3,7},{4,8},{5,9},{6,10},{7,11},{8,12},{9,13},{1... | collective-permute-start | bytes 393224 | tf_op jit(solution)/shard_map/ppermute | solution.py:359
  38.4 12.3 %collective-permute-start.19 = (bf16[256,256]{1,0:T(8,128)(2,1)S(1)}, bf16[256,256]{1,0:T(8,128)(2,1)S(1)}, u32[]{:S(2)}, u32[]{:S(2)}) collective-permute-start(bf16[256,256]{1,0:T(8,128)(2,1)S(1)} %project.1), channel_id=1, source_target_pairs={{0,2},{1,3},{2,0},{3,1},{4,6},{5,7},{6,4},{7,5},{8,10},{9,11},{10,... | collective-permute-start | bytes 393224 | tf_op jit(solution)/shard_map/ppermute | solution.py:359
  39.8 15.5 %collective-permute-start.22 = (bf16[256,256]{1,0:T(8,128)(2,1)S(1)}, bf16[256,256]{1,0:T(8,128)(2,1)S(1)}, u32[]{:S(2)}, u32[]{:S(2)}) collective-permute-start(bf16[256,256]{1,0:T(8,128)(2,1)S(1)} %collective-permute-done.18), channel_id=1, source_target_pairs={{0,2},{1,3},{2,0},{3,1},{4,6},{5,7},{6,4},{7,5},{8,10},{9,11},{10,... | collective-permute-start | bytes 393224 | tf_op jit(solution)/shard_map/ppermute | solution.py:359
  49.2 6.0 %collective-permute-start.21 = (bf16[256,256]{1,0:T(8,128)(2,1)S(1)}, bf16[256,256]{1,0:T(8,128)(2,1)S(1)}, u32[]{:S(2)}, u32[]{:S(2)}) collective-permute-start(bf16[256,256]{1,0:T(8,128)(2,1)S(1)} %collective-permute-done.17), channel_id=1, source_target_pairs={{0,2},{1,3},{2,0},{3,1},{4,6},{5,7},{6,4},{7,5},{8,10},{9,11},{10,... | collective-permute-start | bytes 393224 | tf_op jit(solution)/shard_map/ppermute | solution.py:359
  49.3 5.9 %collective-permute-start.20 = (bf16[256,256]{1,0:T(8,128)(2,1)S(1)}, bf16[256,256]{1,0:T(8,128)(2,1)S(1)}, u32[]{:S(2)}, u32[]{:S(2)}) collective-permute-start(bf16[256,256]{1,0:T(8,128)(2,1)S(1)} %collective-permute-done.16), channel_id=1, source_target_pairs={{0,2},{1,3},{2,0},{3,1},{4,6},{5,7},{6,4},{7,5},{8,10},{9,11},{10,... | collective-permute-start | bytes 393224 | tf_op jit(solution)/shard_map/ppermute | solution.py:359
  55.3 31.2 %collective-permute-start.23 = (bf16[2048,256]{1,0:T(8,128)(2,1)S(1)}, bf16[2048,256]{1,0:T(8,128)(2,1)S(1)}, u32[]{:S(2)}, u32[]{:S(2)}) collective-permute-start(bf16[2048,256]{1,0:T(8,128)(2,1)S(1)} %constant_dynamic-update-slice_fusion.k_ref.v_ref), channel_id=1, source_target_pairs={{0,1},{1,0},{2,3},{3,2},{4,5},{5,4},{6,7},{7,6},{8,9},{9,8},{10,11... | collective-permute-start | bytes 3145736 | tf_op jit(solution)/shard_map/ppermute | solution.py:355

commit v6 on v5

v6 whole, which is shorter than its diff:
```python
import functools
import math

import jax
import jax.numpy as jnp
from jax import lax
from jax.experimental import pallas as pl
from jax.experimental.pallas import tpu as pltpu
from jax.sharding import PartitionSpec as P

D = 4096
CH = 32
CHD = 128
MEM = 32
LEN = 128
QLEN = 64
TOPK = 16
H = 116
HD = 64
KVH = 4
GROUP = 29
KVW = 512

LANES = 2 * HD
PAIRS = GROUP
HALF = PAIRS * LANES
ROWS = TOPK * MEM
KEYS = 2 * (ROWS + QLEN)
NEG = -1e30
SUM_LOW, SUM_HIGH = 2.0 ** -40, 2.0 ** 60
POOL_HEADS = 16
CHIP = 8
STEP = 8
POOL_TURNS = ((0, 1), (2,), (3,))
SOURCE_OF = (0,) * 2 + (1,) * 8 + (2,) * 6
STAGES = (
    (tuple(range(2)), True, SOURCE_OF),
    (tuple(range(2, 10)), False, SOURCE_OF),
    (tuple(range(10, TOPK)), False, SOURCE_OF),
)
MIB = 1024 * 1024


def place_of(chip, ring):
    line, lane = lax.div(chip, 2), lax.rem(chip, 2)
    return line + lane * (ring - 1 - 2 * line)


def chip_at(place, ring):
    lane = lax.div(place, ring // 2)
    line = place + lane * (ring - 1 - 2 * place)
    return 2 * line + lane


def pool_kernel(states_ref, queries_ref, gain_ref, out_ref, pooled):
    squares = jnp.zeros((MEM, CHD), jnp.float32)
    for base in range(0, CH, POOL_HEADS):
        spans = [slice(h * CHD, (h + 1) * CHD) for h in range(base, base + POOL_HEADS)]
        scores = jnp.concatenate(
            [
                lax.dot_general(
                    queries_ref[:, span], states_ref[0, :, span], (((1,), (1,)), ((), ())),
                    preferred_element_type=jnp.float32,
                )
                for span in spans
            ],
            axis=0,
        ) * (1.0 / math.sqrt(CHD))
        scores = jnp.exp(scores - jnp.max(scores, axis=1, keepdims=True))
        weights = (scores / jnp.sum(scores, axis=1, keepdims=True)).astype(jnp.bfloat16)
        for i, span in enumerate(spans):
            part = jnp.dot(
                weights[i * MEM:(i + 1) * MEM], states_ref[0, :, span], preferred_element_type=jnp.float32
            )
            pooled[:, span] = part
            squares += part * part
    mean_square = jnp.sum(squares, axis=1, keepdims=True) * (1.0 / D)
    scale = lax.rsqrt(mean_square + 1e-06)
    out_ref[...] = (pooled[...] * scale * gain_ref[...].astype(jnp.float32).reshape(1, D)).astype(jnp.bfloat16)


def pool(states, queries, gain, passage):
    return pl.pallas_call(
        pool_kernel,
        grid=(1,),
        in_specs=[
            pl.BlockSpec((1, LEN, D), lambda _: (passage, 0, 0)),
            pl.BlockSpec((MEM, D), lambda _: (0, 0)),
            pl.BlockSpec((D,), lambda _: (0,)),
        ],
        out_specs=pl.BlockSpec((MEM, D), lambda _: (0, 0)),
        out_shape=jax.ShapeDtypeStruct((MEM, D), jnp.bfloat16),
        scratch_shapes=[pltpu.VMEM((MEM, D), jnp.float32)],
        compiler_params=pltpu.CompilerParams(vmem_limit_bytes=52 * MIB),
        cost_estimate=pl.CostEstimate(
            flops=4 * MEM * LEN * D, bytes_accessed=2 * LEN * D, transcendentals=CH * MEM * LEN
        ),
        name="pool",
    )(states, queries, gain)


def attend_kernel(plan, half_ref, start_ref, length_ref, *rest):
    positions, with_own, first, last, source_of = plan
    rest = list(rest)
    q_ref = rest.pop(0)
    sources = {source: rest.pop(0) for source in sorted({source_of[p] for p in needed_positions(plan)})}
    own_k_ref, own_v_ref = (rest.pop(0), rest.pop(0)) if with_own or last else (None, None)
    sums_ref = None if first else rest.pop(0)
    scratch_count = 11 if last else 7
    out_ref = rest[-scratch_count - 1]
    keys, values, key_side, value_side, weights, bias, marker = rest[-scratch_count:][:7]
    query = pl.program_id(0)
    count = MEM * len(positions) + (QLEN if with_own else 0)
    whole = count // LANES * LANES
    width = 2 * count

    @pl.when(query == 0)
    def _():
        key_side[...] = jnp.zeros_like(key_side)
        lane = lax.broadcasted_iota(jnp.int32, (width, LANES), 1)
        row = lax.broadcasted_iota(jnp.int32, (width, LANES), 0)
        in_b = ((row >= whole) & (row < 2 * whole)) | (row >= 2 * whole + HD)
        ones = jnp.where((lane >= HD) == in_b, 1.0, 0.0).astype(jnp.bfloat16)
        for g in range(2):
            value_side[g, :, LANES:] = ones

    def fetch(position):
        start = pl.multiple_of(start_ref[query, position], MEM)
        source = sources[source_of[position]]
        return (
            source[pl.ds(start, MEM), :LANES].astype(jnp.float32),
            source[pl.ds(start, MEM), LANES:].astype(jnp.float32),
        )

    for n, position in enumerate(positions):
        rows = slice(n * MEM, (n + 1) * MEM)
        keys[rows, :], values[rows, :] = fetch(position)
    if with_own:
        keys[count - QLEN:count, :] = own_k_ref[0].astype(jnp.float32)
        values[count - QLEN:count, :] = own_v_ref[0].astype(jnp.float32)
    length = length_ref[query]
    factor = math.log2(math.e) / math.sqrt(HD)

    def fill_keys(block, tail, side, at):
        turned = jnp.transpose(block).astype(jnp.bfloat16)
        size = block.shape[0]
        if tail is not None:
            both = jnp.transpose(jnp.concatenate([tail, tail], axis=0))
            column = lax.broadcasted_iota(jnp.int32, (HD, LANES), 1)
        for g in range(2):
            for member in range(2):
                rows = slice(member * HD, (member + 1) * HD)
                side[g, rows, member * size:(member + 1) * size] = turned[g * HD:(g + 1) * HD]
                if tail is not None:
                    mine = (column >= HD) if member else (column < HD)
                    side[g, rows, at:at + LANES] = jnp.where(
                        mine, both[g * HD:(g + 1) * HD], 0.0
                    ).astype(jnp.bfloat16)

    def fill_values(block, tail, side, at):
        size = block.shape[0]
        parts = [(block, 0, size)]
        if tail is not None:
            parts.append((tail, at, HD))
        for part, start, step in parts:
            swapped = pltpu.roll(part, HD, 1)
            lower = lax.broadcasted_iota(jnp.int32, part.shape, 1) < HD
            for g in range(2):
                one, two = (part, swapped) if g == 0 else (swapped, part)
                side[g, start:start + step, :LANES] = jnp.where(lower, one, 0.0).astype(jnp.bfloat16)
                side[g, start + step:start + 2 * step, :LANES] = jnp.where(lower, 0.0, two).astype(
                    jnp.bfloat16
                )

    tail = slice(whole, count)
    fill_keys(keys[:whole], keys[tail] if count > whole else None, key_side, 2 * whole)
    if with_own:
        token = lax.broadcasted_iota(jnp.int32, (QLEN, LANES), 0)
        key = lax.broadcasted_iota(jnp.int32, (QLEN, LANES), 1) - (LANES - QLEN)
        bias[...] = jnp.where((key < 0) | ((key <= token) & (key < length)), 0.0, NEG)

    half = PAIRS // 2
    chunks = []
    for g in range(2):
        tiles = list(range(half + 1)) if g == 0 else list(range(half, PAIRS))
        chunks += [
            (g, tiles[at:at + STEP], (g * len(tiles) + at) * QLEN) for at in range(0, len(tiles), STEP)
        ]

    def questions(tiles):
        return jnp.concatenate([q_ref[0, :, t * LANES:(t + 1) * LANES] for t in tiles], axis=0)

    def key_product(i):
        g, tiles, _ = chunks[i]
        lhs = questions(tiles)
        rows = slice(0, len(tiles) * QLEN)
        for c in range(0, width, 2 * LANES):
            part = slice(c, min(c + 2 * LANES, width))
            got = jnp.dot(lhs, key_side[g, :, part], preferred_element_type=jnp.float32) * factor
            if with_own:
                got = got + jnp.concatenate(
                    [jnp.concatenate([bias[...]] * len(tiles), axis=0)] * 2, axis=1
                )
            weights[i % 2, rows, part] = jnp.exp2(got).astype(jnp.bfloat16)

    def finish(i, mixed):
        g, tiles, _ = chunks[i]
        token = lax.broadcasted_iota(jnp.int32, (QLEN, LANES), 0)
        low = lax.broadcasted_iota(jnp.int32, (QLEN, LANES), 1) < HD
        for n, t in enumerate(tiles):
            rows = slice(n * QLEN, (n + 1) * QLEN)
            result = jnp.where(token < length, mixed[rows, :LANES] / mixed[rows, LANES:], 0.0)
            result = result.astype(jnp.bfloat16)
            at = slice(t * LANES, (t + 1) * LANES)
            if t == half and g == 1:
                result = jnp.where(low, out_ref[0, :, at], result)
            out_ref[0, :, at] = result

    def value_product(i, seen):
        g, tiles, base = chunks[i]
        size = len(tiles) * QLEN
        mixed = jnp.dot(weights[i % 2, :size, :], value_side[g], preferred_element_type=jnp.float32)
        if not first:
            mixed = mixed + sums_ref[0, base:base + size, :]
        if not last:
            out_ref[0, base:base + size, :] = mixed
            return seen
        for at in range(0, size, QLEN):
            total = mixed[at:at + QLEN, LANES:]
            seen = jnp.where((total > SUM_LOW) & (total < SUM_HIGH), seen, 1.0)
        finish(i, mixed)
        return seen

    key_product(0)
    fill_values(values[:whole], values[tail] if count > whole else None, value_side, 2 * whole)
    seen = jnp.zeros((QLEN, LANES), jnp.float32)
    for i in range(len(chunks)):
        if i + 1 < len(chunks):
            key_product(i + 1)
        seen = value_product(i, seen)
    if not last:
        return

    marker[0] = jnp.max(seen)
    all_keys, all_values, scores, all_weights = rest[-4:]

    @pl.when(marker[0] > 0.0)
    def _():
        own = (own_k_ref[0].astype(jnp.float32), own_v_ref[0].astype(jnp.float32))
        fetched = [fetch(position) for position in range(TOPK)]
        memory = [jnp.concatenate([x[n] for x in fetched], axis=0) for n in range(2)]
        all_keys[...] = jnp.zeros_like(all_keys)
        fill_keys(memory[0], own[0], all_keys, 2 * ROWS)
        fill_values(memory[1], own[1], all_values, 2 * ROWS)
        lane = lax.broadcasted_iota(jnp.int32, (KEYS, LANES), 1)
        row = lax.broadcasted_iota(jnp.int32, (KEYS, LANES), 0)
        in_b = ((row >= ROWS) & (row < 2 * ROWS)) | (row >= 2 * ROWS + QLEN)
        for g in range(2):
            all_values[g, :, LANES:] = jnp.where((lane >= HD) == in_b, 1.0, 0.0).astype(jnp.bfloat16)
        token = lax.broadcasted_iota(jnp.int32, (QLEN, LANES), 0)
        key = lax.rem(lax.broadcasted_iota(jnp.int32, (QLEN, LANES), 1), HD)
        causal = jnp.where((key <= token) & (key < length), 0.0, NEG)
        low = lax.broadcasted_iota(jnp.int32, (QLEN, LANES), 1) < HD
        for i, (g, tiles, _) in enumerate(chunks):
            size = len(tiles) * QLEN
            scores[:size, :] = jnp.dot(questions(tiles), all_keys[g], preferred_element_type=jnp.float32)

            def soften(n, carry):
                rows = pl.ds(pl.multiple_of(n * QLEN, QLEN), QLEN)
                own_scores = scores[rows, 2 * ROWS:] + causal
                tops = []
                for member in range(2):
                    span = slice(member * ROWS, (member + 1) * ROWS)
                    top = jnp.max(jnp.where(low == (member == 0), own_scores, NEG), axis=1, keepdims=True)
                    top = jnp.maximum(top, jnp.max(scores[rows, span], axis=1, keepdims=True))
                    all_weights[rows, span] = jnp.exp2((scores[rows, span] - top) * factor).astype(
                        jnp.bfloat16
                    )
                    tops.append(top)
                all_weights[rows, 2 * ROWS:] = jnp.exp2(
                    (own_scores - jnp.where(low, tops[0], tops[1])) * factor
                ).astype(jnp.bfloat16)
                return carry

            lax.fori_loop(0, len(tiles), soften, 0)
            finish(i, jnp.dot(all_weights[:size, :], all_values[g], preferred_element_type=jnp.float32))


def needed_positions(plan):
    positions, _, _, last, _ = plan
    return list(range(TOPK)) if last else positions


def attend(stage, half, starts, lengths, questions, own_kv, sources, sums=None, earlier=None):
    positions, with_own, source_of = stage
    first, last = sums is None, max(positions) == TOPK - 1
    plan = (positions, with_own, first, last, source_of)
    count = questions.shape[0]
    keys = MEM * len(positions) + (QLEN if with_own else 0)
    grouped = (1, 2 * (PAIRS // 2 + 1) * QLEN, 2 * LANES)
    operands = [half.reshape(1), starts, lengths, questions]
    in_specs = [pl.BlockSpec((1, QLEN, HALF), lambda q, h, *_: (q, 0, h[0]))]
    for source in sorted({source_of[p] for p in needed_positions(plan)}):
        operands.append(sources[source])
        in_specs.append(pl.BlockSpec(sources[source].shape, lambda q, *_: (0, 0)))
    if with_own or last:
        operands += [own_kv, own_kv]
        in_specs.append(pl.BlockSpec((1, QLEN, LANES), lambda q, h, *_: (q, 0, h[0])))
        in_specs.append(pl.BlockSpec((1, QLEN, LANES), lambda q, h, *_: (q, 0, 2 + h[0])))
    if not first:
        operands.append(sums)
        in_specs.append(pl.BlockSpec(grouped, lambda q, *_: (q, 0, 0)))
    aliases = {}
    if earlier is not None:
        aliases = {len(operands): 0}
        operands.append(earlier)
        in_specs.append(pl.BlockSpec(memory_space=pl.ANY))
    if last:
        out_shape = jax.ShapeDtypeStruct((count, QLEN, H * HD), jnp.bfloat16)
        out_spec = pl.BlockSpec((1, QLEN, HALF), lambda q, h, *_: (q, 0, h[0]))
    else:
        out_shape = jax.ShapeDtypeStruct((count,) + grouped[1:], jnp.float32)
        out_spec = pl.BlockSpec(grouped, lambda q, *_: (q, 0, 0))
    scratch = [
        pltpu.VMEM((keys, LANES), jnp.float32),
        pltpu.VMEM((keys, LANES), jnp.float32),
        pltpu.VMEM((2, LANES, 2 * keys), jnp.bfloat16),
        pltpu.VMEM((2, 2 * keys, 2 * LANES), jnp.bfloat16),
        pltpu.VMEM((2, STEP * QLEN, 2 * keys), jnp.bfloat16),
        pltpu.VMEM((QLEN, LANES), jnp.float32),
        pltpu.SMEM((1,), jnp.float32),
    ]
    if last:
        scratch += [
            pltpu.VMEM((2, LANES, KEYS), jnp.bfloat16),
            pltpu.VMEM((2, KEYS, 2 * LANES), jnp.bfloat16),
            pltpu.VMEM((STEP * QLEN, KEYS), jnp.float32),
            pltpu.VMEM((STEP * QLEN, KEYS), jnp.bfloat16),
        ]
    return pl.pallas_call(
        functools.partial(attend_kernel, plan),
        grid_spec=pltpu.PrefetchScalarGridSpec(
            num_scalar_prefetch=3, grid=(count,), in_specs=in_specs, out_specs=out_spec,
            scratch_shapes=scratch,
        ),
        out_shape=out_shape,
        input_output_aliases=aliases,
        compiler_params=pltpu.CompilerParams(vmem_limit_bytes=48 * MIB),
        cost_estimate=pl.CostEstimate(
            flops=2 * count * QLEN * H * HD * keys,
            bytes_accessed=2 * count * QLEN * H * HD,
            transcendentals=count * QLEN * H * keys // 2,
        ),
        name="attend",
    )(*operands)


def project_kernel(ring, passages, core_ref, place_ref, *rest):
    row_refs, weights, out_ref = rest[:2 * passages], rest[2 * passages:-1], rest[-1]
    count = passages * MEM
    depth = weights[0].shape[0]
    total = jnp.zeros((2 * count, weights[0].shape[1]), jnp.float32)
    core = core_ref[0]
    for n, weight in enumerate(weights):
        part, i = n // ring, n % ring
        chip = chip_at(lax.rem(ring + place_ref[0] - i, ring), ring)
        at = pl.multiple_of((2 * chip + (1 - core if part else core)) * depth, depth)
        rows = jnp.concatenate([x[:, pl.ds(at, depth)] for x in row_refs], axis=0)
        total += jnp.dot(rows, weight[...], preferred_element_type=jnp.float32)
    result = total.astype(jnp.bfloat16)
    out_ref[pl.ds(pl.multiple_of(core * count, count), count)] = result[:count]
    out_ref[pl.ds(pl.multiple_of((1 - core) * count, count), count)] = result[count:]


def project(core, place, own_rows, other_rows, weights):
    count = len(own_rows) * MEM
    width = weights[0].shape[1]
    vmem = pl.BlockSpec(memory_space=pltpu.VMEM)
    smem = pl.BlockSpec(memory_space=pltpu.SMEM)
    return pl.pallas_call(
        functools.partial(project_kernel, len(weights) // 2, len(own_rows)),
        in_specs=[smem, smem] + [vmem] * (2 * len(own_rows) + len(weights)),
        out_specs=vmem,
        out_shape=jax.ShapeDtypeStruct((2 * count, width), jnp.bfloat16),
        compiler_params=pltpu.CompilerParams(vmem_limit_bytes=16 * MIB),
        cost_estimate=pl.CostEstimate(
            flops=4 * count * D * width, bytes_accessed=2 * D * width, transcendentals=0
        ),
        name="project",
    )(core.reshape(1), place, *own_rows, *other_rows, *weights)


def local(
    extent,
    passage_states,
    memory_queries,
    memory_gain,
    kv_weight,
    retrieval,
    question_queries,
    question_kv,
    question_lengths,
):
    me = lax.axis_index("pass")
    core, chip = me & 1, lax.div(me, 2)
    chips = extent // 2
    depth = kv_weight.shape[0]
    own_count = passage_states.shape[0]

    if chips != 8 or depth % LANES:
        memory_rows = [pool(passage_states, memory_queries, memory_gain, i) for i in range(own_count)]
        whole_weight = lax.all_gather(kv_weight, "pass", axis=0, tiled=True)
        memory_kv = jnp.dot(
            jnp.concatenate(memory_rows, axis=0), whole_weight, preferred_element_type=jnp.float32
        )
        everything = lax.all_gather(memory_kv.astype(jnp.bfloat16), "pass", axis=0, tiled=True)
        halves = everything.reshape(-1, 2, 2, LANES).transpose(2, 0, 1, 3).reshape(2, -1, 2 * LANES)
        context = None
        for half in range(2):
            sums = None
            for positions, with_own, _ in STAGES:
                stage = (positions, with_own, (0,) * TOPK)
                last = max(positions) == TOPK - 1
                got = attend(
                    stage, jnp.int32(half), retrieval * MEM, question_lengths, question_queries, question_kv,
                    [halves[half]], sums, context if last else None,
                )
                sums, context = (sums, got) if last else (got, context)
        return context

    place = place_of(chip, chips).reshape(1)
    order = [2 * line for line in range(chips // 2)] + [2 * line + 1 for line in range(chips // 2)][::-1]

    def to_partner(x):
        return lax.ppermute(x, "pass", [(i, i ^ 1) for i in range(extent)])

    def along(x, target):
        pairs = [(c, target(c // 2, c % 2)) for c in range(chips)]
        return lax.ppermute(x, "pass", [(2 * s + c, 2 * d + c) for s, d in pairs for c in range(2)])

    def along_ring(x, step):
        return along(x, lambda line, lane: order[(order.index(2 * line + lane) + step) % chips])

    def columns(half):
        return jnp.concatenate(
            [
                lax.dynamic_slice_in_dim(kv_weight, half * LANES + at, LANES, axis=1)
                for at in (0, KVH * HD)
            ],
            axis=1,
        )

    up = [[columns(core)], [to_partner(columns(1 - core))]]
    down = [[x[0]] for x in up]
    memory_rows = []
    for turn in range(1, chips // 2):
        for piece in range(2):
            up[piece].append(along_ring(up[piece][-1], 1))
            down[piece].append(along_ring(down[piece][-1], -1))
        passages = POOL_TURNS[turn - 1]
        rows = [pool(passage_states, memory_queries, memory_gain, i) for i in passages]
        down[1][-1], rows = lax.optimization_barrier((down[1][-1], rows))
        memory_rows += rows
    up[0].append(along_ring(up[0][-1], 1))
    down[1].append(along_ring(down[1][-1], -1))
    weights = [x for piece in range(2) for x in up[piece] + down[piece][:0:-1]]
    memory_kv = project(core, place, memory_rows, [to_partner(x) for x in memory_rows], weights)

    lines = chips // 2
    line_blocks = [
        along(memory_kv, lambda line, lane: 2 * ((line + k) % lines) + lane) for k in range(1, lines)
    ]
    of_chip = lax.div(retrieval, CHIP)
    back = lax.rem(lines + lax.div(chip, 2) - lax.div(of_chip, 2), lines)
    slot = back + lines * lax.rem(lax.rem(chip, 2) + lax.rem(of_chip, 2), 2)
    at = 2 * slot + lax.rem(lax.div(retrieval, CHIP // 2), 2)
    row = MEM * lax.rem(retrieval, CHIP)
    row += CHIP * MEM * (slot - jnp.where(slot > lines, lines + 1, jnp.where(slot > 0, 1, 0)))
    wanted = lax.broadcasted_iota(jnp.int32, (1, TOPK, 1), 1)
    starts = jnp.sum(jnp.where(at[:, None, :] == wanted, row[:, None, :], 0), axis=2)

    rest = (starts, question_lengths, question_queries, question_kv)
    near, far = [memory_kv], [to_partner(memory_kv)]
    lane_blocks = [along(memory_kv, lambda line, lane: 2 * line + 1 - lane)]
    near_sums = attend(STAGES[0], core, *rest, near)
    far_sums = attend(STAGES[0], 1 - core, *rest, far)
    *line_blocks, near_sums, far_sums = lax.optimization_barrier((*line_blocks, near_sums, far_sums))
    lane_blocks += [along(x, lambda line, lane: 2 * line + 1 - lane) for x in line_blocks]
    near.append(jnp.concatenate(line_blocks + lane_blocks[:1], axis=0))
    far.append(to_partner(near[-1]))
    near_sums = attend(STAGES[1], core, *rest, near, near_sums)
    far_sums = attend(STAGES[1], 1 - core, *rest, far, far_sums)
    *lane_blocks, near_sums = lax.optimization_barrier((*lane_blocks[1:], near_sums))
    near.append(jnp.concatenate(lane_blocks, axis=0))
    far.append(to_partner(near[-1]))
    context = attend(STAGES[2], core, *rest, near, near_sums)
    return attend(STAGES[2], 1 - core, *rest, far, far_sums, context)


def solution(mesh):
    placed = (
        P(("groups", "pass"), None, None),
        P(),
        P(),
        P("pass", None),
        P(("groups", "pass"), None),
        P(("groups", "pass"), None, None),
        P(("groups", "pass"), None, None),
        P(("groups", "pass")),
    )
    return jax.shard_map(
        functools.partial(local, mesh.shape["pass"]),
        mesh=mesh,
        in_specs=placed,
        out_specs=P(("groups", "pass"), None, None),
        check_vma=False,
    )
```

time: 115 us -> 172 us (1.50)
  Pallas kernels: 65.4 us -> 126 us
  waiting for transfers between devices: 24.6 us -> 7.93 us
  starting transfers between devices: 21.2 us -> 28.5 us
  local copies, waits for them, and re-layouts: 3.58 us -> 7.98 us
    pallas_call x4 -> x11, Pallas kernels: 65.4 us -> 126 us  [the longest x6 114 us: attend(): pl.pallas_call(functools.partial(attend_kernel, plan), grid_spec=pltpu.Pr...]
    ppermute x21, waiting for transfers between devices: 24.6 us -> 6.62 us  [along(): lax.ppermute(x, 'pass', [(2 * s + c, 2 * d + c) for s, d in pairs for c i...]
    unnamed x17 -> x33, local copies, waits for them, and re-layouts: 1.31 us -> 6.96 us
    ppermute x3 -> x8, starting transfers between devices: 3.81 us -> 8.15 us  [to_partner(): return lax.ppermute(x, 'pass', [(i, i ^ 1) for i in range(extent)])]
    ppermute x21, starting transfers between devices: 17.4 us -> 20.4 us  [along(): lax.ppermute(x, 'pass', [(2 * s + c, 2 * d + c) for s, d in pairs for c i...]
  transfers between devices with their start and end apart: 24 -> 29, of which waited for: 8 -> 3; matrix products, arithmetic and copies ran while one was open for 1% -> 0% of each run, Pallas kernels for 31% -> 48%
where the time goes in v6:
time: 172 us; the launch traced here: 171 us
  Pallas kernels  126 us (73%)
  starting transfers between devices  28.5 us (17%)
  local copies, waits for them, and re-layouts  7.98 us (5%)
  waiting for transfers between devices  7.93 us (5%)
    pallas_call x6, Pallas kernels, attend(): pl.pallas_call(functools.partial(attend_kernel, plan), grid_spec=pltpu.Pr...  114 us
    ppermute x21, starting transfers between devices, along(): lax.ppermute(x, 'pass', [(2 * s + c, 2 * d + c) for s, d in pairs for c i...  20.4 us
    pallas_call x4, Pallas kernels, pool(): pl.pallas_call(pool_kernel, grid=(1,), in_specs=[pl.BlockSpec((1, LEN, D)...  10.4 us
    ppermute x8, starting transfers between devices, to_partner(): return lax.ppermute(x, 'pass', [(i, i ^ 1) for i in range(extent)])  8.15 us
    unnamed x33, local copies, waits for them, and re-layouts  6.96 us
    ppermute x21, waiting for transfers between devices, along(): lax.ppermute(x, 'pass', [(2 * s + c, 2 * d + c) for s, d in pairs for c i...  6.62 us
  transfers between devices with their start and end apart: 29, of which 3 were waited for; matrix products, arithmetic and copies ran while one was open for 0% of the time, Pallas kernels for 48%

profile of v6, /device:TPU:1, one launch (start us, length us, event | category | flops | bytes accessed | tf_op | source)
XLA Modules:
  0.0 170.7 jit_solution(10898183381774228212)
XLA Ops:
  0.0 1.0 constant_dynamic-slice_fusion
  1.0 0.1 collective-permute-start
  1.2 1.3 collective-permute-done.rest_16_
  2.4 2.4 %collective-permute-start.1 = (bf16[256,256]{1,0:T(8,128)(2,1)S(1)}, bf16[256,256]{1,0:T(8,128)(2,1)S(1)}, u32[]{:S(2)}, u32[]{:S(2)}) collective-permute-start(bf16[256,256]{1,0:T(8,128)(2,1)S(1)} %collective-permute-done.rest_16_), channel_id=1, source_target_pairs={{0,2},{1,3},{2,6},{3,7},{4,0},{5,1},{6,10},{7,11},{8,4},{9,5},{10,... | collective-permute-start | bytes 393224 | tf_op jit(solution)/shard_map/ppermute | solution.py:439
  4.8 1.3 collective-permute-start.12
  6.2 0.2 collective-permute-start.8
  6.3 0.2 collective-permute-start.15
  6.5 0.9 copy-done.3
  7.4 0.7 copy-done.5
  8.1 2.6 %pool.5.rest_1_ = bf16[32,4096]{1,0:T(8,128)(2,1)S(1)} custom-call(bf16[4,128,4096]{2,1,0:T(8,128)(2,1)} %states_ref.7, bf16[32,4096]{1,0:T(8,128)(2,1)S(1)} %copy-done.3, bf16[4096]{0:T(1024)(128)(2,1)S(1)} %copy-done.5), custom_call_target="tpu_custom_call" | custom-call | flops 67108864 | bytes 1048576 | tf_op jit(solution)/shard_map/pool/pallas_call | solution.py:83
  10.7 0.0 copy-start.6
  10.8 0.7 copy-done.6
  11.4 2.6 %pool.4.rest_0_ = bf16[32,4096]{1,0:T(8,128)(2,1)S(1)} custom-call(bf16[4,128,4096]{2,1,0:T(8,128)(2,1)} %states_ref.7, bf16[32,4096]{1,0:T(8,128)(2,1)S(1)} %copy-done.3, bf16[4096]{0:T(1024)(128)(2,1)S(1)} %copy-done.6), custom_call_target="tpu_custom_call" | custom-call | flops 67108864 | bytes 1048576 | tf_op jit(solution)/shard_map/pool/pallas_call | solution.py:83
  14.1 0.0 copy-start.2
  14.1 0.0 copy-start.12
  14.1 0.0 collective-permute-done.1.rest_23_
  14.1 1.4 collective-permute-start.2
  15.5 0.0 collective-permute-done.12.rest_15_
  15.5 1.3 collective-permute-start.13
  16.8 0.2 collective-permute-start.9
  16.9 0.0 collective-permute-done.15.rest_17_
  16.9 0.2 collective-permute-start.16
  17.1 2.6 %pool.6.rest_2_ = bf16[32,4096]{1,0:T(8,128)(2,1)S(1)} custom-call(bf16[4,128,4096]{2,1,0:T(8,128)(2,1)} %states_ref.7, bf16[32,4096]{1,0:T(8,128)(2,1)S(1)} %copy-done.3, bf16[4096]{0:T(1024)(128)(2,1)S(1)} %copy-done.7), custom_call_target="tpu_custom_call" | custom-call | flops 67108864 | bytes 1048576 | tf_op jit(solution)/shard_map/pool/pallas_call | solution.py:83
  19.7 0.0 collective-permute-done.2.rest_22_
  19.7 1.4 collective-permute-start.3
  21.1 1.3 collective-permute-start.14
  22.4 0.2 collective-permute-start.10
  22.5 0.0 collective-permute-done.16.rest_18_
  22.5 0.8 collective-permute-start.17
  23.3 2.6 %pool.7.rest_3_ = bf16[32,4096]{1,0:T(8,128)(2,1)S(1)} custom-call(bf16[4,128,4096]{2,1,0:T(8,128)(2,1)} %states_ref.7, bf16[32,4096]{1,0:T(8,128)(2,1)S(1)} %copy-done.4, bf16[4096]{0:T(1024)(128)(2,1)S(1)} %copy-done.7), custom_call_target="tpu_custom_call" | custom-call | flops 67108864 | bytes 1048576 | tf_op jit(solution)/shard_map/pool/pallas_call | solution.py:83
  25.9 3.3 %collective-permute-start.4 = (bf16[32,4096]{1,0:T(8,128)(2,1)S(1)}, bf16[32,4096]{1,0:T(8,128)(2,1)S(1)}, u32[]{:S(2)}, u32[]{:S(2)}) collective-permute-start(bf16[32,4096]{1,0:T(8,128)(2,1)S(1)} %pool.4.rest_0_), channel_id=1, source_target_pairs={{0,1},{1,0},{2,3},{3,2},{4,5},{5,4},{6,7},{7,6},{8,9},{9,8},{10,11... | collective-permute-start | bytes 786440 | tf_op jit(solution)/shard_map/ppermute | solution.py:435
  29.2 0.1 collective-permute-start.5
  29.3 0.7 copy-done.10
  30.0 0.4 collective-permute-start.6
  30.4 0.0 collective-permute-done.10.rest_11_
  30.4 1.3 collective-permute-start.11
  31.7 0.0 collective-permute-done.17.rest_19_
  31.7 0.4 collective-permute-start.7
  32.1 3.5 %collective-permute-done.11.rest_12_ = bf16[256,256]{1,0:T(8,128)(2,1)} collective-permute-done((bf16[256,256]{1,0:T(8,128)(2,1)}, bf16[256,256]{1,0:T(8,128)(2,1)}, u32[]{:S(2)}, u32[]{:S(2)}) %collective-permute-start.11) | collective-permute-done | bytes 131104 | tf_op jit(solution)/shard_map/ppermute | solution.py:439
  35.7 1.0 collective-permute-start.18
  36.7 0.0 collective-permute-done.4.rest_4_
  36.7 3.0 %collective-permute-done.18.rest_20_ = bf16[256,256]{1,0:T(8,128)(2,1)S(1)} collective-permute-done((bf16[256,256]{1,0:T(8,128)(2,1)}, bf16[256,256]{1,0:T(8,128)(2,1)S(1)}, u32[]{:S(2)}, u32[]{:S(2)}) %collective-permute-start.18) | collective-permute-done | bytes 131104 | tf_op jit(solution)/shard_map/ppermute | solution.py:439
  39.7 0.0 collective-permute-done.6.rest_6_
  39.7 0.0 collective-permute-done.7.rest_7_
  39.7 0.9 copy-done.9
  40.6 0.9 copy-done.11
  41.5 2.0 %project.1.rest_1_ = bf16[256,256]{1,0:T(8,128)(2,1)S(1)} custom-call(s32[1]{0:T(128)} %bitcast.1.core_ref.half_ref, s32[1]{0:T(128)} %bitcast.2.place_ref, bf16[32,4096]{1,0:T(8,128)(2,1)S(1)} %pool.4.rest_0_, bf16[32,4096]{1,0:T(8,128)(2,1)S(1)} %pool.5.rest_1_, bf16[32,4096]{1,0:T(8,128)(2,1)S(1)} %pool.6.rest_2_, bf16[32,4096]{1,0:T(8,128)(2,1)S(1)} %pool.7.rest_3_, ...), custom_call_target="tpu_custom_call" | custom-call | flops 536870912 | bytes 2097152 | tf_op jit(solution)/shard_map/project/pallas_call | solution.py:380
  43.5 3.8 %collective-permute-start.22 = (bf16[256,256]{1,0:T(8,128)(2,1)S(1)}, bf16[256,256]{1,0:T(8,128)(2,1)S(1)}, u32[]{:S(2)}, u32[]{:S(2)}) collective-permute-start(bf16[256,256]{1,0:T(8,128)(2,1)S(1)} %project.1.rest_1_), channel_id=1, source_target_pairs={{0,12},{1,13},{2,14},{3,15},{4,0},{5,1},{6,2},{7,3},{8,4},{9,5},{1... | collective-permute-start | bytes 393224 | tf_op jit(solution)/shard_map/ppermute | solution.py:439
  47.3 0.5 collective-permute-start.20
  47.8 2.6 %collective-permute-start.19 = (bf16[256,256]{1,0:T(8,128)(2,1)S(1)}, bf16[256,256]{1,0:T(8,128)(2,1)S(1)}, u32[]{:S(2)}, u32[]{:S(2)}) collective-permute-start(bf16[256,256]{1,0:T(8,128)(2,1)S(1)} %project.1.rest_1_), channel_id=1, source_target_pairs={{0,1},{1,0},{2,3},{3,2},{4,5},{5,4},{6,7},{7,6},{8,9},{9,8},{10,11... | collective-permute-start | bytes 393224 | tf_op jit(solution)/shard_map/ppermute | solution.py:435
  50.4 0.1 select_reduce_fusion.start_ref
  50.5 1.2 collective-permute-start.23
  51.8 2.1 %copy-done = bf16[4,64,7424]{2,1,0:T(8,128)(2,1)S(1)} copy-done((bf16[4,64,7424]{2,1,0:T(8,128)(2,1)S(1)}, bf16[4,64,7424]{2,1,0:T(8,128)(2,1)}, u32[]{:S(2)}) %copy-start) | copy-done | bytes 3801112
  53.8 5.7 %attend.6.rest_2_ = f32[4,1920,256]{2,1,0:T(8,128)} custom-call(s32[1]{0:T(128)} %bitcast.1.core_ref.half_ref, s32[4,16]{1,0:T(4,128)S(1)} %select_reduce_fusion.start_ref, s32[4]{0:T(128)S(1)} %copy-done.12, bf16[4,64,7424]{2,1,0:T(8,128)(2,1)S(1)} %copy-done, bf16[256,256]{1,0:T(8,128)(2,1)S(1)} %project.1.rest_1_, bf16[4,64,512]{2,1,0:T(8,128)(2,1)S(1)} %copy-done.2, ...), custom_call_target="tpu_custom_call" | custom-call | flops 486539264 | bytes 3801088 | tf_op jit(solution)/shard_map/attend/pallas_call | solution.py:340
  59.6 5.7 %attend.7.rest_2_ = f32[4,1920,256]{2,1,0:T(8,128)} custom-call(s32[1]{0:T(128)} %bitcast.half_ref, s32[4,16]{1,0:T(4,128)S(1)} %select_reduce_fusion.start_ref, s32[4]{0:T(128)S(1)} %copy-done.12, bf16[4,64,7424]{2,1,0:T(8,128)(2,1)S(1)} %copy-done.1, bf16[256,256]{1,0:T(8,128)(2,1)S(1)} %collective-permute-done.19.rest_1_, ...), custom_call_target="tpu_custom_call" | custom-call | flops 486539264 | bytes 3801088 | tf_op jit(solution)/shard_map/attend/pallas_call | solution.py:340
  65.3 0.4 collective-permute-start.25
  65.7 1.2 collective-permute-start.26
  66.9 0.3 collective-permute-start.27
  67.3 1.2 collective-permute-start.24
  68.5 9.9 %attend.8.rest_6_ = f32[4,1920,256]{2,1,0:T(8,128)} custom-call(s32[1]{0:T(128)} %bitcast.1.core_ref.half_ref, s32[4,16]{1,0:T(4,128)S(1)} %select_reduce_fusion.start_ref, s32[4]{0:T(128)S(1)} %copy-done.12, bf16[4,64,7424]{2,1,0:T(8,128)(2,1)S(1)} %copy-done.1, bf16[1024,256]{1,0:T(8,128)(2,1)S(1)} %constant_dynamic-update-slice_fusion.rest_1_.rest_2_, ...), custom_call_target="tpu_custom_call" | custom-call | flops 973078528 | bytes 3801088 | tf_op jit(solution)/shard_map/attend/pallas_call | solution.py:340
  78.4 0.1 collective-permute-start.28
  78.5 41.1 %attend.10.rest_7_ = bf16[4,64,7424]{2,1,0:T(8,128)(2,1)} custom-call(s32[1]{0:T(128)} %bitcast.1.core_ref.half_ref, s32[4,16]{1,0:T(4,128)S(1)} %select_reduce_fusion.start_ref, s32[4]{0:T(128)S(1)} %copy-done.12, bf16[4,64,7424]{2,1,0:T(8,128)(2,1)S(1)} %copy-done.1, bf16[256,256]{1,0:T(8,128)(2,1)S(1)} %project.1.rest_1_, ...), custom_call_target="tpu_custom_call" | custom-call | flops 729808896 | bytes 3801088 | tf_op jit(solution)/shard_map/attend/pallas_call | solution.py:340
  119.6 9.8 %attend.9.rest_6_ = f32[4,1920,256]{2,1,0:T(8,128)} custom-call(s32[1]{0:T(128)} %bitcast.half_ref, s32[4,16]{1,0:T(4,128)S(1)} %select_reduce_fusion.start_ref, s32[4]{0:T(128)S(1)} %copy-done.12, bf16[4,64,7424]{2,1,0:T(8,128)(2,1)S(1)} %copy-done.1, bf16[1024,256]{1,0:T(8,128)(2,1)S(1)} %collective-permute-done.24.rest_1_.rest_2_, ...), custom_call_target="tpu_custom_call" | custom-call | flops 973078528 | bytes 3801088 | tf_op jit(solution)/shard_map/attend/pallas_call | solution.py:340
  129.4 41.3 %attend.11 = bf16[4,64,7424]{2,1,0:T(8,128)(2,1)} custom-call(s32[1]{0:T(128)} %bitcast.half_ref, s32[4,16]{1,0:T(4,128)S(1)} %select_reduce_fusion.start_ref, s32[4]{0:T(128)S(1)} %copy-done.12, bf16[4,64,7424]{2,1,0:T(8,128)(2,1)S(1)} %copy-done.1, bf16[256,256]{1,0:T(8,128)(2,1)S(1)} %collective-permute-done.19.rest_1_, ...), custom_call_target="tpu_custom_call", output_to_operand_aliasing={{}: (10, {})} | custom-call | flops 729808896 | bytes 3801088 | tf_op jit(solution)/shard_map/attend/pallas_call | solution.py:340
  (46 shorter events, 0.2 us)
Async XLA Ops:
  0.0 17.1 %copy-start.7 = (bf16[4096]{0:T(1024)(128)(2,1)S(1)}, bf16[4096]{0:T(1024)(128)(2,1)}, u32[]{:S(2)}) copy-start(bf16[4096]{0:T(1024)(128)(2,1)} %gain_ref.7) | copy-start | bytes 24580
  0.0 23.3 %copy-start.4 = (bf16[32,4096]{1,0:T(8,128)(2,1)S(1)}, bf16[32,4096]{1,0:T(8,128)(2,1)}, u32[]{:S(2)}) copy-start(bf16[32,4096]{1,0:T(8,128)(2,1)} %queries_ref.7) | copy-start | bytes 786436
  1.0 1.4 collective-permute-start
  2.4 11.6 %collective-permute-start.1 = (bf16[256,256]{1,0:T(8,128)(2,1)S(1)}, bf16[256,256]{1,0:T(8,128)(2,1)S(1)}, u32[]{:S(2)}, u32[]{:S(2)}) collective-permute-start(bf16[256,256]{1,0:T(8,128)(2,1)S(1)} %collective-permute-done.rest_16_), channel_id=1, source_target_pairs={{0,2},{1,3},{2,6},{3,7},{4,0},{5,1},{6,10},{7,11},{8,4},{9,5},{10,... | collective-permute-start | bytes 393224 | tf_op jit(solution)/shard_map/ppermute | solution.py:439
  4.8 10.6 %collective-permute-start.12 = (bf16[256,256]{1,0:T(8,128)(2,1)S(1)}, bf16[256,256]{1,0:T(8,128)(2,1)S(1)}, u32[]{:S(2)}, u32[]{:S(2)}) collective-permute-start(bf16[256,256]{1,0:T(8,128)(2,1)S(1)} %pad_maximum_fusion.1.rest_8_), channel_id=1, source_target_pairs={{0,2},{1,3},{2,6},{3,7},{4,0},{5,1},{6,10},{7,11},{8,4},{9,5},{10,... | collective-permute-start | bytes 393224 | tf_op jit(solution)/shard_map/ppermute | solution.py:439
  6.2 10.6 %collective-permute-start.8 = (bf16[256,256]{1,0:T(8,128)(2,1)S(1)}, bf16[256,256]{1,0:T(8,128)(2,1)S(1)}, u32[]{:S(2)}, u32[]{:S(2)}) collective-permute-start(bf16[256,256]{1,0:T(8,128)(2,1)S(1)} %pad_maximum_fusion.1.rest_8_), channel_id=1, source_target_pairs={{0,4},{1,5},{2,0},{3,1},{4,8},{5,9},{6,2},{7,3},{8,12},{9,13},{10,... | collective-permute-start | bytes 393224 | tf_op jit(solution)/shard_map/ppermute | solution.py:439
  6.3 10.6 %collective-permute-start.15 = (bf16[256,256]{1,0:T(8,128)(2,1)S(1)}, bf16[256,256]{1,0:T(8,128)(2,1)S(1)}, u32[]{:S(2)}, u32[]{:S(2)}) collective-permute-start(bf16[256,256]{1,0:T(8,128)(2,1)S(1)} %collective-permute-done.rest_16_), channel_id=1, source_target_pairs={{0,4},{1,5},{2,0},{3,1},{4,8},{5,9},{6,2},{7,3},{8,12},{9,13},{10,... | collective-permute-start | bytes 393224 | tf_op jit(solution)/shard_map/ppermute | solution.py:439
  6.5 0.9 copy-start.3
  7.4 0.7 copy-start.5
  10.7 0.7 copy-start.6
  11.4 20.7 %copy-start.13 = (s32[4,16]{1,0:T(4,128)S(1)}, s32[4,16]{1,0:T(4,128)}, u32[]{:S(2)}) copy-start(s32[4,16]{1,0:T(4,128)} %param.12) | copy-start | bytes 772
  14.1 37.7 %copy-start.2 = (bf16[4,64,512]{2,1,0:T(8,128)(2,1)S(1)}, bf16[4,64,512]{2,1,0:T(8,128)(2,1)}, u32[]{:S(2)}) copy-start(bf16[4,64,512]{2,1,0:T(8,128)(2,1)} %rest_5_.3) | copy-start | bytes 786436
  14.1 37.7 %copy-start.12 = (s32[4]{0:T(128)S(1)}, s32[4]{0:T(128)}, u32[]{:S(2)}) copy-start(s32[4]{0:T(128)} %length_ref.11) | copy-start | bytes 52
  14.1 5.6 %collective-permute-start.2 = (bf16[256,256]{1,0:T(8,128)(2,1)S(1)}, bf16[256,256]{1,0:T(8,128)(2,1)S(1)}, u32[]{:S(2)}, u32[]{:S(2)}) collective-permute-start(bf16[256,256]{1,0:T(8,128)(2,1)S(1)} %collective-permute-done.1.rest_23_), channel_id=1, source_target_pairs={{0,2},{1,3},{2,6},{3,7},{4,0},{5,1},{6,10},{7,11},{8,4},{9,5},{10,... | collective-permute-start | bytes 393224 | tf_op jit(solution)/shard_map/ppermute | solution.py:439
  15.5 5.6 %collective-permute-start.13 = (bf16[256,256]{1,0:T(8,128)(2,1)S(1)}, bf16[256,256]{1,0:T(8,128)(2,1)S(1)}, u32[]{:S(2)}, u32[]{:S(2)}) collective-permute-start(bf16[256,256]{1,0:T(8,128)(2,1)S(1)} %collective-permute-done.12.rest_15_), channel_id=1, source_target_pairs={{0,2},{1,3},{2,6},{3,7},{4,0},{5,1},{6,10},{7,11},{8,4},{9,5},{10,... | collective-permute-start | bytes 393224 | tf_op jit(solution)/shard_map/ppermute | solution.py:439
  16.8 5.6 %collective-permute-start.9 = (bf16[256,256]{1,0:T(8,128)(2,1)S(1)}, bf16[256,256]{1,0:T(8,128)(2,1)S(1)}, u32[]{:S(2)}, u32[]{:S(2)}) collective-permute-start(bf16[256,256]{1,0:T(8,128)(2,1)S(1)} %collective-permute-done.8.rest_9_), channel_id=1, source_target_pairs={{0,4},{1,5},{2,0},{3,1},{4,8},{5,9},{6,2},{7,3},{8,12},{9,13},{10,... | collective-permute-start | bytes 393224 | tf_op jit(solution)/shard_map/ppermute | solution.py:439
  16.9 5.6 %collective-permute-start.16 = (bf16[256,256]{1,0:T(8,128)(2,1)S(1)}, bf16[256,256]{1,0:T(8,128)(2,1)S(1)}, u32[]{:S(2)}, u32[]{:S(2)}) collective-permute-start(bf16[256,256]{1,0:T(8,128)(2,1)S(1)} %collective-permute-done.15.rest_17_), channel_id=1, source_target_pairs={{0,4},{1,5},{2,0},{3,1},{4,8},{5,9},{6,2},{7,3},{8,12},{9,13},{10,... | collective-permute-start | bytes 393224 | tf_op jit(solution)/shard_map/ppermute | solution.py:439
  19.7 9.5 %collective-permute-start.3 = (bf16[256,256]{1,0:T(8,128)(2,1)S(1)}, bf16[256,256]{1,0:T(8,128)(2,1)}, u32[]{:S(2)}, u32[]{:S(2)}) collective-permute-start(bf16[256,256]{1,0:T(8,128)(2,1)S(1)} %collective-permute-done.2.rest_22_), channel_id=1, source_target_pairs={{0,2},{1,3},{2,6},{3,7},{4,0},{5,1},{6,10},{7,11},{8,4},{9,5},{10,... | collective-permute-start | bytes 393224 | tf_op jit(solution)/shard_map/ppermute | solution.py:439
  21.1 8.3 %collective-permute-start.14 = (bf16[256,256]{1,0:T(8,128)(2,1)S(1)}, bf16[256,256]{1,0:T(8,128)(2,1)S(1)}, u32[]{:S(2)}, u32[]{:S(2)}) collective-permute-start(bf16[256,256]{1,0:T(8,128)(2,1)S(1)} %collective-permute-done.13.rest_14_), channel_id=1, source_target_pairs={{0,2},{1,3},{2,6},{3,7},{4,0},{5,1},{6,10},{7,11},{8,4},{9,5},{10,... | collective-permute-start | bytes 393224 | tf_op jit(solution)/shard_map/ppermute | solution.py:439
  22.4 8.1 %collective-permute-start.10 = (bf16[256,256]{1,0:T(8,128)(2,1)S(1)}, bf16[256,256]{1,0:T(8,128)(2,1)}, u32[]{:S(2)}, u32[]{:S(2)}) collective-permute-start(bf16[256,256]{1,0:T(8,128)(2,1)S(1)} %collective-permute-done.9.rest_10_), channel_id=1, source_target_pairs={{0,4},{1,5},{2,0},{3,1},{4,8},{5,9},{6,2},{7,3},{8,12},{9,13},{10,... | collective-permute-start | bytes 393224 | tf_op jit(solution)/shard_map/ppermute | solution.py:439
  22.5 9.2 %copy-start.8 = (bf16[256,256]{1,0:T(8,128)(2,1)}, bf16[256,256]{1,0:T(8,128)(2,1)S(1)}, u32[]{:S(2)}) copy-start(bf16[256,256]{1,0:T(8,128)(2,1)S(1)} %collective-permute-done.16.rest_18_) | copy-start | bytes 393220
  22.5 9.2 %collective-permute-start.17 = (bf16[256,256]{1,0:T(8,128)(2,1)S(1)}, bf16[256,256]{1,0:T(8,128)(2,1)}, u32[]{:S(2)}, u32[]{:S(2)}) collective-permute-start(bf16[256,256]{1,0:T(8,128)(2,1)S(1)} %collective-permute-done.16.rest_18_), channel_id=1, source_target_pairs={{0,4},{1,5},{2,0},{3,1},{4,8},{5,9},{6,2},{7,3},{8,12},{9,13},{10,... | collective-permute-start | bytes 393224 | tf_op jit(solution)/shard_map/ppermute | solution.py:439
  25.9 10.7 %collective-permute-start.4 = (bf16[32,4096]{1,0:T(8,128)(2,1)S(1)}, bf16[32,4096]{1,0:T(8,128)(2,1)S(1)}, u32[]{:S(2)}, u32[]{:S(2)}) collective-permute-start(bf16[32,4096]{1,0:T(8,128)(2,1)S(1)} %pool.4.rest_0_), channel_id=1, source_target_pairs={{0,1},{1,0},{2,3},{3,2},{4,5},{5,4},{6,7},{7,6},{8,9},{9,8},{10,11... | collective-permute-start | bytes 786440 | tf_op jit(solution)/shard_map/ppermute | solution.py:435
  29.2 7.4 %collective-permute-start.5 = (bf16[32,4096]{1,0:T(8,128)(2,1)S(1)}, bf16[32,4096]{1,0:T(8,128)(2,1)S(1)}, u32[]{:S(2)}, u32[]{:S(2)}) collective-permute-start(bf16[32,4096]{1,0:T(8,128)(2,1)S(1)} %pool.5.rest_1_), channel_id=1, source_target_pairs={{0,1},{1,0},{2,3},{3,2},{4,5},{5,4},{6,7},{7,6},{8,9},{9,8},{10,11... | collective-permute-start | bytes 786440 | tf_op jit(solution)/shard_map/ppermute | solution.py:435
  29.3 0.7 copy-start.10
  30.0 9.7 %collective-permute-start.6 = (bf16[32,4096]{1,0:T(8,128)(2,1)S(1)}, bf16[32,4096]{1,0:T(8,128)(2,1)S(1)}, u32[]{:S(2)}, u32[]{:S(2)}) collective-permute-start(bf16[32,4096]{1,0:T(8,128)(2,1)S(1)} %pool.6.rest_2_), channel_id=1, source_target_pairs={{0,1},{1,0},{2,3},{3,2},{4,5},{5,4},{6,7},{7,6},{8,9},{9,8},{10,11... | collective-permute-start | bytes 786440 | tf_op jit(solution)/shard_map/ppermute | solution.py:435
  30.4 5.2 %collective-permute-start.11 = (bf16[256,256]{1,0:T(8,128)(2,1)}, bf16[256,256]{1,0:T(8,128)(2,1)}, u32[]{:S(2)}, u32[]{:S(2)}) collective-permute-start(bf16[256,256]{1,0:T(8,128)(2,1)} %collective-permute-done.10.rest_11_), channel_id=1, source_target_pairs={{0,4},{1,5},{2,0},{3,1},{4,8},{5,9},{6,2},{7,3},{8,12},{9,13},{10,... | collective-permute-start | bytes 393224 | tf_op jit(solution)/shard_map/ppermute | solution.py:439
  31.7 8.0 %collective-permute-start.7 = (bf16[32,4096]{1,0:T(8,128)(2,1)S(1)}, bf16[32,4096]{1,0:T(8,128)(2,1)S(1)}, u32[]{:S(2)}, u32[]{:S(2)}) collective-permute-start(bf16[32,4096]{1,0:T(8,128)(2,1)S(1)} %pool.7.rest_3_), channel_id=1, source_target_pairs={{0,1},{1,0},{2,3},{3,2},{4,5},{5,4},{6,7},{7,6},{8,9},{9,8},{10,11... | collective-permute-start | bytes 786440 | tf_op jit(solution)/shard_map/ppermute | solution.py:435
  35.7 4.0 %collective-permute-start.18 = (bf16[256,256]{1,0:T(8,128)(2,1)}, bf16[256,256]{1,0:T(8,128)(2,1)S(1)}, u32[]{:S(2)}, u32[]{:S(2)}) collective-permute-start(bf16[256,256]{1,0:T(8,128)(2,1)} %collective-permute-done.3.rest_21_), channel_id=1, source_target_pairs={{0,2},{1,3},{2,6},{3,7},{4,0},{5,1},{6,10},{7,11},{8,4},{9,5},{10,... | collective-permute-start | bytes 393224 | tf_op jit(solution)/shard_map/ppermute | solution.py:439
  39.7 0.9 copy-start.9
  40.6 0.9 copy-start.11
  41.5 18.1 %copy-start.1 = (bf16[4,64,7424]{2,1,0:T(8,128)(2,1)S(1)}, bf16[4,64,7424]{2,1,0:T(8,128)(2,1)}, u32[]{:S(2)}) copy-start(bf16[4,64,7424]{2,1,0:T(8,128)(2,1)} %rest_0_.11) | copy-start | bytes 11403268
  43.5 21.8 %collective-permute-start.22 = (bf16[256,256]{1,0:T(8,128)(2,1)S(1)}, bf16[256,256]{1,0:T(8,128)(2,1)S(1)}, u32[]{:S(2)}, u32[]{:S(2)}) collective-permute-start(bf16[256,256]{1,0:T(8,128)(2,1)S(1)} %project.1.rest_1_), channel_id=1, source_target_pairs={{0,12},{1,13},{2,14},{3,15},{4,0},{5,1},{6,2},{7,3},{8,4},{9,5},{1... | collective-permute-start | bytes 393224 | tf_op jit(solution)/shard_map/ppermute | solution.py:439
  47.3 18.0 %collective-permute-start.21 = (bf16[256,256]{1,0:T(8,128)(2,1)S(1)}, bf16[256,256]{1,0:T(8,128)(2,1)S(1)}, u32[]{:S(2)}, u32[]{:S(2)}) collective-permute-start(bf16[256,256]{1,0:T(8,128)(2,1)S(1)} %project.1.rest_1_), channel_id=1, source_target_pairs={{0,8},{1,9},{2,10},{3,11},{4,12},{5,13},{6,14},{7,15},{8,0},{9,1},... | collective-permute-start | bytes 393224 | tf_op jit(solution)/shard_map/ppermute | solution.py:439
  47.3 18.0 %collective-permute-start.20 = (bf16[256,256]{1,0:T(8,128)(2,1)S(1)}, bf16[256,256]{1,0:T(8,128)(2,1)S(1)}, u32[]{:S(2)}, u32[]{:S(2)}) collective-permute-start(bf16[256,256]{1,0:T(8,128)(2,1)S(1)} %project.1.rest_1_), channel_id=1, source_target_pairs={{0,4},{1,5},{2,6},{3,7},{4,8},{5,9},{6,10},{7,11},{8,12},{9,13},{1... | collective-permute-start | bytes 393224 | tf_op jit(solution)/shard_map/ppermute | solution.py:439
  47.8 11.8 %collective-permute-start.19 = (bf16[256,256]{1,0:T(8,128)(2,1)S(1)}, bf16[256,256]{1,0:T(8,128)(2,1)S(1)}, u32[]{:S(2)}, u32[]{:S(2)}) collective-permute-start(bf16[256,256]{1,0:T(8,128)(2,1)S(1)} %project.1.rest_1_), channel_id=1, source_target_pairs={{0,1},{1,0},{2,3},{3,2},{4,5},{5,4},{6,7},{7,6},{8,9},{9,8},{10,11... | collective-permute-start | bytes 393224 | tf_op jit(solution)/shard_map/ppermute | solution.py:435
  50.5 16.8 %collective-permute-start.23 = (bf16[256,256]{1,0:T(8,128)(2,1)S(1)}, bf16[256,256]{1,0:T(8,128)(2,1)S(1)}, u32[]{:S(2)}, u32[]{:S(2)}) collective-permute-start(bf16[256,256]{1,0:T(8,128)(2,1)S(1)} %project.1.rest_1_), channel_id=1, source_target_pairs={{0,2},{1,3},{2,0},{3,1},{4,6},{5,7},{6,4},{7,5},{8,10},{9,11},{10,... | collective-permute-start | bytes 393224 | tf_op jit(solution)/shard_map/ppermute | solution.py:439
  51.8 2.1 %copy-start = (bf16[4,64,7424]{2,1,0:T(8,128)(2,1)S(1)}, bf16[4,64,7424]{2,1,0:T(8,128)(2,1)}, u32[]{:S(2)}) copy-start(bf16[4,64,7424]{2,1,0:T(8,128)(2,1)} %rest_0_.11) | copy-start | bytes 11403268
  65.3 13.0 %collective-permute-start.25 = (bf16[256,256]{1,0:T(8,128)(2,1)S(1)}, bf16[256,256]{1,0:T(8,128)(2,1)S(1)}, u32[]{:S(2)}, u32[]{:S(2)}) collective-permute-start(bf16[256,256]{1,0:T(8,128)(2,1)S(1)} %collective-permute-done.20), channel_id=1, source_target_pairs={{0,2},{1,3},{2,0},{3,1},{4,6},{5,7},{6,4},{7,5},{8,10},{9,11},{10,... | collective-permute-start | bytes 393224 | tf_op jit(solution)/shard_map/ppermute | solution.py:439
  65.7 12.6 %collective-permute-start.26 = (bf16[256,256]{1,0:T(8,128)(2,1)S(1)}, bf16[256,256]{1,0:T(8,128)(2,1)S(1)}, u32[]{:S(2)}, u32[]{:S(2)}) collective-permute-start(bf16[256,256]{1,0:T(8,128)(2,1)S(1)} %collective-permute-done.21), channel_id=1, source_target_pairs={{0,2},{1,3},{2,0},{3,1},{4,6},{5,7},{6,4},{7,5},{8,10},{9,11},{10,... | collective-permute-start | bytes 393224 | tf_op jit(solution)/shard_map/ppermute | solution.py:439
  66.9 11.4 %collective-permute-start.27 = (bf16[256,256]{1,0:T(8,128)(2,1)S(1)}, bf16[256,256]{1,0:T(8,128)(2,1)S(1)}, u32[]{:S(2)}, u32[]{:S(2)}) collective-permute-start(bf16[256,256]{1,0:T(8,128)(2,1)S(1)} %collective-permute-done.22), channel_id=1, source_target_pairs={{0,2},{1,3},{2,0},{3,1},{4,6},{5,7},{6,4},{7,5},{8,10},{9,11},{10,... | collective-permute-start | bytes 393224 | tf_op jit(solution)/shard_map/ppermute | solution.py:439
  67.3 52.3 %collective-permute-start.24 = (bf16[1024,256]{1,0:T(8,128)(2,1)S(1)}, bf16[1024,256]{1,0:T(8,128)(2,1)S(1)}, u32[]{:S(2)}, u32[]{:S(2)}) collective-permute-start(bf16[1024,256]{1,0:T(8,128)(2,1)S(1)} %constant_dynamic-update-slice_fusion.rest_1_.rest_2_), channel_id=1, source_target_pairs={{0,1},{1,0},{2,3},{3,2},{4,5},{5,4},{6,7},{7,6},{8,9},{9,8},{10,11... | collective-permute-start | bytes 1572872 | tf_op jit(solution)/shard_map/ppermute | solution.py:435
  78.4 51.0 %collective-permute-start.28 = (bf16[768,256]{1,0:T(8,128)(2,1)S(1)}, bf16[768,256]{1,0:T(8,128)(2,1)S(1)}, u32[]{:S(2)}, u32[]{:S(2)}) collective-permute-start(bf16[768,256]{1,0:T(8,128)(2,1)S(1)} %constant_dynamic-update-slice_fusion.4.rest_3_), channel_id=1, source_target_pairs={{0,1},{1,0},{2,3},{3,2},{4,5},{5,4},{6,7},{7,6},{8,9},{9,8},{10,11... | collective-permute-start | bytes 1179656 | tf_op jit(solution)/shard_map/ppermute | solution.py:435

commit v7 on v0

v7 whole, which is shorter than its diff:
```python
import functools
import math

import jax
import jax.numpy as jnp
from jax import lax
from jax.experimental import pallas as pl
from jax.experimental.pallas import tpu as pltpu
from jax.sharding import PartitionSpec as P

D = 4096
CH = 32
CHD = 128
MEM = 32
LEN = 128
QLEN = 64
TOPK = 16
H = 116
HD = 64
KVH = 4
GROUP = 29
KVW = 512

LANES = 2 * HD
PAIRS = GROUP
HALF = PAIRS * LANES
ROWS = TOPK * MEM
KEYS = 2 * (ROWS + QLEN)
NEG = -1e30
SUM_LOW, SUM_HIGH = 2.0 ** -40, 2.0 ** 60
CHIP = 8
STEP = 8
GROUP_QUERIES = 2
MIB = 1024 * 1024


def place_of(chip, ring):
    line, lane = lax.div(chip, 2), lax.rem(chip, 2)
    return line + lane * (ring - 1 - 2 * line)


def chip_at(place, ring):
    lane = lax.div(place, ring // 2)
    line = place + lane * (ring - 1 - 2 * place)
    return 2 * line + lane


def pool_kernel(states_ref, queries_ref, gain_ref, out_ref, pooled, squares):
    step = pl.program_id(0)
    passages = states_ref.shape[0]
    heads = CHD // MEM
    stacked = jnp.concatenate(
        [queries_ref[:, i * CHD:(i + 1) * CHD] for i in range(heads)], axis=0
    ).astype(jnp.float32)
    turned = jnp.transpose(stacked)
    head_of = lax.broadcasted_iota(jnp.int32, (CHD, CHD), 1) // MEM
    side = jnp.concatenate(
        [jnp.where(head_of == i, turned, 0.0).astype(jnp.bfloat16) for i in range(heads)], axis=0
    )
    tokens = states_ref[...].reshape(passages * LEN, heads * CHD)
    scores = jnp.dot(tokens, side, preferred_element_type=jnp.float32) * (1.0 / math.sqrt(CHD))
    for p in range(passages):
        part = scores[p * LEN:(p + 1) * LEN]
        part = jnp.exp(part - jnp.max(part, axis=0, keepdims=True))
        weights = (part / jnp.sum(part, axis=0, keepdims=True)).astype(jnp.bfloat16)
        mixed = lax.dot_general(
            weights, states_ref[p], (((0,), (0,)), ((), ())), preferred_element_type=jnp.float32
        )
        rows = slice(p * MEM, (p + 1) * MEM)
        total = jnp.zeros((MEM, CHD), jnp.float32)
        for i in range(heads):
            block = mixed[i * MEM:(i + 1) * MEM, i * CHD:(i + 1) * CHD]
            at = pl.multiple_of(step * (heads * CHD) + i * CHD, CHD)
            pooled[rows, pl.ds(at, CHD)] = block
            total += block * block
        squares[rows, :] = total + jnp.where(step == 0, 0.0, squares[rows, :])

    @pl.when(step == pl.num_programs(0) - 1)
    def _():
        mean_square = jnp.sum(squares[...], axis=1, keepdims=True) * (1.0 / D)
        scale = lax.rsqrt(mean_square + 1e-06)
        gain = gain_ref[...].astype(jnp.float32).reshape(1, D)
        out_ref[...] = (pooled[...] * scale * gain).astype(jnp.bfloat16)


def pool(states, queries, gain):
    count = states.shape[0]
    width = CHD // MEM * CHD
    return pl.pallas_call(
        pool_kernel,
        grid=(D // width,),
        in_specs=[
            pl.BlockSpec((count, LEN, width), lambda j: (0, 0, j)),
            pl.BlockSpec((MEM, width), lambda j: (0, j)),
            pl.BlockSpec((D,), lambda j: (0,)),
        ],
        out_specs=pl.BlockSpec((count * MEM, D), lambda j: (0, 0)),
        out_shape=jax.ShapeDtypeStruct((count * MEM, D), jnp.bfloat16),
        scratch_shapes=[
            pltpu.VMEM((count * MEM, D), jnp.float32),
            pltpu.VMEM((count * MEM, CHD), jnp.float32),
        ],
        compiler_params=pltpu.CompilerParams(vmem_limit_bytes=52 * MIB),
        cost_estimate=pl.CostEstimate(
            flops=4 * count * MEM * LEN * D, bytes_accessed=2 * count * LEN * D,
            transcendentals=count * CH * MEM * LEN,
        ),
        name="pool",
    )(states, queries, gain)


def attend_kernel(g, half_ref, start_ref, length_ref, q_ref, kv_ref, own_k_ref, own_v_ref, *rest):
    tile_ref = rest[0] if g else None
    out_ref, memory, key_side, value_side, weights, marker, scores, all_weights = rest[-8:]
    step = pl.program_id(0)
    group = q_ref.shape[0]
    factor = math.log2(math.e) / math.sqrt(HD)
    token = lax.broadcasted_iota(jnp.int32, (QLEN, LANES), 0)
    low = lax.broadcasted_iota(jnp.int32, (QLEN, LANES), 1) < HD
    own_key = lax.rem(lax.broadcasted_iota(jnp.int32, (QLEN, LANES), 1), HD)
    lengths = [length_ref[step * group + u] for u in range(group)]
    causal = [jnp.where((own_key <= token) & (own_key < n), 0.0, NEG) for n in lengths]

    @pl.when(step == 0)
    def _():
        lane = lax.broadcasted_iota(jnp.int32, (KEYS, LANES), 1)
        row = lax.broadcasted_iota(jnp.int32, (KEYS, LANES), 0)
        in_b = ((row >= ROWS) & (row < 2 * ROWS)) | (row >= 2 * ROWS + QLEN)
        ones = jnp.where((lane >= HD) == in_b, 1.0, 0.0).astype(jnp.bfloat16)
        for u in range(group):
            key_side[u] = jnp.zeros((LANES, KEYS), jnp.bfloat16)
            value_side[u, :, LANES:] = ones

    def fill_keys(u):
        for slot in range(TOPK):
            start = pl.multiple_of(start_ref[step * group + u, slot], MEM)
            memory[u, slot * MEM:(slot + 1) * MEM, :] = kv_ref[pl.ds(start, MEM), :].astype(jnp.float32)
        turned = jnp.transpose(memory[u])[:HD].astype(jnp.bfloat16)
        own = own_k_ref[u].astype(jnp.float32)
        own = jnp.transpose(jnp.concatenate([own, own], axis=0))[g * HD:(g + 1) * HD]
        column = lax.broadcasted_iota(jnp.int32, (HD, LANES), 1)
        for member in range(2):
            rows = slice(member * HD, (member + 1) * HD)
            key_side[u, rows, member * ROWS:(member + 1) * ROWS] = turned
            mine = (column >= HD) if member else (column < HD)
            key_side[u, rows, 2 * ROWS:] = jnp.where(mine, own, 0.0).astype(jnp.bfloat16)

    def fill_values(u):
        own = own_v_ref[u].astype(jnp.float32)
        parts = (
            (pltpu.roll(memory[u], HD, 1), memory[u], 0, ROWS),
            (pltpu.roll(own, HD, 1) if g else own, own if g else pltpu.roll(own, HD, 1), 2 * ROWS, QLEN),
        )
        for in_low, in_high, at, size in parts:
            lower = lax.broadcasted_iota(jnp.int32, in_low.shape, 1) < HD
            value_side[u, at:at + size, :LANES] = jnp.where(lower, in_low, 0.0).astype(jnp.bfloat16)
            value_side[u, at + size:at + 2 * size, :LANES] = jnp.where(lower, 0.0, in_high).astype(
                jnp.bfloat16
            )

    tiles = list(range(PAIRS // 2 + 1))
    chunks = [(u, tiles[at:at + STEP]) for u in range(group) for at in range(0, len(tiles), STEP)]

    def questions(u, span):
        return jnp.concatenate([q_ref[u, :, t * LANES:(t + 1) * LANES] for t in span], axis=0)

    def key_product(i):
        u, span = chunks[i]
        lhs = questions(u, span)
        for c in range(0, KEYS, 2 * LANES):
            part = slice(c, min(c + 2 * LANES, KEYS))
            got = jnp.dot(lhs, key_side[u, :, part], preferred_element_type=jnp.float32) * factor
            if c == 2 * ROWS:
                got = got + jnp.concatenate([causal[u]] * len(span), axis=0)
            weights[i % 2, :len(span) * QLEN, part] = jnp.exp2(got).astype(jnp.bfloat16)

    def finish(i, mixed):
        u, span = chunks[i]
        for n, t in enumerate(span):
            rows = slice(n * QLEN, (n + 1) * QLEN)
            result = jnp.where(token < lengths[u], mixed[rows, :LANES] / mixed[rows, LANES:], 0.0)
            result = result.astype(jnp.bfloat16)
            if g and t == 0:
                result = jnp.where(low, tile_ref[u], result)
            out_ref[u, :, t * LANES:(t + 1) * LANES] = result

    def value_product(i, seen):
        u, span = chunks[i]
        size = len(span) * QLEN
        mixed = jnp.dot(weights[i % 2, :size, :], value_side[u], preferred_element_type=jnp.float32)
        for at in range(0, size, QLEN):
            total = mixed[at:at + QLEN, LANES:]
            seen[u] = jnp.where((total > SUM_LOW) & (total < SUM_HIGH), seen[u], 1.0)
        finish(i, mixed)

    seen = [jnp.zeros((QLEN, LANES), jnp.float32) for _ in range(group)]
    fill_keys(0)
    key_product(0)
    fill_values(0)
    for i, (u, _) in enumerate(chunks):
        if i + 1 < len(chunks):
            if chunks[i + 1][0] != u:
                fill_keys(u + 1)
            key_product(i + 1)
        value_product(i, seen)
        if i + 1 < len(chunks) and chunks[i + 1][0] != u:
            fill_values(u + 1)
    for u in range(group):
        marker[u] = jnp.max(seen[u])

    for u in range(group):

        @pl.when(marker[u] > 0.0)
        def _(u=u):
            for i, (owner, span) in enumerate(chunks):
                if owner != u:
                    continue
                size = len(span) * QLEN
                scores[:size, :] = jnp.dot(
                    questions(u, span), key_side[u], preferred_element_type=jnp.float32
                )

                def soften(n, carry):
                    rows = pl.ds(pl.multiple_of(n * QLEN, QLEN), QLEN)
                    own_scores = scores[rows, 2 * ROWS:] + causal[u]
                    tops = []
                    for member in range(2):
                        columns = slice(member * ROWS, (member + 1) * ROWS)
                        top = jnp.where(low, own_scores, NEG) if member == 0 else jnp.where(low, NEG, own_scores)
                        top = jnp.maximum(
                            jnp.max(top, axis=1, keepdims=True),
                            jnp.max(scores[rows, columns], axis=1, keepdims=True),
                        )
                        all_weights[rows, columns] = jnp.exp2(
                            (scores[rows, columns] - top) * factor
                        ).astype(jnp.bfloat16)
                        tops.append(top)
                    all_weights[rows, 2 * ROWS:] = jnp.exp2(
                        (own_scores - jnp.where(low, tops[0], tops[1])) * factor
                    ).astype(jnp.bfloat16)
                    return carry

                lax.fori_loop(0, len(span), soften, 0)
                finish(
                    i, jnp.dot(all_weights[:size, :], value_side[u], preferred_element_type=jnp.float32)
                )


def attend(g, half, starts, lengths, questions, own_kv, memory_kv, earlier=None):
    count = questions.shape[0]
    width = (PAIRS // 2 + 1) * LANES
    shift = HALF - width if g else 0

    def columns(q, h, *_):
        return q * GROUP_QUERIES, 0, pl.multiple_of(h[0] * HALF + shift, LANES)

    block = (pl.Element(GROUP_QUERIES), pl.Element(QLEN), pl.Element(width))
    own_block = (GROUP_QUERIES, QLEN, LANES)
    operands = [half.reshape(1), starts, lengths, questions, memory_kv, own_kv, own_kv]
    in_specs = [
        pl.BlockSpec(block, columns),
        pl.BlockSpec(memory_kv.shape, lambda q, *_: (0, 0)),
        pl.BlockSpec(own_block, lambda q, h, *_: (q, 0, h[0])),
        pl.BlockSpec(own_block, lambda q, h, *_: (q, 0, 2 + h[0])),
    ]
    aliases = {}
    if earlier is not None:
        aliases = {len(operands): 0}
        operands.append(earlier)
        if g:
            in_specs.append(pl.BlockSpec(own_block, lambda q, h, *_: (q, 0, h[0] * PAIRS + PAIRS // 2)))
        else:
            in_specs.append(pl.BlockSpec(memory_space=pl.ANY))
    return pl.pallas_call(
        functools.partial(attend_kernel, g),
        grid_spec=pltpu.PrefetchScalarGridSpec(
            num_scalar_prefetch=3,
            grid=(count // GROUP_QUERIES,),
            in_specs=in_specs,
            out_specs=pl.BlockSpec(block, columns),
            scratch_shapes=[
                pltpu.VMEM((GROUP_QUERIES, ROWS, LANES), jnp.float32),
                pltpu.VMEM((GROUP_QUERIES, LANES, KEYS), jnp.bfloat16),
                pltpu.VMEM((GROUP_QUERIES, KEYS, 2 * LANES), jnp.bfloat16),
                pltpu.VMEM((2, STEP * QLEN, KEYS), jnp.bfloat16),
                pltpu.SMEM((GROUP_QUERIES,), jnp.float32),
                pltpu.VMEM((STEP * QLEN, KEYS), jnp.float32),
                pltpu.VMEM((STEP * QLEN, KEYS), jnp.bfloat16),
            ],
        ),
        out_shape=jax.ShapeDtypeStruct((count, QLEN, H * HD), jnp.bfloat16),
        input_output_aliases=aliases,
        compiler_params=pltpu.CompilerParams(vmem_limit_bytes=48 * MIB),
        cost_estimate=pl.CostEstimate(
            flops=8 * count * QLEN * H * HD * (ROWS + QLEN) // 2,
            bytes_accessed=count * QLEN * H * HD,
            transcendentals=count * QLEN * H * (ROWS + QLEN) // 4,
        ),
        name="attend",
    )(*operands)


def project_kernel(ring, core_ref, place_ref, *rest):
    own_ref, other_ref, *weights, first_ref, second_ref = rest
    count = own_ref.shape[0]
    depth = weights[0].shape[0]
    total = jnp.zeros((2 * count, weights[0].shape[1]), jnp.float32)
    core = core_ref[0]
    for n, weight in enumerate(weights):
        part, i = n // ring, n % ring
        chip = chip_at(lax.rem(ring + place_ref[0] - i, ring), ring)
        at = pl.multiple_of((2 * chip + (1 - core if part else core)) * depth, depth)
        rows = jnp.concatenate([own_ref[:, pl.ds(at, depth)], other_ref[:, pl.ds(at, depth)]], axis=0)
        total += jnp.dot(rows, weight[...], preferred_element_type=jnp.float32)
    keys, values = total[:, :LANES], total[:, LANES:]
    low = lax.broadcasted_iota(jnp.int32, keys.shape, 1) < HD
    for out_ref, result in (
        (first_ref, jnp.where(low, keys, pltpu.roll(values, HD, 1))),
        (second_ref, jnp.where(low, pltpu.roll(keys, HD, 1), values)),
    ):
        result = result.astype(jnp.bfloat16)
        out_ref[pl.ds(pl.multiple_of(core * count, count), count)] = result[:count]
        out_ref[pl.ds(pl.multiple_of((1 - core) * count, count), count)] = result[count:]


def project(core, place, own_rows, other_rows, weights):
    count = own_rows.shape[0]
    width = weights[0].shape[1]
    vmem = pl.BlockSpec(memory_space=pltpu.VMEM)
    smem = pl.BlockSpec(memory_space=pltpu.SMEM)
    return pl.pallas_call(
        functools.partial(project_kernel, len(weights) // 2),
        in_specs=[smem, smem] + [vmem] * (2 + len(weights)),
        out_specs=[vmem, vmem],
        out_shape=[jax.ShapeDtypeStruct((2 * count, LANES), jnp.bfloat16)] * 2,
        compiler_params=pltpu.CompilerParams(vmem_limit_bytes=16 * MIB),
        cost_estimate=pl.CostEstimate(
            flops=4 * count * D * width, bytes_accessed=2 * D * width, transcendentals=0
        ),
        name="project",
    )(core.reshape(1), place, own_rows, other_rows, *weights)


def local(
    extent,
    passage_states,
    memory_queries,
    memory_gain,
    kv_weight,
    retrieval,
    question_queries,
    question_kv,
    question_lengths,
):
    me = lax.axis_index("pass")
    core, chip = me & 1, lax.div(me, 2)
    chips = extent // 2
    depth = kv_weight.shape[0]

    if chips != 8 or depth % LANES:
        memory_rows = pool(passage_states, memory_queries, memory_gain)
        whole_weight = lax.all_gather(kv_weight, "pass", axis=0, tiled=True)
        memory_kv = jnp.dot(memory_rows, whole_weight, preferred_element_type=jnp.float32)
        everything = lax.all_gather(memory_kv.astype(jnp.bfloat16), "pass", axis=0, tiled=True)
        by_head = everything.reshape(-1, 2, KVH, HD).transpose(2, 0, 1, 3).reshape(KVH, -1, LANES)
        rest = (retrieval * MEM, question_lengths, question_queries, question_kv)
        context = None
        for g in range(2):
            for half in range(2):
                context = attend(g, jnp.int32(half), *rest, by_head[2 * half + g], context)
        return context

    place = place_of(chip, chips).reshape(1)
    order = [2 * line for line in range(chips // 2)] + [2 * line + 1 for line in range(chips // 2)][::-1]

    def to_partner(x):
        return lax.ppermute(x, "pass", [(i, i ^ 1) for i in range(extent)])

    def along(x, target):
        pairs = [(c, target(c // 2, c % 2)) for c in range(chips)]
        return lax.ppermute(x, "pass", [(2 * s + c, 2 * d + c) for s, d in pairs for c in range(2)])

    def along_ring(x, step):
        return along(x, lambda line, lane: order[(order.index(2 * line + lane) + step) % chips])

    def round_the_ring(x, up, down, rounds):
        up, down = [x, up], [down]
        while len(up) <= rounds:
            up.append(along_ring(up[-1], 1))
        while len(up) + len(down) < chips:
            down.append(along_ring(down[-1], -1))
        return up + down[::-1]

    def columns(half):
        return jnp.concatenate(
            [
                lax.dynamic_slice_in_dim(kv_weight, half * LANES + at, LANES, axis=1)
                for at in (0, KVH * HD)
            ],
            axis=1,
        )

    pieces = [columns(core), to_partner(columns(1 - core))]
    hops = [along_ring(x, step) for x in pieces for step in (1, -1)]
    memory_rows = pool(passage_states, memory_queries, memory_gain)
    *hops, memory_rows = lax.optimization_barrier((*hops, memory_rows))
    weights = round_the_ring(pieces[0], hops[0], hops[1], chips // 2)
    weights += round_the_ring(pieces[1], hops[2], hops[3], chips // 2 - 1)
    by_head = project(core, place, memory_rows, to_partner(memory_rows), weights)

    lines = chips // 2
    of_chip = lax.div(retrieval, CHIP)
    back = lax.rem(lines + lax.div(chip, 2) - lax.div(of_chip, 2), lines)
    slot = back + lines * lax.rem(lax.rem(chip, 2) + lax.rem(of_chip, 2), 2)
    starts = (slot * CHIP + lax.rem(retrieval, CHIP)) * MEM

    def along_lines(block):
        return [along(block, lambda line, lane: 2 * ((line + k) % lines) + lane) for k in range(1, lines)]

    def to_lane(blocks):
        return [along(x, lambda line, lane: 2 * line + 1 - lane) for x in blocks]

    rest = (starts, question_lengths, question_queries, question_kv)
    first, second = by_head
    line_blocks = along_lines(first)
    second, *line_blocks = lax.optimization_barrier((second, *line_blocks))
    second_blocks = along_lines(second)
    first_blocks = [first] + line_blocks
    near = jnp.concatenate(first_blocks + to_lane(first_blocks), axis=0)
    far = to_partner(near)
    context = attend(0, core, *rest, near)
    context, *second_blocks = lax.optimization_barrier((context, second, *second_blocks))
    lane_blocks = to_lane(second_blocks)
    context = attend(0, 1 - core, *rest, far, context)
    context, *lane_blocks = lax.optimization_barrier((context, *lane_blocks))
    near = jnp.concatenate(second_blocks + lane_blocks, axis=0)
    far = to_partner(near)
    context = attend(1, core, *rest, near, context)
    return attend(1, 1 - core, *rest, far, context)


def solution(mesh):
    placed = (
        P(("groups", "pass"), None, None),
        P(),
        P(),
        P("pass", None),
        P(("groups", "pass"), None),
        P(("groups", "pass"), None, None),
        P(("groups", "pass"), None, None),
        P(("groups", "pass")),
    )
    return jax.shard_map(
        functools.partial(local, mesh.shape["pass"]),
        mesh=mesh,
        in_specs=placed,
        out_specs=P(("groups", "pass"), None, None),
        check_vma=False,
    )
```

time: 242 us -> 160 us (0.66)
  Pallas kernels: 0 us -> 110 us
  matrix products: 95.4 us -> 0 us
  waiting for transfers between devices: 74.9 us -> 14.8 us
  local copies, waits for them, and re-layouts: 45.9 us -> 2.83 us
  starting transfers between devices: 0.04 us -> 31.6 us
  between operations: 13.5 us -> 0.2 us
  other arithmetic: 10.9 us -> 0.06 us
    pallas_call x0 -> x6, Pallas kernels: none -> 110 us  [the longest x4 99.1 us: attend(): pl.pallas_call(functools.partial(attend_kernel, g), grid_spec=pltpu.Prefe...]
    all_gather x2 -> x0, waiting for transfers between devices: 74.1 us -> none  [the longest x1 39.7 us: local(): everything = lax.all_gather(memory_kv, 'pass', axis=0, tiled=True)]
    dot_general x13 -> x0, matrix products: 48.9 us -> none  [the longest x4 36.3 us: attend_query(): jnp.einsum('gjts,sgd->tgjd', weights, value_rows, preferred_element_type=...]
    sub x4 -> x0, matrix products: 46.5 us -> none  [attend_query(): weights = jax.nn.softmax(scores, axis=-1).astype(jnp.bfloat16)]
    ppermute x0 -> x32, starting transfers between devices: none -> 31.6 us  [the longest x28 23.5 us: along(): lax.ppermute(x, 'pass', [(2 * s + c, 2 * d + c) for s, d in pairs for c i...]
    dynamic_slice x32 -> x1, local copies, waits for them, and re-layouts: 24.7 us -> 0.97 us  [columns(): lax.dynamic_slice_in_dim(kv_weight, half * LANES + at, LANES, axis=1)]
    ppermute x0 -> x32, waiting for transfers between devices: none -> 14.8 us  [the longest x28 14.7 us: along(): lax.ppermute(x, 'pass', [(2 * s + c, 2 * d + c) for s, d in pairs for c i...]
    reshape x9 -> x0, local copies, waits for them, and re-layouts: 9.55 us -> none  [the longest x4 9.07 us: attend_query(): query_heads = question.reshape(QLEN, KVH, GROUP, HD)]
  transfers between devices with their start and end apart: 2 -> 32, of which waited for: 2 -> 9; matrix products, arithmetic and copies ran while one was open for 9% -> 0% of each run, Pallas kernels for 0% -> 52%
where the time goes in v7:
time: 160 us
  Pallas kernels  110 us (69%)
  starting transfers between devices  31.6 us (20%)
  waiting for transfers between devices  14.8 us (9%)
  local copies, waits for them, and re-layouts  2.83 us (2%)
    pallas_call x4, Pallas kernels, attend(): pl.pallas_call(functools.partial(attend_kernel, g), grid_spec=pltpu.Prefe...  99.1 us
    ppermute x28, starting transfers between devices, along(): lax.ppermute(x, 'pass', [(2 * s + c, 2 * d + c) for s, d in pairs for c i...  23.5 us
    ppermute x28, waiting for transfers between devices, along(): lax.ppermute(x, 'pass', [(2 * s + c, 2 * d + c) for s, d in pairs for c i...  14.7 us
    pallas_call x1, Pallas kernels, pool(): pl.pallas_call(pool_kernel, grid=(D // width,), in_specs=[pl.BlockSpec((c...  9.23 us
    ppermute x4, starting transfers between devices, to_partner(): return lax.ppermute(x, 'pass', [(i, i ^ 1) for i in range(extent)])  8.06 us
  transfers between devices with their start and end apart: 32, of which 9 were waited for; matrix products, arithmetic and copies ran while one was open for 0% of the time, Pallas kernels for 52%

profile of v7, /device:TPU:1, one launch (start us, length us, event | category | flops | bytes accessed | tf_op | source)
XLA Modules:
  0.0 159.5 jit_solution(6369855541241084191)
XLA Ops:
  0.0 1.0 constant_dynamic-slice_fusion.1
  1.0 0.1 collective-permute-start.2
  1.1 2.7 %collective-permute-start.1 = (bf16[256,256]{1,0:T(8,128)(2,1)S(1)}, bf16[256,256]{1,0:T(8,128)(2,1)S(1)}, u32[]{:S(2)}, u32[]{:S(2)}) collective-permute-start(bf16[256,256]{1,0:T(8,128)(2,1)S(1)} %pad_maximum_fusion.rest_2_), channel_id=1, source_target_pairs={{0,2},{1,3},{2,6},{3,7},{4,0},{5,1},{6,10},{7,11},{8,4},{9,5},{10,... | collective-permute-start | bytes 393224 | tf_op jit(solution)/shard_map/ppermute | solution.py:381
  3.9 0.2 collective-permute-start
  4.0 1.3 collective-permute-start.4
  5.3 0.2 collective-permute-start.3
  5.5 0.9 copy-done
  6.4 0.7 copy-done.1
  7.1 9.2 %pool.1.rest_0_ = bf16[128,4096]{1,0:T(8,128)(2,1)S(1)} custom-call(bf16[4,128,4096]{2,1,0:T(8,128)(2,1)} %states_ref.1, bf16[32,4096]{1,0:T(8,128)(2,1)S(1)} %copy-done, bf16[4096]{0:T(1024)(128)(2,1)S(1)} %copy-done.1), custom_call_target="tpu_custom_call" | custom-call | flops 268435456 | bytes 4194304 | tf_op jit(solution)/shard_map/pool/pallas_call | solution.py:89
  16.4 0.0 copy-start.4
  16.4 0.0 collective-permute-done.rest_3_
  16.4 0.0 collective-permute-done.4.rest_17_
  16.4 0.9 collective-permute-start.5
  17.3 1.7 %collective-permute-start.6 = (bf16[256,256]{1,0:T(8,128)(2,1)S(1)}, bf16[256,256]{1,0:T(8,128)(2,1)S(1)}, u32[]{:S(2)}, u32[]{:S(2)}) collective-permute-start(bf16[256,256]{1,0:T(8,128)(2,1)S(1)} %collective-permute-done.rest_3_), channel_id=1, source_target_pairs={{0,4},{1,5},{2,0},{3,1},{4,8},{5,9},{6,2},{7,3},{8,12},{9,13},{10,... | collective-permute-start | bytes 393224 | tf_op jit(solution)/shard_map/ppermute | solution.py:381
  19.0 0.0 collective-permute-start.13
  19.0 1.4 collective-permute-start.9
  20.4 0.1 collective-permute-start.11
  20.5 2.2 %collective-permute-done.6.rest_4_ = bf16[256,256]{1,0:T(8,128)(2,1)S(1)} collective-permute-done((bf16[256,256]{1,0:T(8,128)(2,1)S(1)}, bf16[256,256]{1,0:T(8,128)(2,1)S(1)}, u32[]{:S(2)}, u32[]{:S(2)}) %collective-permute-start.6) | collective-permute-done | bytes 131104 | tf_op jit(solution)/shard_map/ppermute | solution.py:381
  22.7 1.4 collective-permute-start.7
  24.1 0.0 collective-permute-done.13.rest_16_
  24.1 0.1 collective-permute-start.14
  24.2 2.4 %collective-permute-done.9.rest_8_ = bf16[256,256]{1,0:T(8,128)(2,1)S(1)} collective-permute-done((bf16[256,256]{1,0:T(8,128)(2,1)S(1)}, bf16[256,256]{1,0:T(8,128)(2,1)S(1)}, u32[]{:S(2)}, u32[]{:S(2)}) %collective-permute-start.9) | collective-permute-done | bytes 131104 | tf_op jit(solution)/shard_map/ppermute | solution.py:381
  26.6 0.3 collective-permute-start.10
  26.8 0.0 collective-permute-done.11.rest_12_
  26.8 1.2 collective-permute-start.12
  28.0 0.0 collective-permute-done.7.rest_5_
  28.1 1.3 collective-permute-start.8
  29.3 0.0 collective-permute-done.14.rest_15_
  29.3 0.2 collective-permute-start.15
  29.6 2.3 %collective-permute-done.10.rest_7_ = bf16[256,256]{1,0:T(8,128)(2,1)S(1)} collective-permute-done((bf16[256,256]{1,0:T(8,128)(2,1)S(1)}, bf16[256,256]{1,0:T(8,128)(2,1)S(1)}, u32[]{:S(2)}, u32[]{:S(2)}) %collective-permute-start.10) | collective-permute-done | bytes 131104 | tf_op jit(solution)/shard_map/ppermute | solution.py:381
  31.9 0.0 collective-permute-done.12.rest_13_
  31.9 1.1 collective-permute-done.8.rest_6_
  33.0 1.5 collective-permute-done.15.rest_14_
  34.5 0.0 collective-permute-done.5.rest_1_
  34.5 1.7 %project.1 = (bf16[256,128]{1,0:T(8,128)(2,1)S(1)}, bf16[256,128]{1,0:T(8,128)(2,1)S(1)}) custom-call(s32[1]{0:T(128)} %bitcast.1.core_ref.half_ref, s32[1]{0:T(128)} %bitcast.2.place_ref, bf16[128,4096]{1,0:T(8,128)(2,1)S(1)} %pool.1.rest_0_, bf16[128,4096]{1,0:T(8,128)(2,1)S(1)} %collective-permute-done.5.rest_1_, ...), custom_call_target="tpu_custom_call" | custom-call | flops 536870912 | bytes 2097152 | tf_op jit(solution)/shard_map/project/pallas_call | solution.py:331
  36.2 0.1 collective-permute-start.19
  36.3 3.4 %collective-permute-start.18 = (bf16[256,128]{1,0:T(8,128)(2,1)S(1)}, bf16[256,128]{1,0:T(8,128)(2,1)S(1)}, u32[]{:S(2)}, u32[]{:S(2)}) collective-permute-start(bf16[256,128]{1,0:T(8,128)(2,1)S(1)} %get-tuple-element.31), channel_id=1, source_target_pairs={{0,12},{1,13},{2,14},{3,15},{4,0},{5,1},{6,2},{7,3},{8,4},{9,5},{1... | collective-permute-start | bytes 196616 | tf_op jit(solution)/shard_map/ppermute | solution.py:381
  39.7 0.0 collective-permute-start.17
  39.7 0.4 collective-permute-start.16
  40.2 0.9 collective-permute-done.18
  41.0 3.9 %collective-permute-done.17 = bf16[256,128]{1,0:T(8,128)(2,1)S(1)} collective-permute-done((bf16[256,128]{1,0:T(8,128)(2,1)S(1)}, bf16[256,128]{1,0:T(8,128)(2,1)S(1)}, u32[]{:S(2)}, u32[]{:S(2)}) %collective-permute-start.17) | collective-permute-done | bytes 65568 | tf_op jit(solution)/shard_map/ppermute | solution.py:381
  45.0 0.2 collective-permute-done.16
  45.1 1.2 collective-permute-start.20
  46.4 0.2 collective-permute-start.21
  46.6 1.2 collective-permute-start.22
  47.8 0.3 collective-permute-start.25
  48.2 0.0 collective-permute-done.19
  48.2 0.4 collective-permute-start.24
  48.6 0.0 collective-permute-done.20
  48.6 1.3 collective-permute-start.23
  49.9 0.0 collective-permute-done.21
  50.0 0.2 collective-permute-done.22
  50.2 5.8 %collective-permute-start.26 = (bf16[2048,128]{1,0:T(8,128)(2,1)S(1)}, bf16[2048,128]{1,0:T(8,128)(2,1)S(1)}, u32[]{:S(2)}, u32[]{:S(2)}) collective-permute-start(bf16[2048,128]{1,0:T(8,128)(2,1)S(1)} %constant_dynamic-update-slice_fusion.kv_ref), channel_id=1, source_target_pairs={{0,1},{1,0},{2,3},{3,2},{4,5},{5,4},{6,7},{7,6},{8,9},{9,8},{10,11... | collective-permute-start | bytes 1572872 | tf_op jit(solution)/shard_map/ppermute | solution.py:377
  56.0 24.3 %attend.4.rest_0_ = bf16[4,64,7424]{2,1,0:T(8,128)(2,1)} custom-call(s32[1]{0:T(128)} %bitcast.1.core_ref.half_ref, s32[4,16]{1,0:T(4,128)S(1)} %fusion.6.start_ref, s32[4]{0:T(128)S(1)} %copy-done.4, bf16[4,64,7424]{2,1,0:T(8,128)(2,1)S(1)} %copy-done.2, bf16[2048,128]{1,0:T(8,128)(2,1)S(1)} %constant_dynamic-update-slice_fusion.kv_ref, ...), custom_call_target="tpu_custom_call" | custom-call | flops 4378853376 | bytes 1900544 | tf_op jit(solution)/shard_map/attend/pallas_call | solution.py:274
  80.3 0.6 collective-permute-start.27
  80.9 0.9 collective-permute-start.28
  81.8 0.6 collective-permute-start.29
  82.4 0.9 collective-permute-start.30
  83.3 0.0 collective-permute-done.26.kv_ref
  83.3 24.4 %attend.5.rest_0_ = bf16[4,64,7424]{2,1,0:T(8,128)(2,1)} custom-call(s32[1]{0:T(128)} %bitcast.half_ref, s32[4,16]{1,0:T(4,128)S(1)} %fusion.6.start_ref, s32[4]{0:T(128)S(1)} %copy-done.4, bf16[4,64,7424]{2,1,0:T(8,128)(2,1)S(1)} %copy-done.2, bf16[2048,128]{1,0:T(8,128)(2,1)S(1)} %collective-permute-done.26.kv_ref, ...), custom_call_target="tpu_custom_call", output_to_operand_aliasing={{}: (7, {})} | custom-call | flops 4378853376 | bytes 1900544 | tf_op jit(solution)/shard_map/attend/pallas_call | solution.py:274
  107.8 0.0 collective-permute-done.30
  107.9 1.2 collective-permute-start.31
  109.1 25.2 %attend.6.rest_0_ = bf16[4,64,7424]{2,1,0:T(8,128)(2,1)} custom-call(s32[1]{0:T(128)} %bitcast.1.core_ref.half_ref, s32[4,16]{1,0:T(4,128)S(1)} %fusion.6.start_ref, s32[4]{0:T(128)S(1)} %copy-done.4, bf16[4,64,7424]{2,1,0:T(8,128)(2,1)S(1)} %copy-done.2, ...), custom_call_target="tpu_custom_call", output_to_operand_aliasing={{}: (7, {})} | custom-call | flops 4378853376 | bytes 1900544 | tf_op jit(solution)/shard_map/attend/pallas_call | solution.py:274
  134.3 25.2 %attend.7 = bf16[4,64,7424]{2,1,0:T(8,128)(2,1)} custom-call(s32[1]{0:T(128)} %bitcast.half_ref, s32[4,16]{1,0:T(4,128)S(1)} %fusion.6.start_ref, s32[4]{0:T(128)S(1)} %copy-done.4, bf16[4,64,7424]{2,1,0:T(8,128)(2,1)S(1)} %copy-done.2, bf16[2048,128]{1,0:T(8,128)(2,1)S(1)} %collective-permute-done.31.kv_ref, ...), custom_call_target="tpu_custom_call", output_to_operand_aliasing={{}: (7, {})} | custom-call | flops 4378853376 | bytes 1900544 | tf_op jit(solution)/shard_map/attend/pallas_call | solution.py:274
  (38 shorter events, 0.3 us)
Async XLA Ops:
  0.0 29.5 %copy-start.5 = (s32[4,16]{1,0:T(4,128)S(1)}, s32[4,16]{1,0:T(4,128)}, u32[]{:S(2)}) copy-start(s32[4,16]{1,0:T(4,128)} %param.12) | copy-start | bytes 772
  1.0 3.0 %collective-permute-start.2 = (bf16[256,256]{1,0:T(8,128)(2,1)S(1)}, bf16[256,256]{1,0:T(8,128)(2,1)S(1)}, u32[]{:S(2)}, u32[]{:S(2)}) collective-permute-start(bf16[256,256]{1,0:T(8,128)(2,1)S(1)} %pad_maximum_fusion.1), channel_id=1, source_target_pairs={{0,1},{1,0},{2,3},{3,2},{4,5},{5,4},{6,7},{7,6},{8,9},{9,8},{10,11... | collective-permute-start | bytes 393224 | tf_op jit(solution)/shard_map/ppermute | solution.py:377
  1.1 15.2 %collective-permute-start.1 = (bf16[256,256]{1,0:T(8,128)(2,1)S(1)}, bf16[256,256]{1,0:T(8,128)(2,1)S(1)}, u32[]{:S(2)}, u32[]{:S(2)}) collective-permute-start(bf16[256,256]{1,0:T(8,128)(2,1)S(1)} %pad_maximum_fusion.rest_2_), channel_id=1, source_target_pairs={{0,2},{1,3},{2,6},{3,7},{4,0},{5,1},{6,10},{7,11},{8,4},{9,5},{10,... | collective-permute-start | bytes 393224 | tf_op jit(solution)/shard_map/ppermute | solution.py:381
  3.9 12.5 %collective-permute-start = (bf16[256,256]{1,0:T(8,128)(2,1)S(1)}, bf16[256,256]{1,0:T(8,128)(2,1)S(1)}, u32[]{:S(2)}, u32[]{:S(2)}) collective-permute-start(bf16[256,256]{1,0:T(8,128)(2,1)S(1)} %pad_maximum_fusion.rest_2_), channel_id=1, source_target_pairs={{0,4},{1,5},{2,0},{3,1},{4,8},{5,9},{6,2},{7,3},{8,12},{9,13},{10,... | collective-permute-start | bytes 393224 | tf_op jit(solution)/shard_map/ppermute | solution.py:381
  4.0 12.4 %collective-permute-start.4 = (bf16[256,256]{1,0:T(8,128)(2,1)S(1)}, bf16[256,256]{1,0:T(8,128)(2,1)S(1)}, u32[]{:S(2)}, u32[]{:S(2)}) collective-permute-start(bf16[256,256]{1,0:T(8,128)(2,1)S(1)} %collective-permute-done.2.rest_10_), channel_id=1, source_target_pairs={{0,2},{1,3},{2,6},{3,7},{4,0},{5,1},{6,10},{7,11},{8,4},{9,5},{10,... | collective-permute-start | bytes 393224 | tf_op jit(solution)/shard_map/ppermute | solution.py:381
  5.3 11.1 %collective-permute-start.3 = (bf16[256,256]{1,0:T(8,128)(2,1)S(1)}, bf16[256,256]{1,0:T(8,128)(2,1)S(1)}, u32[]{:S(2)}, u32[]{:S(2)}) collective-permute-start(bf16[256,256]{1,0:T(8,128)(2,1)S(1)} %collective-permute-done.2.rest_10_), channel_id=1, source_target_pairs={{0,4},{1,5},{2,0},{3,1},{4,8},{5,9},{6,2},{7,3},{8,12},{9,13},{10,... | collective-permute-start | bytes 393224 | tf_op jit(solution)/shard_map/ppermute | solution.py:381
  5.5 0.9 copy-start
  6.4 0.7 copy-start.1
  16.4 39.6 %copy-start.4 = (s32[4]{0:T(128)S(1)}, s32[4]{0:T(128)}, u32[]{:S(2)}) copy-start(s32[4]{0:T(128)} %length_ref.7) | copy-start | bytes 52
  16.4 18.1 %collective-permute-start.5 = (bf16[128,4096]{1,0:T(8,128)(2,1)S(1)}, bf16[128,4096]{1,0:T(8,128)(2,1)S(1)}, u32[]{:S(2)}, u32[]{:S(2)}) collective-permute-start(bf16[128,4096]{1,0:T(8,128)(2,1)S(1)} %pool.1.rest_0_), channel_id=1, source_target_pairs={{0,1},{1,0},{2,3},{3,2},{4,5},{5,4},{6,7},{7,6},{8,9},{9,8},{10,11... | collective-permute-start | bytes 3145736 | tf_op jit(solution)/shard_map/ppermute | solution.py:377
  17.3 5.3 %collective-permute-start.6 = (bf16[256,256]{1,0:T(8,128)(2,1)S(1)}, bf16[256,256]{1,0:T(8,128)(2,1)S(1)}, u32[]{:S(2)}, u32[]{:S(2)}) collective-permute-start(bf16[256,256]{1,0:T(8,128)(2,1)S(1)} %collective-permute-done.rest_3_), channel_id=1, source_target_pairs={{0,4},{1,5},{2,0},{3,1},{4,8},{5,9},{6,2},{7,3},{8,12},{9,13},{10,... | collective-permute-start | bytes 393224 | tf_op jit(solution)/shard_map/ppermute | solution.py:381
  19.0 5.1 %collective-permute-start.13 = (bf16[256,256]{1,0:T(8,128)(2,1)S(1)}, bf16[256,256]{1,0:T(8,128)(2,1)S(1)}, u32[]{:S(2)}, u32[]{:S(2)}) collective-permute-start(bf16[256,256]{1,0:T(8,128)(2,1)S(1)} %collective-permute-done.4.rest_17_), channel_id=1, source_target_pairs={{0,2},{1,3},{2,6},{3,7},{4,0},{5,1},{6,10},{7,11},{8,4},{9,5},{10,... | collective-permute-start | bytes 393224 | tf_op jit(solution)/shard_map/ppermute | solution.py:381
  19.0 7.5 %collective-permute-start.9 = (bf16[256,256]{1,0:T(8,128)(2,1)S(1)}, bf16[256,256]{1,0:T(8,128)(2,1)S(1)}, u32[]{:S(2)}, u32[]{:S(2)}) collective-permute-start(bf16[256,256]{1,0:T(8,128)(2,1)S(1)} %collective-permute-done.1.rest_9_), channel_id=1, source_target_pairs={{0,2},{1,3},{2,6},{3,7},{4,0},{5,1},{6,10},{7,11},{8,4},{9,5},{10,... | collective-permute-start | bytes 393224 | tf_op jit(solution)/shard_map/ppermute | solution.py:381
  20.4 6.4 %collective-permute-start.11 = (bf16[256,256]{1,0:T(8,128)(2,1)S(1)}, bf16[256,256]{1,0:T(8,128)(2,1)S(1)}, u32[]{:S(2)}, u32[]{:S(2)}) collective-permute-start(bf16[256,256]{1,0:T(8,128)(2,1)S(1)} %collective-permute-done.3.rest_11_), channel_id=1, source_target_pairs={{0,4},{1,5},{2,0},{3,1},{4,8},{5,9},{6,2},{7,3},{8,12},{9,13},{10,... | collective-permute-start | bytes 393224 | tf_op jit(solution)/shard_map/ppermute | solution.py:381
  22.7 5.4 %collective-permute-start.7 = (bf16[256,256]{1,0:T(8,128)(2,1)S(1)}, bf16[256,256]{1,0:T(8,128)(2,1)S(1)}, u32[]{:S(2)}, u32[]{:S(2)}) collective-permute-start(bf16[256,256]{1,0:T(8,128)(2,1)S(1)} %collective-permute-done.6.rest_4_), channel_id=1, source_target_pairs={{0,4},{1,5},{2,0},{3,1},{4,8},{5,9},{6,2},{7,3},{8,12},{9,13},{10,... | collective-permute-start | bytes 393224 | tf_op jit(solution)/shard_map/ppermute | solution.py:381
  24.1 5.3 %collective-permute-start.14 = (bf16[256,256]{1,0:T(8,128)(2,1)S(1)}, bf16[256,256]{1,0:T(8,128)(2,1)}, u32[]{:S(2)}, u32[]{:S(2)}) collective-permute-start(bf16[256,256]{1,0:T(8,128)(2,1)S(1)} %collective-permute-done.13.rest_16_), channel_id=1, source_target_pairs={{0,2},{1,3},{2,6},{3,7},{4,0},{5,1},{6,10},{7,11},{8,4},{9,5},{10,... | collective-permute-start | bytes 393224 | tf_op jit(solution)/shard_map/ppermute | solution.py:381
  24.2 31.8 %copy-start.2 = (bf16[4,64,7424]{2,1,0:T(8,128)(2,1)S(1)}, bf16[4,64,7424]{2,1,0:T(8,128)(2,1)}, u32[]{:S(2)}) copy-start(bf16[4,64,7424]{2,1,0:T(8,128)(2,1)} %q_ref.7) | copy-start | bytes 11403268
  24.2 31.8 %copy-start.3 = (bf16[4,64,512]{2,1,0:T(8,128)(2,1)S(1)}, bf16[4,64,512]{2,1,0:T(8,128)(2,1)}, u32[]{:S(2)}) copy-start(bf16[4,64,512]{2,1,0:T(8,128)(2,1)} %own_v_ref.7) | copy-start | bytes 786436
  26.6 5.3 %collective-permute-start.10 = (bf16[256,256]{1,0:T(8,128)(2,1)S(1)}, bf16[256,256]{1,0:T(8,128)(2,1)S(1)}, u32[]{:S(2)}, u32[]{:S(2)}) collective-permute-start(bf16[256,256]{1,0:T(8,128)(2,1)S(1)} %collective-permute-done.9.rest_8_), channel_id=1, source_target_pairs={{0,2},{1,3},{2,6},{3,7},{4,0},{5,1},{6,10},{7,11},{8,4},{9,5},{10,... | collective-permute-start | bytes 393224 | tf_op jit(solution)/shard_map/ppermute | solution.py:381
  26.8 5.1 %collective-permute-start.12 = (bf16[256,256]{1,0:T(8,128)(2,1)S(1)}, bf16[256,256]{1,0:T(8,128)(2,1)S(1)}, u32[]{:S(2)}, u32[]{:S(2)}) collective-permute-start(bf16[256,256]{1,0:T(8,128)(2,1)S(1)} %collective-permute-done.11.rest_12_), channel_id=1, source_target_pairs={{0,4},{1,5},{2,0},{3,1},{4,8},{5,9},{6,2},{7,3},{8,12},{9,13},{10,... | collective-permute-start | bytes 393224 | tf_op jit(solution)/shard_map/ppermute | solution.py:381
  28.1 4.9 %collective-permute-start.8 = (bf16[256,256]{1,0:T(8,128)(2,1)S(1)}, bf16[256,256]{1,0:T(8,128)(2,1)S(1)}, u32[]{:S(2)}, u32[]{:S(2)}) collective-permute-start(bf16[256,256]{1,0:T(8,128)(2,1)S(1)} %collective-permute-done.7.rest_5_), channel_id=1, source_target_pairs={{0,4},{1,5},{2,0},{3,1},{4,8},{5,9},{6,2},{7,3},{8,12},{9,13},{10,... | collective-permute-start | bytes 393224 | tf_op jit(solution)/shard_map/ppermute | solution.py:381
  29.3 5.2 %collective-permute-start.15 = (bf16[256,256]{1,0:T(8,128)(2,1)}, bf16[256,256]{1,0:T(8,128)(2,1)S(1)}, u32[]{:S(2)}, u32[]{:S(2)}) collective-permute-start(bf16[256,256]{1,0:T(8,128)(2,1)} %collective-permute-done.14.rest_15_), channel_id=1, source_target_pairs={{0,2},{1,3},{2,6},{3,7},{4,0},{5,1},{6,10},{7,11},{8,4},{9,5},{10,... | collective-permute-start | bytes 393224 | tf_op jit(solution)/shard_map/ppermute | solution.py:381
  36.2 12.0 %collective-permute-start.19 = (bf16[256,128]{1,0:T(8,128)(2,1)S(1)}, bf16[256,128]{1,0:T(8,128)(2,1)S(1)}, u32[]{:S(2)}, u32[]{:S(2)}) collective-permute-start(bf16[256,128]{1,0:T(8,128)(2,1)S(1)} %get-tuple-element.31), channel_id=1, source_target_pairs={{0,2},{1,3},{2,0},{3,1},{4,6},{5,7},{6,4},{7,5},{8,10},{9,11},{10,... | collective-permute-start | bytes 196616 | tf_op jit(solution)/shard_map/ppermute | solution.py:381
  36.3 4.7 %collective-permute-start.18 = (bf16[256,128]{1,0:T(8,128)(2,1)S(1)}, bf16[256,128]{1,0:T(8,128)(2,1)S(1)}, u32[]{:S(2)}, u32[]{:S(2)}) collective-permute-start(bf16[256,128]{1,0:T(8,128)(2,1)S(1)} %get-tuple-element.31), channel_id=1, source_target_pairs={{0,12},{1,13},{2,14},{3,15},{4,0},{5,1},{6,2},{7,3},{8,4},{9,5},{1... | collective-permute-start | bytes 196616 | tf_op jit(solution)/shard_map/ppermute | solution.py:381
  39.7 5.3 %collective-permute-start.17 = (bf16[256,128]{1,0:T(8,128)(2,1)S(1)}, bf16[256,128]{1,0:T(8,128)(2,1)S(1)}, u32[]{:S(2)}, u32[]{:S(2)}) collective-permute-start(bf16[256,128]{1,0:T(8,128)(2,1)S(1)} %get-tuple-element.31), channel_id=1, source_target_pairs={{0,8},{1,9},{2,10},{3,11},{4,12},{5,13},{6,14},{7,15},{8,0},{9,1},... | collective-permute-start | bytes 196616 | tf_op jit(solution)/shard_map/ppermute | solution.py:381
  39.7 5.4 %collective-permute-start.16 = (bf16[256,128]{1,0:T(8,128)(2,1)S(1)}, bf16[256,128]{1,0:T(8,128)(2,1)S(1)}, u32[]{:S(2)}, u32[]{:S(2)}) collective-permute-start(bf16[256,128]{1,0:T(8,128)(2,1)S(1)} %get-tuple-element.31), channel_id=1, source_target_pairs={{0,4},{1,5},{2,6},{3,7},{4,8},{5,9},{6,10},{7,11},{8,12},{9,13},{1... | collective-permute-start | bytes 196616 | tf_op jit(solution)/shard_map/ppermute | solution.py:381
  45.1 3.5 %collective-permute-start.20 = (bf16[256,128]{1,0:T(8,128)(2,1)S(1)}, bf16[256,128]{1,0:T(8,128)(2,1)S(1)}, u32[]{:S(2)}, u32[]{:S(2)}) collective-permute-start(bf16[256,128]{1,0:T(8,128)(2,1)S(1)} %collective-permute-done.16), channel_id=1, source_target_pairs={{0,2},{1,3},{2,0},{3,1},{4,6},{5,7},{6,4},{7,5},{8,10},{9,11},{10,... | collective-permute-start | bytes 196616 | tf_op jit(solution)/shard_map/ppermute | solution.py:381
  46.4 3.6 %collective-permute-start.21 = (bf16[256,128]{1,0:T(8,128)(2,1)S(1)}, bf16[256,128]{1,0:T(8,128)(2,1)S(1)}, u32[]{:S(2)}, u32[]{:S(2)}) collective-permute-start(bf16[256,128]{1,0:T(8,128)(2,1)S(1)} %collective-permute-done.17), channel_id=1, source_target_pairs={{0,2},{1,3},{2,0},{3,1},{4,6},{5,7},{6,4},{7,5},{8,10},{9,11},{10,... | collective-permute-start | bytes 196616 | tf_op jit(solution)/shard_map/ppermute | solution.py:381
  46.6 3.6 %collective-permute-start.22 = (bf16[256,128]{1,0:T(8,128)(2,1)S(1)}, bf16[256,128]{1,0:T(8,128)(2,1)S(1)}, u32[]{:S(2)}, u32[]{:S(2)}) collective-permute-start(bf16[256,128]{1,0:T(8,128)(2,1)S(1)} %collective-permute-done.18), channel_id=1, source_target_pairs={{0,2},{1,3},{2,0},{3,1},{4,6},{5,7},{6,4},{7,5},{8,10},{9,11},{10,... | collective-permute-start | bytes 196616 | tf_op jit(solution)/shard_map/ppermute | solution.py:381
  47.8 32.4 %collective-permute-start.25 = (bf16[256,128]{1,0:T(8,128)(2,1)S(1)}, bf16[256,128]{1,0:T(8,128)(2,1)S(1)}, u32[]{:S(2)}, u32[]{:S(2)}) collective-permute-start(bf16[256,128]{1,0:T(8,128)(2,1)S(1)} %get-tuple-element.37), channel_id=1, source_target_pairs={{0,12},{1,13},{2,14},{3,15},{4,0},{5,1},{6,2},{7,3},{8,4},{9,5},{1... | collective-permute-start | bytes 196616 | tf_op jit(solution)/shard_map/ppermute | solution.py:381
  48.2 32.1 %collective-permute-start.24 = (bf16[256,128]{1,0:T(8,128)(2,1)S(1)}, bf16[256,128]{1,0:T(8,128)(2,1)S(1)}, u32[]{:S(2)}, u32[]{:S(2)}) collective-permute-start(bf16[256,128]{1,0:T(8,128)(2,1)S(1)} %get-tuple-element.37), channel_id=1, source_target_pairs={{0,8},{1,9},{2,10},{3,11},{4,12},{5,13},{6,14},{7,15},{8,0},{9,1},... | collective-permute-start | bytes 196616 | tf_op jit(solution)/shard_map/ppermute | solution.py:381
  48.6 31.6 %collective-permute-start.23 = (bf16[256,128]{1,0:T(8,128)(2,1)S(1)}, bf16[256,128]{1,0:T(8,128)(2,1)S(1)}, u32[]{:S(2)}, u32[]{:S(2)}) collective-permute-start(bf16[256,128]{1,0:T(8,128)(2,1)S(1)} %get-tuple-element.37), channel_id=1, source_target_pairs={{0,4},{1,5},{2,6},{3,7},{4,8},{5,9},{6,10},{7,11},{8,12},{9,13},{1... | collective-permute-start | bytes 196616 | tf_op jit(solution)/shard_map/ppermute | solution.py:381
  50.2 33.1 %collective-permute-start.26 = (bf16[2048,128]{1,0:T(8,128)(2,1)S(1)}, bf16[2048,128]{1,0:T(8,128)(2,1)S(1)}, u32[]{:S(2)}, u32[]{:S(2)}) collective-permute-start(bf16[2048,128]{1,0:T(8,128)(2,1)S(1)} %constant_dynamic-update-slice_fusion.kv_ref), channel_id=1, source_target_pairs={{0,1},{1,0},{2,3},{3,2},{4,5},{5,4},{6,7},{7,6},{8,9},{9,8},{10,11... | collective-permute-start | bytes 1572872 | tf_op jit(solution)/shard_map/ppermute | solution.py:377
  80.3 27.5 %collective-permute-start.27 = (bf16[256,128]{1,0:T(8,128)(2,1)S(1)}, bf16[256,128]{1,0:T(8,128)(2,1)S(1)}, u32[]{:S(2)}, u32[]{:S(2)}) collective-permute-start(bf16[256,128]{1,0:T(8,128)(2,1)S(1)} %get-tuple-element.37), channel_id=1, source_target_pairs={{0,2},{1,3},{2,0},{3,1},{4,6},{5,7},{6,4},{7,5},{8,10},{9,11},{10,... | collective-permute-start | bytes 196616 | tf_op jit(solution)/shard_map/ppermute | solution.py:381
  80.9 26.9 %collective-permute-start.28 = (bf16[256,128]{1,0:T(8,128)(2,1)S(1)}, bf16[256,128]{1,0:T(8,128)(2,1)S(1)}, u32[]{:S(2)}, u32[]{:S(2)}) collective-permute-start(bf16[256,128]{1,0:T(8,128)(2,1)S(1)} %collective-permute-done.23), channel_id=1, source_target_pairs={{0,2},{1,3},{2,0},{3,1},{4,6},{5,7},{6,4},{7,5},{8,10},{9,11},{10,... | collective-permute-start | bytes 196616 | tf_op jit(solution)/shard_map/ppermute | solution.py:381
  81.8 26.0 %collective-permute-start.29 = (bf16[256,128]{1,0:T(8,128)(2,1)S(1)}, bf16[256,128]{1,0:T(8,128)(2,1)S(1)}, u32[]{:S(2)}, u32[]{:S(2)}) collective-permute-start(bf16[256,128]{1,0:T(8,128)(2,1)S(1)} %collective-permute-done.24), channel_id=1, source_target_pairs={{0,2},{1,3},{2,0},{3,1},{4,6},{5,7},{6,4},{7,5},{8,10},{9,11},{10,... | collective-permute-start | bytes 196616 | tf_op jit(solution)/shard_map/ppermute | solution.py:381
  82.4 25.4 %collective-permute-start.30 = (bf16[256,128]{1,0:T(8,128)(2,1)S(1)}, bf16[256,128]{1,0:T(8,128)(2,1)S(1)}, u32[]{:S(2)}, u32[]{:S(2)}) collective-permute-start(bf16[256,128]{1,0:T(8,128)(2,1)S(1)} %collective-permute-done.25), channel_id=1, source_target_pairs={{0,2},{1,3},{2,0},{3,1},{4,6},{5,7},{6,4},{7,5},{8,10},{9,11},{10,... | collective-permute-start | bytes 196616 | tf_op jit(solution)/shard_map/ppermute | solution.py:381
  107.9 26.4 %collective-permute-start.31 = (bf16[2048,128]{1,0:T(8,128)(2,1)S(1)}, bf16[2048,128]{1,0:T(8,128)(2,1)S(1)}, u32[]{:S(2)}, u32[]{:S(2)}) collective-permute-start(bf16[2048,128]{1,0:T(8,128)(2,1)S(1)} %constant_dynamic-update-slice_fusion.8.kv_ref), channel_id=1, source_target_pairs={{0,1},{1,0},{2,3},{3,2},{4,5},{5,4},{6,7},{7,6},{8,9},{9,8},{10,11... | collective-permute-start | bytes 1572872 | tf_op jit(solution)/shard_map/ppermute | solution.py:377

commit v8 on v5

--- a/solution.py
+++ b/solution.py
@@ -28,9 +28,9 @@
 KEYS = 2 * (ROWS + QLEN)
 NEG = -1e30
 SUM_LOW, SUM_HIGH = 2.0 ** -40, 2.0 ** 60
-POOL_HEADS = 16
+POOL_WIDTH = 1024
 CHIP = 8
-STEP = 8
+STEP = 15
 BLOCK = 16
 MIB = 1024 * 1024
 
@@ -53,53 +53,78 @@
     return back + lines * lax.rem(lax.rem(mine, 2) + lax.rem(chip, 2), 2)
 
 
-def pool_kernel(states_ref, queries_ref, gain_ref, out_ref, pooled):
-    squares = jnp.zeros((MEM, CHD), jnp.float32)
-    for base in range(0, CH, POOL_HEADS):
-        spans = [slice(h * CHD, (h + 1) * CHD) for h in range(base, base + POOL_HEADS)]
-        scores = jnp.concatenate(
+def pool_kernel(states_ref, queries_ref, gain_ref, out_ref, pooled, squares):
+    step = pl.program_id(0)
+    passages, width = states_ref.shape[0], states_ref.shape[2]
+    two = 2 * CHD
+    blocks = []
+    for at in range(0, width, two):
+        zero = jnp.zeros((MEM, CHD), jnp.bfloat16)
+        lhs = jnp.concatenate(
             [
-                lax.dot_general(
-                    queries_ref[:, span], states_ref[0, :, span], (((1,), (1,)), ((), ())),
-                    preferred_element_type=jnp.float32,
-                )
-                for span in spans
+                jnp.concatenate([queries_ref[:, at:at + CHD], zero], axis=1),
+                jnp.concatenate([zero, queries_ref[:, at + CHD:at + two]], axis=1),
             ],
             axis=0,
-        ) * (1.0 / math.sqrt(CHD))
-        scores = jnp.exp(scores - jnp.max(scores, axis=1, keepdims=True))
-        weights = (scores / jnp.sum(scores, axis=1, keepdims=True)).astype(jnp.bfloat16)
-        for i, span in enumerate(spans):
-            part = jnp.dot(
-                weights[i * MEM:(i + 1) * MEM], states_ref[0, :, span], preferred_element_type=jnp.float32
-            )
-            pooled[:, span] = part
-            squares += part * part
-    mean_square = jnp.sum(squares, axis=1, keepdims=True) * (1.0 / D)
-    scale = lax.rsqrt(mean_square + 1e-06)
-    out_ref[...] = (pooled[...] * scale * gain_ref[...].astype(jnp.float32)).astype(jnp.bfloat16)
+        )
+        for p in range(0, passages, 2):
+            tokens = states_ref[p:p + 2, :, at:at + two].reshape(2 * LEN, two)
+            scores = lax.dot_general(
+                lhs, tokens, (((1,), (1,)), ((), ())), preferred_element_type=jnp.float32
+            ) * (1.0 / math.sqrt(CHD))
+            blocks.append((at, p, tokens, scores))
+    zero = jnp.zeros((2 * MEM, LEN), jnp.bfloat16)
+    totals = [jnp.zeros((MEM, CHD), jnp.float32)] * passages
+    for at, p, tokens, scores in blocks:
+        rows = []
+        for n in range(2):
+            part = scores[:, n * LEN:(n + 1) * LEN]
+            part = jnp.exp(part - jnp.max(part, axis=1, keepdims=True))
+            part = (part / jnp.sum(part, axis=1, keepdims=True)).astype(jnp.bfloat16)
+            rows.append(jnp.concatenate([zero, part] if n else [part, zero], axis=1))
+        mixed = jnp.dot(jnp.concatenate(rows, axis=0), tokens, preferred_element_type=jnp.float32)
+        for n in range(2):
+            for head in range(2):
+                top = (2 * n + head) * MEM
+                block = mixed[top:top + MEM, head * CHD:(head + 1) * CHD]
+                column = pl.multiple_of(step * width + at + head * CHD, CHD)
+                pooled[(p + n) * MEM:(p + n + 1) * MEM, pl.ds(column, CHD)] = block
+                totals[p + n] = totals[p + n] + block * block
+    for p in range(passages):
+        rows = slice(p * MEM, (p + 1) * MEM)
+        squares[rows, :] = totals[p] + jnp.where(step == 0, 0.0, squares[rows, :])
+
+    @pl.when(step == pl.num_programs(0) - 1)
+    def _():
+        mean_square = jnp.sum(squares[...], axis=1, keepdims=True) * (1.0 / D)
+        scale = lax.rsqrt(mean_square + 1e-06)
+        gain = gain_ref[...].astype(jnp.float32).reshape(1, D)
+        out_ref[...] = (pooled[...] * scale * gain).astype(jnp.bfloat16)
 
 
 def pool(states, queries, gain):
     count = states.shape[0]
     return pl.pallas_call(
         pool_kernel,
-        grid=(count,),
+        grid=(D // POOL_WIDTH,),
         in_specs=[
-            pl.BlockSpec((1, LEN, D), lambda p: (p, 0, 0)),
-            pl.BlockSpec((MEM, D), lambda p: (0, 0)),
-            pl.BlockSpec((1, D), lambda p: (0, 0)),
+            pl.BlockSpec((count, LEN, POOL_WIDTH), lambda j: (0, 0, j)),
+            pl.BlockSpec((MEM, POOL_WIDTH), lambda j: (0, j)),
+            pl.BlockSpec((D,), lambda j: (0,)),
         ],
-        out_specs=pl.BlockSpec((MEM, D), lambda p: (p, 0)),
+        out_specs=pl.BlockSpec((count * MEM, D), lambda j: (0, 0)),
         out_shape=jax.ShapeDtypeStruct((count * MEM, D), jnp.bfloat16),
-        scratch_shapes=[pltpu.VMEM((MEM, D), jnp.float32)],
-        compiler_params=pltpu.CompilerParams(vmem_limit_bytes=56 * MIB),
+        scratch_shapes=[
+            pltpu.VMEM((count * MEM, D), jnp.float32),
+            pltpu.VMEM((count * MEM, CHD), jnp.float32),
+        ],
+        compiler_params=pltpu.CompilerParams(vmem_limit_bytes=52 * MIB),
         cost_estimate=pl.CostEstimate(
             flops=4 * count * MEM * LEN * D, bytes_accessed=2 * count * LEN * D,
             transcendentals=count * CH * MEM * LEN,
         ),
         name="pool",
-    )(states, queries, gain.reshape(1, D))
+    )(states, queries, gain)
 
 
 def attend_kernel(

time: 115 us -> 116 us (level)
  Pallas kernels: 65.4 us -> 66.6 us
    pallas_call x2, Pallas kernels: 57 us -> 59.3 us  [attend(): pl.pallas_call(functools.partial(attend_kernel, chips), grid_spec=pltpu.P...]
    pallas_call x1, Pallas kernels: 7.75 us -> 5.43 us  [pool(): pl.pallas_call(pool_kernel, grid=(D // POOL_WIDTH,), in_specs=[pl.BlockSp...]
    reshape x1 -> x0, local copies, waits for them, and re-layouts: 1.3 us -> none  [pool(): gain.reshape(1, D)]
  transfers between devices with their start and end apart: 24 -> 24, of which waited for: 8 -> 8; matrix products, arithmetic and copies ran while one was open for 1% -> 0% of each run, Pallas kernels for 31% -> 30%
where the time goes in v8:
time: 116 us; the launch traced here: 115 us
  Pallas kernels  66.6 us (57%)
  waiting for transfers between devices  24.1 us (21%)
  starting transfers between devices  21.6 us (19%)
  local copies, waits for them, and re-layouts  2.71 us (2%)
    pallas_call x2, Pallas kernels, attend(): pl.pallas_call(functools.partial(attend_kernel, chips), grid_spec=pltpu.P...  59.3 us
    ppermute x21, waiting for transfers between devices, along(): lax.ppermute(x, 'pass', [(2 * s + c, 2 * d + c) for s, d in pairs for c i...  24.1 us
    ppermute x21, starting transfers between devices, along(): lax.ppermute(x, 'pass', [(2 * s + c, 2 * d + c) for s, d in pairs for c i...  17.5 us
    pallas_call x1, Pallas kernels, pool(): pl.pallas_call(pool_kernel, grid=(D // POOL_WIDTH,), in_specs=[pl.BlockSp...  5.43 us
    ppermute x3, starting transfers between devices, to_partner(): return lax.ppermute(x, 'pass', [(i, i ^ 1) for i in range(extent)])  4.13 us
  transfers between devices with their start and end apart: 24, of which 8 were waited for; matrix products, arithmetic and copies ran while one was open for 0% of the time, Pallas kernels for 30%

profile of v8, /device:TPU:1, one launch (start us, length us, event | category | flops | bytes accessed | tf_op | source)
XLA Modules:
  0.0 115.2 jit_solution(4096713135851255664)
XLA Ops:
  0.0 1.0 constant_dynamic-slice_fusion.1
  1.0 0.1 collective-permute-start.2
  1.1 2.7 %collective-permute-start.1 = (bf16[256,256]{1,0:T(8,128)(2,1)S(1)}, bf16[256,256]{1,0:T(8,128)(2,1)S(1)}, u32[]{:S(2)}, u32[]{:S(2)}) collective-permute-start(bf16[256,256]{1,0:T(8,128)(2,1)S(1)} %pad_maximum_fusion.rest_2_), channel_id=1, source_target_pairs={{0,2},{1,3},{2,6},{3,7},{4,0},{5,1},{6,10},{7,11},{8,4},{9,5},{10,... | collective-permute-start | bytes 393224 | tf_op jit(solution)/shard_map/ppermute | solution.py:384
  3.8 0.2 collective-permute-start
  4.0 0.0 collective-permute-done.2.rest_10_
  4.0 1.3 %collective-permute-start.4 = (bf16[256,256]{1,0:T(8,128)(2,1)S(1)}, bf16[256,256]{1,0:T(8,128)(2,1)S(1)}, u32[]{:S(2)}, u32[]{:S(2)}) collective-permute-start(bf16[256,256]{1,0:T(8,128)(2,1)S(1)} %collective-permute-done.2.rest_10_), channel_id=1, source_target_pairs={{0,2},{1,3},{2,6},{3,7},{4,0},{5,1},{6,10},{7,11},{8,4},{9,5},{10,... | collective-permute-start | bytes 393224 | tf_op jit(solution)/shard_map/ppermute | solution.py:384
  5.3 0.2 collective-permute-start.3
  5.5 0.0 copy-start
  5.5 0.9 copy-done
  6.4 0.0 copy-start.1
  6.4 0.7 copy-done.1
  7.1 5.4 %pool.1.rest_0_ = bf16[128,4096]{1,0:T(8,128)(2,1)S(1)} custom-call(bf16[4,128,4096]{2,1,0:T(8,128)(2,1)} %states_ref.1, bf16[32,4096]{1,0:T(8,128)(2,1)S(1)} %copy-done, bf16[4096]{0:T(1024)(128)(2,1)S(1)} %copy-done.1), custom_call_target="tpu_custom_call" | custom-call | flops 268435456 | bytes 4194304 | tf_op jit(solution)/shard_map/pool/pallas_call | solution.py:107
  12.5 0.0 copy-start.4
  12.6 0.0 copy-start.5
  12.6 0.0 collective-permute-done.1.rest_9_
  12.6 0.0 collective-permute-done.rest_3_
  12.6 0.0 collective-permute-done.4.rest_17_
  12.6 0.0 collective-permute-done.3.rest_11_
  12.6 0.9 collective-permute-start.5
  13.5 1.7 %collective-permute-start.6 = (bf16[256,256]{1,0:T(8,128)(2,1)S(1)}, bf16[256,256]{1,0:T(8,128)(2,1)S(1)}, u32[]{:S(2)}, u32[]{:S(2)}) collective-permute-start(bf16[256,256]{1,0:T(8,128)(2,1)S(1)} %collective-permute-done.rest_3_), channel_id=1, source_target_pairs={{0,4},{1,5},{2,0},{3,1},{4,8},{5,9},{6,2},{7,3},{8,12},{9,13},{10,... | collective-permute-start | bytes 393224 | tf_op jit(solution)/shard_map/ppermute | solution.py:384
  15.2 0.0 collective-permute-start.13
  15.2 1.4 %collective-permute-start.9 = (bf16[256,256]{1,0:T(8,128)(2,1)S(1)}, bf16[256,256]{1,0:T(8,128)(2,1)S(1)}, u32[]{:S(2)}, u32[]{:S(2)}) collective-permute-start(bf16[256,256]{1,0:T(8,128)(2,1)S(1)} %collective-permute-done.1.rest_9_), channel_id=1, source_target_pairs={{0,2},{1,3},{2,6},{3,7},{4,0},{5,1},{6,10},{7,11},{8,4},{9,5},{10,... | collective-permute-start | bytes 393224 | tf_op jit(solution)/shard_map/ppermute | solution.py:384
  16.6 0.1 collective-permute-start.11
  16.7 2.2 %collective-permute-done.6.rest_4_ = bf16[256,256]{1,0:T(8,128)(2,1)S(1)} collective-permute-done((bf16[256,256]{1,0:T(8,128)(2,1)S(1)}, bf16[256,256]{1,0:T(8,128)(2,1)S(1)}, u32[]{:S(2)}, u32[]{:S(2)}) %collective-permute-start.6) | collective-permute-done | bytes 131104 | tf_op jit(solution)/shard_map/ppermute | solution.py:384
  18.9 1.4 %collective-permute-start.7 = (bf16[256,256]{1,0:T(8,128)(2,1)S(1)}, bf16[256,256]{1,0:T(8,128)(2,1)S(1)}, u32[]{:S(2)}, u32[]{:S(2)}) collective-permute-start(bf16[256,256]{1,0:T(8,128)(2,1)S(1)} %collective-permute-done.6.rest_4_), channel_id=1, source_target_pairs={{0,4},{1,5},{2,0},{3,1},{4,8},{5,9},{6,2},{7,3},{8,12},{9,13},{10,... | collective-permute-start | bytes 393224 | tf_op jit(solution)/shard_map/ppermute | solution.py:384
  20.3 0.0 collective-permute-done.13.rest_16_
  20.3 0.1 collective-permute-start.14
  20.4 2.4 %collective-permute-done.9.rest_8_ = bf16[256,256]{1,0:T(8,128)(2,1)S(1)} collective-permute-done((bf16[256,256]{1,0:T(8,128)(2,1)S(1)}, bf16[256,256]{1,0:T(8,128)(2,1)S(1)}, u32[]{:S(2)}, u32[]{:S(2)}) %collective-permute-start.9) | collective-permute-done | bytes 131104 | tf_op jit(solution)/shard_map/ppermute | solution.py:384
  22.8 0.2 collective-permute-start.10
  23.0 0.0 collective-permute-done.11.rest_12_
  23.0 1.2 %collective-permute-start.12 = (bf16[256,256]{1,0:T(8,128)(2,1)S(1)}, bf16[256,256]{1,0:T(8,128)(2,1)}, u32[]{:S(2)}, u32[]{:S(2)}) collective-permute-start(bf16[256,256]{1,0:T(8,128)(2,1)S(1)} %collective-permute-done.11.rest_12_), channel_id=1, source_target_pairs={{0,4},{1,5},{2,0},{3,1},{4,8},{5,9},{6,2},{7,3},{8,12},{9,13},{10,... | collective-permute-start | bytes 393224 | tf_op jit(solution)/shard_map/ppermute | solution.py:384
  24.2 0.0 collective-permute-done.7.rest_5_
  24.3 1.3 %collective-permute-start.8 = (bf16[256,256]{1,0:T(8,128)(2,1)S(1)}, bf16[256,256]{1,0:T(8,128)(2,1)}, u32[]{:S(2)}, u32[]{:S(2)}) collective-permute-start(bf16[256,256]{1,0:T(8,128)(2,1)S(1)} %collective-permute-done.7.rest_5_), channel_id=1, source_target_pairs={{0,4},{1,5},{2,0},{3,1},{4,8},{5,9},{6,2},{7,3},{8,12},{9,13},{10,... | collective-permute-start | bytes 393224 | tf_op jit(solution)/shard_map/ppermute | solution.py:384
  25.5 0.0 collective-permute-done.14.rest_15_
  25.5 0.2 collective-permute-start.15
  25.7 0.0 copy-start.2
  25.7 2.5 %collective-permute-done.10.rest_7_ = bf16[256,256]{1,0:T(8,128)(2,1)} collective-permute-done((bf16[256,256]{1,0:T(8,128)(2,1)S(1)}, bf16[256,256]{1,0:T(8,128)(2,1)}, u32[]{:S(2)}, u32[]{:S(2)}) %collective-permute-start.10) | collective-permute-done | bytes 131104 | tf_op jit(solution)/shard_map/ppermute | solution.py:384
  28.2 0.0 collective-permute-done.12.rest_13_
  28.2 1.1 collective-permute-done.8.rest_6_
  29.3 1.5 %collective-permute-done.15.rest_14_ = bf16[256,256]{1,0:T(8,128)(2,1)} collective-permute-done((bf16[256,256]{1,0:T(8,128)(2,1)}, bf16[256,256]{1,0:T(8,128)(2,1)}, u32[]{:S(2)}, u32[]{:S(2)}) %collective-permute-start.15) | collective-permute-done | bytes 131104 | tf_op jit(solution)/shard_map/ppermute | solution.py:384
  30.8 0.0 collective-permute-done.5.rest_1_
  30.8 1.9 %project.1 = bf16[256,256]{1,0:T(8,128)(2,1)S(1)} custom-call(s32[1]{0:T(128)} %bitcast.2.core_ref.half_ref, s32[1]{0:T(128)} %bitcast.1.place_ref, bf16[128,4096]{1,0:T(8,128)(2,1)S(1)} %pool.1.rest_0_, bf16[128,4096]{1,0:T(8,128)(2,1)S(1)} %collective-permute-done.5.rest_1_, bf16[256,256]{1,0:T(8,128)(2,1)S(1)} %pad_maximum_fusion.rest_2_, ...), custom_call_target="tpu_custom_call" | custom-call | flops 536870912 | bytes 2097152 | tf_op jit(solution)/shard_map/project/pallas_call | solution.py:337
  32.7 3.3 %collective-permute-start.18 = (bf16[256,256]{1,0:T(8,128)(2,1)S(1)}, bf16[256,256]{1,0:T(8,128)(2,1)S(1)}, u32[]{:S(2)}, u32[]{:S(2)}) collective-permute-start(bf16[256,256]{1,0:T(8,128)(2,1)S(1)} %project.1), channel_id=1, source_target_pairs={{0,12},{1,13},{2,14},{3,15},{4,0},{5,1},{6,2},{7,3},{8,4},{9,5},{1... | collective-permute-start | bytes 393224 | tf_op jit(solution)/shard_map/ppermute | solution.py:384
  36.0 0.0 collective-permute-start.17
  36.0 0.5 collective-permute-start.16
  36.5 0.1 collective-permute-start.19
  36.6 1.3 %collective-permute-done.18 = bf16[256,256]{1,0:T(8,128)(2,1)S(1)} collective-permute-done((bf16[256,256]{1,0:T(8,128)(2,1)S(1)}, bf16[256,256]{1,0:T(8,128)(2,1)S(1)}, u32[]{:S(2)}, u32[]{:S(2)}) %collective-permute-start.18) | collective-permute-done | bytes 131104 | tf_op jit(solution)/shard_map/ppermute | solution.py:384
  37.9 0.2 collective-permute-start.22
  38.1 8.9 %collective-permute-done.17 = bf16[256,256]{1,0:T(8,128)(2,1)S(1)} collective-permute-done((bf16[256,256]{1,0:T(8,128)(2,1)S(1)}, bf16[256,256]{1,0:T(8,128)(2,1)S(1)}, u32[]{:S(2)}, u32[]{:S(2)}) %collective-permute-start.17) | collective-permute-done | bytes 131104 | tf_op jit(solution)/shard_map/ppermute | solution.py:384
  47.0 0.4 collective-permute-start.21
  47.4 0.0 collective-permute-done.16
  47.4 1.1 collective-permute-start.20
  48.5 0.0 collective-permute-done.19
  48.6 4.2 %collective-permute-done.20 = bf16[256,256]{1,0:T(8,128)(2,1)S(1)} collective-permute-done((bf16[256,256]{1,0:T(8,128)(2,1)S(1)}, bf16[256,256]{1,0:T(8,128)(2,1)S(1)}, u32[]{:S(2)}, u32[]{:S(2)}) %collective-permute-start.20) | collective-permute-done | bytes 131104 | tf_op jit(solution)/shard_map/ppermute | solution.py:384
  52.7 0.0 collective-permute-done.21
  52.8 0.0 collective-permute-done.22
  52.8 3.1 %collective-permute-start.23 = (bf16[2048,256]{1,0:T(8,128)(2,1)S(1)}, bf16[2048,256]{1,0:T(8,128)(2,1)S(1)}, u32[]{:S(2)}, u32[]{:S(2)}) collective-permute-start(bf16[2048,256]{1,0:T(8,128)(2,1)S(1)} %constant_dynamic-update-slice_fusion.k_ref.v_ref), channel_id=1, source_target_pairs={{0,1},{1,0},{2,3},{3,2},{4,5},{5,4},{6,7},{7,6},{8,9},{9,8},{10,11... | collective-permute-start | bytes 3145736 | tf_op jit(solution)/shard_map/ppermute | solution.py:380
  55.9 0.0 copy-done.4
  55.9 0.0 copy-done.5
  55.9 0.0 copy-done.2
  55.9 0.0 copy-done.3
  55.9 29.6 %attend.2.rest_0_ = bf16[4,64,7424]{2,1,0:T(8,128)(2,1)} custom-call(s32[1]{0:T(128)} %bitcast.2.core_ref.half_ref, s32[1]{0:T(128)} %bitcast.1.place_ref, s32[4,16]{1,0:T(4,128)S(1)} %copy-done.4, s32[4]{0:T(128)S(1)} %copy-done.5, bf16[4,64,7424]{2,1,0:T(8,128)(2,1)S(1)} %copy-done.2, bf16[2048,256]{1,0:T(8,128)(2,1)S(1)} %constant_dynamic-update-slice_fusion.k_ref.v_ref, ...), custom_call_target="tpu_custom_call" | custom-call | flops 2189426688 | bytes 4849664 | tf_op jit(solution)/shard_map/attend/pallas_call | solution.py:286
  85.5 0.0 collective-permute-done.23.k_ref.v_ref
  85.5 29.7 %attend.3 = bf16[4,64,7424]{2,1,0:T(8,128)(2,1)} custom-call(s32[1]{0:T(128)} %bitcast.half_ref, s32[1]{0:T(128)} %bitcast.1.place_ref, s32[4,16]{1,0:T(4,128)S(1)} %copy-done.4, s32[4]{0:T(128)S(1)} %copy-done.5, bf16[4,64,7424]{2,1,0:T(8,128)(2,1)S(1)} %copy-done.2, ...), custom_call_target="tpu_custom_call", output_to_operand_aliasing={{}: (9, {})} | custom-call | flops 2189426688 | bytes 4849664 | tf_op jit(solution)/shard_map/attend/pallas_call | solution.py:286
  (11 shorter events, 0.1 us)
Async XLA Ops:
  1.0 3.0 %collective-permute-start.2 = (bf16[256,256]{1,0:T(8,128)(2,1)S(1)}, bf16[256,256]{1,0:T(8,128)(2,1)S(1)}, u32[]{:S(2)}, u32[]{:S(2)}) collective-permute-start(bf16[256,256]{1,0:T(8,128)(2,1)S(1)} %pad_maximum_fusion.1), channel_id=1, source_target_pairs={{0,1},{1,0},{2,3},{3,2},{4,5},{5,4},{6,7},{7,6},{8,9},{9,8},{10,11... | collective-permute-start | bytes 393224 | tf_op jit(solution)/shard_map/ppermute | solution.py:380
  1.1 11.4 %collective-permute-start.1 = (bf16[256,256]{1,0:T(8,128)(2,1)S(1)}, bf16[256,256]{1,0:T(8,128)(2,1)S(1)}, u32[]{:S(2)}, u32[]{:S(2)}) collective-permute-start(bf16[256,256]{1,0:T(8,128)(2,1)S(1)} %pad_maximum_fusion.rest_2_), channel_id=1, source_target_pairs={{0,2},{1,3},{2,6},{3,7},{4,0},{5,1},{6,10},{7,11},{8,4},{9,5},{10,... | collective-permute-start | bytes 393224 | tf_op jit(solution)/shard_map/ppermute | solution.py:384
  3.8 8.7 %collective-permute-start = (bf16[256,256]{1,0:T(8,128)(2,1)S(1)}, bf16[256,256]{1,0:T(8,128)(2,1)S(1)}, u32[]{:S(2)}, u32[]{:S(2)}) collective-permute-start(bf16[256,256]{1,0:T(8,128)(2,1)S(1)} %pad_maximum_fusion.rest_2_), channel_id=1, source_target_pairs={{0,4},{1,5},{2,0},{3,1},{4,8},{5,9},{6,2},{7,3},{8,12},{9,13},{10,... | collective-permute-start | bytes 393224 | tf_op jit(solution)/shard_map/ppermute | solution.py:384
  4.0 8.6 %collective-permute-start.4 = (bf16[256,256]{1,0:T(8,128)(2,1)S(1)}, bf16[256,256]{1,0:T(8,128)(2,1)S(1)}, u32[]{:S(2)}, u32[]{:S(2)}) collective-permute-start(bf16[256,256]{1,0:T(8,128)(2,1)S(1)} %collective-permute-done.2.rest_10_), channel_id=1, source_target_pairs={{0,2},{1,3},{2,6},{3,7},{4,0},{5,1},{6,10},{7,11},{8,4},{9,5},{10,... | collective-permute-start | bytes 393224 | tf_op jit(solution)/shard_map/ppermute | solution.py:384
  5.3 7.3 %collective-permute-start.3 = (bf16[256,256]{1,0:T(8,128)(2,1)S(1)}, bf16[256,256]{1,0:T(8,128)(2,1)S(1)}, u32[]{:S(2)}, u32[]{:S(2)}) collective-permute-start(bf16[256,256]{1,0:T(8,128)(2,1)S(1)} %collective-permute-done.2.rest_10_), channel_id=1, source_target_pairs={{0,4},{1,5},{2,0},{3,1},{4,8},{5,9},{6,2},{7,3},{8,12},{9,13},{10,... | collective-permute-start | bytes 393224 | tf_op jit(solution)/shard_map/ppermute | solution.py:384
  5.5 0.9 copy-start
  6.4 0.7 copy-start.1
  12.5 43.3 %copy-start.4 = (s32[4,16]{1,0:T(4,128)S(1)}, s32[4,16]{1,0:T(4,128)}, u32[]{:S(2)}) copy-start(s32[4,16]{1,0:T(4,128)} %passage_ref.3) | copy-start | bytes 772
  12.6 43.3 %copy-start.5 = (s32[4]{0:T(128)S(1)}, s32[4]{0:T(128)}, u32[]{:S(2)}) copy-start(s32[4]{0:T(128)} %length_ref.3) | copy-start | bytes 52
  12.6 18.2 %collective-permute-start.5 = (bf16[128,4096]{1,0:T(8,128)(2,1)S(1)}, bf16[128,4096]{1,0:T(8,128)(2,1)S(1)}, u32[]{:S(2)}, u32[]{:S(2)}) collective-permute-start(bf16[128,4096]{1,0:T(8,128)(2,1)S(1)} %pool.1.rest_0_), channel_id=1, source_target_pairs={{0,1},{1,0},{2,3},{3,2},{4,5},{5,4},{6,7},{7,6},{8,9},{9,8},{10,11... | collective-permute-start | bytes 3145736 | tf_op jit(solution)/shard_map/ppermute | solution.py:380
  13.5 5.3 %collective-permute-start.6 = (bf16[256,256]{1,0:T(8,128)(2,1)S(1)}, bf16[256,256]{1,0:T(8,128)(2,1)S(1)}, u32[]{:S(2)}, u32[]{:S(2)}) collective-permute-start(bf16[256,256]{1,0:T(8,128)(2,1)S(1)} %collective-permute-done.rest_3_), channel_id=1, source_target_pairs={{0,4},{1,5},{2,0},{3,1},{4,8},{5,9},{6,2},{7,3},{8,12},{9,13},{10,... | collective-permute-start | bytes 393224 | tf_op jit(solution)/shard_map/ppermute | solution.py:384
  15.2 5.1 %collective-permute-start.13 = (bf16[256,256]{1,0:T(8,128)(2,1)S(1)}, bf16[256,256]{1,0:T(8,128)(2,1)S(1)}, u32[]{:S(2)}, u32[]{:S(2)}) collective-permute-start(bf16[256,256]{1,0:T(8,128)(2,1)S(1)} %collective-permute-done.4.rest_17_), channel_id=1, source_target_pairs={{0,2},{1,3},{2,6},{3,7},{4,0},{5,1},{6,10},{7,11},{8,4},{9,5},{10,... | collective-permute-start | bytes 393224 | tf_op jit(solution)/shard_map/ppermute | solution.py:384
  15.2 7.5 %collective-permute-start.9 = (bf16[256,256]{1,0:T(8,128)(2,1)S(1)}, bf16[256,256]{1,0:T(8,128)(2,1)S(1)}, u32[]{:S(2)}, u32[]{:S(2)}) collective-permute-start(bf16[256,256]{1,0:T(8,128)(2,1)S(1)} %collective-permute-done.1.rest_9_), channel_id=1, source_target_pairs={{0,2},{1,3},{2,6},{3,7},{4,0},{5,1},{6,10},{7,11},{8,4},{9,5},{10,... | collective-permute-start | bytes 393224 | tf_op jit(solution)/shard_map/ppermute | solution.py:384
  16.6 6.4 %collective-permute-start.11 = (bf16[256,256]{1,0:T(8,128)(2,1)S(1)}, bf16[256,256]{1,0:T(8,128)(2,1)S(1)}, u32[]{:S(2)}, u32[]{:S(2)}) collective-permute-start(bf16[256,256]{1,0:T(8,128)(2,1)S(1)} %collective-permute-done.3.rest_11_), channel_id=1, source_target_pairs={{0,4},{1,5},{2,0},{3,1},{4,8},{5,9},{6,2},{7,3},{8,12},{9,13},{10,... | collective-permute-start | bytes 393224 | tf_op jit(solution)/shard_map/ppermute | solution.py:384
  18.9 5.4 %collective-permute-start.7 = (bf16[256,256]{1,0:T(8,128)(2,1)S(1)}, bf16[256,256]{1,0:T(8,128)(2,1)S(1)}, u32[]{:S(2)}, u32[]{:S(2)}) collective-permute-start(bf16[256,256]{1,0:T(8,128)(2,1)S(1)} %collective-permute-done.6.rest_4_), channel_id=1, source_target_pairs={{0,4},{1,5},{2,0},{3,1},{4,8},{5,9},{6,2},{7,3},{8,12},{9,13},{10,... | collective-permute-start | bytes 393224 | tf_op jit(solution)/shard_map/ppermute | solution.py:384
  20.3 5.3 %collective-permute-start.14 = (bf16[256,256]{1,0:T(8,128)(2,1)S(1)}, bf16[256,256]{1,0:T(8,128)(2,1)}, u32[]{:S(2)}, u32[]{:S(2)}) collective-permute-start(bf16[256,256]{1,0:T(8,128)(2,1)S(1)} %collective-permute-done.13.rest_16_), channel_id=1, source_target_pairs={{0,2},{1,3},{2,6},{3,7},{4,0},{5,1},{6,10},{7,11},{8,4},{9,5},{10,... | collective-permute-start | bytes 393224 | tf_op jit(solution)/shard_map/ppermute | solution.py:384
  22.8 5.4 %collective-permute-start.10 = (bf16[256,256]{1,0:T(8,128)(2,1)S(1)}, bf16[256,256]{1,0:T(8,128)(2,1)}, u32[]{:S(2)}, u32[]{:S(2)}) collective-permute-start(bf16[256,256]{1,0:T(8,128)(2,1)S(1)} %collective-permute-done.9.rest_8_), channel_id=1, source_target_pairs={{0,2},{1,3},{2,6},{3,7},{4,0},{5,1},{6,10},{7,11},{8,4},{9,5},{10,... | collective-permute-start | bytes 393224 | tf_op jit(solution)/shard_map/ppermute | solution.py:384
  23.0 5.2 %collective-permute-start.12 = (bf16[256,256]{1,0:T(8,128)(2,1)S(1)}, bf16[256,256]{1,0:T(8,128)(2,1)}, u32[]{:S(2)}, u32[]{:S(2)}) collective-permute-start(bf16[256,256]{1,0:T(8,128)(2,1)S(1)} %collective-permute-done.11.rest_12_), channel_id=1, source_target_pairs={{0,4},{1,5},{2,0},{3,1},{4,8},{5,9},{6,2},{7,3},{8,12},{9,13},{10,... | collective-permute-start | bytes 393224 | tf_op jit(solution)/shard_map/ppermute | solution.py:384
  24.3 5.0 %collective-permute-start.8 = (bf16[256,256]{1,0:T(8,128)(2,1)S(1)}, bf16[256,256]{1,0:T(8,128)(2,1)}, u32[]{:S(2)}, u32[]{:S(2)}) collective-permute-start(bf16[256,256]{1,0:T(8,128)(2,1)S(1)} %collective-permute-done.7.rest_5_), channel_id=1, source_target_pairs={{0,4},{1,5},{2,0},{3,1},{4,8},{5,9},{6,2},{7,3},{8,12},{9,13},{10,... | collective-permute-start | bytes 393224 | tf_op jit(solution)/shard_map/ppermute | solution.py:384
  25.5 5.3 %collective-permute-start.15 = (bf16[256,256]{1,0:T(8,128)(2,1)}, bf16[256,256]{1,0:T(8,128)(2,1)}, u32[]{:S(2)}, u32[]{:S(2)}) collective-permute-start(bf16[256,256]{1,0:T(8,128)(2,1)} %collective-permute-done.14.rest_15_), channel_id=1, source_target_pairs={{0,2},{1,3},{2,6},{3,7},{4,0},{5,1},{6,10},{7,11},{8,4},{9,5},{10,... | collective-permute-start | bytes 393224 | tf_op jit(solution)/shard_map/ppermute | solution.py:384
  25.7 30.1 %copy-start.2 = (bf16[4,64,7424]{2,1,0:T(8,128)(2,1)S(1)}, bf16[4,64,7424]{2,1,0:T(8,128)(2,1)}, u32[]{:S(2)}) copy-start(bf16[4,64,7424]{2,1,0:T(8,128)(2,1)} %q_ref.3) | copy-start | bytes 11403268
  25.7 30.1 %copy-start.3 = (bf16[4,64,512]{2,1,0:T(8,128)(2,1)S(1)}, bf16[4,64,512]{2,1,0:T(8,128)(2,1)}, u32[]{:S(2)}) copy-start(bf16[4,64,512]{2,1,0:T(8,128)(2,1)} %own_v_ref.3) | copy-start | bytes 786436
  32.7 5.2 %collective-permute-start.18 = (bf16[256,256]{1,0:T(8,128)(2,1)S(1)}, bf16[256,256]{1,0:T(8,128)(2,1)S(1)}, u32[]{:S(2)}, u32[]{:S(2)}) collective-permute-start(bf16[256,256]{1,0:T(8,128)(2,1)S(1)} %project.1), channel_id=1, source_target_pairs={{0,12},{1,13},{2,14},{3,15},{4,0},{5,1},{6,2},{7,3},{8,4},{9,5},{1... | collective-permute-start | bytes 393224 | tf_op jit(solution)/shard_map/ppermute | solution.py:384
  36.0 11.0 %collective-permute-start.17 = (bf16[256,256]{1,0:T(8,128)(2,1)S(1)}, bf16[256,256]{1,0:T(8,128)(2,1)S(1)}, u32[]{:S(2)}, u32[]{:S(2)}) collective-permute-start(bf16[256,256]{1,0:T(8,128)(2,1)S(1)} %project.1), channel_id=1, source_target_pairs={{0,8},{1,9},{2,10},{3,11},{4,12},{5,13},{6,14},{7,15},{8,0},{9,1},... | collective-permute-start | bytes 393224 | tf_op jit(solution)/shard_map/ppermute | solution.py:384
  36.0 11.4 %collective-permute-start.16 = (bf16[256,256]{1,0:T(8,128)(2,1)S(1)}, bf16[256,256]{1,0:T(8,128)(2,1)S(1)}, u32[]{:S(2)}, u32[]{:S(2)}) collective-permute-start(bf16[256,256]{1,0:T(8,128)(2,1)S(1)} %project.1), channel_id=1, source_target_pairs={{0,4},{1,5},{2,6},{3,7},{4,8},{5,9},{6,10},{7,11},{8,12},{9,13},{1... | collective-permute-start | bytes 393224 | tf_op jit(solution)/shard_map/ppermute | solution.py:384
  36.5 12.0 %collective-permute-start.19 = (bf16[256,256]{1,0:T(8,128)(2,1)S(1)}, bf16[256,256]{1,0:T(8,128)(2,1)S(1)}, u32[]{:S(2)}, u32[]{:S(2)}) collective-permute-start(bf16[256,256]{1,0:T(8,128)(2,1)S(1)} %project.1), channel_id=1, source_target_pairs={{0,2},{1,3},{2,0},{3,1},{4,6},{5,7},{6,4},{7,5},{8,10},{9,11},{10,... | collective-permute-start | bytes 393224 | tf_op jit(solution)/shard_map/ppermute | solution.py:384
  37.9 14.8 %collective-permute-start.22 = (bf16[256,256]{1,0:T(8,128)(2,1)S(1)}, bf16[256,256]{1,0:T(8,128)(2,1)S(1)}, u32[]{:S(2)}, u32[]{:S(2)}) collective-permute-start(bf16[256,256]{1,0:T(8,128)(2,1)S(1)} %collective-permute-done.18), channel_id=1, source_target_pairs={{0,2},{1,3},{2,0},{3,1},{4,6},{5,7},{6,4},{7,5},{8,10},{9,11},{10,... | collective-permute-start | bytes 393224 | tf_op jit(solution)/shard_map/ppermute | solution.py:384
  47.0 5.7 %collective-permute-start.21 = (bf16[256,256]{1,0:T(8,128)(2,1)S(1)}, bf16[256,256]{1,0:T(8,128)(2,1)S(1)}, u32[]{:S(2)}, u32[]{:S(2)}) collective-permute-start(bf16[256,256]{1,0:T(8,128)(2,1)S(1)} %collective-permute-done.17), channel_id=1, source_target_pairs={{0,2},{1,3},{2,0},{3,1},{4,6},{5,7},{6,4},{7,5},{8,10},{9,11},{10,... | collective-permute-start | bytes 393224 | tf_op jit(solution)/shard_map/ppermute | solution.py:384
  47.4 5.3 %collective-permute-start.20 = (bf16[256,256]{1,0:T(8,128)(2,1)S(1)}, bf16[256,256]{1,0:T(8,128)(2,1)S(1)}, u32[]{:S(2)}, u32[]{:S(2)}) collective-permute-start(bf16[256,256]{1,0:T(8,128)(2,1)S(1)} %collective-permute-done.16), channel_id=1, source_target_pairs={{0,2},{1,3},{2,0},{3,1},{4,6},{5,7},{6,4},{7,5},{8,10},{9,11},{10,... | collective-permute-start | bytes 393224 | tf_op jit(solution)/shard_map/ppermute | solution.py:384
  52.8 32.7 %collective-permute-start.23 = (bf16[2048,256]{1,0:T(8,128)(2,1)S(1)}, bf16[2048,256]{1,0:T(8,128)(2,1)S(1)}, u32[]{:S(2)}, u32[]{:S(2)}) collective-permute-start(bf16[2048,256]{1,0:T(8,128)(2,1)S(1)} %constant_dynamic-update-slice_fusion.k_ref.v_ref), channel_id=1, source_target_pairs={{0,1},{1,0},{2,3},{3,2},{4,5},{5,4},{6,7},{7,6},{8,9},{9,8},{10,11... | collective-permute-start | bytes 3145736 | tf_op jit(solution)/shard_map/ppermute | solution.py:380

commit v9 on v0

v9 whole, which is shorter than its diff:
```python
import functools
import math

import jax
import jax.numpy as jnp
from jax import lax
from jax.experimental import pallas as pl
from jax.experimental.pallas import tpu as pltpu
from jax.sharding import PartitionSpec as P

D = 4096
CH = 32
CHD = 128
MEM = 32
LEN = 128
QLEN = 64
TOPK = 16
H = 116
HD = 64
KVH = 4
GROUP = 29
KVW = 512

LANES = 2 * HD
PAIRS = GROUP
HALF = PAIRS * LANES
ROWS = TOPK * MEM
KEYS = 2 * (ROWS + QLEN)
NEG = -1e30
SUM_LOW, SUM_HIGH = 2.0 ** -40, 2.0 ** 60
POOL_WIDTH = 1024
CHIP = 8
STEP = 8
BLOCK = 16
MIB = 1024 * 1024


def place_of(chip, ring):
    line, lane = lax.div(chip, 2), lax.rem(chip, 2)
    return line + lane * (ring - 1 - 2 * line)


def chip_at(place, ring):
    lane = lax.div(place, ring // 2)
    line = place + lane * (ring - 1 - 2 * place)
    return 2 * line + lane


def pool_kernel(states_hbm, queries_hbm, gain_hbm, out_ref, states, queries, gain, pooled, arrived):
    passages = states_hbm.shape[0]
    two = 2 * CHD
    groups = D // POOL_WIDTH
    small = [
        pltpu.make_async_copy(queries_hbm, queries, arrived.at[groups]),
        pltpu.make_async_copy(gain_hbm, gain, arrived.at[groups + 1]),
    ]
    large = [
        pltpu.make_async_copy(
            states_hbm.at[:, :, pl.ds(j * POOL_WIDTH, POOL_WIDTH)], states.at[j], arrived.at[j]
        )
        for j in range(groups)
    ]
    for copy in small[:1] + large + small[1:]:
        copy.start()
    small[0].wait()
    zero = jnp.zeros((MEM, CHD), jnp.bfloat16)
    blank = jnp.zeros((2 * MEM, LEN), jnp.bfloat16)
    totals = [jnp.zeros((MEM, CHD), jnp.float32)] * passages
    for j in range(groups):
        large[j].wait()
        blocks = []
        for at in range(0, POOL_WIDTH, two):
            column = j * POOL_WIDTH + at
            lhs = jnp.concatenate(
                [
                    jnp.concatenate([queries[:, column:column + CHD], zero], axis=1),
                    jnp.concatenate([zero, queries[:, column + CHD:column + two]], axis=1),
                ],
                axis=0,
            )
            for p in range(0, passages, 2):
                tokens = states[j, p:p + 2, :, at:at + two].reshape(2 * LEN, two)
                scores = lax.dot_general(
                    lhs, tokens, (((1,), (1,)), ((), ())), preferred_element_type=jnp.float32
                ) * (1.0 / math.sqrt(CHD))
                blocks.append((column, p, tokens, scores))
        for column, p, tokens, scores in blocks:
            rows = []
            for n in range(2):
                part = scores[:, n * LEN:(n + 1) * LEN]
                part = jnp.exp(part - jnp.max(part, axis=1, keepdims=True))
                part = (part / jnp.sum(part, axis=1, keepdims=True)).astype(jnp.bfloat16)
                rows.append(jnp.concatenate([blank, part] if n else [part, blank], axis=1))
            mixed = jnp.dot(jnp.concatenate(rows, axis=0), tokens, preferred_element_type=jnp.float32)
            for n in range(2):
                for head in range(2):
                    top = (2 * n + head) * MEM
                    block = mixed[top:top + MEM, head * CHD:(head + 1) * CHD]
                    place = slice(column + head * CHD, column + (head + 1) * CHD)
                    pooled[(p + n) * MEM:(p + n + 1) * MEM, place] = block
                    totals[p + n] = totals[p + n] + block * block
    small[1].wait()
    mean_square = jnp.sum(jnp.concatenate(totals, axis=0), axis=1, keepdims=True) * (1.0 / D)
    scale = lax.rsqrt(mean_square + 1e-06)
    factor = gain[...].astype(jnp.float32).reshape(1, D)
    out_ref[...] = (pooled[...] * scale * factor).astype(jnp.bfloat16)


def pool(states, queries, gain):
    count = states.shape[0]
    groups = D // POOL_WIDTH
    hbm = pl.BlockSpec(memory_space=pltpu.HBM)
    return pl.pallas_call(
        pool_kernel,
        in_specs=[hbm] * 3,
        out_specs=pl.BlockSpec(memory_space=pltpu.VMEM),
        out_shape=jax.ShapeDtypeStruct((count * MEM, D), jnp.bfloat16),
        scratch_shapes=[
            pltpu.VMEM((groups, count, LEN, POOL_WIDTH), jnp.bfloat16),
            pltpu.VMEM((MEM, D), jnp.bfloat16),
            pltpu.VMEM((D,), jnp.bfloat16),
            pltpu.VMEM((count * MEM, D), jnp.float32),
            pltpu.SemaphoreType.DMA((groups + 2,)),
        ],
        compiler_params=pltpu.CompilerParams(vmem_limit_bytes=56 * MIB),
        cost_estimate=pl.CostEstimate(
            flops=4 * count * MEM * LEN * D, bytes_accessed=2 * count * LEN * D,
            transcendentals=count * CH * MEM * LEN,
        ),
        name="pool",
    )(states, queries, gain)


def attend_kernel(half_ref, start_ref, length_ref, q_hbm, kv_ref, own_kv_ref, *rest):
    out_hbm = rest[-13]
    (
        questions, answers, memory, key_side, value_side, weights, bias, marker, scores, all_weights,
        arrived, sent,
    ) = rest[-12:]
    count = q_hbm.shape[0]
    half_at = pl.multiple_of(half_ref[0] * HALF, LANES)
    own_at = pl.multiple_of(half_ref[0] * LANES, LANES)
    factor = math.log2(math.e) / math.sqrt(HD)

    def fetch(query):
        return pltpu.make_async_copy(
            q_hbm.at[query, :, pl.ds(half_at, HALF)], questions.at[query], arrived.at[query]
        )

    def send(query):
        return pltpu.make_async_copy(
            answers.at[query], out_hbm.at[query, :, pl.ds(half_at, HALF)], sent.at[query]
        )

    for query in range(count):
        fetch(query).start()

    lane = lax.broadcasted_iota(jnp.int32, (KEYS, LANES), 1)
    row = lax.broadcasted_iota(jnp.int32, (KEYS, LANES), 0)
    in_b = ((row >= ROWS) & (row < 2 * ROWS)) | (row >= 2 * ROWS + QLEN)
    ones = jnp.where((lane >= HD) == in_b, 1.0, 0.0).astype(jnp.bfloat16)
    key_side[...] = jnp.zeros_like(key_side)
    for g in range(2):
        value_side[g, :, LANES:] = ones

    half = PAIRS // 2
    chunks = []
    for g in range(2):
        tiles = list(range(half + 1)) if g == 0 else list(range(half, PAIRS))
        chunks += [(g, tiles[at:at + STEP]) for at in range(0, len(tiles), STEP)]

    def answer(query, carry):
        for slot in range(TOPK):
            start = pl.multiple_of(start_ref[query, slot], MEM)
            memory[slot * MEM:(slot + 1) * MEM, :] = kv_ref[pl.ds(start, MEM), :].astype(jnp.float32)
        length = length_ref[query]

        turned = jnp.transpose(memory[:, :LANES]).astype(jnp.bfloat16)
        own_k = own_kv_ref[query, :, pl.ds(own_at, LANES)].astype(jnp.float32)
        own_turned = jnp.transpose(jnp.concatenate([own_k, own_k], axis=0))
        column = lax.broadcasted_iota(jnp.int32, (HD, LANES), 1)
        for g in range(2):
            for member in range(2):
                rows = slice(member * HD, (member + 1) * HD)
                key_side[g, rows, member * ROWS:(member + 1) * ROWS] = turned[g * HD:(g + 1) * HD]
                own = own_turned[g * HD:(g + 1) * HD]
                mine = (column >= HD) if member else (column < HD)
                key_side[g, rows, 2 * ROWS:] = jnp.where(mine, own, 0.0).astype(jnp.bfloat16)

        token = lax.broadcasted_iota(jnp.int32, (QLEN, LANES), 0)
        low = lax.broadcasted_iota(jnp.int32, (QLEN, LANES), 1) < HD
        key = lax.rem(lax.broadcasted_iota(jnp.int32, (QLEN, LANES), 1), HD)
        bias[...] = jnp.where((key <= token) & (key < length), 0.0, NEG)
        alive = token < length
        fetch(query).wait()

        def stacked(tiles):
            return jnp.concatenate([questions[query, :, t * LANES:(t + 1) * LANES] for t in tiles], axis=0)

        def key_product(i):
            g, tiles = chunks[i]
            lhs = stacked(tiles)
            for c in range(0, KEYS, 2 * LANES):
                part = slice(c, min(c + 2 * LANES, KEYS))
                got = jnp.dot(lhs, key_side[g, :, part], preferred_element_type=jnp.float32) * factor
                if c == 2 * ROWS:
                    got = got + jnp.concatenate([bias[...]] * len(tiles), axis=0)
                weights[i % 2, :len(tiles) * QLEN, part] = jnp.exp2(got).astype(jnp.bfloat16)

        def finish(i, mixed):
            g, tiles = chunks[i]
            for n, t in enumerate(tiles):
                rows = slice(n * QLEN, (n + 1) * QLEN)
                result = jnp.where(alive, mixed[rows, :LANES] / mixed[rows, LANES:], 0.0)
                result = result.astype(jnp.bfloat16)
                at = slice(t * LANES, (t + 1) * LANES)
                if t == half and g == 1:
                    result = jnp.where(low, answers[query, :, at], result)
                answers[query, :, at] = result

        def value_product(i, seen):
            g, tiles = chunks[i]
            size = len(tiles) * QLEN
            mixed = jnp.dot(weights[i % 2, :size, :], value_side[g], preferred_element_type=jnp.float32)
            for at in range(0, size, QLEN):
                sums = mixed[at:at + QLEN, LANES:]
                seen = jnp.where((sums > SUM_LOW) & (sums < SUM_HIGH), seen, 1.0)
            finish(i, mixed)
            return seen

        key_product(0)

        own_v_at = pl.multiple_of(own_at + KVH * HD, LANES)
        own_v = own_kv_ref[query, :, pl.ds(own_v_at, LANES)].astype(jnp.float32)
        for block, at in ((memory[:, LANES:], 0), (own_v, 2 * ROWS)):
            size = block.shape[0]
            swapped = pltpu.roll(block, HD, 1)
            lower = lax.broadcasted_iota(jnp.int32, block.shape, 1) < HD
            for g in range(2):
                one, two = (block, swapped) if g == 0 else (swapped, block)
                value_side[g, at:at + size, :LANES] = jnp.where(lower, one, 0.0).astype(jnp.bfloat16)
                value_side[g, at + size:at + 2 * size, :LANES] = jnp.where(lower, 0.0, two).astype(
                    jnp.bfloat16
                )

        seen = jnp.zeros((QLEN, LANES), jnp.float32)
        for i in range(len(chunks)):
            if i + 1 < len(chunks):
                key_product(i + 1)
            seen = value_product(i, seen)
        marker[0] = jnp.max(seen)

        @pl.when(marker[0] > 0.0)
        def _():
            for i, (g, tiles) in enumerate(chunks):
                size = len(tiles) * QLEN
                scores[:size, :] = jnp.dot(stacked(tiles), key_side[g], preferred_element_type=jnp.float32)

                def soften(n, carry):
                    rows = pl.ds(pl.multiple_of(n * QLEN, QLEN), QLEN)
                    own_scores = scores[rows, 2 * ROWS:] + bias[...]
                    tops = []
                    for member in range(2):
                        columns = slice(member * ROWS, (member + 1) * ROWS)
                        top = jnp.where(low, own_scores, NEG) if member == 0 else jnp.where(low, NEG, own_scores)
                        top = jnp.maximum(
                            jnp.max(top, axis=1, keepdims=True),
                            jnp.max(scores[rows, columns], axis=1, keepdims=True),
                        )
                        all_weights[rows, columns] = jnp.exp2(
                            (scores[rows, columns] - top) * factor
                        ).astype(jnp.bfloat16)
                        tops.append(top)
                    all_weights[rows, 2 * ROWS:] = jnp.exp2(
                        (own_scores - jnp.where(low, tops[0], tops[1])) * factor
                    ).astype(jnp.bfloat16)
                    return carry

                lax.fori_loop(0, len(tiles), soften, 0)
                finish(
                    i, jnp.dot(all_weights[:size, :], value_side[g], preferred_element_type=jnp.float32)
                )

        send(query).start()
        return carry

    lax.fori_loop(0, count, answer, 0)
    for query in range(count):
        send(query).wait()


def attend(half, starts, lengths, questions, memory_kv, own_kv, earlier=None):
    count = questions.shape[0]
    hbm, vmem, smem = (pl.BlockSpec(memory_space=x) for x in (pltpu.HBM, pltpu.VMEM, pltpu.SMEM))
    operands = [half.reshape(1), starts, lengths, questions, memory_kv, own_kv]
    in_specs = [smem, smem, smem, hbm, vmem, vmem]
    aliases = {}
    if earlier is not None:
        aliases = {len(operands): 0}
        operands.append(earlier)
        in_specs.append(hbm)
    return pl.pallas_call(
        attend_kernel,
        in_specs=in_specs,
        out_specs=hbm,
        out_shape=jax.ShapeDtypeStruct((count, QLEN, H * HD), jnp.bfloat16),
        scratch_shapes=[
            pltpu.VMEM((count, QLEN, HALF), jnp.bfloat16),
            pltpu.VMEM((count, QLEN, HALF), jnp.bfloat16),
            pltpu.VMEM((ROWS, 2 * LANES), jnp.float32),
            pltpu.VMEM((2, LANES, KEYS), jnp.bfloat16),
            pltpu.VMEM((2, KEYS, 2 * LANES), jnp.bfloat16),
            pltpu.VMEM((2, STEP * QLEN, KEYS), jnp.bfloat16),
            pltpu.VMEM((QLEN, LANES), jnp.float32),
            pltpu.SMEM((1,), jnp.float32),
            pltpu.VMEM((STEP * QLEN, KEYS), jnp.float32),
            pltpu.VMEM((STEP * QLEN, KEYS), jnp.bfloat16),
            pltpu.SemaphoreType.DMA((count,)),
            pltpu.SemaphoreType.DMA((count,)),
        ],
        input_output_aliases=aliases,
        compiler_params=pltpu.CompilerParams(vmem_limit_bytes=40 * MIB),
        cost_estimate=pl.CostEstimate(
            flops=2 * count * QLEN * H * HD * (ROWS + QLEN),
            bytes_accessed=2 * count * QLEN * H * HD,
            transcendentals=count * QLEN * H * (ROWS + QLEN) // 2,
        ),
        name="attend",
    )(*operands)


def project_kernel(ring, core_ref, place_ref, own_hbm, other_ref, *rest):
    weights, (out_ref, own, arrived) = rest[:-3], rest[-3:]
    count = own.shape[0]
    depth = weights[0].shape[0]
    core = core_ref[0]
    pieces = []
    for n, weight in enumerate(weights):
        part, i = n // ring, n % ring
        chip = chip_at(lax.rem(ring + place_ref[0] - i, ring), ring)
        columns = pl.ds(pl.multiple_of((2 * chip + (1 - core if part else core)) * depth, depth), depth)
        copy = pltpu.make_async_copy(own_hbm.at[:, columns], own.at[:, columns], arrived.at[n])
        copy.start()
        pieces.append((weight, columns, copy))
    total = jnp.zeros((2 * count, weights[0].shape[1]), jnp.float32)
    for weight, columns, copy in pieces:
        copy.wait()
        rows = jnp.concatenate([own[:, columns], other_ref[:, columns]], axis=0)
        total += jnp.dot(rows, weight[...], preferred_element_type=jnp.float32)
    result = total.astype(jnp.bfloat16)
    out_ref[pl.ds(pl.multiple_of(core * count, count), count)] = result[:count]
    out_ref[pl.ds(pl.multiple_of((1 - core) * count, count), count)] = result[count:]


def project(core, place, own_rows, other_rows, weights):
    count = own_rows.shape[0]
    width = weights[0].shape[1]
    vmem = pl.BlockSpec(memory_space=pltpu.VMEM)
    smem = pl.BlockSpec(memory_space=pltpu.SMEM)
    return pl.pallas_call(
        functools.partial(project_kernel, len(weights) // 2),
        in_specs=[smem, smem, pl.BlockSpec(memory_space=pltpu.HBM)] + [vmem] * (1 + len(weights)),
        out_specs=vmem,
        scratch_shapes=[pltpu.VMEM(own_rows.shape, jnp.bfloat16), pltpu.SemaphoreType.DMA((len(weights),))],
        out_shape=jax.ShapeDtypeStruct((2 * count, width), jnp.bfloat16),
        compiler_params=pltpu.CompilerParams(vmem_limit_bytes=16 * MIB),
        cost_estimate=pl.CostEstimate(
            flops=4 * count * D * width, bytes_accessed=2 * D * width, transcendentals=0
        ),
        name="project",
    )(core.reshape(1), place, own_rows, other_rows, *weights)


def local(
    extent,
    passage_states,
    memory_queries,
    memory_gain,
    kv_weight,
    retrieval,
    question_queries,
    question_kv,
    question_lengths,
):
    me = lax.axis_index("pass")
    core, chip = me & 1, lax.div(me, 2)
    chips = extent // 2
    depth = kv_weight.shape[0]

    if chips != 8 or depth % LANES:
        memory_rows = pool(passage_states, memory_queries, memory_gain)
        whole_weight = lax.all_gather(kv_weight, "pass", axis=0, tiled=True)
        memory_kv = jnp.dot(memory_rows, whole_weight, preferred_element_type=jnp.float32)
        everything = lax.all_gather(memory_kv.astype(jnp.bfloat16), "pass", axis=0, tiled=True)
        halves = everything.reshape(-1, 2, 2, LANES).transpose(2, 0, 1, 3).reshape(2, -1, 2 * LANES)
        rest = (retrieval * MEM, question_lengths, question_queries)
        context = attend(jnp.int32(0), *rest, halves[0], question_kv)
        return attend(jnp.int32(1), *rest, halves[1], question_kv, context)

    place = place_of(chip, chips).reshape(1)
    order = [2 * line for line in range(chips // 2)] + [2 * line + 1 for line in range(chips // 2)][::-1]

    def to_partner(x):
        return lax.ppermute(x, "pass", [(i, i ^ 1) for i in range(extent)])

    def along(x, target):
        pairs = [(c, target(c // 2, c % 2)) for c in range(chips)]
        return lax.ppermute(x, "pass", [(2 * s + c, 2 * d + c) for s, d in pairs for c in range(2)])

    def along_ring(x, step):
        return along(x, lambda line, lane: order[(order.index(2 * line + lane) + step) % chips])

    def round_the_ring(x, up, down, rounds):
        up, down = [x, up], [down]
        while len(up) <= rounds:
            up.append(along_ring(up[-1], 1))
        while len(up) + len(down) < chips:
            down.append(along_ring(down[-1], -1))
        return up + down[::-1]

    def line_by_line(block):
        lines = chips // 2
        blocks = [block]
        for k in range(1, lines):
            blocks.append(along(block, lambda line, lane: 2 * ((line + k) % lines) + lane))
        return blocks + [along(x, lambda line, lane: 2 * line + 1 - lane) for x in blocks]

    def columns(half):
        return jnp.concatenate(
            [
                lax.dynamic_slice_in_dim(kv_weight, half * LANES + at, LANES, axis=1)
                for at in (0, KVH * HD)
            ],
            axis=1,
        )

    pieces = [columns(core), to_partner(columns(1 - core))]
    hops = [along_ring(x, step) for x in pieces for step in (1, -1)]
    memory_rows = pool(passage_states, memory_queries, memory_gain)
    *hops, memory_rows = lax.optimization_barrier((*hops, memory_rows))
    weights = round_the_ring(pieces[0], hops[0], hops[1], chips // 2)
    weights += round_the_ring(pieces[1], hops[2], hops[3], chips // 2 - 1)
    memory_kv = project(core, place, memory_rows, to_partner(memory_rows), weights)
    near = jnp.concatenate(line_by_line(memory_kv), axis=0)
    far = to_partner(near)

    lines = chips // 2
    of_chip = lax.div(retrieval, CHIP)
    back = lax.rem(lines + lax.div(chip, 2) - lax.div(of_chip, 2), lines)
    slot = back + lines * lax.rem(lax.rem(chip, 2) + lax.rem(of_chip, 2), 2)
    starts = (slot * CHIP + lax.rem(retrieval, CHIP)) * MEM
    rest = (starts, question_lengths, question_queries)
    context = attend(core, *rest, near, question_kv)
    return attend(1 - core, *rest, far, question_kv, context)


def solution(mesh):
    placed = (
        P(("groups", "pass"), None, None),
        P(),
        P(),
        P("pass", None),
        P(("groups", "pass"), None),
        P(("groups", "pass"), None, None),
        P(("groups", "pass"), None, None),
        P(("groups", "pass")),
    )
    return jax.shard_map(
        functools.partial(local, mesh.shape["pass"]),
        mesh=mesh,
        in_specs=placed,
        out_specs=P(("groups", "pass"), None, None),
        check_vma=False,
    )
```

time: 242 us -> 150 us (0.62)
  Pallas kernels: 0 us -> 99 us
  matrix products: 95.4 us -> 0 us
  waiting for transfers between devices: 74.9 us -> 24.6 us
  local copies, waits for them, and re-layouts: 45.9 us -> 4.36 us
  starting transfers between devices: 0.04 us -> 21.3 us
  between operations: 13.5 us -> 0.38 us
  other arithmetic: 10.9 us -> 0.06 us
    pallas_call x0 -> x4, Pallas kernels: none -> 99 us  [the longest x2 90.5 us: attend(): pl.pallas_call(attend_kernel, in_specs=in_specs, out_specs=hbm, out_shape...]
    all_gather x2 -> x0, waiting for transfers between devices: 74.1 us -> none  [the longest x1 39.7 us: local(): everything = lax.all_gather(memory_kv, 'pass', axis=0, tiled=True)]
    dot_general x13 -> x0, matrix products: 48.9 us -> none  [the longest x4 36.3 us: attend_query(): jnp.einsum('gjts,sgd->tgjd', weights, value_rows, preferred_element_type=...]
    sub x4 -> x0, matrix products: 46.5 us -> none  [attend_query(): weights = jax.nn.softmax(scores, axis=-1).astype(jnp.bfloat16)]
    ppermute x0 -> x24, waiting for transfers between devices: none -> 24.6 us  [the longest x21 24.6 us: along(): lax.ppermute(x, 'pass', [(2 * s + c, 2 * d + c) for s, d in pairs for c i...]
    dynamic_slice x32 -> x1, local copies, waits for them, and re-layouts: 24.7 us -> 0.96 us  [columns(): lax.dynamic_slice_in_dim(kv_weight, half * LANES + at, LANES, axis=1)]
    ppermute x0 -> x24, starting transfers between devices: none -> 21.3 us  [the longest x21 17.4 us: along(): lax.ppermute(x, 'pass', [(2 * s + c, 2 * d + c) for s, d in pairs for c i...]
    reshape x9 -> x0, local copies, waits for them, and re-layouts: 9.55 us -> none  [the longest x4 9.07 us: attend_query(): query_heads = question.reshape(QLEN, KVH, GROUP, HD)]
  transfers between devices with their start and end apart: 2 -> 24, of which waited for: 2 -> 8; matrix products, arithmetic and copies ran while one was open for 9% -> 0% of each run, Pallas kernels for 0% -> 34%
where the time goes in v9:
time: 150 us
  Pallas kernels  99 us (66%)
  waiting for transfers between devices  24.6 us (16%)
  starting transfers between devices  21.3 us (14%)
  local copies, waits for them, and re-layouts  4.36 us (3%)
    pallas_call x2, Pallas kernels, attend(): pl.pallas_call(attend_kernel, in_specs=in_specs, out_specs=hbm, out_shape...  90.5 us
    ppermute x21, waiting for transfers between devices, along(): lax.ppermute(x, 'pass', [(2 * s + c, 2 * d + c) for s, d in pairs for c i...  24.6 us
    ppermute x21, starting transfers between devices, along(): lax.ppermute(x, 'pass', [(2 * s + c, 2 * d + c) for s, d in pairs for c i...  17.4 us
    pallas_call x1, Pallas kernels, pool(): pl.pallas_call(pool_kernel, in_specs=[hbm] * 3, out_specs=pl.BlockSpec(me...  6.07 us
    ppermute x3, starting transfers between devices, to_partner(): return lax.ppermute(x, 'pass', [(i, i ^ 1) for i in range(extent)])  3.84 us
    unnamed x19, local copies, waits for them, and re-layouts  3.39 us
  transfers between devices with their start and end apart: 24, of which 8 were waited for; matrix products, arithmetic and copies ran while one was open for 0% of the time, Pallas kernels for 34%

profile of v9, /device:TPU:1, one launch (start us, length us, event | category | flops | bytes accessed | tf_op | source)
XLA Modules:
  0.0 149.6 jit_solution(17989206149695025081)
XLA Ops:
  0.0 1.0 constant_dynamic-slice_fusion.1
  1.0 0.1 collective-permute-start.2
  1.1 2.7 %collective-permute-start.1 = (bf16[256,256]{1,0:T(8,128)(2,1)S(1)}, bf16[256,256]{1,0:T(8,128)(2,1)S(1)}, u32[]{:S(2)}, u32[]{:S(2)}) collective-permute-start(bf16[256,256]{1,0:T(8,128)(2,1)S(1)} %pad_maximum_fusion.rest_0_), channel_id=1, source_target_pairs={{0,2},{1,3},{2,6},{3,7},{4,0},{5,1},{6,10},{7,11},{8,4},{9,5},{10,... | collective-permute-start | bytes 393224 | tf_op jit(solution)/shard_map/ppermute | solution.py:408
  3.8 0.2 collective-permute-start
  4.0 0.0 collective-permute-done.2.rest_8_
  4.0 1.3 collective-permute-start.4
  5.3 0.2 collective-permute-start.3
  5.5 0.0 copy-start.3
  5.5 6.1 %pool.1.own_hbm = bf16[128,4096]{1,0:T(8,128)(2,1)} custom-call(bf16[4,128,4096]{2,1,0:T(8,128)(2,1)} %states_hbm.1, bf16[32,4096]{1,0:T(8,128)(2,1)} %queries_hbm.1, bf16[4096]{0:T(1024)(128)(2,1)} %gain_hbm.1), custom_call_target="tpu_custom_call" | custom-call | flops 268435456 | bytes 4194304 | tf_op jit(solution)/shard_map/pool/pallas_call | solution.py:113
  11.5 0.0 copy-start.5
  11.6 0.0 copy-start.4
  11.6 0.0 collective-permute-done.1.rest_7_
  11.6 0.0 collective-permute-done.rest_1_
  11.6 0.0 collective-permute-done.4.rest_15_
  11.6 0.0 collective-permute-done.3.rest_9_
  11.6 1.0 collective-permute-start.5
  12.6 1.6 %collective-permute-start.6 = (bf16[256,256]{1,0:T(8,128)(2,1)S(1)}, bf16[256,256]{1,0:T(8,128)(2,1)S(1)}, u32[]{:S(2)}, u32[]{:S(2)}) collective-permute-start(bf16[256,256]{1,0:T(8,128)(2,1)S(1)} %collective-permute-done.rest_1_), channel_id=1, source_target_pairs={{0,4},{1,5},{2,0},{3,1},{4,8},{5,9},{6,2},{7,3},{8,12},{9,13},{10,... | collective-permute-start | bytes 393224 | tf_op jit(solution)/shard_map/ppermute | solution.py:408
  14.2 0.0 collective-permute-start.13
  14.2 1.4 collective-permute-start.9
  15.6 0.1 collective-permute-start.11
  15.7 2.2 %collective-permute-done.6.rest_2_ = bf16[256,256]{1,0:T(8,128)(2,1)S(1)} collective-permute-done((bf16[256,256]{1,0:T(8,128)(2,1)S(1)}, bf16[256,256]{1,0:T(8,128)(2,1)S(1)}, u32[]{:S(2)}, u32[]{:S(2)}) %collective-permute-start.6) | collective-permute-done | bytes 131104 | tf_op jit(solution)/shard_map/ppermute | solution.py:408
  17.9 1.4 collective-permute-start.7
  19.3 0.0 collective-permute-done.13.rest_14_
  19.3 0.1 collective-permute-start.14
  19.3 2.4 %collective-permute-done.9.rest_6_ = bf16[256,256]{1,0:T(8,128)(2,1)S(1)} collective-permute-done((bf16[256,256]{1,0:T(8,128)(2,1)S(1)}, bf16[256,256]{1,0:T(8,128)(2,1)S(1)}, u32[]{:S(2)}, u32[]{:S(2)}) %collective-permute-start.9) | collective-permute-done | bytes 131104 | tf_op jit(solution)/shard_map/ppermute | solution.py:408
  21.8 0.2 collective-permute-start.10
  22.0 0.0 collective-permute-done.11.rest_10_
  22.0 1.2 collective-permute-start.12
  23.2 0.0 collective-permute-done.7.rest_3_
  23.3 1.3 collective-permute-start.8
  24.5 0.0 collective-permute-done.14.rest_13_
  24.5 0.2 collective-permute-start.15
  24.7 2.4 %collective-permute-done.10.rest_5_ = bf16[256,256]{1,0:T(8,128)(2,1)S(1)} collective-permute-done((bf16[256,256]{1,0:T(8,128)(2,1)S(1)}, bf16[256,256]{1,0:T(8,128)(2,1)S(1)}, u32[]{:S(2)}, u32[]{:S(2)}) %collective-permute-start.10) | collective-permute-done | bytes 131104 | tf_op jit(solution)/shard_map/ppermute | solution.py:408
  27.1 0.0 collective-permute-done.12.rest_11_
  27.1 1.1 collective-permute-done.8.rest_4_
  28.2 1.5 collective-permute-done.15.rest_12_
  29.7 0.0 collective-permute-done.5.other_ref
  29.7 0.0 copy-start
  29.7 1.2 copy-done
  30.9 2.4 %project.1 = bf16[256,256]{1,0:T(8,128)(2,1)S(1)} custom-call(s32[1]{0:T(128)} %bitcast.1.core_ref.half_ref, s32[1]{0:T(128)} %bitcast.2.place_ref, bf16[128,4096]{1,0:T(8,128)(2,1)S(1)} %copy-done, bf16[128,4096]{1,0:T(8,128)(2,1)S(1)} %collective-permute-done.5.other_ref, bf16[256,256]{1,0:T(8,128)(2,1)S(1)} %pad_maximum_fusion.rest_0_, ...), custom_call_target="tpu_custom_call" | custom-call | flops 536870912 | bytes 2097152 | tf_op jit(solution)/shard_map/project/pallas_call | solution.py:360
  33.3 3.3 %collective-permute-start.18 = (bf16[256,256]{1,0:T(8,128)(2,1)S(1)}, bf16[256,256]{1,0:T(8,128)(2,1)S(1)}, u32[]{:S(2)}, u32[]{:S(2)}) collective-permute-start(bf16[256,256]{1,0:T(8,128)(2,1)S(1)} %project.1), channel_id=1, source_target_pairs={{0,12},{1,13},{2,14},{3,15},{4,0},{5,1},{6,2},{7,3},{8,4},{9,5},{1... | collective-permute-start | bytes 393224 | tf_op jit(solution)/shard_map/ppermute | solution.py:408
  36.6 0.0 collective-permute-start.17
  36.6 0.5 collective-permute-start.16
  37.1 0.1 collective-permute-start.19
  37.2 1.3 collective-permute-done.18
  38.5 0.2 collective-permute-start.22
  38.7 9.2 %collective-permute-done.17 = bf16[256,256]{1,0:T(8,128)(2,1)S(1)} collective-permute-done((bf16[256,256]{1,0:T(8,128)(2,1)S(1)}, bf16[256,256]{1,0:T(8,128)(2,1)S(1)}, u32[]{:S(2)}, u32[]{:S(2)}) %collective-permute-start.17) | collective-permute-done | bytes 131104 | tf_op jit(solution)/shard_map/ppermute | solution.py:408
  47.9 0.1 collective-permute-start.21
  48.0 0.0 collective-permute-done.16
  48.0 1.4 collective-permute-start.20
  49.5 0.0 collective-permute-done.19
  49.5 4.5 %collective-permute-done.20 = bf16[256,256]{1,0:T(8,128)(2,1)S(1)} collective-permute-done((bf16[256,256]{1,0:T(8,128)(2,1)S(1)}, bf16[256,256]{1,0:T(8,128)(2,1)S(1)}, u32[]{:S(2)}, u32[]{:S(2)}) %collective-permute-start.20) | collective-permute-done | bytes 131104 | tf_op jit(solution)/shard_map/ppermute | solution.py:408
  54.0 0.0 collective-permute-done.21
  54.0 0.0 collective-permute-done.22
  54.0 2.8 %collective-permute-start.23 = (bf16[2048,256]{1,0:T(8,128)(2,1)S(1)}, bf16[2048,256]{1,0:T(8,128)(2,1)S(1)}, u32[]{:S(2)}, u32[]{:S(2)}) collective-permute-start(bf16[2048,256]{1,0:T(8,128)(2,1)S(1)} %constant_dynamic-update-slice_fusion.kv_ref), channel_id=1, source_target_pairs={{0,1},{1,0},{2,3},{3,2},{4,5},{5,4},{6,7},{7,6},{8,9},{9,8},{10,11... | collective-permute-start | bytes 3145736 | tf_op jit(solution)/shard_map/ppermute | solution.py:404
  56.8 0.0 copy-done.5
  56.8 0.0 copy-done.3
  56.8 0.0 copy-done.4
  56.8 0.0 copy-start.1
  56.9 2.1 %copy-done.1 = bf16[4,64,7424]{2,1,0:T(8,128)(2,1)S(1)} copy-done((bf16[4,64,7424]{2,1,0:T(8,128)(2,1)S(1)}, bf16[4,64,7424]{2,1,0:T(8,128)(2,1)}, u32[]{:S(2)}) %copy-start.1) | copy-done | bytes 3801112
  58.9 45.4 %attend.2.rest_0_ = bf16[4,64,7424]{2,1,0:T(8,128)(2,1)} custom-call(s32[1]{0:T(128)} %bitcast.1.core_ref.half_ref, s32[4,16]{1,0:T(4,128)S(1)} %fusion.6.start_ref, s32[4]{0:T(128)S(1)} %copy-done.4, bf16[4,64,7424]{2,1,0:T(8,128)(2,1)S(1)} %copy-done.1, bf16[2048,256]{1,0:T(8,128)(2,1)S(1)} %constant_dynamic-update-slice_fusion.kv_ref, ...), custom_call_target="tpu_custom_call" | custom-call | flops 2189426688 | bytes 3801088 | tf_op jit(solution)/shard_map/attend/pallas_call | solution.py:302
  104.3 0.0 collective-permute-done.23.kv_ref
  104.3 0.0 copy-done.2
  104.3 45.2 %attend.3 = bf16[4,64,7424]{2,1,0:T(8,128)(2,1)} custom-call(s32[1]{0:T(128)} %bitcast.half_ref, s32[4,16]{1,0:T(4,128)S(1)} %fusion.6.start_ref, s32[4]{0:T(128)S(1)} %copy-done.4, bf16[4,64,7424]{2,1,0:T(8,128)(2,1)S(1)} %copy-done.2, bf16[2048,256]{1,0:T(8,128)(2,1)S(1)} %collective-permute-done.23.kv_ref, ...), custom_call_target="tpu_custom_call", output_to_operand_aliasing={{}: (6, {})} | custom-call | flops 2189426688 | bytes 3801088 | tf_op jit(solution)/shard_map/attend/pallas_call | solution.py:302
  (12 shorter events, 0.1 us)
Async XLA Ops:
  1.0 3.0 %collective-permute-start.2 = (bf16[256,256]{1,0:T(8,128)(2,1)S(1)}, bf16[256,256]{1,0:T(8,128)(2,1)S(1)}, u32[]{:S(2)}, u32[]{:S(2)}) collective-permute-start(bf16[256,256]{1,0:T(8,128)(2,1)S(1)} %pad_maximum_fusion.1), channel_id=1, source_target_pairs={{0,1},{1,0},{2,3},{3,2},{4,5},{5,4},{6,7},{7,6},{8,9},{9,8},{10,11... | collective-permute-start | bytes 393224 | tf_op jit(solution)/shard_map/ppermute | solution.py:404
  1.1 10.4 %collective-permute-start.1 = (bf16[256,256]{1,0:T(8,128)(2,1)S(1)}, bf16[256,256]{1,0:T(8,128)(2,1)S(1)}, u32[]{:S(2)}, u32[]{:S(2)}) collective-permute-start(bf16[256,256]{1,0:T(8,128)(2,1)S(1)} %pad_maximum_fusion.rest_0_), channel_id=1, source_target_pairs={{0,2},{1,3},{2,6},{3,7},{4,0},{5,1},{6,10},{7,11},{8,4},{9,5},{10,... | collective-permute-start | bytes 393224 | tf_op jit(solution)/shard_map/ppermute | solution.py:408
  3.8 7.7 %collective-permute-start = (bf16[256,256]{1,0:T(8,128)(2,1)S(1)}, bf16[256,256]{1,0:T(8,128)(2,1)S(1)}, u32[]{:S(2)}, u32[]{:S(2)}) collective-permute-start(bf16[256,256]{1,0:T(8,128)(2,1)S(1)} %pad_maximum_fusion.rest_0_), channel_id=1, source_target_pairs={{0,4},{1,5},{2,0},{3,1},{4,8},{5,9},{6,2},{7,3},{8,12},{9,13},{10,... | collective-permute-start | bytes 393224 | tf_op jit(solution)/shard_map/ppermute | solution.py:408
  4.0 7.6 %collective-permute-start.4 = (bf16[256,256]{1,0:T(8,128)(2,1)S(1)}, bf16[256,256]{1,0:T(8,128)(2,1)S(1)}, u32[]{:S(2)}, u32[]{:S(2)}) collective-permute-start(bf16[256,256]{1,0:T(8,128)(2,1)S(1)} %collective-permute-done.2.rest_8_), channel_id=1, source_target_pairs={{0,2},{1,3},{2,6},{3,7},{4,0},{5,1},{6,10},{7,11},{8,4},{9,5},{10,... | collective-permute-start | bytes 393224 | tf_op jit(solution)/shard_map/ppermute | solution.py:408
  5.3 6.3 %collective-permute-start.3 = (bf16[256,256]{1,0:T(8,128)(2,1)S(1)}, bf16[256,256]{1,0:T(8,128)(2,1)S(1)}, u32[]{:S(2)}, u32[]{:S(2)}) collective-permute-start(bf16[256,256]{1,0:T(8,128)(2,1)S(1)} %collective-permute-done.2.rest_8_), channel_id=1, source_target_pairs={{0,4},{1,5},{2,0},{3,1},{4,8},{5,9},{6,2},{7,3},{8,12},{9,13},{10,... | collective-permute-start | bytes 393224 | tf_op jit(solution)/shard_map/ppermute | solution.py:408
  5.5 51.4 %copy-start.3 = (bf16[4,64,512]{2,1,0:T(8,128)(2,1)S(1)}, bf16[4,64,512]{2,1,0:T(8,128)(2,1)}, u32[]{:S(2)}) copy-start(bf16[4,64,512]{2,1,0:T(8,128)(2,1)} %own_kv_ref.3) | copy-start | bytes 786436
  11.5 45.3 %copy-start.5 = (s32[4,16]{1,0:T(4,128)S(1)}, s32[4,16]{1,0:T(4,128)}, u32[]{:S(2)}) copy-start(s32[4,16]{1,0:T(4,128)} %param.12) | copy-start | bytes 772
  11.6 45.3 %copy-start.4 = (s32[4]{0:T(128)S(1)}, s32[4]{0:T(128)}, u32[]{:S(2)}) copy-start(s32[4]{0:T(128)} %length_ref.3) | copy-start | bytes 52
  11.6 18.1 %collective-permute-start.5 = (bf16[128,4096]{1,0:T(8,128)(2,1)}, bf16[128,4096]{1,0:T(8,128)(2,1)S(1)}, u32[]{:S(2)}, u32[]{:S(2)}) collective-permute-start(bf16[128,4096]{1,0:T(8,128)(2,1)} %pool.1.own_hbm), channel_id=1, source_target_pairs={{0,1},{1,0},{2,3},{3,2},{4,5},{5,4},{6,7},{7,6},{8,9},{9,8},{10,11... | collective-permute-start | bytes 3145736 | tf_op jit(solution)/shard_map/ppermute | solution.py:404
  12.6 5.3 %collective-permute-start.6 = (bf16[256,256]{1,0:T(8,128)(2,1)S(1)}, bf16[256,256]{1,0:T(8,128)(2,1)S(1)}, u32[]{:S(2)}, u32[]{:S(2)}) collective-permute-start(bf16[256,256]{1,0:T(8,128)(2,1)S(1)} %collective-permute-done.rest_1_), channel_id=1, source_target_pairs={{0,4},{1,5},{2,0},{3,1},{4,8},{5,9},{6,2},{7,3},{8,12},{9,13},{10,... | collective-permute-start | bytes 393224 | tf_op jit(solution)/shard_map/ppermute | solution.py:408
  14.2 5.1 %collective-permute-start.13 = (bf16[256,256]{1,0:T(8,128)(2,1)S(1)}, bf16[256,256]{1,0:T(8,128)(2,1)S(1)}, u32[]{:S(2)}, u32[]{:S(2)}) collective-permute-start(bf16[256,256]{1,0:T(8,128)(2,1)S(1)} %collective-permute-done.4.rest_15_), channel_id=1, source_target_pairs={{0,2},{1,3},{2,6},{3,7},{4,0},{5,1},{6,10},{7,11},{8,4},{9,5},{10,... | collective-permute-start | bytes 393224 | tf_op jit(solution)/shard_map/ppermute | solution.py:408
  14.2 7.5 %collective-permute-start.9 = (bf16[256,256]{1,0:T(8,128)(2,1)S(1)}, bf16[256,256]{1,0:T(8,128)(2,1)S(1)}, u32[]{:S(2)}, u32[]{:S(2)}) collective-permute-start(bf16[256,256]{1,0:T(8,128)(2,1)S(1)} %collective-permute-done.1.rest_7_), channel_id=1, source_target_pairs={{0,2},{1,3},{2,6},{3,7},{4,0},{5,1},{6,10},{7,11},{8,4},{9,5},{10,... | collective-permute-start | bytes 393224 | tf_op jit(solution)/shard_map/ppermute | solution.py:408
  15.6 6.4 %collective-permute-start.11 = (bf16[256,256]{1,0:T(8,128)(2,1)S(1)}, bf16[256,256]{1,0:T(8,128)(2,1)S(1)}, u32[]{:S(2)}, u32[]{:S(2)}) collective-permute-start(bf16[256,256]{1,0:T(8,128)(2,1)S(1)} %collective-permute-done.3.rest_9_), channel_id=1, source_target_pairs={{0,4},{1,5},{2,0},{3,1},{4,8},{5,9},{6,2},{7,3},{8,12},{9,13},{10,... | collective-permute-start | bytes 393224 | tf_op jit(solution)/shard_map/ppermute | solution.py:408
  17.9 5.4 %collective-permute-start.7 = (bf16[256,256]{1,0:T(8,128)(2,1)S(1)}, bf16[256,256]{1,0:T(8,128)(2,1)S(1)}, u32[]{:S(2)}, u32[]{:S(2)}) collective-permute-start(bf16[256,256]{1,0:T(8,128)(2,1)S(1)} %collective-permute-done.6.rest_2_), channel_id=1, source_target_pairs={{0,4},{1,5},{2,0},{3,1},{4,8},{5,9},{6,2},{7,3},{8,12},{9,13},{10,... | collective-permute-start | bytes 393224 | tf_op jit(solution)/shard_map/ppermute | solution.py:408
  19.3 5.3 %collective-permute-start.14 = (bf16[256,256]{1,0:T(8,128)(2,1)S(1)}, bf16[256,256]{1,0:T(8,128)(2,1)S(1)}, u32[]{:S(2)}, u32[]{:S(2)}) collective-permute-start(bf16[256,256]{1,0:T(8,128)(2,1)S(1)} %collective-permute-done.13.rest_14_), channel_id=1, source_target_pairs={{0,2},{1,3},{2,6},{3,7},{4,0},{5,1},{6,10},{7,11},{8,4},{9,5},{10,... | collective-permute-start | bytes 393224 | tf_op jit(solution)/shard_map/ppermute | solution.py:408
  21.8 5.3 %collective-permute-start.10 = (bf16[256,256]{1,0:T(8,128)(2,1)S(1)}, bf16[256,256]{1,0:T(8,128)(2,1)S(1)}, u32[]{:S(2)}, u32[]{:S(2)}) collective-permute-start(bf16[256,256]{1,0:T(8,128)(2,1)S(1)} %collective-permute-done.9.rest_6_), channel_id=1, source_target_pairs={{0,2},{1,3},{2,6},{3,7},{4,0},{5,1},{6,10},{7,11},{8,4},{9,5},{10,... | collective-permute-start | bytes 393224 | tf_op jit(solution)/shard_map/ppermute | solution.py:408
  22.0 5.1 %collective-permute-start.12 = (bf16[256,256]{1,0:T(8,128)(2,1)S(1)}, bf16[256,256]{1,0:T(8,128)(2,1)S(1)}, u32[]{:S(2)}, u32[]{:S(2)}) collective-permute-start(bf16[256,256]{1,0:T(8,128)(2,1)S(1)} %collective-permute-done.11.rest_10_), channel_id=1, source_target_pairs={{0,4},{1,5},{2,0},{3,1},{4,8},{5,9},{6,2},{7,3},{8,12},{9,13},{10,... | collective-permute-start | bytes 393224 | tf_op jit(solution)/shard_map/ppermute | solution.py:408
  23.3 4.9 %collective-permute-start.8 = (bf16[256,256]{1,0:T(8,128)(2,1)S(1)}, bf16[256,256]{1,0:T(8,128)(2,1)S(1)}, u32[]{:S(2)}, u32[]{:S(2)}) collective-permute-start(bf16[256,256]{1,0:T(8,128)(2,1)S(1)} %collective-permute-done.7.rest_3_), channel_id=1, source_target_pairs={{0,4},{1,5},{2,0},{3,1},{4,8},{5,9},{6,2},{7,3},{8,12},{9,13},{10,... | collective-permute-start | bytes 393224 | tf_op jit(solution)/shard_map/ppermute | solution.py:408
  24.5 5.1 %collective-permute-start.15 = (bf16[256,256]{1,0:T(8,128)(2,1)S(1)}, bf16[256,256]{1,0:T(8,128)(2,1)S(1)}, u32[]{:S(2)}, u32[]{:S(2)}) collective-permute-start(bf16[256,256]{1,0:T(8,128)(2,1)S(1)} %collective-permute-done.14.rest_13_), channel_id=1, source_target_pairs={{0,2},{1,3},{2,6},{3,7},{4,0},{5,1},{6,10},{7,11},{8,4},{9,5},{10,... | collective-permute-start | bytes 393224 | tf_op jit(solution)/shard_map/ppermute | solution.py:408
  29.7 1.2 copy-start
  33.3 5.2 %collective-permute-start.18 = (bf16[256,256]{1,0:T(8,128)(2,1)S(1)}, bf16[256,256]{1,0:T(8,128)(2,1)S(1)}, u32[]{:S(2)}, u32[]{:S(2)}) collective-permute-start(bf16[256,256]{1,0:T(8,128)(2,1)S(1)} %project.1), channel_id=1, source_target_pairs={{0,12},{1,13},{2,14},{3,15},{4,0},{5,1},{6,2},{7,3},{8,4},{9,5},{1... | collective-permute-start | bytes 393224 | tf_op jit(solution)/shard_map/ppermute | solution.py:408
  36.6 11.4 %collective-permute-start.17 = (bf16[256,256]{1,0:T(8,128)(2,1)S(1)}, bf16[256,256]{1,0:T(8,128)(2,1)S(1)}, u32[]{:S(2)}, u32[]{:S(2)}) collective-permute-start(bf16[256,256]{1,0:T(8,128)(2,1)S(1)} %project.1), channel_id=1, source_target_pairs={{0,8},{1,9},{2,10},{3,11},{4,12},{5,13},{6,14},{7,15},{8,0},{9,1},... | collective-permute-start | bytes 393224 | tf_op jit(solution)/shard_map/ppermute | solution.py:408
  36.6 11.5 %collective-permute-start.16 = (bf16[256,256]{1,0:T(8,128)(2,1)S(1)}, bf16[256,256]{1,0:T(8,128)(2,1)S(1)}, u32[]{:S(2)}, u32[]{:S(2)}) collective-permute-start(bf16[256,256]{1,0:T(8,128)(2,1)S(1)} %project.1), channel_id=1, source_target_pairs={{0,4},{1,5},{2,6},{3,7},{4,8},{5,9},{6,10},{7,11},{8,12},{9,13},{1... | collective-permute-start | bytes 393224 | tf_op jit(solution)/shard_map/ppermute | solution.py:408
  37.1 12.3 %collective-permute-start.19 = (bf16[256,256]{1,0:T(8,128)(2,1)S(1)}, bf16[256,256]{1,0:T(8,128)(2,1)S(1)}, u32[]{:S(2)}, u32[]{:S(2)}) collective-permute-start(bf16[256,256]{1,0:T(8,128)(2,1)S(1)} %project.1), channel_id=1, source_target_pairs={{0,2},{1,3},{2,0},{3,1},{4,6},{5,7},{6,4},{7,5},{8,10},{9,11},{10,... | collective-permute-start | bytes 393224 | tf_op jit(solution)/shard_map/ppermute | solution.py:408
  38.5 15.5 %collective-permute-start.22 = (bf16[256,256]{1,0:T(8,128)(2,1)S(1)}, bf16[256,256]{1,0:T(8,128)(2,1)S(1)}, u32[]{:S(2)}, u32[]{:S(2)}) collective-permute-start(bf16[256,256]{1,0:T(8,128)(2,1)S(1)} %collective-permute-done.18), channel_id=1, source_target_pairs={{0,2},{1,3},{2,0},{3,1},{4,6},{5,7},{6,4},{7,5},{8,10},{9,11},{10,... | collective-permute-start | bytes 393224 | tf_op jit(solution)/shard_map/ppermute | solution.py:408
  47.9 6.0 %collective-permute-start.21 = (bf16[256,256]{1,0:T(8,128)(2,1)S(1)}, bf16[256,256]{1,0:T(8,128)(2,1)S(1)}, u32[]{:S(2)}, u32[]{:S(2)}) collective-permute-start(bf16[256,256]{1,0:T(8,128)(2,1)S(1)} %collective-permute-done.17), channel_id=1, source_target_pairs={{0,2},{1,3},{2,0},{3,1},{4,6},{5,7},{6,4},{7,5},{8,10},{9,11},{10,... | collective-permute-start | bytes 393224 | tf_op jit(solution)/shard_map/ppermute | solution.py:408
  48.0 5.9 %collective-permute-start.20 = (bf16[256,256]{1,0:T(8,128)(2,1)S(1)}, bf16[256,256]{1,0:T(8,128)(2,1)S(1)}, u32[]{:S(2)}, u32[]{:S(2)}) collective-permute-start(bf16[256,256]{1,0:T(8,128)(2,1)S(1)} %collective-permute-done.16), channel_id=1, source_target_pairs={{0,2},{1,3},{2,0},{3,1},{4,6},{5,7},{6,4},{7,5},{8,10},{9,11},{10,... | collective-permute-start | bytes 393224 | tf_op jit(solution)/shard_map/ppermute | solution.py:408
  54.0 50.2 %collective-permute-start.23 = (bf16[2048,256]{1,0:T(8,128)(2,1)S(1)}, bf16[2048,256]{1,0:T(8,128)(2,1)S(1)}, u32[]{:S(2)}, u32[]{:S(2)}) collective-permute-start(bf16[2048,256]{1,0:T(8,128)(2,1)S(1)} %constant_dynamic-update-slice_fusion.kv_ref), channel_id=1, source_target_pairs={{0,1},{1,0},{2,3},{3,2},{4,5},{5,4},{6,7},{7,6},{8,9},{9,8},{10,11... | collective-permute-start | bytes 3145736 | tf_op jit(solution)/shard_map/ppermute | solution.py:404
  56.8 2.1 %copy-start.1 = (bf16[4,64,7424]{2,1,0:T(8,128)(2,1)S(1)}, bf16[4,64,7424]{2,1,0:T(8,128)(2,1)}, u32[]{:S(2)}) copy-start(bf16[4,64,7424]{2,1,0:T(8,128)(2,1)} %q_hbm.3) | copy-start | bytes 11403268
  58.9 45.4 %copy-start.2 = (bf16[4,64,7424]{2,1,0:T(8,128)(2,1)S(1)}, bf16[4,64,7424]{2,1,0:T(8,128)(2,1)}, u32[]{:S(2)}) copy-start(bf16[4,64,7424]{2,1,0:T(8,128)(2,1)} %q_hbm.3) | copy-start | bytes 11403268

commit v10 on v9

--- a/solution.py
+++ b/solution.py
@@ -29,6 +29,7 @@
 NEG = -1e30
 SUM_LOW, SUM_HIGH = 2.0 ** -40, 2.0 ** 60
 POOL_WIDTH = 1024
+POOL_CALLS = 2
 CHIP = 8
 STEP = 8
 BLOCK = 16
@@ -46,8 +47,8 @@
     return 2 * line + lane
 
 
-def pool_kernel(states_hbm, queries_hbm, gain_hbm, out_ref, states, queries, gain, pooled, arrived):
-    passages = states_hbm.shape[0]
+def pool_kernel(first, states_hbm, queries_hbm, gain_hbm, out_ref, states, queries, gain, pooled, arrived):
+    passages = states.shape[1]
     two = 2 * CHD
     groups = D // POOL_WIDTH
     small = [
@@ -56,7 +57,9 @@
     ]
     large = [
         pltpu.make_async_copy(
-            states_hbm.at[:, :, pl.ds(j * POOL_WIDTH, POOL_WIDTH)], states.at[j], arrived.at[j]
+            states_hbm.at[pl.ds(first, passages), :, pl.ds(j * POOL_WIDTH, POOL_WIDTH)],
+            states.at[j],
+            arrived.at[j],
         )
         for j in range(groups)
     ]
@@ -106,12 +109,11 @@
     out_ref[...] = (pooled[...] * scale * factor).astype(jnp.bfloat16)
 
 
-def pool(states, queries, gain):
-    count = states.shape[0]
+def pool(states, queries, gain, first, count):
     groups = D // POOL_WIDTH
     hbm = pl.BlockSpec(memory_space=pltpu.HBM)
     return pl.pallas_call(
-        pool_kernel,
+        functools.partial(pool_kernel, first),
         in_specs=[hbm] * 3,
         out_specs=pl.BlockSpec(memory_space=pltpu.VMEM),
         out_shape=jax.ShapeDtypeStruct((count * MEM, D), jnp.bfloat16),
@@ -172,11 +174,11 @@
     def answer(query, carry):
         for slot in range(TOPK):
             start = pl.multiple_of(start_ref[query, slot], MEM)
-            memory[slot * MEM:(slot + 1) * MEM, :] = kv_ref[pl.ds(start, MEM), :].astype(jnp.float32)
+            memory[slot * MEM:(slot + 1) * MEM, :] = kv_ref[pl.ds(start, MEM), :]
         length = length_ref[query]
 
-        turned = jnp.transpose(memory[:, :LANES]).astype(jnp.bfloat16)
-        own_k = own_kv_ref[query, :, pl.ds(own_at, LANES)].astype(jnp.float32)
+        turned = jnp.transpose(memory[:, :LANES])
+        own_k = own_kv_ref[query, :, pl.ds(own_at, LANES)]
         own_turned = jnp.transpose(jnp.concatenate([own_k, own_k], axis=0))
         column = lax.broadcasted_iota(jnp.int32, (HD, LANES), 1)
         for g in range(2):
@@ -185,13 +187,14 @@
                 key_side[g, rows, member * ROWS:(member + 1) * ROWS] = turned[g * HD:(g + 1) * HD]
                 own = own_turned[g * HD:(g + 1) * HD]
                 mine = (column >= HD) if member else (column < HD)
-                key_side[g, rows, 2 * ROWS:] = jnp.where(mine, own, 0.0).astype(jnp.bfloat16)
+                key_side[g, rows, 2 * ROWS:] = jnp.where(mine, own, jnp.zeros_like(own))
 
         token = lax.broadcasted_iota(jnp.int32, (QLEN, LANES), 0)
         low = lax.broadcasted_iota(jnp.int32, (QLEN, LANES), 1) < HD
         key = lax.rem(lax.broadcasted_iota(jnp.int32, (QLEN, LANES), 1), HD)
         bias[...] = jnp.where((key <= token) & (key < length), 0.0, NEG)
         alive = token < length
+        sample = lax.div(key, HD // STEP)
         fetch(query).wait()
 
         def stacked(tiles):
@@ -211,8 +214,10 @@
             g, tiles = chunks[i]
             for n, t in enumerate(tiles):
                 rows = slice(n * QLEN, (n + 1) * QLEN)
-                result = jnp.where(alive, mixed[rows, :LANES] / mixed[rows, LANES:], 0.0)
-                result = result.astype(jnp.bfloat16)
+                sums = mixed[rows, LANES:]
+                inverse = pl.reciprocal(sums, approx=True)
+                inverse = inverse * (2.0 - sums * inverse)
+                result = jnp.where(alive, mixed[rows, :LANES] * inverse, 0.0).astype(jnp.bfloat16)
                 at = slice(t * LANES, (t + 1) * LANES)
                 if t == half and g == 1:
                     result = jnp.where(low, answers[query, :, at], result)
@@ -222,26 +227,26 @@
             g, tiles = chunks[i]
             size = len(tiles) * QLEN
             mixed = jnp.dot(weights[i % 2, :size, :], value_side[g], preferred_element_type=jnp.float32)
-            for at in range(0, size, QLEN):
-                sums = mixed[at:at + QLEN, LANES:]
-                seen = jnp.where((sums > SUM_LOW) & (sums < SUM_HIGH), seen, 1.0)
+            sums = mixed[:QLEN, LANES:]
+            for n in range(1, len(tiles)):
+                sums = jnp.where(sample == n, mixed[n * QLEN:(n + 1) * QLEN, LANES:], sums)
+            seen = jnp.where((sums > SUM_LOW) & (sums < SUM_HIGH), seen, 1.0)
             finish(i, mixed)
             return seen
 
         key_product(0)
 
         own_v_at = pl.multiple_of(own_at + KVH * HD, LANES)
-        own_v = own_kv_ref[query, :, pl.ds(own_v_at, LANES)].astype(jnp.float32)
+        own_v = own_kv_ref[query, :, pl.ds(own_v_at, LANES)]
         for block, at in ((memory[:, LANES:], 0), (own_v, 2 * ROWS)):
             size = block.shape[0]
-            swapped = pltpu.roll(block, HD, 1)
+            swapped = jnp.concatenate([block[:, HD:], block[:, :HD]], axis=1)
             lower = lax.broadcasted_iota(jnp.int32, block.shape, 1) < HD
+            zero = jnp.zeros_like(block)
             for g in range(2):
                 one, two = (block, swapped) if g == 0 else (swapped, block)
-                value_side[g, at:at + size, :LANES] = jnp.where(lower, one, 0.0).astype(jnp.bfloat16)
-                value_side[g, at + size:at + 2 * size, :LANES] = jnp.where(lower, 0.0, two).astype(
-                    jnp.bfloat16
-                )
+                value_side[g, at:at + size, :LANES] = jnp.where(lower, one, zero)
+                value_side[g, at + size:at + 2 * size, :LANES] = jnp.where(lower, zero, two)
 
         seen = jnp.zeros((QLEN, LANES), jnp.float32)
         for i in range(len(chunks)):
@@ -307,7 +312,7 @@
         scratch_shapes=[
             pltpu.VMEM((count, QLEN, HALF), jnp.bfloat16),
             pltpu.VMEM((count, QLEN, HALF), jnp.bfloat16),
-            pltpu.VMEM((ROWS, 2 * LANES), jnp.float32),
+            pltpu.VMEM((ROWS, 2 * LANES), jnp.bfloat16),
             pltpu.VMEM((2, LANES, KEYS), jnp.bfloat16),
             pltpu.VMEM((2, KEYS, 2 * LANES), jnp.bfloat16),
             pltpu.VMEM((2, STEP * QLEN, KEYS), jnp.bfloat16),
@@ -319,7 +324,7 @@
             pltpu.SemaphoreType.DMA((count,)),
         ],
         input_output_aliases=aliases,
-        compiler_params=pltpu.CompilerParams(vmem_limit_bytes=40 * MIB),
+        compiler_params=pltpu.CompilerParams(vmem_limit_bytes=50 * MIB),
         cost_estimate=pl.CostEstimate(
             flops=2 * count * QLEN * H * HD * (ROWS + QLEN),
             bytes_accessed=2 * count * QLEN * H * HD,
@@ -329,23 +334,17 @@
     )(*operands)
 
 
-def project_kernel(ring, core_ref, place_ref, own_hbm, other_ref, *rest):
-    weights, (out_ref, own, arrived) = rest[:-3], rest[-3:]
-    count = own.shape[0]
+def project_kernel(ring, parts, core_ref, place_ref, *rest):
+    row_refs, weights, out_ref = rest[:2 * parts], rest[2 * parts:-1], rest[-1]
+    count = parts * row_refs[0].shape[0]
     depth = weights[0].shape[0]
+    total = jnp.zeros((2 * count, weights[0].shape[1]), jnp.float32)
     core = core_ref[0]
-    pieces = []
     for n, weight in enumerate(weights):
         part, i = n // ring, n % ring
         chip = chip_at(lax.rem(ring + place_ref[0] - i, ring), ring)
-        columns = pl.ds(pl.multiple_of((2 * chip + (1 - core if part else core)) * depth, depth), depth)
-        copy = pltpu.make_async_copy(own_hbm.at[:, columns], own.at[:, columns], arrived.at[n])
-        copy.start()
-        pieces.append((weight, columns, copy))
-    total = jnp.zeros((2 * count, weights[0].shape[1]), jnp.float32)
-    for weight, columns, copy in pieces:
-        copy.wait()
-        rows = jnp.concatenate([own[:, columns], other_ref[:, columns]], axis=0)
+        at = pl.multiple_of((2 * chip + (1 - core if part else core)) * depth, depth)
+        rows = jnp.concatenate([x[:, pl.ds(at, depth)] for x in row_refs], axis=0)
         total += jnp.dot(rows, weight[...], preferred_element_type=jnp.float32)
     result = total.astype(jnp.bfloat16)
     out_ref[pl.ds(pl.multiple_of(core * count, count), count)] = result[:count]
@@ -353,22 +352,21 @@
 
 
 def project(core, place, own_rows, other_rows, weights):
-    count = own_rows.shape[0]
+    count = len(own_rows) * own_rows[0].shape[0]
     width = weights[0].shape[1]
     vmem = pl.BlockSpec(memory_space=pltpu.VMEM)
     smem = pl.BlockSpec(memory_space=pltpu.SMEM)
     return pl.pallas_call(
-        functools.partial(project_kernel, len(weights) // 2),
-        in_specs=[smem, smem, pl.BlockSpec(memory_space=pltpu.HBM)] + [vmem] * (1 + len(weights)),
+        functools.partial(project_kernel, len(weights) // 2, len(own_rows)),
+        in_specs=[smem, smem] + [vmem] * (2 * len(own_rows) + len(weights)),
         out_specs=vmem,
-        scratch_shapes=[pltpu.VMEM(own_rows.shape, jnp.bfloat16), pltpu.SemaphoreType.DMA((len(weights),))],
         out_shape=jax.ShapeDtypeStruct((2 * count, width), jnp.bfloat16),
         compiler_params=pltpu.CompilerParams(vmem_limit_bytes=16 * MIB),
         cost_estimate=pl.CostEstimate(
             flops=4 * count * D * width, bytes_accessed=2 * D * width, transcendentals=0
         ),
         name="project",
-    )(core.reshape(1), place, own_rows, other_rows, *weights)
+    )(core.reshape(1), place, *own_rows, *other_rows, *weights)
 
 
 def local(
@@ -386,9 +384,10 @@
     core, chip = me & 1, lax.div(me, 2)
     chips = extent // 2
     depth = kv_weight.shape[0]
+    own_count = passage_states.shape[0]
 
     if chips != 8 or depth % LANES:
-        memory_rows = pool(passage_states, memory_queries, memory_gain)
+        memory_rows = pool(passage_states, memory_queries, memory_gain, 0, own_count)
         whole_weight = lax.all_gather(kv_weight, "pass", axis=0, tiled=True)
         memory_kv = jnp.dot(memory_rows, whole_weight, preferred_element_type=jnp.float32)
         everything = lax.all_gather(memory_kv.astype(jnp.bfloat16), "pass", axis=0, tiled=True)
@@ -409,14 +408,6 @@
 
     def along_ring(x, step):
         return along(x, lambda line, lane: order[(order.index(2 * line + lane) + step) % chips])
-
-    def round_the_ring(x, up, down, rounds):
-        up, down = [x, up], [down]
-        while len(up) <= rounds:
-            up.append(along_ring(up[-1], 1))
-        while len(up) + len(down) < chips:
-            down.append(along_ring(down[-1], -1))
-        return up + down[::-1]
 
     def line_by_line(block):
         lines = chips // 2
@@ -434,13 +425,24 @@
             axis=1,
         )
 
-    pieces = [columns(core), to_partner(columns(1 - core))]
-    hops = [along_ring(x, step) for x in pieces for step in (1, -1)]
-    memory_rows = pool(passage_states, memory_queries, memory_gain)
-    *hops, memory_rows = lax.optimization_barrier((*hops, memory_rows))
-    weights = round_the_ring(pieces[0], hops[0], hops[1], chips // 2)
-    weights += round_the_ring(pieces[1], hops[2], hops[3], chips // 2 - 1)
-    memory_kv = project(core, place, memory_rows, to_partner(memory_rows), weights)
+    up = [[columns(core)], [to_partner(columns(1 - core))]]
+    down = [[x[0]] for x in up]
+    memory_rows = []
+    for turn in range(1, chips // 2):
+        for piece in range(2):
+            up[piece].append(along_ring(up[piece][-1], 1))
+            down[piece].append(along_ring(down[piece][-1], -1))
+        if turn <= POOL_CALLS:
+            part = own_count // POOL_CALLS
+            rows = pool(passage_states, memory_queries, memory_gain, (turn - 1) * part, part)
+            *hops, rows = lax.optimization_barrier((*(x[-1] for x in up + down), rows))
+            for chain, hop in zip(up + down, hops):
+                chain[-1] = hop
+            memory_rows.append(rows)
+    up[0].append(along_ring(up[0][-1], 1))
+    down[1].append(along_ring(down[1][-1], -1))
+    weights = [x for piece in range(2) for x in up[piece] + down[piece][:0:-1]]
+    memory_kv = project(core, place, memory_rows, [to_partner(x) for x in memory_rows], weights)
     near = jnp.concatenate(line_by_line(memory_kv), axis=0)
     far = to_partner(near)
 

time: 150 us -> 153 us (1.020)
  Pallas kernels: 99 us -> 102 us
  starting transfers between devices: 21.3 us -> 24.3 us
  waiting for transfers between devices: 24.6 us -> 22.8 us
    pallas_call x2 -> x3, Pallas kernels: 8.44 us -> 11.1 us  [the longest x2 9.46 us: pool(): pl.pallas_call(functools.partial(pool_kernel, first), in_specs=[hbm] * 3,...]
    ppermute x3 -> x4, starting transfers between devices: 3.84 us -> 5.91 us  [to_partner(): return lax.ppermute(x, 'pass', [(i, i ^ 1) for i in range(extent)])]
    ppermute x21, waiting for transfers between devices: 24.6 us -> 22.8 us  [along(): lax.ppermute(x, 'pass', [(2 * s + c, 2 * d + c) for s, d in pairs for c i...]
  transfers between devices with their start and end apart: 24 -> 25, of which waited for: 8 -> 10; matrix products, arithmetic and copies ran while one was open for 0% -> 0% of each run, Pallas kernels for 34% -> 36%
where the time goes in v10:
time: 153 us
  Pallas kernels  102 us (67%)
  starting transfers between devices  24.3 us (16%)
  waiting for transfers between devices  22.8 us (15%)
  local copies, waits for them, and re-layouts  3.05 us (2%)
    pallas_call x2, Pallas kernels, attend(): pl.pallas_call(attend_kernel, in_specs=in_specs, out_specs=hbm, out_shape...  91.2 us
    ppermute x21, waiting for transfers between devices, along(): lax.ppermute(x, 'pass', [(2 * s + c, 2 * d + c) for s, d in pairs for c i...  22.8 us
    ppermute x21, starting transfers between devices, along(): lax.ppermute(x, 'pass', [(2 * s + c, 2 * d + c) for s, d in pairs for c i...  18.4 us
    pallas_call x2, Pallas kernels, pool(): pl.pallas_call(functools.partial(pool_kernel, first), in_specs=[hbm] * 3,...  9.46 us
    ppermute x4, starting transfers between devices, to_partner(): return lax.ppermute(x, 'pass', [(i, i ^ 1) for i in range(extent)])  5.91 us
  transfers between devices with their start and end apart: 25, of which 10 were waited for; matrix products, arithmetic and copies ran while one was open for 0% of the time, Pallas kernels for 36%

profile of v10, /device:TPU:1, one launch (start us, length us, event | category | flops | bytes accessed | tf_op | source)
XLA Modules:
  0.0 152.9 jit_solution(10958407794058461900)
XLA Ops:
  0.0 1.0 constant_dynamic-slice_fusion.1
  1.0 0.1 collective-permute-start.1
  1.1 2.7 %collective-permute-start.3 = (bf16[256,256]{1,0:T(8,128)(2,1)S(1)}, bf16[256,256]{1,0:T(8,128)(2,1)S(1)}, u32[]{:S(2)}, u32[]{:S(2)}) collective-permute-start(bf16[256,256]{1,0:T(8,128)(2,1)S(1)} %pad_maximum_fusion.rest_4_), channel_id=1, source_target_pairs={{0,2},{1,3},{2,6},{3,7},{4,0},{5,1},{6,10},{7,11},{8,4},{9,5},{10,... | collective-permute-start | bytes 393224 | tf_op jit(solution)/shard_map/ppermute | solution.py:407
  3.8 0.2 collective-permute-start
  4.0 0.0 collective-permute-done.1.rest_12_
  4.0 1.3 collective-permute-start.4
  5.3 0.2 collective-permute-start.2
  5.5 4.7 %pool.2.rest_0_ = bf16[64,4096]{1,0:T(8,128)(2,1)} custom-call(bf16[4,128,4096]{2,1,0:T(8,128)(2,1)} %states_hbm.3, bf16[32,4096]{1,0:T(8,128)(2,1)} %queries_hbm.3, bf16[4096]{0:T(1024)(128)(2,1)} %gain_hbm.3), custom_call_target="tpu_custom_call" | custom-call | flops 134217728 | bytes 2097152 | tf_op jit(solution)/shard_map/pool/pallas_call | solution.py:115
  10.2 0.0 copy-start
  10.2 0.0 collective-permute-done.3.rest_11_
  10.2 0.0 collective-permute-done.rest_5_
  10.2 0.4 collective-permute-done.4.rest_19_
  10.6 0.9 collective-permute-done.2.rest_13_
  11.4 0.5 collective-permute-start.5
  11.9 1.2 collective-permute-start.6
  13.1 0.2 collective-permute-start.7
  13.4 1.0 collective-permute-start.8
  14.4 4.7 %pool.3.rest_1_ = bf16[64,4096]{1,0:T(8,128)(2,1)} custom-call(bf16[4,128,4096]{2,1,0:T(8,128)(2,1)} %states_hbm.3, bf16[32,4096]{1,0:T(8,128)(2,1)} %queries_hbm.3, bf16[4096]{0:T(1024)(128)(2,1)} %gain_hbm.3), custom_call_target="tpu_custom_call" | custom-call | flops 134217728 | bytes 2097152 | tf_op jit(solution)/shard_map/pool/pallas_call | solution.py:115
  19.1 0.0 copy-done
  19.1 0.0 copy-start.5
  19.1 0.0 copy-start.4
  19.2 2.3 %collective-permute-start.9 = (bf16[64,4096]{1,0:T(8,128)(2,1)S(1)}, bf16[64,4096]{1,0:T(8,128)(2,1)S(1)}, u32[]{:S(2)}, u32[]{:S(2)}) collective-permute-start(bf16[64,4096]{1,0:T(8,128)(2,1)S(1)} %copy-done), channel_id=1, source_target_pairs={{0,1},{1,0},{2,3},{3,2},{4,5},{5,4},{6,7},{7,6},{8,9},{9,8},{10,11... | collective-permute-start | bytes 1572872 | tf_op jit(solution)/shard_map/ppermute | solution.py:403
  21.5 0.0 collective-permute-done.5.rest_6_
  21.5 0.0 collective-permute-done.6.rest_14_
  21.5 0.0 collective-permute-done.7.rest_10_
  21.5 0.0 collective-permute-done.8.rest_18_
  21.5 0.4 collective-permute-start.10
  21.9 1.3 collective-permute-start.11
  23.2 0.2 collective-permute-start.13
  23.3 1.0 collective-permute-start.15
  24.4 2.4 %collective-permute-done.11.rest_7_ = bf16[256,256]{1,0:T(8,128)(2,1)S(1)} collective-permute-done((bf16[256,256]{1,0:T(8,128)(2,1)S(1)}, bf16[256,256]{1,0:T(8,128)(2,1)S(1)}, u32[]{:S(2)}, u32[]{:S(2)}) %collective-permute-start.11) | collective-permute-done | bytes 131104 | tf_op jit(solution)/shard_map/ppermute | solution.py:407
  26.8 1.5 collective-permute-start.14
  28.3 0.0 collective-permute-done.13.rest_9_
  28.3 1.2 collective-permute-start.12
  29.5 1.3 collective-permute-done.15.rest_17_
  30.8 0.0 collective-permute-start.16
  30.8 0.1 collective-permute-done.14.rest_15_
  30.9 2.9 %collective-permute-done.12.rest_8_ = bf16[256,256]{1,0:T(8,128)(2,1)S(1)} collective-permute-done((bf16[256,256]{1,0:T(8,128)(2,1)S(1)}, bf16[256,256]{1,0:T(8,128)(2,1)S(1)}, u32[]{:S(2)}, u32[]{:S(2)}) %collective-permute-start.12) | collective-permute-done | bytes 131104 | tf_op jit(solution)/shard_map/ppermute | solution.py:407
  33.8 1.1 collective-permute-done.16.rest_16_
  34.9 0.0 collective-permute-done.9.rest_2_
  34.9 0.0 collective-permute-done.10.rest_3_
  34.9 1.0 copy-done.1
  36.0 1.6 %project.1 = bf16[256,256]{1,0:T(8,128)(2,1)S(1)} custom-call(s32[1]{0:T(128)} %bitcast.1.core_ref.half_ref, s32[1]{0:T(128)} %bitcast.2.place_ref, bf16[64,4096]{1,0:T(8,128)(2,1)S(1)} %copy-done, bf16[64,4096]{1,0:T(8,128)(2,1)S(1)} %copy-done.1, bf16[64,4096]{1,0:T(8,128)(2,1)S(1)} %collective-permute-done.9.rest_2_, ...), custom_call_target="tpu_custom_call" | custom-call | flops 536870912 | bytes 2097152 | tf_op jit(solution)/shard_map/project/pallas_call | solution.py:359
  37.6 2.4 %collective-permute-start.19 = (bf16[256,256]{1,0:T(8,128)(2,1)S(1)}, bf16[256,256]{1,0:T(8,128)(2,1)S(1)}, u32[]{:S(2)}, u32[]{:S(2)}) collective-permute-start(bf16[256,256]{1,0:T(8,128)(2,1)S(1)} %project.1), channel_id=1, source_target_pairs={{0,12},{1,13},{2,14},{3,15},{4,0},{5,1},{6,2},{7,3},{8,4},{9,5},{1... | collective-permute-start | bytes 393224 | tf_op jit(solution)/shard_map/ppermute | solution.py:407
  40.0 0.1 collective-permute-start.18
  40.0 1.1 collective-permute-start.17
  41.2 0.0 collective-permute-start.20
  41.2 0.7 collective-permute-done.19
  41.9 0.8 collective-permute-start.23
  42.7 8.9 %collective-permute-done.18 = bf16[256,256]{1,0:T(8,128)(2,1)S(1)} collective-permute-done((bf16[256,256]{1,0:T(8,128)(2,1)S(1)}, bf16[256,256]{1,0:T(8,128)(2,1)S(1)}, u32[]{:S(2)}, u32[]{:S(2)}) %collective-permute-start.18) | collective-permute-done | bytes 131104 | tf_op jit(solution)/shard_map/ppermute | solution.py:407
  51.7 0.0 collective-permute-start.22
  51.7 0.0 collective-permute-done.17
  51.7 1.5 collective-permute-start.21
  53.2 0.0 collective-permute-done.20
  53.2 4.1 %collective-permute-done.21 = bf16[256,256]{1,0:T(8,128)(2,1)S(1)} collective-permute-done((bf16[256,256]{1,0:T(8,128)(2,1)S(1)}, bf16[256,256]{1,0:T(8,128)(2,1)S(1)}, u32[]{:S(2)}, u32[]{:S(2)}) %collective-permute-start.21) | collective-permute-done | bytes 131104 | tf_op jit(solution)/shard_map/ppermute | solution.py:407
  57.4 0.0 collective-permute-done.22
  57.4 0.0 collective-permute-done.23
  57.4 3.1 %collective-permute-start.24 = (bf16[2048,256]{1,0:T(8,128)(2,1)S(1)}, bf16[2048,256]{1,0:T(8,128)(2,1)S(1)}, u32[]{:S(2)}, u32[]{:S(2)}) collective-permute-start(bf16[2048,256]{1,0:T(8,128)(2,1)S(1)} %constant_dynamic-update-slice_fusion.kv_ref), channel_id=1, source_target_pairs={{0,1},{1,0},{2,3},{3,2},{4,5},{5,4},{6,7},{7,6},{8,9},{9,8},{10,11... | collective-permute-start | bytes 3145736 | tf_op jit(solution)/shard_map/ppermute | solution.py:403
  60.5 0.0 copy-done.5
  60.5 0.0 copy-start.2
  60.6 0.9 copy-done.2
  61.5 45.6 %attend.2.rest_0_ = bf16[4,64,7424]{2,1,0:T(8,128)(2,1)} custom-call(s32[1]{0:T(128)} %bitcast.1.core_ref.half_ref, s32[4,16]{1,0:T(4,128)S(1)} %fusion.6.start_ref, s32[4]{0:T(128)S(1)} %copy-done.4, bf16[4,64,7424]{2,1,0:T(8,128)(2,1)} %q_hbm.3, bf16[2048,256]{1,0:T(8,128)(2,1)S(1)} %constant_dynamic-update-slice_fusion.kv_ref, ...), custom_call_target="tpu_custom_call" | custom-call | flops 2189426688 | bytes 3801088 | tf_op jit(solution)/shard_map/attend/pallas_call | solution.py:307
  107.1 0.0 collective-permute-done.24.kv_ref
  107.1 45.6 %attend.3 = bf16[4,64,7424]{2,1,0:T(8,128)(2,1)} custom-call(s32[1]{0:T(128)} %bitcast.half_ref, s32[4,16]{1,0:T(4,128)S(1)} %fusion.6.start_ref, s32[4]{0:T(128)S(1)} %copy-done.4, bf16[4,64,7424]{2,1,0:T(8,128)(2,1)} %q_hbm.3, bf16[2048,256]{1,0:T(8,128)(2,1)S(1)} %collective-permute-done.24.kv_ref, ...), custom_call_target="tpu_custom_call", output_to_operand_aliasing={{}: (6, {})} | custom-call | flops 2189426688 | bytes 3801088 | tf_op jit(solution)/shard_map/attend/pallas_call | solution.py:307
  (15 shorter events, 0.1 us)
Async XLA Ops:
  1.0 3.0 %collective-permute-start.1 = (bf16[256,256]{1,0:T(8,128)(2,1)S(1)}, bf16[256,256]{1,0:T(8,128)(2,1)S(1)}, u32[]{:S(2)}, u32[]{:S(2)}) collective-permute-start(bf16[256,256]{1,0:T(8,128)(2,1)S(1)} %pad_maximum_fusion.1), channel_id=1, source_target_pairs={{0,1},{1,0},{2,3},{3,2},{4,5},{5,4},{6,7},{7,6},{8,9},{9,8},{10,11... | collective-permute-start | bytes 393224 | tf_op jit(solution)/shard_map/ppermute | solution.py:403
  1.1 9.1 %collective-permute-start.3 = (bf16[256,256]{1,0:T(8,128)(2,1)S(1)}, bf16[256,256]{1,0:T(8,128)(2,1)S(1)}, u32[]{:S(2)}, u32[]{:S(2)}) collective-permute-start(bf16[256,256]{1,0:T(8,128)(2,1)S(1)} %pad_maximum_fusion.rest_4_), channel_id=1, source_target_pairs={{0,2},{1,3},{2,6},{3,7},{4,0},{5,1},{6,10},{7,11},{8,4},{9,5},{10,... | collective-permute-start | bytes 393224 | tf_op jit(solution)/shard_map/ppermute | solution.py:407
  3.8 6.4 %collective-permute-start = (bf16[256,256]{1,0:T(8,128)(2,1)S(1)}, bf16[256,256]{1,0:T(8,128)(2,1)S(1)}, u32[]{:S(2)}, u32[]{:S(2)}) collective-permute-start(bf16[256,256]{1,0:T(8,128)(2,1)S(1)} %pad_maximum_fusion.rest_4_), channel_id=1, source_target_pairs={{0,4},{1,5},{2,0},{3,1},{4,8},{5,9},{6,2},{7,3},{8,12},{9,13},{10,... | collective-permute-start | bytes 393224 | tf_op jit(solution)/shard_map/ppermute | solution.py:407
  4.0 6.6 %collective-permute-start.4 = (bf16[256,256]{1,0:T(8,128)(2,1)S(1)}, bf16[256,256]{1,0:T(8,128)(2,1)S(1)}, u32[]{:S(2)}, u32[]{:S(2)}) collective-permute-start(bf16[256,256]{1,0:T(8,128)(2,1)S(1)} %collective-permute-done.1.rest_12_), channel_id=1, source_target_pairs={{0,2},{1,3},{2,6},{3,7},{4,0},{5,1},{6,10},{7,11},{8,4},{9,5},{10,... | collective-permute-start | bytes 393224 | tf_op jit(solution)/shard_map/ppermute | solution.py:407
  5.3 6.1 %collective-permute-start.2 = (bf16[256,256]{1,0:T(8,128)(2,1)S(1)}, bf16[256,256]{1,0:T(8,128)(2,1)S(1)}, u32[]{:S(2)}, u32[]{:S(2)}) collective-permute-start(bf16[256,256]{1,0:T(8,128)(2,1)S(1)} %collective-permute-done.1.rest_12_), channel_id=1, source_target_pairs={{0,4},{1,5},{2,0},{3,1},{4,8},{5,9},{6,2},{7,3},{8,12},{9,13},{10,... | collective-permute-start | bytes 393224 | tf_op jit(solution)/shard_map/ppermute | solution.py:407
  10.2 8.9 %copy-start = (bf16[64,4096]{1,0:T(8,128)(2,1)S(1)}, bf16[64,4096]{1,0:T(8,128)(2,1)}, u32[]{:S(2)}) copy-start(bf16[64,4096]{1,0:T(8,128)(2,1)} %pool.2.rest_0_) | copy-start | bytes 1572868
  11.4 10.0 %collective-permute-start.5 = (bf16[256,256]{1,0:T(8,128)(2,1)S(1)}, bf16[256,256]{1,0:T(8,128)(2,1)S(1)}, u32[]{:S(2)}, u32[]{:S(2)}) collective-permute-start(bf16[256,256]{1,0:T(8,128)(2,1)S(1)} %collective-permute-done.rest_5_), channel_id=1, source_target_pairs={{0,4},{1,5},{2,0},{3,1},{4,8},{5,9},{6,2},{7,3},{8,12},{9,13},{10,... | collective-permute-start | bytes 393224 | tf_op jit(solution)/shard_map/ppermute | solution.py:407
  11.9 9.6 %collective-permute-start.6 = (bf16[256,256]{1,0:T(8,128)(2,1)S(1)}, bf16[256,256]{1,0:T(8,128)(2,1)S(1)}, u32[]{:S(2)}, u32[]{:S(2)}) collective-permute-start(bf16[256,256]{1,0:T(8,128)(2,1)S(1)} %collective-permute-done.2.rest_13_), channel_id=1, source_target_pairs={{0,4},{1,5},{2,0},{3,1},{4,8},{5,9},{6,2},{7,3},{8,12},{9,13},{10,... | collective-permute-start | bytes 393224 | tf_op jit(solution)/shard_map/ppermute | solution.py:407
  13.1 8.3 %collective-permute-start.7 = (bf16[256,256]{1,0:T(8,128)(2,1)S(1)}, bf16[256,256]{1,0:T(8,128)(2,1)S(1)}, u32[]{:S(2)}, u32[]{:S(2)}) collective-permute-start(bf16[256,256]{1,0:T(8,128)(2,1)S(1)} %collective-permute-done.3.rest_11_), channel_id=1, source_target_pairs={{0,2},{1,3},{2,6},{3,7},{4,0},{5,1},{6,10},{7,11},{8,4},{9,5},{10,... | collective-permute-start | bytes 393224 | tf_op jit(solution)/shard_map/ppermute | solution.py:407
  13.4 8.1 %collective-permute-start.8 = (bf16[256,256]{1,0:T(8,128)(2,1)S(1)}, bf16[256,256]{1,0:T(8,128)(2,1)S(1)}, u32[]{:S(2)}, u32[]{:S(2)}) collective-permute-start(bf16[256,256]{1,0:T(8,128)(2,1)S(1)} %collective-permute-done.4.rest_19_), channel_id=1, source_target_pairs={{0,2},{1,3},{2,6},{3,7},{4,0},{5,1},{6,10},{7,11},{8,4},{9,5},{10,... | collective-permute-start | bytes 393224 | tf_op jit(solution)/shard_map/ppermute | solution.py:407
  19.1 41.4 %copy-start.5 = (s32[4,16]{1,0:T(4,128)S(1)}, s32[4,16]{1,0:T(4,128)}, u32[]{:S(2)}) copy-start(s32[4,16]{1,0:T(4,128)} %param.12) | copy-start | bytes 772
  19.1 41.4 %copy-start.4 = (s32[4]{0:T(128)S(1)}, s32[4]{0:T(128)}, u32[]{:S(2)}) copy-start(s32[4]{0:T(128)} %length_ref.3) | copy-start | bytes 52
  19.2 15.7 %collective-permute-start.9 = (bf16[64,4096]{1,0:T(8,128)(2,1)S(1)}, bf16[64,4096]{1,0:T(8,128)(2,1)S(1)}, u32[]{:S(2)}, u32[]{:S(2)}) collective-permute-start(bf16[64,4096]{1,0:T(8,128)(2,1)S(1)} %copy-done), channel_id=1, source_target_pairs={{0,1},{1,0},{2,3},{3,2},{4,5},{5,4},{6,7},{7,6},{8,9},{9,8},{10,11... | collective-permute-start | bytes 1572872 | tf_op jit(solution)/shard_map/ppermute | solution.py:403
  21.5 13.4 %collective-permute-start.10 = (bf16[64,4096]{1,0:T(8,128)(2,1)}, bf16[64,4096]{1,0:T(8,128)(2,1)S(1)}, u32[]{:S(2)}, u32[]{:S(2)}) collective-permute-start(bf16[64,4096]{1,0:T(8,128)(2,1)} %pool.3.rest_1_), channel_id=1, source_target_pairs={{0,1},{1,0},{2,3},{3,2},{4,5},{5,4},{6,7},{7,6},{8,9},{9,8},{10,11... | collective-permute-start | bytes 1572872 | tf_op jit(solution)/shard_map/ppermute | solution.py:403
  21.9 4.9 %collective-permute-start.11 = (bf16[256,256]{1,0:T(8,128)(2,1)S(1)}, bf16[256,256]{1,0:T(8,128)(2,1)S(1)}, u32[]{:S(2)}, u32[]{:S(2)}) collective-permute-start(bf16[256,256]{1,0:T(8,128)(2,1)S(1)} %collective-permute-done.5.rest_6_), channel_id=1, source_target_pairs={{0,4},{1,5},{2,0},{3,1},{4,8},{5,9},{6,2},{7,3},{8,12},{9,13},{10,... | collective-permute-start | bytes 393224 | tf_op jit(solution)/shard_map/ppermute | solution.py:407
  23.2 5.1 %collective-permute-start.13 = (bf16[256,256]{1,0:T(8,128)(2,1)S(1)}, bf16[256,256]{1,0:T(8,128)(2,1)S(1)}, u32[]{:S(2)}, u32[]{:S(2)}) collective-permute-start(bf16[256,256]{1,0:T(8,128)(2,1)S(1)} %collective-permute-done.7.rest_10_), channel_id=1, source_target_pairs={{0,2},{1,3},{2,6},{3,7},{4,0},{5,1},{6,10},{7,11},{8,4},{9,5},{10,... | collective-permute-start | bytes 393224 | tf_op jit(solution)/shard_map/ppermute | solution.py:407
  23.3 7.4 %collective-permute-start.15 = (bf16[256,256]{1,0:T(8,128)(2,1)S(1)}, bf16[256,256]{1,0:T(8,128)(2,1)S(1)}, u32[]{:S(2)}, u32[]{:S(2)}) collective-permute-start(bf16[256,256]{1,0:T(8,128)(2,1)S(1)} %collective-permute-done.8.rest_18_), channel_id=1, source_target_pairs={{0,2},{1,3},{2,6},{3,7},{4,0},{5,1},{6,10},{7,11},{8,4},{9,5},{10,... | collective-permute-start | bytes 393224 | tf_op jit(solution)/shard_map/ppermute | solution.py:407
  26.8 4.1 %collective-permute-start.14 = (bf16[256,256]{1,0:T(8,128)(2,1)S(1)}, bf16[256,256]{1,0:T(8,128)(2,1)S(1)}, u32[]{:S(2)}, u32[]{:S(2)}) collective-permute-start(bf16[256,256]{1,0:T(8,128)(2,1)S(1)} %collective-permute-done.6.rest_14_), channel_id=1, source_target_pairs={{0,4},{1,5},{2,0},{3,1},{4,8},{5,9},{6,2},{7,3},{8,12},{9,13},{10,... | collective-permute-start | bytes 393224 | tf_op jit(solution)/shard_map/ppermute | solution.py:407
  28.3 5.5 %collective-permute-start.12 = (bf16[256,256]{1,0:T(8,128)(2,1)S(1)}, bf16[256,256]{1,0:T(8,128)(2,1)S(1)}, u32[]{:S(2)}, u32[]{:S(2)}) collective-permute-start(bf16[256,256]{1,0:T(8,128)(2,1)S(1)} %collective-permute-done.11.rest_7_), channel_id=1, source_target_pairs={{0,4},{1,5},{2,0},{3,1},{4,8},{5,9},{6,2},{7,3},{8,12},{9,13},{10,... | collective-permute-start | bytes 393224 | tf_op jit(solution)/shard_map/ppermute | solution.py:407
  30.8 4.1 %collective-permute-start.16 = (bf16[256,256]{1,0:T(8,128)(2,1)S(1)}, bf16[256,256]{1,0:T(8,128)(2,1)}, u32[]{:S(2)}, u32[]{:S(2)}) collective-permute-start(bf16[256,256]{1,0:T(8,128)(2,1)S(1)} %collective-permute-done.15.rest_17_), channel_id=1, source_target_pairs={{0,2},{1,3},{2,6},{3,7},{4,0},{5,1},{6,10},{7,11},{8,4},{9,5},{10,... | collective-permute-start | bytes 393224 | tf_op jit(solution)/shard_map/ppermute | solution.py:407
  34.9 1.0 copy-start.1
  37.6 4.3 %collective-permute-start.19 = (bf16[256,256]{1,0:T(8,128)(2,1)S(1)}, bf16[256,256]{1,0:T(8,128)(2,1)S(1)}, u32[]{:S(2)}, u32[]{:S(2)}) collective-permute-start(bf16[256,256]{1,0:T(8,128)(2,1)S(1)} %project.1), channel_id=1, source_target_pairs={{0,12},{1,13},{2,14},{3,15},{4,0},{5,1},{6,2},{7,3},{8,4},{9,5},{1... | collective-permute-start | bytes 393224 | tf_op jit(solution)/shard_map/ppermute | solution.py:407
  40.0 11.7 %collective-permute-start.18 = (bf16[256,256]{1,0:T(8,128)(2,1)S(1)}, bf16[256,256]{1,0:T(8,128)(2,1)S(1)}, u32[]{:S(2)}, u32[]{:S(2)}) collective-permute-start(bf16[256,256]{1,0:T(8,128)(2,1)S(1)} %project.1), channel_id=1, source_target_pairs={{0,8},{1,9},{2,10},{3,11},{4,12},{5,13},{6,14},{7,15},{8,0},{9,1},... | collective-permute-start | bytes 393224 | tf_op jit(solution)/shard_map/ppermute | solution.py:407
  40.0 11.6 %collective-permute-start.17 = (bf16[256,256]{1,0:T(8,128)(2,1)S(1)}, bf16[256,256]{1,0:T(8,128)(2,1)S(1)}, u32[]{:S(2)}, u32[]{:S(2)}) collective-permute-start(bf16[256,256]{1,0:T(8,128)(2,1)S(1)} %project.1), channel_id=1, source_target_pairs={{0,4},{1,5},{2,6},{3,7},{4,8},{5,9},{6,10},{7,11},{8,12},{9,13},{1... | collective-permute-start | bytes 393224 | tf_op jit(solution)/shard_map/ppermute | solution.py:407
  41.2 12.0 %collective-permute-start.20 = (bf16[256,256]{1,0:T(8,128)(2,1)S(1)}, bf16[256,256]{1,0:T(8,128)(2,1)S(1)}, u32[]{:S(2)}, u32[]{:S(2)}) collective-permute-start(bf16[256,256]{1,0:T(8,128)(2,1)S(1)} %project.1), channel_id=1, source_target_pairs={{0,2},{1,3},{2,0},{3,1},{4,6},{5,7},{6,4},{7,5},{8,10},{9,11},{10,... | collective-permute-start | bytes 393224 | tf_op jit(solution)/shard_map/ppermute | solution.py:407
  41.9 15.5 %collective-permute-start.23 = (bf16[256,256]{1,0:T(8,128)(2,1)S(1)}, bf16[256,256]{1,0:T(8,128)(2,1)S(1)}, u32[]{:S(2)}, u32[]{:S(2)}) collective-permute-start(bf16[256,256]{1,0:T(8,128)(2,1)S(1)} %collective-permute-done.19), channel_id=1, source_target_pairs={{0,2},{1,3},{2,0},{3,1},{4,6},{5,7},{6,4},{7,5},{8,10},{9,11},{10,... | collective-permute-start | bytes 393224 | tf_op jit(solution)/shard_map/ppermute | solution.py:407
  51.7 5.7 %collective-permute-start.22 = (bf16[256,256]{1,0:T(8,128)(2,1)S(1)}, bf16[256,256]{1,0:T(8,128)(2,1)S(1)}, u32[]{:S(2)}, u32[]{:S(2)}) collective-permute-start(bf16[256,256]{1,0:T(8,128)(2,1)S(1)} %collective-permute-done.18), channel_id=1, source_target_pairs={{0,2},{1,3},{2,0},{3,1},{4,6},{5,7},{6,4},{7,5},{8,10},{9,11},{10,... | collective-permute-start | bytes 393224 | tf_op jit(solution)/shard_map/ppermute | solution.py:407
  51.7 5.7 %collective-permute-start.21 = (bf16[256,256]{1,0:T(8,128)(2,1)S(1)}, bf16[256,256]{1,0:T(8,128)(2,1)S(1)}, u32[]{:S(2)}, u32[]{:S(2)}) collective-permute-start(bf16[256,256]{1,0:T(8,128)(2,1)S(1)} %collective-permute-done.17), channel_id=1, source_target_pairs={{0,2},{1,3},{2,0},{3,1},{4,6},{5,7},{6,4},{7,5},{8,10},{9,11},{10,... | collective-permute-start | bytes 393224 | tf_op jit(solution)/shard_map/ppermute | solution.py:407
  57.4 49.7 %collective-permute-start.24 = (bf16[2048,256]{1,0:T(8,128)(2,1)S(1)}, bf16[2048,256]{1,0:T(8,128)(2,1)S(1)}, u32[]{:S(2)}, u32[]{:S(2)}) collective-permute-start(bf16[2048,256]{1,0:T(8,128)(2,1)S(1)} %constant_dynamic-update-slice_fusion.kv_ref), channel_id=1, source_target_pairs={{0,1},{1,0},{2,3},{3,2},{4,5},{5,4},{6,7},{7,6},{8,9},{9,8},{10,11... | collective-permute-start | bytes 3145736 | tf_op jit(solution)/shard_map/ppermute | solution.py:403
  60.5 1.0 copy-start.2
  61.5 45.6 %copy-start.3 = (bf16[4,64,512]{2,1,0:T(8,128)(2,1)S(1)}, bf16[4,64,512]{2,1,0:T(8,128)(2,1)}, u32[]{:S(2)}) copy-start(bf16[4,64,512]{2,1,0:T(8,128)(2,1)} %own_kv_ref.3) | copy-start | bytes 786436

commit v11 on v10

--- a/solution.py
+++ b/solution.py
@@ -29,9 +29,10 @@
 NEG = -1e30
 SUM_LOW, SUM_HIGH = 2.0 ** -40, 2.0 ** 60
 POOL_WIDTH = 1024
-POOL_CALLS = 2
+FIRST_COST = 8 * 10**9
+PROJECT_COST = 8
 CHIP = 8
-STEP = 8
+STEP = 5
 BLOCK = 16
 MIB = 1024 * 1024
 
@@ -47,33 +48,35 @@
     return 2 * line + lane
 
 
-def pool_kernel(first, states_hbm, queries_hbm, gain_hbm, out_ref, states, queries, gain, pooled, arrived):
-    passages = states.shape[1]
+def split_kernel(core_ref, weight_ref, mine_ref, theirs_ref):
+    for out_ref, half in ((mine_ref, core_ref[0]), (theirs_ref, 1 - core_ref[0])):
+        for n in range(2):
+            at = pl.multiple_of(half * LANES + n * KVH * HD, LANES)
+            out_ref[:, n * LANES:(n + 1) * LANES] = weight_ref[:, pl.ds(at, LANES)]
+
+
+def split(core, weight):
+    vmem = pl.BlockSpec(memory_space=pltpu.VMEM)
+    return pl.pallas_call(
+        split_kernel,
+        in_specs=[pl.BlockSpec(memory_space=pltpu.SMEM), vmem],
+        out_specs=[vmem, vmem],
+        out_shape=[jax.ShapeDtypeStruct((weight.shape[0], 2 * LANES), weight.dtype)] * 2,
+        compiler_params=pltpu.CompilerParams(vmem_limit_bytes=8 * MIB),
+        cost_estimate=pl.CostEstimate(flops=FIRST_COST, bytes_accessed=4 * weight.size, transcendentals=0),
+        name="split",
+    )(core.reshape(1), weight)
+
+
+def pool_kernel(states, queries, gain, out_ref, pooled):
+    passages = states.shape[0]
     two = 2 * CHD
-    groups = D // POOL_WIDTH
-    small = [
-        pltpu.make_async_copy(queries_hbm, queries, arrived.at[groups]),
-        pltpu.make_async_copy(gain_hbm, gain, arrived.at[groups + 1]),
-    ]
-    large = [
-        pltpu.make_async_copy(
-            states_hbm.at[pl.ds(first, passages), :, pl.ds(j * POOL_WIDTH, POOL_WIDTH)],
-            states.at[j],
-            arrived.at[j],
-        )
-        for j in range(groups)
-    ]
-    for copy in small[:1] + large + small[1:]:
-        copy.start()
-    small[0].wait()
     zero = jnp.zeros((MEM, CHD), jnp.bfloat16)
     blank = jnp.zeros((2 * MEM, LEN), jnp.bfloat16)
     totals = [jnp.zeros((MEM, CHD), jnp.float32)] * passages
-    for j in range(groups):
-        large[j].wait()
+    for base in range(0, D, POOL_WIDTH):
         blocks = []
-        for at in range(0, POOL_WIDTH, two):
-            column = j * POOL_WIDTH + at
+        for column in range(base, base + POOL_WIDTH, two):
             lhs = jnp.concatenate(
                 [
                     jnp.concatenate([queries[:, column:column + CHD], zero], axis=1),
@@ -82,7 +85,7 @@
                 axis=0,
             )
             for p in range(0, passages, 2):
-                tokens = states[j, p:p + 2, :, at:at + two].reshape(2 * LEN, two)
+                tokens = states[p:p + 2, :, column:column + two].reshape(2 * LEN, two)
                 scores = lax.dot_general(
                     lhs, tokens, (((1,), (1,)), ((), ())), preferred_element_type=jnp.float32
                 ) * (1.0 / math.sqrt(CHD))
@@ -102,29 +105,22 @@
                     place = slice(column + head * CHD, column + (head + 1) * CHD)
                     pooled[(p + n) * MEM:(p + n + 1) * MEM, place] = block
                     totals[p + n] = totals[p + n] + block * block
-    small[1].wait()
     mean_square = jnp.sum(jnp.concatenate(totals, axis=0), axis=1, keepdims=True) * (1.0 / D)
     scale = lax.rsqrt(mean_square + 1e-06)
     factor = gain[...].astype(jnp.float32).reshape(1, D)
     out_ref[...] = (pooled[...] * scale * factor).astype(jnp.bfloat16)
 
 
-def pool(states, queries, gain, first, count):
-    groups = D // POOL_WIDTH
-    hbm = pl.BlockSpec(memory_space=pltpu.HBM)
+def pool(states, queries, gain):
+    count = states.shape[0]
+    vmem = pl.BlockSpec(memory_space=pltpu.VMEM)
     return pl.pallas_call(
-        functools.partial(pool_kernel, first),
-        in_specs=[hbm] * 3,
-        out_specs=pl.BlockSpec(memory_space=pltpu.VMEM),
+        pool_kernel,
+        in_specs=[vmem] * 3,
+        out_specs=vmem,
         out_shape=jax.ShapeDtypeStruct((count * MEM, D), jnp.bfloat16),
-        scratch_shapes=[
-            pltpu.VMEM((groups, count, LEN, POOL_WIDTH), jnp.bfloat16),
-            pltpu.VMEM((MEM, D), jnp.bfloat16),
-            pltpu.VMEM((D,), jnp.bfloat16),
-            pltpu.VMEM((count * MEM, D), jnp.float32),
-            pltpu.SemaphoreType.DMA((groups + 2,)),
-        ],
-        compiler_params=pltpu.CompilerParams(vmem_limit_bytes=56 * MIB),
+        scratch_shapes=[pltpu.VMEM((count * MEM, D), jnp.float32)],
+        compiler_params=pltpu.CompilerParams(vmem_limit_bytes=20 * MIB),
         cost_estimate=pl.CostEstimate(
             flops=4 * count * MEM * LEN * D, bytes_accessed=2 * count * LEN * D,
             transcendentals=count * CH * MEM * LEN,
@@ -133,29 +129,20 @@
     )(states, queries, gain)
 
 
-def attend_kernel(half_ref, start_ref, length_ref, q_hbm, kv_ref, own_kv_ref, *rest):
-    out_hbm = rest[-13]
+def attend_kernel(half_ref, start_ref, length_ref, q_ref, kv_ref, own_kv_ref, *rest):
+    out_hbm = rest[-11]
     (
-        questions, answers, memory, key_side, value_side, weights, bias, marker, scores, all_weights,
-        arrived, sent,
-    ) = rest[-12:]
-    count = q_hbm.shape[0]
+        answers, memory, key_side, value_side, weights, bias, marker, scores, all_weights, sent,
+    ) = rest[-10:]
+    count = q_ref.shape[0]
     half_at = pl.multiple_of(half_ref[0] * HALF, LANES)
     own_at = pl.multiple_of(half_ref[0] * LANES, LANES)
     factor = math.log2(math.e) / math.sqrt(HD)
-
-    def fetch(query):
-        return pltpu.make_async_copy(
-            q_hbm.at[query, :, pl.ds(half_at, HALF)], questions.at[query], arrived.at[query]
-        )
 
     def send(query):
         return pltpu.make_async_copy(
             answers.at[query], out_hbm.at[query, :, pl.ds(half_at, HALF)], sent.at[query]
         )
-
-    for query in range(count):
-        fetch(query).start()
 
     lane = lax.broadcasted_iota(jnp.int32, (KEYS, LANES), 1)
     row = lax.broadcasted_iota(jnp.int32, (KEYS, LANES), 0)
@@ -195,10 +182,11 @@
         bias[...] = jnp.where((key <= token) & (key < length), 0.0, NEG)
         alive = token < length
         sample = lax.div(key, HD // STEP)
-        fetch(query).wait()
 
         def stacked(tiles):
-            return jnp.concatenate([questions[query, :, t * LANES:(t + 1) * LANES] for t in tiles], axis=0)
+            return jnp.concatenate(
+                [q_ref[query, :, pl.ds(pl.multiple_of(half_at + t * LANES, LANES), LANES)] for t in tiles], axis=0
+            )
 
         def key_product(i):
             g, tiles = chunks[i]
@@ -298,7 +286,7 @@
     count = questions.shape[0]
     hbm, vmem, smem = (pl.BlockSpec(memory_space=x) for x in (pltpu.HBM, pltpu.VMEM, pltpu.SMEM))
     operands = [half.reshape(1), starts, lengths, questions, memory_kv, own_kv]
-    in_specs = [smem, smem, smem, hbm, vmem, vmem]
+    in_specs = [smem, smem, smem, vmem, vmem, vmem]
     aliases = {}
     if earlier is not None:
         aliases = {len(operands): 0}
@@ -311,7 +299,6 @@
         out_shape=jax.ShapeDtypeStruct((count, QLEN, H * HD), jnp.bfloat16),
         scratch_shapes=[
             pltpu.VMEM((count, QLEN, HALF), jnp.bfloat16),
-            pltpu.VMEM((count, QLEN, HALF), jnp.bfloat16),
             pltpu.VMEM((ROWS, 2 * LANES), jnp.bfloat16),
             pltpu.VMEM((2, LANES, KEYS), jnp.bfloat16),
             pltpu.VMEM((2, KEYS, 2 * LANES), jnp.bfloat16),
@@ -321,10 +308,9 @@
             pltpu.VMEM((STEP * QLEN, KEYS), jnp.float32),
             pltpu.VMEM((STEP * QLEN, KEYS), jnp.bfloat16),
             pltpu.SemaphoreType.DMA((count,)),
-            pltpu.SemaphoreType.DMA((count,)),
         ],
         input_output_aliases=aliases,
-        compiler_params=pltpu.CompilerParams(vmem_limit_bytes=50 * MIB),
+        compiler_params=pltpu.CompilerParams(vmem_limit_bytes=32 * MIB),
         cost_estimate=pl.CostEstimate(
             flops=2 * count * QLEN * H * HD * (ROWS + QLEN),
             bytes_accessed=2 * count * QLEN * H * HD,
@@ -334,9 +320,9 @@
     )(*operands)
 
 
-def project_kernel(ring, parts, core_ref, place_ref, *rest):
-    row_refs, weights, out_ref = rest[:2 * parts], rest[2 * parts:-1], rest[-1]
-    count = parts * row_refs[0].shape[0]
+def project_kernel(ring, core_ref, place_ref, *rest):
+    own_ref, other_ref, *weights, out_ref = rest
+    count = own_ref.shape[0]
     depth = weights[0].shape[0]
     total = jnp.zeros((2 * count, weights[0].shape[1]), jnp.float32)
     core = core_ref[0]
@@ -344,7 +330,7 @@
         part, i = n // ring, n % ring
         chip = chip_at(lax.rem(ring + place_ref[0] - i, ring), ring)
         at = pl.multiple_of((2 * chip + (1 - core if part else core)) * depth, depth)
-        rows = jnp.concatenate([x[:, pl.ds(at, depth)] for x in row_refs], axis=0)
+        rows = jnp.concatenate([own_ref[:, pl.ds(at, depth)], other_ref[:, pl.ds(at, depth)]], axis=0)
         total += jnp.dot(rows, weight[...], preferred_element_type=jnp.float32)
     result = total.astype(jnp.bfloat16)
     out_ref[pl.ds(pl.multiple_of(core * count, count), count)] = result[:count]
@@ -352,21 +338,21 @@
 
 
 def project(core, place, own_rows, other_rows, weights):
-    count = len(own_rows) * own_rows[0].shape[0]
+    count = own_rows.shape[0]
     width = weights[0].shape[1]
     vmem = pl.BlockSpec(memory_space=pltpu.VMEM)
     smem = pl.BlockSpec(memory_space=pltpu.SMEM)
     return pl.pallas_call(
-        functools.partial(project_kernel, len(weights) // 2, len(own_rows)),
-        in_specs=[smem, smem] + [vmem] * (2 * len(own_rows) + len(weights)),
+        functools.partial(project_kernel, len(weights) // 2),
+        in_specs=[smem, smem] + [vmem] * (2 + len(weights)),
         out_specs=vmem,
         out_shape=jax.ShapeDtypeStruct((2 * count, width), jnp.bfloat16),
         compiler_params=pltpu.CompilerParams(vmem_limit_bytes=16 * MIB),
         cost_estimate=pl.CostEstimate(
-            flops=4 * count * D * width, bytes_accessed=2 * D * width, transcendentals=0
+            flops=PROJECT_COST * 4 * count * D * width, bytes_accessed=2 * D * width, transcendentals=0
         ),
         name="project",
-    )(core.reshape(1), place, *own_rows, *other_rows, *weights)
+    )(core.reshape(1), place, own_rows, other_rows, *weights)
 
 
 def local(
@@ -384,10 +370,9 @@
     core, chip = me & 1, lax.div(me, 2)
     chips = extent // 2
     depth = kv_weight.shape[0]
-    own_count = passage_states.shape[0]
 
     if chips != 8 or depth % LANES:
-        memory_rows = pool(passage_states, memory_queries, memory_gain, 0, own_count)
+        memory_rows = pool(passage_states, memory_queries, memory_gain)
         whole_weight = lax.all_gather(kv_weight, "pass", axis=0, tiled=True)
         memory_kv = jnp.dot(memory_rows, whole_weight, preferred_element_type=jnp.float32)
         everything = lax.all_gather(memory_kv.astype(jnp.bfloat16), "pass", axis=0, tiled=True)
@@ -416,33 +401,22 @@
             blocks.append(along(block, lambda line, lane: 2 * ((line + k) % lines) + lane))
         return blocks + [along(x, lambda line, lane: 2 * line + 1 - lane) for x in blocks]
 
-    def columns(half):
-        return jnp.concatenate(
-            [
-                lax.dynamic_slice_in_dim(kv_weight, half * LANES + at, LANES, axis=1)
-                for at in (0, KVH * HD)
-            ],
-            axis=1,
-        )
-
-    up = [[columns(core)], [to_partner(columns(1 - core))]]
+    mine, theirs = split(core, kv_weight)
+    up = [[mine], [to_partner(theirs)]]
     down = [[x[0]] for x in up]
-    memory_rows = []
     for turn in range(1, chips // 2):
         for piece in range(2):
             up[piece].append(along_ring(up[piece][-1], 1))
             down[piece].append(along_ring(down[piece][-1], -1))
-        if turn <= POOL_CALLS:
-            part = own_count // POOL_CALLS
-            rows = pool(passage_states, memory_queries, memory_gain, (turn - 1) * part, part)
-            *hops, rows = lax.optimization_barrier((*(x[-1] for x in up + down), rows))
+        if turn == 1:
+            memory_rows = pool(passage_states, memory_queries, memory_gain)
+            *hops, memory_rows = lax.optimization_barrier((*(x[-1] for x in up + down), memory_rows))
             for chain, hop in zip(up + down, hops):
                 chain[-1] = hop
-            memory_rows.append(rows)
     up[0].append(along_ring(up[0][-1], 1))
     down[1].append(along_ring(down[1][-1], -1))
     weights = [x for piece in range(2) for x in up[piece] + down[piece][:0:-1]]
-    memory_kv = project(core, place, memory_rows, [to_partner(x) for x in memory_rows], weights)
+    memory_kv = project(core, place, memory_rows, to_partner(memory_rows), weights)
     near = jnp.concatenate(line_by_line(memory_kv), axis=0)
     far = to_partner(near)
 

time: 153 us -> 149 us (0.974)
  Pallas kernels: 102 us -> 96 us
  local copies, waits for them, and re-layouts: 3.05 us -> 6.24 us
  starting transfers between devices: 24.3 us -> 22.6 us
    pallas_call x3, Pallas kernels: 11.1 us -> 5.06 us  [the longest x1 3.08 us: pool(): pl.pallas_call(pool_kernel, in_specs=[vmem] * 3, out_specs=vmem, out_shap...]
    unnamed x19 -> x33, local copies, waits for them, and re-layouts: 2.08 us -> 6.23 us
    ppermute x4 -> x3, starting transfers between devices: 5.91 us -> 4.43 us  [to_partner(): return lax.ppermute(x, 'pass', [(i, i ^ 1) for i in range(extent)])]
  transfers between devices with their start and end apart: 25 -> 24, of which waited for: 10 -> 13; matrix products, arithmetic and copies ran while one was open for 0% -> 0% of each run, Pallas kernels for 36% -> 33%
where the time goes in v11:
time: 149 us
  Pallas kernels  96 us (64%)
  waiting for transfers between devices  23.9 us (16%)
  starting transfers between devices  22.6 us (15%)
  local copies, waits for them, and re-layouts  6.24 us (4%)
    pallas_call x2, Pallas kernels, attend(): pl.pallas_call(attend_kernel, in_specs=in_specs, out_specs=hbm, out_shape...  90.9 us
    ppermute x21, waiting for transfers between devices, along(): lax.ppermute(x, 'pass', [(2 * s + c, 2 * d + c) for s, d in pairs for c i...  23.9 us
    ppermute x21, starting transfers between devices, along(): lax.ppermute(x, 'pass', [(2 * s + c, 2 * d + c) for s, d in pairs for c i...  18.1 us
    unnamed x33, local copies, waits for them, and re-layouts  6.23 us
    ppermute x3, starting transfers between devices, to_partner(): return lax.ppermute(x, 'pass', [(i, i ^ 1) for i in range(extent)])  4.43 us
    pallas_call x1, Pallas kernels, pool(): pl.pallas_call(pool_kernel, in_specs=[vmem] * 3, out_specs=vmem, out_shap...  3.08 us
  transfers between devices with their start and end apart: 24, of which 13 were waited for; matrix products, arithmetic and copies ran while one was open for 0% of the time, Pallas kernels for 33%

profile of v11, /device:TPU:1, one launch (start us, length us, event | category | flops | bytes accessed | tf_op | source)
XLA Modules:
  0.0 149.0 jit_solution(11912138553922931373)
XLA Ops:
  0.0 0.9 copy-done.5
  1.0 0.1 collective-permute-start.1
  1.1 2.7 %collective-permute-start.3 = (bf16[256,256]{1,0:T(8,128)(2,1)S(1)}, bf16[256,256]{1,0:T(8,128)(2,1)S(1)}, u32[]{:S(2)}, u32[]{:S(2)}) collective-permute-start(bf16[256,256]{1,0:T(8,128)(2,1)S(1)} %get-tuple-element.12.rest_2_), channel_id=1, source_target_pairs={{0,2},{1,3},{2,6},{3,7},{4,0},{5,1},{6,10},{7,11},{8,4},{9,5},{10,... | collective-permute-start | bytes 393224 | tf_op jit(solution)/shard_map/ppermute | solution.py:392
  3.8 0.1 collective-permute-start
  3.9 0.0 collective-permute-done.1.rest_10_
  3.9 1.4 collective-permute-start.4
  5.3 0.1 collective-permute-start.2
  5.3 0.0 copy-done
  5.4 0.0 copy-done.1
  5.4 0.0 copy-done.2
  5.4 3.1 %pool.1.rest_0_ = bf16[128,4096]{1,0:T(8,128)(2,1)S(1)} custom-call(bf16[4,128,4096]{2,1,0:T(8,128)(2,1)S(1)} %copy-done, bf16[32,4096]{1,0:T(8,128)(2,1)S(1)} %copy-done.1, bf16[4096]{0:T(1024)(128)(2,1)S(1)} %copy-done.2), custom_call_target="tpu_custom_call" | custom-call | flops 268435456 | bytes 4194304 | tf_op jit(solution)/shard_map/pool/pallas_call | solution.py:117
  8.4 0.0 collective-permute-done.3.rest_9_
  8.5 0.1 collective-permute-done.rest_3_
  8.5 2.0 %collective-permute-done.4.rest_17_ = bf16[256,256]{1,0:T(8,128)(2,1)S(1)} collective-permute-done((bf16[256,256]{1,0:T(8,128)(2,1)S(1)}, bf16[256,256]{1,0:T(8,128)(2,1)S(1)}, u32[]{:S(2)}, u32[]{:S(2)}) %collective-permute-start.4) | collective-permute-done | bytes 131104 | tf_op jit(solution)/shard_map/ppermute | solution.py:392
  10.5 0.9 collective-permute-done.2.rest_11_
  11.3 1.2 collective-permute-start.5
  12.5 0.1 collective-permute-start.6
  12.6 1.4 collective-permute-start.13
  14.0 1.3 collective-permute-start.9
  15.3 0.2 collective-permute-start.11
  15.4 2.2 %collective-permute-done.6.rest_4_ = bf16[256,256]{1,0:T(8,128)(2,1)S(1)} collective-permute-done((bf16[256,256]{1,0:T(8,128)(2,1)S(1)}, bf16[256,256]{1,0:T(8,128)(2,1)S(1)}, u32[]{:S(2)}, u32[]{:S(2)}) %collective-permute-start.6) | collective-permute-done | bytes 131104 | tf_op jit(solution)/shard_map/ppermute | solution.py:392
  17.6 0.1 collective-permute-start.7
  17.7 0.0 collective-permute-done.13.rest_16_
  17.7 1.4 collective-permute-start.14
  19.1 1.1 collective-permute-done.9.rest_8_
  20.2 1.4 collective-permute-start.10
  21.6 0.0 collective-permute-done.11.rest_12_
  21.6 0.1 collective-permute-start.12
  21.7 0.6 copy-done.7
  22.3 0.6 collective-permute-done.7.rest_5_
  23.0 0.8 collective-permute-start.8
  23.8 0.7 copy-done.9
  24.5 0.0 collective-permute-done.14.rest_15_
  24.5 0.6 collective-permute-start.15
  25.1 0.4 collective-permute-done.10.rest_7_
  25.5 0.3 collective-permute-done.12.rest_13_
  25.8 1.9 %collective-permute-done.8.rest_6_ = bf16[256,256]{1,0:T(8,128)(2,1)} collective-permute-done((bf16[256,256]{1,0:T(8,128)(2,1)S(1)}, bf16[256,256]{1,0:T(8,128)(2,1)}, u32[]{:S(2)}, u32[]{:S(2)}) %collective-permute-start.8) | collective-permute-done | bytes 131104 | tf_op jit(solution)/shard_map/ppermute | solution.py:392
  27.7 1.2 collective-permute-done.15.rest_14_
  28.9 0.0 collective-permute-done.5.rest_1_
  28.9 0.9 copy-done.8
  29.8 0.9 copy-done.10
  30.7 1.9 %project.1 = bf16[256,256]{1,0:T(8,128)(2,1)S(1)} custom-call(s32[1]{0:T(128)} %bitcast.1.core_ref.half_ref, s32[1]{0:T(128)} %bitcast.2.place_ref, bf16[128,4096]{1,0:T(8,128)(2,1)S(1)} %pool.1.rest_0_, bf16[128,4096]{1,0:T(8,128)(2,1)S(1)} %collective-permute-done.5.rest_1_, bf16[256,256]{1,0:T(8,128)(2,1)S(1)} %get-tuple-element.12.rest_2_, ...), custom_call_target="tpu_custom_call" | custom-call | flops 4294967296 | bytes 2097152 | tf_op jit(solution)/shard_map/project/pallas_call | solution.py:345
  32.6 3.3 %collective-permute-start.18 = (bf16[256,256]{1,0:T(8,128)(2,1)S(1)}, bf16[256,256]{1,0:T(8,128)(2,1)S(1)}, u32[]{:S(2)}, u32[]{:S(2)}) collective-permute-start(bf16[256,256]{1,0:T(8,128)(2,1)S(1)} %project.1), channel_id=1, source_target_pairs={{0,12},{1,13},{2,14},{3,15},{4,0},{5,1},{6,2},{7,3},{8,4},{9,5},{1... | collective-permute-start | bytes 393224 | tf_op jit(solution)/shard_map/ppermute | solution.py:392
  35.9 0.0 collective-permute-start.17
  35.9 0.5 collective-permute-start.16
  36.5 0.6 collective-permute-start.19
  37.1 0.8 collective-permute-done.18
  37.9 0.7 collective-permute-start.22
  38.6 8.3 %collective-permute-done.17 = bf16[256,256]{1,0:T(8,128)(2,1)S(1)} collective-permute-done((bf16[256,256]{1,0:T(8,128)(2,1)S(1)}, bf16[256,256]{1,0:T(8,128)(2,1)S(1)}, u32[]{:S(2)}, u32[]{:S(2)}) %collective-permute-start.17) | collective-permute-done | bytes 131104 | tf_op jit(solution)/shard_map/ppermute | solution.py:392
  46.9 0.7 collective-permute-start.21
  47.6 0.0 collective-permute-done.16
  47.6 0.8 collective-permute-start.20
  48.4 0.0 collective-permute-done.19
  48.5 4.1 %collective-permute-done.20 = bf16[256,256]{1,0:T(8,128)(2,1)S(1)} collective-permute-done((bf16[256,256]{1,0:T(8,128)(2,1)S(1)}, bf16[256,256]{1,0:T(8,128)(2,1)S(1)}, u32[]{:S(2)}, u32[]{:S(2)}) %collective-permute-start.20) | collective-permute-done | bytes 131104 | tf_op jit(solution)/shard_map/ppermute | solution.py:392
  52.6 0.0 collective-permute-done.21
  52.6 0.0 collective-permute-done.22
  52.6 3.1 %collective-permute-start.23 = (bf16[2048,256]{1,0:T(8,128)(2,1)S(1)}, bf16[2048,256]{1,0:T(8,128)(2,1)S(1)}, u32[]{:S(2)}, u32[]{:S(2)}) collective-permute-start(bf16[2048,256]{1,0:T(8,128)(2,1)S(1)} %constant_dynamic-update-slice_fusion.kv_ref), channel_id=1, source_target_pairs={{0,1},{1,0},{2,3},{3,2},{4,5},{5,4},{6,7},{7,6},{8,9},{9,8},{10,11... | collective-permute-start | bytes 3145736 | tf_op jit(solution)/shard_map/ppermute | solution.py:388
  55.8 0.0 copy-done.12
  55.8 0.0 copy-done.6
  55.8 0.0 copy-start.3
  55.8 2.1 %copy-done.3 = bf16[4,64,7424]{2,1,0:T(8,128)(2,1)S(1)} copy-done((bf16[4,64,7424]{2,1,0:T(8,128)(2,1)S(1)}, bf16[4,64,7424]{2,1,0:T(8,128)(2,1)}, u32[]{:S(2)}) %copy-start.3) | copy-done | bytes 3801112
  57.9 45.3 %attend.2.rest_0_ = bf16[4,64,7424]{2,1,0:T(8,128)(2,1)} custom-call(s32[1]{0:T(128)} %bitcast.1.core_ref.half_ref, s32[4,16]{1,0:T(4,128)S(1)} %fusion.6.start_ref, s32[4]{0:T(128)S(1)} %copy-done.11, bf16[4,64,7424]{2,1,0:T(8,128)(2,1)S(1)} %copy-done.3, bf16[2048,256]{1,0:T(8,128)(2,1)S(1)} %constant_dynamic-update-slice_fusion.kv_ref, ...), custom_call_target="tpu_custom_call" | custom-call | flops 2189426688 | bytes 3801088 | tf_op jit(solution)/shard_map/attend/pallas_call | solution.py:295
  103.3 0.0 collective-permute-done.23.kv_ref
  103.3 45.6 %attend.3 = bf16[4,64,7424]{2,1,0:T(8,128)(2,1)} custom-call(s32[1]{0:T(128)} %bitcast.half_ref, s32[4,16]{1,0:T(4,128)S(1)} %fusion.6.start_ref, s32[4]{0:T(128)S(1)} %copy-done.11, bf16[4,64,7424]{2,1,0:T(8,128)(2,1)S(1)} %copy-done.4, bf16[2048,256]{1,0:T(8,128)(2,1)S(1)} %collective-permute-done.23.kv_ref, ...), custom_call_target="tpu_custom_call", output_to_operand_aliasing={{}: (6, {})} | custom-call | flops 2189426688 | bytes 3801088 | tf_op jit(solution)/shard_map/attend/pallas_call | solution.py:295
  (24 shorter events, 0.2 us)
Async XLA Ops:
  0.0 0.9 copy-start.5
  1.0 4.4 %copy-start = (bf16[4,128,4096]{2,1,0:T(8,128)(2,1)S(1)}, bf16[4,128,4096]{2,1,0:T(8,128)(2,1)}, u32[]{:S(2)}) copy-start(bf16[4,128,4096]{2,1,0:T(8,128)(2,1)} %states.1) | copy-start | bytes 12582916
  1.0 4.4 %copy-start.1 = (bf16[32,4096]{1,0:T(8,128)(2,1)S(1)}, bf16[32,4096]{1,0:T(8,128)(2,1)}, u32[]{:S(2)}) copy-start(bf16[32,4096]{1,0:T(8,128)(2,1)} %queries.1) | copy-start | bytes 786436
  1.0 4.4 %copy-start.2 = (bf16[4096]{0:T(1024)(128)(2,1)S(1)}, bf16[4096]{0:T(1024)(128)(2,1)}, u32[]{:S(2)}) copy-start(bf16[4096]{0:T(1024)(128)(2,1)} %gain.1) | copy-start | bytes 24580
  1.0 2.9 %collective-permute-start.1 = (bf16[256,256]{1,0:T(8,128)(2,1)S(1)}, bf16[256,256]{1,0:T(8,128)(2,1)S(1)}, u32[]{:S(2)}, u32[]{:S(2)}) collective-permute-start(bf16[256,256]{1,0:T(8,128)(2,1)S(1)} %get-tuple-element.13), channel_id=1, source_target_pairs={{0,1},{1,0},{2,3},{3,2},{4,5},{5,4},{6,7},{7,6},{8,9},{9,8},{10,11... | collective-permute-start | bytes 393224 | tf_op jit(solution)/shard_map/ppermute | solution.py:388
  1.1 7.3 %collective-permute-start.3 = (bf16[256,256]{1,0:T(8,128)(2,1)S(1)}, bf16[256,256]{1,0:T(8,128)(2,1)S(1)}, u32[]{:S(2)}, u32[]{:S(2)}) collective-permute-start(bf16[256,256]{1,0:T(8,128)(2,1)S(1)} %get-tuple-element.12.rest_2_), channel_id=1, source_target_pairs={{0,2},{1,3},{2,6},{3,7},{4,0},{5,1},{6,10},{7,11},{8,4},{9,5},{10,... | collective-permute-start | bytes 393224 | tf_op jit(solution)/shard_map/ppermute | solution.py:392
  3.8 4.7 %collective-permute-start = (bf16[256,256]{1,0:T(8,128)(2,1)S(1)}, bf16[256,256]{1,0:T(8,128)(2,1)S(1)}, u32[]{:S(2)}, u32[]{:S(2)}) collective-permute-start(bf16[256,256]{1,0:T(8,128)(2,1)S(1)} %get-tuple-element.12.rest_2_), channel_id=1, source_target_pairs={{0,4},{1,5},{2,0},{3,1},{4,8},{5,9},{6,2},{7,3},{8,12},{9,13},{10,... | collective-permute-start | bytes 393224 | tf_op jit(solution)/shard_map/ppermute | solution.py:392
  3.9 6.6 %collective-permute-start.4 = (bf16[256,256]{1,0:T(8,128)(2,1)S(1)}, bf16[256,256]{1,0:T(8,128)(2,1)S(1)}, u32[]{:S(2)}, u32[]{:S(2)}) collective-permute-start(bf16[256,256]{1,0:T(8,128)(2,1)S(1)} %collective-permute-done.1.rest_10_), channel_id=1, source_target_pairs={{0,2},{1,3},{2,6},{3,7},{4,0},{5,1},{6,10},{7,11},{8,4},{9,5},{10,... | collective-permute-start | bytes 393224 | tf_op jit(solution)/shard_map/ppermute | solution.py:392
  5.3 6.1 %collective-permute-start.2 = (bf16[256,256]{1,0:T(8,128)(2,1)S(1)}, bf16[256,256]{1,0:T(8,128)(2,1)S(1)}, u32[]{:S(2)}, u32[]{:S(2)}) collective-permute-start(bf16[256,256]{1,0:T(8,128)(2,1)S(1)} %collective-permute-done.1.rest_10_), channel_id=1, source_target_pairs={{0,4},{1,5},{2,0},{3,1},{4,8},{5,9},{6,2},{7,3},{8,12},{9,13},{10,... | collective-permute-start | bytes 393224 | tf_op jit(solution)/shard_map/ppermute | solution.py:392
  11.3 17.6 %collective-permute-start.5 = (bf16[128,4096]{1,0:T(8,128)(2,1)S(1)}, bf16[128,4096]{1,0:T(8,128)(2,1)S(1)}, u32[]{:S(2)}, u32[]{:S(2)}) collective-permute-start(bf16[128,4096]{1,0:T(8,128)(2,1)S(1)} %pool.1.rest_0_), channel_id=1, source_target_pairs={{0,1},{1,0},{2,3},{3,2},{4,5},{5,4},{6,7},{7,6},{8,9},{9,8},{10,11... | collective-permute-start | bytes 3145736 | tf_op jit(solution)/shard_map/ppermute | solution.py:388
  12.5 5.1 %collective-permute-start.6 = (bf16[256,256]{1,0:T(8,128)(2,1)S(1)}, bf16[256,256]{1,0:T(8,128)(2,1)S(1)}, u32[]{:S(2)}, u32[]{:S(2)}) collective-permute-start(bf16[256,256]{1,0:T(8,128)(2,1)S(1)} %collective-permute-done.rest_3_), channel_id=1, source_target_pairs={{0,4},{1,5},{2,0},{3,1},{4,8},{5,9},{6,2},{7,3},{8,12},{9,13},{10,... | collective-permute-start | bytes 393224 | tf_op jit(solution)/shard_map/ppermute | solution.py:392
  12.6 5.1 %collective-permute-start.13 = (bf16[256,256]{1,0:T(8,128)(2,1)S(1)}, bf16[256,256]{1,0:T(8,128)(2,1)S(1)}, u32[]{:S(2)}, u32[]{:S(2)}) collective-permute-start(bf16[256,256]{1,0:T(8,128)(2,1)S(1)} %collective-permute-done.4.rest_17_), channel_id=1, source_target_pairs={{0,2},{1,3},{2,6},{3,7},{4,0},{5,1},{6,10},{7,11},{8,4},{9,5},{10,... | collective-permute-start | bytes 393224 | tf_op jit(solution)/shard_map/ppermute | solution.py:392
  14.0 6.2 %collective-permute-start.9 = (bf16[256,256]{1,0:T(8,128)(2,1)S(1)}, bf16[256,256]{1,0:T(8,128)(2,1)S(1)}, u32[]{:S(2)}, u32[]{:S(2)}) collective-permute-start(bf16[256,256]{1,0:T(8,128)(2,1)S(1)} %collective-permute-done.3.rest_9_), channel_id=1, source_target_pairs={{0,2},{1,3},{2,6},{3,7},{4,0},{5,1},{6,10},{7,11},{8,4},{9,5},{10,... | collective-permute-start | bytes 393224 | tf_op jit(solution)/shard_map/ppermute | solution.py:392
  15.3 6.3 %collective-permute-start.11 = (bf16[256,256]{1,0:T(8,128)(2,1)S(1)}, bf16[256,256]{1,0:T(8,128)(2,1)S(1)}, u32[]{:S(2)}, u32[]{:S(2)}) collective-permute-start(bf16[256,256]{1,0:T(8,128)(2,1)S(1)} %collective-permute-done.2.rest_11_), channel_id=1, source_target_pairs={{0,4},{1,5},{2,0},{3,1},{4,8},{5,9},{6,2},{7,3},{8,12},{9,13},{10,... | collective-permute-start | bytes 393224 | tf_op jit(solution)/shard_map/ppermute | solution.py:392
  17.6 5.3 %collective-permute-start.7 = (bf16[256,256]{1,0:T(8,128)(2,1)S(1)}, bf16[256,256]{1,0:T(8,128)(2,1)S(1)}, u32[]{:S(2)}, u32[]{:S(2)}) collective-permute-start(bf16[256,256]{1,0:T(8,128)(2,1)S(1)} %collective-permute-done.6.rest_4_), channel_id=1, source_target_pairs={{0,4},{1,5},{2,0},{3,1},{4,8},{5,9},{6,2},{7,3},{8,12},{9,13},{10,... | collective-permute-start | bytes 393224 | tf_op jit(solution)/shard_map/ppermute | solution.py:392
  17.7 6.7 %collective-permute-start.14 = (bf16[256,256]{1,0:T(8,128)(2,1)S(1)}, bf16[256,256]{1,0:T(8,128)(2,1)}, u32[]{:S(2)}, u32[]{:S(2)}) collective-permute-start(bf16[256,256]{1,0:T(8,128)(2,1)S(1)} %collective-permute-done.13.rest_16_), channel_id=1, source_target_pairs={{0,2},{1,3},{2,6},{3,7},{4,0},{5,1},{6,10},{7,11},{8,4},{9,5},{10,... | collective-permute-start | bytes 393224 | tf_op jit(solution)/shard_map/ppermute | solution.py:392
  20.2 5.3 %collective-permute-start.10 = (bf16[256,256]{1,0:T(8,128)(2,1)S(1)}, bf16[256,256]{1,0:T(8,128)(2,1)}, u32[]{:S(2)}, u32[]{:S(2)}) collective-permute-start(bf16[256,256]{1,0:T(8,128)(2,1)S(1)} %collective-permute-done.9.rest_8_), channel_id=1, source_target_pairs={{0,2},{1,3},{2,6},{3,7},{4,0},{5,1},{6,10},{7,11},{8,4},{9,5},{10,... | collective-permute-start | bytes 393224 | tf_op jit(solution)/shard_map/ppermute | solution.py:392
  21.6 4.2 %collective-permute-start.12 = (bf16[256,256]{1,0:T(8,128)(2,1)S(1)}, bf16[256,256]{1,0:T(8,128)(2,1)}, u32[]{:S(2)}, u32[]{:S(2)}) collective-permute-start(bf16[256,256]{1,0:T(8,128)(2,1)S(1)} %collective-permute-done.11.rest_12_), channel_id=1, source_target_pairs={{0,4},{1,5},{2,0},{3,1},{4,8},{5,9},{6,2},{7,3},{8,12},{9,13},{10,... | collective-permute-start | bytes 393224 | tf_op jit(solution)/shard_map/ppermute | solution.py:392
  21.7 0.6 copy-start.7
  23.0 4.7 %collective-permute-start.8 = (bf16[256,256]{1,0:T(8,128)(2,1)S(1)}, bf16[256,256]{1,0:T(8,128)(2,1)}, u32[]{:S(2)}, u32[]{:S(2)}) collective-permute-start(bf16[256,256]{1,0:T(8,128)(2,1)S(1)} %collective-permute-done.7.rest_5_), channel_id=1, source_target_pairs={{0,4},{1,5},{2,0},{3,1},{4,8},{5,9},{6,2},{7,3},{8,12},{9,13},{10,... | collective-permute-start | bytes 393224 | tf_op jit(solution)/shard_map/ppermute | solution.py:392
  23.8 0.7 copy-start.9
  24.5 4.4 %collective-permute-start.15 = (bf16[256,256]{1,0:T(8,128)(2,1)}, bf16[256,256]{1,0:T(8,128)(2,1)}, u32[]{:S(2)}, u32[]{:S(2)}) collective-permute-start(bf16[256,256]{1,0:T(8,128)(2,1)} %collective-permute-done.14.rest_15_), channel_id=1, source_target_pairs={{0,2},{1,3},{2,6},{3,7},{4,0},{5,1},{6,10},{7,11},{8,4},{9,5},{10,... | collective-permute-start | bytes 393224 | tf_op jit(solution)/shard_map/ppermute | solution.py:392
  28.9 0.9 copy-start.8
  29.8 0.9 copy-start.10
  30.7 25.1 %copy-start.12 = (s32[4,16]{1,0:T(4,128)S(1)}, s32[4,16]{1,0:T(4,128)}, u32[]{:S(2)}) copy-start(s32[4,16]{1,0:T(4,128)} %param.12) | copy-start | bytes 772
  30.7 25.1 %copy-start.6 = (bf16[4,64,512]{2,1,0:T(8,128)(2,1)S(1)}, bf16[4,64,512]{2,1,0:T(8,128)(2,1)}, u32[]{:S(2)}) copy-start(bf16[4,64,512]{2,1,0:T(8,128)(2,1)} %own_kv_ref.3) | copy-start | bytes 786436
  30.7 25.1 %copy-start.11 = (s32[4]{0:T(128)S(1)}, s32[4]{0:T(128)}, u32[]{:S(2)}) copy-start(s32[4]{0:T(128)} %length_ref.3) | copy-start | bytes 52
  32.6 5.2 %collective-permute-start.18 = (bf16[256,256]{1,0:T(8,128)(2,1)S(1)}, bf16[256,256]{1,0:T(8,128)(2,1)S(1)}, u32[]{:S(2)}, u32[]{:S(2)}) collective-permute-start(bf16[256,256]{1,0:T(8,128)(2,1)S(1)} %project.1), channel_id=1, source_target_pairs={{0,12},{1,13},{2,14},{3,15},{4,0},{5,1},{6,2},{7,3},{8,4},{9,5},{1... | collective-permute-start | bytes 393224 | tf_op jit(solution)/shard_map/ppermute | solution.py:392
  35.9 11.0 %collective-permute-start.17 = (bf16[256,256]{1,0:T(8,128)(2,1)S(1)}, bf16[256,256]{1,0:T(8,128)(2,1)S(1)}, u32[]{:S(2)}, u32[]{:S(2)}) collective-permute-start(bf16[256,256]{1,0:T(8,128)(2,1)S(1)} %project.1), channel_id=1, source_target_pairs={{0,8},{1,9},{2,10},{3,11},{4,12},{5,13},{6,14},{7,15},{8,0},{9,1},... | collective-permute-start | bytes 393224 | tf_op jit(solution)/shard_map/ppermute | solution.py:392
  35.9 11.7 %collective-permute-start.16 = (bf16[256,256]{1,0:T(8,128)(2,1)S(1)}, bf16[256,256]{1,0:T(8,128)(2,1)S(1)}, u32[]{:S(2)}, u32[]{:S(2)}) collective-permute-start(bf16[256,256]{1,0:T(8,128)(2,1)S(1)} %project.1), channel_id=1, source_target_pairs={{0,4},{1,5},{2,6},{3,7},{4,8},{5,9},{6,10},{7,11},{8,12},{9,13},{1... | collective-permute-start | bytes 393224 | tf_op jit(solution)/shard_map/ppermute | solution.py:392
  36.5 12.0 %collective-permute-start.19 = (bf16[256,256]{1,0:T(8,128)(2,1)S(1)}, bf16[256,256]{1,0:T(8,128)(2,1)S(1)}, u32[]{:S(2)}, u32[]{:S(2)}) collective-permute-start(bf16[256,256]{1,0:T(8,128)(2,1)S(1)} %project.1), channel_id=1, source_target_pairs={{0,2},{1,3},{2,0},{3,1},{4,6},{5,7},{6,4},{7,5},{8,10},{9,11},{10,... | collective-permute-start | bytes 393224 | tf_op jit(solution)/shard_map/ppermute | solution.py:392
  37.9 14.7 %collective-permute-start.22 = (bf16[256,256]{1,0:T(8,128)(2,1)S(1)}, bf16[256,256]{1,0:T(8,128)(2,1)S(1)}, u32[]{:S(2)}, u32[]{:S(2)}) collective-permute-start(bf16[256,256]{1,0:T(8,128)(2,1)S(1)} %collective-permute-done.18), channel_id=1, source_target_pairs={{0,2},{1,3},{2,0},{3,1},{4,6},{5,7},{6,4},{7,5},{8,10},{9,11},{10,... | collective-permute-start | bytes 393224 | tf_op jit(solution)/shard_map/ppermute | solution.py:392
  46.9 5.7 %collective-permute-start.21 = (bf16[256,256]{1,0:T(8,128)(2,1)S(1)}, bf16[256,256]{1,0:T(8,128)(2,1)S(1)}, u32[]{:S(2)}, u32[]{:S(2)}) collective-permute-start(bf16[256,256]{1,0:T(8,128)(2,1)S(1)} %collective-permute-done.17), channel_id=1, source_target_pairs={{0,2},{1,3},{2,0},{3,1},{4,6},{5,7},{6,4},{7,5},{8,10},{9,11},{10,... | collective-permute-start | bytes 393224 | tf_op jit(solution)/shard_map/ppermute | solution.py:392
  47.6 5.0 %collective-permute-start.20 = (bf16[256,256]{1,0:T(8,128)(2,1)S(1)}, bf16[256,256]{1,0:T(8,128)(2,1)S(1)}, u32[]{:S(2)}, u32[]{:S(2)}) collective-permute-start(bf16[256,256]{1,0:T(8,128)(2,1)S(1)} %collective-permute-done.16), channel_id=1, source_target_pairs={{0,2},{1,3},{2,0},{3,1},{4,6},{5,7},{6,4},{7,5},{8,10},{9,11},{10,... | collective-permute-start | bytes 393224 | tf_op jit(solution)/shard_map/ppermute | solution.py:392
  52.6 50.6 %collective-permute-start.23 = (bf16[2048,256]{1,0:T(8,128)(2,1)S(1)}, bf16[2048,256]{1,0:T(8,128)(2,1)S(1)}, u32[]{:S(2)}, u32[]{:S(2)}) collective-permute-start(bf16[2048,256]{1,0:T(8,128)(2,1)S(1)} %constant_dynamic-update-slice_fusion.kv_ref), channel_id=1, source_target_pairs={{0,1},{1,0},{2,3},{3,2},{4,5},{5,4},{6,7},{7,6},{8,9},{9,8},{10,11... | collective-permute-start | bytes 3145736 | tf_op jit(solution)/shard_map/ppermute | solution.py:388
  55.8 2.1 %copy-start.3 = (bf16[4,64,7424]{2,1,0:T(8,128)(2,1)S(1)}, bf16[4,64,7424]{2,1,0:T(8,128)(2,1)}, u32[]{:S(2)}) copy-start(bf16[4,64,7424]{2,1,0:T(8,128)(2,1)} %q_ref.3) | copy-start | bytes 11403268
  57.9 45.4 %copy-start.4 = (bf16[4,64,7424]{2,1,0:T(8,128)(2,1)S(1)}, bf16[4,64,7424]{2,1,0:T(8,128)(2,1)}, u32[]{:S(2)}) copy-start(bf16[4,64,7424]{2,1,0:T(8,128)(2,1)} %q_ref.3) | copy-start | bytes 11403268

commit v12 on v11

--- a/solution.py
+++ b/solution.py
@@ -32,7 +32,7 @@
 FIRST_COST = 8 * 10**9
 PROJECT_COST = 8
 CHIP = 8
-STEP = 5
+STEP = 4
 BLOCK = 16
 MIB = 1024 * 1024
 
@@ -129,21 +129,28 @@
     )(states, queries, gain)
 
 
-def attend_kernel(half_ref, start_ref, length_ref, q_ref, kv_ref, own_kv_ref, *rest):
-    out_hbm = rest[-11]
+def attend_kernel(half_ref, start_ref, length_ref, q_hbm, kv_ref, own_kv_ref, *rest):
+    out_hbm = rest[-13]
     (
-        answers, memory, key_side, value_side, weights, bias, marker, scores, all_weights, sent,
-    ) = rest[-10:]
-    count = q_ref.shape[0]
+        questions, answers, memory, key_side, value_side, weights, bias, marker, scores, all_weights,
+        arrived, sent,
+    ) = rest[-12:]
+    count = q_hbm.shape[0]
     half_at = pl.multiple_of(half_ref[0] * HALF, LANES)
     own_at = pl.multiple_of(half_ref[0] * LANES, LANES)
     factor = math.log2(math.e) / math.sqrt(HD)
+
+    def fetch(query):
+        return pltpu.make_async_copy(
+            q_hbm.at[query, :, pl.ds(half_at, HALF)], questions.at[query], arrived.at[query]
+        )
 
     def send(query):
         return pltpu.make_async_copy(
             answers.at[query], out_hbm.at[query, :, pl.ds(half_at, HALF)], sent.at[query]
         )
 
+    fetch(0).start()
     lane = lax.broadcasted_iota(jnp.int32, (KEYS, LANES), 1)
     row = lax.broadcasted_iota(jnp.int32, (KEYS, LANES), 0)
     in_b = ((row >= ROWS) & (row < 2 * ROWS)) | (row >= 2 * ROWS + QLEN)
@@ -183,10 +190,14 @@
         alive = token < length
         sample = lax.div(key, HD // STEP)
 
+        fetch(query).wait()
+
+        @pl.when(query + 1 < count)
+        def _():
+            fetch(query + 1).start()
+
         def stacked(tiles):
-            return jnp.concatenate(
-                [q_ref[query, :, pl.ds(pl.multiple_of(half_at + t * LANES, LANES), LANES)] for t in tiles], axis=0
-            )
+            return jnp.concatenate([questions[query, :, t * LANES:(t + 1) * LANES] for t in tiles], axis=0)
 
         def key_product(i):
             g, tiles = chunks[i]
@@ -286,7 +297,7 @@
     count = questions.shape[0]
     hbm, vmem, smem = (pl.BlockSpec(memory_space=x) for x in (pltpu.HBM, pltpu.VMEM, pltpu.SMEM))
     operands = [half.reshape(1), starts, lengths, questions, memory_kv, own_kv]
-    in_specs = [smem, smem, smem, vmem, vmem, vmem]
+    in_specs = [smem, smem, smem, hbm, vmem, vmem]
     aliases = {}
     if earlier is not None:
         aliases = {len(operands): 0}
@@ -299,6 +310,7 @@
         out_shape=jax.ShapeDtypeStruct((count, QLEN, H * HD), jnp.bfloat16),
         scratch_shapes=[
             pltpu.VMEM((count, QLEN, HALF), jnp.bfloat16),
+            pltpu.VMEM((count, QLEN, HALF), jnp.bfloat16),
             pltpu.VMEM((ROWS, 2 * LANES), jnp.bfloat16),
             pltpu.VMEM((2, LANES, KEYS), jnp.bfloat16),
             pltpu.VMEM((2, KEYS, 2 * LANES), jnp.bfloat16),
@@ -308,9 +320,10 @@
             pltpu.VMEM((STEP * QLEN, KEYS), jnp.float32),
             pltpu.VMEM((STEP * QLEN, KEYS), jnp.bfloat16),
             pltpu.SemaphoreType.DMA((count,)),
+            pltpu.SemaphoreType.DMA((count,)),
         ],
         input_output_aliases=aliases,
-        compiler_params=pltpu.CompilerParams(vmem_limit_bytes=32 * MIB),
+        compiler_params=pltpu.CompilerParams(vmem_limit_bytes=50 * MIB),
         cost_estimate=pl.CostEstimate(
             flops=2 * count * QLEN * H * HD * (ROWS + QLEN),
             bytes_accessed=2 * count * QLEN * H * HD,
@@ -320,39 +333,45 @@
     )(*operands)
 
 
-def project_kernel(ring, core_ref, place_ref, *rest):
-    own_ref, other_ref, *weights, out_ref = rest
+def project_kernel(ring, pieces, more, core_ref, place_ref, own_ref, other_ref, *rest):
+    weights, rest = rest[:len(pieces)], rest[len(pieces):]
+    out_ref = rest[-1]
     count = own_ref.shape[0]
     depth = weights[0].shape[0]
-    total = jnp.zeros((2 * count, weights[0].shape[1]), jnp.float32)
     core = core_ref[0]
-    for n, weight in enumerate(weights):
-        part, i = n // ring, n % ring
+    total = jnp.zeros((2 * count, weights[0].shape[1]), jnp.float32) if more else rest[0][...]
+    for (part, i), weight in zip(pieces, weights):
         chip = chip_at(lax.rem(ring + place_ref[0] - i, ring), ring)
         at = pl.multiple_of((2 * chip + (1 - core if part else core)) * depth, depth)
         rows = jnp.concatenate([own_ref[:, pl.ds(at, depth)], other_ref[:, pl.ds(at, depth)]], axis=0)
         total += jnp.dot(rows, weight[...], preferred_element_type=jnp.float32)
+    if more:
+        out_ref[...] = total
+        return
     result = total.astype(jnp.bfloat16)
     out_ref[pl.ds(pl.multiple_of(core * count, count), count)] = result[:count]
     out_ref[pl.ds(pl.multiple_of((1 - core) * count, count), count)] = result[count:]
 
 
-def project(core, place, own_rows, other_rows, weights):
+def project(ring, core, place, own_rows, other_rows, weights, sums=None):
     count = own_rows.shape[0]
-    width = weights[0].shape[1]
+    pieces, blocks = tuple(weights), list(weights.values())
+    width = blocks[0].shape[1]
     vmem = pl.BlockSpec(memory_space=pltpu.VMEM)
     smem = pl.BlockSpec(memory_space=pltpu.SMEM)
+    more = sums is None
+    operands = [own_rows, other_rows, *blocks] + ([] if more else [sums])
     return pl.pallas_call(
-        functools.partial(project_kernel, len(weights) // 2),
-        in_specs=[smem, smem] + [vmem] * (2 + len(weights)),
+        functools.partial(project_kernel, ring, pieces, more),
+        in_specs=[smem, smem] + [vmem] * len(operands),
         out_specs=vmem,
-        out_shape=jax.ShapeDtypeStruct((2 * count, width), jnp.bfloat16),
+        out_shape=jax.ShapeDtypeStruct((2 * count, width), jnp.float32 if more else jnp.bfloat16),
         compiler_params=pltpu.CompilerParams(vmem_limit_bytes=16 * MIB),
         cost_estimate=pl.CostEstimate(
             flops=PROJECT_COST * 4 * count * D * width, bytes_accessed=2 * D * width, transcendentals=0
         ),
         name="project",
-    )(core.reshape(1), place, own_rows, other_rows, *weights)
+    )(core.reshape(1), place, *operands)
 
 
 def local(
@@ -404,19 +423,36 @@
     mine, theirs = split(core, kv_weight)
     up = [[mine], [to_partner(theirs)]]
     down = [[x[0]] for x in up]
+
+    def blocks(turns):
+        found = {}
+        for part in range(2):
+            for turn in turns:
+                if turn < len(up[part]):
+                    found[part, turn] = up[part][turn]
+                if 0 < turn < len(down[part]):
+                    found[part, chips - turn] = down[part][turn]
+        return found
+
     for turn in range(1, chips // 2):
-        for piece in range(2):
-            up[piece].append(along_ring(up[piece][-1], 1))
-            down[piece].append(along_ring(down[piece][-1], -1))
+        for part in range(2):
+            up[part].append(along_ring(up[part][-1], 1))
+            down[part].append(along_ring(down[part][-1], -1))
         if turn == 1:
-            memory_rows = pool(passage_states, memory_queries, memory_gain)
-            *hops, memory_rows = lax.optimization_barrier((*(x[-1] for x in up + down), memory_rows))
-            for chain, hop in zip(up + down, hops):
-                chain[-1] = hop
+            beside = rows = pool(passage_states, memory_queries, memory_gain)
+        elif turn == 3:
+            beside = project(chips, core, place, rows, other_rows, blocks((0, 1, 2)))
+        else:
+            continue
+        *hops, beside = lax.optimization_barrier((*(x[-1] for x in up + down), beside))
+        for chain, hop in zip(up + down, hops):
+            chain[-1] = hop
+        if turn == 1:
+            rows = beside
+            other_rows = to_partner(rows)
     up[0].append(along_ring(up[0][-1], 1))
     down[1].append(along_ring(down[1][-1], -1))
-    weights = [x for piece in range(2) for x in up[piece] + down[piece][:0:-1]]
-    memory_kv = project(core, place, memory_rows, to_partner(memory_rows), weights)
+    memory_kv = project(chips, core, place, rows, other_rows, blocks((3, 4)), beside)
     near = jnp.concatenate(line_by_line(memory_kv), axis=0)
     far = to_partner(near)
 

time: 149 us -> 151 us (1.013)
  waiting for transfers between devices: 23.9 us -> 29.5 us
  local copies, waits for them, and re-layouts: 6.24 us -> 1.06 us
  Pallas kernels: 96 us -> 98.4 us
    ppermute x21, waiting for transfers between devices: 23.9 us -> 29.5 us  [along(): lax.ppermute(x, 'pass', [(2 * s + c, 2 * d + c) for s, d in pairs for c i...]
    unnamed x33 -> x21, local copies, waits for them, and re-layouts: 6.23 us -> 1.05 us
    pallas_call x2, Pallas kernels: 90.9 us -> 94.4 us  [attend(): pl.pallas_call(attend_kernel, in_specs=in_specs, out_specs=hbm, out_shape...]
  transfers between devices with their start and end apart: 24 -> 24, of which waited for: 13 -> 12; matrix products, arithmetic and copies ran while one was open for 0% -> 0% of each run, Pallas kernels for 33% -> 34%
where the time goes in v12:
time: 151 us
  Pallas kernels  98.4 us (65%)
  waiting for transfers between devices  29.5 us (20%)
  starting transfers between devices  21.2 us (14%)
    pallas_call x2, Pallas kernels, attend(): pl.pallas_call(attend_kernel, in_specs=in_specs, out_specs=hbm, out_shape...  94.4 us
    ppermute x21, waiting for transfers between devices, along(): lax.ppermute(x, 'pass', [(2 * s + c, 2 * d + c) for s, d in pairs for c i...  29.5 us
    ppermute x21, starting transfers between devices, along(): lax.ppermute(x, 'pass', [(2 * s + c, 2 * d + c) for s, d in pairs for c i...  16.7 us
    ppermute x3, starting transfers between devices, to_partner(): return lax.ppermute(x, 'pass', [(i, i ^ 1) for i in range(extent)])  4.48 us
    pallas_call x1, Pallas kernels, pool(): pl.pallas_call(pool_kernel, in_specs=[vmem] * 3, out_specs=vmem, out_shap...  3.08 us
  transfers between devices with their start and end apart: 24, of which 12 were waited for; matrix products, arithmetic and copies ran while one was open for 0% of the time, Pallas kernels for 34%

profile of v12, /device:TPU:1, one launch (start us, length us, event | category | flops | bytes accessed | tf_op | source)
XLA Modules:
  0.0 150.5 jit_solution(4556608173523788789)
XLA Ops:
  0.0 0.0 copy-start.3
  0.0 0.9 copy-done.3
  1.0 0.1 collective-permute-start.1
  1.1 2.7 %collective-permute-start.3 = (bf16[256,256]{1,0:T(8,128)(2,1)S(1)}, bf16[256,256]{1,0:T(8,128)(2,1)S(1)}, u32[]{:S(2)}, u32[]{:S(2)}) collective-permute-start(bf16[256,256]{1,0:T(8,128)(2,1)S(1)} %get-tuple-element.17.rest_0_), channel_id=1, source_target_pairs={{0,2},{1,3},{2,6},{3,7},{4,0},{5,1},{6,10},{7,11},{8,4},{9,5},{10,... | collective-permute-start | bytes 393224 | tf_op jit(solution)/shard_map/ppermute | solution.py:411
  3.8 0.1 collective-permute-start
  3.9 0.0 collective-permute-done.1.rest_5_
  3.9 1.4 collective-permute-start.4
  5.3 0.1 collective-permute-start.2
  5.3 0.0 copy-done
  5.4 0.0 copy-done.1
  5.4 0.0 copy-done.2
  5.4 3.1 %pool.1.own_ref = bf16[128,4096]{1,0:T(8,128)(2,1)S(1)} custom-call(bf16[4,128,4096]{2,1,0:T(8,128)(2,1)S(1)} %copy-done, bf16[32,4096]{1,0:T(8,128)(2,1)S(1)} %copy-done.1, bf16[4096]{0:T(1024)(128)(2,1)S(1)} %copy-done.2), custom_call_target="tpu_custom_call" | custom-call | flops 268435456 | bytes 4194304 | tf_op jit(solution)/shard_map/pool/pallas_call | solution.py:117
  8.4 0.0 collective-permute-done.3.rest_2_
  8.5 0.1 collective-permute-done.rest_1_
  8.5 2.0 %collective-permute-done.4.rest_7_ = bf16[256,256]{1,0:T(8,128)(2,1)S(1)} collective-permute-done((bf16[256,256]{1,0:T(8,128)(2,1)S(1)}, bf16[256,256]{1,0:T(8,128)(2,1)S(1)}, u32[]{:S(2)}, u32[]{:S(2)}) %collective-permute-start.4) | collective-permute-done | bytes 131104 | tf_op jit(solution)/shard_map/ppermute | solution.py:411
  10.5 0.9 collective-permute-done.2.rest_6_
  11.3 1.2 collective-permute-start.5
  12.5 0.1 collective-permute-start.6
  12.6 1.5 collective-permute-start.8
  14.1 0.0 collective-permute-start.10
  14.1 1.4 collective-permute-start.12
  15.4 2.2 %collective-permute-done.6.rest_3_ = bf16[256,256]{1,0:T(8,128)(2,1)S(1)} collective-permute-done((bf16[256,256]{1,0:T(8,128)(2,1)S(1)}, bf16[256,256]{1,0:T(8,128)(2,1)S(1)}, u32[]{:S(2)}, u32[]{:S(2)}) %collective-permute-start.6) | collective-permute-done | bytes 131104 | tf_op jit(solution)/shard_map/ppermute | solution.py:411
  17.6 0.1 collective-permute-start.7
  17.7 2.7 %collective-permute-done.8.rest_8_ = bf16[256,256]{1,0:T(8,128)(2,1)S(1)} collective-permute-done((bf16[256,256]{1,0:T(8,128)(2,1)S(1)}, bf16[256,256]{1,0:T(8,128)(2,1)S(1)}, u32[]{:S(2)}, u32[]{:S(2)}) %collective-permute-start.8) | collective-permute-done | bytes 131104 | tf_op jit(solution)/shard_map/ppermute | solution.py:411
  20.4 0.1 collective-permute-start.9
  20.5 0.0 collective-permute-done.10.rest_4_
  20.5 1.4 collective-permute-start.11
  21.9 0.0 collective-permute-done.12.rest_9_
  21.9 1.3 collective-permute-start.13
  23.2 0.0 collective-permute-done.5.other_ref
  23.2 0.5 project.2.rest_6_
  23.7 0.0 copy-start.6
  23.8 0.0 copy-start.4
  23.8 0.0 copy-start.5
  23.8 0.0 collective-permute-done.7.rest_0_
  23.8 1.5 collective-permute-done.9.rest_3_
  25.2 0.0 collective-permute-done.11.rest_1_
  25.3 1.6 %collective-permute-done.13.rest_4_ = bf16[256,256]{1,0:T(8,128)(2,1)S(1)} collective-permute-done((bf16[256,256]{1,0:T(8,128)(2,1)S(1)}, bf16[256,256]{1,0:T(8,128)(2,1)S(1)}, u32[]{:S(2)}, u32[]{:S(2)}) %collective-permute-start.13) | collective-permute-done | bytes 131104 | tf_op jit(solution)/shard_map/ppermute | solution.py:411
  26.9 1.5 collective-permute-start.14
  28.4 0.0 collective-permute-start.15
  28.4 2.4 %collective-permute-done.14.rest_2_ = bf16[256,256]{1,0:T(8,128)(2,1)S(1)} collective-permute-done((bf16[256,256]{1,0:T(8,128)(2,1)S(1)}, bf16[256,256]{1,0:T(8,128)(2,1)S(1)}, u32[]{:S(2)}, u32[]{:S(2)}) %collective-permute-start.14) | collective-permute-done | bytes 131104 | tf_op jit(solution)/shard_map/ppermute | solution.py:411
  30.7 1.8 %collective-permute-done.15.rest_5_ = bf16[256,256]{1,0:T(8,128)(2,1)S(1)} collective-permute-done((bf16[256,256]{1,0:T(8,128)(2,1)S(1)}, bf16[256,256]{1,0:T(8,128)(2,1)S(1)}, u32[]{:S(2)}, u32[]{:S(2)}) %collective-permute-start.15) | collective-permute-done | bytes 131104 | tf_op jit(solution)/shard_map/ppermute | solution.py:411
  32.5 0.4 project.3
  32.9 3.0 %collective-permute-start.18 = (bf16[256,256]{1,0:T(8,128)(2,1)S(1)}, bf16[256,256]{1,0:T(8,128)(2,1)S(1)}, u32[]{:S(2)}, u32[]{:S(2)}) collective-permute-start(bf16[256,256]{1,0:T(8,128)(2,1)S(1)} %project.3), channel_id=1, source_target_pairs={{0,12},{1,13},{2,14},{3,15},{4,0},{5,1},{6,2},{7,3},{8,4},{9,5},{1... | collective-permute-start | bytes 393224 | tf_op jit(solution)/shard_map/ppermute | solution.py:411
  35.9 0.0 collective-permute-start.17
  35.9 0.5 collective-permute-start.16
  36.4 0.1 collective-permute-start.19
  36.5 1.3 collective-permute-done.18
  37.8 0.1 collective-permute-start.22
  38.0 9.1 %collective-permute-done.17 = bf16[256,256]{1,0:T(8,128)(2,1)S(1)} collective-permute-done((bf16[256,256]{1,0:T(8,128)(2,1)S(1)}, bf16[256,256]{1,0:T(8,128)(2,1)S(1)}, u32[]{:S(2)}, u32[]{:S(2)}) %collective-permute-start.17) | collective-permute-done | bytes 131104 | tf_op jit(solution)/shard_map/ppermute | solution.py:411
  47.1 0.0 collective-permute-start.21
  47.1 0.0 collective-permute-done.16
  47.1 1.5 collective-permute-start.20
  48.6 0.0 collective-permute-done.19
  48.6 4.1 %collective-permute-done.20 = bf16[256,256]{1,0:T(8,128)(2,1)S(1)} collective-permute-done((bf16[256,256]{1,0:T(8,128)(2,1)S(1)}, bf16[256,256]{1,0:T(8,128)(2,1)S(1)}, u32[]{:S(2)}, u32[]{:S(2)}) %collective-permute-start.20) | collective-permute-done | bytes 131104 | tf_op jit(solution)/shard_map/ppermute | solution.py:411
  52.7 0.0 collective-permute-done.21
  52.7 0.0 collective-permute-done.22
  52.8 3.2 %collective-permute-start.23 = (bf16[2048,256]{1,0:T(8,128)(2,1)S(1)}, bf16[2048,256]{1,0:T(8,128)(2,1)S(1)}, u32[]{:S(2)}, u32[]{:S(2)}) collective-permute-start(bf16[2048,256]{1,0:T(8,128)(2,1)S(1)} %constant_dynamic-update-slice_fusion.kv_ref), channel_id=1, source_target_pairs={{0,1},{1,0},{2,3},{3,2},{4,5},{5,4},{6,7},{7,6},{8,9},{9,8},{10,11... | collective-permute-start | bytes 3145736 | tf_op jit(solution)/shard_map/ppermute | solution.py:407
  55.9 0.0 copy-done.6
  56.0 0.0 copy-done.4
  56.0 0.0 copy-done.5
  56.0 47.2 %attend.2.rest_0_ = bf16[4,64,7424]{2,1,0:T(8,128)(2,1)} custom-call(s32[1]{0:T(128)} %bitcast.1.core_ref.half_ref, s32[4,16]{1,0:T(4,128)S(1)} %fusion.6.start_ref, s32[4]{0:T(128)S(1)} %copy-done.5, bf16[4,64,7424]{2,1,0:T(8,128)(2,1)} %q_hbm.3, bf16[2048,256]{1,0:T(8,128)(2,1)S(1)} %constant_dynamic-update-slice_fusion.kv_ref, ...), custom_call_target="tpu_custom_call" | custom-call | flops 2189426688 | bytes 3801088 | tf_op jit(solution)/shard_map/attend/pallas_call | solution.py:306
  103.2 0.0 collective-permute-done.23.kv_ref
  103.2 47.2 %attend.3 = bf16[4,64,7424]{2,1,0:T(8,128)(2,1)} custom-call(s32[1]{0:T(128)} %bitcast.half_ref, s32[4,16]{1,0:T(4,128)S(1)} %fusion.6.start_ref, s32[4]{0:T(128)S(1)} %copy-done.5, bf16[4,64,7424]{2,1,0:T(8,128)(2,1)} %q_hbm.3, bf16[2048,256]{1,0:T(8,128)(2,1)S(1)} %collective-permute-done.23.kv_ref, ...), custom_call_target="tpu_custom_call", output_to_operand_aliasing={{}: (6, {})} | custom-call | flops 2189426688 | bytes 3801088 | tf_op jit(solution)/shard_map/attend/pallas_call | solution.py:306
  (13 shorter events, 0.2 us)
Async XLA Ops:
  0.0 0.9 copy-start.3
  1.0 4.4 %copy-start = (bf16[4,128,4096]{2,1,0:T(8,128)(2,1)S(1)}, bf16[4,128,4096]{2,1,0:T(8,128)(2,1)}, u32[]{:S(2)}) copy-start(bf16[4,128,4096]{2,1,0:T(8,128)(2,1)} %states.1) | copy-start | bytes 12582916
  1.0 4.4 %copy-start.1 = (bf16[32,4096]{1,0:T(8,128)(2,1)S(1)}, bf16[32,4096]{1,0:T(8,128)(2,1)}, u32[]{:S(2)}) copy-start(bf16[32,4096]{1,0:T(8,128)(2,1)} %queries.1) | copy-start | bytes 786436
  1.0 4.4 %copy-start.2 = (bf16[4096]{0:T(1024)(128)(2,1)S(1)}, bf16[4096]{0:T(1024)(128)(2,1)}, u32[]{:S(2)}) copy-start(bf16[4096]{0:T(1024)(128)(2,1)} %gain.1) | copy-start | bytes 24580
  1.0 2.9 %collective-permute-start.1 = (bf16[256,256]{1,0:T(8,128)(2,1)S(1)}, bf16[256,256]{1,0:T(8,128)(2,1)S(1)}, u32[]{:S(2)}, u32[]{:S(2)}) collective-permute-start(bf16[256,256]{1,0:T(8,128)(2,1)S(1)} %get-tuple-element.18), channel_id=1, source_target_pairs={{0,1},{1,0},{2,3},{3,2},{4,5},{5,4},{6,7},{7,6},{8,9},{9,8},{10,11... | collective-permute-start | bytes 393224 | tf_op jit(solution)/shard_map/ppermute | solution.py:407
  1.1 7.3 %collective-permute-start.3 = (bf16[256,256]{1,0:T(8,128)(2,1)S(1)}, bf16[256,256]{1,0:T(8,128)(2,1)S(1)}, u32[]{:S(2)}, u32[]{:S(2)}) collective-permute-start(bf16[256,256]{1,0:T(8,128)(2,1)S(1)} %get-tuple-element.17.rest_0_), channel_id=1, source_target_pairs={{0,2},{1,3},{2,6},{3,7},{4,0},{5,1},{6,10},{7,11},{8,4},{9,5},{10,... | collective-permute-start | bytes 393224 | tf_op jit(solution)/shard_map/ppermute | solution.py:411
  3.8 4.7 %collective-permute-start = (bf16[256,256]{1,0:T(8,128)(2,1)S(1)}, bf16[256,256]{1,0:T(8,128)(2,1)S(1)}, u32[]{:S(2)}, u32[]{:S(2)}) collective-permute-start(bf16[256,256]{1,0:T(8,128)(2,1)S(1)} %get-tuple-element.17.rest_0_), channel_id=1, source_target_pairs={{0,4},{1,5},{2,0},{3,1},{4,8},{5,9},{6,2},{7,3},{8,12},{9,13},{10,... | collective-permute-start | bytes 393224 | tf_op jit(solution)/shard_map/ppermute | solution.py:411
  3.9 6.6 %collective-permute-start.4 = (bf16[256,256]{1,0:T(8,128)(2,1)S(1)}, bf16[256,256]{1,0:T(8,128)(2,1)S(1)}, u32[]{:S(2)}, u32[]{:S(2)}) collective-permute-start(bf16[256,256]{1,0:T(8,128)(2,1)S(1)} %collective-permute-done.1.rest_5_), channel_id=1, source_target_pairs={{0,2},{1,3},{2,6},{3,7},{4,0},{5,1},{6,10},{7,11},{8,4},{9,5},{10,... | collective-permute-start | bytes 393224 | tf_op jit(solution)/shard_map/ppermute | solution.py:411
  5.3 6.1 %collective-permute-start.2 = (bf16[256,256]{1,0:T(8,128)(2,1)S(1)}, bf16[256,256]{1,0:T(8,128)(2,1)S(1)}, u32[]{:S(2)}, u32[]{:S(2)}) collective-permute-start(bf16[256,256]{1,0:T(8,128)(2,1)S(1)} %collective-permute-done.1.rest_5_), channel_id=1, source_target_pairs={{0,4},{1,5},{2,0},{3,1},{4,8},{5,9},{6,2},{7,3},{8,12},{9,13},{10,... | collective-permute-start | bytes 393224 | tf_op jit(solution)/shard_map/ppermute | solution.py:411
  11.3 11.9 %collective-permute-start.5 = (bf16[128,4096]{1,0:T(8,128)(2,1)S(1)}, bf16[128,4096]{1,0:T(8,128)(2,1)S(1)}, u32[]{:S(2)}, u32[]{:S(2)}) collective-permute-start(bf16[128,4096]{1,0:T(8,128)(2,1)S(1)} %pool.1.own_ref), channel_id=1, source_target_pairs={{0,1},{1,0},{2,3},{3,2},{4,5},{5,4},{6,7},{7,6},{8,9},{9,8},{10,11... | collective-permute-start | bytes 3145736 | tf_op jit(solution)/shard_map/ppermute | solution.py:407
  12.5 5.1 %collective-permute-start.6 = (bf16[256,256]{1,0:T(8,128)(2,1)S(1)}, bf16[256,256]{1,0:T(8,128)(2,1)S(1)}, u32[]{:S(2)}, u32[]{:S(2)}) collective-permute-start(bf16[256,256]{1,0:T(8,128)(2,1)S(1)} %collective-permute-done.rest_1_), channel_id=1, source_target_pairs={{0,4},{1,5},{2,0},{3,1},{4,8},{5,9},{6,2},{7,3},{8,12},{9,13},{10,... | collective-permute-start | bytes 393224 | tf_op jit(solution)/shard_map/ppermute | solution.py:411
  12.6 7.8 %collective-permute-start.8 = (bf16[256,256]{1,0:T(8,128)(2,1)S(1)}, bf16[256,256]{1,0:T(8,128)(2,1)S(1)}, u32[]{:S(2)}, u32[]{:S(2)}) collective-permute-start(bf16[256,256]{1,0:T(8,128)(2,1)S(1)} %collective-permute-done.2.rest_6_), channel_id=1, source_target_pairs={{0,4},{1,5},{2,0},{3,1},{4,8},{5,9},{6,2},{7,3},{8,12},{9,13},{10,... | collective-permute-start | bytes 393224 | tf_op jit(solution)/shard_map/ppermute | solution.py:411
  14.1 6.5 %collective-permute-start.10 = (bf16[256,256]{1,0:T(8,128)(2,1)S(1)}, bf16[256,256]{1,0:T(8,128)(2,1)S(1)}, u32[]{:S(2)}, u32[]{:S(2)}) collective-permute-start(bf16[256,256]{1,0:T(8,128)(2,1)S(1)} %collective-permute-done.3.rest_2_), channel_id=1, source_target_pairs={{0,2},{1,3},{2,6},{3,7},{4,0},{5,1},{6,10},{7,11},{8,4},{9,5},{10,... | collective-permute-start | bytes 393224 | tf_op jit(solution)/shard_map/ppermute | solution.py:411
  14.1 7.9 %collective-permute-start.12 = (bf16[256,256]{1,0:T(8,128)(2,1)S(1)}, bf16[256,256]{1,0:T(8,128)(2,1)S(1)}, u32[]{:S(2)}, u32[]{:S(2)}) collective-permute-start(bf16[256,256]{1,0:T(8,128)(2,1)S(1)} %collective-permute-done.4.rest_7_), channel_id=1, source_target_pairs={{0,2},{1,3},{2,6},{3,7},{4,0},{5,1},{6,10},{7,11},{8,4},{9,5},{10,... | collective-permute-start | bytes 393224 | tf_op jit(solution)/shard_map/ppermute | solution.py:411
  17.6 6.1 %collective-permute-start.7 = (bf16[256,256]{1,0:T(8,128)(2,1)S(1)}, bf16[256,256]{1,0:T(8,128)(2,1)S(1)}, u32[]{:S(2)}, u32[]{:S(2)}) collective-permute-start(bf16[256,256]{1,0:T(8,128)(2,1)S(1)} %collective-permute-done.6.rest_3_), channel_id=1, source_target_pairs={{0,4},{1,5},{2,0},{3,1},{4,8},{5,9},{6,2},{7,3},{8,12},{9,13},{10,... | collective-permute-start | bytes 393224 | tf_op jit(solution)/shard_map/ppermute | solution.py:411
  20.4 4.8 %collective-permute-start.9 = (bf16[256,256]{1,0:T(8,128)(2,1)S(1)}, bf16[256,256]{1,0:T(8,128)(2,1)S(1)}, u32[]{:S(2)}, u32[]{:S(2)}) collective-permute-start(bf16[256,256]{1,0:T(8,128)(2,1)S(1)} %collective-permute-done.8.rest_8_), channel_id=1, source_target_pairs={{0,4},{1,5},{2,0},{3,1},{4,8},{5,9},{6,2},{7,3},{8,12},{9,13},{10,... | collective-permute-start | bytes 393224 | tf_op jit(solution)/shard_map/ppermute | solution.py:411
  20.5 4.7 %collective-permute-start.11 = (bf16[256,256]{1,0:T(8,128)(2,1)S(1)}, bf16[256,256]{1,0:T(8,128)(2,1)S(1)}, u32[]{:S(2)}, u32[]{:S(2)}) collective-permute-start(bf16[256,256]{1,0:T(8,128)(2,1)S(1)} %collective-permute-done.10.rest_4_), channel_id=1, source_target_pairs={{0,2},{1,3},{2,6},{3,7},{4,0},{5,1},{6,10},{7,11},{8,4},{9,5},{10,... | collective-permute-start | bytes 393224 | tf_op jit(solution)/shard_map/ppermute | solution.py:411
  21.9 5.0 %collective-permute-start.13 = (bf16[256,256]{1,0:T(8,128)(2,1)S(1)}, bf16[256,256]{1,0:T(8,128)(2,1)S(1)}, u32[]{:S(2)}, u32[]{:S(2)}) collective-permute-start(bf16[256,256]{1,0:T(8,128)(2,1)S(1)} %collective-permute-done.12.rest_9_), channel_id=1, source_target_pairs={{0,2},{1,3},{2,6},{3,7},{4,0},{5,1},{6,10},{7,11},{8,4},{9,5},{10,... | collective-permute-start | bytes 393224 | tf_op jit(solution)/shard_map/ppermute | solution.py:411
  23.7 32.2 %copy-start.6 = (s32[4,16]{1,0:T(4,128)S(1)}, s32[4,16]{1,0:T(4,128)}, u32[]{:S(2)}) copy-start(s32[4,16]{1,0:T(4,128)} %param.12) | copy-start | bytes 772
  23.8 32.2 %copy-start.4 = (bf16[4,64,512]{2,1,0:T(8,128)(2,1)S(1)}, bf16[4,64,512]{2,1,0:T(8,128)(2,1)}, u32[]{:S(2)}) copy-start(bf16[4,64,512]{2,1,0:T(8,128)(2,1)} %own_kv_ref.3) | copy-start | bytes 786436
  23.8 32.2 %copy-start.5 = (s32[4]{0:T(128)S(1)}, s32[4]{0:T(128)}, u32[]{:S(2)}) copy-start(s32[4]{0:T(128)} %length_ref.3) | copy-start | bytes 52
  26.9 3.8 %collective-permute-start.14 = (bf16[256,256]{1,0:T(8,128)(2,1)S(1)}, bf16[256,256]{1,0:T(8,128)(2,1)S(1)}, u32[]{:S(2)}, u32[]{:S(2)}) collective-permute-start(bf16[256,256]{1,0:T(8,128)(2,1)S(1)} %collective-permute-done.7.rest_0_), channel_id=1, source_target_pairs={{0,4},{1,5},{2,0},{3,1},{4,8},{5,9},{6,2},{7,3},{8,12},{9,13},{10,... | collective-permute-start | bytes 393224 | tf_op jit(solution)/shard_map/ppermute | solution.py:411
  28.4 4.1 %collective-permute-start.15 = (bf16[256,256]{1,0:T(8,128)(2,1)S(1)}, bf16[256,256]{1,0:T(8,128)(2,1)S(1)}, u32[]{:S(2)}, u32[]{:S(2)}) collective-permute-start(bf16[256,256]{1,0:T(8,128)(2,1)S(1)} %collective-permute-done.13.rest_4_), channel_id=1, source_target_pairs={{0,2},{1,3},{2,6},{3,7},{4,0},{5,1},{6,10},{7,11},{8,4},{9,5},{10,... | collective-permute-start | bytes 393224 | tf_op jit(solution)/shard_map/ppermute | solution.py:411
  32.9 5.0 %collective-permute-start.18 = (bf16[256,256]{1,0:T(8,128)(2,1)S(1)}, bf16[256,256]{1,0:T(8,128)(2,1)S(1)}, u32[]{:S(2)}, u32[]{:S(2)}) collective-permute-start(bf16[256,256]{1,0:T(8,128)(2,1)S(1)} %project.3), channel_id=1, source_target_pairs={{0,12},{1,13},{2,14},{3,15},{4,0},{5,1},{6,2},{7,3},{8,4},{9,5},{1... | collective-permute-start | bytes 393224 | tf_op jit(solution)/shard_map/ppermute | solution.py:411
  35.9 11.2 %collective-permute-start.17 = (bf16[256,256]{1,0:T(8,128)(2,1)S(1)}, bf16[256,256]{1,0:T(8,128)(2,1)S(1)}, u32[]{:S(2)}, u32[]{:S(2)}) collective-permute-start(bf16[256,256]{1,0:T(8,128)(2,1)S(1)} %project.3), channel_id=1, source_target_pairs={{0,8},{1,9},{2,10},{3,11},{4,12},{5,13},{6,14},{7,15},{8,0},{9,1},... | collective-permute-start | bytes 393224 | tf_op jit(solution)/shard_map/ppermute | solution.py:411
  35.9 11.2 %collective-permute-start.16 = (bf16[256,256]{1,0:T(8,128)(2,1)S(1)}, bf16[256,256]{1,0:T(8,128)(2,1)S(1)}, u32[]{:S(2)}, u32[]{:S(2)}) collective-permute-start(bf16[256,256]{1,0:T(8,128)(2,1)S(1)} %project.3), channel_id=1, source_target_pairs={{0,4},{1,5},{2,6},{3,7},{4,8},{5,9},{6,10},{7,11},{8,12},{9,13},{1... | collective-permute-start | bytes 393224 | tf_op jit(solution)/shard_map/ppermute | solution.py:411
  36.4 12.2 %collective-permute-start.19 = (bf16[256,256]{1,0:T(8,128)(2,1)S(1)}, bf16[256,256]{1,0:T(8,128)(2,1)S(1)}, u32[]{:S(2)}, u32[]{:S(2)}) collective-permute-start(bf16[256,256]{1,0:T(8,128)(2,1)S(1)} %project.3), channel_id=1, source_target_pairs={{0,2},{1,3},{2,0},{3,1},{4,6},{5,7},{6,4},{7,5},{8,10},{9,11},{10,... | collective-permute-start | bytes 393224 | tf_op jit(solution)/shard_map/ppermute | solution.py:411
  37.8 14.9 %collective-permute-start.22 = (bf16[256,256]{1,0:T(8,128)(2,1)S(1)}, bf16[256,256]{1,0:T(8,128)(2,1)S(1)}, u32[]{:S(2)}, u32[]{:S(2)}) collective-permute-start(bf16[256,256]{1,0:T(8,128)(2,1)S(1)} %collective-permute-done.18), channel_id=1, source_target_pairs={{0,2},{1,3},{2,0},{3,1},{4,6},{5,7},{6,4},{7,5},{8,10},{9,11},{10,... | collective-permute-start | bytes 393224 | tf_op jit(solution)/shard_map/ppermute | solution.py:411
  47.1 5.6 %collective-permute-start.21 = (bf16[256,256]{1,0:T(8,128)(2,1)S(1)}, bf16[256,256]{1,0:T(8,128)(2,1)S(1)}, u32[]{:S(2)}, u32[]{:S(2)}) collective-permute-start(bf16[256,256]{1,0:T(8,128)(2,1)S(1)} %collective-permute-done.17), channel_id=1, source_target_pairs={{0,2},{1,3},{2,0},{3,1},{4,6},{5,7},{6,4},{7,5},{8,10},{9,11},{10,... | collective-permute-start | bytes 393224 | tf_op jit(solution)/shard_map/ppermute | solution.py:411
  47.1 5.6 %collective-permute-start.20 = (bf16[256,256]{1,0:T(8,128)(2,1)S(1)}, bf16[256,256]{1,0:T(8,128)(2,1)S(1)}, u32[]{:S(2)}, u32[]{:S(2)}) collective-permute-start(bf16[256,256]{1,0:T(8,128)(2,1)S(1)} %collective-permute-done.16), channel_id=1, source_target_pairs={{0,2},{1,3},{2,0},{3,1},{4,6},{5,7},{6,4},{7,5},{8,10},{9,11},{10,... | collective-permute-start | bytes 393224 | tf_op jit(solution)/shard_map/ppermute | solution.py:411
  52.8 50.4 %collective-permute-start.23 = (bf16[2048,256]{1,0:T(8,128)(2,1)S(1)}, bf16[2048,256]{1,0:T(8,128)(2,1)S(1)}, u32[]{:S(2)}, u32[]{:S(2)}) collective-permute-start(bf16[2048,256]{1,0:T(8,128)(2,1)S(1)} %constant_dynamic-update-slice_fusion.kv_ref), channel_id=1, source_target_pairs={{0,1},{1,0},{2,3},{3,2},{4,5},{5,4},{6,7},{7,6},{8,9},{9,8},{10,11... | collective-permute-start | bytes 3145736 | tf_op jit(solution)/shard_map/ppermute | solution.py:407

commit v13 on v12

--- a/solution.py
+++ b/solution.py
@@ -32,7 +32,7 @@
 FIRST_COST = 8 * 10**9
 PROJECT_COST = 8
 CHIP = 8
-STEP = 4
+STEP = 5
 BLOCK = 16
 MIB = 1024 * 1024
 
@@ -129,28 +129,21 @@
     )(states, queries, gain)
 
 
-def attend_kernel(half_ref, start_ref, length_ref, q_hbm, kv_ref, own_kv_ref, *rest):
-    out_hbm = rest[-13]
+def attend_kernel(half_ref, start_ref, length_ref, q_ref, kv_ref, own_kv_ref, *rest):
+    out_hbm = rest[-11]
     (
-        questions, answers, memory, key_side, value_side, weights, bias, marker, scores, all_weights,
-        arrived, sent,
-    ) = rest[-12:]
-    count = q_hbm.shape[0]
+        answers, memory, key_side, value_side, weights, bias, marker, scores, all_weights, sent,
+    ) = rest[-10:]
+    count = q_ref.shape[0]
     half_at = pl.multiple_of(half_ref[0] * HALF, LANES)
     own_at = pl.multiple_of(half_ref[0] * LANES, LANES)
     factor = math.log2(math.e) / math.sqrt(HD)
-
-    def fetch(query):
-        return pltpu.make_async_copy(
-            q_hbm.at[query, :, pl.ds(half_at, HALF)], questions.at[query], arrived.at[query]
-        )
 
     def send(query):
         return pltpu.make_async_copy(
             answers.at[query], out_hbm.at[query, :, pl.ds(half_at, HALF)], sent.at[query]
         )
 
-    fetch(0).start()
     lane = lax.broadcasted_iota(jnp.int32, (KEYS, LANES), 1)
     row = lax.broadcasted_iota(jnp.int32, (KEYS, LANES), 0)
     in_b = ((row >= ROWS) & (row < 2 * ROWS)) | (row >= 2 * ROWS + QLEN)
@@ -190,14 +183,10 @@
         alive = token < length
         sample = lax.div(key, HD // STEP)
 
-        fetch(query).wait()
-
-        @pl.when(query + 1 < count)
-        def _():
-            fetch(query + 1).start()
-
         def stacked(tiles):
-            return jnp.concatenate([questions[query, :, t * LANES:(t + 1) * LANES] for t in tiles], axis=0)
+            return jnp.concatenate(
+                [q_ref[query, :, pl.ds(pl.multiple_of(half_at + t * LANES, LANES), LANES)] for t in tiles], axis=0
+            )
 
         def key_product(i):
             g, tiles = chunks[i]
@@ -297,7 +286,7 @@
     count = questions.shape[0]
     hbm, vmem, smem = (pl.BlockSpec(memory_space=x) for x in (pltpu.HBM, pltpu.VMEM, pltpu.SMEM))
     operands = [half.reshape(1), starts, lengths, questions, memory_kv, own_kv]
-    in_specs = [smem, smem, smem, hbm, vmem, vmem]
+    in_specs = [smem, smem, smem, vmem, vmem, vmem]
     aliases = {}
     if earlier is not None:
         aliases = {len(operands): 0}
@@ -310,7 +299,6 @@
         out_shape=jax.ShapeDtypeStruct((count, QLEN, H * HD), jnp.bfloat16),
         scratch_shapes=[
             pltpu.VMEM((count, QLEN, HALF), jnp.bfloat16),
-            pltpu.VMEM((count, QLEN, HALF), jnp.bfloat16),
             pltpu.VMEM((ROWS, 2 * LANES), jnp.bfloat16),
             pltpu.VMEM((2, LANES, KEYS), jnp.bfloat16),
             pltpu.VMEM((2, KEYS, 2 * LANES), jnp.bfloat16),
@@ -320,10 +308,9 @@
             pltpu.VMEM((STEP * QLEN, KEYS), jnp.float32),
             pltpu.VMEM((STEP * QLEN, KEYS), jnp.bfloat16),
             pltpu.SemaphoreType.DMA((count,)),
-            pltpu.SemaphoreType.DMA((count,)),
         ],
         input_output_aliases=aliases,
-        compiler_params=pltpu.CompilerParams(vmem_limit_bytes=50 * MIB),
+        compiler_params=pltpu.CompilerParams(vmem_limit_bytes=48 * MIB),
         cost_estimate=pl.CostEstimate(
             flops=2 * count * QLEN * H * HD * (ROWS + QLEN),
             bytes_accessed=2 * count * QLEN * H * HD,
@@ -415,10 +402,15 @@
 
     def line_by_line(block):
         lines = chips // 2
-        blocks = [block]
-        for k in range(1, lines):
-            blocks.append(along(block, lambda line, lane: 2 * ((line + k) % lines) + lane))
-        return blocks + [along(x, lambda line, lane: 2 * line + 1 - lane) for x in blocks]
+
+        def lane_of(x):
+            return along(x, lambda line, lane: 2 * line + 1 - lane)
+
+        near = {k: along(block, lambda line, lane: 2 * ((line + k) % lines) + lane) for k in (2, 1, 3)}
+        far = {0: lane_of(block)}
+        far[3] = along(block, lambda line, lane: 2 * ((line + 3) % lines) + 1 - lane)
+        far[1], far[2] = lane_of(near[1]), lane_of(near[2])
+        return [block, near[1], near[2], near[3], far[0], far[1], far[2], far[3]]
 
     mine, theirs = split(core, kv_weight)
     up = [[mine], [to_partner(theirs)]]
@@ -439,20 +431,15 @@
             up[part].append(along_ring(up[part][-1], 1))
             down[part].append(along_ring(down[part][-1], -1))
         if turn == 1:
-            beside = rows = pool(passage_states, memory_queries, memory_gain)
-        elif turn == 3:
-            beside = project(chips, core, place, rows, other_rows, blocks((0, 1, 2)))
-        else:
-            continue
-        *hops, beside = lax.optimization_barrier((*(x[-1] for x in up + down), beside))
-        for chain, hop in zip(up + down, hops):
-            chain[-1] = hop
-        if turn == 1:
-            rows = beside
+            rows = pool(passage_states, memory_queries, memory_gain)
+            *hops, rows = lax.optimization_barrier((*(x[-1] for x in up + down), rows))
+            for chain, hop in zip(up + down, hops):
+                chain[-1] = hop
             other_rows = to_partner(rows)
     up[0].append(along_ring(up[0][-1], 1))
     down[1].append(along_ring(down[1][-1], -1))
-    memory_kv = project(chips, core, place, rows, other_rows, blocks((3, 4)), beside)
+    early = project(chips, core, place, rows, other_rows, blocks((0, 1, 2)))
+    memory_kv = project(chips, core, place, rows, other_rows, blocks((3, 4)), early)
     near = jnp.concatenate(line_by_line(memory_kv), axis=0)
     far = to_partner(near)
 

time: 151 us -> 145 us (0.960)
  waiting for transfers between devices: 29.5 us -> 17.9 us
  starting transfers between devices: 21.2 us -> 26 us
  Pallas kernels: 98.4 us -> 95.9 us
  local copies, waits for them, and re-layouts: 1.06 us -> 3.14 us
    ppermute x21, waiting for transfers between devices: 29.5 us -> 17.9 us  [along(): lax.ppermute(x, 'pass', [(2 * s + c, 2 * d + c) for s, d in pairs for c i...]
    ppermute x21, starting transfers between devices: 16.7 us -> 21.2 us  [along(): lax.ppermute(x, 'pass', [(2 * s + c, 2 * d + c) for s, d in pairs for c i...]
    pallas_call x2, Pallas kernels: 94.4 us -> 90.9 us  [attend(): pl.pallas_call(attend_kernel, in_specs=in_specs, out_specs=hbm, out_shape...]
    unnamed x21 -> x25, local copies, waits for them, and re-layouts: 1.05 us -> 3.13 us
  transfers between devices with their start and end apart: 24 -> 24, of which waited for: 12 -> 13; matrix products, arithmetic and copies ran while one was open for 0% -> 0% of each run, Pallas kernels for 34% -> 34%
where the time goes in v13:
time: 145 us; the launch traced here: 143 us
  Pallas kernels  95.9 us (66%)
  starting transfers between devices  26 us (18%)
  waiting for transfers between devices  17.9 us (12%)
  local copies, waits for them, and re-layouts  3.14 us (2%)
    pallas_call x2, Pallas kernels, attend(): pl.pallas_call(attend_kernel, in_specs=in_specs, out_specs=hbm, out_shape...  90.9 us
    ppermute x21, starting transfers between devices, along(): lax.ppermute(x, 'pass', [(2 * s + c, 2 * d + c) for s, d in pairs for c i...  21.2 us
    ppermute x21, waiting for transfers between devices, along(): lax.ppermute(x, 'pass', [(2 * s + c, 2 * d + c) for s, d in pairs for c i...  17.9 us
    ppermute x3, starting transfers between devices, to_partner(): return lax.ppermute(x, 'pass', [(i, i ^ 1) for i in range(extent)])  4.8 us
    unnamed x25, local copies, waits for them, and re-layouts  3.13 us
    pallas_call x1, Pallas kernels, pool(): pl.pallas_call(pool_kernel, in_specs=[vmem] * 3, out_specs=vmem, out_shap...  3.08 us
  transfers between devices with their start and end apart: 24, of which 13 were waited for; matrix products, arithmetic and copies ran while one was open for 0% of the time, Pallas kernels for 34%

profile of v13, /device:TPU:1, one launch (start us, length us, event | category | flops | bytes accessed | tf_op | source)
XLA Modules:
  0.0 143.3 jit_solution(6406562797309491908)
XLA Ops:
  0.0 0.9 copy-done.5
  1.0 0.1 collective-permute-start.1
  1.1 2.7 %collective-permute-start.3 = (bf16[256,256]{1,0:T(8,128)(2,1)S(1)}, bf16[256,256]{1,0:T(8,128)(2,1)S(1)}, u32[]{:S(2)}, u32[]{:S(2)}) collective-permute-start(bf16[256,256]{1,0:T(8,128)(2,1)S(1)} %get-tuple-element.12.rest_0_), channel_id=1, source_target_pairs={{0,2},{1,3},{2,6},{3,7},{4,0},{5,1},{6,10},{7,11},{8,4},{9,5},{10,... | collective-permute-start | bytes 393224 | tf_op jit(solution)/shard_map/ppermute | solution.py:398
  3.8 0.1 collective-permute-start
  3.9 0.0 collective-permute-done.1.rest_5_
  3.9 1.4 collective-permute-start.4
  5.3 0.1 collective-permute-start.2
  5.3 0.0 copy-done
  5.4 0.0 copy-done.2
  5.4 3.1 %pool.1.own_ref = bf16[128,4096]{1,0:T(8,128)(2,1)S(1)} custom-call(bf16[4,128,4096]{2,1,0:T(8,128)(2,1)S(1)} %copy-done, bf16[32,4096]{1,0:T(8,128)(2,1)S(1)} %copy-done.1, bf16[4096]{0:T(1024)(128)(2,1)S(1)} %copy-done.2), custom_call_target="tpu_custom_call" | custom-call | flops 268435456 | bytes 4194304 | tf_op jit(solution)/shard_map/pool/pallas_call | solution.py:117
  8.4 0.0 collective-permute-done.3.rest_2_
  8.5 0.1 collective-permute-done.rest_1_
  8.5 2.0 %collective-permute-done.4.rest_7_ = bf16[256,256]{1,0:T(8,128)(2,1)S(1)} collective-permute-done((bf16[256,256]{1,0:T(8,128)(2,1)S(1)}, bf16[256,256]{1,0:T(8,128)(2,1)S(1)}, u32[]{:S(2)}, u32[]{:S(2)}) %collective-permute-start.4) | collective-permute-done | bytes 131104 | tf_op jit(solution)/shard_map/ppermute | solution.py:398
  10.5 0.9 collective-permute-done.2.rest_6_
  11.3 1.2 collective-permute-start.5
  12.5 0.1 collective-permute-start.6
  12.6 1.4 collective-permute-start.13
  14.0 1.3 collective-permute-start.8
  15.3 0.2 collective-permute-start.11
  15.4 2.2 %collective-permute-done.6.rest_3_ = bf16[256,256]{1,0:T(8,128)(2,1)S(1)} collective-permute-done((bf16[256,256]{1,0:T(8,128)(2,1)S(1)}, bf16[256,256]{1,0:T(8,128)(2,1)S(1)}, u32[]{:S(2)}, u32[]{:S(2)}) %collective-permute-start.6) | collective-permute-done | bytes 131104 | tf_op jit(solution)/shard_map/ppermute | solution.py:398
  17.6 0.1 collective-permute-start.7
  17.7 0.0 collective-permute-done.13.rest_9_
  17.7 1.4 collective-permute-start.14
  19.1 1.1 collective-permute-done.8.rest_4_
  20.2 1.4 collective-permute-start.9
  21.6 0.0 collective-permute-done.11.rest_8_
  21.6 0.1 collective-permute-start.12
  21.7 1.3 collective-permute-done.7.rest_0_
  23.0 0.2 collective-permute-start.10
  23.2 0.0 collective-permute-done.14.rest_4_
  23.2 1.3 collective-permute-start.15
  24.4 0.0 collective-permute-done.5.other_ref
  24.4 0.5 project.2.rest_6_
  25.0 0.0 copy-start.8
  25.0 0.0 copy-start.6
  25.0 0.0 copy-start.7
  25.0 0.4 collective-permute-done.9.rest_1_
  25.4 0.3 collective-permute-done.12.rest_3_
  25.7 1.9 %collective-permute-done.10.rest_2_ = bf16[256,256]{1,0:T(8,128)(2,1)S(1)} collective-permute-done((bf16[256,256]{1,0:T(8,128)(2,1)S(1)}, bf16[256,256]{1,0:T(8,128)(2,1)S(1)}, u32[]{:S(2)}, u32[]{:S(2)}) %collective-permute-start.10) | collective-permute-done | bytes 131104 | tf_op jit(solution)/shard_map/ppermute | solution.py:398
  27.6 0.4 collective-permute-done.15.rest_5_
  28.0 1.3 project.3
  29.3 2.5 %collective-permute-start.17 = (bf16[256,256]{1,0:T(8,128)(2,1)S(1)}, bf16[256,256]{1,0:T(8,128)(2,1)S(1)}, u32[]{:S(2)}, u32[]{:S(2)}) collective-permute-start(bf16[256,256]{1,0:T(8,128)(2,1)S(1)} %project.3), channel_id=1, source_target_pairs={{0,8},{1,9},{2,10},{3,11},{4,12},{5,13},{6,14},{7,15},{8,0},{9,1},... | collective-permute-start | bytes 393224 | tf_op jit(solution)/shard_map/ppermute | solution.py:398
  31.8 1.3 collective-permute-start.16
  33.1 2.9 %collective-permute-start.22 = (bf16[256,256]{1,0:T(8,128)(2,1)S(1)}, bf16[256,256]{1,0:T(8,128)(2,1)S(1)}, u32[]{:S(2)}, u32[]{:S(2)}) collective-permute-start(bf16[256,256]{1,0:T(8,128)(2,1)S(1)} %project.3), channel_id=1, source_target_pairs={{0,14},{1,15},{2,12},{3,13},{4,2},{5,3},{6,0},{7,1},{8,6},{9,7},{1... | collective-permute-start | bytes 393224 | tf_op jit(solution)/shard_map/ppermute | solution.py:398
  36.0 0.2 collective-permute-start.19
  36.3 0.0 collective-permute-start.18
  36.3 0.0 collective-permute-done.17
  36.3 1.2 collective-permute-start.21
  37.6 0.6 collective-permute-done.16
  38.2 1.4 collective-permute-start.20
  39.6 4.5 %collective-permute-done.18 = bf16[256,256]{1,0:T(8,128)(2,1)S(1)} collective-permute-done((bf16[256,256]{1,0:T(8,128)(2,1)S(1)}, bf16[256,256]{1,0:T(8,128)(2,1)S(1)}, u32[]{:S(2)}, u32[]{:S(2)}) %collective-permute-start.18) | collective-permute-done | bytes 131104 | tf_op jit(solution)/shard_map/ppermute | solution.py:398
  44.1 0.0 collective-permute-done.19
  44.1 2.4 %collective-permute-done.20 = bf16[256,256]{1,0:T(8,128)(2,1)S(1)} collective-permute-done((bf16[256,256]{1,0:T(8,128)(2,1)S(1)}, bf16[256,256]{1,0:T(8,128)(2,1)S(1)}, u32[]{:S(2)}, u32[]{:S(2)}) %collective-permute-start.20) | collective-permute-done | bytes 131104 | tf_op jit(solution)/shard_map/ppermute | solution.py:398
  46.5 0.0 collective-permute-done.21
  46.5 0.0 collective-permute-done.22
  46.6 3.5 %collective-permute-start.23 = (bf16[2048,256]{1,0:T(8,128)(2,1)S(1)}, bf16[2048,256]{1,0:T(8,128)(2,1)S(1)}, u32[]{:S(2)}, u32[]{:S(2)}) collective-permute-start(bf16[2048,256]{1,0:T(8,128)(2,1)S(1)} %constant_dynamic-update-slice_fusion.kv_ref), channel_id=1, source_target_pairs={{0,1},{1,0},{2,3},{3,2},{4,5},{5,4},{6,7},{7,6},{8,9},{9,8},{10,11... | collective-permute-start | bytes 3145736 | tf_op jit(solution)/shard_map/ppermute | solution.py:394
  50.1 0.0 copy-done.6
  50.1 0.0 copy-done.7
  50.1 0.0 copy-start.3
  50.1 2.1 %copy-done.3 = bf16[4,64,7424]{2,1,0:T(8,128)(2,1)S(1)} copy-done((bf16[4,64,7424]{2,1,0:T(8,128)(2,1)S(1)}, bf16[4,64,7424]{2,1,0:T(8,128)(2,1)}, u32[]{:S(2)}) %copy-start.3) | copy-done | bytes 3801112
  52.2 45.3 %attend.2.rest_0_ = bf16[4,64,7424]{2,1,0:T(8,128)(2,1)} custom-call(s32[1]{0:T(128)} %bitcast.1.core_ref.half_ref, s32[4,16]{1,0:T(4,128)S(1)} %fusion.6.start_ref, s32[4]{0:T(128)S(1)} %copy-done.7, bf16[4,64,7424]{2,1,0:T(8,128)(2,1)S(1)} %copy-done.3, bf16[2048,256]{1,0:T(8,128)(2,1)S(1)} %constant_dynamic-update-slice_fusion.kv_ref, ...), custom_call_target="tpu_custom_call" | custom-call | flops 2189426688 | bytes 3801088 | tf_op jit(solution)/shard_map/attend/pallas_call | solution.py:295
  97.5 0.0 collective-permute-done.23.kv_ref
  97.5 0.0 copy-done.4
  97.6 45.6 %attend.3 = bf16[4,64,7424]{2,1,0:T(8,128)(2,1)} custom-call(s32[1]{0:T(128)} %bitcast.half_ref, s32[4,16]{1,0:T(4,128)S(1)} %fusion.6.start_ref, s32[4]{0:T(128)S(1)} %copy-done.7, bf16[4,64,7424]{2,1,0:T(8,128)(2,1)S(1)} %copy-done.4, bf16[2048,256]{1,0:T(8,128)(2,1)S(1)} %collective-permute-done.23.kv_ref, ...), custom_call_target="tpu_custom_call", output_to_operand_aliasing={{}: (6, {})} | custom-call | flops 2189426688 | bytes 3801088 | tf_op jit(solution)/shard_map/attend/pallas_call | solution.py:295
  (17 shorter events, 0.2 us)
Async XLA Ops:
  0.0 0.9 copy-start.5
  1.0 4.4 %copy-start = (bf16[4,128,4096]{2,1,0:T(8,128)(2,1)S(1)}, bf16[4,128,4096]{2,1,0:T(8,128)(2,1)}, u32[]{:S(2)}) copy-start(bf16[4,128,4096]{2,1,0:T(8,128)(2,1)} %states.1) | copy-start | bytes 12582916
  1.0 4.4 %copy-start.1 = (bf16[32,4096]{1,0:T(8,128)(2,1)S(1)}, bf16[32,4096]{1,0:T(8,128)(2,1)}, u32[]{:S(2)}) copy-start(bf16[32,4096]{1,0:T(8,128)(2,1)} %queries.1) | copy-start | bytes 786436
  1.0 4.4 %copy-start.2 = (bf16[4096]{0:T(1024)(128)(2,1)S(1)}, bf16[4096]{0:T(1024)(128)(2,1)}, u32[]{:S(2)}) copy-start(bf16[4096]{0:T(1024)(128)(2,1)} %gain.1) | copy-start | bytes 24580
  1.0 2.9 %collective-permute-start.1 = (bf16[256,256]{1,0:T(8,128)(2,1)S(1)}, bf16[256,256]{1,0:T(8,128)(2,1)S(1)}, u32[]{:S(2)}, u32[]{:S(2)}) collective-permute-start(bf16[256,256]{1,0:T(8,128)(2,1)S(1)} %get-tuple-element.13), channel_id=1, source_target_pairs={{0,1},{1,0},{2,3},{3,2},{4,5},{5,4},{6,7},{7,6},{8,9},{9,8},{10,11... | collective-permute-start | bytes 393224 | tf_op jit(solution)/shard_map/ppermute | solution.py:394
  1.1 7.3 %collective-permute-start.3 = (bf16[256,256]{1,0:T(8,128)(2,1)S(1)}, bf16[256,256]{1,0:T(8,128)(2,1)S(1)}, u32[]{:S(2)}, u32[]{:S(2)}) collective-permute-start(bf16[256,256]{1,0:T(8,128)(2,1)S(1)} %get-tuple-element.12.rest_0_), channel_id=1, source_target_pairs={{0,2},{1,3},{2,6},{3,7},{4,0},{5,1},{6,10},{7,11},{8,4},{9,5},{10,... | collective-permute-start | bytes 393224 | tf_op jit(solution)/shard_map/ppermute | solution.py:398
  3.8 4.7 %collective-permute-start = (bf16[256,256]{1,0:T(8,128)(2,1)S(1)}, bf16[256,256]{1,0:T(8,128)(2,1)S(1)}, u32[]{:S(2)}, u32[]{:S(2)}) collective-permute-start(bf16[256,256]{1,0:T(8,128)(2,1)S(1)} %get-tuple-element.12.rest_0_), channel_id=1, source_target_pairs={{0,4},{1,5},{2,0},{3,1},{4,8},{5,9},{6,2},{7,3},{8,12},{9,13},{10,... | collective-permute-start | bytes 393224 | tf_op jit(solution)/shard_map/ppermute | solution.py:398
  3.9 6.6 %collective-permute-start.4 = (bf16[256,256]{1,0:T(8,128)(2,1)S(1)}, bf16[256,256]{1,0:T(8,128)(2,1)S(1)}, u32[]{:S(2)}, u32[]{:S(2)}) collective-permute-start(bf16[256,256]{1,0:T(8,128)(2,1)S(1)} %collective-permute-done.1.rest_5_), channel_id=1, source_target_pairs={{0,2},{1,3},{2,6},{3,7},{4,0},{5,1},{6,10},{7,11},{8,4},{9,5},{10,... | collective-permute-start | bytes 393224 | tf_op jit(solution)/shard_map/ppermute | solution.py:398
  5.3 6.1 %collective-permute-start.2 = (bf16[256,256]{1,0:T(8,128)(2,1)S(1)}, bf16[256,256]{1,0:T(8,128)(2,1)S(1)}, u32[]{:S(2)}, u32[]{:S(2)}) collective-permute-start(bf16[256,256]{1,0:T(8,128)(2,1)S(1)} %collective-permute-done.1.rest_5_), channel_id=1, source_target_pairs={{0,4},{1,5},{2,0},{3,1},{4,8},{5,9},{6,2},{7,3},{8,12},{9,13},{10,... | collective-permute-start | bytes 393224 | tf_op jit(solution)/shard_map/ppermute | solution.py:398
  11.3 13.1 %collective-permute-start.5 = (bf16[128,4096]{1,0:T(8,128)(2,1)S(1)}, bf16[128,4096]{1,0:T(8,128)(2,1)S(1)}, u32[]{:S(2)}, u32[]{:S(2)}) collective-permute-start(bf16[128,4096]{1,0:T(8,128)(2,1)S(1)} %pool.1.own_ref), channel_id=1, source_target_pairs={{0,1},{1,0},{2,3},{3,2},{4,5},{5,4},{6,7},{7,6},{8,9},{9,8},{10,11... | collective-permute-start | bytes 3145736 | tf_op jit(solution)/shard_map/ppermute | solution.py:394
  12.5 5.1 %collective-permute-start.6 = (bf16[256,256]{1,0:T(8,128)(2,1)S(1)}, bf16[256,256]{1,0:T(8,128)(2,1)S(1)}, u32[]{:S(2)}, u32[]{:S(2)}) collective-permute-start(bf16[256,256]{1,0:T(8,128)(2,1)S(1)} %collective-permute-done.rest_1_), channel_id=1, source_target_pairs={{0,4},{1,5},{2,0},{3,1},{4,8},{5,9},{6,2},{7,3},{8,12},{9,13},{10,... | collective-permute-start | bytes 393224 | tf_op jit(solution)/shard_map/ppermute | solution.py:398
  12.6 5.1 %collective-permute-start.13 = (bf16[256,256]{1,0:T(8,128)(2,1)S(1)}, bf16[256,256]{1,0:T(8,128)(2,1)S(1)}, u32[]{:S(2)}, u32[]{:S(2)}) collective-permute-start(bf16[256,256]{1,0:T(8,128)(2,1)S(1)} %collective-permute-done.4.rest_7_), channel_id=1, source_target_pairs={{0,2},{1,3},{2,6},{3,7},{4,0},{5,1},{6,10},{7,11},{8,4},{9,5},{10,... | collective-permute-start | bytes 393224 | tf_op jit(solution)/shard_map/ppermute | solution.py:398
  14.0 6.2 %collective-permute-start.8 = (bf16[256,256]{1,0:T(8,128)(2,1)S(1)}, bf16[256,256]{1,0:T(8,128)(2,1)S(1)}, u32[]{:S(2)}, u32[]{:S(2)}) collective-permute-start(bf16[256,256]{1,0:T(8,128)(2,1)S(1)} %collective-permute-done.3.rest_2_), channel_id=1, source_target_pairs={{0,2},{1,3},{2,6},{3,7},{4,0},{5,1},{6,10},{7,11},{8,4},{9,5},{10,... | collective-permute-start | bytes 393224 | tf_op jit(solution)/shard_map/ppermute | solution.py:398
  15.3 6.3 %collective-permute-start.11 = (bf16[256,256]{1,0:T(8,128)(2,1)S(1)}, bf16[256,256]{1,0:T(8,128)(2,1)S(1)}, u32[]{:S(2)}, u32[]{:S(2)}) collective-permute-start(bf16[256,256]{1,0:T(8,128)(2,1)S(1)} %collective-permute-done.2.rest_6_), channel_id=1, source_target_pairs={{0,4},{1,5},{2,0},{3,1},{4,8},{5,9},{6,2},{7,3},{8,12},{9,13},{10,... | collective-permute-start | bytes 393224 | tf_op jit(solution)/shard_map/ppermute | solution.py:398
  17.6 5.3 %collective-permute-start.7 = (bf16[256,256]{1,0:T(8,128)(2,1)S(1)}, bf16[256,256]{1,0:T(8,128)(2,1)S(1)}, u32[]{:S(2)}, u32[]{:S(2)}) collective-permute-start(bf16[256,256]{1,0:T(8,128)(2,1)S(1)} %collective-permute-done.6.rest_3_), channel_id=1, source_target_pairs={{0,4},{1,5},{2,0},{3,1},{4,8},{5,9},{6,2},{7,3},{8,12},{9,13},{10,... | collective-permute-start | bytes 393224 | tf_op jit(solution)/shard_map/ppermute | solution.py:398
  17.7 5.4 %collective-permute-start.14 = (bf16[256,256]{1,0:T(8,128)(2,1)S(1)}, bf16[256,256]{1,0:T(8,128)(2,1)}, u32[]{:S(2)}, u32[]{:S(2)}) collective-permute-start(bf16[256,256]{1,0:T(8,128)(2,1)S(1)} %collective-permute-done.13.rest_9_), channel_id=1, source_target_pairs={{0,2},{1,3},{2,6},{3,7},{4,0},{5,1},{6,10},{7,11},{8,4},{9,5},{10,... | collective-permute-start | bytes 393224 | tf_op jit(solution)/shard_map/ppermute | solution.py:398
  20.2 5.2 %collective-permute-start.9 = (bf16[256,256]{1,0:T(8,128)(2,1)S(1)}, bf16[256,256]{1,0:T(8,128)(2,1)S(1)}, u32[]{:S(2)}, u32[]{:S(2)}) collective-permute-start(bf16[256,256]{1,0:T(8,128)(2,1)S(1)} %collective-permute-done.8.rest_4_), channel_id=1, source_target_pairs={{0,2},{1,3},{2,6},{3,7},{4,0},{5,1},{6,10},{7,11},{8,4},{9,5},{10,... | collective-permute-start | bytes 393224 | tf_op jit(solution)/shard_map/ppermute | solution.py:398
  21.6 4.1 %collective-permute-start.12 = (bf16[256,256]{1,0:T(8,128)(2,1)S(1)}, bf16[256,256]{1,0:T(8,128)(2,1)S(1)}, u32[]{:S(2)}, u32[]{:S(2)}) collective-permute-start(bf16[256,256]{1,0:T(8,128)(2,1)S(1)} %collective-permute-done.11.rest_8_), channel_id=1, source_target_pairs={{0,4},{1,5},{2,0},{3,1},{4,8},{5,9},{6,2},{7,3},{8,12},{9,13},{10,... | collective-permute-start | bytes 393224 | tf_op jit(solution)/shard_map/ppermute | solution.py:398
  23.0 4.6 %collective-permute-start.10 = (bf16[256,256]{1,0:T(8,128)(2,1)S(1)}, bf16[256,256]{1,0:T(8,128)(2,1)S(1)}, u32[]{:S(2)}, u32[]{:S(2)}) collective-permute-start(bf16[256,256]{1,0:T(8,128)(2,1)S(1)} %collective-permute-done.7.rest_0_), channel_id=1, source_target_pairs={{0,4},{1,5},{2,0},{3,1},{4,8},{5,9},{6,2},{7,3},{8,12},{9,13},{10,... | collective-permute-start | bytes 393224 | tf_op jit(solution)/shard_map/ppermute | solution.py:398
  23.2 4.8 %collective-permute-start.15 = (bf16[256,256]{1,0:T(8,128)(2,1)}, bf16[256,256]{1,0:T(8,128)(2,1)S(1)}, u32[]{:S(2)}, u32[]{:S(2)}) collective-permute-start(bf16[256,256]{1,0:T(8,128)(2,1)} %collective-permute-done.14.rest_4_), channel_id=1, source_target_pairs={{0,2},{1,3},{2,6},{3,7},{4,0},{5,1},{6,10},{7,11},{8,4},{9,5},{10,... | collective-permute-start | bytes 393224 | tf_op jit(solution)/shard_map/ppermute | solution.py:398
  25.0 25.1 %copy-start.8 = (s32[4,16]{1,0:T(4,128)S(1)}, s32[4,16]{1,0:T(4,128)}, u32[]{:S(2)}) copy-start(s32[4,16]{1,0:T(4,128)} %param.12) | copy-start | bytes 772
  25.0 25.1 %copy-start.6 = (bf16[4,64,512]{2,1,0:T(8,128)(2,1)S(1)}, bf16[4,64,512]{2,1,0:T(8,128)(2,1)}, u32[]{:S(2)}) copy-start(bf16[4,64,512]{2,1,0:T(8,128)(2,1)} %own_kv_ref.3) | copy-start | bytes 786436
  25.0 25.1 %copy-start.7 = (s32[4]{0:T(128)S(1)}, s32[4]{0:T(128)}, u32[]{:S(2)}) copy-start(s32[4]{0:T(128)} %length_ref.3) | copy-start | bytes 52
  29.3 7.0 %collective-permute-start.17 = (bf16[256,256]{1,0:T(8,128)(2,1)S(1)}, bf16[256,256]{1,0:T(8,128)(2,1)S(1)}, u32[]{:S(2)}, u32[]{:S(2)}) collective-permute-start(bf16[256,256]{1,0:T(8,128)(2,1)S(1)} %project.3), channel_id=1, source_target_pairs={{0,8},{1,9},{2,10},{3,11},{4,12},{5,13},{6,14},{7,15},{8,0},{9,1},... | collective-permute-start | bytes 393224 | tf_op jit(solution)/shard_map/ppermute | solution.py:398
  31.8 6.4 %collective-permute-start.16 = (bf16[256,256]{1,0:T(8,128)(2,1)S(1)}, bf16[256,256]{1,0:T(8,128)(2,1)S(1)}, u32[]{:S(2)}, u32[]{:S(2)}) collective-permute-start(bf16[256,256]{1,0:T(8,128)(2,1)S(1)} %project.3), channel_id=1, source_target_pairs={{0,4},{1,5},{2,6},{3,7},{4,8},{5,9},{6,10},{7,11},{8,12},{9,13},{1... | collective-permute-start | bytes 393224 | tf_op jit(solution)/shard_map/ppermute | solution.py:398
  33.1 13.4 %collective-permute-start.22 = (bf16[256,256]{1,0:T(8,128)(2,1)S(1)}, bf16[256,256]{1,0:T(8,128)(2,1)S(1)}, u32[]{:S(2)}, u32[]{:S(2)}) collective-permute-start(bf16[256,256]{1,0:T(8,128)(2,1)S(1)} %project.3), channel_id=1, source_target_pairs={{0,14},{1,15},{2,12},{3,13},{4,2},{5,3},{6,0},{7,1},{8,6},{9,7},{1... | collective-permute-start | bytes 393224 | tf_op jit(solution)/shard_map/ppermute | solution.py:398
  36.0 8.1 %collective-permute-start.19 = (bf16[256,256]{1,0:T(8,128)(2,1)S(1)}, bf16[256,256]{1,0:T(8,128)(2,1)S(1)}, u32[]{:S(2)}, u32[]{:S(2)}) collective-permute-start(bf16[256,256]{1,0:T(8,128)(2,1)S(1)} %project.3), channel_id=1, source_target_pairs={{0,2},{1,3},{2,0},{3,1},{4,6},{5,7},{6,4},{7,5},{8,10},{9,11},{10,... | collective-permute-start | bytes 393224 | tf_op jit(solution)/shard_map/ppermute | solution.py:398
  36.3 7.8 %collective-permute-start.18 = (bf16[256,256]{1,0:T(8,128)(2,1)S(1)}, bf16[256,256]{1,0:T(8,128)(2,1)S(1)}, u32[]{:S(2)}, u32[]{:S(2)}) collective-permute-start(bf16[256,256]{1,0:T(8,128)(2,1)S(1)} %project.3), channel_id=1, source_target_pairs={{0,12},{1,13},{2,14},{3,15},{4,0},{5,1},{6,2},{7,3},{8,4},{9,5},{1... | collective-permute-start | bytes 393224 | tf_op jit(solution)/shard_map/ppermute | solution.py:398
  36.3 10.2 %collective-permute-start.21 = (bf16[256,256]{1,0:T(8,128)(2,1)S(1)}, bf16[256,256]{1,0:T(8,128)(2,1)S(1)}, u32[]{:S(2)}, u32[]{:S(2)}) collective-permute-start(bf16[256,256]{1,0:T(8,128)(2,1)S(1)} %collective-permute-done.17), channel_id=1, source_target_pairs={{0,2},{1,3},{2,0},{3,1},{4,6},{5,7},{6,4},{7,5},{8,10},{9,11},{10,... | collective-permute-start | bytes 393224 | tf_op jit(solution)/shard_map/ppermute | solution.py:398
  38.2 8.3 %collective-permute-start.20 = (bf16[256,256]{1,0:T(8,128)(2,1)S(1)}, bf16[256,256]{1,0:T(8,128)(2,1)S(1)}, u32[]{:S(2)}, u32[]{:S(2)}) collective-permute-start(bf16[256,256]{1,0:T(8,128)(2,1)S(1)} %collective-permute-done.16), channel_id=1, source_target_pairs={{0,2},{1,3},{2,0},{3,1},{4,6},{5,7},{6,4},{7,5},{8,10},{9,11},{10,... | collective-permute-start | bytes 393224 | tf_op jit(solution)/shard_map/ppermute | solution.py:398
  46.6 51.0 %collective-permute-start.23 = (bf16[2048,256]{1,0:T(8,128)(2,1)S(1)}, bf16[2048,256]{1,0:T(8,128)(2,1)S(1)}, u32[]{:S(2)}, u32[]{:S(2)}) collective-permute-start(bf16[2048,256]{1,0:T(8,128)(2,1)S(1)} %constant_dynamic-update-slice_fusion.kv_ref), channel_id=1, source_target_pairs={{0,1},{1,0},{2,3},{3,2},{4,5},{5,4},{6,7},{7,6},{8,9},{9,8},{10,11... | collective-permute-start | bytes 3145736 | tf_op jit(solution)/shard_map/ppermute | solution.py:394
  50.1 2.1 %copy-start.3 = (bf16[4,64,7424]{2,1,0:T(8,128)(2,1)S(1)}, bf16[4,64,7424]{2,1,0:T(8,128)(2,1)}, u32[]{:S(2)}) copy-start(bf16[4,64,7424]{2,1,0:T(8,128)(2,1)} %q_ref.3) | copy-start | bytes 11403268
  52.2 45.4 %copy-start.4 = (bf16[4,64,7424]{2,1,0:T(8,128)(2,1)S(1)}, bf16[4,64,7424]{2,1,0:T(8,128)(2,1)}, u32[]{:S(2)}) copy-start(bf16[4,64,7424]{2,1,0:T(8,128)(2,1)} %q_ref.3) | copy-start | bytes 11403268

commit v14 on v13

--- a/solution.py
+++ b/solution.py
@@ -30,9 +30,8 @@
 SUM_LOW, SUM_HIGH = 2.0 ** -40, 2.0 ** 60
 POOL_WIDTH = 1024
 FIRST_COST = 8 * 10**9
-PROJECT_COST = 8
 CHIP = 8
-STEP = 5
+STEP = 3
 BLOCK = 16
 MIB = 1024 * 1024
 
@@ -129,8 +128,18 @@
     )(states, queries, gain)
 
 
-def attend_kernel(half_ref, start_ref, length_ref, q_ref, kv_ref, own_kv_ref, *rest):
-    out_hbm = rest[-11]
+def ask(half, questions_hbm, asked, semaphore):
+    at = pl.multiple_of(half * HALF, LANES)
+    return pltpu.make_async_copy(questions_hbm.at[:, :, pl.ds(at, HALF)], asked, semaphore)
+
+
+def attend_kernel(ahead, half_ref, start_ref, length_ref, q_ref, kv_ref, own_kv_ref, *rest):
+    if ahead:
+        coming = ask(1 - half_ref[0], rest[-14], rest[-12], rest[-1])
+        coming.start()
+        out_hbm, rest = rest[-13], rest[:-1]
+    else:
+        out_hbm = rest[-11]
     (
         answers, memory, key_side, value_side, weights, bias, marker, scores, all_weights, sent,
     ) = rest[-10:]
@@ -185,7 +194,7 @@
 
         def stacked(tiles):
             return jnp.concatenate(
-                [q_ref[query, :, pl.ds(pl.multiple_of(half_at + t * LANES, LANES), LANES)] for t in tiles], axis=0
+                [q_ref[query, :, t * LANES:(t + 1) * LANES] for t in tiles], axis=0
             )
 
         def key_product(i):
@@ -280,23 +289,35 @@
     lax.fori_loop(0, count, answer, 0)
     for query in range(count):
         send(query).wait()
-
-
-def attend(half, starts, lengths, questions, memory_kv, own_kv, earlier=None):
-    count = questions.shape[0]
+    if ahead:
+        coming.wait()
+
+
+def attend(half, starts, lengths, asked, memory_kv, own_kv, earlier=None, questions=None):
+    count = asked.shape[0]
+    ahead = questions is not None
     hbm, vmem, smem = (pl.BlockSpec(memory_space=x) for x in (pltpu.HBM, pltpu.VMEM, pltpu.SMEM))
-    operands = [half.reshape(1), starts, lengths, questions, memory_kv, own_kv]
+    operands = [half.reshape(1), starts, lengths, asked, memory_kv, own_kv]
     in_specs = [smem, smem, smem, vmem, vmem, vmem]
     aliases = {}
     if earlier is not None:
         aliases = {len(operands): 0}
         operands.append(earlier)
         in_specs.append(hbm)
-    return pl.pallas_call(
-        attend_kernel,
+    out_specs = [hbm]
+    out_shape = [jax.ShapeDtypeStruct((count, QLEN, H * HD), jnp.bfloat16)]
+    extra = []
+    if ahead:
+        operands.append(questions)
+        in_specs.append(hbm)
+        out_specs.append(vmem)
+        out_shape.append(jax.ShapeDtypeStruct(asked.shape, asked.dtype))
+        extra = [pltpu.SemaphoreType.DMA]
+    got = pl.pallas_call(
+        functools.partial(attend_kernel, ahead),
         in_specs=in_specs,
-        out_specs=hbm,
-        out_shape=jax.ShapeDtypeStruct((count, QLEN, H * HD), jnp.bfloat16),
+        out_specs=out_specs,
+        out_shape=out_shape,
         scratch_shapes=[
             pltpu.VMEM((count, QLEN, HALF), jnp.bfloat16),
             pltpu.VMEM((ROWS, 2 * LANES), jnp.bfloat16),
@@ -308,9 +329,10 @@
             pltpu.VMEM((STEP * QLEN, KEYS), jnp.float32),
             pltpu.VMEM((STEP * QLEN, KEYS), jnp.bfloat16),
             pltpu.SemaphoreType.DMA((count,)),
+            *extra,
         ],
         input_output_aliases=aliases,
-        compiler_params=pltpu.CompilerParams(vmem_limit_bytes=48 * MIB),
+        compiler_params=pltpu.CompilerParams(vmem_limit_bytes=24 * MIB),
         cost_estimate=pl.CostEstimate(
             flops=2 * count * QLEN * H * HD * (ROWS + QLEN),
             bytes_accessed=2 * count * QLEN * H * HD,
@@ -318,11 +340,17 @@
         ),
         name="attend",
     )(*operands)
+    return got if ahead else got[0]
 
 
 def project_kernel(ring, pieces, more, core_ref, place_ref, own_ref, other_ref, *rest):
     weights, rest = rest[:len(pieces)], rest[len(pieces):]
-    out_ref = rest[-1]
+    if more:
+        questions_hbm, out_ref, asked, arrived = rest
+        coming = ask(core_ref[0], questions_hbm, asked, arrived)
+        coming.start()
+    else:
+        out_ref = rest[-1]
     count = own_ref.shape[0]
     depth = weights[0].shape[0]
     core = core_ref[0]
@@ -334,28 +362,38 @@
         total += jnp.dot(rows, weight[...], preferred_element_type=jnp.float32)
     if more:
         out_ref[...] = total
+        coming.wait()
         return
     result = total.astype(jnp.bfloat16)
     out_ref[pl.ds(pl.multiple_of(core * count, count), count)] = result[:count]
     out_ref[pl.ds(pl.multiple_of((1 - core) * count, count), count)] = result[count:]
 
 
-def project(ring, core, place, own_rows, other_rows, weights, sums=None):
+def project(ring, core, place, own_rows, other_rows, weights, questions=None, sums=None):
     count = own_rows.shape[0]
     pieces, blocks = tuple(weights), list(weights.values())
     width = blocks[0].shape[1]
-    vmem = pl.BlockSpec(memory_space=pltpu.VMEM)
-    smem = pl.BlockSpec(memory_space=pltpu.SMEM)
+    hbm, vmem, smem = (pl.BlockSpec(memory_space=x) for x in (pltpu.HBM, pltpu.VMEM, pltpu.SMEM))
     more = sums is None
-    operands = [own_rows, other_rows, *blocks] + ([] if more else [sums])
+    operands = [own_rows, other_rows, *blocks, questions if more else sums]
+    in_specs = [smem, smem] + [vmem] * (2 + len(blocks)) + [hbm if more else vmem]
+    if more:
+        asked = questions.shape[:2] + (HALF,)
+        out_shape = [
+            jax.ShapeDtypeStruct((2 * count, width), jnp.float32),
+            jax.ShapeDtypeStruct(asked, questions.dtype),
+        ]
+    else:
+        out_shape = jax.ShapeDtypeStruct((2 * count, width), jnp.bfloat16)
     return pl.pallas_call(
         functools.partial(project_kernel, ring, pieces, more),
-        in_specs=[smem, smem] + [vmem] * len(operands),
-        out_specs=vmem,
-        out_shape=jax.ShapeDtypeStruct((2 * count, width), jnp.float32 if more else jnp.bfloat16),
+        in_specs=in_specs,
+        out_specs=[vmem, vmem] if more else vmem,
+        out_shape=out_shape,
+        scratch_shapes=[pltpu.SemaphoreType.DMA] if more else [],
         compiler_params=pltpu.CompilerParams(vmem_limit_bytes=16 * MIB),
         cost_estimate=pl.CostEstimate(
-            flops=PROJECT_COST * 4 * count * D * width, bytes_accessed=2 * D * width, transcendentals=0
+            flops=4 * count * D * width, bytes_accessed=2 * D * width, transcendentals=0
         ),
         name="project",
     )(core.reshape(1), place, *operands)
@@ -383,9 +421,13 @@
         memory_kv = jnp.dot(memory_rows, whole_weight, preferred_element_type=jnp.float32)
         everything = lax.all_gather(memory_kv.astype(jnp.bfloat16), "pass", axis=0, tiled=True)
         halves = everything.reshape(-1, 2, 2, LANES).transpose(2, 0, 1, 3).reshape(2, -1, 2 * LANES)
-        rest = (retrieval * MEM, question_lengths, question_queries)
-        context = attend(jnp.int32(0), *rest, halves[0], question_kv)
-        return attend(jnp.int32(1), *rest, halves[1], question_kv, context)
+        context = None
+        for half in range(2):
+            asked = question_queries[:, :, half * HALF:(half + 1) * HALF]
+            context = attend(
+                jnp.int32(half), retrieval * MEM, question_lengths, asked, halves[half], question_kv, context
+            )
+        return context
 
     place = place_of(chip, chips).reshape(1)
     order = [2 * line for line in range(chips // 2)] + [2 * line + 1 for line in range(chips // 2)][::-1]
@@ -407,10 +449,8 @@
             return along(x, lambda line, lane: 2 * line + 1 - lane)
 
         near = {k: along(block, lambda line, lane: 2 * ((line + k) % lines) + lane) for k in (2, 1, 3)}
-        far = {0: lane_of(block)}
-        far[3] = along(block, lambda line, lane: 2 * ((line + 3) % lines) + 1 - lane)
-        far[1], far[2] = lane_of(near[1]), lane_of(near[2])
-        return [block, near[1], near[2], near[3], far[0], far[1], far[2], far[3]]
+        own_line = [block, near[1], near[2], near[3]]
+        return own_line + [lane_of(x) for x in own_line]
 
     mine, theirs = split(core, kv_weight)
     up = [[mine], [to_partner(theirs)]]
@@ -438,8 +478,8 @@
             other_rows = to_partner(rows)
     up[0].append(along_ring(up[0][-1], 1))
     down[1].append(along_ring(down[1][-1], -1))
-    early = project(chips, core, place, rows, other_rows, blocks((0, 1, 2)))
-    memory_kv = project(chips, core, place, rows, other_rows, blocks((3, 4)), early)
+    early, asked = project(chips, core, place, rows, other_rows, blocks((0, 1, 2)), questions=question_queries)
+    memory_kv = project(chips, core, place, rows, other_rows, blocks((3, 4)), sums=early)
     near = jnp.concatenate(line_by_line(memory_kv), axis=0)
     far = to_partner(near)
 
@@ -448,9 +488,10 @@
     back = lax.rem(lines + lax.div(chip, 2) - lax.div(of_chip, 2), lines)
     slot = back + lines * lax.rem(lax.rem(chip, 2) + lax.rem(of_chip, 2), 2)
     starts = (slot * CHIP + lax.rem(retrieval, CHIP)) * MEM
-    rest = (starts, question_lengths, question_queries)
-    context = attend(core, *rest, near, question_kv)
-    return attend(1 - core, *rest, far, question_kv, context)
+    context, other = attend(
+        core, starts, question_lengths, asked, near, question_kv, questions=question_queries
+    )
+    return attend(1 - core, starts, question_lengths, other, far, question_kv, context)
 
 
 def solution(mesh):

time: 145 us -> 153 us (1.055)
  Pallas kernels: 95.9 us -> 101 us
  local copies, waits for them, and re-layouts: 3.14 us -> 7.97 us
  starting transfers between devices: 26 us -> 23.1 us
  waiting for transfers between devices: 17.9 us -> 20.3 us
    unnamed x25 -> x29, local copies, waits for them, and re-layouts: 3.13 us -> 7.96 us
    pallas_call x2, Pallas kernels: 90.9 us -> 95.6 us  [attend(): pl.pallas_call(functools.partial(attend_kernel, ahead), in_specs=in_specs...]
    ppermute x21, waiting for transfers between devices: 17.9 us -> 20.3 us  [along(): lax.ppermute(x, 'pass', [(2 * s + c, 2 * d + c) for s, d in pairs for c i...]
    ppermute x21, starting transfers between devices: 21.2 us -> 19 us  [along(): lax.ppermute(x, 'pass', [(2 * s + c, 2 * d + c) for s, d in pairs for c i...]
  transfers between devices with their start and end apart: 24 -> 24, of which waited for: 13 -> 9; matrix products, arithmetic and copies ran while one was open for 0% -> 0% of each run, Pallas kernels for 34% -> 34%
where the time goes in v14:
time: 153 us
  Pallas kernels  101 us (66%)
  starting transfers between devices  23.1 us (15%)
  waiting for transfers between devices  20.3 us (13%)
  local copies, waits for them, and re-layouts  7.97 us (5%)
    pallas_call x2, Pallas kernels, attend(): pl.pallas_call(functools.partial(attend_kernel, ahead), in_specs=in_specs...  95.6 us
    ppermute x21, waiting for transfers between devices, along(): lax.ppermute(x, 'pass', [(2 * s + c, 2 * d + c) for s, d in pairs for c i...  20.3 us
    ppermute x21, starting transfers between devices, along(): lax.ppermute(x, 'pass', [(2 * s + c, 2 * d + c) for s, d in pairs for c i...  19 us
    unnamed x29, local copies, waits for them, and re-layouts  7.96 us
    ppermute x3, starting transfers between devices, to_partner(): return lax.ppermute(x, 'pass', [(i, i ^ 1) for i in range(extent)])  4.07 us
    pallas_call x1, Pallas kernels, pool(): pl.pallas_call(pool_kernel, in_specs=[vmem] * 3, out_specs=vmem, out_shap...  3.08 us
  transfers between devices with their start and end apart: 24, of which 9 were waited for; matrix products, arithmetic and copies ran while one was open for 0% of the time, Pallas kernels for 34%

profile of v14, /device:TPU:1, one launch (start us, length us, event | category | flops | bytes accessed | tf_op | source)
XLA Modules:
  0.0 152.7 jit_solution(8085328365028620466)
XLA Ops:
  0.0 0.9 copy-done.7
  1.0 0.1 collective-permute-start.1
  1.1 2.7 %collective-permute-start.3 = (bf16[256,256]{1,0:T(8,128)(2,1)S(1)}, bf16[256,256]{1,0:T(8,128)(2,1)S(1)}, u32[]{:S(2)}, u32[]{:S(2)}) collective-permute-start(bf16[256,256]{1,0:T(8,128)(2,1)S(1)} %get-tuple-element.16.rest_0_), channel_id=1, source_target_pairs={{0,2},{1,3},{2,6},{3,7},{4,0},{5,1},{6,10},{7,11},{8,4},{9,5},{10,... | collective-permute-start | bytes 393224 | tf_op jit(solution)/shard_map/ppermute | solution.py:440
  3.8 0.1 collective-permute-start
  3.9 0.0 collective-permute-done.1.rest_5_
  3.9 1.4 collective-permute-start.4
  5.3 0.1 collective-permute-start.2
  5.3 0.0 copy-done
  5.4 0.0 copy-done.3
  5.4 3.1 %pool.1.own_ref = bf16[128,4096]{1,0:T(8,128)(2,1)S(1)} custom-call(bf16[4,128,4096]{2,1,0:T(8,128)(2,1)S(1)} %copy-done, bf16[32,4096]{1,0:T(8,128)(2,1)S(1)} %copy-done.3, bf16[4096]{0:T(1024)(128)(2,1)S(1)} %copy-done.4), custom_call_target="tpu_custom_call" | custom-call | flops 268435456 | bytes 4194304 | tf_op jit(solution)/shard_map/pool/pallas_call | solution.py:116
  8.4 0.0 collective-permute-done.3.rest_2_
  8.5 0.1 collective-permute-done.rest_1_
  8.5 2.0 %collective-permute-done.4.rest_7_ = bf16[256,256]{1,0:T(8,128)(2,1)S(1)} collective-permute-done((bf16[256,256]{1,0:T(8,128)(2,1)S(1)}, bf16[256,256]{1,0:T(8,128)(2,1)S(1)}, u32[]{:S(2)}, u32[]{:S(2)}) %collective-permute-start.4) | collective-permute-done | bytes 131104 | tf_op jit(solution)/shard_map/ppermute | solution.py:440
  10.5 0.9 collective-permute-done.2.rest_6_
  11.3 1.2 collective-permute-start.5
  12.5 0.1 collective-permute-start.6
  12.6 1.4 collective-permute-start.9
  14.0 1.3 collective-permute-start.7
  15.3 0.2 collective-permute-start.8
  15.4 2.2 %collective-permute-done.6.rest_3_ = bf16[256,256]{1,0:T(8,128)(2,1)S(1)} collective-permute-done((bf16[256,256]{1,0:T(8,128)(2,1)S(1)}, bf16[256,256]{1,0:T(8,128)(2,1)S(1)}, u32[]{:S(2)}, u32[]{:S(2)}) %collective-permute-start.6) | collective-permute-done | bytes 131104 | tf_op jit(solution)/shard_map/ppermute | solution.py:440
  17.6 0.1 collective-permute-start.10
  17.7 0.0 collective-permute-done.9.rest_9_
  17.7 1.4 collective-permute-start.14
  19.1 1.1 collective-permute-done.7.rest_4_
  20.2 1.4 collective-permute-start.11
  21.6 0.0 collective-permute-done.8.rest_8_
  21.6 0.1 collective-permute-start.13
  21.7 1.3 collective-permute-done.10.rest_0_
  23.0 0.2 collective-permute-start.12
  23.2 0.0 collective-permute-done.14.rest_4_
  23.2 1.3 collective-permute-start.15
  24.4 0.0 collective-permute-done.5.other_ref
  24.4 2.1 %copy-done.1 = bf16[4,64,7424]{2,1,0:T(8,128)(2,1)S(1)} copy-done((bf16[4,64,7424]{2,1,0:T(8,128)(2,1)S(1)}, bf16[4,64,7424]{2,1,0:T(8,128)(2,1)}, u32[]{:S(2)}) %copy-start.1) | copy-done | bytes 3801112
  26.5 0.7 project.2
  27.2 0.0 copy-start.5
  27.2 1.2 copy-done.5
  28.4 0.0 collective-permute-done.11.rest_1_
  28.4 0.0 collective-permute-done.13.rest_3_
  28.5 0.0 collective-permute-done.12.rest_2_
  28.5 0.0 collective-permute-done.15.rest_5_
  28.5 1.6 %project.3 = bf16[256,256]{1,0:T(8,128)(2,1)S(1)} custom-call(s32[1]{0:T(128)} %bitcast.1.core_ref.half_ref, s32[1]{0:T(128)} %bitcast.2.place_ref, bf16[128,4096]{1,0:T(8,128)(2,1)S(1)} %pool.1.own_ref, bf16[128,4096]{1,0:T(8,128)(2,1)S(1)} %collective-permute-done.5.other_ref, bf16[256,256]{1,0:T(8,128)(2,1)S(1)} %collective-permute-done.10.rest_0_, ...), custom_call_target="tpu_custom_call" | custom-call | flops 536870912 | bytes 2097152 | tf_op jit(solution)/shard_map/project/pallas_call | solution.py:388
  30.1 3.1 %collective-permute-start.18 = (bf16[256,256]{1,0:T(8,128)(2,1)S(1)}, bf16[256,256]{1,0:T(8,128)(2,1)S(1)}, u32[]{:S(2)}, u32[]{:S(2)}) collective-permute-start(bf16[256,256]{1,0:T(8,128)(2,1)S(1)} %project.3), channel_id=1, source_target_pairs={{0,12},{1,13},{2,14},{3,15},{4,0},{5,1},{6,2},{7,3},{8,4},{9,5},{1... | collective-permute-start | bytes 393224 | tf_op jit(solution)/shard_map/ppermute | solution.py:440
  33.2 0.0 collective-permute-start.17
  33.2 0.5 collective-permute-start.16
  33.7 1.2 collective-permute-start.19
  34.9 0.3 collective-permute-done.18
  35.2 1.2 collective-permute-start.22
  36.4 8.1 %collective-permute-done.17 = bf16[256,256]{1,0:T(8,128)(2,1)S(1)} collective-permute-done((bf16[256,256]{1,0:T(8,128)(2,1)S(1)}, bf16[256,256]{1,0:T(8,128)(2,1)S(1)}, u32[]{:S(2)}, u32[]{:S(2)}) %collective-permute-start.17) | collective-permute-done | bytes 131104 | tf_op jit(solution)/shard_map/ppermute | solution.py:440
  44.5 0.9 collective-permute-start.21
  45.3 0.0 collective-permute-done.16
  45.4 0.6 collective-permute-start.20
  46.0 0.0 collective-permute-done.19
  46.0 4.5 %collective-permute-done.20 = bf16[256,256]{1,0:T(8,128)(2,1)S(1)} collective-permute-done((bf16[256,256]{1,0:T(8,128)(2,1)S(1)}, bf16[256,256]{1,0:T(8,128)(2,1)S(1)}, u32[]{:S(2)}, u32[]{:S(2)}) %collective-permute-start.20) | collective-permute-done | bytes 131104 | tf_op jit(solution)/shard_map/ppermute | solution.py:440
  50.5 0.0 collective-permute-done.21
  50.5 0.0 collective-permute-done.22
  50.5 2.8 %collective-permute-start.23 = (bf16[2048,256]{1,0:T(8,128)(2,1)S(1)}, bf16[2048,256]{1,0:T(8,128)(2,1)S(1)}, u32[]{:S(2)}, u32[]{:S(2)}) collective-permute-start(bf16[2048,256]{1,0:T(8,128)(2,1)S(1)} %constant_dynamic-update-slice_fusion.kv_ref), channel_id=1, source_target_pairs={{0,1},{1,0},{2,3},{3,2},{4,5},{5,4},{6,7},{7,6},{8,9},{9,8},{10,11... | collective-permute-start | bytes 3145736 | tf_op jit(solution)/shard_map/ppermute | solution.py:436
  53.3 0.0 copy-done.10
  53.3 0.0 copy-done.8
  53.4 0.0 copy-start.2
  53.4 2.1 %copy-done.2 = bf16[4,64,7424]{2,1,0:T(8,128)(2,1)S(1)} copy-done((bf16[4,64,7424]{2,1,0:T(8,128)(2,1)S(1)}, bf16[4,64,7424]{2,1,0:T(8,128)(2,1)}, u32[]{:S(2)}) %copy-start.2) | copy-done | bytes 3801112
  55.4 1.5 copy-done.6
  57.0 47.7 %attend.2 = (bf16[4,64,7424]{2,1,0:T(8,128)(2,1)}, bf16[4,64,3712]{2,1,0:T(8,128)(2,1)S(1)}) custom-call(s32[1]{0:T(128)} %bitcast.1.core_ref.half_ref, s32[4,16]{1,0:T(4,128)S(1)} %fusion.6.start_ref, s32[4]{0:T(128)S(1)} %copy-done.9, bf16[4,64,3712]{2,1,0:T(8,128)(2,1)S(1)} %copy-done.6, bf16[2048,256]{1,0:T(8,128)(2,1)S(1)} %constant_dynamic-update-slice_fusion.kv_ref, ...), custom_call_target="tpu_custom_call" | custom-call | flops 2189426688 | bytes 3801088 | tf_op jit(solution)/shard_map/attend/pallas_call | solution.py:316
  104.7 0.0 collective-permute-done.23.kv_ref
  104.7 47.8 %attend.3 = bf16[4,64,7424]{2,1,0:T(8,128)(2,1)} custom-call(s32[1]{0:T(128)} %bitcast.half_ref, s32[4,16]{1,0:T(4,128)S(1)} %fusion.6.start_ref, s32[4]{0:T(128)S(1)} %copy-done.9, bf16[4,64,3712]{2,1,0:T(8,128)(2,1)S(1)} %get-tuple-element.25.q_ref, bf16[2048,256]{1,0:T(8,128)(2,1)S(1)} %collective-permute-done.23.kv_ref, ...), custom_call_target="tpu_custom_call", output_to_operand_aliasing={{}: (6, {})} | custom-call | flops 2189426688 | bytes 3801088 | tf_op jit(solution)/shard_map/attend/pallas_call | solution.py:316
  (21 shorter events, 0.2 us)
Async XLA Ops:
  0.0 0.9 copy-start.7
  1.0 4.4 %copy-start = (bf16[4,128,4096]{2,1,0:T(8,128)(2,1)S(1)}, bf16[4,128,4096]{2,1,0:T(8,128)(2,1)}, u32[]{:S(2)}) copy-start(bf16[4,128,4096]{2,1,0:T(8,128)(2,1)} %states.1) | copy-start | bytes 12582916
  1.0 4.4 %copy-start.3 = (bf16[32,4096]{1,0:T(8,128)(2,1)S(1)}, bf16[32,4096]{1,0:T(8,128)(2,1)}, u32[]{:S(2)}) copy-start(bf16[32,4096]{1,0:T(8,128)(2,1)} %queries.1) | copy-start | bytes 786436
  1.0 4.4 %copy-start.4 = (bf16[4096]{0:T(1024)(128)(2,1)S(1)}, bf16[4096]{0:T(1024)(128)(2,1)}, u32[]{:S(2)}) copy-start(bf16[4096]{0:T(1024)(128)(2,1)} %gain.1) | copy-start | bytes 24580
  1.0 2.9 %collective-permute-start.1 = (bf16[256,256]{1,0:T(8,128)(2,1)S(1)}, bf16[256,256]{1,0:T(8,128)(2,1)S(1)}, u32[]{:S(2)}, u32[]{:S(2)}) collective-permute-start(bf16[256,256]{1,0:T(8,128)(2,1)S(1)} %get-tuple-element.17), channel_id=1, source_target_pairs={{0,1},{1,0},{2,3},{3,2},{4,5},{5,4},{6,7},{7,6},{8,9},{9,8},{10,11... | collective-permute-start | bytes 393224 | tf_op jit(solution)/shard_map/ppermute | solution.py:436
  1.1 7.3 %collective-permute-start.3 = (bf16[256,256]{1,0:T(8,128)(2,1)S(1)}, bf16[256,256]{1,0:T(8,128)(2,1)S(1)}, u32[]{:S(2)}, u32[]{:S(2)}) collective-permute-start(bf16[256,256]{1,0:T(8,128)(2,1)S(1)} %get-tuple-element.16.rest_0_), channel_id=1, source_target_pairs={{0,2},{1,3},{2,6},{3,7},{4,0},{5,1},{6,10},{7,11},{8,4},{9,5},{10,... | collective-permute-start | bytes 393224 | tf_op jit(solution)/shard_map/ppermute | solution.py:440
  3.8 4.7 %collective-permute-start = (bf16[256,256]{1,0:T(8,128)(2,1)S(1)}, bf16[256,256]{1,0:T(8,128)(2,1)S(1)}, u32[]{:S(2)}, u32[]{:S(2)}) collective-permute-start(bf16[256,256]{1,0:T(8,128)(2,1)S(1)} %get-tuple-element.16.rest_0_), channel_id=1, source_target_pairs={{0,4},{1,5},{2,0},{3,1},{4,8},{5,9},{6,2},{7,3},{8,12},{9,13},{10,... | collective-permute-start | bytes 393224 | tf_op jit(solution)/shard_map/ppermute | solution.py:440
  3.9 6.6 %collective-permute-start.4 = (bf16[256,256]{1,0:T(8,128)(2,1)S(1)}, bf16[256,256]{1,0:T(8,128)(2,1)S(1)}, u32[]{:S(2)}, u32[]{:S(2)}) collective-permute-start(bf16[256,256]{1,0:T(8,128)(2,1)S(1)} %collective-permute-done.1.rest_5_), channel_id=1, source_target_pairs={{0,2},{1,3},{2,6},{3,7},{4,0},{5,1},{6,10},{7,11},{8,4},{9,5},{10,... | collective-permute-start | bytes 393224 | tf_op jit(solution)/shard_map/ppermute | solution.py:440
  5.3 6.1 %collective-permute-start.2 = (bf16[256,256]{1,0:T(8,128)(2,1)S(1)}, bf16[256,256]{1,0:T(8,128)(2,1)S(1)}, u32[]{:S(2)}, u32[]{:S(2)}) collective-permute-start(bf16[256,256]{1,0:T(8,128)(2,1)S(1)} %collective-permute-done.1.rest_5_), channel_id=1, source_target_pairs={{0,4},{1,5},{2,0},{3,1},{4,8},{5,9},{6,2},{7,3},{8,12},{9,13},{10,... | collective-permute-start | bytes 393224 | tf_op jit(solution)/shard_map/ppermute | solution.py:440
  11.3 13.1 %collective-permute-start.5 = (bf16[128,4096]{1,0:T(8,128)(2,1)S(1)}, bf16[128,4096]{1,0:T(8,128)(2,1)S(1)}, u32[]{:S(2)}, u32[]{:S(2)}) collective-permute-start(bf16[128,4096]{1,0:T(8,128)(2,1)S(1)} %pool.1.own_ref), channel_id=1, source_target_pairs={{0,1},{1,0},{2,3},{3,2},{4,5},{5,4},{6,7},{7,6},{8,9},{9,8},{10,11... | collective-permute-start | bytes 3145736 | tf_op jit(solution)/shard_map/ppermute | solution.py:436
  12.5 5.1 %collective-permute-start.6 = (bf16[256,256]{1,0:T(8,128)(2,1)S(1)}, bf16[256,256]{1,0:T(8,128)(2,1)S(1)}, u32[]{:S(2)}, u32[]{:S(2)}) collective-permute-start(bf16[256,256]{1,0:T(8,128)(2,1)S(1)} %collective-permute-done.rest_1_), channel_id=1, source_target_pairs={{0,4},{1,5},{2,0},{3,1},{4,8},{5,9},{6,2},{7,3},{8,12},{9,13},{10,... | collective-permute-start | bytes 393224 | tf_op jit(solution)/shard_map/ppermute | solution.py:440
  12.6 5.1 %collective-permute-start.9 = (bf16[256,256]{1,0:T(8,128)(2,1)S(1)}, bf16[256,256]{1,0:T(8,128)(2,1)S(1)}, u32[]{:S(2)}, u32[]{:S(2)}) collective-permute-start(bf16[256,256]{1,0:T(8,128)(2,1)S(1)} %collective-permute-done.4.rest_7_), channel_id=1, source_target_pairs={{0,2},{1,3},{2,6},{3,7},{4,0},{5,1},{6,10},{7,11},{8,4},{9,5},{10,... | collective-permute-start | bytes 393224 | tf_op jit(solution)/shard_map/ppermute | solution.py:440
  14.0 6.2 %collective-permute-start.7 = (bf16[256,256]{1,0:T(8,128)(2,1)S(1)}, bf16[256,256]{1,0:T(8,128)(2,1)S(1)}, u32[]{:S(2)}, u32[]{:S(2)}) collective-permute-start(bf16[256,256]{1,0:T(8,128)(2,1)S(1)} %collective-permute-done.3.rest_2_), channel_id=1, source_target_pairs={{0,2},{1,3},{2,6},{3,7},{4,0},{5,1},{6,10},{7,11},{8,4},{9,5},{10,... | collective-permute-start | bytes 393224 | tf_op jit(solution)/shard_map/ppermute | solution.py:440
  15.3 6.3 %collective-permute-start.8 = (bf16[256,256]{1,0:T(8,128)(2,1)S(1)}, bf16[256,256]{1,0:T(8,128)(2,1)S(1)}, u32[]{:S(2)}, u32[]{:S(2)}) collective-permute-start(bf16[256,256]{1,0:T(8,128)(2,1)S(1)} %collective-permute-done.2.rest_6_), channel_id=1, source_target_pairs={{0,4},{1,5},{2,0},{3,1},{4,8},{5,9},{6,2},{7,3},{8,12},{9,13},{10,... | collective-permute-start | bytes 393224 | tf_op jit(solution)/shard_map/ppermute | solution.py:440
  17.6 5.3 %collective-permute-start.10 = (bf16[256,256]{1,0:T(8,128)(2,1)S(1)}, bf16[256,256]{1,0:T(8,128)(2,1)S(1)}, u32[]{:S(2)}, u32[]{:S(2)}) collective-permute-start(bf16[256,256]{1,0:T(8,128)(2,1)S(1)} %collective-permute-done.6.rest_3_), channel_id=1, source_target_pairs={{0,4},{1,5},{2,0},{3,1},{4,8},{5,9},{6,2},{7,3},{8,12},{9,13},{10,... | collective-permute-start | bytes 393224 | tf_op jit(solution)/shard_map/ppermute | solution.py:440
  17.7 5.4 %collective-permute-start.14 = (bf16[256,256]{1,0:T(8,128)(2,1)S(1)}, bf16[256,256]{1,0:T(8,128)(2,1)}, u32[]{:S(2)}, u32[]{:S(2)}) collective-permute-start(bf16[256,256]{1,0:T(8,128)(2,1)S(1)} %collective-permute-done.9.rest_9_), channel_id=1, source_target_pairs={{0,2},{1,3},{2,6},{3,7},{4,0},{5,1},{6,10},{7,11},{8,4},{9,5},{10,... | collective-permute-start | bytes 393224 | tf_op jit(solution)/shard_map/ppermute | solution.py:440
  20.2 8.2 %collective-permute-start.11 = (bf16[256,256]{1,0:T(8,128)(2,1)S(1)}, bf16[256,256]{1,0:T(8,128)(2,1)}, u32[]{:S(2)}, u32[]{:S(2)}) collective-permute-start(bf16[256,256]{1,0:T(8,128)(2,1)S(1)} %collective-permute-done.7.rest_4_), channel_id=1, source_target_pairs={{0,2},{1,3},{2,6},{3,7},{4,0},{5,1},{6,10},{7,11},{8,4},{9,5},{10,... | collective-permute-start | bytes 393224 | tf_op jit(solution)/shard_map/ppermute | solution.py:440
  21.6 6.8 %collective-permute-start.13 = (bf16[256,256]{1,0:T(8,128)(2,1)S(1)}, bf16[256,256]{1,0:T(8,128)(2,1)}, u32[]{:S(2)}, u32[]{:S(2)}) collective-permute-start(bf16[256,256]{1,0:T(8,128)(2,1)S(1)} %collective-permute-done.8.rest_8_), channel_id=1, source_target_pairs={{0,4},{1,5},{2,0},{3,1},{4,8},{5,9},{6,2},{7,3},{8,12},{9,13},{10,... | collective-permute-start | bytes 393224 | tf_op jit(solution)/shard_map/ppermute | solution.py:440
  23.0 5.5 %collective-permute-start.12 = (bf16[256,256]{1,0:T(8,128)(2,1)S(1)}, bf16[256,256]{1,0:T(8,128)(2,1)}, u32[]{:S(2)}, u32[]{:S(2)}) collective-permute-start(bf16[256,256]{1,0:T(8,128)(2,1)S(1)} %collective-permute-done.10.rest_0_), channel_id=1, source_target_pairs={{0,4},{1,5},{2,0},{3,1},{4,8},{5,9},{6,2},{7,3},{8,12},{9,13},{10,... | collective-permute-start | bytes 393224 | tf_op jit(solution)/shard_map/ppermute | solution.py:440
  23.2 5.3 %collective-permute-start.15 = (bf16[256,256]{1,0:T(8,128)(2,1)}, bf16[256,256]{1,0:T(8,128)(2,1)}, u32[]{:S(2)}, u32[]{:S(2)}) collective-permute-start(bf16[256,256]{1,0:T(8,128)(2,1)} %collective-permute-done.14.rest_4_), channel_id=1, source_target_pairs={{0,2},{1,3},{2,6},{3,7},{4,0},{5,1},{6,10},{7,11},{8,4},{9,5},{10,... | collective-permute-start | bytes 393224 | tf_op jit(solution)/shard_map/ppermute | solution.py:440
  24.4 2.1 %copy-start.1 = (bf16[4,64,7424]{2,1,0:T(8,128)(2,1)S(1)}, bf16[4,64,7424]{2,1,0:T(8,128)(2,1)}, u32[]{:S(2)}) copy-start(bf16[4,64,7424]{2,1,0:T(8,128)(2,1)} %rest_0_.1) | copy-start | bytes 11403268
  27.2 1.3 copy-start.5
  28.4 24.9 %copy-start.10 = (s32[4,16]{1,0:T(4,128)S(1)}, s32[4,16]{1,0:T(4,128)}, u32[]{:S(2)}) copy-start(s32[4,16]{1,0:T(4,128)} %param.12) | copy-start | bytes 772
  28.4 24.9 %copy-start.8 = (bf16[4,64,512]{2,1,0:T(8,128)(2,1)S(1)}, bf16[4,64,512]{2,1,0:T(8,128)(2,1)}, u32[]{:S(2)}) copy-start(bf16[4,64,512]{2,1,0:T(8,128)(2,1)} %own_kv_ref.3) | copy-start | bytes 786436
  28.4 24.9 %copy-start.9 = (s32[4]{0:T(128)S(1)}, s32[4]{0:T(128)}, u32[]{:S(2)}) copy-start(s32[4]{0:T(128)} %length_ref.3) | copy-start | bytes 52
  30.1 5.1 %collective-permute-start.18 = (bf16[256,256]{1,0:T(8,128)(2,1)S(1)}, bf16[256,256]{1,0:T(8,128)(2,1)S(1)}, u32[]{:S(2)}, u32[]{:S(2)}) collective-permute-start(bf16[256,256]{1,0:T(8,128)(2,1)S(1)} %project.3), channel_id=1, source_target_pairs={{0,12},{1,13},{2,14},{3,15},{4,0},{5,1},{6,2},{7,3},{8,4},{9,5},{1... | collective-permute-start | bytes 393224 | tf_op jit(solution)/shard_map/ppermute | solution.py:440
  33.2 11.3 %collective-permute-start.17 = (bf16[256,256]{1,0:T(8,128)(2,1)S(1)}, bf16[256,256]{1,0:T(8,128)(2,1)S(1)}, u32[]{:S(2)}, u32[]{:S(2)}) collective-permute-start(bf16[256,256]{1,0:T(8,128)(2,1)S(1)} %project.3), channel_id=1, source_target_pairs={{0,8},{1,9},{2,10},{3,11},{4,12},{5,13},{6,14},{7,15},{8,0},{9,1},... | collective-permute-start | bytes 393224 | tf_op jit(solution)/shard_map/ppermute | solution.py:440
  33.2 12.2 %collective-permute-start.16 = (bf16[256,256]{1,0:T(8,128)(2,1)S(1)}, bf16[256,256]{1,0:T(8,128)(2,1)S(1)}, u32[]{:S(2)}, u32[]{:S(2)}) collective-permute-start(bf16[256,256]{1,0:T(8,128)(2,1)S(1)} %project.3), channel_id=1, source_target_pairs={{0,4},{1,5},{2,6},{3,7},{4,8},{5,9},{6,10},{7,11},{8,12},{9,13},{1... | collective-permute-start | bytes 393224 | tf_op jit(solution)/shard_map/ppermute | solution.py:440
  33.7 12.3 %collective-permute-start.19 = (bf16[256,256]{1,0:T(8,128)(2,1)S(1)}, bf16[256,256]{1,0:T(8,128)(2,1)S(1)}, u32[]{:S(2)}, u32[]{:S(2)}) collective-permute-start(bf16[256,256]{1,0:T(8,128)(2,1)S(1)} %project.3), channel_id=1, source_target_pairs={{0,2},{1,3},{2,0},{3,1},{4,6},{5,7},{6,4},{7,5},{8,10},{9,11},{10,... | collective-permute-start | bytes 393224 | tf_op jit(solution)/shard_map/ppermute | solution.py:440
  35.2 15.4 %collective-permute-start.22 = (bf16[256,256]{1,0:T(8,128)(2,1)S(1)}, bf16[256,256]{1,0:T(8,128)(2,1)S(1)}, u32[]{:S(2)}, u32[]{:S(2)}) collective-permute-start(bf16[256,256]{1,0:T(8,128)(2,1)S(1)} %collective-permute-done.18), channel_id=1, source_target_pairs={{0,2},{1,3},{2,0},{3,1},{4,6},{5,7},{6,4},{7,5},{8,10},{9,11},{10,... | collective-permute-start | bytes 393224 | tf_op jit(solution)/shard_map/ppermute | solution.py:440
  44.5 6.0 %collective-permute-start.21 = (bf16[256,256]{1,0:T(8,128)(2,1)S(1)}, bf16[256,256]{1,0:T(8,128)(2,1)S(1)}, u32[]{:S(2)}, u32[]{:S(2)}) collective-permute-start(bf16[256,256]{1,0:T(8,128)(2,1)S(1)} %collective-permute-done.17), channel_id=1, source_target_pairs={{0,2},{1,3},{2,0},{3,1},{4,6},{5,7},{6,4},{7,5},{8,10},{9,11},{10,... | collective-permute-start | bytes 393224 | tf_op jit(solution)/shard_map/ppermute | solution.py:440
  45.4 5.1 %collective-permute-start.20 = (bf16[256,256]{1,0:T(8,128)(2,1)S(1)}, bf16[256,256]{1,0:T(8,128)(2,1)S(1)}, u32[]{:S(2)}, u32[]{:S(2)}) collective-permute-start(bf16[256,256]{1,0:T(8,128)(2,1)S(1)} %collective-permute-done.16), channel_id=1, source_target_pairs={{0,2},{1,3},{2,0},{3,1},{4,6},{5,7},{6,4},{7,5},{8,10},{9,11},{10,... | collective-permute-start | bytes 393224 | tf_op jit(solution)/shard_map/ppermute | solution.py:440
  50.5 54.2 %collective-permute-start.23 = (bf16[2048,256]{1,0:T(8,128)(2,1)S(1)}, bf16[2048,256]{1,0:T(8,128)(2,1)S(1)}, u32[]{:S(2)}, u32[]{:S(2)}) collective-permute-start(bf16[2048,256]{1,0:T(8,128)(2,1)S(1)} %constant_dynamic-update-slice_fusion.kv_ref), channel_id=1, source_target_pairs={{0,1},{1,0},{2,3},{3,2},{4,5},{5,4},{6,7},{7,6},{8,9},{9,8},{10,11... | collective-permute-start | bytes 3145736 | tf_op jit(solution)/shard_map/ppermute | solution.py:436
  53.4 2.1 %copy-start.2 = (bf16[4,64,7424]{2,1,0:T(8,128)(2,1)S(1)}, bf16[4,64,7424]{2,1,0:T(8,128)(2,1)}, u32[]{:S(2)}) copy-start(bf16[4,64,7424]{2,1,0:T(8,128)(2,1)} %rest_0_.1) | copy-start | bytes 11403268
  55.4 1.5 copy-start.6

commit v15 on v13

--- a/solution.py
+++ b/solution.py
@@ -30,7 +30,6 @@
 SUM_LOW, SUM_HIGH = 2.0 ** -40, 2.0 ** 60
 POOL_WIDTH = 1024
 FIRST_COST = 8 * 10**9
-PROJECT_COST = 8
 CHIP = 8
 STEP = 5
 BLOCK = 16
@@ -129,21 +128,28 @@
     )(states, queries, gain)
 
 
-def attend_kernel(half_ref, start_ref, length_ref, q_ref, kv_ref, own_kv_ref, *rest):
-    out_hbm = rest[-11]
+def attend_kernel(half_ref, start_ref, length_ref, q_hbm, kv_ref, own_kv_ref, *rest):
+    out_hbm = rest[-13]
     (
-        answers, memory, key_side, value_side, weights, bias, marker, scores, all_weights, sent,
-    ) = rest[-10:]
-    count = q_ref.shape[0]
+        questions, answers, memory, key_side, value_side, weights, bias, marker, scores, all_weights,
+        arrived, sent,
+    ) = rest[-12:]
+    count = q_hbm.shape[0]
     half_at = pl.multiple_of(half_ref[0] * HALF, LANES)
     own_at = pl.multiple_of(half_ref[0] * LANES, LANES)
     factor = math.log2(math.e) / math.sqrt(HD)
+
+    def fetch(query):
+        return pltpu.make_async_copy(
+            q_hbm.at[query, :, pl.ds(half_at, HALF)], questions.at[query], arrived.at[query]
+        )
 
     def send(query):
         return pltpu.make_async_copy(
             answers.at[query], out_hbm.at[query, :, pl.ds(half_at, HALF)], sent.at[query]
         )
 
+    fetch(0).start()
     lane = lax.broadcasted_iota(jnp.int32, (KEYS, LANES), 1)
     row = lax.broadcasted_iota(jnp.int32, (KEYS, LANES), 0)
     in_b = ((row >= ROWS) & (row < 2 * ROWS)) | (row >= 2 * ROWS + QLEN)
@@ -183,10 +189,14 @@
         alive = token < length
         sample = lax.div(key, HD // STEP)
 
+        fetch(query).wait()
+
+        @pl.when(query + 1 < count)
+        def _():
+            fetch(query + 1).start()
+
         def stacked(tiles):
-            return jnp.concatenate(
-                [q_ref[query, :, pl.ds(pl.multiple_of(half_at + t * LANES, LANES), LANES)] for t in tiles], axis=0
-            )
+            return jnp.concatenate([questions[query, :, t * LANES:(t + 1) * LANES] for t in tiles], axis=0)
 
         def key_product(i):
             g, tiles = chunks[i]
@@ -286,7 +296,7 @@
     count = questions.shape[0]
     hbm, vmem, smem = (pl.BlockSpec(memory_space=x) for x in (pltpu.HBM, pltpu.VMEM, pltpu.SMEM))
     operands = [half.reshape(1), starts, lengths, questions, memory_kv, own_kv]
-    in_specs = [smem, smem, smem, vmem, vmem, vmem]
+    in_specs = [smem, smem, smem, hbm, vmem, vmem]
     aliases = {}
     if earlier is not None:
         aliases = {len(operands): 0}
@@ -299,6 +309,7 @@
         out_shape=jax.ShapeDtypeStruct((count, QLEN, H * HD), jnp.bfloat16),
         scratch_shapes=[
             pltpu.VMEM((count, QLEN, HALF), jnp.bfloat16),
+            pltpu.VMEM((count, QLEN, HALF), jnp.bfloat16),
             pltpu.VMEM((ROWS, 2 * LANES), jnp.bfloat16),
             pltpu.VMEM((2, LANES, KEYS), jnp.bfloat16),
             pltpu.VMEM((2, KEYS, 2 * LANES), jnp.bfloat16),
@@ -308,9 +319,10 @@
             pltpu.VMEM((STEP * QLEN, KEYS), jnp.float32),
             pltpu.VMEM((STEP * QLEN, KEYS), jnp.bfloat16),
             pltpu.SemaphoreType.DMA((count,)),
+            pltpu.SemaphoreType.DMA((count,)),
         ],
         input_output_aliases=aliases,
-        compiler_params=pltpu.CompilerParams(vmem_limit_bytes=48 * MIB),
+        compiler_params=pltpu.CompilerParams(vmem_limit_bytes=50 * MIB),
         cost_estimate=pl.CostEstimate(
             flops=2 * count * QLEN * H * HD * (ROWS + QLEN),
             bytes_accessed=2 * count * QLEN * H * HD,
@@ -355,7 +367,7 @@
         out_shape=jax.ShapeDtypeStruct((2 * count, width), jnp.float32 if more else jnp.bfloat16),
         compiler_params=pltpu.CompilerParams(vmem_limit_bytes=16 * MIB),
         cost_estimate=pl.CostEstimate(
-            flops=PROJECT_COST * 4 * count * D * width, bytes_accessed=2 * D * width, transcendentals=0
+            flops=4 * count * D * width, bytes_accessed=2 * D * width, transcendentals=0
         ),
         name="project",
     )(core.reshape(1), place, *operands)

time: 145 us -> 145 us (level)
  local copies, waits for them, and re-layouts: 3.14 us -> 1.06 us
  Pallas kernels: 95.9 us -> 97.6 us
    unnamed x25 -> x21, local copies, waits for them, and re-layouts: 3.13 us -> 1.05 us
    pallas_call x2, Pallas kernels: 90.9 us -> 92.4 us  [attend(): pl.pallas_call(attend_kernel, in_specs=in_specs, out_specs=hbm, out_shape...]
  transfers between devices with their start and end apart: 24 -> 24, of which waited for: 13 -> 13; matrix products, arithmetic and copies ran while one was open for 0% -> 0% of each run, Pallas kernels for 34% -> 35%
where the time goes in v15:
time: 145 us; the launch traced here: 143 us
  Pallas kernels  97.6 us (67%)
  starting transfers between devices  26 us (18%)
  waiting for transfers between devices  18.1 us (12%)
    pallas_call x2, Pallas kernels, attend(): pl.pallas_call(attend_kernel, in_specs=in_specs, out_specs=hbm, out_shape...  92.4 us
    ppermute x21, starting transfers between devices, along(): lax.ppermute(x, 'pass', [(2 * s + c, 2 * d + c) for s, d in pairs for c i...  21.2 us
    ppermute x21, waiting for transfers between devices, along(): lax.ppermute(x, 'pass', [(2 * s + c, 2 * d + c) for s, d in pairs for c i...  18.1 us
    ppermute x3, starting transfers between devices, to_partner(): return lax.ppermute(x, 'pass', [(i, i ^ 1) for i in range(extent)])  4.77 us
    pallas_call x1, Pallas kernels, pool(): pl.pallas_call(pool_kernel, in_specs=[vmem] * 3, out_specs=vmem, out_shap...  3.08 us
  transfers between devices with their start and end apart: 24, of which 13 were waited for; matrix products, arithmetic and copies ran while one was open for 0% of the time, Pallas kernels for 35%

profile of v15, /device:TPU:1, one launch (start us, length us, event | category | flops | bytes accessed | tf_op | source)
XLA Modules:
  0.0 143.1 jit_solution(16545635032974437446)
XLA Ops:
  0.0 0.0 copy-start.3
  0.0 0.9 copy-done.3
  1.0 0.0 copy-start
  1.0 0.0 copy-start.1
  1.0 0.1 collective-permute-start.1
  1.1 2.7 %collective-permute-start.3 = (bf16[256,256]{1,0:T(8,128)(2,1)S(1)}, bf16[256,256]{1,0:T(8,128)(2,1)S(1)}, u32[]{:S(2)}, u32[]{:S(2)}) collective-permute-start(bf16[256,256]{1,0:T(8,128)(2,1)S(1)} %get-tuple-element.12.rest_0_), channel_id=1, source_target_pairs={{0,2},{1,3},{2,6},{3,7},{4,0},{5,1},{6,10},{7,11},{8,4},{9,5},{10,... | collective-permute-start | bytes 393224 | tf_op jit(solution)/shard_map/ppermute | solution.py:410
  3.8 0.1 collective-permute-start
  3.9 0.0 collective-permute-done.1.rest_5_
  3.9 1.4 collective-permute-start.4
  5.3 0.1 collective-permute-start.2
  5.3 0.0 copy-done
  5.4 0.0 copy-done.1
  5.4 0.0 copy-done.2
  5.4 3.1 %pool.1.own_ref = bf16[128,4096]{1,0:T(8,128)(2,1)S(1)} custom-call(bf16[4,128,4096]{2,1,0:T(8,128)(2,1)S(1)} %copy-done, bf16[32,4096]{1,0:T(8,128)(2,1)S(1)} %copy-done.1, bf16[4096]{0:T(1024)(128)(2,1)S(1)} %copy-done.2), custom_call_target="tpu_custom_call" | custom-call | flops 268435456 | bytes 4194304 | tf_op jit(solution)/shard_map/pool/pallas_call | solution.py:116
  8.4 0.0 collective-permute-done.3.rest_2_
  8.5 0.1 collective-permute-done.rest_1_
  8.5 2.0 %collective-permute-done.4.rest_7_ = bf16[256,256]{1,0:T(8,128)(2,1)S(1)} collective-permute-done((bf16[256,256]{1,0:T(8,128)(2,1)S(1)}, bf16[256,256]{1,0:T(8,128)(2,1)S(1)}, u32[]{:S(2)}, u32[]{:S(2)}) %collective-permute-start.4) | collective-permute-done | bytes 131104 | tf_op jit(solution)/shard_map/ppermute | solution.py:410
  10.5 0.9 collective-permute-done.2.rest_6_
  11.3 1.2 collective-permute-start.5
  12.5 0.1 collective-permute-start.6
  12.6 1.4 collective-permute-start.13
  14.0 1.3 collective-permute-start.8
  15.3 0.2 collective-permute-start.11
  15.4 2.2 %collective-permute-done.6.rest_3_ = bf16[256,256]{1,0:T(8,128)(2,1)S(1)} collective-permute-done((bf16[256,256]{1,0:T(8,128)(2,1)S(1)}, bf16[256,256]{1,0:T(8,128)(2,1)S(1)}, u32[]{:S(2)}, u32[]{:S(2)}) %collective-permute-start.6) | collective-permute-done | bytes 131104 | tf_op jit(solution)/shard_map/ppermute | solution.py:410
  17.6 0.1 collective-permute-start.7
  17.7 0.0 collective-permute-done.13.rest_9_
  17.7 1.4 collective-permute-start.14
  19.1 1.1 collective-permute-done.8.rest_4_
  20.2 1.4 collective-permute-start.9
  21.6 0.0 collective-permute-done.11.rest_8_
  21.6 0.1 collective-permute-start.12
  21.7 1.3 collective-permute-done.7.rest_0_
  23.0 0.2 collective-permute-start.10
  23.2 0.0 collective-permute-done.14.rest_4_
  23.2 1.3 collective-permute-start.15
  24.4 0.0 collective-permute-done.5.other_ref
  24.4 0.5 project.2.rest_6_
  25.0 0.0 copy-start.4
  25.0 0.5 collective-permute-done.9.rest_1_
  25.5 0.3 collective-permute-done.12.rest_3_
  25.8 1.9 %collective-permute-done.10.rest_2_ = bf16[256,256]{1,0:T(8,128)(2,1)} collective-permute-done((bf16[256,256]{1,0:T(8,128)(2,1)S(1)}, bf16[256,256]{1,0:T(8,128)(2,1)}, u32[]{:S(2)}, u32[]{:S(2)}) %collective-permute-start.10) | collective-permute-done | bytes 131104 | tf_op jit(solution)/shard_map/ppermute | solution.py:410
  27.7 0.4 collective-permute-done.15.rest_5_
  28.1 1.5 %project.3 = bf16[256,256]{1,0:T(8,128)(2,1)S(1)} custom-call(s32[1]{0:T(128)} %bitcast.1.core_ref.half_ref, s32[1]{0:T(128)} %bitcast.2.place_ref, bf16[128,4096]{1,0:T(8,128)(2,1)S(1)} %pool.1.own_ref, bf16[128,4096]{1,0:T(8,128)(2,1)S(1)} %collective-permute-done.5.other_ref, bf16[256,256]{1,0:T(8,128)(2,1)S(1)} %collective-permute-done.7.rest_0_, ...), custom_call_target="tpu_custom_call" | custom-call | flops 536870912 | bytes 2097152 | tf_op jit(solution)/shard_map/project/pallas_call | solution.py:363
  29.7 2.5 %collective-permute-start.17 = (bf16[256,256]{1,0:T(8,128)(2,1)S(1)}, bf16[256,256]{1,0:T(8,128)(2,1)S(1)}, u32[]{:S(2)}, u32[]{:S(2)}) collective-permute-start(bf16[256,256]{1,0:T(8,128)(2,1)S(1)} %project.3), channel_id=1, source_target_pairs={{0,8},{1,9},{2,10},{3,11},{4,12},{5,13},{6,14},{7,15},{8,0},{9,1},... | collective-permute-start | bytes 393224 | tf_op jit(solution)/shard_map/ppermute | solution.py:410
  32.2 1.3 collective-permute-start.16
  33.5 2.9 %collective-permute-start.22 = (bf16[256,256]{1,0:T(8,128)(2,1)S(1)}, bf16[256,256]{1,0:T(8,128)(2,1)S(1)}, u32[]{:S(2)}, u32[]{:S(2)}) collective-permute-start(bf16[256,256]{1,0:T(8,128)(2,1)S(1)} %project.3), channel_id=1, source_target_pairs={{0,14},{1,15},{2,12},{3,13},{4,2},{5,3},{6,0},{7,1},{8,6},{9,7},{1... | collective-permute-start | bytes 393224 | tf_op jit(solution)/shard_map/ppermute | solution.py:410
  36.4 0.3 collective-permute-start.19
  36.6 0.0 collective-permute-start.18
  36.7 0.0 collective-permute-done.17
  36.7 1.2 collective-permute-start.21
  37.9 0.6 collective-permute-done.16
  38.6 1.4 collective-permute-start.20
  40.0 4.5 %collective-permute-done.18 = bf16[256,256]{1,0:T(8,128)(2,1)S(1)} collective-permute-done((bf16[256,256]{1,0:T(8,128)(2,1)S(1)}, bf16[256,256]{1,0:T(8,128)(2,1)S(1)}, u32[]{:S(2)}, u32[]{:S(2)}) %collective-permute-start.18) | collective-permute-done | bytes 131104 | tf_op jit(solution)/shard_map/ppermute | solution.py:410
  44.5 0.0 collective-permute-done.19
  44.5 2.4 %collective-permute-done.20 = bf16[256,256]{1,0:T(8,128)(2,1)S(1)} collective-permute-done((bf16[256,256]{1,0:T(8,128)(2,1)S(1)}, bf16[256,256]{1,0:T(8,128)(2,1)S(1)}, u32[]{:S(2)}, u32[]{:S(2)}) %collective-permute-start.20) | collective-permute-done | bytes 131104 | tf_op jit(solution)/shard_map/ppermute | solution.py:410
  46.9 0.0 collective-permute-done.21
  46.9 0.0 collective-permute-done.22
  46.9 3.5 %collective-permute-start.23 = (bf16[2048,256]{1,0:T(8,128)(2,1)S(1)}, bf16[2048,256]{1,0:T(8,128)(2,1)S(1)}, u32[]{:S(2)}, u32[]{:S(2)}) collective-permute-start(bf16[2048,256]{1,0:T(8,128)(2,1)S(1)} %constant_dynamic-update-slice_fusion.kv_ref), channel_id=1, source_target_pairs={{0,1},{1,0},{2,3},{3,2},{4,5},{5,4},{6,7},{7,6},{8,9},{9,8},{10,11... | collective-permute-start | bytes 3145736 | tf_op jit(solution)/shard_map/ppermute | solution.py:406
  50.4 0.0 copy-done.6
  50.4 0.0 copy-done.5
  50.5 0.0 copy-done.4
  50.5 46.2 %attend.2.rest_0_ = bf16[4,64,7424]{2,1,0:T(8,128)(2,1)} custom-call(s32[1]{0:T(128)} %bitcast.1.core_ref.half_ref, s32[4,16]{1,0:T(4,128)S(1)} %fusion.6.start_ref, s32[4]{0:T(128)S(1)} %copy-done.5, bf16[4,64,7424]{2,1,0:T(8,128)(2,1)} %q_hbm.3, bf16[2048,256]{1,0:T(8,128)(2,1)S(1)} %constant_dynamic-update-slice_fusion.kv_ref, ...), custom_call_target="tpu_custom_call" | custom-call | flops 2189426688 | bytes 3801088 | tf_op jit(solution)/shard_map/attend/pallas_call | solution.py:305
  96.7 0.0 collective-permute-done.23.kv_ref
  96.7 46.2 %attend.3 = bf16[4,64,7424]{2,1,0:T(8,128)(2,1)} custom-call(s32[1]{0:T(128)} %bitcast.half_ref, s32[4,16]{1,0:T(4,128)S(1)} %fusion.6.start_ref, s32[4]{0:T(128)S(1)} %copy-done.5, bf16[4,64,7424]{2,1,0:T(8,128)(2,1)} %q_hbm.3, bf16[2048,256]{1,0:T(8,128)(2,1)S(1)} %collective-permute-done.23.kv_ref, ...), custom_call_target="tpu_custom_call", output_to_operand_aliasing={{}: (6, {})} | custom-call | flops 2189426688 | bytes 3801088 | tf_op jit(solution)/shard_map/attend/pallas_call | solution.py:305
  (13 shorter events, 0.2 us)
Async XLA Ops:
  0.0 0.9 copy-start.3
  1.0 4.4 %copy-start = (bf16[4,128,4096]{2,1,0:T(8,128)(2,1)S(1)}, bf16[4,128,4096]{2,1,0:T(8,128)(2,1)}, u32[]{:S(2)}) copy-start(bf16[4,128,4096]{2,1,0:T(8,128)(2,1)} %states.1) | copy-start | bytes 12582916
  1.0 4.4 %copy-start.1 = (bf16[32,4096]{1,0:T(8,128)(2,1)S(1)}, bf16[32,4096]{1,0:T(8,128)(2,1)}, u32[]{:S(2)}) copy-start(bf16[32,4096]{1,0:T(8,128)(2,1)} %queries.1) | copy-start | bytes 786436
  1.0 4.4 %copy-start.2 = (bf16[4096]{0:T(1024)(128)(2,1)S(1)}, bf16[4096]{0:T(1024)(128)(2,1)}, u32[]{:S(2)}) copy-start(bf16[4096]{0:T(1024)(128)(2,1)} %gain.1) | copy-start | bytes 24580
  1.0 2.9 %collective-permute-start.1 = (bf16[256,256]{1,0:T(8,128)(2,1)S(1)}, bf16[256,256]{1,0:T(8,128)(2,1)S(1)}, u32[]{:S(2)}, u32[]{:S(2)}) collective-permute-start(bf16[256,256]{1,0:T(8,128)(2,1)S(1)} %get-tuple-element.13), channel_id=1, source_target_pairs={{0,1},{1,0},{2,3},{3,2},{4,5},{5,4},{6,7},{7,6},{8,9},{9,8},{10,11... | collective-permute-start | bytes 393224 | tf_op jit(solution)/shard_map/ppermute | solution.py:406
  1.1 7.3 %collective-permute-start.3 = (bf16[256,256]{1,0:T(8,128)(2,1)S(1)}, bf16[256,256]{1,0:T(8,128)(2,1)S(1)}, u32[]{:S(2)}, u32[]{:S(2)}) collective-permute-start(bf16[256,256]{1,0:T(8,128)(2,1)S(1)} %get-tuple-element.12.rest_0_), channel_id=1, source_target_pairs={{0,2},{1,3},{2,6},{3,7},{4,0},{5,1},{6,10},{7,11},{8,4},{9,5},{10,... | collective-permute-start | bytes 393224 | tf_op jit(solution)/shard_map/ppermute | solution.py:410
  3.8 4.7 %collective-permute-start = (bf16[256,256]{1,0:T(8,128)(2,1)S(1)}, bf16[256,256]{1,0:T(8,128)(2,1)S(1)}, u32[]{:S(2)}, u32[]{:S(2)}) collective-permute-start(bf16[256,256]{1,0:T(8,128)(2,1)S(1)} %get-tuple-element.12.rest_0_), channel_id=1, source_target_pairs={{0,4},{1,5},{2,0},{3,1},{4,8},{5,9},{6,2},{7,3},{8,12},{9,13},{10,... | collective-permute-start | bytes 393224 | tf_op jit(solution)/shard_map/ppermute | solution.py:410
  3.9 6.6 %collective-permute-start.4 = (bf16[256,256]{1,0:T(8,128)(2,1)S(1)}, bf16[256,256]{1,0:T(8,128)(2,1)S(1)}, u32[]{:S(2)}, u32[]{:S(2)}) collective-permute-start(bf16[256,256]{1,0:T(8,128)(2,1)S(1)} %collective-permute-done.1.rest_5_), channel_id=1, source_target_pairs={{0,2},{1,3},{2,6},{3,7},{4,0},{5,1},{6,10},{7,11},{8,4},{9,5},{10,... | collective-permute-start | bytes 393224 | tf_op jit(solution)/shard_map/ppermute | solution.py:410
  5.3 6.1 %collective-permute-start.2 = (bf16[256,256]{1,0:T(8,128)(2,1)S(1)}, bf16[256,256]{1,0:T(8,128)(2,1)S(1)}, u32[]{:S(2)}, u32[]{:S(2)}) collective-permute-start(bf16[256,256]{1,0:T(8,128)(2,1)S(1)} %collective-permute-done.1.rest_5_), channel_id=1, source_target_pairs={{0,4},{1,5},{2,0},{3,1},{4,8},{5,9},{6,2},{7,3},{8,12},{9,13},{10,... | collective-permute-start | bytes 393224 | tf_op jit(solution)/shard_map/ppermute | solution.py:410
  11.3 13.1 %collective-permute-start.5 = (bf16[128,4096]{1,0:T(8,128)(2,1)S(1)}, bf16[128,4096]{1,0:T(8,128)(2,1)S(1)}, u32[]{:S(2)}, u32[]{:S(2)}) collective-permute-start(bf16[128,4096]{1,0:T(8,128)(2,1)S(1)} %pool.1.own_ref), channel_id=1, source_target_pairs={{0,1},{1,0},{2,3},{3,2},{4,5},{5,4},{6,7},{7,6},{8,9},{9,8},{10,11... | collective-permute-start | bytes 3145736 | tf_op jit(solution)/shard_map/ppermute | solution.py:406
  12.5 5.1 %collective-permute-start.6 = (bf16[256,256]{1,0:T(8,128)(2,1)S(1)}, bf16[256,256]{1,0:T(8,128)(2,1)S(1)}, u32[]{:S(2)}, u32[]{:S(2)}) collective-permute-start(bf16[256,256]{1,0:T(8,128)(2,1)S(1)} %collective-permute-done.rest_1_), channel_id=1, source_target_pairs={{0,4},{1,5},{2,0},{3,1},{4,8},{5,9},{6,2},{7,3},{8,12},{9,13},{10,... | collective-permute-start | bytes 393224 | tf_op jit(solution)/shard_map/ppermute | solution.py:410
  12.6 5.1 %collective-permute-start.13 = (bf16[256,256]{1,0:T(8,128)(2,1)S(1)}, bf16[256,256]{1,0:T(8,128)(2,1)S(1)}, u32[]{:S(2)}, u32[]{:S(2)}) collective-permute-start(bf16[256,256]{1,0:T(8,128)(2,1)S(1)} %collective-permute-done.4.rest_7_), channel_id=1, source_target_pairs={{0,2},{1,3},{2,6},{3,7},{4,0},{5,1},{6,10},{7,11},{8,4},{9,5},{10,... | collective-permute-start | bytes 393224 | tf_op jit(solution)/shard_map/ppermute | solution.py:410
  14.0 6.2 %collective-permute-start.8 = (bf16[256,256]{1,0:T(8,128)(2,1)S(1)}, bf16[256,256]{1,0:T(8,128)(2,1)S(1)}, u32[]{:S(2)}, u32[]{:S(2)}) collective-permute-start(bf16[256,256]{1,0:T(8,128)(2,1)S(1)} %collective-permute-done.3.rest_2_), channel_id=1, source_target_pairs={{0,2},{1,3},{2,6},{3,7},{4,0},{5,1},{6,10},{7,11},{8,4},{9,5},{10,... | collective-permute-start | bytes 393224 | tf_op jit(solution)/shard_map/ppermute | solution.py:410
  15.3 6.3 %collective-permute-start.11 = (bf16[256,256]{1,0:T(8,128)(2,1)S(1)}, bf16[256,256]{1,0:T(8,128)(2,1)S(1)}, u32[]{:S(2)}, u32[]{:S(2)}) collective-permute-start(bf16[256,256]{1,0:T(8,128)(2,1)S(1)} %collective-permute-done.2.rest_6_), channel_id=1, source_target_pairs={{0,4},{1,5},{2,0},{3,1},{4,8},{5,9},{6,2},{7,3},{8,12},{9,13},{10,... | collective-permute-start | bytes 393224 | tf_op jit(solution)/shard_map/ppermute | solution.py:410
  17.6 5.3 %collective-permute-start.7 = (bf16[256,256]{1,0:T(8,128)(2,1)S(1)}, bf16[256,256]{1,0:T(8,128)(2,1)S(1)}, u32[]{:S(2)}, u32[]{:S(2)}) collective-permute-start(bf16[256,256]{1,0:T(8,128)(2,1)S(1)} %collective-permute-done.6.rest_3_), channel_id=1, source_target_pairs={{0,4},{1,5},{2,0},{3,1},{4,8},{5,9},{6,2},{7,3},{8,12},{9,13},{10,... | collective-permute-start | bytes 393224 | tf_op jit(solution)/shard_map/ppermute | solution.py:410
  17.7 5.4 %collective-permute-start.14 = (bf16[256,256]{1,0:T(8,128)(2,1)S(1)}, bf16[256,256]{1,0:T(8,128)(2,1)}, u32[]{:S(2)}, u32[]{:S(2)}) collective-permute-start(bf16[256,256]{1,0:T(8,128)(2,1)S(1)} %collective-permute-done.13.rest_9_), channel_id=1, source_target_pairs={{0,2},{1,3},{2,6},{3,7},{4,0},{5,1},{6,10},{7,11},{8,4},{9,5},{10,... | collective-permute-start | bytes 393224 | tf_op jit(solution)/shard_map/ppermute | solution.py:410
  20.2 5.3 %collective-permute-start.9 = (bf16[256,256]{1,0:T(8,128)(2,1)S(1)}, bf16[256,256]{1,0:T(8,128)(2,1)}, u32[]{:S(2)}, u32[]{:S(2)}) collective-permute-start(bf16[256,256]{1,0:T(8,128)(2,1)S(1)} %collective-permute-done.8.rest_4_), channel_id=1, source_target_pairs={{0,2},{1,3},{2,6},{3,7},{4,0},{5,1},{6,10},{7,11},{8,4},{9,5},{10,... | collective-permute-start | bytes 393224 | tf_op jit(solution)/shard_map/ppermute | solution.py:410
  21.6 4.2 %collective-permute-start.12 = (bf16[256,256]{1,0:T(8,128)(2,1)S(1)}, bf16[256,256]{1,0:T(8,128)(2,1)}, u32[]{:S(2)}, u32[]{:S(2)}) collective-permute-start(bf16[256,256]{1,0:T(8,128)(2,1)S(1)} %collective-permute-done.11.rest_8_), channel_id=1, source_target_pairs={{0,4},{1,5},{2,0},{3,1},{4,8},{5,9},{6,2},{7,3},{8,12},{9,13},{10,... | collective-permute-start | bytes 393224 | tf_op jit(solution)/shard_map/ppermute | solution.py:410
  23.0 4.7 %collective-permute-start.10 = (bf16[256,256]{1,0:T(8,128)(2,1)S(1)}, bf16[256,256]{1,0:T(8,128)(2,1)}, u32[]{:S(2)}, u32[]{:S(2)}) collective-permute-start(bf16[256,256]{1,0:T(8,128)(2,1)S(1)} %collective-permute-done.7.rest_0_), channel_id=1, source_target_pairs={{0,4},{1,5},{2,0},{3,1},{4,8},{5,9},{6,2},{7,3},{8,12},{9,13},{10,... | collective-permute-start | bytes 393224 | tf_op jit(solution)/shard_map/ppermute | solution.py:410
  23.2 4.9 %collective-permute-start.15 = (bf16[256,256]{1,0:T(8,128)(2,1)}, bf16[256,256]{1,0:T(8,128)(2,1)}, u32[]{:S(2)}, u32[]{:S(2)}) collective-permute-start(bf16[256,256]{1,0:T(8,128)(2,1)} %collective-permute-done.14.rest_4_), channel_id=1, source_target_pairs={{0,2},{1,3},{2,6},{3,7},{4,0},{5,1},{6,10},{7,11},{8,4},{9,5},{10,... | collective-permute-start | bytes 393224 | tf_op jit(solution)/shard_map/ppermute | solution.py:410
  24.4 26.0 %copy-start.6 = (s32[4,16]{1,0:T(4,128)S(1)}, s32[4,16]{1,0:T(4,128)}, u32[]{:S(2)}) copy-start(s32[4,16]{1,0:T(4,128)} %param.12) | copy-start | bytes 772
  24.4 26.0 %copy-start.5 = (s32[4]{0:T(128)S(1)}, s32[4]{0:T(128)}, u32[]{:S(2)}) copy-start(s32[4]{0:T(128)} %length_ref.3) | copy-start | bytes 52
  25.0 25.5 %copy-start.4 = (bf16[4,64,512]{2,1,0:T(8,128)(2,1)S(1)}, bf16[4,64,512]{2,1,0:T(8,128)(2,1)}, u32[]{:S(2)}) copy-start(bf16[4,64,512]{2,1,0:T(8,128)(2,1)} %own_kv_ref.3) | copy-start | bytes 786436
  29.7 7.0 %collective-permute-start.17 = (bf16[256,256]{1,0:T(8,128)(2,1)S(1)}, bf16[256,256]{1,0:T(8,128)(2,1)S(1)}, u32[]{:S(2)}, u32[]{:S(2)}) collective-permute-start(bf16[256,256]{1,0:T(8,128)(2,1)S(1)} %project.3), channel_id=1, source_target_pairs={{0,8},{1,9},{2,10},{3,11},{4,12},{5,13},{6,14},{7,15},{8,0},{9,1},... | collective-permute-start | bytes 393224 | tf_op jit(solution)/shard_map/ppermute | solution.py:410
  32.2 6.4 %collective-permute-start.16 = (bf16[256,256]{1,0:T(8,128)(2,1)S(1)}, bf16[256,256]{1,0:T(8,128)(2,1)S(1)}, u32[]{:S(2)}, u32[]{:S(2)}) collective-permute-start(bf16[256,256]{1,0:T(8,128)(2,1)S(1)} %project.3), channel_id=1, source_target_pairs={{0,4},{1,5},{2,6},{3,7},{4,8},{5,9},{6,10},{7,11},{8,12},{9,13},{1... | collective-permute-start | bytes 393224 | tf_op jit(solution)/shard_map/ppermute | solution.py:410
  33.5 13.4 %collective-permute-start.22 = (bf16[256,256]{1,0:T(8,128)(2,1)S(1)}, bf16[256,256]{1,0:T(8,128)(2,1)S(1)}, u32[]{:S(2)}, u32[]{:S(2)}) collective-permute-start(bf16[256,256]{1,0:T(8,128)(2,1)S(1)} %project.3), channel_id=1, source_target_pairs={{0,14},{1,15},{2,12},{3,13},{4,2},{5,3},{6,0},{7,1},{8,6},{9,7},{1... | collective-permute-start | bytes 393224 | tf_op jit(solution)/shard_map/ppermute | solution.py:410
  36.4 8.1 %collective-permute-start.19 = (bf16[256,256]{1,0:T(8,128)(2,1)S(1)}, bf16[256,256]{1,0:T(8,128)(2,1)S(1)}, u32[]{:S(2)}, u32[]{:S(2)}) collective-permute-start(bf16[256,256]{1,0:T(8,128)(2,1)S(1)} %project.3), channel_id=1, source_target_pairs={{0,2},{1,3},{2,0},{3,1},{4,6},{5,7},{6,4},{7,5},{8,10},{9,11},{10,... | collective-permute-start | bytes 393224 | tf_op jit(solution)/shard_map/ppermute | solution.py:410
  36.6 7.8 %collective-permute-start.18 = (bf16[256,256]{1,0:T(8,128)(2,1)S(1)}, bf16[256,256]{1,0:T(8,128)(2,1)S(1)}, u32[]{:S(2)}, u32[]{:S(2)}) collective-permute-start(bf16[256,256]{1,0:T(8,128)(2,1)S(1)} %project.3), channel_id=1, source_target_pairs={{0,12},{1,13},{2,14},{3,15},{4,0},{5,1},{6,2},{7,3},{8,4},{9,5},{1... | collective-permute-start | bytes 393224 | tf_op jit(solution)/shard_map/ppermute | solution.py:410
  36.7 10.2 %collective-permute-start.21 = (bf16[256,256]{1,0:T(8,128)(2,1)S(1)}, bf16[256,256]{1,0:T(8,128)(2,1)S(1)}, u32[]{:S(2)}, u32[]{:S(2)}) collective-permute-start(bf16[256,256]{1,0:T(8,128)(2,1)S(1)} %collective-permute-done.17), channel_id=1, source_target_pairs={{0,2},{1,3},{2,0},{3,1},{4,6},{5,7},{6,4},{7,5},{8,10},{9,11},{10,... | collective-permute-start | bytes 393224 | tf_op jit(solution)/shard_map/ppermute | solution.py:410
  38.6 8.3 %collective-permute-start.20 = (bf16[256,256]{1,0:T(8,128)(2,1)S(1)}, bf16[256,256]{1,0:T(8,128)(2,1)S(1)}, u32[]{:S(2)}, u32[]{:S(2)}) collective-permute-start(bf16[256,256]{1,0:T(8,128)(2,1)S(1)} %collective-permute-done.16), channel_id=1, source_target_pairs={{0,2},{1,3},{2,0},{3,1},{4,6},{5,7},{6,4},{7,5},{8,10},{9,11},{10,... | collective-permute-start | bytes 393224 | tf_op jit(solution)/shard_map/ppermute | solution.py:410
  46.9 49.8 %collective-permute-start.23 = (bf16[2048,256]{1,0:T(8,128)(2,1)S(1)}, bf16[2048,256]{1,0:T(8,128)(2,1)S(1)}, u32[]{:S(2)}, u32[]{:S(2)}) collective-permute-start(bf16[2048,256]{1,0:T(8,128)(2,1)S(1)} %constant_dynamic-update-slice_fusion.kv_ref), channel_id=1, source_target_pairs={{0,1},{1,0},{2,3},{3,2},{4,5},{5,4},{6,7},{7,6},{8,9},{9,8},{10,11... | collective-permute-start | bytes 3145736 | tf_op jit(solution)/shard_map/ppermute | solution.py:406

commit v16 on v15

--- a/solution.py
+++ b/solution.py
@@ -128,8 +128,14 @@
     )(states, queries, gain)
 
 
-def attend_kernel(half_ref, start_ref, length_ref, q_hbm, kv_ref, own_kv_ref, *rest):
-    out_hbm = rest[-13]
+def attend_kernel(begun, ahead, half_ref, start_ref, length_ref, q_hbm, kv_ref, own_kv_ref, *rest):
+    if ahead:
+        other_at = pl.multiple_of((1 - half_ref[0]) * HALF, LANES)
+        coming = pltpu.make_async_copy(q_hbm.at[0, :, pl.ds(other_at, HALF)], rest[-14], rest[-1])
+        coming.start()
+        out_hbm, rest = rest[-15], rest[:-1]
+    else:
+        out_hbm = rest[-13]
     (
         questions, answers, memory, key_side, value_side, weights, bias, marker, scores, all_weights,
         arrived, sent,
@@ -149,7 +155,10 @@
             answers.at[query], out_hbm.at[query, :, pl.ds(half_at, HALF)], sent.at[query]
         )
 
-    fetch(0).start()
+    if begun:
+        questions[0] = rest[0][...]
+    else:
+        fetch(0).start()
     lane = lax.broadcasted_iota(jnp.int32, (KEYS, LANES), 1)
     row = lax.broadcasted_iota(jnp.int32, (KEYS, LANES), 0)
     in_b = ((row >= ROWS) & (row < 2 * ROWS)) | (row >= 2 * ROWS + QLEN)
@@ -189,7 +198,13 @@
         alive = token < length
         sample = lax.div(key, HD // STEP)
 
-        fetch(query).wait()
+        if begun:
+
+            @pl.when(query > 0)
+            def _():
+                fetch(query).wait()
+        else:
+            fetch(query).wait()
 
         @pl.when(query + 1 < count)
         def _():
@@ -290,23 +305,34 @@
     lax.fori_loop(0, count, answer, 0)
     for query in range(count):
         send(query).wait()
-
-
-def attend(half, starts, lengths, questions, memory_kv, own_kv, earlier=None):
+    if ahead:
+        coming.wait()
+
+
+def attend(half, starts, lengths, questions, memory_kv, own_kv, earlier=None, begun=None, ahead=False):
     count = questions.shape[0]
     hbm, vmem, smem = (pl.BlockSpec(memory_space=x) for x in (pltpu.HBM, pltpu.VMEM, pltpu.SMEM))
     operands = [half.reshape(1), starts, lengths, questions, memory_kv, own_kv]
     in_specs = [smem, smem, smem, hbm, vmem, vmem]
     aliases = {}
+    if begun is not None:
+        operands.append(begun)
+        in_specs.append(vmem)
     if earlier is not None:
         aliases = {len(operands): 0}
         operands.append(earlier)
         in_specs.append(hbm)
-    return pl.pallas_call(
-        attend_kernel,
+    out_specs, extra = [hbm], []
+    out_shape = [jax.ShapeDtypeStruct((count, QLEN, H * HD), jnp.bfloat16)]
+    if ahead:
+        out_specs.append(vmem)
+        out_shape.append(jax.ShapeDtypeStruct((QLEN, HALF), jnp.bfloat16))
+        extra = [pltpu.SemaphoreType.DMA]
+    got = pl.pallas_call(
+        functools.partial(attend_kernel, begun is not None, ahead),
         in_specs=in_specs,
-        out_specs=hbm,
-        out_shape=jax.ShapeDtypeStruct((count, QLEN, H * HD), jnp.bfloat16),
+        out_specs=out_specs,
+        out_shape=out_shape,
         scratch_shapes=[
             pltpu.VMEM((count, QLEN, HALF), jnp.bfloat16),
             pltpu.VMEM((count, QLEN, HALF), jnp.bfloat16),
@@ -320,6 +346,7 @@
             pltpu.VMEM((STEP * QLEN, KEYS), jnp.bfloat16),
             pltpu.SemaphoreType.DMA((count,)),
             pltpu.SemaphoreType.DMA((count,)),
+            *extra,
         ],
         input_output_aliases=aliases,
         compiler_params=pltpu.CompilerParams(vmem_limit_bytes=50 * MIB),
@@ -330,6 +357,7 @@
         ),
         name="attend",
     )(*operands)
+    return got if ahead else got[0]
 
 
 def project_kernel(ring, pieces, more, core_ref, place_ref, own_ref, other_ref, *rest):
@@ -367,7 +395,7 @@
         out_shape=jax.ShapeDtypeStruct((2 * count, width), jnp.float32 if more else jnp.bfloat16),
         compiler_params=pltpu.CompilerParams(vmem_limit_bytes=16 * MIB),
         cost_estimate=pl.CostEstimate(
-            flops=4 * count * D * width, bytes_accessed=2 * D * width, transcendentals=0
+            flops=count * D * width, bytes_accessed=32 * D * width, transcendentals=0
         ),
         name="project",
     )(core.reshape(1), place, *operands)
@@ -461,8 +489,8 @@
     slot = back + lines * lax.rem(lax.rem(chip, 2) + lax.rem(of_chip, 2), 2)
     starts = (slot * CHIP + lax.rem(retrieval, CHIP)) * MEM
     rest = (starts, question_lengths, question_queries)
-    context = attend(core, *rest, near, question_kv)
-    return attend(1 - core, *rest, far, question_kv, context)
+    context, begun = attend(core, *rest, near, question_kv, ahead=True)
+    return attend(1 - core, *rest, far, question_kv, context, begun)
 
 
 def solution(mesh):

time: 145 us -> 145 us (level)
  no operation moved by 1% of the time
where the time goes in v16:
time: 145 us; the launch traced here: 143 us
  Pallas kernels  97.3 us (67%)
  starting transfers between devices  26 us (18%)
  waiting for transfers between devices  18.1 us (12%)
    pallas_call x2, Pallas kernels, attend(): pl.pallas_call(functools.partial(attend_kernel, begun is not None, ahead)...  92.1 us
    ppermute x21, starting transfers between devices, along(): lax.ppermute(x, 'pass', [(2 * s + c, 2 * d + c) for s, d in pairs for c i...  21.2 us
    ppermute x21, waiting for transfers between devices, along(): lax.ppermute(x, 'pass', [(2 * s + c, 2 * d + c) for s, d in pairs for c i...  18.1 us
    ppermute x3, starting transfers between devices, to_partner(): return lax.ppermute(x, 'pass', [(i, i ^ 1) for i in range(extent)])  4.77 us
    pallas_call x1, Pallas kernels, pool(): pl.pallas_call(pool_kernel, in_specs=[vmem] * 3, out_specs=vmem, out_shap...  3.08 us
  transfers between devices with their start and end apart: 24, of which 13 were waited for; matrix products, arithmetic and copies ran while one was open for 0% of the time, Pallas kernels for 35%

profile of v16, /device:TPU:1, one launch (start us, length us, event | category | flops | bytes accessed | tf_op | source)
XLA Modules:
  0.0 142.7 jit_solution(12058158521556861942)
XLA Ops:
  0.0 0.0 copy-start.3
  0.0 0.9 copy-done.3
  1.0 0.0 copy-start
  1.0 0.0 copy-start.1
  1.0 0.1 collective-permute-start.1
  1.1 2.7 %collective-permute-start.3 = (bf16[256,256]{1,0:T(8,128)(2,1)S(1)}, bf16[256,256]{1,0:T(8,128)(2,1)S(1)}, u32[]{:S(2)}, u32[]{:S(2)}) collective-permute-start(bf16[256,256]{1,0:T(8,128)(2,1)S(1)} %get-tuple-element.14.rest_0_), channel_id=1, source_target_pairs={{0,2},{1,3},{2,6},{3,7},{4,0},{5,1},{6,10},{7,11},{8,4},{9,5},{10,... | collective-permute-start | bytes 393224 | tf_op jit(solution)/shard_map/ppermute | solution.py:438
  3.8 0.1 collective-permute-start
  3.9 0.0 collective-permute-done.1.rest_5_
  3.9 1.4 collective-permute-start.4
  5.3 0.1 collective-permute-start.2
  5.3 0.0 copy-done
  5.4 0.0 copy-done.1
  5.4 0.0 copy-done.2
  5.4 3.1 %pool.1.own_ref = bf16[128,4096]{1,0:T(8,128)(2,1)S(1)} custom-call(bf16[4,128,4096]{2,1,0:T(8,128)(2,1)S(1)} %copy-done, bf16[32,4096]{1,0:T(8,128)(2,1)S(1)} %copy-done.1, bf16[4096]{0:T(1024)(128)(2,1)S(1)} %copy-done.2), custom_call_target="tpu_custom_call" | custom-call | flops 268435456 | bytes 4194304 | tf_op jit(solution)/shard_map/pool/pallas_call | solution.py:116
  8.4 0.0 collective-permute-done.3.rest_2_
  8.5 0.1 collective-permute-done.rest_1_
  8.5 2.0 %collective-permute-done.4.rest_7_ = bf16[256,256]{1,0:T(8,128)(2,1)S(1)} collective-permute-done((bf16[256,256]{1,0:T(8,128)(2,1)S(1)}, bf16[256,256]{1,0:T(8,128)(2,1)S(1)}, u32[]{:S(2)}, u32[]{:S(2)}) %collective-permute-start.4) | collective-permute-done | bytes 131104 | tf_op jit(solution)/shard_map/ppermute | solution.py:438
  10.5 0.9 collective-permute-done.2.rest_6_
  11.3 1.2 collective-permute-start.5
  12.5 0.1 collective-permute-start.6
  12.6 1.4 collective-permute-start.13
  14.0 1.3 collective-permute-start.8
  15.3 0.2 collective-permute-start.11
  15.4 2.2 %collective-permute-done.6.rest_3_ = bf16[256,256]{1,0:T(8,128)(2,1)S(1)} collective-permute-done((bf16[256,256]{1,0:T(8,128)(2,1)S(1)}, bf16[256,256]{1,0:T(8,128)(2,1)S(1)}, u32[]{:S(2)}, u32[]{:S(2)}) %collective-permute-start.6) | collective-permute-done | bytes 131104 | tf_op jit(solution)/shard_map/ppermute | solution.py:438
  17.6 0.1 collective-permute-start.7
  17.7 0.0 collective-permute-done.13.rest_9_
  17.7 1.4 collective-permute-start.14
  19.1 1.1 collective-permute-done.8.rest_4_
  20.2 1.4 collective-permute-start.9
  21.6 0.0 collective-permute-done.11.rest_8_
  21.6 0.1 collective-permute-start.12
  21.7 1.3 collective-permute-done.7.rest_0_
  23.0 0.2 collective-permute-start.10
  23.2 0.0 collective-permute-done.14.rest_4_
  23.2 1.3 collective-permute-start.15
  24.4 0.0 collective-permute-done.5.other_ref
  24.4 0.5 project.2.rest_6_
  25.0 0.0 copy-start.4
  25.0 0.5 collective-permute-done.9.rest_1_
  25.5 0.3 collective-permute-done.12.rest_3_
  25.8 1.9 %collective-permute-done.10.rest_2_ = bf16[256,256]{1,0:T(8,128)(2,1)} collective-permute-done((bf16[256,256]{1,0:T(8,128)(2,1)S(1)}, bf16[256,256]{1,0:T(8,128)(2,1)}, u32[]{:S(2)}, u32[]{:S(2)}) %collective-permute-start.10) | collective-permute-done | bytes 131104 | tf_op jit(solution)/shard_map/ppermute | solution.py:438
  27.7 0.4 collective-permute-done.15.rest_5_
  28.1 1.5 %project.3 = bf16[256,256]{1,0:T(8,128)(2,1)S(1)} custom-call(s32[1]{0:T(128)} %bitcast.1.core_ref.half_ref, s32[1]{0:T(128)} %bitcast.2.place_ref, bf16[128,4096]{1,0:T(8,128)(2,1)S(1)} %pool.1.own_ref, bf16[128,4096]{1,0:T(8,128)(2,1)S(1)} %collective-permute-done.5.other_ref, bf16[256,256]{1,0:T(8,128)(2,1)S(1)} %collective-permute-done.7.rest_0_, ...), custom_call_target="tpu_custom_call" | custom-call | flops 134217728 | bytes 33554432 | tf_op jit(solution)/shard_map/project/pallas_call | solution.py:391
  29.7 2.5 %collective-permute-start.17 = (bf16[256,256]{1,0:T(8,128)(2,1)S(1)}, bf16[256,256]{1,0:T(8,128)(2,1)S(1)}, u32[]{:S(2)}, u32[]{:S(2)}) collective-permute-start(bf16[256,256]{1,0:T(8,128)(2,1)S(1)} %project.3), channel_id=1, source_target_pairs={{0,8},{1,9},{2,10},{3,11},{4,12},{5,13},{6,14},{7,15},{8,0},{9,1},... | collective-permute-start | bytes 393224 | tf_op jit(solution)/shard_map/ppermute | solution.py:438
  32.2 1.3 collective-permute-start.16
  33.5 2.9 %collective-permute-start.22 = (bf16[256,256]{1,0:T(8,128)(2,1)S(1)}, bf16[256,256]{1,0:T(8,128)(2,1)S(1)}, u32[]{:S(2)}, u32[]{:S(2)}) collective-permute-start(bf16[256,256]{1,0:T(8,128)(2,1)S(1)} %project.3), channel_id=1, source_target_pairs={{0,14},{1,15},{2,12},{3,13},{4,2},{5,3},{6,0},{7,1},{8,6},{9,7},{1... | collective-permute-start | bytes 393224 | tf_op jit(solution)/shard_map/ppermute | solution.py:438
  36.4 0.3 collective-permute-start.19
  36.6 0.0 collective-permute-start.18
  36.7 0.0 collective-permute-done.17
  36.7 1.2 collective-permute-start.21
  37.9 0.6 collective-permute-done.16
  38.6 1.4 collective-permute-start.20
  40.0 4.5 %collective-permute-done.18 = bf16[256,256]{1,0:T(8,128)(2,1)S(1)} collective-permute-done((bf16[256,256]{1,0:T(8,128)(2,1)S(1)}, bf16[256,256]{1,0:T(8,128)(2,1)S(1)}, u32[]{:S(2)}, u32[]{:S(2)}) %collective-permute-start.18) | collective-permute-done | bytes 131104 | tf_op jit(solution)/shard_map/ppermute | solution.py:438
  44.5 0.0 collective-permute-done.19
  44.5 2.4 %collective-permute-done.20 = bf16[256,256]{1,0:T(8,128)(2,1)S(1)} collective-permute-done((bf16[256,256]{1,0:T(8,128)(2,1)S(1)}, bf16[256,256]{1,0:T(8,128)(2,1)S(1)}, u32[]{:S(2)}, u32[]{:S(2)}) %collective-permute-start.20) | collective-permute-done | bytes 131104 | tf_op jit(solution)/shard_map/ppermute | solution.py:438
  46.9 0.0 collective-permute-done.21
  46.9 0.0 collective-permute-done.22
  46.9 3.5 %collective-permute-start.23 = (bf16[2048,256]{1,0:T(8,128)(2,1)S(1)}, bf16[2048,256]{1,0:T(8,128)(2,1)S(1)}, u32[]{:S(2)}, u32[]{:S(2)}) collective-permute-start(bf16[2048,256]{1,0:T(8,128)(2,1)S(1)} %constant_dynamic-update-slice_fusion.kv_ref), channel_id=1, source_target_pairs={{0,1},{1,0},{2,3},{3,2},{4,5},{5,4},{6,7},{7,6},{8,9},{9,8},{10,11... | collective-permute-start | bytes 3145736 | tf_op jit(solution)/shard_map/ppermute | solution.py:434
  50.4 0.0 copy-done.6
  50.4 0.0 copy-done.5
  50.5 0.0 copy-done.4
  50.5 46.4 %attend.2 = (bf16[4,64,7424]{2,1,0:T(8,128)(2,1)}, bf16[64,3712]{1,0:T(8,128)(2,1)S(1)}) custom-call(s32[1]{0:T(128)} %bitcast.1.core_ref.half_ref, s32[4,16]{1,0:T(4,128)S(1)} %fusion.6.start_ref, s32[4]{0:T(128)S(1)} %copy-done.5, bf16[4,64,7424]{2,1,0:T(8,128)(2,1)} %q_hbm.3, bf16[2048,256]{1,0:T(8,128)(2,1)S(1)} %constant_dynamic-update-slice_fusion.kv_ref, ...), custom_call_target="tpu_custom_call" | custom-call | flops 2189426688 | bytes 3801088 | tf_op jit(solution)/shard_map/attend/pallas_call | solution.py:331
  96.9 0.0 collective-permute-done.23.kv_ref
  96.9 45.7 %attend.3 = bf16[4,64,7424]{2,1,0:T(8,128)(2,1)} custom-call(s32[1]{0:T(128)} %bitcast.half_ref, s32[4,16]{1,0:T(4,128)S(1)} %fusion.6.start_ref, s32[4]{0:T(128)S(1)} %copy-done.5, bf16[4,64,7424]{2,1,0:T(8,128)(2,1)} %q_hbm.3, bf16[2048,256]{1,0:T(8,128)(2,1)S(1)} %collective-permute-done.23.kv_ref, ...), custom_call_target="tpu_custom_call", output_to_operand_aliasing={{}: (7, {})} | custom-call | flops 2189426688 | bytes 3801088 | tf_op jit(solution)/shard_map/attend/pallas_call | solution.py:331
  (13 shorter events, 0.2 us)
Async XLA Ops:
  0.0 0.9 copy-start.3
  1.0 4.4 %copy-start = (bf16[4,128,4096]{2,1,0:T(8,128)(2,1)S(1)}, bf16[4,128,4096]{2,1,0:T(8,128)(2,1)}, u32[]{:S(2)}) copy-start(bf16[4,128,4096]{2,1,0:T(8,128)(2,1)} %states.1) | copy-start | bytes 12582916
  1.0 4.4 %copy-start.1 = (bf16[32,4096]{1,0:T(8,128)(2,1)S(1)}, bf16[32,4096]{1,0:T(8,128)(2,1)}, u32[]{:S(2)}) copy-start(bf16[32,4096]{1,0:T(8,128)(2,1)} %queries.1) | copy-start | bytes 786436
  1.0 4.4 %copy-start.2 = (bf16[4096]{0:T(1024)(128)(2,1)S(1)}, bf16[4096]{0:T(1024)(128)(2,1)}, u32[]{:S(2)}) copy-start(bf16[4096]{0:T(1024)(128)(2,1)} %gain.1) | copy-start | bytes 24580
  1.0 2.9 %collective-permute-start.1 = (bf16[256,256]{1,0:T(8,128)(2,1)S(1)}, bf16[256,256]{1,0:T(8,128)(2,1)S(1)}, u32[]{:S(2)}, u32[]{:S(2)}) collective-permute-start(bf16[256,256]{1,0:T(8,128)(2,1)S(1)} %get-tuple-element.15), channel_id=1, source_target_pairs={{0,1},{1,0},{2,3},{3,2},{4,5},{5,4},{6,7},{7,6},{8,9},{9,8},{10,11... | collective-permute-start | bytes 393224 | tf_op jit(solution)/shard_map/ppermute | solution.py:434
  1.1 7.3 %collective-permute-start.3 = (bf16[256,256]{1,0:T(8,128)(2,1)S(1)}, bf16[256,256]{1,0:T(8,128)(2,1)S(1)}, u32[]{:S(2)}, u32[]{:S(2)}) collective-permute-start(bf16[256,256]{1,0:T(8,128)(2,1)S(1)} %get-tuple-element.14.rest_0_), channel_id=1, source_target_pairs={{0,2},{1,3},{2,6},{3,7},{4,0},{5,1},{6,10},{7,11},{8,4},{9,5},{10,... | collective-permute-start | bytes 393224 | tf_op jit(solution)/shard_map/ppermute | solution.py:438
  3.8 4.7 %collective-permute-start = (bf16[256,256]{1,0:T(8,128)(2,1)S(1)}, bf16[256,256]{1,0:T(8,128)(2,1)S(1)}, u32[]{:S(2)}, u32[]{:S(2)}) collective-permute-start(bf16[256,256]{1,0:T(8,128)(2,1)S(1)} %get-tuple-element.14.rest_0_), channel_id=1, source_target_pairs={{0,4},{1,5},{2,0},{3,1},{4,8},{5,9},{6,2},{7,3},{8,12},{9,13},{10,... | collective-permute-start | bytes 393224 | tf_op jit(solution)/shard_map/ppermute | solution.py:438
  3.9 6.6 %collective-permute-start.4 = (bf16[256,256]{1,0:T(8,128)(2,1)S(1)}, bf16[256,256]{1,0:T(8,128)(2,1)S(1)}, u32[]{:S(2)}, u32[]{:S(2)}) collective-permute-start(bf16[256,256]{1,0:T(8,128)(2,1)S(1)} %collective-permute-done.1.rest_5_), channel_id=1, source_target_pairs={{0,2},{1,3},{2,6},{3,7},{4,0},{5,1},{6,10},{7,11},{8,4},{9,5},{10,... | collective-permute-start | bytes 393224 | tf_op jit(solution)/shard_map/ppermute | solution.py:438
  5.3 6.1 %collective-permute-start.2 = (bf16[256,256]{1,0:T(8,128)(2,1)S(1)}, bf16[256,256]{1,0:T(8,128)(2,1)S(1)}, u32[]{:S(2)}, u32[]{:S(2)}) collective-permute-start(bf16[256,256]{1,0:T(8,128)(2,1)S(1)} %collective-permute-done.1.rest_5_), channel_id=1, source_target_pairs={{0,4},{1,5},{2,0},{3,1},{4,8},{5,9},{6,2},{7,3},{8,12},{9,13},{10,... | collective-permute-start | bytes 393224 | tf_op jit(solution)/shard_map/ppermute | solution.py:438
  11.3 13.1 %collective-permute-start.5 = (bf16[128,4096]{1,0:T(8,128)(2,1)S(1)}, bf16[128,4096]{1,0:T(8,128)(2,1)S(1)}, u32[]{:S(2)}, u32[]{:S(2)}) collective-permute-start(bf16[128,4096]{1,0:T(8,128)(2,1)S(1)} %pool.1.own_ref), channel_id=1, source_target_pairs={{0,1},{1,0},{2,3},{3,2},{4,5},{5,4},{6,7},{7,6},{8,9},{9,8},{10,11... | collective-permute-start | bytes 3145736 | tf_op jit(solution)/shard_map/ppermute | solution.py:434
  12.5 5.1 %collective-permute-start.6 = (bf16[256,256]{1,0:T(8,128)(2,1)S(1)}, bf16[256,256]{1,0:T(8,128)(2,1)S(1)}, u32[]{:S(2)}, u32[]{:S(2)}) collective-permute-start(bf16[256,256]{1,0:T(8,128)(2,1)S(1)} %collective-permute-done.rest_1_), channel_id=1, source_target_pairs={{0,4},{1,5},{2,0},{3,1},{4,8},{5,9},{6,2},{7,3},{8,12},{9,13},{10,... | collective-permute-start | bytes 393224 | tf_op jit(solution)/shard_map/ppermute | solution.py:438
  12.6 5.1 %collective-permute-start.13 = (bf16[256,256]{1,0:T(8,128)(2,1)S(1)}, bf16[256,256]{1,0:T(8,128)(2,1)S(1)}, u32[]{:S(2)}, u32[]{:S(2)}) collective-permute-start(bf16[256,256]{1,0:T(8,128)(2,1)S(1)} %collective-permute-done.4.rest_7_), channel_id=1, source_target_pairs={{0,2},{1,3},{2,6},{3,7},{4,0},{5,1},{6,10},{7,11},{8,4},{9,5},{10,... | collective-permute-start | bytes 393224 | tf_op jit(solution)/shard_map/ppermute | solution.py:438
  14.0 6.2 %collective-permute-start.8 = (bf16[256,256]{1,0:T(8,128)(2,1)S(1)}, bf16[256,256]{1,0:T(8,128)(2,1)S(1)}, u32[]{:S(2)}, u32[]{:S(2)}) collective-permute-start(bf16[256,256]{1,0:T(8,128)(2,1)S(1)} %collective-permute-done.3.rest_2_), channel_id=1, source_target_pairs={{0,2},{1,3},{2,6},{3,7},{4,0},{5,1},{6,10},{7,11},{8,4},{9,5},{10,... | collective-permute-start | bytes 393224 | tf_op jit(solution)/shard_map/ppermute | solution.py:438
  15.3 6.3 %collective-permute-start.11 = (bf16[256,256]{1,0:T(8,128)(2,1)S(1)}, bf16[256,256]{1,0:T(8,128)(2,1)S(1)}, u32[]{:S(2)}, u32[]{:S(2)}) collective-permute-start(bf16[256,256]{1,0:T(8,128)(2,1)S(1)} %collective-permute-done.2.rest_6_), channel_id=1, source_target_pairs={{0,4},{1,5},{2,0},{3,1},{4,8},{5,9},{6,2},{7,3},{8,12},{9,13},{10,... | collective-permute-start | bytes 393224 | tf_op jit(solution)/shard_map/ppermute | solution.py:438
  17.6 5.3 %collective-permute-start.7 = (bf16[256,256]{1,0:T(8,128)(2,1)S(1)}, bf16[256,256]{1,0:T(8,128)(2,1)S(1)}, u32[]{:S(2)}, u32[]{:S(2)}) collective-permute-start(bf16[256,256]{1,0:T(8,128)(2,1)S(1)} %collective-permute-done.6.rest_3_), channel_id=1, source_target_pairs={{0,4},{1,5},{2,0},{3,1},{4,8},{5,9},{6,2},{7,3},{8,12},{9,13},{10,... | collective-permute-start | bytes 393224 | tf_op jit(solution)/shard_map/ppermute | solution.py:438
  17.7 5.4 %collective-permute-start.14 = (bf16[256,256]{1,0:T(8,128)(2,1)S(1)}, bf16[256,256]{1,0:T(8,128)(2,1)}, u32[]{:S(2)}, u32[]{:S(2)}) collective-permute-start(bf16[256,256]{1,0:T(8,128)(2,1)S(1)} %collective-permute-done.13.rest_9_), channel_id=1, source_target_pairs={{0,2},{1,3},{2,6},{3,7},{4,0},{5,1},{6,10},{7,11},{8,4},{9,5},{10,... | collective-permute-start | bytes 393224 | tf_op jit(solution)/shard_map/ppermute | solution.py:438
  20.2 5.3 %collective-permute-start.9 = (bf16[256,256]{1,0:T(8,128)(2,1)S(1)}, bf16[256,256]{1,0:T(8,128)(2,1)}, u32[]{:S(2)}, u32[]{:S(2)}) collective-permute-start(bf16[256,256]{1,0:T(8,128)(2,1)S(1)} %collective-permute-done.8.rest_4_), channel_id=1, source_target_pairs={{0,2},{1,3},{2,6},{3,7},{4,0},{5,1},{6,10},{7,11},{8,4},{9,5},{10,... | collective-permute-start | bytes 393224 | tf_op jit(solution)/shard_map/ppermute | solution.py:438
  21.6 4.2 %collective-permute-start.12 = (bf16[256,256]{1,0:T(8,128)(2,1)S(1)}, bf16[256,256]{1,0:T(8,128)(2,1)}, u32[]{:S(2)}, u32[]{:S(2)}) collective-permute-start(bf16[256,256]{1,0:T(8,128)(2,1)S(1)} %collective-permute-done.11.rest_8_), channel_id=1, source_target_pairs={{0,4},{1,5},{2,0},{3,1},{4,8},{5,9},{6,2},{7,3},{8,12},{9,13},{10,... | collective-permute-start | bytes 393224 | tf_op jit(solution)/shard_map/ppermute | solution.py:438
  23.0 4.7 %collective-permute-start.10 = (bf16[256,256]{1,0:T(8,128)(2,1)S(1)}, bf16[256,256]{1,0:T(8,128)(2,1)}, u32[]{:S(2)}, u32[]{:S(2)}) collective-permute-start(bf16[256,256]{1,0:T(8,128)(2,1)S(1)} %collective-permute-done.7.rest_0_), channel_id=1, source_target_pairs={{0,4},{1,5},{2,0},{3,1},{4,8},{5,9},{6,2},{7,3},{8,12},{9,13},{10,... | collective-permute-start | bytes 393224 | tf_op jit(solution)/shard_map/ppermute | solution.py:438
  23.2 4.9 %collective-permute-start.15 = (bf16[256,256]{1,0:T(8,128)(2,1)}, bf16[256,256]{1,0:T(8,128)(2,1)}, u32[]{:S(2)}, u32[]{:S(2)}) collective-permute-start(bf16[256,256]{1,0:T(8,128)(2,1)} %collective-permute-done.14.rest_4_), channel_id=1, source_target_pairs={{0,2},{1,3},{2,6},{3,7},{4,0},{5,1},{6,10},{7,11},{8,4},{9,5},{10,... | collective-permute-start | bytes 393224 | tf_op jit(solution)/shard_map/ppermute | solution.py:438
  24.4 26.0 %copy-start.6 = (s32[4,16]{1,0:T(4,128)S(1)}, s32[4,16]{1,0:T(4,128)}, u32[]{:S(2)}) copy-start(s32[4,16]{1,0:T(4,128)} %param.12) | copy-start | bytes 772
  24.4 26.0 %copy-start.5 = (s32[4]{0:T(128)S(1)}, s32[4]{0:T(128)}, u32[]{:S(2)}) copy-start(s32[4]{0:T(128)} %length_ref.3) | copy-start | bytes 52
  25.0 25.5 %copy-start.4 = (bf16[4,64,512]{2,1,0:T(8,128)(2,1)S(1)}, bf16[4,64,512]{2,1,0:T(8,128)(2,1)}, u32[]{:S(2)}) copy-start(bf16[4,64,512]{2,1,0:T(8,128)(2,1)} %own_kv_ref.3) | copy-start | bytes 786436
  29.7 7.0 %collective-permute-start.17 = (bf16[256,256]{1,0:T(8,128)(2,1)S(1)}, bf16[256,256]{1,0:T(8,128)(2,1)S(1)}, u32[]{:S(2)}, u32[]{:S(2)}) collective-permute-start(bf16[256,256]{1,0:T(8,128)(2,1)S(1)} %project.3), channel_id=1, source_target_pairs={{0,8},{1,9},{2,10},{3,11},{4,12},{5,13},{6,14},{7,15},{8,0},{9,1},... | collective-permute-start | bytes 393224 | tf_op jit(solution)/shard_map/ppermute | solution.py:438
  32.2 6.4 %collective-permute-start.16 = (bf16[256,256]{1,0:T(8,128)(2,1)S(1)}, bf16[256,256]{1,0:T(8,128)(2,1)S(1)}, u32[]{:S(2)}, u32[]{:S(2)}) collective-permute-start(bf16[256,256]{1,0:T(8,128)(2,1)S(1)} %project.3), channel_id=1, source_target_pairs={{0,4},{1,5},{2,6},{3,7},{4,8},{5,9},{6,10},{7,11},{8,12},{9,13},{1... | collective-permute-start | bytes 393224 | tf_op jit(solution)/shard_map/ppermute | solution.py:438
  33.5 13.4 %collective-permute-start.22 = (bf16[256,256]{1,0:T(8,128)(2,1)S(1)}, bf16[256,256]{1,0:T(8,128)(2,1)S(1)}, u32[]{:S(2)}, u32[]{:S(2)}) collective-permute-start(bf16[256,256]{1,0:T(8,128)(2,1)S(1)} %project.3), channel_id=1, source_target_pairs={{0,14},{1,15},{2,12},{3,13},{4,2},{5,3},{6,0},{7,1},{8,6},{9,7},{1... | collective-permute-start | bytes 393224 | tf_op jit(solution)/shard_map/ppermute | solution.py:438
  36.4 8.1 %collective-permute-start.19 = (bf16[256,256]{1,0:T(8,128)(2,1)S(1)}, bf16[256,256]{1,0:T(8,128)(2,1)S(1)}, u32[]{:S(2)}, u32[]{:S(2)}) collective-permute-start(bf16[256,256]{1,0:T(8,128)(2,1)S(1)} %project.3), channel_id=1, source_target_pairs={{0,2},{1,3},{2,0},{3,1},{4,6},{5,7},{6,4},{7,5},{8,10},{9,11},{10,... | collective-permute-start | bytes 393224 | tf_op jit(solution)/shard_map/ppermute | solution.py:438
  36.6 7.8 %collective-permute-start.18 = (bf16[256,256]{1,0:T(8,128)(2,1)S(1)}, bf16[256,256]{1,0:T(8,128)(2,1)S(1)}, u32[]{:S(2)}, u32[]{:S(2)}) collective-permute-start(bf16[256,256]{1,0:T(8,128)(2,1)S(1)} %project.3), channel_id=1, source_target_pairs={{0,12},{1,13},{2,14},{3,15},{4,0},{5,1},{6,2},{7,3},{8,4},{9,5},{1... | collective-permute-start | bytes 393224 | tf_op jit(solution)/shard_map/ppermute | solution.py:438
  36.7 10.2 %collective-permute-start.21 = (bf16[256,256]{1,0:T(8,128)(2,1)S(1)}, bf16[256,256]{1,0:T(8,128)(2,1)S(1)}, u32[]{:S(2)}, u32[]{:S(2)}) collective-permute-start(bf16[256,256]{1,0:T(8,128)(2,1)S(1)} %collective-permute-done.17), channel_id=1, source_target_pairs={{0,2},{1,3},{2,0},{3,1},{4,6},{5,7},{6,4},{7,5},{8,10},{9,11},{10,... | collective-permute-start | bytes 393224 | tf_op jit(solution)/shard_map/ppermute | solution.py:438
  38.6 8.3 %collective-permute-start.20 = (bf16[256,256]{1,0:T(8,128)(2,1)S(1)}, bf16[256,256]{1,0:T(8,128)(2,1)S(1)}, u32[]{:S(2)}, u32[]{:S(2)}) collective-permute-start(bf16[256,256]{1,0:T(8,128)(2,1)S(1)} %collective-permute-done.16), channel_id=1, source_target_pairs={{0,2},{1,3},{2,0},{3,1},{4,6},{5,7},{6,4},{7,5},{8,10},{9,11},{10,... | collective-permute-start | bytes 393224 | tf_op jit(solution)/shard_map/ppermute | solution.py:438
  46.9 49.9 %collective-permute-start.23 = (bf16[2048,256]{1,0:T(8,128)(2,1)S(1)}, bf16[2048,256]{1,0:T(8,128)(2,1)S(1)}, u32[]{:S(2)}, u32[]{:S(2)}) collective-permute-start(bf16[2048,256]{1,0:T(8,128)(2,1)S(1)} %constant_dynamic-update-slice_fusion.kv_ref), channel_id=1, source_target_pairs={{0,1},{1,0},{2,3},{3,2},{4,5},{5,4},{6,7},{7,6},{8,9},{9,8},{10,11... | collective-permute-start | bytes 3145736 | tf_op jit(solution)/shard_map/ppermute | solution.py:434

commit v17 on v16

--- a/solution.py
+++ b/solution.py
@@ -198,6 +198,18 @@
         alive = token < length
         sample = lax.div(key, HD // STEP)
 
+        own_v_at = pl.multiple_of(own_at + KVH * HD, LANES)
+        own_v = own_kv_ref[query, :, pl.ds(own_v_at, LANES)]
+        for block, at in ((memory[:, LANES:], 0), (own_v, 2 * ROWS)):
+            size = block.shape[0]
+            swapped = jnp.concatenate([block[:, HD:], block[:, :HD]], axis=1)
+            lower = lax.broadcasted_iota(jnp.int32, block.shape, 1) < HD
+            zero = jnp.zeros_like(block)
+            for g in range(2):
+                one, two = (block, swapped) if g == 0 else (swapped, block)
+                value_side[g, at:at + size, :LANES] = jnp.where(lower, one, zero)
+                value_side[g, at + size:at + 2 * size, :LANES] = jnp.where(lower, zero, two)
+
         if begun:
 
             @pl.when(query > 0)
@@ -216,8 +228,8 @@
         def key_product(i):
             g, tiles = chunks[i]
             lhs = stacked(tiles)
-            for c in range(0, KEYS, 2 * LANES):
-                part = slice(c, min(c + 2 * LANES, KEYS))
+            for c in range(0, KEYS, ROWS):
+                part = slice(c, min(c + ROWS, KEYS))
                 got = jnp.dot(lhs, key_side[g, :, part], preferred_element_type=jnp.float32) * factor
                 if c == 2 * ROWS:
                     got = got + jnp.concatenate([bias[...]] * len(tiles), axis=0)
@@ -248,19 +260,6 @@
             return seen
 
         key_product(0)
-
-        own_v_at = pl.multiple_of(own_at + KVH * HD, LANES)
-        own_v = own_kv_ref[query, :, pl.ds(own_v_at, LANES)]
-        for block, at in ((memory[:, LANES:], 0), (own_v, 2 * ROWS)):
-            size = block.shape[0]
-            swapped = jnp.concatenate([block[:, HD:], block[:, :HD]], axis=1)
-            lower = lax.broadcasted_iota(jnp.int32, block.shape, 1) < HD
-            zero = jnp.zeros_like(block)
-            for g in range(2):
-                one, two = (block, swapped) if g == 0 else (swapped, block)
-                value_side[g, at:at + size, :LANES] = jnp.where(lower, one, zero)
-                value_side[g, at + size:at + 2 * size, :LANES] = jnp.where(lower, zero, two)
-
         seen = jnp.zeros((QLEN, LANES), jnp.float32)
         for i in range(len(chunks)):
             if i + 1 < len(chunks):

time: 145 us -> 145 us (level)
  no operation moved by 1% of the time
where the time goes in v17:
time: 145 us; the launch traced here: 143 us
  Pallas kernels  97.3 us (67%)
  starting transfers between devices  26 us (18%)
  waiting for transfers between devices  18.1 us (12%)
    pallas_call x2, Pallas kernels, attend(): pl.pallas_call(functools.partial(attend_kernel, begun is not None, ahead)...  92.1 us
    ppermute x21, starting transfers between devices, along(): lax.ppermute(x, 'pass', [(2 * s + c, 2 * d + c) for s, d in pairs for c i...  21.2 us
    ppermute x21, waiting for transfers between devices, along(): lax.ppermute(x, 'pass', [(2 * s + c, 2 * d + c) for s, d in pairs for c i...  18.1 us
    ppermute x3, starting transfers between devices, to_partner(): return lax.ppermute(x, 'pass', [(i, i ^ 1) for i in range(extent)])  4.77 us
    pallas_call x1, Pallas kernels, pool(): pl.pallas_call(pool_kernel, in_specs=[vmem] * 3, out_specs=vmem, out_shap...  3.08 us
  transfers between devices with their start and end apart: 24, of which 13 were waited for; matrix products, arithmetic and copies ran while one was open for 0% of the time, Pallas kernels for 35%

profile of v17, /device:TPU:1, one launch (start us, length us, event | category | flops | bytes accessed | tf_op | source)
XLA Modules:
  0.0 142.8 jit_solution(8090683889317379863)
XLA Ops:
  0.0 0.0 copy-start.3
  0.0 0.9 copy-done.3
  1.0 0.0 copy-start
  1.0 0.0 copy-start.1
  1.0 0.1 collective-permute-start.1
  1.1 2.7 %collective-permute-start.3 = (bf16[256,256]{1,0:T(8,128)(2,1)S(1)}, bf16[256,256]{1,0:T(8,128)(2,1)S(1)}, u32[]{:S(2)}, u32[]{:S(2)}) collective-permute-start(bf16[256,256]{1,0:T(8,128)(2,1)S(1)} %get-tuple-element.14.rest_0_), channel_id=1, source_target_pairs={{0,2},{1,3},{2,6},{3,7},{4,0},{5,1},{6,10},{7,11},{8,4},{9,5},{10,... | collective-permute-start | bytes 393224 | tf_op jit(solution)/shard_map/ppermute | solution.py:437
  3.8 0.1 collective-permute-start
  3.9 0.0 collective-permute-done.1.rest_5_
  3.9 1.4 collective-permute-start.4
  5.3 0.1 collective-permute-start.2
  5.3 0.0 copy-done
  5.4 0.0 copy-done.1
  5.4 0.0 copy-done.2
  5.4 3.1 %pool.1.own_ref = bf16[128,4096]{1,0:T(8,128)(2,1)S(1)} custom-call(bf16[4,128,4096]{2,1,0:T(8,128)(2,1)S(1)} %copy-done, bf16[32,4096]{1,0:T(8,128)(2,1)S(1)} %copy-done.1, bf16[4096]{0:T(1024)(128)(2,1)S(1)} %copy-done.2), custom_call_target="tpu_custom_call" | custom-call | flops 268435456 | bytes 4194304 | tf_op jit(solution)/shard_map/pool/pallas_call | solution.py:116
  8.4 0.0 collective-permute-done.3.rest_2_
  8.5 0.1 collective-permute-done.rest_1_
  8.5 2.0 %collective-permute-done.4.rest_7_ = bf16[256,256]{1,0:T(8,128)(2,1)S(1)} collective-permute-done((bf16[256,256]{1,0:T(8,128)(2,1)S(1)}, bf16[256,256]{1,0:T(8,128)(2,1)S(1)}, u32[]{:S(2)}, u32[]{:S(2)}) %collective-permute-start.4) | collective-permute-done | bytes 131104 | tf_op jit(solution)/shard_map/ppermute | solution.py:437
  10.5 0.9 collective-permute-done.2.rest_6_
  11.3 1.2 collective-permute-start.5
  12.5 0.1 collective-permute-start.6
  12.6 1.4 collective-permute-start.13
  14.0 1.3 collective-permute-start.8
  15.3 0.2 collective-permute-start.11
  15.4 2.2 %collective-permute-done.6.rest_3_ = bf16[256,256]{1,0:T(8,128)(2,1)S(1)} collective-permute-done((bf16[256,256]{1,0:T(8,128)(2,1)S(1)}, bf16[256,256]{1,0:T(8,128)(2,1)S(1)}, u32[]{:S(2)}, u32[]{:S(2)}) %collective-permute-start.6) | collective-permute-done | bytes 131104 | tf_op jit(solution)/shard_map/ppermute | solution.py:437
  17.6 0.1 collective-permute-start.7
  17.7 0.0 collective-permute-done.13.rest_9_
  17.7 1.4 collective-permute-start.14
  19.1 1.1 collective-permute-done.8.rest_4_
  20.2 1.4 collective-permute-start.9
  21.6 0.0 collective-permute-done.11.rest_8_
  21.6 0.1 collective-permute-start.12
  21.7 1.3 collective-permute-done.7.rest_0_
  23.0 0.2 collective-permute-start.10
  23.2 0.0 collective-permute-done.14.rest_4_
  23.2 1.3 collective-permute-start.15
  24.4 0.0 collective-permute-done.5.other_ref
  24.4 0.5 project.2.rest_6_
  25.0 0.0 copy-start.4
  25.0 0.5 collective-permute-done.9.rest_1_
  25.5 0.3 collective-permute-done.12.rest_3_
  25.8 1.9 %collective-permute-done.10.rest_2_ = bf16[256,256]{1,0:T(8,128)(2,1)} collective-permute-done((bf16[256,256]{1,0:T(8,128)(2,1)S(1)}, bf16[256,256]{1,0:T(8,128)(2,1)}, u32[]{:S(2)}, u32[]{:S(2)}) %collective-permute-start.10) | collective-permute-done | bytes 131104 | tf_op jit(solution)/shard_map/ppermute | solution.py:437
  27.7 0.4 collective-permute-done.15.rest_5_
  28.1 1.5 %project.3 = bf16[256,256]{1,0:T(8,128)(2,1)S(1)} custom-call(s32[1]{0:T(128)} %bitcast.1.core_ref.half_ref, s32[1]{0:T(128)} %bitcast.2.place_ref, bf16[128,4096]{1,0:T(8,128)(2,1)S(1)} %pool.1.own_ref, bf16[128,4096]{1,0:T(8,128)(2,1)S(1)} %collective-permute-done.5.other_ref, bf16[256,256]{1,0:T(8,128)(2,1)S(1)} %collective-permute-done.7.rest_0_, ...), custom_call_target="tpu_custom_call" | custom-call | flops 134217728 | bytes 33554432 | tf_op jit(solution)/shard_map/project/pallas_call | solution.py:390
  29.7 2.5 %collective-permute-start.17 = (bf16[256,256]{1,0:T(8,128)(2,1)S(1)}, bf16[256,256]{1,0:T(8,128)(2,1)S(1)}, u32[]{:S(2)}, u32[]{:S(2)}) collective-permute-start(bf16[256,256]{1,0:T(8,128)(2,1)S(1)} %project.3), channel_id=1, source_target_pairs={{0,8},{1,9},{2,10},{3,11},{4,12},{5,13},{6,14},{7,15},{8,0},{9,1},... | collective-permute-start | bytes 393224 | tf_op jit(solution)/shard_map/ppermute | solution.py:437
  32.2 1.3 collective-permute-start.16
  33.5 2.9 %collective-permute-start.22 = (bf16[256,256]{1,0:T(8,128)(2,1)S(1)}, bf16[256,256]{1,0:T(8,128)(2,1)S(1)}, u32[]{:S(2)}, u32[]{:S(2)}) collective-permute-start(bf16[256,256]{1,0:T(8,128)(2,1)S(1)} %project.3), channel_id=1, source_target_pairs={{0,14},{1,15},{2,12},{3,13},{4,2},{5,3},{6,0},{7,1},{8,6},{9,7},{1... | collective-permute-start | bytes 393224 | tf_op jit(solution)/shard_map/ppermute | solution.py:437
  36.4 0.3 collective-permute-start.19
  36.6 0.0 collective-permute-start.18
  36.7 0.0 collective-permute-done.17
  36.7 1.2 collective-permute-start.21
  37.9 0.6 collective-permute-done.16
  38.6 1.4 collective-permute-start.20
  40.0 4.5 %collective-permute-done.18 = bf16[256,256]{1,0:T(8,128)(2,1)S(1)} collective-permute-done((bf16[256,256]{1,0:T(8,128)(2,1)S(1)}, bf16[256,256]{1,0:T(8,128)(2,1)S(1)}, u32[]{:S(2)}, u32[]{:S(2)}) %collective-permute-start.18) | collective-permute-done | bytes 131104 | tf_op jit(solution)/shard_map/ppermute | solution.py:437
  44.5 0.0 collective-permute-done.19
  44.5 2.4 %collective-permute-done.20 = bf16[256,256]{1,0:T(8,128)(2,1)S(1)} collective-permute-done((bf16[256,256]{1,0:T(8,128)(2,1)S(1)}, bf16[256,256]{1,0:T(8,128)(2,1)S(1)}, u32[]{:S(2)}, u32[]{:S(2)}) %collective-permute-start.20) | collective-permute-done | bytes 131104 | tf_op jit(solution)/shard_map/ppermute | solution.py:437
  46.9 0.0 collective-permute-done.21
  46.9 0.0 collective-permute-done.22
  46.9 3.5 %collective-permute-start.23 = (bf16[2048,256]{1,0:T(8,128)(2,1)S(1)}, bf16[2048,256]{1,0:T(8,128)(2,1)S(1)}, u32[]{:S(2)}, u32[]{:S(2)}) collective-permute-start(bf16[2048,256]{1,0:T(8,128)(2,1)S(1)} %constant_dynamic-update-slice_fusion.kv_ref), channel_id=1, source_target_pairs={{0,1},{1,0},{2,3},{3,2},{4,5},{5,4},{6,7},{7,6},{8,9},{9,8},{10,11... | collective-permute-start | bytes 3145736 | tf_op jit(solution)/shard_map/ppermute | solution.py:433
  50.4 0.0 copy-done.6
  50.4 0.0 copy-done.5
  50.5 0.0 copy-done.4
  50.5 46.4 %attend.2 = (bf16[4,64,7424]{2,1,0:T(8,128)(2,1)}, bf16[64,3712]{1,0:T(8,128)(2,1)S(1)}) custom-call(s32[1]{0:T(128)} %bitcast.1.core_ref.half_ref, s32[4,16]{1,0:T(4,128)S(1)} %fusion.6.start_ref, s32[4]{0:T(128)S(1)} %copy-done.5, bf16[4,64,7424]{2,1,0:T(8,128)(2,1)} %q_hbm.3, bf16[2048,256]{1,0:T(8,128)(2,1)S(1)} %constant_dynamic-update-slice_fusion.kv_ref, ...), custom_call_target="tpu_custom_call" | custom-call | flops 2189426688 | bytes 3801088 | tf_op jit(solution)/shard_map/attend/pallas_call | solution.py:330
  96.9 0.0 collective-permute-done.23.kv_ref
  96.9 45.7 %attend.3 = bf16[4,64,7424]{2,1,0:T(8,128)(2,1)} custom-call(s32[1]{0:T(128)} %bitcast.half_ref, s32[4,16]{1,0:T(4,128)S(1)} %fusion.6.start_ref, s32[4]{0:T(128)S(1)} %copy-done.5, bf16[4,64,7424]{2,1,0:T(8,128)(2,1)} %q_hbm.3, bf16[2048,256]{1,0:T(8,128)(2,1)S(1)} %collective-permute-done.23.kv_ref, ...), custom_call_target="tpu_custom_call", output_to_operand_aliasing={{}: (7, {})} | custom-call | flops 2189426688 | bytes 3801088 | tf_op jit(solution)/shard_map/attend/pallas_call | solution.py:330
  (13 shorter events, 0.2 us)
Async XLA Ops:
  0.0 0.9 copy-start.3
  1.0 4.4 %copy-start = (bf16[4,128,4096]{2,1,0:T(8,128)(2,1)S(1)}, bf16[4,128,4096]{2,1,0:T(8,128)(2,1)}, u32[]{:S(2)}) copy-start(bf16[4,128,4096]{2,1,0:T(8,128)(2,1)} %states.1) | copy-start | bytes 12582916
  1.0 4.4 %copy-start.1 = (bf16[32,4096]{1,0:T(8,128)(2,1)S(1)}, bf16[32,4096]{1,0:T(8,128)(2,1)}, u32[]{:S(2)}) copy-start(bf16[32,4096]{1,0:T(8,128)(2,1)} %queries.1) | copy-start | bytes 786436
  1.0 4.4 %copy-start.2 = (bf16[4096]{0:T(1024)(128)(2,1)S(1)}, bf16[4096]{0:T(1024)(128)(2,1)}, u32[]{:S(2)}) copy-start(bf16[4096]{0:T(1024)(128)(2,1)} %gain.1) | copy-start | bytes 24580
  1.0 2.9 %collective-permute-start.1 = (bf16[256,256]{1,0:T(8,128)(2,1)S(1)}, bf16[256,256]{1,0:T(8,128)(2,1)S(1)}, u32[]{:S(2)}, u32[]{:S(2)}) collective-permute-start(bf16[256,256]{1,0:T(8,128)(2,1)S(1)} %get-tuple-element.15), channel_id=1, source_target_pairs={{0,1},{1,0},{2,3},{3,2},{4,5},{5,4},{6,7},{7,6},{8,9},{9,8},{10,11... | collective-permute-start | bytes 393224 | tf_op jit(solution)/shard_map/ppermute | solution.py:433
  1.1 7.3 %collective-permute-start.3 = (bf16[256,256]{1,0:T(8,128)(2,1)S(1)}, bf16[256,256]{1,0:T(8,128)(2,1)S(1)}, u32[]{:S(2)}, u32[]{:S(2)}) collective-permute-start(bf16[256,256]{1,0:T(8,128)(2,1)S(1)} %get-tuple-element.14.rest_0_), channel_id=1, source_target_pairs={{0,2},{1,3},{2,6},{3,7},{4,0},{5,1},{6,10},{7,11},{8,4},{9,5},{10,... | collective-permute-start | bytes 393224 | tf_op jit(solution)/shard_map/ppermute | solution.py:437
  3.8 4.7 %collective-permute-start = (bf16[256,256]{1,0:T(8,128)(2,1)S(1)}, bf16[256,256]{1,0:T(8,128)(2,1)S(1)}, u32[]{:S(2)}, u32[]{:S(2)}) collective-permute-start(bf16[256,256]{1,0:T(8,128)(2,1)S(1)} %get-tuple-element.14.rest_0_), channel_id=1, source_target_pairs={{0,4},{1,5},{2,0},{3,1},{4,8},{5,9},{6,2},{7,3},{8,12},{9,13},{10,... | collective-permute-start | bytes 393224 | tf_op jit(solution)/shard_map/ppermute | solution.py:437
  3.9 6.6 %collective-permute-start.4 = (bf16[256,256]{1,0:T(8,128)(2,1)S(1)}, bf16[256,256]{1,0:T(8,128)(2,1)S(1)}, u32[]{:S(2)}, u32[]{:S(2)}) collective-permute-start(bf16[256,256]{1,0:T(8,128)(2,1)S(1)} %collective-permute-done.1.rest_5_), channel_id=1, source_target_pairs={{0,2},{1,3},{2,6},{3,7},{4,0},{5,1},{6,10},{7,11},{8,4},{9,5},{10,... | collective-permute-start | bytes 393224 | tf_op jit(solution)/shard_map/ppermute | solution.py:437
  5.3 6.1 %collective-permute-start.2 = (bf16[256,256]{1,0:T(8,128)(2,1)S(1)}, bf16[256,256]{1,0:T(8,128)(2,1)S(1)}, u32[]{:S(2)}, u32[]{:S(2)}) collective-permute-start(bf16[256,256]{1,0:T(8,128)(2,1)S(1)} %collective-permute-done.1.rest_5_), channel_id=1, source_target_pairs={{0,4},{1,5},{2,0},{3,1},{4,8},{5,9},{6,2},{7,3},{8,12},{9,13},{10,... | collective-permute-start | bytes 393224 | tf_op jit(solution)/shard_map/ppermute | solution.py:437
  11.3 13.1 %collective-permute-start.5 = (bf16[128,4096]{1,0:T(8,128)(2,1)S(1)}, bf16[128,4096]{1,0:T(8,128)(2,1)S(1)}, u32[]{:S(2)}, u32[]{:S(2)}) collective-permute-start(bf16[128,4096]{1,0:T(8,128)(2,1)S(1)} %pool.1.own_ref), channel_id=1, source_target_pairs={{0,1},{1,0},{2,3},{3,2},{4,5},{5,4},{6,7},{7,6},{8,9},{9,8},{10,11... | collective-permute-start | bytes 3145736 | tf_op jit(solution)/shard_map/ppermute | solution.py:433
  12.5 5.1 %collective-permute-start.6 = (bf16[256,256]{1,0:T(8,128)(2,1)S(1)}, bf16[256,256]{1,0:T(8,128)(2,1)S(1)}, u32[]{:S(2)}, u32[]{:S(2)}) collective-permute-start(bf16[256,256]{1,0:T(8,128)(2,1)S(1)} %collective-permute-done.rest_1_), channel_id=1, source_target_pairs={{0,4},{1,5},{2,0},{3,1},{4,8},{5,9},{6,2},{7,3},{8,12},{9,13},{10,... | collective-permute-start | bytes 393224 | tf_op jit(solution)/shard_map/ppermute | solution.py:437
  12.6 5.1 %collective-permute-start.13 = (bf16[256,256]{1,0:T(8,128)(2,1)S(1)}, bf16[256,256]{1,0:T(8,128)(2,1)S(1)}, u32[]{:S(2)}, u32[]{:S(2)}) collective-permute-start(bf16[256,256]{1,0:T(8,128)(2,1)S(1)} %collective-permute-done.4.rest_7_), channel_id=1, source_target_pairs={{0,2},{1,3},{2,6},{3,7},{4,0},{5,1},{6,10},{7,11},{8,4},{9,5},{10,... | collective-permute-start | bytes 393224 | tf_op jit(solution)/shard_map/ppermute | solution.py:437
  14.0 6.2 %collective-permute-start.8 = (bf16[256,256]{1,0:T(8,128)(2,1)S(1)}, bf16[256,256]{1,0:T(8,128)(2,1)S(1)}, u32[]{:S(2)}, u32[]{:S(2)}) collective-permute-start(bf16[256,256]{1,0:T(8,128)(2,1)S(1)} %collective-permute-done.3.rest_2_), channel_id=1, source_target_pairs={{0,2},{1,3},{2,6},{3,7},{4,0},{5,1},{6,10},{7,11},{8,4},{9,5},{10,... | collective-permute-start | bytes 393224 | tf_op jit(solution)/shard_map/ppermute | solution.py:437
  15.3 6.3 %collective-permute-start.11 = (bf16[256,256]{1,0:T(8,128)(2,1)S(1)}, bf16[256,256]{1,0:T(8,128)(2,1)S(1)}, u32[]{:S(2)}, u32[]{:S(2)}) collective-permute-start(bf16[256,256]{1,0:T(8,128)(2,1)S(1)} %collective-permute-done.2.rest_6_), channel_id=1, source_target_pairs={{0,4},{1,5},{2,0},{3,1},{4,8},{5,9},{6,2},{7,3},{8,12},{9,13},{10,... | collective-permute-start | bytes 393224 | tf_op jit(solution)/shard_map/ppermute | solution.py:437
  17.6 5.3 %collective-permute-start.7 = (bf16[256,256]{1,0:T(8,128)(2,1)S(1)}, bf16[256,256]{1,0:T(8,128)(2,1)S(1)}, u32[]{:S(2)}, u32[]{:S(2)}) collective-permute-start(bf16[256,256]{1,0:T(8,128)(2,1)S(1)} %collective-permute-done.6.rest_3_), channel_id=1, source_target_pairs={{0,4},{1,5},{2,0},{3,1},{4,8},{5,9},{6,2},{7,3},{8,12},{9,13},{10,... | collective-permute-start | bytes 393224 | tf_op jit(solution)/shard_map/ppermute | solution.py:437
  17.7 5.4 %collective-permute-start.14 = (bf16[256,256]{1,0:T(8,128)(2,1)S(1)}, bf16[256,256]{1,0:T(8,128)(2,1)}, u32[]{:S(2)}, u32[]{:S(2)}) collective-permute-start(bf16[256,256]{1,0:T(8,128)(2,1)S(1)} %collective-permute-done.13.rest_9_), channel_id=1, source_target_pairs={{0,2},{1,3},{2,6},{3,7},{4,0},{5,1},{6,10},{7,11},{8,4},{9,5},{10,... | collective-permute-start | bytes 393224 | tf_op jit(solution)/shard_map/ppermute | solution.py:437
  20.2 5.3 %collective-permute-start.9 = (bf16[256,256]{1,0:T(8,128)(2,1)S(1)}, bf16[256,256]{1,0:T(8,128)(2,1)}, u32[]{:S(2)}, u32[]{:S(2)}) collective-permute-start(bf16[256,256]{1,0:T(8,128)(2,1)S(1)} %collective-permute-done.8.rest_4_), channel_id=1, source_target_pairs={{0,2},{1,3},{2,6},{3,7},{4,0},{5,1},{6,10},{7,11},{8,4},{9,5},{10,... | collective-permute-start | bytes 393224 | tf_op jit(solution)/shard_map/ppermute | solution.py:437
  21.6 4.2 %collective-permute-start.12 = (bf16[256,256]{1,0:T(8,128)(2,1)S(1)}, bf16[256,256]{1,0:T(8,128)(2,1)}, u32[]{:S(2)}, u32[]{:S(2)}) collective-permute-start(bf16[256,256]{1,0:T(8,128)(2,1)S(1)} %collective-permute-done.11.rest_8_), channel_id=1, source_target_pairs={{0,4},{1,5},{2,0},{3,1},{4,8},{5,9},{6,2},{7,3},{8,12},{9,13},{10,... | collective-permute-start | bytes 393224 | tf_op jit(solution)/shard_map/ppermute | solution.py:437
  23.0 4.7 %collective-permute-start.10 = (bf16[256,256]{1,0:T(8,128)(2,1)S(1)}, bf16[256,256]{1,0:T(8,128)(2,1)}, u32[]{:S(2)}, u32[]{:S(2)}) collective-permute-start(bf16[256,256]{1,0:T(8,128)(2,1)S(1)} %collective-permute-done.7.rest_0_), channel_id=1, source_target_pairs={{0,4},{1,5},{2,0},{3,1},{4,8},{5,9},{6,2},{7,3},{8,12},{9,13},{10,... | collective-permute-start | bytes 393224 | tf_op jit(solution)/shard_map/ppermute | solution.py:437
  23.2 4.9 %collective-permute-start.15 = (bf16[256,256]{1,0:T(8,128)(2,1)}, bf16[256,256]{1,0:T(8,128)(2,1)}, u32[]{:S(2)}, u32[]{:S(2)}) collective-permute-start(bf16[256,256]{1,0:T(8,128)(2,1)} %collective-permute-done.14.rest_4_), channel_id=1, source_target_pairs={{0,2},{1,3},{2,6},{3,7},{4,0},{5,1},{6,10},{7,11},{8,4},{9,5},{10,... | collective-permute-start | bytes 393224 | tf_op jit(solution)/shard_map/ppermute | solution.py:437
  24.4 26.0 %copy-start.6 = (s32[4,16]{1,0:T(4,128)S(1)}, s32[4,16]{1,0:T(4,128)}, u32[]{:S(2)}) copy-start(s32[4,16]{1,0:T(4,128)} %param.12) | copy-start | bytes 772
  24.4 26.0 %copy-start.5 = (s32[4]{0:T(128)S(1)}, s32[4]{0:T(128)}, u32[]{:S(2)}) copy-start(s32[4]{0:T(128)} %length_ref.3) | copy-start | bytes 52
  25.0 25.5 %copy-start.4 = (bf16[4,64,512]{2,1,0:T(8,128)(2,1)S(1)}, bf16[4,64,512]{2,1,0:T(8,128)(2,1)}, u32[]{:S(2)}) copy-start(bf16[4,64,512]{2,1,0:T(8,128)(2,1)} %own_kv_ref.3) | copy-start | bytes 786436
  29.7 7.0 %collective-permute-start.17 = (bf16[256,256]{1,0:T(8,128)(2,1)S(1)}, bf16[256,256]{1,0:T(8,128)(2,1)S(1)}, u32[]{:S(2)}, u32[]{:S(2)}) collective-permute-start(bf16[256,256]{1,0:T(8,128)(2,1)S(1)} %project.3), channel_id=1, source_target_pairs={{0,8},{1,9},{2,10},{3,11},{4,12},{5,13},{6,14},{7,15},{8,0},{9,1},... | collective-permute-start | bytes 393224 | tf_op jit(solution)/shard_map/ppermute | solution.py:437
  32.2 6.4 %collective-permute-start.16 = (bf16[256,256]{1,0:T(8,128)(2,1)S(1)}, bf16[256,256]{1,0:T(8,128)(2,1)S(1)}, u32[]{:S(2)}, u32[]{:S(2)}) collective-permute-start(bf16[256,256]{1,0:T(8,128)(2,1)S(1)} %project.3), channel_id=1, source_target_pairs={{0,4},{1,5},{2,6},{3,7},{4,8},{5,9},{6,10},{7,11},{8,12},{9,13},{1... | collective-permute-start | bytes 393224 | tf_op jit(solution)/shard_map/ppermute | solution.py:437
  33.5 13.4 %collective-permute-start.22 = (bf16[256,256]{1,0:T(8,128)(2,1)S(1)}, bf16[256,256]{1,0:T(8,128)(2,1)S(1)}, u32[]{:S(2)}, u32[]{:S(2)}) collective-permute-start(bf16[256,256]{1,0:T(8,128)(2,1)S(1)} %project.3), channel_id=1, source_target_pairs={{0,14},{1,15},{2,12},{3,13},{4,2},{5,3},{6,0},{7,1},{8,6},{9,7},{1... | collective-permute-start | bytes 393224 | tf_op jit(solution)/shard_map/ppermute | solution.py:437
  36.4 8.1 %collective-permute-start.19 = (bf16[256,256]{1,0:T(8,128)(2,1)S(1)}, bf16[256,256]{1,0:T(8,128)(2,1)S(1)}, u32[]{:S(2)}, u32[]{:S(2)}) collective-permute-start(bf16[256,256]{1,0:T(8,128)(2,1)S(1)} %project.3), channel_id=1, source_target_pairs={{0,2},{1,3},{2,0},{3,1},{4,6},{5,7},{6,4},{7,5},{8,10},{9,11},{10,... | collective-permute-start | bytes 393224 | tf_op jit(solution)/shard_map/ppermute | solution.py:437
  36.6 7.8 %collective-permute-start.18 = (bf16[256,256]{1,0:T(8,128)(2,1)S(1)}, bf16[256,256]{1,0:T(8,128)(2,1)S(1)}, u32[]{:S(2)}, u32[]{:S(2)}) collective-permute-start(bf16[256,256]{1,0:T(8,128)(2,1)S(1)} %project.3), channel_id=1, source_target_pairs={{0,12},{1,13},{2,14},{3,15},{4,0},{5,1},{6,2},{7,3},{8,4},{9,5},{1... | collective-permute-start | bytes 393224 | tf_op jit(solution)/shard_map/ppermute | solution.py:437
  36.7 10.2 %collective-permute-start.21 = (bf16[256,256]{1,0:T(8,128)(2,1)S(1)}, bf16[256,256]{1,0:T(8,128)(2,1)S(1)}, u32[]{:S(2)}, u32[]{:S(2)}) collective-permute-start(bf16[256,256]{1,0:T(8,128)(2,1)S(1)} %collective-permute-done.17), channel_id=1, source_target_pairs={{0,2},{1,3},{2,0},{3,1},{4,6},{5,7},{6,4},{7,5},{8,10},{9,11},{10,... | collective-permute-start | bytes 393224 | tf_op jit(solution)/shard_map/ppermute | solution.py:437
  38.6 8.3 %collective-permute-start.20 = (bf16[256,256]{1,0:T(8,128)(2,1)S(1)}, bf16[256,256]{1,0:T(8,128)(2,1)S(1)}, u32[]{:S(2)}, u32[]{:S(2)}) collective-permute-start(bf16[256,256]{1,0:T(8,128)(2,1)S(1)} %collective-permute-done.16), channel_id=1, source_target_pairs={{0,2},{1,3},{2,0},{3,1},{4,6},{5,7},{6,4},{7,5},{8,10},{9,11},{10,... | collective-permute-start | bytes 393224 | tf_op jit(solution)/shard_map/ppermute | solution.py:437
  46.9 49.9 %collective-permute-start.23 = (bf16[2048,256]{1,0:T(8,128)(2,1)S(1)}, bf16[2048,256]{1,0:T(8,128)(2,1)S(1)}, u32[]{:S(2)}, u32[]{:S(2)}) collective-permute-start(bf16[2048,256]{1,0:T(8,128)(2,1)S(1)} %constant_dynamic-update-slice_fusion.kv_ref), channel_id=1, source_target_pairs={{0,1},{1,0},{2,3},{3,2},{4,5},{5,4},{6,7},{7,6},{8,9},{9,8},{10,11... | collective-permute-start | bytes 3145736 | tf_op jit(solution)/shard_map/ppermute | solution.py:433

commit v18 on v17

--- a/solution.py
+++ b/solution.py
@@ -119,7 +119,7 @@
         out_specs=vmem,
         out_shape=jax.ShapeDtypeStruct((count * MEM, D), jnp.bfloat16),
         scratch_shapes=[pltpu.VMEM((count * MEM, D), jnp.float32)],
-        compiler_params=pltpu.CompilerParams(vmem_limit_bytes=20 * MIB),
+        compiler_params=pltpu.CompilerParams(vmem_limit_bytes=12 * MIB),
         cost_estimate=pl.CostEstimate(
             flops=4 * count * MEM * LEN * D, bytes_accessed=2 * count * LEN * D,
             transcendentals=count * CH * MEM * LEN,
@@ -392,7 +392,7 @@
         in_specs=[smem, smem] + [vmem] * len(operands),
         out_specs=vmem,
         out_shape=jax.ShapeDtypeStruct((2 * count, width), jnp.float32 if more else jnp.bfloat16),
-        compiler_params=pltpu.CompilerParams(vmem_limit_bytes=16 * MIB),
+        compiler_params=pltpu.CompilerParams(vmem_limit_bytes=6 * MIB),
         cost_estimate=pl.CostEstimate(
             flops=count * D * width, bytes_accessed=32 * D * width, transcendentals=0
         ),

time: 145 us -> 145 us (level)
  no operation moved by 1% of the time
where the time goes in v18:
time: 145 us; the launch traced here: 143 us
  Pallas kernels  97.3 us (67%)
  starting transfers between devices  26 us (18%)
  waiting for transfers between devices  18.1 us (12%)
    pallas_call x2, Pallas kernels, attend(): pl.pallas_call(functools.partial(attend_kernel, begun is not None, ahead)...  92.1 us
    ppermute x21, starting transfers between devices, along(): lax.ppermute(x, 'pass', [(2 * s + c, 2 * d + c) for s, d in pairs for c i...  21.2 us
    ppermute x21, waiting for transfers between devices, along(): lax.ppermute(x, 'pass', [(2 * s + c, 2 * d + c) for s, d in pairs for c i...  18.1 us
    ppermute x3, starting transfers between devices, to_partner(): return lax.ppermute(x, 'pass', [(i, i ^ 1) for i in range(extent)])  4.77 us
    pallas_call x1, Pallas kernels, pool(): pl.pallas_call(pool_kernel, in_specs=[vmem] * 3, out_specs=vmem, out_shap...  3.08 us
  transfers between devices with their start and end apart: 24, of which 13 were waited for; matrix products, arithmetic and copies ran while one was open for 0% of the time, Pallas kernels for 35%

profile of v18, /device:TPU:1, one launch (start us, length us, event | category | flops | bytes accessed | tf_op | source)
XLA Modules:
  0.0 142.8 jit_solution(1979040415022400384)
XLA Ops:
  0.0 0.0 copy-start.3
  0.0 0.9 copy-done.3
  1.0 0.0 copy-start
  1.0 0.0 copy-start.1
  1.0 0.1 collective-permute-start.1
  1.1 2.7 %collective-permute-start.3 = (bf16[256,256]{1,0:T(8,128)(2,1)S(1)}, bf16[256,256]{1,0:T(8,128)(2,1)S(1)}, u32[]{:S(2)}, u32[]{:S(2)}) collective-permute-start(bf16[256,256]{1,0:T(8,128)(2,1)S(1)} %get-tuple-element.14.rest_0_), channel_id=1, source_target_pairs={{0,2},{1,3},{2,6},{3,7},{4,0},{5,1},{6,10},{7,11},{8,4},{9,5},{10,... | collective-permute-start | bytes 393224 | tf_op jit(solution)/shard_map/ppermute | solution.py:437
  3.8 0.1 collective-permute-start
  3.9 0.0 collective-permute-done.1.rest_5_
  3.9 1.4 collective-permute-start.4
  5.3 0.1 collective-permute-start.2
  5.3 0.0 copy-done
  5.4 0.0 copy-done.1
  5.4 0.0 copy-done.2
  5.4 3.1 %pool.1.own_ref = bf16[128,4096]{1,0:T(8,128)(2,1)S(1)} custom-call(bf16[4,128,4096]{2,1,0:T(8,128)(2,1)S(1)} %copy-done, bf16[32,4096]{1,0:T(8,128)(2,1)S(1)} %copy-done.1, bf16[4096]{0:T(1024)(128)(2,1)S(1)} %copy-done.2), custom_call_target="tpu_custom_call" | custom-call | flops 268435456 | bytes 4194304 | tf_op jit(solution)/shard_map/pool/pallas_call | solution.py:116
  8.4 0.0 collective-permute-done.3.rest_2_
  8.5 0.1 collective-permute-done.rest_1_
  8.5 2.0 %collective-permute-done.4.rest_7_ = bf16[256,256]{1,0:T(8,128)(2,1)S(1)} collective-permute-done((bf16[256,256]{1,0:T(8,128)(2,1)S(1)}, bf16[256,256]{1,0:T(8,128)(2,1)S(1)}, u32[]{:S(2)}, u32[]{:S(2)}) %collective-permute-start.4) | collective-permute-done | bytes 131104 | tf_op jit(solution)/shard_map/ppermute | solution.py:437
  10.5 0.9 collective-permute-done.2.rest_6_
  11.3 1.2 collective-permute-start.5
  12.5 0.1 collective-permute-start.6
  12.6 1.4 collective-permute-start.13
  14.0 1.3 collective-permute-start.8
  15.3 0.2 collective-permute-start.11
  15.4 2.2 %collective-permute-done.6.rest_3_ = bf16[256,256]{1,0:T(8,128)(2,1)S(1)} collective-permute-done((bf16[256,256]{1,0:T(8,128)(2,1)S(1)}, bf16[256,256]{1,0:T(8,128)(2,1)S(1)}, u32[]{:S(2)}, u32[]{:S(2)}) %collective-permute-start.6) | collective-permute-done | bytes 131104 | tf_op jit(solution)/shard_map/ppermute | solution.py:437
  17.6 0.1 collective-permute-start.7
  17.7 0.0 collective-permute-done.13.rest_9_
  17.7 1.4 collective-permute-start.14
  19.1 1.1 collective-permute-done.8.rest_4_
  20.2 1.4 collective-permute-start.9
  21.6 0.0 collective-permute-done.11.rest_8_
  21.6 0.1 collective-permute-start.12
  21.7 1.3 collective-permute-done.7.rest_0_
  23.0 0.2 collective-permute-start.10
  23.2 0.0 collective-permute-done.14.rest_4_
  23.2 1.3 collective-permute-start.15
  24.4 0.0 collective-permute-done.5.other_ref
  24.4 0.5 project.2.rest_6_
  25.0 0.0 copy-start.4
  25.0 0.5 collective-permute-done.9.rest_1_
  25.5 0.3 collective-permute-done.12.rest_3_
  25.8 1.9 %collective-permute-done.10.rest_2_ = bf16[256,256]{1,0:T(8,128)(2,1)} collective-permute-done((bf16[256,256]{1,0:T(8,128)(2,1)S(1)}, bf16[256,256]{1,0:T(8,128)(2,1)}, u32[]{:S(2)}, u32[]{:S(2)}) %collective-permute-start.10) | collective-permute-done | bytes 131104 | tf_op jit(solution)/shard_map/ppermute | solution.py:437
  27.7 0.4 collective-permute-done.15.rest_5_
  28.1 1.5 %project.3 = bf16[256,256]{1,0:T(8,128)(2,1)S(1)} custom-call(s32[1]{0:T(128)} %bitcast.1.core_ref.half_ref, s32[1]{0:T(128)} %bitcast.2.place_ref, bf16[128,4096]{1,0:T(8,128)(2,1)S(1)} %pool.1.own_ref, bf16[128,4096]{1,0:T(8,128)(2,1)S(1)} %collective-permute-done.5.other_ref, bf16[256,256]{1,0:T(8,128)(2,1)S(1)} %collective-permute-done.7.rest_0_, ...), custom_call_target="tpu_custom_call" | custom-call | flops 134217728 | bytes 33554432 | tf_op jit(solution)/shard_map/project/pallas_call | solution.py:390
  29.7 2.5 %collective-permute-start.17 = (bf16[256,256]{1,0:T(8,128)(2,1)S(1)}, bf16[256,256]{1,0:T(8,128)(2,1)S(1)}, u32[]{:S(2)}, u32[]{:S(2)}) collective-permute-start(bf16[256,256]{1,0:T(8,128)(2,1)S(1)} %project.3), channel_id=1, source_target_pairs={{0,8},{1,9},{2,10},{3,11},{4,12},{5,13},{6,14},{7,15},{8,0},{9,1},... | collective-permute-start | bytes 393224 | tf_op jit(solution)/shard_map/ppermute | solution.py:437
  32.2 1.3 collective-permute-start.16
  33.5 2.9 %collective-permute-start.22 = (bf16[256,256]{1,0:T(8,128)(2,1)S(1)}, bf16[256,256]{1,0:T(8,128)(2,1)S(1)}, u32[]{:S(2)}, u32[]{:S(2)}) collective-permute-start(bf16[256,256]{1,0:T(8,128)(2,1)S(1)} %project.3), channel_id=1, source_target_pairs={{0,14},{1,15},{2,12},{3,13},{4,2},{5,3},{6,0},{7,1},{8,6},{9,7},{1... | collective-permute-start | bytes 393224 | tf_op jit(solution)/shard_map/ppermute | solution.py:437
  36.4 0.3 collective-permute-start.19
  36.6 0.0 collective-permute-start.18
  36.7 0.0 collective-permute-done.17
  36.7 1.2 collective-permute-start.21
  37.9 0.6 collective-permute-done.16
  38.6 1.4 collective-permute-start.20
  40.0 4.5 %collective-permute-done.18 = bf16[256,256]{1,0:T(8,128)(2,1)S(1)} collective-permute-done((bf16[256,256]{1,0:T(8,128)(2,1)S(1)}, bf16[256,256]{1,0:T(8,128)(2,1)S(1)}, u32[]{:S(2)}, u32[]{:S(2)}) %collective-permute-start.18) | collective-permute-done | bytes 131104 | tf_op jit(solution)/shard_map/ppermute | solution.py:437
  44.5 0.0 collective-permute-done.19
  44.5 2.4 %collective-permute-done.20 = bf16[256,256]{1,0:T(8,128)(2,1)S(1)} collective-permute-done((bf16[256,256]{1,0:T(8,128)(2,1)S(1)}, bf16[256,256]{1,0:T(8,128)(2,1)S(1)}, u32[]{:S(2)}, u32[]{:S(2)}) %collective-permute-start.20) | collective-permute-done | bytes 131104 | tf_op jit(solution)/shard_map/ppermute | solution.py:437
  46.9 0.0 collective-permute-done.21
  46.9 0.0 collective-permute-done.22
  46.9 3.5 %collective-permute-start.23 = (bf16[2048,256]{1,0:T(8,128)(2,1)S(1)}, bf16[2048,256]{1,0:T(8,128)(2,1)S(1)}, u32[]{:S(2)}, u32[]{:S(2)}) collective-permute-start(bf16[2048,256]{1,0:T(8,128)(2,1)S(1)} %constant_dynamic-update-slice_fusion.kv_ref), channel_id=1, source_target_pairs={{0,1},{1,0},{2,3},{3,2},{4,5},{5,4},{6,7},{7,6},{8,9},{9,8},{10,11... | collective-permute-start | bytes 3145736 | tf_op jit(solution)/shard_map/ppermute | solution.py:433
  50.4 0.0 copy-done.6
  50.4 0.0 copy-done.5
  50.5 0.0 copy-done.4
  50.5 46.4 %attend.2 = (bf16[4,64,7424]{2,1,0:T(8,128)(2,1)}, bf16[64,3712]{1,0:T(8,128)(2,1)S(1)}) custom-call(s32[1]{0:T(128)} %bitcast.1.core_ref.half_ref, s32[4,16]{1,0:T(4,128)S(1)} %fusion.6.start_ref, s32[4]{0:T(128)S(1)} %copy-done.5, bf16[4,64,7424]{2,1,0:T(8,128)(2,1)} %q_hbm.3, bf16[2048,256]{1,0:T(8,128)(2,1)S(1)} %constant_dynamic-update-slice_fusion.kv_ref, ...), custom_call_target="tpu_custom_call" | custom-call | flops 2189426688 | bytes 3801088 | tf_op jit(solution)/shard_map/attend/pallas_call | solution.py:330
  96.9 0.0 collective-permute-done.23.kv_ref
  96.9 45.7 %attend.3 = bf16[4,64,7424]{2,1,0:T(8,128)(2,1)} custom-call(s32[1]{0:T(128)} %bitcast.half_ref, s32[4,16]{1,0:T(4,128)S(1)} %fusion.6.start_ref, s32[4]{0:T(128)S(1)} %copy-done.5, bf16[4,64,7424]{2,1,0:T(8,128)(2,1)} %q_hbm.3, bf16[2048,256]{1,0:T(8,128)(2,1)S(1)} %collective-permute-done.23.kv_ref, ...), custom_call_target="tpu_custom_call", output_to_operand_aliasing={{}: (7, {})} | custom-call | flops 2189426688 | bytes 3801088 | tf_op jit(solution)/shard_map/attend/pallas_call | solution.py:330
  (13 shorter events, 0.2 us)
Async XLA Ops:
  0.0 0.9 copy-start.3
  1.0 4.4 %copy-start = (bf16[4,128,4096]{2,1,0:T(8,128)(2,1)S(1)}, bf16[4,128,4096]{2,1,0:T(8,128)(2,1)}, u32[]{:S(2)}) copy-start(bf16[4,128,4096]{2,1,0:T(8,128)(2,1)} %states.1) | copy-start | bytes 12582916
  1.0 4.4 %copy-start.1 = (bf16[32,4096]{1,0:T(8,128)(2,1)S(1)}, bf16[32,4096]{1,0:T(8,128)(2,1)}, u32[]{:S(2)}) copy-start(bf16[32,4096]{1,0:T(8,128)(2,1)} %queries.1) | copy-start | bytes 786436
  1.0 4.4 %copy-start.2 = (bf16[4096]{0:T(1024)(128)(2,1)S(1)}, bf16[4096]{0:T(1024)(128)(2,1)}, u32[]{:S(2)}) copy-start(bf16[4096]{0:T(1024)(128)(2,1)} %gain.1) | copy-start | bytes 24580
  1.0 2.9 %collective-permute-start.1 = (bf16[256,256]{1,0:T(8,128)(2,1)S(1)}, bf16[256,256]{1,0:T(8,128)(2,1)S(1)}, u32[]{:S(2)}, u32[]{:S(2)}) collective-permute-start(bf16[256,256]{1,0:T(8,128)(2,1)S(1)} %get-tuple-element.15), channel_id=1, source_target_pairs={{0,1},{1,0},{2,3},{3,2},{4,5},{5,4},{6,7},{7,6},{8,9},{9,8},{10,11... | collective-permute-start | bytes 393224 | tf_op jit(solution)/shard_map/ppermute | solution.py:433
  1.1 7.3 %collective-permute-start.3 = (bf16[256,256]{1,0:T(8,128)(2,1)S(1)}, bf16[256,256]{1,0:T(8,128)(2,1)S(1)}, u32[]{:S(2)}, u32[]{:S(2)}) collective-permute-start(bf16[256,256]{1,0:T(8,128)(2,1)S(1)} %get-tuple-element.14.rest_0_), channel_id=1, source_target_pairs={{0,2},{1,3},{2,6},{3,7},{4,0},{5,1},{6,10},{7,11},{8,4},{9,5},{10,... | collective-permute-start | bytes 393224 | tf_op jit(solution)/shard_map/ppermute | solution.py:437
  3.8 4.7 %collective-permute-start = (bf16[256,256]{1,0:T(8,128)(2,1)S(1)}, bf16[256,256]{1,0:T(8,128)(2,1)S(1)}, u32[]{:S(2)}, u32[]{:S(2)}) collective-permute-start(bf16[256,256]{1,0:T(8,128)(2,1)S(1)} %get-tuple-element.14.rest_0_), channel_id=1, source_target_pairs={{0,4},{1,5},{2,0},{3,1},{4,8},{5,9},{6,2},{7,3},{8,12},{9,13},{10,... | collective-permute-start | bytes 393224 | tf_op jit(solution)/shard_map/ppermute | solution.py:437
  3.9 6.6 %collective-permute-start.4 = (bf16[256,256]{1,0:T(8,128)(2,1)S(1)}, bf16[256,256]{1,0:T(8,128)(2,1)S(1)}, u32[]{:S(2)}, u32[]{:S(2)}) collective-permute-start(bf16[256,256]{1,0:T(8,128)(2,1)S(1)} %collective-permute-done.1.rest_5_), channel_id=1, source_target_pairs={{0,2},{1,3},{2,6},{3,7},{4,0},{5,1},{6,10},{7,11},{8,4},{9,5},{10,... | collective-permute-start | bytes 393224 | tf_op jit(solution)/shard_map/ppermute | solution.py:437
  5.3 6.1 %collective-permute-start.2 = (bf16[256,256]{1,0:T(8,128)(2,1)S(1)}, bf16[256,256]{1,0:T(8,128)(2,1)S(1)}, u32[]{:S(2)}, u32[]{:S(2)}) collective-permute-start(bf16[256,256]{1,0:T(8,128)(2,1)S(1)} %collective-permute-done.1.rest_5_), channel_id=1, source_target_pairs={{0,4},{1,5},{2,0},{3,1},{4,8},{5,9},{6,2},{7,3},{8,12},{9,13},{10,... | collective-permute-start | bytes 393224 | tf_op jit(solution)/shard_map/ppermute | solution.py:437
  11.3 13.1 %collective-permute-start.5 = (bf16[128,4096]{1,0:T(8,128)(2,1)S(1)}, bf16[128,4096]{1,0:T(8,128)(2,1)S(1)}, u32[]{:S(2)}, u32[]{:S(2)}) collective-permute-start(bf16[128,4096]{1,0:T(8,128)(2,1)S(1)} %pool.1.own_ref), channel_id=1, source_target_pairs={{0,1},{1,0},{2,3},{3,2},{4,5},{5,4},{6,7},{7,6},{8,9},{9,8},{10,11... | collective-permute-start | bytes 3145736 | tf_op jit(solution)/shard_map/ppermute | solution.py:433
  12.5 5.1 %collective-permute-start.6 = (bf16[256,256]{1,0:T(8,128)(2,1)S(1)}, bf16[256,256]{1,0:T(8,128)(2,1)S(1)}, u32[]{:S(2)}, u32[]{:S(2)}) collective-permute-start(bf16[256,256]{1,0:T(8,128)(2,1)S(1)} %collective-permute-done.rest_1_), channel_id=1, source_target_pairs={{0,4},{1,5},{2,0},{3,1},{4,8},{5,9},{6,2},{7,3},{8,12},{9,13},{10,... | collective-permute-start | bytes 393224 | tf_op jit(solution)/shard_map/ppermute | solution.py:437
  12.6 5.1 %collective-permute-start.13 = (bf16[256,256]{1,0:T(8,128)(2,1)S(1)}, bf16[256,256]{1,0:T(8,128)(2,1)S(1)}, u32[]{:S(2)}, u32[]{:S(2)}) collective-permute-start(bf16[256,256]{1,0:T(8,128)(2,1)S(1)} %collective-permute-done.4.rest_7_), channel_id=1, source_target_pairs={{0,2},{1,3},{2,6},{3,7},{4,0},{5,1},{6,10},{7,11},{8,4},{9,5},{10,... | collective-permute-start | bytes 393224 | tf_op jit(solution)/shard_map/ppermute | solution.py:437
  14.0 6.2 %collective-permute-start.8 = (bf16[256,256]{1,0:T(8,128)(2,1)S(1)}, bf16[256,256]{1,0:T(8,128)(2,1)S(1)}, u32[]{:S(2)}, u32[]{:S(2)}) collective-permute-start(bf16[256,256]{1,0:T(8,128)(2,1)S(1)} %collective-permute-done.3.rest_2_), channel_id=1, source_target_pairs={{0,2},{1,3},{2,6},{3,7},{4,0},{5,1},{6,10},{7,11},{8,4},{9,5},{10,... | collective-permute-start | bytes 393224 | tf_op jit(solution)/shard_map/ppermute | solution.py:437
  15.3 6.3 %collective-permute-start.11 = (bf16[256,256]{1,0:T(8,128)(2,1)S(1)}, bf16[256,256]{1,0:T(8,128)(2,1)S(1)}, u32[]{:S(2)}, u32[]{:S(2)}) collective-permute-start(bf16[256,256]{1,0:T(8,128)(2,1)S(1)} %collective-permute-done.2.rest_6_), channel_id=1, source_target_pairs={{0,4},{1,5},{2,0},{3,1},{4,8},{5,9},{6,2},{7,3},{8,12},{9,13},{10,... | collective-permute-start | bytes 393224 | tf_op jit(solution)/shard_map/ppermute | solution.py:437
  17.6 5.3 %collective-permute-start.7 = (bf16[256,256]{1,0:T(8,128)(2,1)S(1)}, bf16[256,256]{1,0:T(8,128)(2,1)S(1)}, u32[]{:S(2)}, u32[]{:S(2)}) collective-permute-start(bf16[256,256]{1,0:T(8,128)(2,1)S(1)} %collective-permute-done.6.rest_3_), channel_id=1, source_target_pairs={{0,4},{1,5},{2,0},{3,1},{4,8},{5,9},{6,2},{7,3},{8,12},{9,13},{10,... | collective-permute-start | bytes 393224 | tf_op jit(solution)/shard_map/ppermute | solution.py:437
  17.7 5.4 %collective-permute-start.14 = (bf16[256,256]{1,0:T(8,128)(2,1)S(1)}, bf16[256,256]{1,0:T(8,128)(2,1)}, u32[]{:S(2)}, u32[]{:S(2)}) collective-permute-start(bf16[256,256]{1,0:T(8,128)(2,1)S(1)} %collective-permute-done.13.rest_9_), channel_id=1, source_target_pairs={{0,2},{1,3},{2,6},{3,7},{4,0},{5,1},{6,10},{7,11},{8,4},{9,5},{10,... | collective-permute-start | bytes 393224 | tf_op jit(solution)/shard_map/ppermute | solution.py:437
  20.2 5.3 %collective-permute-start.9 = (bf16[256,256]{1,0:T(8,128)(2,1)S(1)}, bf16[256,256]{1,0:T(8,128)(2,1)}, u32[]{:S(2)}, u32[]{:S(2)}) collective-permute-start(bf16[256,256]{1,0:T(8,128)(2,1)S(1)} %collective-permute-done.8.rest_4_), channel_id=1, source_target_pairs={{0,2},{1,3},{2,6},{3,7},{4,0},{5,1},{6,10},{7,11},{8,4},{9,5},{10,... | collective-permute-start | bytes 393224 | tf_op jit(solution)/shard_map/ppermute | solution.py:437
  21.6 4.2 %collective-permute-start.12 = (bf16[256,256]{1,0:T(8,128)(2,1)S(1)}, bf16[256,256]{1,0:T(8,128)(2,1)}, u32[]{:S(2)}, u32[]{:S(2)}) collective-permute-start(bf16[256,256]{1,0:T(8,128)(2,1)S(1)} %collective-permute-done.11.rest_8_), channel_id=1, source_target_pairs={{0,4},{1,5},{2,0},{3,1},{4,8},{5,9},{6,2},{7,3},{8,12},{9,13},{10,... | collective-permute-start | bytes 393224 | tf_op jit(solution)/shard_map/ppermute | solution.py:437
  23.0 4.7 %collective-permute-start.10 = (bf16[256,256]{1,0:T(8,128)(2,1)S(1)}, bf16[256,256]{1,0:T(8,128)(2,1)}, u32[]{:S(2)}, u32[]{:S(2)}) collective-permute-start(bf16[256,256]{1,0:T(8,128)(2,1)S(1)} %collective-permute-done.7.rest_0_), channel_id=1, source_target_pairs={{0,4},{1,5},{2,0},{3,1},{4,8},{5,9},{6,2},{7,3},{8,12},{9,13},{10,... | collective-permute-start | bytes 393224 | tf_op jit(solution)/shard_map/ppermute | solution.py:437
  23.2 4.9 %collective-permute-start.15 = (bf16[256,256]{1,0:T(8,128)(2,1)}, bf16[256,256]{1,0:T(8,128)(2,1)}, u32[]{:S(2)}, u32[]{:S(2)}) collective-permute-start(bf16[256,256]{1,0:T(8,128)(2,1)} %collective-permute-done.14.rest_4_), channel_id=1, source_target_pairs={{0,2},{1,3},{2,6},{3,7},{4,0},{5,1},{6,10},{7,11},{8,4},{9,5},{10,... | collective-permute-start | bytes 393224 | tf_op jit(solution)/shard_map/ppermute | solution.py:437
  24.4 26.0 %copy-start.6 = (s32[4,16]{1,0:T(4,128)S(1)}, s32[4,16]{1,0:T(4,128)}, u32[]{:S(2)}) copy-start(s32[4,16]{1,0:T(4,128)} %param.12) | copy-start | bytes 772
  24.4 26.0 %copy-start.5 = (s32[4]{0:T(128)S(1)}, s32[4]{0:T(128)}, u32[]{:S(2)}) copy-start(s32[4]{0:T(128)} %length_ref.3) | copy-start | bytes 52
  25.0 25.5 %copy-start.4 = (bf16[4,64,512]{2,1,0:T(8,128)(2,1)S(1)}, bf16[4,64,512]{2,1,0:T(8,128)(2,1)}, u32[]{:S(2)}) copy-start(bf16[4,64,512]{2,1,0:T(8,128)(2,1)} %own_kv_ref.3) | copy-start | bytes 786436
  29.7 7.0 %collective-permute-start.17 = (bf16[256,256]{1,0:T(8,128)(2,1)S(1)}, bf16[256,256]{1,0:T(8,128)(2,1)S(1)}, u32[]{:S(2)}, u32[]{:S(2)}) collective-permute-start(bf16[256,256]{1,0:T(8,128)(2,1)S(1)} %project.3), channel_id=1, source_target_pairs={{0,8},{1,9},{2,10},{3,11},{4,12},{5,13},{6,14},{7,15},{8,0},{9,1},... | collective-permute-start | bytes 393224 | tf_op jit(solution)/shard_map/ppermute | solution.py:437
  32.2 6.4 %collective-permute-start.16 = (bf16[256,256]{1,0:T(8,128)(2,1)S(1)}, bf16[256,256]{1,0:T(8,128)(2,1)S(1)}, u32[]{:S(2)}, u32[]{:S(2)}) collective-permute-start(bf16[256,256]{1,0:T(8,128)(2,1)S(1)} %project.3), channel_id=1, source_target_pairs={{0,4},{1,5},{2,6},{3,7},{4,8},{5,9},{6,10},{7,11},{8,12},{9,13},{1... | collective-permute-start | bytes 393224 | tf_op jit(solution)/shard_map/ppermute | solution.py:437
  33.5 13.4 %collective-permute-start.22 = (bf16[256,256]{1,0:T(8,128)(2,1)S(1)}, bf16[256,256]{1,0:T(8,128)(2,1)S(1)}, u32[]{:S(2)}, u32[]{:S(2)}) collective-permute-start(bf16[256,256]{1,0:T(8,128)(2,1)S(1)} %project.3), channel_id=1, source_target_pairs={{0,14},{1,15},{2,12},{3,13},{4,2},{5,3},{6,0},{7,1},{8,6},{9,7},{1... | collective-permute-start | bytes 393224 | tf_op jit(solution)/shard_map/ppermute | solution.py:437
  36.4 8.1 %collective-permute-start.19 = (bf16[256,256]{1,0:T(8,128)(2,1)S(1)}, bf16[256,256]{1,0:T(8,128)(2,1)S(1)}, u32[]{:S(2)}, u32[]{:S(2)}) collective-permute-start(bf16[256,256]{1,0:T(8,128)(2,1)S(1)} %project.3), channel_id=1, source_target_pairs={{0,2},{1,3},{2,0},{3,1},{4,6},{5,7},{6,4},{7,5},{8,10},{9,11},{10,... | collective-permute-start | bytes 393224 | tf_op jit(solution)/shard_map/ppermute | solution.py:437
  36.6 7.8 %collective-permute-start.18 = (bf16[256,256]{1,0:T(8,128)(2,1)S(1)}, bf16[256,256]{1,0:T(8,128)(2,1)S(1)}, u32[]{:S(2)}, u32[]{:S(2)}) collective-permute-start(bf16[256,256]{1,0:T(8,128)(2,1)S(1)} %project.3), channel_id=1, source_target_pairs={{0,12},{1,13},{2,14},{3,15},{4,0},{5,1},{6,2},{7,3},{8,4},{9,5},{1... | collective-permute-start | bytes 393224 | tf_op jit(solution)/shard_map/ppermute | solution.py:437
  36.7 10.2 %collective-permute-start.21 = (bf16[256,256]{1,0:T(8,128)(2,1)S(1)}, bf16[256,256]{1,0:T(8,128)(2,1)S(1)}, u32[]{:S(2)}, u32[]{:S(2)}) collective-permute-start(bf16[256,256]{1,0:T(8,128)(2,1)S(1)} %collective-permute-done.17), channel_id=1, source_target_pairs={{0,2},{1,3},{2,0},{3,1},{4,6},{5,7},{6,4},{7,5},{8,10},{9,11},{10,... | collective-permute-start | bytes 393224 | tf_op jit(solution)/shard_map/ppermute | solution.py:437
  38.6 8.3 %collective-permute-start.20 = (bf16[256,256]{1,0:T(8,128)(2,1)S(1)}, bf16[256,256]{1,0:T(8,128)(2,1)S(1)}, u32[]{:S(2)}, u32[]{:S(2)}) collective-permute-start(bf16[256,256]{1,0:T(8,128)(2,1)S(1)} %collective-permute-done.16), channel_id=1, source_target_pairs={{0,2},{1,3},{2,0},{3,1},{4,6},{5,7},{6,4},{7,5},{8,10},{9,11},{10,... | collective-permute-start | bytes 393224 | tf_op jit(solution)/shard_map/ppermute | solution.py:437
  46.9 49.9 %collective-permute-start.23 = (bf16[2048,256]{1,0:T(8,128)(2,1)S(1)}, bf16[2048,256]{1,0:T(8,128)(2,1)S(1)}, u32[]{:S(2)}, u32[]{:S(2)}) collective-permute-start(bf16[2048,256]{1,0:T(8,128)(2,1)S(1)} %constant_dynamic-update-slice_fusion.kv_ref), channel_id=1, source_target_pairs={{0,1},{1,0},{2,3},{3,2},{4,5},{5,4},{6,7},{7,6},{8,9},{9,8},{10,11... | collective-permute-start | bytes 3145736 | tf_op jit(solution)/shard_map/ppermute | solution.py:433

commit v19 on v17

--- a/solution.py
+++ b/solution.py
@@ -475,10 +475,12 @@
             for chain, hop in zip(up + down, hops):
                 chain[-1] = hop
             other_rows = to_partner(rows)
+        elif turn == 2:
+            early = project(chips, core, place, rows, other_rows, blocks((0, 1)))
+            down[1][-1], early = lax.optimization_barrier((down[1][-1], early))
     up[0].append(along_ring(up[0][-1], 1))
     down[1].append(along_ring(down[1][-1], -1))
-    early = project(chips, core, place, rows, other_rows, blocks((0, 1, 2)))
-    memory_kv = project(chips, core, place, rows, other_rows, blocks((3, 4)), early)
+    memory_kv = project(chips, core, place, rows, other_rows, blocks((2, 3, 4)), early)
     near = jnp.concatenate(line_by_line(memory_kv), axis=0)
     far = to_partner(near)
 

time: 145 us -> 144 us (level)
  no operation moved by 1% of the time
where the time goes in v19:
time: 144 us; the launch traced here: 142 us
  Pallas kernels  96.2 us (67%)
  starting transfers between devices  24.6 us (17%)
  waiting for transfers between devices  19.5 us (14%)
    pallas_call x2, Pallas kernels, attend(): pl.pallas_call(functools.partial(attend_kernel, begun is not None, ahead)...  92.1 us
    ppermute x21, starting transfers between devices, along(): lax.ppermute(x, 'pass', [(2 * s + c, 2 * d + c) for s, d in pairs for c i...  20.5 us
    ppermute x21, waiting for transfers between devices, along(): lax.ppermute(x, 'pass', [(2 * s + c, 2 * d + c) for s, d in pairs for c i...  19.5 us
    ppermute x3, starting transfers between devices, to_partner(): return lax.ppermute(x, 'pass', [(i, i ^ 1) for i in range(extent)])  4.13 us
    pallas_call x1, Pallas kernels, pool(): pl.pallas_call(pool_kernel, in_specs=[vmem] * 3, out_specs=vmem, out_shap...  3.08 us
  transfers between devices with their start and end apart: 24, of which 13 were waited for; matrix products, arithmetic and copies ran while one was open for 0% of the time, Pallas kernels for 35%

profile of v19, /device:TPU:1, one launch (start us, length us, event | category | flops | bytes accessed | tf_op | source)
XLA Modules:
  0.0 141.7 jit_solution(13236317217803943626)
XLA Ops:
  0.0 0.0 copy-start.3
  0.0 0.9 copy-done.3
  1.0 0.0 copy-start
  1.0 0.0 copy-start.1
  1.0 0.0 copy-start.2
  1.0 0.1 collective-permute-start.1
  1.1 2.7 %collective-permute-start.3 = (bf16[256,256]{1,0:T(8,128)(2,1)S(1)}, bf16[256,256]{1,0:T(8,128)(2,1)S(1)}, u32[]{:S(2)}, u32[]{:S(2)}) collective-permute-start(bf16[256,256]{1,0:T(8,128)(2,1)S(1)} %get-tuple-element.16.rest_0_), channel_id=1, source_target_pairs={{0,2},{1,3},{2,6},{3,7},{4,0},{5,1},{6,10},{7,11},{8,4},{9,5},{10,... | collective-permute-start | bytes 393224 | tf_op jit(solution)/shard_map/ppermute | solution.py:437
  3.8 0.1 collective-permute-start
  3.9 0.0 collective-permute-done.1.rest_3_
  3.9 1.4 collective-permute-start.4
  5.3 0.1 collective-permute-start.2
  5.3 0.0 copy-done
  5.4 0.0 copy-done.1
  5.4 0.0 copy-done.2
  5.4 3.1 %pool.1.own_ref = bf16[128,4096]{1,0:T(8,128)(2,1)S(1)} custom-call(bf16[4,128,4096]{2,1,0:T(8,128)(2,1)S(1)} %copy-done, bf16[32,4096]{1,0:T(8,128)(2,1)S(1)} %copy-done.1, bf16[4096]{0:T(1024)(128)(2,1)S(1)} %copy-done.2), custom_call_target="tpu_custom_call" | custom-call | flops 268435456 | bytes 4194304 | tf_op jit(solution)/shard_map/pool/pallas_call | solution.py:116
  8.4 0.0 collective-permute-done.3.rest_2_
  8.5 0.1 collective-permute-done.rest_1_
  8.5 2.0 %collective-permute-done.4.rest_5_ = bf16[256,256]{1,0:T(8,128)(2,1)S(1)} collective-permute-done((bf16[256,256]{1,0:T(8,128)(2,1)S(1)}, bf16[256,256]{1,0:T(8,128)(2,1)S(1)}, u32[]{:S(2)}, u32[]{:S(2)}) %collective-permute-start.4) | collective-permute-done | bytes 131104 | tf_op jit(solution)/shard_map/ppermute | solution.py:437
  10.5 0.9 collective-permute-done.2.rest_4_
  11.3 1.2 collective-permute-start.5
  12.5 0.1 collective-permute-start.6
  12.6 1.4 collective-permute-start.12
  14.0 1.3 collective-permute-start.7
  15.3 0.2 collective-permute-start.11
  15.4 2.2 %collective-permute-done.6.rest_0_ = bf16[256,256]{1,0:T(8,128)(2,1)S(1)} collective-permute-done((bf16[256,256]{1,0:T(8,128)(2,1)S(1)}, bf16[256,256]{1,0:T(8,128)(2,1)S(1)}, u32[]{:S(2)}, u32[]{:S(2)}) %collective-permute-start.6) | collective-permute-done | bytes 131104 | tf_op jit(solution)/shard_map/ppermute | solution.py:437
  17.6 0.1 collective-permute-start.8
  17.7 0.0 collective-permute-done.5.other_ref
  17.7 0.4 project.2.rest_10_
  18.1 0.0 collective-permute-done.12.rest_6_
  18.1 1.4 %collective-permute-start.14 = (bf16[256,256]{1,0:T(8,128)(2,1)S(1)}, bf16[256,256]{1,0:T(8,128)(2,1)S(1)}, u32[]{:S(2)}, u32[]{:S(2)}) collective-permute-start(bf16[256,256]{1,0:T(8,128)(2,1)S(1)} %collective-permute-done.12.rest_6_), channel_id=1, source_target_pairs={{0,2},{1,3},{2,6},{3,7},{4,0},{5,1},{6,10},{7,11},{8,4},{9,5},{10,... | collective-permute-start | bytes 393224 | tf_op jit(solution)/shard_map/ppermute | solution.py:437
  19.6 0.6 collective-permute-done.7.rest_1_
  20.2 1.4 collective-permute-start.9
  21.6 0.0 collective-permute-done.11.rest_5_
  21.6 0.1 collective-permute-start.13
  21.7 1.2 collective-permute-done.8.rest_2_
  22.9 0.3 collective-permute-start.10
  23.2 0.0 collective-permute-done.14.rest_8_
  23.2 1.2 collective-permute-start.15
  24.3 1.3 collective-permute-done.9.rest_3_
  25.6 0.1 collective-permute-done.13.rest_7_
  25.7 2.3 %collective-permute-done.10.rest_4_ = bf16[256,256]{1,0:T(8,128)(2,1)S(1)} collective-permute-done((bf16[256,256]{1,0:T(8,128)(2,1)S(1)}, bf16[256,256]{1,0:T(8,128)(2,1)S(1)}, u32[]{:S(2)}, u32[]{:S(2)}) %collective-permute-start.10) | collective-permute-done | bytes 131104 | tf_op jit(solution)/shard_map/ppermute | solution.py:437
  28.0 0.1 collective-permute-done.15.rest_9_
  28.1 0.5 project.3
  28.7 2.8 %collective-permute-start.17 = (bf16[256,256]{1,0:T(8,128)(2,1)S(1)}, bf16[256,256]{1,0:T(8,128)(2,1)S(1)}, u32[]{:S(2)}, u32[]{:S(2)}) collective-permute-start(bf16[256,256]{1,0:T(8,128)(2,1)S(1)} %project.3), channel_id=1, source_target_pairs={{0,8},{1,9},{2,10},{3,11},{4,12},{5,13},{6,14},{7,15},{8,0},{9,1},... | collective-permute-start | bytes 393224 | tf_op jit(solution)/shard_map/ppermute | solution.py:437
  31.5 1.3 collective-permute-start.16
  32.8 2.5 %collective-permute-start.22 = (bf16[256,256]{1,0:T(8,128)(2,1)S(1)}, bf16[256,256]{1,0:T(8,128)(2,1)S(1)}, u32[]{:S(2)}, u32[]{:S(2)}) collective-permute-start(bf16[256,256]{1,0:T(8,128)(2,1)S(1)} %project.3), channel_id=1, source_target_pairs={{0,14},{1,15},{2,12},{3,13},{4,2},{5,3},{6,0},{7,1},{8,6},{9,7},{1... | collective-permute-start | bytes 393224 | tf_op jit(solution)/shard_map/ppermute | solution.py:437
  35.3 0.6 collective-permute-start.19
  35.9 0.0 collective-permute-start.18
  36.0 0.0 collective-permute-done.17
  36.0 0.9 collective-permute-start.21
  36.9 1.1 collective-permute-done.16
  38.0 0.7 collective-permute-start.20
  38.7 4.8 %collective-permute-done.18 = bf16[256,256]{1,0:T(8,128)(2,1)S(1)} collective-permute-done((bf16[256,256]{1,0:T(8,128)(2,1)S(1)}, bf16[256,256]{1,0:T(8,128)(2,1)S(1)}, u32[]{:S(2)}, u32[]{:S(2)}) %collective-permute-start.18) | collective-permute-done | bytes 131104 | tf_op jit(solution)/shard_map/ppermute | solution.py:437
  43.5 0.0 collective-permute-done.19
  43.5 2.9 %collective-permute-done.20 = bf16[256,256]{1,0:T(8,128)(2,1)S(1)} collective-permute-done((bf16[256,256]{1,0:T(8,128)(2,1)S(1)}, bf16[256,256]{1,0:T(8,128)(2,1)S(1)}, u32[]{:S(2)}, u32[]{:S(2)}) %collective-permute-start.20) | collective-permute-done | bytes 131104 | tf_op jit(solution)/shard_map/ppermute | solution.py:437
  46.4 0.0 collective-permute-done.21
  46.5 0.0 collective-permute-done.22
  46.5 2.8 %collective-permute-start.23 = (bf16[2048,256]{1,0:T(8,128)(2,1)S(1)}, bf16[2048,256]{1,0:T(8,128)(2,1)S(1)}, u32[]{:S(2)}, u32[]{:S(2)}) collective-permute-start(bf16[2048,256]{1,0:T(8,128)(2,1)S(1)} %constant_dynamic-update-slice_fusion.kv_ref), channel_id=1, source_target_pairs={{0,1},{1,0},{2,3},{3,2},{4,5},{5,4},{6,7},{7,6},{8,9},{9,8},{10,11... | collective-permute-start | bytes 3145736 | tf_op jit(solution)/shard_map/ppermute | solution.py:433
  49.3 0.0 copy-done.6
  49.4 0.0 copy-done.4
  49.4 0.0 copy-done.5
  49.4 46.4 %attend.2 = (bf16[4,64,7424]{2,1,0:T(8,128)(2,1)}, bf16[64,3712]{1,0:T(8,128)(2,1)S(1)}) custom-call(s32[1]{0:T(128)} %bitcast.1.core_ref.half_ref, s32[4,16]{1,0:T(4,128)S(1)} %fusion.6.start_ref, s32[4]{0:T(128)S(1)} %copy-done.5, bf16[4,64,7424]{2,1,0:T(8,128)(2,1)} %q_hbm.3, bf16[2048,256]{1,0:T(8,128)(2,1)S(1)} %constant_dynamic-update-slice_fusion.kv_ref, ...), custom_call_target="tpu_custom_call" | custom-call | flops 2189426688 | bytes 3801088 | tf_op jit(solution)/shard_map/attend/pallas_call | solution.py:330
  95.8 0.0 collective-permute-done.23.kv_ref
  95.8 45.7 %attend.3 = bf16[4,64,7424]{2,1,0:T(8,128)(2,1)} custom-call(s32[1]{0:T(128)} %bitcast.half_ref, s32[4,16]{1,0:T(4,128)S(1)} %fusion.6.start_ref, s32[4]{0:T(128)S(1)} %copy-done.5, bf16[4,64,7424]{2,1,0:T(8,128)(2,1)} %q_hbm.3, bf16[2048,256]{1,0:T(8,128)(2,1)S(1)} %collective-permute-done.23.kv_ref, ...), custom_call_target="tpu_custom_call", output_to_operand_aliasing={{}: (7, {})} | custom-call | flops 2189426688 | bytes 3801088 | tf_op jit(solution)/shard_map/attend/pallas_call | solution.py:330
  (13 shorter events, 0.2 us)
Async XLA Ops:
  0.0 0.9 copy-start.3
  1.0 4.4 %copy-start = (bf16[4,128,4096]{2,1,0:T(8,128)(2,1)S(1)}, bf16[4,128,4096]{2,1,0:T(8,128)(2,1)}, u32[]{:S(2)}) copy-start(bf16[4,128,4096]{2,1,0:T(8,128)(2,1)} %states.1) | copy-start | bytes 12582916
  1.0 4.4 %copy-start.1 = (bf16[32,4096]{1,0:T(8,128)(2,1)S(1)}, bf16[32,4096]{1,0:T(8,128)(2,1)}, u32[]{:S(2)}) copy-start(bf16[32,4096]{1,0:T(8,128)(2,1)} %queries.1) | copy-start | bytes 786436
  1.0 4.4 %copy-start.2 = (bf16[4096]{0:T(1024)(128)(2,1)S(1)}, bf16[4096]{0:T(1024)(128)(2,1)}, u32[]{:S(2)}) copy-start(bf16[4096]{0:T(1024)(128)(2,1)} %gain.1) | copy-start | bytes 24580
  1.0 2.9 %collective-permute-start.1 = (bf16[256,256]{1,0:T(8,128)(2,1)S(1)}, bf16[256,256]{1,0:T(8,128)(2,1)S(1)}, u32[]{:S(2)}, u32[]{:S(2)}) collective-permute-start(bf16[256,256]{1,0:T(8,128)(2,1)S(1)} %get-tuple-element.17), channel_id=1, source_target_pairs={{0,1},{1,0},{2,3},{3,2},{4,5},{5,4},{6,7},{7,6},{8,9},{9,8},{10,11... | collective-permute-start | bytes 393224 | tf_op jit(solution)/shard_map/ppermute | solution.py:433
  1.1 7.3 %collective-permute-start.3 = (bf16[256,256]{1,0:T(8,128)(2,1)S(1)}, bf16[256,256]{1,0:T(8,128)(2,1)S(1)}, u32[]{:S(2)}, u32[]{:S(2)}) collective-permute-start(bf16[256,256]{1,0:T(8,128)(2,1)S(1)} %get-tuple-element.16.rest_0_), channel_id=1, source_target_pairs={{0,2},{1,3},{2,6},{3,7},{4,0},{5,1},{6,10},{7,11},{8,4},{9,5},{10,... | collective-permute-start | bytes 393224 | tf_op jit(solution)/shard_map/ppermute | solution.py:437
  3.8 4.7 %collective-permute-start = (bf16[256,256]{1,0:T(8,128)(2,1)S(1)}, bf16[256,256]{1,0:T(8,128)(2,1)S(1)}, u32[]{:S(2)}, u32[]{:S(2)}) collective-permute-start(bf16[256,256]{1,0:T(8,128)(2,1)S(1)} %get-tuple-element.16.rest_0_), channel_id=1, source_target_pairs={{0,4},{1,5},{2,0},{3,1},{4,8},{5,9},{6,2},{7,3},{8,12},{9,13},{10,... | collective-permute-start | bytes 393224 | tf_op jit(solution)/shard_map/ppermute | solution.py:437
  3.9 6.6 %collective-permute-start.4 = (bf16[256,256]{1,0:T(8,128)(2,1)S(1)}, bf16[256,256]{1,0:T(8,128)(2,1)S(1)}, u32[]{:S(2)}, u32[]{:S(2)}) collective-permute-start(bf16[256,256]{1,0:T(8,128)(2,1)S(1)} %collective-permute-done.1.rest_3_), channel_id=1, source_target_pairs={{0,2},{1,3},{2,6},{3,7},{4,0},{5,1},{6,10},{7,11},{8,4},{9,5},{10,... | collective-permute-start | bytes 393224 | tf_op jit(solution)/shard_map/ppermute | solution.py:437
  5.3 6.1 %collective-permute-start.2 = (bf16[256,256]{1,0:T(8,128)(2,1)S(1)}, bf16[256,256]{1,0:T(8,128)(2,1)S(1)}, u32[]{:S(2)}, u32[]{:S(2)}) collective-permute-start(bf16[256,256]{1,0:T(8,128)(2,1)S(1)} %collective-permute-done.1.rest_3_), channel_id=1, source_target_pairs={{0,4},{1,5},{2,0},{3,1},{4,8},{5,9},{6,2},{7,3},{8,12},{9,13},{10,... | collective-permute-start | bytes 393224 | tf_op jit(solution)/shard_map/ppermute | solution.py:437
  11.3 6.4 %collective-permute-start.5 = (bf16[128,4096]{1,0:T(8,128)(2,1)S(1)}, bf16[128,4096]{1,0:T(8,128)(2,1)S(1)}, u32[]{:S(2)}, u32[]{:S(2)}) collective-permute-start(bf16[128,4096]{1,0:T(8,128)(2,1)S(1)} %pool.1.own_ref), channel_id=1, source_target_pairs={{0,1},{1,0},{2,3},{3,2},{4,5},{5,4},{6,7},{7,6},{8,9},{9,8},{10,11... | collective-permute-start | bytes 3145736 | tf_op jit(solution)/shard_map/ppermute | solution.py:433
  12.5 5.1 %collective-permute-start.6 = (bf16[256,256]{1,0:T(8,128)(2,1)S(1)}, bf16[256,256]{1,0:T(8,128)(2,1)S(1)}, u32[]{:S(2)}, u32[]{:S(2)}) collective-permute-start(bf16[256,256]{1,0:T(8,128)(2,1)S(1)} %collective-permute-done.rest_1_), channel_id=1, source_target_pairs={{0,4},{1,5},{2,0},{3,1},{4,8},{5,9},{6,2},{7,3},{8,12},{9,13},{10,... | collective-permute-start | bytes 393224 | tf_op jit(solution)/shard_map/ppermute | solution.py:437
  12.6 5.5 %collective-permute-start.12 = (bf16[256,256]{1,0:T(8,128)(2,1)S(1)}, bf16[256,256]{1,0:T(8,128)(2,1)S(1)}, u32[]{:S(2)}, u32[]{:S(2)}) collective-permute-start(bf16[256,256]{1,0:T(8,128)(2,1)S(1)} %collective-permute-done.4.rest_5_), channel_id=1, source_target_pairs={{0,2},{1,3},{2,6},{3,7},{4,0},{5,1},{6,10},{7,11},{8,4},{9,5},{10,... | collective-permute-start | bytes 393224 | tf_op jit(solution)/shard_map/ppermute | solution.py:437
  14.0 6.2 %collective-permute-start.7 = (bf16[256,256]{1,0:T(8,128)(2,1)S(1)}, bf16[256,256]{1,0:T(8,128)(2,1)S(1)}, u32[]{:S(2)}, u32[]{:S(2)}) collective-permute-start(bf16[256,256]{1,0:T(8,128)(2,1)S(1)} %collective-permute-done.3.rest_2_), channel_id=1, source_target_pairs={{0,2},{1,3},{2,6},{3,7},{4,0},{5,1},{6,10},{7,11},{8,4},{9,5},{10,... | collective-permute-start | bytes 393224 | tf_op jit(solution)/shard_map/ppermute | solution.py:437
  15.3 6.3 %collective-permute-start.11 = (bf16[256,256]{1,0:T(8,128)(2,1)S(1)}, bf16[256,256]{1,0:T(8,128)(2,1)S(1)}, u32[]{:S(2)}, u32[]{:S(2)}) collective-permute-start(bf16[256,256]{1,0:T(8,128)(2,1)S(1)} %collective-permute-done.2.rest_4_), channel_id=1, source_target_pairs={{0,4},{1,5},{2,0},{3,1},{4,8},{5,9},{6,2},{7,3},{8,12},{9,13},{10,... | collective-permute-start | bytes 393224 | tf_op jit(solution)/shard_map/ppermute | solution.py:437
  17.6 5.2 %collective-permute-start.8 = (bf16[256,256]{1,0:T(8,128)(2,1)S(1)}, bf16[256,256]{1,0:T(8,128)(2,1)S(1)}, u32[]{:S(2)}, u32[]{:S(2)}) collective-permute-start(bf16[256,256]{1,0:T(8,128)(2,1)S(1)} %collective-permute-done.6.rest_0_), channel_id=1, source_target_pairs={{0,4},{1,5},{2,0},{3,1},{4,8},{5,9},{6,2},{7,3},{8,12},{9,13},{10,... | collective-permute-start | bytes 393224 | tf_op jit(solution)/shard_map/ppermute | solution.py:437
  17.7 31.6 %copy-start.6 = (s32[4,16]{1,0:T(4,128)S(1)}, s32[4,16]{1,0:T(4,128)}, u32[]{:S(2)}) copy-start(s32[4,16]{1,0:T(4,128)} %param.12) | copy-start | bytes 772
  17.7 31.6 %copy-start.4 = (bf16[4,64,512]{2,1,0:T(8,128)(2,1)S(1)}, bf16[4,64,512]{2,1,0:T(8,128)(2,1)}, u32[]{:S(2)}) copy-start(bf16[4,64,512]{2,1,0:T(8,128)(2,1)} %own_kv_ref.3) | copy-start | bytes 786436
  17.7 31.6 %copy-start.5 = (s32[4]{0:T(128)S(1)}, s32[4]{0:T(128)}, u32[]{:S(2)}) copy-start(s32[4]{0:T(128)} %length_ref.3) | copy-start | bytes 52
  18.1 5.0 %collective-permute-start.14 = (bf16[256,256]{1,0:T(8,128)(2,1)S(1)}, bf16[256,256]{1,0:T(8,128)(2,1)S(1)}, u32[]{:S(2)}, u32[]{:S(2)}) collective-permute-start(bf16[256,256]{1,0:T(8,128)(2,1)S(1)} %collective-permute-done.12.rest_6_), channel_id=1, source_target_pairs={{0,2},{1,3},{2,6},{3,7},{4,0},{5,1},{6,10},{7,11},{8,4},{9,5},{10,... | collective-permute-start | bytes 393224 | tf_op jit(solution)/shard_map/ppermute | solution.py:437
  20.2 5.4 %collective-permute-start.9 = (bf16[256,256]{1,0:T(8,128)(2,1)S(1)}, bf16[256,256]{1,0:T(8,128)(2,1)S(1)}, u32[]{:S(2)}, u32[]{:S(2)}) collective-permute-start(bf16[256,256]{1,0:T(8,128)(2,1)S(1)} %collective-permute-done.7.rest_1_), channel_id=1, source_target_pairs={{0,2},{1,3},{2,6},{3,7},{4,0},{5,1},{6,10},{7,11},{8,4},{9,5},{10,... | collective-permute-start | bytes 393224 | tf_op jit(solution)/shard_map/ppermute | solution.py:437
  21.6 4.1 %collective-permute-start.13 = (bf16[256,256]{1,0:T(8,128)(2,1)S(1)}, bf16[256,256]{1,0:T(8,128)(2,1)S(1)}, u32[]{:S(2)}, u32[]{:S(2)}) collective-permute-start(bf16[256,256]{1,0:T(8,128)(2,1)S(1)} %collective-permute-done.11.rest_5_), channel_id=1, source_target_pairs={{0,4},{1,5},{2,0},{3,1},{4,8},{5,9},{6,2},{7,3},{8,12},{9,13},{10,... | collective-permute-start | bytes 393224 | tf_op jit(solution)/shard_map/ppermute | solution.py:437
  22.9 5.1 %collective-permute-start.10 = (bf16[256,256]{1,0:T(8,128)(2,1)S(1)}, bf16[256,256]{1,0:T(8,128)(2,1)S(1)}, u32[]{:S(2)}, u32[]{:S(2)}) collective-permute-start(bf16[256,256]{1,0:T(8,128)(2,1)S(1)} %collective-permute-done.8.rest_2_), channel_id=1, source_target_pairs={{0,4},{1,5},{2,0},{3,1},{4,8},{5,9},{6,2},{7,3},{8,12},{9,13},{10,... | collective-permute-start | bytes 393224 | tf_op jit(solution)/shard_map/ppermute | solution.py:437
  23.2 5.0 %collective-permute-start.15 = (bf16[256,256]{1,0:T(8,128)(2,1)S(1)}, bf16[256,256]{1,0:T(8,128)(2,1)S(1)}, u32[]{:S(2)}, u32[]{:S(2)}) collective-permute-start(bf16[256,256]{1,0:T(8,128)(2,1)S(1)} %collective-permute-done.14.rest_8_), channel_id=1, source_target_pairs={{0,2},{1,3},{2,6},{3,7},{4,0},{5,1},{6,10},{7,11},{8,4},{9,5},{10,... | collective-permute-start | bytes 393224 | tf_op jit(solution)/shard_map/ppermute | solution.py:437
  28.7 7.3 %collective-permute-start.17 = (bf16[256,256]{1,0:T(8,128)(2,1)S(1)}, bf16[256,256]{1,0:T(8,128)(2,1)S(1)}, u32[]{:S(2)}, u32[]{:S(2)}) collective-permute-start(bf16[256,256]{1,0:T(8,128)(2,1)S(1)} %project.3), channel_id=1, source_target_pairs={{0,8},{1,9},{2,10},{3,11},{4,12},{5,13},{6,14},{7,15},{8,0},{9,1},... | collective-permute-start | bytes 393224 | tf_op jit(solution)/shard_map/ppermute | solution.py:437
  31.5 6.5 %collective-permute-start.16 = (bf16[256,256]{1,0:T(8,128)(2,1)S(1)}, bf16[256,256]{1,0:T(8,128)(2,1)S(1)}, u32[]{:S(2)}, u32[]{:S(2)}) collective-permute-start(bf16[256,256]{1,0:T(8,128)(2,1)S(1)} %project.3), channel_id=1, source_target_pairs={{0,4},{1,5},{2,6},{3,7},{4,8},{5,9},{6,10},{7,11},{8,12},{9,13},{1... | collective-permute-start | bytes 393224 | tf_op jit(solution)/shard_map/ppermute | solution.py:437
  32.8 13.7 %collective-permute-start.22 = (bf16[256,256]{1,0:T(8,128)(2,1)S(1)}, bf16[256,256]{1,0:T(8,128)(2,1)S(1)}, u32[]{:S(2)}, u32[]{:S(2)}) collective-permute-start(bf16[256,256]{1,0:T(8,128)(2,1)S(1)} %project.3), channel_id=1, source_target_pairs={{0,14},{1,15},{2,12},{3,13},{4,2},{5,3},{6,0},{7,1},{8,6},{9,7},{1... | collective-permute-start | bytes 393224 | tf_op jit(solution)/shard_map/ppermute | solution.py:437
  35.3 8.2 %collective-permute-start.19 = (bf16[256,256]{1,0:T(8,128)(2,1)S(1)}, bf16[256,256]{1,0:T(8,128)(2,1)S(1)}, u32[]{:S(2)}, u32[]{:S(2)}) collective-permute-start(bf16[256,256]{1,0:T(8,128)(2,1)S(1)} %project.3), channel_id=1, source_target_pairs={{0,2},{1,3},{2,0},{3,1},{4,6},{5,7},{6,4},{7,5},{8,10},{9,11},{10,... | collective-permute-start | bytes 393224 | tf_op jit(solution)/shard_map/ppermute | solution.py:437
  35.9 7.6 %collective-permute-start.18 = (bf16[256,256]{1,0:T(8,128)(2,1)S(1)}, bf16[256,256]{1,0:T(8,128)(2,1)S(1)}, u32[]{:S(2)}, u32[]{:S(2)}) collective-permute-start(bf16[256,256]{1,0:T(8,128)(2,1)S(1)} %project.3), channel_id=1, source_target_pairs={{0,12},{1,13},{2,14},{3,15},{4,0},{5,1},{6,2},{7,3},{8,4},{9,5},{1... | collective-permute-start | bytes 393224 | tf_op jit(solution)/shard_map/ppermute | solution.py:437
  36.0 10.5 %collective-permute-start.21 = (bf16[256,256]{1,0:T(8,128)(2,1)S(1)}, bf16[256,256]{1,0:T(8,128)(2,1)S(1)}, u32[]{:S(2)}, u32[]{:S(2)}) collective-permute-start(bf16[256,256]{1,0:T(8,128)(2,1)S(1)} %collective-permute-done.17), channel_id=1, source_target_pairs={{0,2},{1,3},{2,0},{3,1},{4,6},{5,7},{6,4},{7,5},{8,10},{9,11},{10,... | collective-permute-start | bytes 393224 | tf_op jit(solution)/shard_map/ppermute | solution.py:437
  38.0 8.5 %collective-permute-start.20 = (bf16[256,256]{1,0:T(8,128)(2,1)S(1)}, bf16[256,256]{1,0:T(8,128)(2,1)S(1)}, u32[]{:S(2)}, u32[]{:S(2)}) collective-permute-start(bf16[256,256]{1,0:T(8,128)(2,1)S(1)} %collective-permute-done.16), channel_id=1, source_target_pairs={{0,2},{1,3},{2,0},{3,1},{4,6},{5,7},{6,4},{7,5},{8,10},{9,11},{10,... | collective-permute-start | bytes 393224 | tf_op jit(solution)/shard_map/ppermute | solution.py:437
  46.5 49.3 %collective-permute-start.23 = (bf16[2048,256]{1,0:T(8,128)(2,1)S(1)}, bf16[2048,256]{1,0:T(8,128)(2,1)S(1)}, u32[]{:S(2)}, u32[]{:S(2)}) collective-permute-start(bf16[2048,256]{1,0:T(8,128)(2,1)S(1)} %constant_dynamic-update-slice_fusion.kv_ref), channel_id=1, source_target_pairs={{0,1},{1,0},{2,3},{3,2},{4,5},{5,4},{6,7},{7,6},{8,9},{9,8},{10,11... | collective-permute-start | bytes 3145736 | tf_op jit(solution)/shard_map/ppermute | solution.py:433

commit v20 on v19

--- a/solution.py
+++ b/solution.py
@@ -439,7 +439,7 @@
     def along_ring(x, step):
         return along(x, lambda line, lane: order[(order.index(2 * line + lane) + step) % chips])
 
-    def line_by_line(block):
+    def line_by_line(block, beside):
         lines = chips // 2
 
         def lane_of(x):
@@ -449,7 +449,8 @@
         far = {0: lane_of(block)}
         far[3] = along(block, lambda line, lane: 2 * ((line + 3) % lines) + 1 - lane)
         far[1], far[2] = lane_of(near[1]), lane_of(near[2])
-        return [block, near[1], near[2], near[3], far[0], far[1], far[2], far[3]]
+        near[3], far[1], beside = lax.optimization_barrier((near[3], far[1], beside))
+        return [block, near[1], near[2], near[3], far[0], far[1], far[2], far[3]], beside
 
     mine, theirs = split(core, kv_weight)
     up = [[mine], [to_partner(theirs)]]
@@ -481,7 +482,9 @@
     up[0].append(along_ring(up[0][-1], 1))
     down[1].append(along_ring(down[1][-1], -1))
     memory_kv = project(chips, core, place, rows, other_rows, blocks((2, 3, 4)), early)
-    near = jnp.concatenate(line_by_line(memory_kv), axis=0)
+    begun = lax.dynamic_slice(question_queries, (0, 0, core * HALF), (1, QLEN, HALF))[0]
+    near_blocks, begun = line_by_line(memory_kv, begun)
+    near = jnp.concatenate(near_blocks, axis=0)
     far = to_partner(near)
 
     lines = chips // 2
@@ -490,7 +493,7 @@
     slot = back + lines * lax.rem(lax.rem(chip, 2) + lax.rem(of_chip, 2), 2)
     starts = (slot * CHIP + lax.rem(retrieval, CHIP)) * MEM
     rest = (starts, question_lengths, question_queries)
-    context, begun = attend(core, *rest, near, question_kv, ahead=True)
+    context, begun = attend(core, *rest, near, question_kv, begun=begun, ahead=True)
     return attend(1 - core, *rest, far, question_kv, context, begun)
 
 

time: 144 us -> 145 us (level)
  local copies, waits for them, and re-layouts: 1.05 us -> 3.06 us
  transfers between devices with their start and end apart: 24 -> 24, of which waited for: 13 -> 11; matrix products, arithmetic and copies ran while one was open for 0% -> 1% of each run, Pallas kernels for 35% -> 34%
where the time goes in v20:
time: 145 us; the launch traced here: 144 us
  Pallas kernels  96.3 us (66%)
  starting transfers between devices  25.2 us (17%)
  waiting for transfers between devices  18.6 us (13%)
  local copies, waits for them, and re-layouts  3.06 us (2%)
    pallas_call x2, Pallas kernels, attend(): pl.pallas_call(functools.partial(attend_kernel, begun is not None, ahead)...  91.3 us
    ppermute x21, starting transfers between devices, along(): lax.ppermute(x, 'pass', [(2 * s + c, 2 * d + c) for s, d in pairs for c i...  20.5 us
    ppermute x21, waiting for transfers between devices, along(): lax.ppermute(x, 'pass', [(2 * s + c, 2 * d + c) for s, d in pairs for c i...  18.6 us
    ppermute x3, starting transfers between devices, to_partner(): return lax.ppermute(x, 'pass', [(i, i ^ 1) for i in range(extent)])  4.74 us
    pallas_call x1, Pallas kernels, pool(): pl.pallas_call(pool_kernel, in_specs=[vmem] * 3, out_specs=vmem, out_shap...  3.08 us
  transfers between devices with their start and end apart: 24, of which 11 were waited for; matrix products, arithmetic and copies ran while one was open for 1% of the time, Pallas kernels for 34%

profile of v20, /device:TPU:1, one launch (start us, length us, event | category | flops | bytes accessed | tf_op | source)
XLA Modules:
  0.0 143.5 jit_solution(1310638417495949538)
XLA Ops:
  0.0 0.9 copy-done.3
  1.0 0.1 collective-permute-start.1
  1.1 2.7 %collective-permute-start.3 = (bf16[256,256]{1,0:T(8,128)(2,1)S(1)}, bf16[256,256]{1,0:T(8,128)(2,1)S(1)}, u32[]{:S(2)}, u32[]{:S(2)}) collective-permute-start(bf16[256,256]{1,0:T(8,128)(2,1)S(1)} %get-tuple-element.19.rest_0_), channel_id=1, source_target_pairs={{0,2},{1,3},{2,6},{3,7},{4,0},{5,1},{6,10},{7,11},{8,4},{9,5},{10,... | collective-permute-start | bytes 393224 | tf_op jit(solution)/shard_map/ppermute | solution.py:437
  3.8 0.1 collective-permute-start
  3.9 0.0 collective-permute-done.1.rest_3_
  3.9 1.4 collective-permute-start.4
  5.3 0.1 collective-permute-start.2
  5.3 0.0 copy-done
  5.4 0.0 copy-done.1
  5.4 0.0 copy-done.2
  5.4 3.1 %pool.1.own_ref = bf16[128,4096]{1,0:T(8,128)(2,1)S(1)} custom-call(bf16[4,128,4096]{2,1,0:T(8,128)(2,1)S(1)} %copy-done, bf16[32,4096]{1,0:T(8,128)(2,1)S(1)} %copy-done.1, bf16[4096]{0:T(1024)(128)(2,1)S(1)} %copy-done.2), custom_call_target="tpu_custom_call" | custom-call | flops 268435456 | bytes 4194304 | tf_op jit(solution)/shard_map/pool/pallas_call | solution.py:116
  8.4 0.0 collective-permute-done.3.rest_2_
  8.5 0.1 collective-permute-done.rest_1_
  8.5 2.0 %collective-permute-done.4.rest_5_ = bf16[256,256]{1,0:T(8,128)(2,1)S(1)} collective-permute-done((bf16[256,256]{1,0:T(8,128)(2,1)S(1)}, bf16[256,256]{1,0:T(8,128)(2,1)S(1)}, u32[]{:S(2)}, u32[]{:S(2)}) %collective-permute-start.4) | collective-permute-done | bytes 131104 | tf_op jit(solution)/shard_map/ppermute | solution.py:437
  10.5 0.9 collective-permute-done.2.rest_4_
  11.3 1.2 collective-permute-start.5
  12.5 0.1 collective-permute-start.6
  12.6 1.4 collective-permute-start.12
  14.0 1.3 collective-permute-start.7
  15.3 0.2 collective-permute-start.11
  15.4 2.2 %collective-permute-done.6.rest_0_ = bf16[256,256]{1,0:T(8,128)(2,1)S(1)} collective-permute-done((bf16[256,256]{1,0:T(8,128)(2,1)S(1)}, bf16[256,256]{1,0:T(8,128)(2,1)S(1)}, u32[]{:S(2)}, u32[]{:S(2)}) %collective-permute-start.6) | collective-permute-done | bytes 131104 | tf_op jit(solution)/shard_map/ppermute | solution.py:437
  17.6 0.1 collective-permute-start.8
  17.7 0.0 collective-permute-done.5.other_ref
  17.7 0.4 project.2.rest_10_
  18.1 0.0 copy-start.7
  18.1 0.0 copy-start.6
  18.1 0.0 collective-permute-done.12.rest_6_
  18.2 1.4 collective-permute-start.14
  19.6 0.7 collective-permute-done.7.rest_1_
  20.3 1.4 collective-permute-start.9
  21.7 0.0 collective-permute-done.11.rest_5_
  21.7 0.1 collective-permute-start.13
  21.8 1.2 collective-permute-done.8.rest_2_
  23.0 0.2 collective-permute-start.10
  23.2 0.0 collective-permute-done.14.rest_8_
  23.2 1.3 collective-permute-start.15
  24.4 1.3 collective-permute-done.9.rest_3_
  25.8 0.3 collective-permute-done.13.rest_7_
  26.0 2.4 %collective-permute-done.10.rest_4_ = bf16[256,256]{1,0:T(8,128)(2,1)S(1)} collective-permute-done((bf16[256,256]{1,0:T(8,128)(2,1)}, bf16[256,256]{1,0:T(8,128)(2,1)S(1)}, u32[]{:S(2)}, u32[]{:S(2)}) %collective-permute-start.10) | collective-permute-done | bytes 131104 | tf_op jit(solution)/shard_map/ppermute | solution.py:437
  28.4 0.0 collective-permute-done.15.rest_9_
  28.4 1.5 %project.3 = bf16[256,256]{1,0:T(8,128)(2,1)S(1)} custom-call(s32[1]{0:T(128)} %bitcast.1.core_ref.half_ref, s32[1]{0:T(128)} %bitcast.2.place_ref, bf16[128,4096]{1,0:T(8,128)(2,1)S(1)} %pool.1.own_ref, bf16[128,4096]{1,0:T(8,128)(2,1)S(1)} %collective-permute-done.5.other_ref, bf16[256,256]{1,0:T(8,128)(2,1)S(1)} %collective-permute-done.6.rest_0_, ...), custom_call_target="tpu_custom_call" | custom-call | flops 134217728 | bytes 33554432 | tf_op jit(solution)/shard_map/project/pallas_call | solution.py:390
  29.9 2.5 %collective-permute-start.17 = (bf16[256,256]{1,0:T(8,128)(2,1)S(1)}, bf16[256,256]{1,0:T(8,128)(2,1)S(1)}, u32[]{:S(2)}, u32[]{:S(2)}) collective-permute-start(bf16[256,256]{1,0:T(8,128)(2,1)S(1)} %project.3), channel_id=1, source_target_pairs={{0,8},{1,9},{2,10},{3,11},{4,12},{5,13},{6,14},{7,15},{8,0},{9,1},... | collective-permute-start | bytes 393224 | tf_op jit(solution)/shard_map/ppermute | solution.py:437
  32.5 1.3 collective-permute-start.16
  33.8 1.1 dynamic-slice_bitcast_fusion.rest_0_
  34.8 2.7 %collective-permute-start.22 = (bf16[256,256]{1,0:T(8,128)(2,1)S(1)}, bf16[256,256]{1,0:T(8,128)(2,1)S(1)}, u32[]{:S(2)}, u32[]{:S(2)}) collective-permute-start(bf16[256,256]{1,0:T(8,128)(2,1)S(1)} %project.3), channel_id=1, source_target_pairs={{0,14},{1,15},{2,12},{3,13},{4,2},{5,3},{6,0},{7,1},{8,6},{9,7},{1... | collective-permute-start | bytes 393224 | tf_op jit(solution)/shard_map/ppermute | solution.py:437
  37.5 0.5 collective-permute-start.20
  38.0 0.0 collective-permute-start.18
  38.0 0.0 collective-permute-done.17
  38.1 1.0 collective-permute-start.21
  39.0 0.0 collective-permute-done.16
  39.0 0.8 collective-permute-start.19
  39.9 5.1 %collective-permute-done.18 = bf16[256,256]{1,0:T(8,128)(2,1)S(1)} collective-permute-done((bf16[256,256]{1,0:T(8,128)(2,1)S(1)}, bf16[256,256]{1,0:T(8,128)(2,1)S(1)}, u32[]{:S(2)}, u32[]{:S(2)}) %collective-permute-start.18) | collective-permute-done | bytes 131104 | tf_op jit(solution)/shard_map/ppermute | solution.py:437
  45.0 2.5 %collective-permute-done.19 = bf16[256,256]{1,0:T(8,128)(2,1)S(1)} collective-permute-done((bf16[256,256]{1,0:T(8,128)(2,1)S(1)}, bf16[256,256]{1,0:T(8,128)(2,1)S(1)}, u32[]{:S(2)}, u32[]{:S(2)}) %collective-permute-start.19) | collective-permute-done | bytes 131104 | tf_op jit(solution)/shard_map/ppermute | solution.py:437
  47.5 0.0 collective-permute-done.20
  47.6 0.0 collective-permute-done.21
  47.6 0.0 collective-permute-done.22
  47.6 3.4 %collective-permute-start.23 = (bf16[2048,256]{1,0:T(8,128)(2,1)S(1)}, bf16[2048,256]{1,0:T(8,128)(2,1)S(1)}, u32[]{:S(2)}, u32[]{:S(2)}) collective-permute-start(bf16[2048,256]{1,0:T(8,128)(2,1)S(1)} %constant_dynamic-update-slice_fusion.kv_ref), channel_id=1, source_target_pairs={{0,1},{1,0},{2,3},{3,2},{4,5},{5,4},{6,7},{7,6},{8,9},{9,8},{10,11... | collective-permute-start | bytes 3145736 | tf_op jit(solution)/shard_map/ppermute | solution.py:433
  51.1 0.0 copy-done.7
  51.1 0.0 copy-done.6
  51.1 0.0 copy-start.4
  51.1 0.9 copy-done.4
  52.0 45.5 %attend.2 = (bf16[4,64,7424]{2,1,0:T(8,128)(2,1)}, bf16[64,3712]{1,0:T(8,128)(2,1)S(1)}) custom-call(s32[1]{0:T(128)} %bitcast.1.core_ref.half_ref, s32[4,16]{1,0:T(4,128)S(1)} %fusion.6.start_ref, s32[4]{0:T(128)S(1)} %copy-done.6, bf16[4,64,7424]{2,1,0:T(8,128)(2,1)} %q_hbm.3, bf16[2048,256]{1,0:T(8,128)(2,1)S(1)} %constant_dynamic-update-slice_fusion.kv_ref, ...), custom_call_target="tpu_custom_call" | custom-call | flops 2189426688 | bytes 3801088 | tf_op jit(solution)/shard_map/attend/pallas_call | solution.py:330
  97.6 0.0 collective-permute-done.23.kv_ref
  97.6 45.7 %attend.3 = bf16[4,64,7424]{2,1,0:T(8,128)(2,1)} custom-call(s32[1]{0:T(128)} %bitcast.half_ref, s32[4,16]{1,0:T(4,128)S(1)} %fusion.6.start_ref, s32[4]{0:T(128)S(1)} %copy-done.6, bf16[4,64,7424]{2,1,0:T(8,128)(2,1)} %q_hbm.3, bf16[2048,256]{1,0:T(8,128)(2,1)S(1)} %collective-permute-done.23.kv_ref, ...), custom_call_target="tpu_custom_call", output_to_operand_aliasing={{}: (7, {})} | custom-call | flops 2189426688 | bytes 3801088 | tf_op jit(solution)/shard_map/attend/pallas_call | solution.py:330
  (16 shorter events, 0.2 us)
Async XLA Ops:
  0.0 0.9 copy-start.3
  1.0 4.4 %copy-start = (bf16[4,128,4096]{2,1,0:T(8,128)(2,1)S(1)}, bf16[4,128,4096]{2,1,0:T(8,128)(2,1)}, u32[]{:S(2)}) copy-start(bf16[4,128,4096]{2,1,0:T(8,128)(2,1)} %states.1) | copy-start | bytes 12582916
  1.0 4.4 %copy-start.1 = (bf16[32,4096]{1,0:T(8,128)(2,1)S(1)}, bf16[32,4096]{1,0:T(8,128)(2,1)}, u32[]{:S(2)}) copy-start(bf16[32,4096]{1,0:T(8,128)(2,1)} %queries.1) | copy-start | bytes 786436
  1.0 4.4 %copy-start.2 = (bf16[4096]{0:T(1024)(128)(2,1)S(1)}, bf16[4096]{0:T(1024)(128)(2,1)}, u32[]{:S(2)}) copy-start(bf16[4096]{0:T(1024)(128)(2,1)} %gain.1) | copy-start | bytes 24580
  1.0 2.9 %collective-permute-start.1 = (bf16[256,256]{1,0:T(8,128)(2,1)S(1)}, bf16[256,256]{1,0:T(8,128)(2,1)S(1)}, u32[]{:S(2)}, u32[]{:S(2)}) collective-permute-start(bf16[256,256]{1,0:T(8,128)(2,1)S(1)} %get-tuple-element.20), channel_id=1, source_target_pairs={{0,1},{1,0},{2,3},{3,2},{4,5},{5,4},{6,7},{7,6},{8,9},{9,8},{10,11... | collective-permute-start | bytes 393224 | tf_op jit(solution)/shard_map/ppermute | solution.py:433
  1.1 7.3 %collective-permute-start.3 = (bf16[256,256]{1,0:T(8,128)(2,1)S(1)}, bf16[256,256]{1,0:T(8,128)(2,1)S(1)}, u32[]{:S(2)}, u32[]{:S(2)}) collective-permute-start(bf16[256,256]{1,0:T(8,128)(2,1)S(1)} %get-tuple-element.19.rest_0_), channel_id=1, source_target_pairs={{0,2},{1,3},{2,6},{3,7},{4,0},{5,1},{6,10},{7,11},{8,4},{9,5},{10,... | collective-permute-start | bytes 393224 | tf_op jit(solution)/shard_map/ppermute | solution.py:437
  3.8 4.7 %collective-permute-start = (bf16[256,256]{1,0:T(8,128)(2,1)S(1)}, bf16[256,256]{1,0:T(8,128)(2,1)S(1)}, u32[]{:S(2)}, u32[]{:S(2)}) collective-permute-start(bf16[256,256]{1,0:T(8,128)(2,1)S(1)} %get-tuple-element.19.rest_0_), channel_id=1, source_target_pairs={{0,4},{1,5},{2,0},{3,1},{4,8},{5,9},{6,2},{7,3},{8,12},{9,13},{10,... | collective-permute-start | bytes 393224 | tf_op jit(solution)/shard_map/ppermute | solution.py:437
  3.9 6.6 %collective-permute-start.4 = (bf16[256,256]{1,0:T(8,128)(2,1)S(1)}, bf16[256,256]{1,0:T(8,128)(2,1)S(1)}, u32[]{:S(2)}, u32[]{:S(2)}) collective-permute-start(bf16[256,256]{1,0:T(8,128)(2,1)S(1)} %collective-permute-done.1.rest_3_), channel_id=1, source_target_pairs={{0,2},{1,3},{2,6},{3,7},{4,0},{5,1},{6,10},{7,11},{8,4},{9,5},{10,... | collective-permute-start | bytes 393224 | tf_op jit(solution)/shard_map/ppermute | solution.py:437
  5.3 6.1 %collective-permute-start.2 = (bf16[256,256]{1,0:T(8,128)(2,1)S(1)}, bf16[256,256]{1,0:T(8,128)(2,1)S(1)}, u32[]{:S(2)}, u32[]{:S(2)}) collective-permute-start(bf16[256,256]{1,0:T(8,128)(2,1)S(1)} %collective-permute-done.1.rest_3_), channel_id=1, source_target_pairs={{0,4},{1,5},{2,0},{3,1},{4,8},{5,9},{6,2},{7,3},{8,12},{9,13},{10,... | collective-permute-start | bytes 393224 | tf_op jit(solution)/shard_map/ppermute | solution.py:437
  11.3 6.4 %collective-permute-start.5 = (bf16[128,4096]{1,0:T(8,128)(2,1)S(1)}, bf16[128,4096]{1,0:T(8,128)(2,1)S(1)}, u32[]{:S(2)}, u32[]{:S(2)}) collective-permute-start(bf16[128,4096]{1,0:T(8,128)(2,1)S(1)} %pool.1.own_ref), channel_id=1, source_target_pairs={{0,1},{1,0},{2,3},{3,2},{4,5},{5,4},{6,7},{7,6},{8,9},{9,8},{10,11... | collective-permute-start | bytes 3145736 | tf_op jit(solution)/shard_map/ppermute | solution.py:433
  12.5 5.1 %collective-permute-start.6 = (bf16[256,256]{1,0:T(8,128)(2,1)S(1)}, bf16[256,256]{1,0:T(8,128)(2,1)S(1)}, u32[]{:S(2)}, u32[]{:S(2)}) collective-permute-start(bf16[256,256]{1,0:T(8,128)(2,1)S(1)} %collective-permute-done.rest_1_), channel_id=1, source_target_pairs={{0,4},{1,5},{2,0},{3,1},{4,8},{5,9},{6,2},{7,3},{8,12},{9,13},{10,... | collective-permute-start | bytes 393224 | tf_op jit(solution)/shard_map/ppermute | solution.py:437
  12.6 5.5 %collective-permute-start.12 = (bf16[256,256]{1,0:T(8,128)(2,1)S(1)}, bf16[256,256]{1,0:T(8,128)(2,1)S(1)}, u32[]{:S(2)}, u32[]{:S(2)}) collective-permute-start(bf16[256,256]{1,0:T(8,128)(2,1)S(1)} %collective-permute-done.4.rest_5_), channel_id=1, source_target_pairs={{0,2},{1,3},{2,6},{3,7},{4,0},{5,1},{6,10},{7,11},{8,4},{9,5},{10,... | collective-permute-start | bytes 393224 | tf_op jit(solution)/shard_map/ppermute | solution.py:437
  14.0 6.3 %collective-permute-start.7 = (bf16[256,256]{1,0:T(8,128)(2,1)S(1)}, bf16[256,256]{1,0:T(8,128)(2,1)S(1)}, u32[]{:S(2)}, u32[]{:S(2)}) collective-permute-start(bf16[256,256]{1,0:T(8,128)(2,1)S(1)} %collective-permute-done.3.rest_2_), channel_id=1, source_target_pairs={{0,2},{1,3},{2,6},{3,7},{4,0},{5,1},{6,10},{7,11},{8,4},{9,5},{10,... | collective-permute-start | bytes 393224 | tf_op jit(solution)/shard_map/ppermute | solution.py:437
  15.3 6.4 %collective-permute-start.11 = (bf16[256,256]{1,0:T(8,128)(2,1)S(1)}, bf16[256,256]{1,0:T(8,128)(2,1)}, u32[]{:S(2)}, u32[]{:S(2)}) collective-permute-start(bf16[256,256]{1,0:T(8,128)(2,1)S(1)} %collective-permute-done.2.rest_4_), channel_id=1, source_target_pairs={{0,4},{1,5},{2,0},{3,1},{4,8},{5,9},{6,2},{7,3},{8,12},{9,13},{10,... | collective-permute-start | bytes 393224 | tf_op jit(solution)/shard_map/ppermute | solution.py:437
  17.6 5.3 %collective-permute-start.8 = (bf16[256,256]{1,0:T(8,128)(2,1)S(1)}, bf16[256,256]{1,0:T(8,128)(2,1)}, u32[]{:S(2)}, u32[]{:S(2)}) collective-permute-start(bf16[256,256]{1,0:T(8,128)(2,1)S(1)} %collective-permute-done.6.rest_0_), channel_id=1, source_target_pairs={{0,4},{1,5},{2,0},{3,1},{4,8},{5,9},{6,2},{7,3},{8,12},{9,13},{10,... | collective-permute-start | bytes 393224 | tf_op jit(solution)/shard_map/ppermute | solution.py:437
  18.1 32.9 %copy-start.7 = (s32[4,16]{1,0:T(4,128)S(1)}, s32[4,16]{1,0:T(4,128)}, u32[]{:S(2)}) copy-start(s32[4,16]{1,0:T(4,128)} %param.12) | copy-start | bytes 772
  18.1 33.0 %copy-start.6 = (s32[4]{0:T(128)S(1)}, s32[4]{0:T(128)}, u32[]{:S(2)}) copy-start(s32[4]{0:T(128)} %length_ref.3) | copy-start | bytes 52
  18.2 5.0 %collective-permute-start.14 = (bf16[256,256]{1,0:T(8,128)(2,1)S(1)}, bf16[256,256]{1,0:T(8,128)(2,1)S(1)}, u32[]{:S(2)}, u32[]{:S(2)}) collective-permute-start(bf16[256,256]{1,0:T(8,128)(2,1)S(1)} %collective-permute-done.12.rest_6_), channel_id=1, source_target_pairs={{0,2},{1,3},{2,6},{3,7},{4,0},{5,1},{6,10},{7,11},{8,4},{9,5},{10,... | collective-permute-start | bytes 393224 | tf_op jit(solution)/shard_map/ppermute | solution.py:437
  20.3 5.4 %collective-permute-start.9 = (bf16[256,256]{1,0:T(8,128)(2,1)S(1)}, bf16[256,256]{1,0:T(8,128)(2,1)S(1)}, u32[]{:S(2)}, u32[]{:S(2)}) collective-permute-start(bf16[256,256]{1,0:T(8,128)(2,1)S(1)} %collective-permute-done.7.rest_1_), channel_id=1, source_target_pairs={{0,2},{1,3},{2,6},{3,7},{4,0},{5,1},{6,10},{7,11},{8,4},{9,5},{10,... | collective-permute-start | bytes 393224 | tf_op jit(solution)/shard_map/ppermute | solution.py:437
  21.7 4.3 %collective-permute-start.13 = (bf16[256,256]{1,0:T(8,128)(2,1)}, bf16[256,256]{1,0:T(8,128)(2,1)S(1)}, u32[]{:S(2)}, u32[]{:S(2)}) collective-permute-start(bf16[256,256]{1,0:T(8,128)(2,1)} %collective-permute-done.11.rest_5_), channel_id=1, source_target_pairs={{0,4},{1,5},{2,0},{3,1},{4,8},{5,9},{6,2},{7,3},{8,12},{9,13},{10,... | collective-permute-start | bytes 393224 | tf_op jit(solution)/shard_map/ppermute | solution.py:437
  23.0 5.5 %collective-permute-start.10 = (bf16[256,256]{1,0:T(8,128)(2,1)}, bf16[256,256]{1,0:T(8,128)(2,1)S(1)}, u32[]{:S(2)}, u32[]{:S(2)}) collective-permute-start(bf16[256,256]{1,0:T(8,128)(2,1)} %collective-permute-done.8.rest_2_), channel_id=1, source_target_pairs={{0,4},{1,5},{2,0},{3,1},{4,8},{5,9},{6,2},{7,3},{8,12},{9,13},{10,... | collective-permute-start | bytes 393224 | tf_op jit(solution)/shard_map/ppermute | solution.py:437
  23.2 5.3 %collective-permute-start.15 = (bf16[256,256]{1,0:T(8,128)(2,1)S(1)}, bf16[256,256]{1,0:T(8,128)(2,1)S(1)}, u32[]{:S(2)}, u32[]{:S(2)}) collective-permute-start(bf16[256,256]{1,0:T(8,128)(2,1)S(1)} %collective-permute-done.14.rest_8_), channel_id=1, source_target_pairs={{0,2},{1,3},{2,6},{3,7},{4,0},{5,1},{6,10},{7,11},{8,4},{9,5},{10,... | collective-permute-start | bytes 393224 | tf_op jit(solution)/shard_map/ppermute | solution.py:437
  29.9 8.1 %collective-permute-start.17 = (bf16[256,256]{1,0:T(8,128)(2,1)S(1)}, bf16[256,256]{1,0:T(8,128)(2,1)S(1)}, u32[]{:S(2)}, u32[]{:S(2)}) collective-permute-start(bf16[256,256]{1,0:T(8,128)(2,1)S(1)} %project.3), channel_id=1, source_target_pairs={{0,8},{1,9},{2,10},{3,11},{4,12},{5,13},{6,14},{7,15},{8,0},{9,1},... | collective-permute-start | bytes 393224 | tf_op jit(solution)/shard_map/ppermute | solution.py:437
  32.5 6.6 %collective-permute-start.16 = (bf16[256,256]{1,0:T(8,128)(2,1)S(1)}, bf16[256,256]{1,0:T(8,128)(2,1)S(1)}, u32[]{:S(2)}, u32[]{:S(2)}) collective-permute-start(bf16[256,256]{1,0:T(8,128)(2,1)S(1)} %project.3), channel_id=1, source_target_pairs={{0,4},{1,5},{2,6},{3,7},{4,8},{5,9},{6,10},{7,11},{8,12},{9,13},{1... | collective-permute-start | bytes 393224 | tf_op jit(solution)/shard_map/ppermute | solution.py:437
  34.8 12.8 %collective-permute-start.22 = (bf16[256,256]{1,0:T(8,128)(2,1)S(1)}, bf16[256,256]{1,0:T(8,128)(2,1)S(1)}, u32[]{:S(2)}, u32[]{:S(2)}) collective-permute-start(bf16[256,256]{1,0:T(8,128)(2,1)S(1)} %project.3), channel_id=1, source_target_pairs={{0,14},{1,15},{2,12},{3,13},{4,2},{5,3},{6,0},{7,1},{8,6},{9,7},{1... | collective-permute-start | bytes 393224 | tf_op jit(solution)/shard_map/ppermute | solution.py:437
  37.5 10.0 %collective-permute-start.20 = (bf16[256,256]{1,0:T(8,128)(2,1)S(1)}, bf16[256,256]{1,0:T(8,128)(2,1)S(1)}, u32[]{:S(2)}, u32[]{:S(2)}) collective-permute-start(bf16[256,256]{1,0:T(8,128)(2,1)S(1)} %project.3), channel_id=1, source_target_pairs={{0,2},{1,3},{2,0},{3,1},{4,6},{5,7},{6,4},{7,5},{8,10},{9,11},{10,... | collective-permute-start | bytes 393224 | tf_op jit(solution)/shard_map/ppermute | solution.py:437
  38.0 7.0 %collective-permute-start.18 = (bf16[256,256]{1,0:T(8,128)(2,1)S(1)}, bf16[256,256]{1,0:T(8,128)(2,1)S(1)}, u32[]{:S(2)}, u32[]{:S(2)}) collective-permute-start(bf16[256,256]{1,0:T(8,128)(2,1)S(1)} %project.3), channel_id=1, source_target_pairs={{0,12},{1,13},{2,14},{3,15},{4,0},{5,1},{6,2},{7,3},{8,4},{9,5},{1... | collective-permute-start | bytes 393224 | tf_op jit(solution)/shard_map/ppermute | solution.py:437
  38.1 9.5 %collective-permute-start.21 = (bf16[256,256]{1,0:T(8,128)(2,1)S(1)}, bf16[256,256]{1,0:T(8,128)(2,1)S(1)}, u32[]{:S(2)}, u32[]{:S(2)}) collective-permute-start(bf16[256,256]{1,0:T(8,128)(2,1)S(1)} %collective-permute-done.17), channel_id=1, source_target_pairs={{0,2},{1,3},{2,0},{3,1},{4,6},{5,7},{6,4},{7,5},{8,10},{9,11},{10,... | collective-permute-start | bytes 393224 | tf_op jit(solution)/shard_map/ppermute | solution.py:437
  39.0 8.5 %collective-permute-start.19 = (bf16[256,256]{1,0:T(8,128)(2,1)S(1)}, bf16[256,256]{1,0:T(8,128)(2,1)S(1)}, u32[]{:S(2)}, u32[]{:S(2)}) collective-permute-start(bf16[256,256]{1,0:T(8,128)(2,1)S(1)} %collective-permute-done.16), channel_id=1, source_target_pairs={{0,2},{1,3},{2,0},{3,1},{4,6},{5,7},{6,4},{7,5},{8,10},{9,11},{10,... | collective-permute-start | bytes 393224 | tf_op jit(solution)/shard_map/ppermute | solution.py:437
  47.6 50.0 %collective-permute-start.23 = (bf16[2048,256]{1,0:T(8,128)(2,1)S(1)}, bf16[2048,256]{1,0:T(8,128)(2,1)S(1)}, u32[]{:S(2)}, u32[]{:S(2)}) collective-permute-start(bf16[2048,256]{1,0:T(8,128)(2,1)S(1)} %constant_dynamic-update-slice_fusion.kv_ref), channel_id=1, source_target_pairs={{0,1},{1,0},{2,3},{3,2},{4,5},{5,4},{6,7},{7,6},{8,9},{9,8},{10,11... | collective-permute-start | bytes 3145736 | tf_op jit(solution)/shard_map/ppermute | solution.py:433
  51.1 1.0 copy-start.4
  52.0 45.5 %copy-start.5 = (bf16[4,64,512]{2,1,0:T(8,128)(2,1)S(1)}, bf16[4,64,512]{2,1,0:T(8,128)(2,1)}, u32[]{:S(2)}) copy-start(bf16[4,64,512]{2,1,0:T(8,128)(2,1)} %own_kv_ref.3) | copy-start | bytes 786436

commit v21 on v19

--- a/solution.py
+++ b/solution.py
@@ -447,8 +447,8 @@
 
         near = {k: along(block, lambda line, lane: 2 * ((line + k) % lines) + lane) for k in (2, 1, 3)}
         far = {0: lane_of(block)}
-        far[3] = along(block, lambda line, lane: 2 * ((line + 3) % lines) + 1 - lane)
-        far[1], far[2] = lane_of(near[1]), lane_of(near[2])
+        far[2] = along(block, lambda line, lane: 2 * ((line + 2) % lines) + 1 - lane)
+        far[1], far[3] = lane_of(near[1]), lane_of(near[3])
         return [block, near[1], near[2], near[3], far[0], far[1], far[2], far[3]]
 
     mine, theirs = split(core, kv_weight)

time: 144 us -> 144 us (level); the launches traced: 142 us -> 144 us
  waiting for transfers between devices: 19.5 us -> 22.7 us
    ppermute x21, waiting for transfers between devices: 19.5 us -> 22.7 us  [along(): lax.ppermute(x, 'pass', [(2 * s + c, 2 * d + c) for s, d in pairs for c i...]
  transfers between devices with their start and end apart: 24 -> 24, of which waited for: 13 -> 12; matrix products, arithmetic and copies ran while one was open for 0% -> 0% of each run, Pallas kernels for 35% -> 35%
where the time goes in v21:
time: 144 us
  Pallas kernels  96.2 us (67%)
  starting transfers between devices  23.9 us (17%)
  waiting for transfers between devices  22.7 us (16%)
    pallas_call x2, Pallas kernels, attend(): pl.pallas_call(functools.partial(attend_kernel, begun is not None, ahead)...  92.1 us
    ppermute x21, waiting for transfers between devices, along(): lax.ppermute(x, 'pass', [(2 * s + c, 2 * d + c) for s, d in pairs for c i...  22.7 us
    ppermute x21, starting transfers between devices, along(): lax.ppermute(x, 'pass', [(2 * s + c, 2 * d + c) for s, d in pairs for c i...  20.9 us
    pallas_call x1, Pallas kernels, pool(): pl.pallas_call(pool_kernel, in_specs=[vmem] * 3, out_specs=vmem, out_shap...  3.08 us
    ppermute x3, starting transfers between devices, to_partner(): return lax.ppermute(x, 'pass', [(i, i ^ 1) for i in range(extent)])  2.94 us
  transfers between devices with their start and end apart: 24, of which 12 were waited for; matrix products, arithmetic and copies ran while one was open for 0% of the time, Pallas kernels for 35%

profile of v21, /device:TPU:1, one launch (start us, length us, event | category | flops | bytes accessed | tf_op | source)
XLA Modules:
  0.0 144.2 jit_solution(8314538791340421730)
XLA Ops:
  0.0 0.0 copy-start.3
  0.0 0.9 copy-done.3
  1.0 0.0 copy-start
  1.0 0.0 copy-start.1
  1.0 0.0 copy-start.2
  1.0 0.1 collective-permute-start.1
  1.1 2.7 %collective-permute-start.3 = (bf16[256,256]{1,0:T(8,128)(2,1)S(1)}, bf16[256,256]{1,0:T(8,128)(2,1)S(1)}, u32[]{:S(2)}, u32[]{:S(2)}) collective-permute-start(bf16[256,256]{1,0:T(8,128)(2,1)S(1)} %get-tuple-element.16.rest_0_), channel_id=1, source_target_pairs={{0,2},{1,3},{2,6},{3,7},{4,0},{5,1},{6,10},{7,11},{8,4},{9,5},{10,... | collective-permute-start | bytes 393224 | tf_op jit(solution)/shard_map/ppermute | solution.py:437
  3.8 0.1 collective-permute-start
  3.9 0.0 collective-permute-done.1.rest_3_
  3.9 1.4 collective-permute-start.4
  5.3 0.1 collective-permute-start.2
  5.3 0.0 copy-done
  5.4 0.0 copy-done.1
  5.4 0.0 copy-done.2
  5.4 3.1 %pool.1.own_ref = bf16[128,4096]{1,0:T(8,128)(2,1)S(1)} custom-call(bf16[4,128,4096]{2,1,0:T(8,128)(2,1)S(1)} %copy-done, bf16[32,4096]{1,0:T(8,128)(2,1)S(1)} %copy-done.1, bf16[4096]{0:T(1024)(128)(2,1)S(1)} %copy-done.2), custom_call_target="tpu_custom_call" | custom-call | flops 268435456 | bytes 4194304 | tf_op jit(solution)/shard_map/pool/pallas_call | solution.py:116
  8.4 0.0 collective-permute-done.3.rest_2_
  8.5 0.1 collective-permute-done.rest_1_
  8.5 2.0 %collective-permute-done.4.rest_5_ = bf16[256,256]{1,0:T(8,128)(2,1)S(1)} collective-permute-done((bf16[256,256]{1,0:T(8,128)(2,1)S(1)}, bf16[256,256]{1,0:T(8,128)(2,1)S(1)}, u32[]{:S(2)}, u32[]{:S(2)}) %collective-permute-start.4) | collective-permute-done | bytes 131104 | tf_op jit(solution)/shard_map/ppermute | solution.py:437
  10.5 0.9 collective-permute-done.2.rest_4_
  11.3 1.2 collective-permute-start.5
  12.5 0.1 collective-permute-start.6
  12.6 1.4 collective-permute-start.12
  14.0 1.3 collective-permute-start.7
  15.3 0.2 collective-permute-start.11
  15.4 2.2 %collective-permute-done.6.rest_0_ = bf16[256,256]{1,0:T(8,128)(2,1)S(1)} collective-permute-done((bf16[256,256]{1,0:T(8,128)(2,1)S(1)}, bf16[256,256]{1,0:T(8,128)(2,1)S(1)}, u32[]{:S(2)}, u32[]{:S(2)}) %collective-permute-start.6) | collective-permute-done | bytes 131104 | tf_op jit(solution)/shard_map/ppermute | solution.py:437
  17.6 0.1 collective-permute-start.8
  17.7 0.0 collective-permute-done.5.other_ref
  17.7 0.4 project.2.rest_10_
  18.1 0.0 collective-permute-done.12.rest_6_
  18.1 1.4 collective-permute-start.14
  19.6 0.6 collective-permute-done.7.rest_1_
  20.2 1.4 collective-permute-start.9
  21.6 0.0 collective-permute-done.11.rest_5_
  21.6 0.1 collective-permute-start.13
  21.7 1.2 collective-permute-done.8.rest_2_
  22.9 0.3 collective-permute-start.10
  23.2 0.0 collective-permute-done.14.rest_8_
  23.2 1.2 collective-permute-start.15
  24.3 1.3 collective-permute-done.9.rest_3_
  25.6 0.1 collective-permute-done.13.rest_7_
  25.7 2.3 %collective-permute-done.10.rest_4_ = bf16[256,256]{1,0:T(8,128)(2,1)S(1)} collective-permute-done((bf16[256,256]{1,0:T(8,128)(2,1)S(1)}, bf16[256,256]{1,0:T(8,128)(2,1)S(1)}, u32[]{:S(2)}, u32[]{:S(2)}) %collective-permute-start.10) | collective-permute-done | bytes 131104 | tf_op jit(solution)/shard_map/ppermute | solution.py:437
  28.0 0.1 collective-permute-done.15.rest_9_
  28.1 0.5 project.3
  28.7 3.8 %collective-permute-start.18 = (bf16[256,256]{1,0:T(8,128)(2,1)S(1)}, bf16[256,256]{1,0:T(8,128)(2,1)S(1)}, u32[]{:S(2)}, u32[]{:S(2)}) collective-permute-start(bf16[256,256]{1,0:T(8,128)(2,1)S(1)} %project.3), channel_id=1, source_target_pairs={{0,12},{1,13},{2,14},{3,15},{4,0},{5,1},{6,2},{7,3},{8,4},{9,5},{1... | collective-permute-start | bytes 393224 | tf_op jit(solution)/shard_map/ppermute | solution.py:437
  32.5 0.0 collective-permute-start.16
  32.5 1.5 %collective-permute-start.21 = (bf16[256,256]{1,0:T(8,128)(2,1)S(1)}, bf16[256,256]{1,0:T(8,128)(2,1)S(1)}, u32[]{:S(2)}, u32[]{:S(2)}) collective-permute-start(bf16[256,256]{1,0:T(8,128)(2,1)S(1)} %project.3), channel_id=1, source_target_pairs={{0,10},{1,11},{2,8},{3,9},{4,14},{5,15},{6,12},{7,13},{8,2},{9,3},... | collective-permute-start | bytes 393224 | tf_op jit(solution)/shard_map/ppermute | solution.py:437
  34.0 0.2 collective-permute-start.19
  34.2 1.8 %collective-permute-start.17 = (bf16[256,256]{1,0:T(8,128)(2,1)S(1)}, bf16[256,256]{1,0:T(8,128)(2,1)S(1)}, u32[]{:S(2)}, u32[]{:S(2)}) collective-permute-start(bf16[256,256]{1,0:T(8,128)(2,1)S(1)} %project.3), channel_id=1, source_target_pairs={{0,8},{1,9},{2,10},{3,11},{4,12},{5,13},{6,14},{7,15},{8,0},{9,1},... | collective-permute-start | bytes 393224 | tf_op jit(solution)/shard_map/ppermute | solution.py:437
  36.1 0.0 collective-permute-done.18
  36.1 1.3 collective-permute-start.22
  37.3 2.1 %collective-permute-done.16 = bf16[256,256]{1,0:T(8,128)(2,1)S(1)} collective-permute-done((bf16[256,256]{1,0:T(8,128)(2,1)S(1)}, bf16[256,256]{1,0:T(8,128)(2,1)S(1)}, u32[]{:S(2)}, u32[]{:S(2)}) %collective-permute-start.16) | collective-permute-done | bytes 131104 | tf_op jit(solution)/shard_map/ppermute | solution.py:437
  39.4 0.7 collective-permute-start.20
  40.1 9.9 %collective-permute-done.17 = bf16[256,256]{1,0:T(8,128)(2,1)S(1)} collective-permute-done((bf16[256,256]{1,0:T(8,128)(2,1)S(1)}, bf16[256,256]{1,0:T(8,128)(2,1)S(1)}, u32[]{:S(2)}, u32[]{:S(2)}) %collective-permute-start.17) | collective-permute-done | bytes 131104 | tf_op jit(solution)/shard_map/ppermute | solution.py:437
  50.1 0.0 collective-permute-done.19
  50.1 0.0 collective-permute-done.20
  50.1 0.0 collective-permute-done.21
  50.2 0.0 collective-permute-done.22
  50.2 1.6 %collective-permute-start.23 = (bf16[2048,256]{1,0:T(8,128)(2,1)S(1)}, bf16[2048,256]{1,0:T(8,128)(2,1)S(1)}, u32[]{:S(2)}, u32[]{:S(2)}) collective-permute-start(bf16[2048,256]{1,0:T(8,128)(2,1)S(1)} %constant_dynamic-update-slice_fusion.kv_ref), channel_id=1, source_target_pairs={{0,1},{1,0},{2,3},{3,2},{4,5},{5,4},{6,7},{7,6},{8,9},{9,8},{10,11... | collective-permute-start | bytes 3145736 | tf_op jit(solution)/shard_map/ppermute | solution.py:433
  51.8 0.0 copy-done.6
  51.9 0.0 copy-done.4
  51.9 0.0 copy-done.5
  51.9 46.4 %attend.2 = (bf16[4,64,7424]{2,1,0:T(8,128)(2,1)}, bf16[64,3712]{1,0:T(8,128)(2,1)S(1)}) custom-call(s32[1]{0:T(128)} %bitcast.1.core_ref.half_ref, s32[4,16]{1,0:T(4,128)S(1)} %fusion.6.start_ref, s32[4]{0:T(128)S(1)} %copy-done.5, bf16[4,64,7424]{2,1,0:T(8,128)(2,1)} %q_hbm.3, bf16[2048,256]{1,0:T(8,128)(2,1)S(1)} %constant_dynamic-update-slice_fusion.kv_ref, ...), custom_call_target="tpu_custom_call" | custom-call | flops 2189426688 | bytes 3801088 | tf_op jit(solution)/shard_map/attend/pallas_call | solution.py:330
  98.3 0.0 collective-permute-done.23.kv_ref
  98.3 45.8 %attend.3 = bf16[4,64,7424]{2,1,0:T(8,128)(2,1)} custom-call(s32[1]{0:T(128)} %bitcast.half_ref, s32[4,16]{1,0:T(4,128)S(1)} %fusion.6.start_ref, s32[4]{0:T(128)S(1)} %copy-done.5, bf16[4,64,7424]{2,1,0:T(8,128)(2,1)} %q_hbm.3, bf16[2048,256]{1,0:T(8,128)(2,1)S(1)} %collective-permute-done.23.kv_ref, ...), custom_call_target="tpu_custom_call", output_to_operand_aliasing={{}: (7, {})} | custom-call | flops 2189426688 | bytes 3801088 | tf_op jit(solution)/shard_map/attend/pallas_call | solution.py:330
  (13 shorter events, 0.2 us)
Async XLA Ops:
  0.0 0.9 copy-start.3
  1.0 4.4 %copy-start = (bf16[4,128,4096]{2,1,0:T(8,128)(2,1)S(1)}, bf16[4,128,4096]{2,1,0:T(8,128)(2,1)}, u32[]{:S(2)}) copy-start(bf16[4,128,4096]{2,1,0:T(8,128)(2,1)} %states.1) | copy-start | bytes 12582916
  1.0 4.4 %copy-start.1 = (bf16[32,4096]{1,0:T(8,128)(2,1)S(1)}, bf16[32,4096]{1,0:T(8,128)(2,1)}, u32[]{:S(2)}) copy-start(bf16[32,4096]{1,0:T(8,128)(2,1)} %queries.1) | copy-start | bytes 786436
  1.0 4.4 %copy-start.2 = (bf16[4096]{0:T(1024)(128)(2,1)S(1)}, bf16[4096]{0:T(1024)(128)(2,1)}, u32[]{:S(2)}) copy-start(bf16[4096]{0:T(1024)(128)(2,1)} %gain.1) | copy-start | bytes 24580
  1.0 2.9 %collective-permute-start.1 = (bf16[256,256]{1,0:T(8,128)(2,1)S(1)}, bf16[256,256]{1,0:T(8,128)(2,1)S(1)}, u32[]{:S(2)}, u32[]{:S(2)}) collective-permute-start(bf16[256,256]{1,0:T(8,128)(2,1)S(1)} %get-tuple-element.17), channel_id=1, source_target_pairs={{0,1},{1,0},{2,3},{3,2},{4,5},{5,4},{6,7},{7,6},{8,9},{9,8},{10,11... | collective-permute-start | bytes 393224 | tf_op jit(solution)/shard_map/ppermute | solution.py:433
  1.1 7.3 %collective-permute-start.3 = (bf16[256,256]{1,0:T(8,128)(2,1)S(1)}, bf16[256,256]{1,0:T(8,128)(2,1)S(1)}, u32[]{:S(2)}, u32[]{:S(2)}) collective-permute-start(bf16[256,256]{1,0:T(8,128)(2,1)S(1)} %get-tuple-element.16.rest_0_), channel_id=1, source_target_pairs={{0,2},{1,3},{2,6},{3,7},{4,0},{5,1},{6,10},{7,11},{8,4},{9,5},{10,... | collective-permute-start | bytes 393224 | tf_op jit(solution)/shard_map/ppermute | solution.py:437
  3.8 4.7 %collective-permute-start = (bf16[256,256]{1,0:T(8,128)(2,1)S(1)}, bf16[256,256]{1,0:T(8,128)(2,1)S(1)}, u32[]{:S(2)}, u32[]{:S(2)}) collective-permute-start(bf16[256,256]{1,0:T(8,128)(2,1)S(1)} %get-tuple-element.16.rest_0_), channel_id=1, source_target_pairs={{0,4},{1,5},{2,0},{3,1},{4,8},{5,9},{6,2},{7,3},{8,12},{9,13},{10,... | collective-permute-start | bytes 393224 | tf_op jit(solution)/shard_map/ppermute | solution.py:437
  3.9 6.6 %collective-permute-start.4 = (bf16[256,256]{1,0:T(8,128)(2,1)S(1)}, bf16[256,256]{1,0:T(8,128)(2,1)S(1)}, u32[]{:S(2)}, u32[]{:S(2)}) collective-permute-start(bf16[256,256]{1,0:T(8,128)(2,1)S(1)} %collective-permute-done.1.rest_3_), channel_id=1, source_target_pairs={{0,2},{1,3},{2,6},{3,7},{4,0},{5,1},{6,10},{7,11},{8,4},{9,5},{10,... | collective-permute-start | bytes 393224 | tf_op jit(solution)/shard_map/ppermute | solution.py:437
  5.3 6.1 %collective-permute-start.2 = (bf16[256,256]{1,0:T(8,128)(2,1)S(1)}, bf16[256,256]{1,0:T(8,128)(2,1)S(1)}, u32[]{:S(2)}, u32[]{:S(2)}) collective-permute-start(bf16[256,256]{1,0:T(8,128)(2,1)S(1)} %collective-permute-done.1.rest_3_), channel_id=1, source_target_pairs={{0,4},{1,5},{2,0},{3,1},{4,8},{5,9},{6,2},{7,3},{8,12},{9,13},{10,... | collective-permute-start | bytes 393224 | tf_op jit(solution)/shard_map/ppermute | solution.py:437
  11.3 6.4 %collective-permute-start.5 = (bf16[128,4096]{1,0:T(8,128)(2,1)S(1)}, bf16[128,4096]{1,0:T(8,128)(2,1)S(1)}, u32[]{:S(2)}, u32[]{:S(2)}) collective-permute-start(bf16[128,4096]{1,0:T(8,128)(2,1)S(1)} %pool.1.own_ref), channel_id=1, source_target_pairs={{0,1},{1,0},{2,3},{3,2},{4,5},{5,4},{6,7},{7,6},{8,9},{9,8},{10,11... | collective-permute-start | bytes 3145736 | tf_op jit(solution)/shard_map/ppermute | solution.py:433
  12.5 5.1 %collective-permute-start.6 = (bf16[256,256]{1,0:T(8,128)(2,1)S(1)}, bf16[256,256]{1,0:T(8,128)(2,1)S(1)}, u32[]{:S(2)}, u32[]{:S(2)}) collective-permute-start(bf16[256,256]{1,0:T(8,128)(2,1)S(1)} %collective-permute-done.rest_1_), channel_id=1, source_target_pairs={{0,4},{1,5},{2,0},{3,1},{4,8},{5,9},{6,2},{7,3},{8,12},{9,13},{10,... | collective-permute-start | bytes 393224 | tf_op jit(solution)/shard_map/ppermute | solution.py:437
  12.6 5.5 %collective-permute-start.12 = (bf16[256,256]{1,0:T(8,128)(2,1)S(1)}, bf16[256,256]{1,0:T(8,128)(2,1)S(1)}, u32[]{:S(2)}, u32[]{:S(2)}) collective-permute-start(bf16[256,256]{1,0:T(8,128)(2,1)S(1)} %collective-permute-done.4.rest_5_), channel_id=1, source_target_pairs={{0,2},{1,3},{2,6},{3,7},{4,0},{5,1},{6,10},{7,11},{8,4},{9,5},{10,... | collective-permute-start | bytes 393224 | tf_op jit(solution)/shard_map/ppermute | solution.py:437
  14.0 6.2 %collective-permute-start.7 = (bf16[256,256]{1,0:T(8,128)(2,1)S(1)}, bf16[256,256]{1,0:T(8,128)(2,1)S(1)}, u32[]{:S(2)}, u32[]{:S(2)}) collective-permute-start(bf16[256,256]{1,0:T(8,128)(2,1)S(1)} %collective-permute-done.3.rest_2_), channel_id=1, source_target_pairs={{0,2},{1,3},{2,6},{3,7},{4,0},{5,1},{6,10},{7,11},{8,4},{9,5},{10,... | collective-permute-start | bytes 393224 | tf_op jit(solution)/shard_map/ppermute | solution.py:437
  15.3 6.3 %collective-permute-start.11 = (bf16[256,256]{1,0:T(8,128)(2,1)S(1)}, bf16[256,256]{1,0:T(8,128)(2,1)S(1)}, u32[]{:S(2)}, u32[]{:S(2)}) collective-permute-start(bf16[256,256]{1,0:T(8,128)(2,1)S(1)} %collective-permute-done.2.rest_4_), channel_id=1, source_target_pairs={{0,4},{1,5},{2,0},{3,1},{4,8},{5,9},{6,2},{7,3},{8,12},{9,13},{10,... | collective-permute-start | bytes 393224 | tf_op jit(solution)/shard_map/ppermute | solution.py:437
  17.6 5.2 %collective-permute-start.8 = (bf16[256,256]{1,0:T(8,128)(2,1)S(1)}, bf16[256,256]{1,0:T(8,128)(2,1)S(1)}, u32[]{:S(2)}, u32[]{:S(2)}) collective-permute-start(bf16[256,256]{1,0:T(8,128)(2,1)S(1)} %collective-permute-done.6.rest_0_), channel_id=1, source_target_pairs={{0,4},{1,5},{2,0},{3,1},{4,8},{5,9},{6,2},{7,3},{8,12},{9,13},{10,... | collective-permute-start | bytes 393224 | tf_op jit(solution)/shard_map/ppermute | solution.py:437
  17.7 34.1 %copy-start.6 = (s32[4,16]{1,0:T(4,128)S(1)}, s32[4,16]{1,0:T(4,128)}, u32[]{:S(2)}) copy-start(s32[4,16]{1,0:T(4,128)} %param.12) | copy-start | bytes 772
  17.7 34.1 %copy-start.4 = (bf16[4,64,512]{2,1,0:T(8,128)(2,1)S(1)}, bf16[4,64,512]{2,1,0:T(8,128)(2,1)}, u32[]{:S(2)}) copy-start(bf16[4,64,512]{2,1,0:T(8,128)(2,1)} %own_kv_ref.3) | copy-start | bytes 786436
  17.7 34.1 %copy-start.5 = (s32[4]{0:T(128)S(1)}, s32[4]{0:T(128)}, u32[]{:S(2)}) copy-start(s32[4]{0:T(128)} %length_ref.3) | copy-start | bytes 52
  18.1 5.0 %collective-permute-start.14 = (bf16[256,256]{1,0:T(8,128)(2,1)S(1)}, bf16[256,256]{1,0:T(8,128)(2,1)S(1)}, u32[]{:S(2)}, u32[]{:S(2)}) collective-permute-start(bf16[256,256]{1,0:T(8,128)(2,1)S(1)} %collective-permute-done.12.rest_6_), channel_id=1, source_target_pairs={{0,2},{1,3},{2,6},{3,7},{4,0},{5,1},{6,10},{7,11},{8,4},{9,5},{10,... | collective-permute-start | bytes 393224 | tf_op jit(solution)/shard_map/ppermute | solution.py:437
  20.2 5.4 %collective-permute-start.9 = (bf16[256,256]{1,0:T(8,128)(2,1)S(1)}, bf16[256,256]{1,0:T(8,128)(2,1)S(1)}, u32[]{:S(2)}, u32[]{:S(2)}) collective-permute-start(bf16[256,256]{1,0:T(8,128)(2,1)S(1)} %collective-permute-done.7.rest_1_), channel_id=1, source_target_pairs={{0,2},{1,3},{2,6},{3,7},{4,0},{5,1},{6,10},{7,11},{8,4},{9,5},{10,... | collective-permute-start | bytes 393224 | tf_op jit(solution)/shard_map/ppermute | solution.py:437
  21.6 4.1 %collective-permute-start.13 = (bf16[256,256]{1,0:T(8,128)(2,1)S(1)}, bf16[256,256]{1,0:T(8,128)(2,1)S(1)}, u32[]{:S(2)}, u32[]{:S(2)}) collective-permute-start(bf16[256,256]{1,0:T(8,128)(2,1)S(1)} %collective-permute-done.11.rest_5_), channel_id=1, source_target_pairs={{0,4},{1,5},{2,0},{3,1},{4,8},{5,9},{6,2},{7,3},{8,12},{9,13},{10,... | collective-permute-start | bytes 393224 | tf_op jit(solution)/shard_map/ppermute | solution.py:437
  22.9 5.1 %collective-permute-start.10 = (bf16[256,256]{1,0:T(8,128)(2,1)S(1)}, bf16[256,256]{1,0:T(8,128)(2,1)S(1)}, u32[]{:S(2)}, u32[]{:S(2)}) collective-permute-start(bf16[256,256]{1,0:T(8,128)(2,1)S(1)} %collective-permute-done.8.rest_2_), channel_id=1, source_target_pairs={{0,4},{1,5},{2,0},{3,1},{4,8},{5,9},{6,2},{7,3},{8,12},{9,13},{10,... | collective-permute-start | bytes 393224 | tf_op jit(solution)/shard_map/ppermute | solution.py:437
  23.2 5.0 %collective-permute-start.15 = (bf16[256,256]{1,0:T(8,128)(2,1)S(1)}, bf16[256,256]{1,0:T(8,128)(2,1)S(1)}, u32[]{:S(2)}, u32[]{:S(2)}) collective-permute-start(bf16[256,256]{1,0:T(8,128)(2,1)S(1)} %collective-permute-done.14.rest_8_), channel_id=1, source_target_pairs={{0,2},{1,3},{2,6},{3,7},{4,0},{5,1},{6,10},{7,11},{8,4},{9,5},{10,... | collective-permute-start | bytes 393224 | tf_op jit(solution)/shard_map/ppermute | solution.py:437
  28.7 7.4 %collective-permute-start.18 = (bf16[256,256]{1,0:T(8,128)(2,1)S(1)}, bf16[256,256]{1,0:T(8,128)(2,1)S(1)}, u32[]{:S(2)}, u32[]{:S(2)}) collective-permute-start(bf16[256,256]{1,0:T(8,128)(2,1)S(1)} %project.3), channel_id=1, source_target_pairs={{0,12},{1,13},{2,14},{3,15},{4,0},{5,1},{6,2},{7,3},{8,4},{9,5},{1... | collective-permute-start | bytes 393224 | tf_op jit(solution)/shard_map/ppermute | solution.py:437
  32.5 6.9 %collective-permute-start.16 = (bf16[256,256]{1,0:T(8,128)(2,1)S(1)}, bf16[256,256]{1,0:T(8,128)(2,1)S(1)}, u32[]{:S(2)}, u32[]{:S(2)}) collective-permute-start(bf16[256,256]{1,0:T(8,128)(2,1)S(1)} %project.3), channel_id=1, source_target_pairs={{0,4},{1,5},{2,6},{3,7},{4,8},{5,9},{6,10},{7,11},{8,12},{9,13},{1... | collective-permute-start | bytes 393224 | tf_op jit(solution)/shard_map/ppermute | solution.py:437
  32.5 17.6 %collective-permute-start.21 = (bf16[256,256]{1,0:T(8,128)(2,1)S(1)}, bf16[256,256]{1,0:T(8,128)(2,1)S(1)}, u32[]{:S(2)}, u32[]{:S(2)}) collective-permute-start(bf16[256,256]{1,0:T(8,128)(2,1)S(1)} %project.3), channel_id=1, source_target_pairs={{0,10},{1,11},{2,8},{3,9},{4,14},{5,15},{6,12},{7,13},{8,2},{9,3},... | collective-permute-start | bytes 393224 | tf_op jit(solution)/shard_map/ppermute | solution.py:437
  34.0 16.1 %collective-permute-start.19 = (bf16[256,256]{1,0:T(8,128)(2,1)S(1)}, bf16[256,256]{1,0:T(8,128)(2,1)S(1)}, u32[]{:S(2)}, u32[]{:S(2)}) collective-permute-start(bf16[256,256]{1,0:T(8,128)(2,1)S(1)} %project.3), channel_id=1, source_target_pairs={{0,2},{1,3},{2,0},{3,1},{4,6},{5,7},{6,4},{7,5},{8,10},{9,11},{10,... | collective-permute-start | bytes 393224 | tf_op jit(solution)/shard_map/ppermute | solution.py:437
  34.2 15.8 %collective-permute-start.17 = (bf16[256,256]{1,0:T(8,128)(2,1)S(1)}, bf16[256,256]{1,0:T(8,128)(2,1)S(1)}, u32[]{:S(2)}, u32[]{:S(2)}) collective-permute-start(bf16[256,256]{1,0:T(8,128)(2,1)S(1)} %project.3), channel_id=1, source_target_pairs={{0,8},{1,9},{2,10},{3,11},{4,12},{5,13},{6,14},{7,15},{8,0},{9,1},... | collective-permute-start | bytes 393224 | tf_op jit(solution)/shard_map/ppermute | solution.py:437
  36.1 14.1 %collective-permute-start.22 = (bf16[256,256]{1,0:T(8,128)(2,1)S(1)}, bf16[256,256]{1,0:T(8,128)(2,1)S(1)}, u32[]{:S(2)}, u32[]{:S(2)}) collective-permute-start(bf16[256,256]{1,0:T(8,128)(2,1)S(1)} %collective-permute-done.18), channel_id=1, source_target_pairs={{0,2},{1,3},{2,0},{3,1},{4,6},{5,7},{6,4},{7,5},{8,10},{9,11},{10,... | collective-permute-start | bytes 393224 | tf_op jit(solution)/shard_map/ppermute | solution.py:437
  39.4 10.7 %collective-permute-start.20 = (bf16[256,256]{1,0:T(8,128)(2,1)S(1)}, bf16[256,256]{1,0:T(8,128)(2,1)S(1)}, u32[]{:S(2)}, u32[]{:S(2)}) collective-permute-start(bf16[256,256]{1,0:T(8,128)(2,1)S(1)} %collective-permute-done.16), channel_id=1, source_target_pairs={{0,2},{1,3},{2,0},{3,1},{4,6},{5,7},{6,4},{7,5},{8,10},{9,11},{10,... | collective-permute-start | bytes 393224 | tf_op jit(solution)/shard_map/ppermute | solution.py:437
  50.2 48.1 %collective-permute-start.23 = (bf16[2048,256]{1,0:T(8,128)(2,1)S(1)}, bf16[2048,256]{1,0:T(8,128)(2,1)S(1)}, u32[]{:S(2)}, u32[]{:S(2)}) collective-permute-start(bf16[2048,256]{1,0:T(8,128)(2,1)S(1)} %constant_dynamic-update-slice_fusion.kv_ref), channel_id=1, source_target_pairs={{0,1},{1,0},{2,3},{3,2},{4,5},{5,4},{6,7},{7,6},{8,9},{9,8},{10,11... | collective-permute-start | bytes 3145736 | tf_op jit(solution)/shard_map/ppermute | solution.py:433

commit v22 on v19

--- a/solution.py
+++ b/solution.py
@@ -478,8 +478,8 @@
         elif turn == 2:
             early = project(chips, core, place, rows, other_rows, blocks((0, 1)))
             down[1][-1], early = lax.optimization_barrier((down[1][-1], early))
-    up[0].append(along_ring(up[0][-1], 1))
-    down[1].append(along_ring(down[1][-1], -1))
+    down[0].append(along_ring(down[0][-1], -1))
+    up[1].append(along_ring(up[1][-1], 1))
     memory_kv = project(chips, core, place, rows, other_rows, blocks((2, 3, 4)), early)
     near = jnp.concatenate(line_by_line(memory_kv), axis=0)
     far = to_partner(near)

time: 144 us -> 146 us (1.014)
  waiting for transfers between devices: 19.5 us -> 21.7 us
    ppermute x21, waiting for transfers between devices: 19.5 us -> 21.6 us  [along(): lax.ppermute(x, 'pass', [(2 * s + c, 2 * d + c) for s, d in pairs for c i...]
  transfers between devices with their start and end apart: 24 -> 24, of which waited for: 13 -> 15; matrix products, arithmetic and copies ran while one was open for 0% -> 0% of each run, Pallas kernels for 35% -> 34%
where the time goes in v22:
time: 146 us; the launch traced here: 145 us
  Pallas kernels  97.1 us (67%)
  starting transfers between devices  24.9 us (17%)
  waiting for transfers between devices  21.7 us (15%)
    pallas_call x2, Pallas kernels, attend(): pl.pallas_call(functools.partial(attend_kernel, begun is not None, ahead)...  92.1 us
    ppermute x21, waiting for transfers between devices, along(): lax.ppermute(x, 'pass', [(2 * s + c, 2 * d + c) for s, d in pairs for c i...  21.6 us
    ppermute x21, starting transfers between devices, along(): lax.ppermute(x, 'pass', [(2 * s + c, 2 * d + c) for s, d in pairs for c i...  19.9 us
    ppermute x3, starting transfers between devices, to_partner(): return lax.ppermute(x, 'pass', [(i, i ^ 1) for i in range(extent)])  5.02 us
    pallas_call x1, Pallas kernels, pool(): pl.pallas_call(pool_kernel, in_specs=[vmem] * 3, out_specs=vmem, out_shap...  3.08 us
  transfers between devices with their start and end apart: 24, of which 15 were waited for; matrix products, arithmetic and copies ran while one was open for 0% of the time, Pallas kernels for 34%

profile of v22, /device:TPU:1, one launch (start us, length us, event | category | flops | bytes accessed | tf_op | source)
XLA Modules:
  0.0 145.0 jit_solution(3097049353424248128)
XLA Ops:
  0.0 0.0 copy-start.3
  0.0 0.9 copy-done.3
  1.0 0.0 copy-start
  1.0 0.0 copy-start.1
  1.0 0.1 collective-permute-start.1
  1.1 2.7 %collective-permute-start.3 = (bf16[256,256]{1,0:T(8,128)(2,1)S(1)}, bf16[256,256]{1,0:T(8,128)(2,1)S(1)}, u32[]{:S(2)}, u32[]{:S(2)}) collective-permute-start(bf16[256,256]{1,0:T(8,128)(2,1)S(1)} %get-tuple-element.16.rest_0_), channel_id=1, source_target_pairs={{0,2},{1,3},{2,6},{3,7},{4,0},{5,1},{6,10},{7,11},{8,4},{9,5},{10,... | collective-permute-start | bytes 393224 | tf_op jit(solution)/shard_map/ppermute | solution.py:437
  3.8 0.1 collective-permute-start
  3.9 0.0 collective-permute-done.1.rest_3_
  3.9 1.4 collective-permute-start.4
  5.3 0.1 collective-permute-start.2
  5.3 0.0 copy-done
  5.4 0.0 copy-done.1
  5.4 0.0 copy-done.2
  5.4 3.1 %pool.1.own_ref = bf16[128,4096]{1,0:T(8,128)(2,1)S(1)} custom-call(bf16[4,128,4096]{2,1,0:T(8,128)(2,1)S(1)} %copy-done, bf16[32,4096]{1,0:T(8,128)(2,1)S(1)} %copy-done.1, bf16[4096]{0:T(1024)(128)(2,1)S(1)} %copy-done.2), custom_call_target="tpu_custom_call" | custom-call | flops 268435456 | bytes 4194304 | tf_op jit(solution)/shard_map/pool/pallas_call | solution.py:116
  8.4 0.0 collective-permute-done.3.rest_2_
  8.5 0.1 collective-permute-done.rest_1_
  8.5 2.0 %collective-permute-done.4.rest_5_ = bf16[256,256]{1,0:T(8,128)(2,1)S(1)} collective-permute-done((bf16[256,256]{1,0:T(8,128)(2,1)S(1)}, bf16[256,256]{1,0:T(8,128)(2,1)S(1)}, u32[]{:S(2)}, u32[]{:S(2)}) %collective-permute-start.4) | collective-permute-done | bytes 131104 | tf_op jit(solution)/shard_map/ppermute | solution.py:437
  10.5 0.9 collective-permute-done.2.rest_4_
  11.3 1.2 collective-permute-start.5
  12.5 1.3 collective-permute-start.7
  13.8 0.2 collective-permute-start.11
  14.0 0.1 collective-permute-start.6
  14.1 3.6 %collective-permute-done.7.rest_1_ = bf16[256,256]{1,0:T(8,128)(2,1)S(1)} collective-permute-done((bf16[256,256]{1,0:T(8,128)(2,1)S(1)}, bf16[256,256]{1,0:T(8,128)(2,1)S(1)}, u32[]{:S(2)}, u32[]{:S(2)}) %collective-permute-start.7) | collective-permute-done | bytes 131104 | tf_op jit(solution)/shard_map/ppermute | solution.py:437
  17.6 1.3 collective-permute-start.9
  18.9 0.0 collective-permute-done.11.rest_5_
  18.9 0.2 collective-permute-start.13
  19.1 1.3 collective-permute-start.12
  20.4 1.0 collective-permute-done.6.rest_0_
  21.4 0.2 collective-permute-start.8
  21.6 0.3 collective-permute-done.9.rest_3_
  21.9 1.3 collective-permute-start.10
  23.2 0.4 collective-permute-done.13.rest_7_
  23.5 0.2 collective-permute-start.15
  23.7 0.0 collective-permute-done.5.other_ref
  23.7 0.4 project.2.rest_10_
  24.1 0.0 copy-start.4
  24.1 0.7 collective-permute-done.12.rest_6_
  24.8 1.3 collective-permute-start.14
  26.1 0.6 collective-permute-done.8.rest_2_
  26.7 0.6 collective-permute-done.10.rest_4_
  27.4 1.8 %collective-permute-done.15.rest_9_ = bf16[256,256]{1,0:T(8,128)(2,1)S(1)} collective-permute-done((bf16[256,256]{1,0:T(8,128)(2,1)S(1)}, bf16[256,256]{1,0:T(8,128)(2,1)S(1)}, u32[]{:S(2)}, u32[]{:S(2)}) %collective-permute-start.15) | collective-permute-done | bytes 131104 | tf_op jit(solution)/shard_map/ppermute | solution.py:437
  29.2 1.0 collective-permute-done.14.rest_8_
  30.2 1.4 project.3
  31.7 1.3 collective-permute-start.17
  33.0 1.3 collective-permute-start.16
  34.3 4.0 %collective-permute-start.22 = (bf16[256,256]{1,0:T(8,128)(2,1)S(1)}, bf16[256,256]{1,0:T(8,128)(2,1)S(1)}, u32[]{:S(2)}, u32[]{:S(2)}) collective-permute-start(bf16[256,256]{1,0:T(8,128)(2,1)S(1)} %project.3), channel_id=1, source_target_pairs={{0,14},{1,15},{2,12},{3,13},{4,2},{5,3},{6,0},{7,1},{8,6},{9,7},{1... | collective-permute-start | bytes 393224 | tf_op jit(solution)/shard_map/ppermute | solution.py:437
  38.3 0.0 collective-permute-start.19
  38.3 0.3 collective-permute-start.18
  38.6 2.8 %collective-permute-done.17 = bf16[256,256]{1,0:T(8,128)(2,1)S(1)} collective-permute-done((bf16[256,256]{1,0:T(8,128)(2,1)S(1)}, bf16[256,256]{1,0:T(8,128)(2,1)S(1)}, u32[]{:S(2)}, u32[]{:S(2)}) %collective-permute-start.17) | collective-permute-done | bytes 131104 | tf_op jit(solution)/shard_map/ppermute | solution.py:437
  41.4 0.0 collective-permute-start.21
  41.4 0.0 collective-permute-done.16
  41.4 1.5 %collective-permute-start.20 = (bf16[256,256]{1,0:T(8,128)(2,1)S(1)}, bf16[256,256]{1,0:T(8,128)(2,1)S(1)}, u32[]{:S(2)}, u32[]{:S(2)}) collective-permute-start(bf16[256,256]{1,0:T(8,128)(2,1)S(1)} %collective-permute-done.16), channel_id=1, source_target_pairs={{0,2},{1,3},{2,0},{3,1},{4,6},{5,7},{6,4},{7,5},{8,10},{9,11},{10,... | collective-permute-start | bytes 393224 | tf_op jit(solution)/shard_map/ppermute | solution.py:437
  42.9 3.4 %collective-permute-done.18 = bf16[256,256]{1,0:T(8,128)(2,1)S(1)} collective-permute-done((bf16[256,256]{1,0:T(8,128)(2,1)S(1)}, bf16[256,256]{1,0:T(8,128)(2,1)S(1)}, u32[]{:S(2)}, u32[]{:S(2)}) %collective-permute-start.18) | collective-permute-done | bytes 131104 | tf_op jit(solution)/shard_map/ppermute | solution.py:437
  46.4 0.0 collective-permute-done.19
  46.4 2.5 %collective-permute-done.20 = bf16[256,256]{1,0:T(8,128)(2,1)S(1)} collective-permute-done((bf16[256,256]{1,0:T(8,128)(2,1)S(1)}, bf16[256,256]{1,0:T(8,128)(2,1)S(1)}, u32[]{:S(2)}, u32[]{:S(2)}) %collective-permute-start.20) | collective-permute-done | bytes 131104 | tf_op jit(solution)/shard_map/ppermute | solution.py:437
  48.9 0.0 collective-permute-done.21
  48.9 0.0 collective-permute-done.22
  48.9 3.7 %collective-permute-start.23 = (bf16[2048,256]{1,0:T(8,128)(2,1)S(1)}, bf16[2048,256]{1,0:T(8,128)(2,1)S(1)}, u32[]{:S(2)}, u32[]{:S(2)}) collective-permute-start(bf16[2048,256]{1,0:T(8,128)(2,1)S(1)} %constant_dynamic-update-slice_fusion.kv_ref), channel_id=1, source_target_pairs={{0,1},{1,0},{2,3},{3,2},{4,5},{5,4},{6,7},{7,6},{8,9},{9,8},{10,11... | collective-permute-start | bytes 3145736 | tf_op jit(solution)/shard_map/ppermute | solution.py:433
  52.7 0.0 copy-done.6
  52.7 0.0 copy-done.5
  52.7 0.0 copy-done.4
  52.7 46.4 %attend.2 = (bf16[4,64,7424]{2,1,0:T(8,128)(2,1)}, bf16[64,3712]{1,0:T(8,128)(2,1)S(1)}) custom-call(s32[1]{0:T(128)} %bitcast.1.core_ref.half_ref, s32[4,16]{1,0:T(4,128)S(1)} %fusion.6.start_ref, s32[4]{0:T(128)S(1)} %copy-done.5, bf16[4,64,7424]{2,1,0:T(8,128)(2,1)} %q_hbm.3, bf16[2048,256]{1,0:T(8,128)(2,1)S(1)} %constant_dynamic-update-slice_fusion.kv_ref, ...), custom_call_target="tpu_custom_call" | custom-call | flops 2189426688 | bytes 3801088 | tf_op jit(solution)/shard_map/attend/pallas_call | solution.py:330
  99.1 0.0 collective-permute-done.23.kv_ref
  99.1 45.7 %attend.3 = bf16[4,64,7424]{2,1,0:T(8,128)(2,1)} custom-call(s32[1]{0:T(128)} %bitcast.half_ref, s32[4,16]{1,0:T(4,128)S(1)} %fusion.6.start_ref, s32[4]{0:T(128)S(1)} %copy-done.5, bf16[4,64,7424]{2,1,0:T(8,128)(2,1)} %q_hbm.3, bf16[2048,256]{1,0:T(8,128)(2,1)S(1)} %collective-permute-done.23.kv_ref, ...), custom_call_target="tpu_custom_call", output_to_operand_aliasing={{}: (7, {})} | custom-call | flops 2189426688 | bytes 3801088 | tf_op jit(solution)/shard_map/attend/pallas_call | solution.py:330
  (13 shorter events, 0.2 us)
Async XLA Ops:
  0.0 0.9 copy-start.3
  1.0 4.4 %copy-start = (bf16[4,128,4096]{2,1,0:T(8,128)(2,1)S(1)}, bf16[4,128,4096]{2,1,0:T(8,128)(2,1)}, u32[]{:S(2)}) copy-start(bf16[4,128,4096]{2,1,0:T(8,128)(2,1)} %states.1) | copy-start | bytes 12582916
  1.0 4.4 %copy-start.1 = (bf16[32,4096]{1,0:T(8,128)(2,1)S(1)}, bf16[32,4096]{1,0:T(8,128)(2,1)}, u32[]{:S(2)}) copy-start(bf16[32,4096]{1,0:T(8,128)(2,1)} %queries.1) | copy-start | bytes 786436
  1.0 4.4 %copy-start.2 = (bf16[4096]{0:T(1024)(128)(2,1)S(1)}, bf16[4096]{0:T(1024)(128)(2,1)}, u32[]{:S(2)}) copy-start(bf16[4096]{0:T(1024)(128)(2,1)} %gain.1) | copy-start | bytes 24580
  1.0 2.9 %collective-permute-start.1 = (bf16[256,256]{1,0:T(8,128)(2,1)S(1)}, bf16[256,256]{1,0:T(8,128)(2,1)S(1)}, u32[]{:S(2)}, u32[]{:S(2)}) collective-permute-start(bf16[256,256]{1,0:T(8,128)(2,1)S(1)} %get-tuple-element.17), channel_id=1, source_target_pairs={{0,1},{1,0},{2,3},{3,2},{4,5},{5,4},{6,7},{7,6},{8,9},{9,8},{10,11... | collective-permute-start | bytes 393224 | tf_op jit(solution)/shard_map/ppermute | solution.py:433
  1.1 7.3 %collective-permute-start.3 = (bf16[256,256]{1,0:T(8,128)(2,1)S(1)}, bf16[256,256]{1,0:T(8,128)(2,1)S(1)}, u32[]{:S(2)}, u32[]{:S(2)}) collective-permute-start(bf16[256,256]{1,0:T(8,128)(2,1)S(1)} %get-tuple-element.16.rest_0_), channel_id=1, source_target_pairs={{0,2},{1,3},{2,6},{3,7},{4,0},{5,1},{6,10},{7,11},{8,4},{9,5},{10,... | collective-permute-start | bytes 393224 | tf_op jit(solution)/shard_map/ppermute | solution.py:437
  3.8 4.7 %collective-permute-start = (bf16[256,256]{1,0:T(8,128)(2,1)S(1)}, bf16[256,256]{1,0:T(8,128)(2,1)S(1)}, u32[]{:S(2)}, u32[]{:S(2)}) collective-permute-start(bf16[256,256]{1,0:T(8,128)(2,1)S(1)} %get-tuple-element.16.rest_0_), channel_id=1, source_target_pairs={{0,4},{1,5},{2,0},{3,1},{4,8},{5,9},{6,2},{7,3},{8,12},{9,13},{10,... | collective-permute-start | bytes 393224 | tf_op jit(solution)/shard_map/ppermute | solution.py:437
  3.9 6.6 %collective-permute-start.4 = (bf16[256,256]{1,0:T(8,128)(2,1)S(1)}, bf16[256,256]{1,0:T(8,128)(2,1)S(1)}, u32[]{:S(2)}, u32[]{:S(2)}) collective-permute-start(bf16[256,256]{1,0:T(8,128)(2,1)S(1)} %collective-permute-done.1.rest_3_), channel_id=1, source_target_pairs={{0,2},{1,3},{2,6},{3,7},{4,0},{5,1},{6,10},{7,11},{8,4},{9,5},{10,... | collective-permute-start | bytes 393224 | tf_op jit(solution)/shard_map/ppermute | solution.py:437
  5.3 6.1 %collective-permute-start.2 = (bf16[256,256]{1,0:T(8,128)(2,1)S(1)}, bf16[256,256]{1,0:T(8,128)(2,1)S(1)}, u32[]{:S(2)}, u32[]{:S(2)}) collective-permute-start(bf16[256,256]{1,0:T(8,128)(2,1)S(1)} %collective-permute-done.1.rest_3_), channel_id=1, source_target_pairs={{0,4},{1,5},{2,0},{3,1},{4,8},{5,9},{6,2},{7,3},{8,12},{9,13},{10,... | collective-permute-start | bytes 393224 | tf_op jit(solution)/shard_map/ppermute | solution.py:437
  11.3 12.4 %collective-permute-start.5 = (bf16[128,4096]{1,0:T(8,128)(2,1)S(1)}, bf16[128,4096]{1,0:T(8,128)(2,1)S(1)}, u32[]{:S(2)}, u32[]{:S(2)}) collective-permute-start(bf16[128,4096]{1,0:T(8,128)(2,1)S(1)} %pool.1.own_ref), channel_id=1, source_target_pairs={{0,1},{1,0},{2,3},{3,2},{4,5},{5,4},{6,7},{7,6},{8,9},{9,8},{10,11... | collective-permute-start | bytes 3145736 | tf_op jit(solution)/shard_map/ppermute | solution.py:433
  12.5 5.1 %collective-permute-start.7 = (bf16[256,256]{1,0:T(8,128)(2,1)S(1)}, bf16[256,256]{1,0:T(8,128)(2,1)S(1)}, u32[]{:S(2)}, u32[]{:S(2)}) collective-permute-start(bf16[256,256]{1,0:T(8,128)(2,1)S(1)} %collective-permute-done.3.rest_2_), channel_id=1, source_target_pairs={{0,2},{1,3},{2,6},{3,7},{4,0},{5,1},{6,10},{7,11},{8,4},{9,5},{10,... | collective-permute-start | bytes 393224 | tf_op jit(solution)/shard_map/ppermute | solution.py:437
  13.8 5.1 %collective-permute-start.11 = (bf16[256,256]{1,0:T(8,128)(2,1)S(1)}, bf16[256,256]{1,0:T(8,128)(2,1)S(1)}, u32[]{:S(2)}, u32[]{:S(2)}) collective-permute-start(bf16[256,256]{1,0:T(8,128)(2,1)S(1)} %collective-permute-done.2.rest_4_), channel_id=1, source_target_pairs={{0,4},{1,5},{2,0},{3,1},{4,8},{5,9},{6,2},{7,3},{8,12},{9,13},{10,... | collective-permute-start | bytes 393224 | tf_op jit(solution)/shard_map/ppermute | solution.py:437
  14.0 7.4 %collective-permute-start.6 = (bf16[256,256]{1,0:T(8,128)(2,1)S(1)}, bf16[256,256]{1,0:T(8,128)(2,1)S(1)}, u32[]{:S(2)}, u32[]{:S(2)}) collective-permute-start(bf16[256,256]{1,0:T(8,128)(2,1)S(1)} %collective-permute-done.rest_1_), channel_id=1, source_target_pairs={{0,4},{1,5},{2,0},{3,1},{4,8},{5,9},{6,2},{7,3},{8,12},{9,13},{10,... | collective-permute-start | bytes 393224 | tf_op jit(solution)/shard_map/ppermute | solution.py:437
  17.6 4.2 %collective-permute-start.9 = (bf16[256,256]{1,0:T(8,128)(2,1)S(1)}, bf16[256,256]{1,0:T(8,128)(2,1)S(1)}, u32[]{:S(2)}, u32[]{:S(2)}) collective-permute-start(bf16[256,256]{1,0:T(8,128)(2,1)S(1)} %collective-permute-done.7.rest_1_), channel_id=1, source_target_pairs={{0,2},{1,3},{2,6},{3,7},{4,0},{5,1},{6,10},{7,11},{8,4},{9,5},{10,... | collective-permute-start | bytes 393224 | tf_op jit(solution)/shard_map/ppermute | solution.py:437
  18.9 4.6 %collective-permute-start.13 = (bf16[256,256]{1,0:T(8,128)(2,1)S(1)}, bf16[256,256]{1,0:T(8,128)(2,1)S(1)}, u32[]{:S(2)}, u32[]{:S(2)}) collective-permute-start(bf16[256,256]{1,0:T(8,128)(2,1)S(1)} %collective-permute-done.11.rest_5_), channel_id=1, source_target_pairs={{0,4},{1,5},{2,0},{3,1},{4,8},{5,9},{6,2},{7,3},{8,12},{9,13},{10,... | collective-permute-start | bytes 393224 | tf_op jit(solution)/shard_map/ppermute | solution.py:437
  19.1 5.7 %collective-permute-start.12 = (bf16[256,256]{1,0:T(8,128)(2,1)S(1)}, bf16[256,256]{1,0:T(8,128)(2,1)}, u32[]{:S(2)}, u32[]{:S(2)}) collective-permute-start(bf16[256,256]{1,0:T(8,128)(2,1)S(1)} %collective-permute-done.4.rest_5_), channel_id=1, source_target_pairs={{0,2},{1,3},{2,6},{3,7},{4,0},{5,1},{6,10},{7,11},{8,4},{9,5},{10,... | collective-permute-start | bytes 393224 | tf_op jit(solution)/shard_map/ppermute | solution.py:437
  21.4 5.3 %collective-permute-start.8 = (bf16[256,256]{1,0:T(8,128)(2,1)S(1)}, bf16[256,256]{1,0:T(8,128)(2,1)S(1)}, u32[]{:S(2)}, u32[]{:S(2)}) collective-permute-start(bf16[256,256]{1,0:T(8,128)(2,1)S(1)} %collective-permute-done.6.rest_0_), channel_id=1, source_target_pairs={{0,4},{1,5},{2,0},{3,1},{4,8},{5,9},{6,2},{7,3},{8,12},{9,13},{10,... | collective-permute-start | bytes 393224 | tf_op jit(solution)/shard_map/ppermute | solution.py:437
  21.9 5.5 %collective-permute-start.10 = (bf16[256,256]{1,0:T(8,128)(2,1)S(1)}, bf16[256,256]{1,0:T(8,128)(2,1)S(1)}, u32[]{:S(2)}, u32[]{:S(2)}) collective-permute-start(bf16[256,256]{1,0:T(8,128)(2,1)S(1)} %collective-permute-done.9.rest_3_), channel_id=1, source_target_pairs={{0,2},{1,3},{2,6},{3,7},{4,0},{5,1},{6,10},{7,11},{8,4},{9,5},{10,... | collective-permute-start | bytes 393224 | tf_op jit(solution)/shard_map/ppermute | solution.py:437
  23.5 5.7 %collective-permute-start.15 = (bf16[256,256]{1,0:T(8,128)(2,1)S(1)}, bf16[256,256]{1,0:T(8,128)(2,1)S(1)}, u32[]{:S(2)}, u32[]{:S(2)}) collective-permute-start(bf16[256,256]{1,0:T(8,128)(2,1)S(1)} %collective-permute-done.13.rest_7_), channel_id=1, source_target_pairs={{0,4},{1,5},{2,0},{3,1},{4,8},{5,9},{6,2},{7,3},{8,12},{9,13},{10,... | collective-permute-start | bytes 393224 | tf_op jit(solution)/shard_map/ppermute | solution.py:437
  23.7 28.9 %copy-start.6 = (s32[4,16]{1,0:T(4,128)S(1)}, s32[4,16]{1,0:T(4,128)}, u32[]{:S(2)}) copy-start(s32[4,16]{1,0:T(4,128)} %param.12) | copy-start | bytes 772
  23.7 29.0 %copy-start.5 = (s32[4]{0:T(128)S(1)}, s32[4]{0:T(128)}, u32[]{:S(2)}) copy-start(s32[4]{0:T(128)} %length_ref.3) | copy-start | bytes 52
  24.1 28.6 %copy-start.4 = (bf16[4,64,512]{2,1,0:T(8,128)(2,1)S(1)}, bf16[4,64,512]{2,1,0:T(8,128)(2,1)}, u32[]{:S(2)}) copy-start(bf16[4,64,512]{2,1,0:T(8,128)(2,1)} %own_kv_ref.3) | copy-start | bytes 786436
  24.8 5.4 %collective-permute-start.14 = (bf16[256,256]{1,0:T(8,128)(2,1)}, bf16[256,256]{1,0:T(8,128)(2,1)S(1)}, u32[]{:S(2)}, u32[]{:S(2)}) collective-permute-start(bf16[256,256]{1,0:T(8,128)(2,1)} %collective-permute-done.12.rest_6_), channel_id=1, source_target_pairs={{0,2},{1,3},{2,6},{3,7},{4,0},{5,1},{6,10},{7,11},{8,4},{9,5},{10,... | collective-permute-start | bytes 393224 | tf_op jit(solution)/shard_map/ppermute | solution.py:437
  31.7 9.8 %collective-permute-start.17 = (bf16[256,256]{1,0:T(8,128)(2,1)S(1)}, bf16[256,256]{1,0:T(8,128)(2,1)S(1)}, u32[]{:S(2)}, u32[]{:S(2)}) collective-permute-start(bf16[256,256]{1,0:T(8,128)(2,1)S(1)} %project.3), channel_id=1, source_target_pairs={{0,8},{1,9},{2,10},{3,11},{4,12},{5,13},{6,14},{7,15},{8,0},{9,1},... | collective-permute-start | bytes 393224 | tf_op jit(solution)/shard_map/ppermute | solution.py:437
  33.0 8.4 %collective-permute-start.16 = (bf16[256,256]{1,0:T(8,128)(2,1)S(1)}, bf16[256,256]{1,0:T(8,128)(2,1)S(1)}, u32[]{:S(2)}, u32[]{:S(2)}) collective-permute-start(bf16[256,256]{1,0:T(8,128)(2,1)S(1)} %project.3), channel_id=1, source_target_pairs={{0,4},{1,5},{2,6},{3,7},{4,8},{5,9},{6,10},{7,11},{8,12},{9,13},{1... | collective-permute-start | bytes 393224 | tf_op jit(solution)/shard_map/ppermute | solution.py:437
  34.3 14.6 %collective-permute-start.22 = (bf16[256,256]{1,0:T(8,128)(2,1)S(1)}, bf16[256,256]{1,0:T(8,128)(2,1)S(1)}, u32[]{:S(2)}, u32[]{:S(2)}) collective-permute-start(bf16[256,256]{1,0:T(8,128)(2,1)S(1)} %project.3), channel_id=1, source_target_pairs={{0,14},{1,15},{2,12},{3,13},{4,2},{5,3},{6,0},{7,1},{8,6},{9,7},{1... | collective-permute-start | bytes 393224 | tf_op jit(solution)/shard_map/ppermute | solution.py:437
  38.3 8.1 %collective-permute-start.19 = (bf16[256,256]{1,0:T(8,128)(2,1)S(1)}, bf16[256,256]{1,0:T(8,128)(2,1)S(1)}, u32[]{:S(2)}, u32[]{:S(2)}) collective-permute-start(bf16[256,256]{1,0:T(8,128)(2,1)S(1)} %project.3), channel_id=1, source_target_pairs={{0,2},{1,3},{2,0},{3,1},{4,6},{5,7},{6,4},{7,5},{8,10},{9,11},{10,... | collective-permute-start | bytes 393224 | tf_op jit(solution)/shard_map/ppermute | solution.py:437
  38.3 8.0 %collective-permute-start.18 = (bf16[256,256]{1,0:T(8,128)(2,1)S(1)}, bf16[256,256]{1,0:T(8,128)(2,1)S(1)}, u32[]{:S(2)}, u32[]{:S(2)}) collective-permute-start(bf16[256,256]{1,0:T(8,128)(2,1)S(1)} %project.3), channel_id=1, source_target_pairs={{0,12},{1,13},{2,14},{3,15},{4,0},{5,1},{6,2},{7,3},{8,4},{9,5},{1... | collective-permute-start | bytes 393224 | tf_op jit(solution)/shard_map/ppermute | solution.py:437
  41.4 7.4 %collective-permute-start.21 = (bf16[256,256]{1,0:T(8,128)(2,1)S(1)}, bf16[256,256]{1,0:T(8,128)(2,1)S(1)}, u32[]{:S(2)}, u32[]{:S(2)}) collective-permute-start(bf16[256,256]{1,0:T(8,128)(2,1)S(1)} %collective-permute-done.17), channel_id=1, source_target_pairs={{0,2},{1,3},{2,0},{3,1},{4,6},{5,7},{6,4},{7,5},{8,10},{9,11},{10,... | collective-permute-start | bytes 393224 | tf_op jit(solution)/shard_map/ppermute | solution.py:437
  41.4 7.4 %collective-permute-start.20 = (bf16[256,256]{1,0:T(8,128)(2,1)S(1)}, bf16[256,256]{1,0:T(8,128)(2,1)S(1)}, u32[]{:S(2)}, u32[]{:S(2)}) collective-permute-start(bf16[256,256]{1,0:T(8,128)(2,1)S(1)} %collective-permute-done.16), channel_id=1, source_target_pairs={{0,2},{1,3},{2,0},{3,1},{4,6},{5,7},{6,4},{7,5},{8,10},{9,11},{10,... | collective-permute-start | bytes 393224 | tf_op jit(solution)/shard_map/ppermute | solution.py:437
  48.9 50.2 %collective-permute-start.23 = (bf16[2048,256]{1,0:T(8,128)(2,1)S(1)}, bf16[2048,256]{1,0:T(8,128)(2,1)S(1)}, u32[]{:S(2)}, u32[]{:S(2)}) collective-permute-start(bf16[2048,256]{1,0:T(8,128)(2,1)S(1)} %constant_dynamic-update-slice_fusion.kv_ref), channel_id=1, source_target_pairs={{0,1},{1,0},{2,3},{3,2},{4,5},{5,4},{6,7},{7,6},{8,9},{9,8},{10,11... | collective-permute-start | bytes 3145736 | tf_op jit(solution)/shard_map/ppermute | solution.py:433
